TPU v7x, 32 devices: a whole 2x2x4 slice. The times are simulated.
32 devices in a mesh: group: 2 (over x), expert: 8 (over z, y), tensor: 2 (over core).
Axes of the slice: x: 2, y: 2, z: 4, core: 2. Of those that a mesh axis runs over, the one named last changes fastest.
Arguments:
- tokens: bfloat16 [2048, 2048], P(('group', 'expert'), 'tensor'), parts along dimension 0, may hold values from -6 to 6
- expert_ids: int32 [2048, 4], P(('group', 'expert')), parts along dimension 0, may hold values from 0 to 7, as said below
- router_weights: float32 [2048, 4], P(('group', 'expert')), parts along dimension 0, may hold values from 0.02 to 0.5
- gate_weight: bfloat16 [8, 2048, 768], P('expert', None, 'tensor'), may hold values from -0.125 to 0.125
- up_weight: bfloat16 [8, 2048, 768], P('expert', None, 'tensor'), may hold values from -0.125 to 0.125
- down_weight: bfloat16 [8, 768, 2048], P('expert', 'tensor'), may hold values from -0.21875 to 0.21875
- grad_out: bfloat16 [2048, 2048], P(('group', 'expert'), 'tensor'), parts along dimension 0, may hold values from -1.5 to 1.5
Outputs:
- layer_out: bfloat16 [2048, 2048], P(('group', 'expert'), 'tensor'), parts along dimension 0
- input_grad: bfloat16 [2048, 2048], P(('group', 'expert'), 'tensor'), parts along dimension 0
- weight_grad: float32 [2048, 4], P(('group', 'expert')), parts along dimension 0
- gate_grad: bfloat16 [16, 2048, 768], P(('group', 'expert'), None, 'tensor'), parts along dimension 0
- up_grad: bfloat16 [16, 2048, 768], P(('group', 'expert'), None, 'tensor'), parts along dimension 0
- down_grad: bfloat16 [16, 768, 2048], P(('group', 'expert'), 'tensor'), parts along dimension 0
There are 2 independent parts, one for each index of `group`. A program takes and returns all parts, laid end to end along the dimension named above; an argument that names none is the same for every part. Nothing has to cross between parts.
Inputs may be any that keep to these rules, and one draw needn't show every extreme that they name: `expert_ids`: each token names 4 different experts. Among the 128 tokens held by one device along `expert` no expert is named by more than 96 of them, and one expert, the same on every index, is named by exactly 96 of them on each.
All inputs are finite; a program needn't handle non-finite values.
Results may differ from a plain program's by a relative error of at most 0.0073.
Values may be sent and summed in bfloat16 or wider, within the bound.
No kernel may reach another device: no remote copies, remote signals or barrier semaphores. Data moves between devices by JAX's collectives and lax.ppermute only.
A program may use at most 128 MiB of HBM per device.

v0:
```python
import jax
import jax.numpy as jnp
from jax import lax
from jax.sharding import PartitionSpec as P


def route_slots(expert_ids, capacity, peer_count):
    flat_ids = expert_ids.reshape(-1)
    onehot = (flat_ids[:, None] == jnp.arange(peer_count, dtype=jnp.int32)[None, :]).astype(
        jnp.int32
    )
    running = jnp.cumsum(onehot, axis=0)
    ranking = jnp.sum(onehot * running, axis=1) - 1
    return (flat_ids * capacity + ranking).reshape(expert_ids.shape)


def expert_forward(arrived, gate_local, up_local, down_local):
    slot_count = arrived.shape[0] * arrived.shape[1]
    whole_rows = lax.all_gather(arrived, "tensor", axis=2, tiled=True)
    whole_rows = whole_rows.reshape(slot_count, whole_rows.shape[2])
    gate_values = jnp.dot(whole_rows, gate_local, preferred_element_type=jnp.float32)
    upward = jnp.dot(whole_rows, up_local, preferred_element_type=jnp.float32)
    hidden = (jax.nn.silu(gate_values) * upward).astype(jnp.bfloat16)
    partial_out = jnp.dot(hidden, down_local, preferred_element_type=jnp.float32)
    summed = lax.psum_scatter(
        partial_out.astype(jnp.bfloat16), "tensor", scatter_dimension=1, tiled=True
    )
    results = summed.reshape(arrived.shape)
    return (results, (whole_rows, gate_values, upward, hidden))


def expert_backward(arrived, saved_values, gate_local, up_local, down_local):
    whole_rows, gate_values, upward, hidden = saved_values
    contract_last = (((1,), (1,)), ((), ()))
    contract_rows = (((0,), (0,)), ((), ()))
    grad_whole = lax.all_gather(arrived, "tensor", axis=2, tiled=True)
    grad_whole = grad_whole.reshape(whole_rows.shape)
    grad_hidden = lax.dot_general(
        grad_whole, down_local, contract_last, preferred_element_type=jnp.float32
    )
    sigmoid_gate = jax.nn.sigmoid(gate_values)
    grad_gate = (
        grad_hidden * upward * sigmoid_gate * (1.0 + gate_values * (1.0 - sigmoid_gate))
    ).astype(jnp.bfloat16)
    grad_up = (grad_hidden * gate_values * sigmoid_gate).astype(jnp.bfloat16)
    partial_in = lax.dot_general(
        grad_gate, gate_local, contract_last, preferred_element_type=jnp.float32
    )
    partial_in = partial_in + lax.dot_general(
        grad_up, up_local, contract_last, preferred_element_type=jnp.float32
    )
    summed = lax.psum_scatter(
        partial_in.astype(jnp.bfloat16), "tensor", scatter_dimension=1, tiled=True
    )
    returned = summed.reshape(arrived.shape)
    down_part = lax.dot_general(
        hidden, grad_whole, contract_rows, preferred_element_type=jnp.float32
    )
    gate_part = lax.dot_general(
        whole_rows, grad_gate, contract_rows, preferred_element_type=jnp.float32
    )
    up_part = lax.dot_general(
        whole_rows, grad_up, contract_rows, preferred_element_type=jnp.float32
    )
    return (
        returned,
        gate_part.astype(jnp.bfloat16)[None],
        up_part.astype(jnp.bfloat16)[None],
        down_part.astype(jnp.bfloat16)[None],
    )


def per_device(tokens, expert_ids, router_weights, gate_weight, up_weight, down_weight, grad_out):
    token_count, half_width = tokens.shape
    top_count = expert_ids.shape[1]
    peer_count = lax.axis_size("expert")
    capacity = min(token_count, 3 * token_count * top_count // (2 * peer_count))
    slot_count = peer_count * capacity
    slot_of = route_slots(expert_ids, capacity, peer_count)
    picked = jnp.arange(slot_count, dtype=jnp.int32)[:, None, None] == slot_of[None, :, :]
    placing = jnp.sum(picked.astype(jnp.bfloat16), axis=2)
    scaling = jnp.sum(jnp.where(picked, router_weights[None, :, :], 0.0), axis=2)
    sent_rows = jnp.dot(placing, tokens, preferred_element_type=jnp.float32).astype(jnp.bfloat16)
    sent_rows = sent_rows.reshape(peer_count, capacity, half_width)
    sent_grads = jnp.dot(scaling, grad_out.astype(jnp.float32), precision=lax.Precision.HIGHEST)
    sent_grads = sent_grads.astype(jnp.bfloat16).reshape(peer_count, capacity, half_width)
    gate_local = gate_weight[0]
    up_local = up_weight[0]
    down_local = down_weight[0]
    arrived_rows = lax.all_to_all(sent_rows, "expert", split_axis=0, concat_axis=0, tiled=True)
    results, saved_values = expert_forward(arrived_rows, gate_local, up_local, down_local)
    came_out = lax.all_to_all(results, "expert", split_axis=0, concat_axis=0, tiled=True)
    arrived_grads = lax.all_to_all(sent_grads, "expert", split_axis=0, concat_axis=0, tiled=True)
    returned, gate_grad, up_grad, down_grad = expert_backward(
        arrived_grads, saved_values, gate_local, up_local, down_local
    )
    came_in = lax.all_to_all(returned, "expert", split_axis=0, concat_axis=0, tiled=True)
    outputs = came_out.reshape(slot_count, half_width)[slot_of].astype(jnp.float32)
    layer_out = jnp.sum(router_weights[:, :, None] * outputs, axis=1).astype(jnp.bfloat16)
    partial_weight = jnp.sum(grad_out.astype(jnp.float32)[:, None, :] * outputs, axis=2)
    weight_grad = lax.psum(partial_weight, "tensor")
    row_grads = came_in.reshape(slot_count, half_width)[slot_of].astype(jnp.float32)
    input_grad = jnp.sum(row_grads, axis=1).astype(jnp.bfloat16)
    return (layer_out, input_grad, weight_grad, gate_grad, up_grad, down_grad)


def solution(mesh):
    in_specs = (
        P(("group", "expert"), "tensor"),
        P(("group", "expert"), None),
        P(("group", "expert"), None),
        P("expert", None, "tensor"),
        P("expert", None, "tensor"),
        P("expert", "tensor", None),
        P(("group", "expert"), "tensor"),
    )
    out_specs = (
        P(("group", "expert"), "tensor"),
        P(("group", "expert"), "tensor"),
        P(("group", "expert"), None),
        P(("group", "expert"), None, "tensor"),
        P(("group", "expert"), None, "tensor"),
        P(("group", "expert"), "tensor", None),
    )
    return jax.shard_map(
        per_device, mesh=mesh, in_specs=in_specs, out_specs=out_specs, check_vma=False
    )
```

profile of v0, /device:TPU:9, one launch (start us, length us, event | category | flops | bytes accessed | tf_op | source)
XLA Modules:
  0.0 227.6 jit_solution(8326883408487787617)
XLA Ops:
  7.2 0.0 copy-start
  7.2 0.0 all-gather.3.cloned.1.call-start
  7.2 0.9 copy.37
  8.1 0.1 eq.43
  8.2 0.1 eq.39
  8.4 1.1 reduce-window.6
  9.5 0.2 slice_reduce_fusion
  9.8 0.1 fusion.15
  9.9 0.1 sub.10
  10.0 0.1 copy.39
  10.0 0.7 compare_select_fusion
  10.7 0.2 fusion.14
  10.9 1.5 convolution_convert_fusion.4
  12.4 40.8 %all_to_all.20 = bf16[8,96,1024]{2,1,0:T(8,128)(2,1)} all-to-all(bf16[8,96,1024]{2,1,0:T(8,128)(2,1)S(1)} %bitcast.56), channel_id=1, replica_groups=mesh['group'=2,'expert'=8,'tensor'=2] {'expert'}, dimensions={0} | all-to-all | bytes 3145728 | tf_op jit(solution)/shard_map/all_to_all | solution.py:90
  53.2 0.0 all-gather.3.cloned.1.call-update
  53.3 0.0 all-gather.5.cloned.1.call-start
  53.3 0.6 copy-done.8
  53.9 0.2 select_reduce_fusion
  54.1 0.1 copy-done.4
  54.2 1.4 convolution_convert_fusion.5
  55.6 40.1 %all_to_all.21 = bf16[8,96,1024]{2,1,0:T(8,128)(2,1)} all-to-all(bf16[8,96,1024]{2,1,0:T(8,128)(2,1)S(1)} %bitcast.55), channel_id=1, replica_groups=mesh['group'=2,'expert'=8,'tensor'=2] {'expert'}, dimensions={0} | all-to-all | bytes 3145728 | tf_op jit(solution)/shard_map/all_to_all | solution.py:93
  95.7 0.0 all-gather.5.cloned.1.call-update
  95.7 0.0 reduce-scatter.3.cloned.1.call-start
  95.7 0.0 all-gather.3.cloned.1.call-done
  95.8 0.0 copy-start.2
  95.8 0.0 copy-start.9
  95.8 5.3 %fusion.7 = f32[768,384]{1,0:T(8,128)} fusion(bf16[768,2048]{1,0:T(8,128)(2,1)} %bitcast.59, bf16[1,2048,384]{2,1,0:T(8,128)(2,1)} %param.11), kind=kOutput, calls=%fused_computation.18 | convolution fusion | flops 1207959552 | bytes 5898240 | tf_op jit(solution)/shard_map/dot_general | solution.py:22
  101.1 0.0 copy-done.2
  101.1 2.8 %fusion.11 = f32[768,384]{1,0:T(8,128)} fusion(bf16[768,2048]{1,0:T(8,128)(2,1)S(1)} %bitcast.60, bf16[1,2048,384]{2,1,0:T(8,128)(2,1)S(1)} %copy-done.2), kind=kOutput, calls=%fused_computation.22 | convolution fusion | flops 1207959552 | bytes 5898240 | tf_op jit(solution)/shard_map/dot_general | solution.py:21
  103.9 5.7 %all-gather.5.cloned.1.call-done = bf16[8,96,2048]{2,1,0:T(8,128)(2,1)} async-done(((bf16[8,96,1024]{2,1,0:T(8,128)(2,1)}), bf16[8,96,2048]{2,1,0:T(8,128)(2,1)}) %all-gather.5.cloned.1.call-update) | async-done | bytes 3145744 | tf_op jit(solution)/shard_map/all_gather | solution.py:36
  109.6 5.8 %multiply_convert_fusion = (bf16[768,384]{1,0:T(8,128)(2,1)}, bf16[768,384]{1,0:T(8,128)(2,1)}, bf16[768,384]{1,0:T(8,128)(2,1)S(1)}) fusion(f32[768,384]{1,0:T(8,128)} %fusion.11, f32[768,384]{1,0:T(8,128)} %fusion.7, bf16[768,2048]{1,0:T(8,128)(2,1)} %bitcast.63, bf16[1,384,2048]{2,1,0:T(8,128)(2,1)S(1)} %copy-done), kind=kOutput, calls=%fused_computation.27 | convolution fusion | flops 1212678144 | bytes 8847360 | tf_op jit(solution)/shard_map/dot_general | solution.py:38
  115.4 0.8 copy-done.11
  116.2 3.5 %convolution_convert_fusion = bf16[768,2048]{1,0:T(8,128)(2,1)} fusion(bf16[768,384]{1,0:T(8,128)(2,1)S(1)} %get-tuple-element.30, bf16[1,384,2048]{2,1,0:T(8,128)(2,1)S(1)} %copy-done), kind=kOutput, calls=%fused_computation.3 | convolution fusion | flops 1209532416 | bytes 5308416 | tf_op jit(solution)/shard_map/dot_general | solution.py:24
  119.7 0.0 reduce-scatter.3.cloned.1.call-update
  119.7 0.0 reduce-scatter.5.cloned.1.call-start
  119.8 0.0 copy-start.3
  119.8 0.0 copy-start.6
  119.8 3.0 %fusion.9 = f32[768,2048]{1,0:T(8,128)S(1)} fusion(bf16[768,384]{1,0:T(8,128)(2,1)} %get-tuple-element.29, bf16[1,2048,384]{2,1,0:T(8,128)(2,1)S(1)} %copy-done.2), kind=kOutput, calls=%fused_computation.20 | convolution fusion | flops 1207959552 | bytes 8454144 | tf_op jit(solution)/shard_map/dot_general | solution.py:46
  122.9 3.5 %add_convert_fusion = bf16[768,2048]{1,0:T(8,128)(2,1)} fusion(f32[768,2048]{1,0:T(8,128)S(1)} %fusion.9, bf16[768,384]{1,0:T(8,128)(2,1)S(1)} %copy-done.6, bf16[1,2048,384]{2,1,0:T(8,128)(2,1)S(1)} %copy-done.3), kind=kOutput, calls=%fused_computation.2 | convolution fusion | flops 1211105280 | bytes 11599872 | tf_op jit(solution)/shard_map/dot_general | solution.py:49
  126.3 0.0 reduce-scatter.5.cloned.1.call-update
  126.3 5.6 %reduce-scatter.3.cloned.1.call-done = bf16[768,1024]{1,0:T(8,128)(2,1)} async-done(((bf16[768,2048]{1,0:T(8,128)(2,1)}), bf16[768,1024]{1,0:T(8,128)(2,1)}) %reduce-scatter.3.cloned.1.call-update) | async-done | bytes 1572880 | tf_op jit(solution)/shard_map/reduce_scatter | solution.py:25
  132.0 5.5 %all-to-all-start.1 = ((bf16[8,96,1024]{2,1,0:T(8,128)(2,1)}), bf16[8,96,1024]{2,1,0:T(8,128)(2,1)S(1)}, u32[]{:S(2)}, u32[]{:S(2)}) async-start(bf16[8,96,1024]{2,1,0:T(8,128)(2,1)} %bitcast.58), calls=%async_computation.2 | async-start | bytes 3145728 | tf_op jit(solution)/shard_map/all_to_all | solution.py:92
  137.4 8.8 %reduce-scatter.5.cloned.1.call-done = bf16[768,1024]{1,0:T(8,128)(2,1)} async-done(((bf16[768,2048]{1,0:T(8,128)(2,1)}), bf16[768,1024]{1,0:T(8,128)(2,1)}) %reduce-scatter.5.cloned.1.call-update) | async-done | bytes 1572880 | tf_op jit(solution)/shard_map/reduce_scatter | solution.py:52
  146.2 26.5 %all-to-all-done.1 = bf16[8,96,1024]{2,1,0:T(8,128)(2,1)S(1)} async-done(((bf16[8,96,1024]{2,1,0:T(8,128)(2,1)}), bf16[8,96,1024]{2,1,0:T(8,128)(2,1)S(1)}, u32[]{:S(2)}, u32[]{:S(2)}) %all-to-all-start.1) | async-done | bytes 1572896 | tf_op jit(solution)/shard_map/all_to_all | solution.py:92
  172.7 1.1 copy-done.1
  173.9 5.5 %all-to-all-start.3 = ((bf16[8,96,1024]{2,1,0:T(8,128)(2,1)}), bf16[8,96,1024]{2,1,0:T(8,128)(2,1)S(1)}, u32[]{:S(2)}, u32[]{:S(2)}) async-start(bf16[8,96,1024]{2,1,0:T(8,128)(2,1)} %bitcast.57), calls=%async_computation.5 | async-start | bytes 3145728 | tf_op jit(solution)/shard_map/all_to_all | solution.py:97
  179.4 0.1 copy.36
  179.5 0.8 convert_element_type.63
  180.4 0.1 copy.40
  180.5 0.1 reshape.79
  180.6 0.0 copy-start.7
  180.6 4.8 %fusion.2 = bf16[1,384,2048]{2,1,0:T(8,128)(2,1)} fusion(bf16[768,384]{1,0:T(8,128)(2,1)} %copy-done.11, bf16[768,2048]{1,0:T(8,128)(2,1)} %bitcast.64), kind=kOutput, calls=%fused_computation.9 | convolution fusion | flops 1208745984 | bytes 5308416 | tf_op jit(solution)/shard_map/dot_general | solution.py:56
  185.4 0.0 copy-done.10
  185.4 3.0 %fusion.1 = bf16[1,2048,384]{2,1,0:T(8,128)(2,1)} fusion(bf16[768,2048]{1,0:T(8,128)(2,1)S(1)} %bitcast.61, bf16[768,384]{1,0:T(8,128)(2,1)S(1)} %copy-done.7), kind=kOutput, calls=%fused_computation.8 | convolution fusion | flops 1208745984 | bytes 5308416 | tf_op jit(solution)/shard_map/dot_general | solution.py:62
  188.4 3.0 %fusion = bf16[1,2048,384]{2,1,0:T(8,128)(2,1)} fusion(bf16[768,2048]{1,0:T(8,128)(2,1)S(1)} %bitcast.62, bf16[768,384]{1,0:T(8,128)(2,1)S(1)} %copy-done.5), kind=kOutput, calls=%fused_computation.7 | convolution fusion | flops 1208745984 | bytes 5308416 | tf_op jit(solution)/shard_map/dot_general | solution.py:59
  191.5 5.1 %gather_fusion = bf16[512,1024]{1,0:T(8,128)(2,1)} fusion(bf16[768,1024]{1,0:T(8,128)(2,1)} %bitcast.54, s32[1024]{0:T(1024)S(1)} %pad_clamp_fusion), kind=kCustom, calls=%fused_computation | custom fusion | bytes 2099200 | tf_op jit(solution)/shard_map/gather | solution.py:98
  196.6 2.7 %reshape.97 = f32[128,4,1024]{2,1,0:T(4,128)} reshape(bf16[512,1024]{1,0:T(8,128)(2,1)} %gather_fusion) | data formatting | bytes 3145728 | tf_op jit(solution)/shard_map/convert_element_type | solution.py:98
  199.3 4.2 %multiply_reduce_fusion = (f32[128,4]{1,0:T(8,128)S(1)}, bf16[128,1024]{1,0:T(8,128)(2,1)}) fusion(f32[128,4,1024]{2,1,0:T(4,128)} %reshape.97, f32[128,1024]{1,0:T(8,128)} %convert_element_type.63, f32[128,4]{1,0:T(8,128)S(1)} %copy.36), kind=kLoop, calls=%fused_computation.10 | loop fusion | flops 1965568 | bytes 2887680 | tf_op jit(solution)/shard_map/reduce_sum | solution.py:100
  203.6 4.4 %psum.7 = f32[128,4]{1,0:T(8,128)S(1)} all-reduce(f32[128,4]{1,0:T(8,128)S(1)} %get-tuple-element.24), channel_id=1, replica_groups=mesh['group'=2,'expert'=8,'tensor'=2] {'tensor'}, use_global_device_ids=true, to_apply=%region_10.11 | all-reduce | flops 512 | bytes 4096 | tf_op jit(solution)/shard_map/psum | solution.py:101
  208.0 0.7 copy.41
  208.7 6.1 %all-to-all-done.3 = bf16[8,96,1024]{2,1,0:T(8,128)(2,1)S(1)} async-done(((bf16[8,96,1024]{2,1,0:T(8,128)(2,1)}), bf16[8,96,1024]{2,1,0:T(8,128)(2,1)S(1)}, u32[]{:S(2)}, u32[]{:S(2)}) %all-to-all-start.3) | async-done | bytes 1572896 | tf_op jit(solution)/shard_map/all_to_all | solution.py:97
  214.7 2.8 %gather_fusion.1 = bf16[512,1024]{1,0:T(8,128)(2,1)} fusion(bf16[768,1024]{1,0:T(8,128)(2,1)S(1)} %bitcast.53, s32[1024]{0:T(1024)S(1)} %pad_clamp_fusion), kind=kCustom, calls=%fused_computation.1 | custom fusion | bytes 2099200 | tf_op jit(solution)/shard_map/gather | solution.py:102
  217.5 1.5 reshape.90
  219.0 2.1 reduce_sum.64
  (17 shorter events, 0.1 us)
Async XLA Ops:
  7.2 102.5 %copy-start = (bf16[1,384,2048]{2,1,0:T(8,128)(2,1)S(1)}, bf16[1,384,2048]{2,1,0:T(8,128)(2,1)}, u32[]{:S(2)}) copy-start(bf16[1,384,2048]{2,1,0:T(8,128)(2,1)} %param.12) | copy-start | bytes 4718596
  7.2 88.6 %all-gather.3.cloned.1.call-start = ((), (), s32[]{:S(2)}) async-start(), calls=%async_computation.6 | async-start | bytes 4718592 | tf_op jit(solution)/shard_map/all_gather | solution.py:19
  53.2 0.7 copy-start.8
  53.2 1.0 copy-start.4
  53.3 56.4 %all-gather.5.cloned.1.call-start = ((), (), s32[]{:S(2)}) async-start(), calls=%async_computation.8 | async-start | bytes 4718592 | tf_op jit(solution)/shard_map/all_gather | solution.py:36
  95.7 36.3 %reduce-scatter.3.cloned.1.call-start = ((), (), s32[]{:S(2)}) async-start(), calls=%async_computation.7 | async-start | bytes 4718592 | tf_op jit(solution)/shard_map/reduce_scatter | solution.py:25
  95.8 5.3 %copy-start.2 = (bf16[1,2048,384]{2,1,0:T(8,128)(2,1)S(1)}, bf16[1,2048,384]{2,1,0:T(8,128)(2,1)}, u32[]{:S(2)}) copy-start(bf16[1,2048,384]{2,1,0:T(8,128)(2,1)} %param.10) | copy-start | bytes 4718596
  95.8 5.3 %copy-start.9 = (bf16[8,96,2048]{2,1,0:T(8,128)(2,1)S(1)}, bf16[8,96,2048]{2,1,0:T(8,128)(2,1)}, u32[]{:S(2)}) copy-start(bf16[8,96,2048]{2,1,0:T(8,128)(2,1)} %all-gather.3.cloned.1.call-done) | copy-start | bytes 9437188
  115.4 0.8 copy-start.11
  119.7 26.5 %reduce-scatter.5.cloned.1.call-start = ((), (), s32[]{:S(2)}) async-start(), calls=%async_computation.9 | async-start | bytes 4718592 | tf_op jit(solution)/shard_map/reduce_scatter | solution.py:52
  119.8 3.1 %copy-start.3 = (bf16[1,2048,384]{2,1,0:T(8,128)(2,1)S(1)}, bf16[1,2048,384]{2,1,0:T(8,128)(2,1)}, u32[]{:S(2)}) copy-start(bf16[1,2048,384]{2,1,0:T(8,128)(2,1)} %param.11) | copy-start | bytes 4718596
  119.8 3.1 %copy-start.6 = (bf16[768,384]{1,0:T(8,128)(2,1)S(1)}, bf16[768,384]{1,0:T(8,128)(2,1)}, u32[]{:S(2)}) copy-start(bf16[768,384]{1,0:T(8,128)(2,1)} %get-tuple-element.28) | copy-start | bytes 1769476
  132.0 40.8 %all-to-all-start.1 = ((bf16[8,96,1024]{2,1,0:T(8,128)(2,1)}), bf16[8,96,1024]{2,1,0:T(8,128)(2,1)S(1)}, u32[]{:S(2)}, u32[]{:S(2)}) async-start(bf16[8,96,1024]{2,1,0:T(8,128)(2,1)} %bitcast.58), calls=%async_computation.2 | async-start | bytes 3145728 | tf_op jit(solution)/shard_map/all_to_all | solution.py:92
  172.7 1.1 copy-start.1
  173.9 40.8 %all-to-all-start.3 = ((bf16[8,96,1024]{2,1,0:T(8,128)(2,1)}), bf16[8,96,1024]{2,1,0:T(8,128)(2,1)S(1)}, u32[]{:S(2)}, u32[]{:S(2)}) async-start(bf16[8,96,1024]{2,1,0:T(8,128)(2,1)} %bitcast.57), calls=%async_computation.5 | async-start | bytes 3145728 | tf_op jit(solution)/shard_map/all_to_all | solution.py:97
  180.6 4.8 %copy-start.7 = (bf16[768,384]{1,0:T(8,128)(2,1)S(1)}, bf16[768,384]{1,0:T(8,128)(2,1)}, u32[]{:S(2)}) copy-start(bf16[768,384]{1,0:T(8,128)(2,1)} %get-tuple-element.28) | copy-start | bytes 1769476
  180.6 4.8 %copy-start.10 = (bf16[8,96,2048]{2,1,0:T(8,128)(2,1)S(1)}, bf16[8,96,2048]{2,1,0:T(8,128)(2,1)}, u32[]{:S(2)}) copy-start(bf16[8,96,2048]{2,1,0:T(8,128)(2,1)} %all-gather.3.cloned.1.call-done) | copy-start | bytes 9437188
  185.4 3.0 %copy-start.5 = (bf16[768,384]{1,0:T(8,128)(2,1)S(1)}, bf16[768,384]{1,0:T(8,128)(2,1)}, u32[]{:S(2)}) copy-start(bf16[768,384]{1,0:T(8,128)(2,1)} %get-tuple-element.29) | copy-start | bytes 1769476
Sparse Core Ops, SparseCore 0:
  53.4 13.7 all-gather.2
  95.8 13.7 all-gather.4
  119.8 12.0 reduce-scatter.2
  134.1 12.0 reduce-scatter.4
where the time goes:
time: 231 us; the launch traced here: 228 us
  blocking collectives  85.3 us (37%)
  waiting for transfers between devices  52.8 us (23%)
  matrix products  37.6 us (16%)
  local copies, waits for them, and re-layouts  17.3 us (7%)
  between operations  13.9 us (6%)
  starting transfers between devices  11.2 us (5%)
  other arithmetic  9.55 us (4%)
    all_to_all x1, blocking collectives, per_device(): lax.all_to_all(sent_rows, 'expert', split_axis=0, concat_axis=0, tiled=True)  40.8 us
    all_to_all x1, blocking collectives, per_device(): lax.all_to_all(sent_grads, 'expert', split_axis=0, concat_axis=0, tiled=T...  40.1 us
    all_to_all x1, waiting for transfers between devices, per_device(): lax.all_to_all(results, 'expert', split_axis=0, concat_axis=0, tiled=True)  26.5 us
    reduce_scatter x1, waiting for transfers between devices, expert_backward(): lax.psum_scatter(partial_in.astype(jnp.bfloat16), 'tensor', scatter_dimen...  8.79 us
    all_to_all x1, waiting for transfers between devices, per_device(): lax.all_to_all(returned, 'expert', split_axis=0, concat_axis=0, tiled=True)  6.06 us
    dot_general x1, matrix products, expert_backward(): lax.dot_general(grad_whole, down_local, contract_last, preferred_element_...  5.75 us
    all_gather x1, waiting for transfers between devices, expert_backward(): grad_whole = lax.all_gather(arrived, 'tensor', axis=2, tiled=True)  5.73 us
    reduce_scatter x1, waiting for transfers between devices, expert_forward(): lax.psum_scatter(partial_out.astype(jnp.bfloat16), 'tensor', scatter_dime...  5.61 us
  transfers between devices with their start and end apart: 6, of which 5 were waited for; matrix products, arithmetic and copies ran while one was open for 18% of the time, Pallas kernels for 0%

commit v1 on v0

v1 whole, which is shorter than its diff:
```python
import jax
import jax.numpy as jnp
from jax import lax
from jax.sharding import PartitionSpec as P

BF = jnp.bfloat16
F32 = jnp.float32


def dot(a, b, contract):
    return lax.dot_general(a, b, (contract, ((), ())), preferred_element_type=F32)


def split_three(values):
    high = lax.reduce_precision(values, 8, 7)
    rest = values - high
    middle = lax.reduce_precision(rest, 8, 7)
    low = rest - middle
    return [part.astype(BF) for part in (high, middle, low)]


def per_device(tokens, expert_ids, router_weights, gate_weight, up_weight, down_weight, grad_out):
    token_count, half_width = tokens.shape
    top_count = expert_ids.shape[1]
    experts = lax.axis_size("expert")
    capacity = min(token_count, 3 * token_count * top_count // (2 * experts))
    lines = experts // 2
    mine = lax.axis_index("expert")
    core = lax.axis_index("tensor")
    peer = mine + 1 - 2 * (mine % 2)

    def over_pair(x):
        return lax.ppermute(x, "expert", [(i, i + 1 - 2 * (i % 2)) for i in range(experts)])

    def over_line(x, k):
        return lax.ppermute(
            x, "expert",
            [(i, ((i // 2 + k) % lines) * 2 + i % 2) for i in range(experts)],
        )

    def over_core(x):
        return lax.ppermute(x, "tensor", [(0, 1), (1, 0)])

    chosen = expert_ids[:, :, None] == jnp.arange(experts, dtype=jnp.int32)[None, None, :]
    table = jnp.sum(jnp.where(chosen, router_weights[:, :, None], 0.0), axis=1).T
    part_rows = experts * token_count // half_width
    parts = jnp.concatenate([p.reshape(part_rows, half_width) for p in split_three(table)])
    extra = -(-3 * part_rows // 16) * 16
    parts = jnp.pad(parts, ((0, extra - 3 * part_rows), (0, 0)))
    first = jnp.concatenate([tokens, parts])

    line_blocks = [first] + [over_line(first, k) for k in range(1, lines)]
    line_grads = [grad_out] + [over_line(grad_out, k) for k in range(1, lines)]

    dense_w, placings, sent_w = [], [], []
    for k in range(lines):
        rows = line_blocks[k][token_count:token_count + 3 * part_rows].astype(F32)
        rows = jnp.sum(rows.reshape(3, part_rows, half_width), axis=0)
        held = rows.reshape(experts, token_count)
        dense_w.append(lax.dynamic_index_in_dim(held, mine, 0, False))
        theirs = lax.dynamic_index_in_dim(held, peer, 0, False)
        named = theirs > 0.0
        rank = jnp.cumsum(named.astype(jnp.int32)) - 1
        picked = (jnp.arange(capacity, dtype=jnp.int32)[:, None] == rank[None, :]) & named[None, :]
        placings.append(picked)
        sent_w.append(jnp.sum(jnp.where(picked, theirs[None, :], 0.0), axis=1))
    pair_w = over_pair(jnp.stack(sent_w))
    places = [p.astype(BF) for p in placings]

    def packed(k, x):
        return dot(places[k], x, ((1,), (0,))).astype(BF)

    pair_blocks = [over_pair(packed(k, line_blocks[k][:token_count])) for k in range(lines)]
    pair_grads = [over_pair(packed(k, line_grads[k])) for k in range(lines)]

    def whole(dense, compact):
        held = jnp.concatenate([d[:token_count] for d in dense] + compact)
        other = over_core(held)
        lower = jnp.where(core == 0, held, other)
        upper = jnp.where(core == 0, other, held)
        return jnp.concatenate([lower, upper], axis=1)

    weights = jnp.concatenate(dense_w + [pair_w.reshape(-1)])[:, None]
    gate_local = gate_weight[0]
    up_local = up_weight[0]
    down_local = down_weight[0]
    rows = whole(line_blocks, pair_blocks)
    gate = dot(rows, gate_local, ((1,), (0,)))
    upward = dot(rows, up_local, ((1,), (0,)))
    sig = jax.nn.sigmoid(gate)
    hidden = gate * sig * upward
    scaled_hidden = (weights * hidden).astype(BF)

    def summed_over_cores(make):
        sent = over_core(make(1 - core).astype(BF))
        return make(core) + sent.astype(F32)

    def half_of(x, which, axis):
        return lax.dynamic_slice_in_dim(x, which * half_width, half_width, axis)

    dense_rows = lines * token_count

    def go_home(both):
        back = over_pair(both[dense_rows:].astype(BF))
        total = None
        for k in range(lines):
            block = both[k * token_count:(k + 1) * token_count]
            block = block + dot(places[k], back[k * capacity:(k + 1) * capacity], ((0,), (0,)))
            if k:
                block = over_line(block.astype(BF), lines - k).astype(F32)
            total = block if total is None else total + block
        return total.astype(BF)

    layer_out = go_home(summed_over_cores(
        lambda c: dot(scaled_hidden, half_of(down_local, c, 1), ((1,), (0,)))))

    grads = whole(line_grads, pair_grads)
    grad_plain = dot(grads, down_local, ((1,), (1,)))
    row_value = jnp.sum(hidden * grad_plain, axis=1)
    grad_hidden = weights * grad_plain
    grad_gate = (grad_hidden * upward * sig * (1.0 + gate * (1.0 - sig))).astype(BF)
    grad_up = (grad_hidden * gate * sig).astype(BF)
    input_grad = go_home(summed_over_cores(
        lambda c: dot(grad_gate, half_of(gate_local, c, 0), ((1,), (1,)))
        + dot(grad_up, half_of(up_local, c, 0), ((1,), (1,)))))

    down_grad = dot(scaled_hidden, grads, ((0,), (0,))).astype(BF)
    gate_grad = dot(rows, grad_gate, ((0,), (0,))).astype(BF)
    up_grad = dot(rows, grad_up, ((0,), (0,))).astype(BF)

    row_value = row_value + over_core(row_value)
    back_value = over_pair(row_value[dense_rows:])
    by_line = []
    for k in range(lines):
        own = row_value[k * token_count:(k + 1) * token_count]
        value = back_value[k * capacity:(k + 1) * capacity]
        value = jnp.sum(jnp.where(placings[k], value[:, None], 0.0), axis=0)
        both = jnp.stack([own, value])
        by_line.append(over_line(both, lines - k) if k else both)
    held = jnp.stack(by_line)
    ids_line = expert_ids // 2
    place = (ids_line - mine // 2) % lines
    is_peer = (expert_ids % 2) != (mine % 2)
    slot = place * 2 + is_peer.astype(jnp.int32)
    flat = held.reshape(experts, token_count)
    match = slot[:, :, None] == jnp.arange(experts, dtype=jnp.int32)[None, None, :]
    weight_grad = jnp.sum(jnp.where(match, flat.T[:, None, :], 0.0), axis=2)
    return (layer_out, input_grad, weight_grad, gate_grad[None], up_grad[None], down_grad[None])


def solution(mesh):
    in_specs = (
        P(("group", "expert"), "tensor"),
        P(("group", "expert"), None),
        P(("group", "expert"), None),
        P("expert", None, "tensor"),
        P("expert", None, "tensor"),
        P("expert", "tensor", None),
        P(("group", "expert"), "tensor"),
    )
    out_specs = (
        P(("group", "expert"), "tensor"),
        P(("group", "expert"), "tensor"),
        P(("group", "expert"), None),
        P(("group", "expert"), None, "tensor"),
        P(("group", "expert"), None, "tensor"),
        P(("group", "expert"), "tensor", None),
    )
    return jax.shard_map(
        per_device, mesh=mesh, in_specs=in_specs, out_specs=out_specs, check_vma=False
    )
```

time: 231 us -> 206 us (0.89)
  the two profiles are of different devices: /device:TPU:9 before, /device:TPU:0 now
where the time goes in v1:
time: 206 us; the launch traced here: 205 us
  waiting for transfers between devices  70.4 us (34%)
  starting transfers between devices  51.4 us (25%)
  matrix products  39.2 us (19%)
  local copies, waits for them, and re-layouts  25.9 us (13%)
  other arithmetic  16.3 us (8%)
    ppermute x12, waiting for transfers between devices, over_pair(): lax.ppermute(x, 'expert', [(i, i + 1 - 2 * (i % 2)) for i in range(expert...  42.3 us
    dot_general x28, matrix products, dot(): lax.dot_general(a, b, (contract, ((), ())), preferred_element_type=F32)  39.2 us
    ppermute x15, starting transfers between devices, over_line(): lax.ppermute(x, 'expert', [(i, (i // 2 + k) % lines * 2 + i % 2) for i in...  37.6 us
    ppermute x15, waiting for transfers between devices, over_line(): lax.ppermute(x, 'expert', [(i, (i // 2 + k) % lines * 2 + i % 2) for i in...  28 us
    unnamed x69, local copies, waits for them, and re-layouts  20.8 us
    ppermute x12, starting transfers between devices, over_pair(): lax.ppermute(x, 'expert', [(i, i + 1 - 2 * (i % 2)) for i in range(expert...  12.7 us
    select_n x2, other arithmetic, whole(): lower = jnp.where(core == 0, held, other)  4.65 us
  transfers between devices with their start and end apart: 32, of which 11 were waited for; matrix products, arithmetic and copies ran while one was open for 35% of the time, Pallas kernels for 0%

profile of v1, /device:TPU:0, one launch (start us, length us, event | category | flops | bytes accessed | tf_op | source)
XLA Modules:
  0.0 204.6 jit_solution(16880965079199088745)
XLA Ops:
  0.7 5.1 %collective-permute-start.16 = (bf16[128,1024]{1,0:T(8,128)(2,1)}, bf16[128,1024]{1,0:T(8,128)(2,1)}, u32[]{:S(2)}, u32[]{:S(2)}) collective-permute-start(bf16[128,1024]{1,0:T(8,128)(2,1)} %param.13), channel_id=1, source_target_pairs={{0,12},{2,14},{4,0},{6,2},{8,4},{10,6},{12,8},{14,10},{1,13},{3,15... | collective-permute-start | bytes 786440 | tf_op jit(solution)/shard_map/ppermute | solution.py:36
  5.8 1.0 collective-permute-start.14
  7.5 1.7 pad_maximum_fusion.4
  9.2 2.8 %collective-permute-start.2 = (bf16[144,1024]{1,0:T(8,128)(2,1)}, bf16[144,1024]{1,0:T(8,128)(2,1)}, u32[]{:S(2)}, u32[]{:S(2)}) collective-permute-start(bf16[144,1024]{1,0:T(8,128)(2,1)} %pad_maximum_fusion.4), channel_id=1, source_target_pairs={{0,12},{2,14},{4,0},{6,2},{8,4},{10,6},{12,8},{14,10},{1,13},{3,15... | collective-permute-start | bytes 884744 | tf_op jit(solution)/shard_map/ppermute | solution.py:36
  12.0 1.1 collective-permute-start.1
  13.7 1.8 convolution_convert_fusion.7
  15.5 1.8 convolution_convert_fusion.11
  17.9 1.0 constant_dynamic-update-slice_fusion.5
  18.9 1.7 constant_dynamic-update-slice_fusion.13
  21.1 4.0 %collective-permute-done.14 = bf16[128,1024]{1,0:T(8,128)(2,1)} collective-permute-done((bf16[128,1024]{1,0:T(8,128)(2,1)}, bf16[128,1024]{1,0:T(8,128)(2,1)}, u32[]{:S(2)}, u32[]{:S(2)}) %collective-permute-start.14) | collective-permute-done | bytes 262176 | tf_op jit(solution)/shard_map/ppermute | solution.py:36
  25.1 17.7 %collective-permute-start = (bf16[144,1024]{1,0:T(8,128)(2,1)}, bf16[144,1024]{1,0:T(8,128)(2,1)}, u32[]{:S(2)}, u32[]{:S(2)}) collective-permute-start(bf16[144,1024]{1,0:T(8,128)(2,1)} %pad_maximum_fusion.4), channel_id=1, source_target_pairs={{0,4},{2,6},{4,8},{6,10},{8,12},{10,14},{12,0},{14,2},{1,5},{3,7},... | collective-permute-start | bytes 884744 | tf_op jit(solution)/shard_map/ppermute | solution.py:36
  42.8 1.7 constant_dynamic-update-slice_fusion.12
  44.5 1.5 collective-permute-start.4
  46.0 1.7 constant_dynamic-update-slice_fusion.11
  48.2 1.7 constant_dynamic-update-slice_fusion.10
  49.8 0.7 convert_reduce_fusion
  51.4 1.8 convolution_convert_fusion.8
  53.3 1.5 collective-permute-start.7
  56.5 1.8 convolution_convert_fusion.9
  60.6 1.2 convolution_convert_fusion.10
  61.8 1.6 collective-permute-start.5
  63.4 1.0 slice_dynamic-update-slice_fusion.2
  64.3 1.0 slice_dynamic-update-slice_fusion.1
  65.3 1.0 slice_dynamic-update-slice_fusion
  66.3 0.9 constant_dynamic-update-slice_fusion.4
  67.3 1.2 collective-permute-done.5
  68.5 0.9 constant_dynamic-update-slice_fusion.2
  69.5 0.9 constant_dynamic-update-slice_fusion.1
  70.5 1.6 constant_dynamic-update-slice_fusion.9
  72.1 1.1 convolution_convert_fusion.5
  74.0 1.1 convolution_convert_fusion.6
  75.1 1.5 collective-permute-start.18
  76.6 1.1 convolution_convert_fusion.4
  78.4 6.8 %collective-permute-done.18 = bf16[96,1024]{1,0:T(8,128)(2,1)S(1)} collective-permute-done((bf16[96,1024]{1,0:T(8,128)(2,1)S(1)}, bf16[96,1024]{1,0:T(8,128)(2,1)S(1)}, u32[]{:S(2)}, u32[]{:S(2)}) %collective-permute-start.18) | collective-permute-done | bytes 196640 | tf_op jit(solution)/shard_map/ppermute | solution.py:33
  86.6 2.4 %collective-permute-done.20 = bf16[96,1024]{1,0:T(8,128)(2,1)S(1)} collective-permute-done((bf16[96,1024]{1,0:T(8,128)(2,1)S(1)}, bf16[96,1024]{1,0:T(8,128)(2,1)S(1)}, u32[]{:S(2)}, u32[]{:S(2)}) %collective-permute-start.20) | collective-permute-done | bytes 196640 | tf_op jit(solution)/shard_map/ppermute | solution.py:33
  93.9 1.9 broadcast_select_fusion.3
  95.8 1.8 fusion.5
  98.4 1.8 fusion.7
  100.3 2.8 %broadcast_select_fusion.1 = (bf16[896,1024]{1,0:T(8,128)(2,1)S(1)}, bf16[896,1024]{1,0:T(8,128)(2,1)S(1)}) fusion(bf16[896,1024]{1,0:T(8,128)(2,1)} %constant_dynamic-update-slice_fusion.6, bf16[896,1024]{1,0:T(8,128)(2,1)} %collective-permute-done.21, pred[]{:T(512)S(6)} %eq.105), kind=kLoop, calls=%fused_computation.13 | loop fusion | flops 1835008 | bytes 7340033 | tf_op jit(solution)/shard_map/jit(_where)/select_n | solution.py:79
  103.1 3.0 %multiply_reduce_fusion = (f32[896]{0:T(1024)S(1)}, f32[896,384]{0,1:T(8,128)}) fusion(f32[896,384]{0,1:T(8,128)S(1)} %fusion.5, f32[896,384]{0,1:T(8,128)S(1)} %fusion.7, bf16[1,384,2048]{2,1,0:T(8,128)(2,1)S(1)} %copy-done, bf16[896,1024]{1,0:T(8,128)(2,1)S(1)} %get-tuple-element.17, bf16[896,1024]{1,0:T(8,128)(2,1)S(1)} %get-tuple-element.16), kind=kOutput, calls=%fused_computation.24 | convolution fusion | flops 1419033728 | bytes 9375232 | tf_op jit(solution)/shard_map/dot_general | solution.py:11
  108.1 2.9 %collective-permute-done.28 = f32[384]{0:T(512)S(1)} collective-permute-done((f32[384]{0:T(512)S(1)}, f32[384]{0:T(512)S(1)}, u32[]{:S(2)}, u32[]{:S(2)}) %collective-permute-start.28) | collective-permute-done | bytes 1568 | tf_op jit(solution)/shard_map/ppermute | solution.py:33
  111.5 3.3 %collective-permute-start.30 = (f32[2,128]{1,0:T(2,128)S(1)}, f32[2,128]{1,0:T(2,128)S(1)}, u32[]{:S(2)}, u32[]{:S(2)}) collective-permute-start(f32[2,128]{1,0:T(2,128)S(1)} %pad_maximum_fusion.8), channel_id=1, source_target_pairs={{0,8},{2,10},{4,12},{6,14},{8,0},{10,2},{12,4},{14,6},{1,9},{3,11}... | collective-permute-start | bytes 3080 | tf_op jit(solution)/shard_map/ppermute | solution.py:36
  115.0 1.4 collective-permute-start.3
  116.5 2.2 %collective-permute-done.3 = f32[4,96]{1,0:T(4,128)S(1)} collective-permute-done((f32[4,96]{1,0:T(4,128)S(1)}, f32[4,96]{1,0:T(4,128)S(1)}, u32[]{:S(2)}, u32[]{:S(2)}) %collective-permute-start.3) | collective-permute-done | bytes 1568 | tf_op jit(solution)/shard_map/ppermute | solution.py:33
  118.8 3.0 %multiply_convert_fusion = (bf16[896,384]{0,1:T(8,128)(2,1)S(1)}, bf16[896,384]{0,1:T(8,128)(2,1)S(1)}, bf16[896,384]{0,1:T(8,128)(2,1)S(1)}) fusion(f32[896,384]{0,1:T(8,128)} %copy-done.12, f32[896,384]{0,1:T(8,128)} %get-tuple-element.41, f32[896]{0:T(1024)S(1)} %constant_dynamic-update-slice_fusion.14, f32[896,384]{0,1:T(8,128)} %copy-done.11), kind=kLoop, calls=%fused_computation.25 | loop fusion | flops 6193152 | bytes 6196736 | tf_op jit(solution)/shard_map/convert_element_type | solution.py:122
  121.8 1.1 convolution_convert_fusion.3
  123.2 1.2 fusion.10
  124.6 1.2 add_convert_fusion
  126.8 1.2 fusion.13
  128.9 3.4 %fusion.1 = bf16[1,2048,384]{2,1,0:T(8,128)(2,1)} fusion(bf16[896,384]{0,1:T(8,128)(2,1)S(1)} %get-tuple-element.18, bf16[896,1024]{1,0:T(8,128)(2,1)S(1)} %copy-done.6, bf16[896,1024]{1,0:T(8,128)(2,1)S(1)} %copy-done.4), kind=kOutput, calls=%fused_computation.9 | convolution fusion | flops 1417412608 | bytes 5931008 | tf_op jit(solution)/shard_map/dot_general | solution.py:11
  132.3 3.4 %fusion = bf16[1,2048,384]{2,1,0:T(8,128)(2,1)} fusion(bf16[896,384]{0,1:T(8,128)(2,1)S(1)} %get-tuple-element.19, bf16[896,1024]{1,0:T(8,128)(2,1)S(1)} %copy-done.6, bf16[896,1024]{1,0:T(8,128)(2,1)S(1)} %copy-done.4), kind=kOutput, calls=%fused_computation.8 | convolution fusion | flops 1417412608 | bytes 5931008 | tf_op jit(solution)/shard_map/dot_general | solution.py:11
  135.7 1.1 convert_add_fusion.1
  137.0 1.4 collective-permute-start.10
  138.4 1.2 convert_add_fusion
  140.4 3.2 %fusion.2 = bf16[1,384,2048]{2,1,0:T(8,128)(2,1)} fusion(bf16[896,384]{0,1:T(8,128)(2,1)S(1)} %get-tuple-element.20, bf16[896,1024]{1,0:T(8,128)(2,1)S(1)} %copy-done.2, bf16[896,1024]{1,0:T(8,128)(2,1)S(1)} %get-tuple-element.16), kind=kOutput, calls=%fused_computation.10 | convolution fusion | flops 1417412608 | bytes 5931008 | tf_op jit(solution)/shard_map/dot_general | solution.py:11
  143.6 13.8 %collective-permute-done.10 = bf16[384,1024]{1,0:T(8,128)(2,1)S(1)} collective-permute-done((bf16[384,1024]{1,0:T(8,128)(2,1)S(1)}, bf16[384,1024]{1,0:T(8,128)(2,1)S(1)}, u32[]{:S(2)}, u32[]{:S(2)}) %collective-permute-start.10) | collective-permute-done | bytes 786464 | tf_op jit(solution)/shard_map/ppermute | solution.py:33
  157.7 1.7 collective-permute-start.11
  160.6 12.9 %collective-permute-done.23 = bf16[384,1024]{1,0:T(8,128)(2,1)S(1)} collective-permute-done((bf16[384,1024]{1,0:T(8,128)(2,1)S(1)}, bf16[384,1024]{1,0:T(8,128)(2,1)S(1)}, u32[]{:S(2)}, u32[]{:S(2)}) %collective-permute-start.23) | collective-permute-done | bytes 786464 | tf_op jit(solution)/shard_map/ppermute | solution.py:33
  173.8 1.7 collective-permute-start.24
  176.2 2.3 %collective-permute-start.26 = (bf16[128,1024]{1,0:T(8,128)(2,1)S(1)}, bf16[128,1024]{1,0:T(8,128)(2,1)S(1)}, u32[]{:S(2)}, u32[]{:S(2)}) collective-permute-start(bf16[128,1024]{1,0:T(8,128)(2,1)S(1)} %fusion.26), channel_id=1, source_target_pairs={{0,4},{2,6},{4,8},{6,10},{8,12},{10,14},{12,0},{14,2},{1,5},{3,7},... | collective-permute-start | bytes 786440 | tf_op jit(solution)/shard_map/ppermute | solution.py:36
  178.5 16.3 %collective-permute-done.12 = bf16[128,1024]{1,0:T(8,128)(2,1)S(1)} collective-permute-done((bf16[128,1024]{1,0:T(8,128)(2,1)S(1)}, bf16[128,1024]{1,0:T(8,128)(2,1)S(1)}, u32[]{:S(2)}, u32[]{:S(2)}) %collective-permute-start.12) | collective-permute-done | bytes 262176 | tf_op jit(solution)/shard_map/ppermute | solution.py:36
  194.8 1.0 fusion.39
  195.8 7.7 %collective-permute-done.25 = bf16[128,1024]{1,0:T(8,128)(2,1)S(1)} collective-permute-done((bf16[128,1024]{1,0:T(8,128)(2,1)S(1)}, bf16[128,1024]{1,0:T(8,128)(2,1)S(1)}, u32[]{:S(2)}, u32[]{:S(2)}) %collective-permute-start.25) | collective-permute-done | bytes 262176 | tf_op jit(solution)/shard_map/ppermute | solution.py:36
  203.6 1.0 fusion.32
  (155 shorter events, 24.8 us)
Async XLA Ops:
  0.6 102.5 %copy-start = (bf16[1,384,2048]{2,1,0:T(8,128)(2,1)S(1)}, bf16[1,384,2048]{2,1,0:T(8,128)(2,1)}, u32[]{:S(2)}) copy-start(bf16[1,384,2048]{2,1,0:T(8,128)(2,1)} %param.12) | copy-start | bytes 4718596
  0.6 16.7 %copy-start.17 = (s32[128,4]{0,1:T(4,128)S(1)}, s32[128,4]{0,1:T(4,128)}, u32[]{:S(2)}) copy-start(s32[128,4]{0,1:T(4,128)} %param.8) | copy-start | bytes 6148
  0.7 47.0 %collective-permute-start.16 = (bf16[128,1024]{1,0:T(8,128)(2,1)}, bf16[128,1024]{1,0:T(8,128)(2,1)}, u32[]{:S(2)}, u32[]{:S(2)}) collective-permute-start(bf16[128,1024]{1,0:T(8,128)(2,1)} %param.13), channel_id=1, source_target_pairs={{0,12},{2,14},{4,0},{6,2},{8,4},{10,6},{12,8},{14,10},{1,13},{3,15... | collective-permute-start | bytes 786440 | tf_op jit(solution)/shard_map/ppermute | solution.py:36
  5.8 38.7 %collective-permute-start.15 = (bf16[128,1024]{1,0:T(8,128)(2,1)}, bf16[128,1024]{1,0:T(8,128)(2,1)}, u32[]{:S(2)}, u32[]{:S(2)}) collective-permute-start(bf16[128,1024]{1,0:T(8,128)(2,1)} %param.13), channel_id=1, source_target_pairs={{0,8},{2,10},{4,12},{6,14},{8,0},{10,2},{12,4},{14,6},{1,9},{3,11}... | collective-permute-start | bytes 786440 | tf_op jit(solution)/shard_map/ppermute | solution.py:36
  5.8 19.3 %collective-permute-start.14 = (bf16[128,1024]{1,0:T(8,128)(2,1)}, bf16[128,1024]{1,0:T(8,128)(2,1)}, u32[]{:S(2)}, u32[]{:S(2)}) collective-permute-start(bf16[128,1024]{1,0:T(8,128)(2,1)} %param.13), channel_id=1, source_target_pairs={{0,4},{2,6},{4,8},{6,10},{8,12},{10,14},{12,0},{14,2},{1,5},{3,7},... | collective-permute-start | bytes 786440 | tf_op jit(solution)/shard_map/ppermute | solution.py:36
  9.2 40.6 %collective-permute-start.2 = (bf16[144,1024]{1,0:T(8,128)(2,1)}, bf16[144,1024]{1,0:T(8,128)(2,1)}, u32[]{:S(2)}, u32[]{:S(2)}) collective-permute-start(bf16[144,1024]{1,0:T(8,128)(2,1)} %pad_maximum_fusion.4), channel_id=1, source_target_pairs={{0,12},{2,14},{4,0},{6,2},{8,4},{10,6},{12,8},{14,10},{1,13},{3,15... | collective-permute-start | bytes 884744 | tf_op jit(solution)/shard_map/ppermute | solution.py:36
  12.0 42.7 %collective-permute-start.1 = (bf16[144,1024]{1,0:T(8,128)(2,1)}, bf16[144,1024]{1,0:T(8,128)(2,1)}, u32[]{:S(2)}, u32[]{:S(2)}) collective-permute-start(bf16[144,1024]{1,0:T(8,128)(2,1)} %pad_maximum_fusion.4), channel_id=1, source_target_pairs={{0,8},{2,10},{4,12},{6,14},{8,0},{10,2},{12,4},{14,6},{1,9},{3,11}... | collective-permute-start | bytes 884744 | tf_op jit(solution)/shard_map/ppermute | solution.py:36
  13.2 36.6 %copy-start.22 = (f32[1024]{0:T(1024)}, f32[1024]{0:T(1024)S(1)}, u32[]{:S(2)}) copy-start(f32[1024]{0:T(1024)S(1)} %fusion.132) | copy-start | bytes 12292
  25.1 33.8 %collective-permute-start = (bf16[144,1024]{1,0:T(8,128)(2,1)}, bf16[144,1024]{1,0:T(8,128)(2,1)}, u32[]{:S(2)}, u32[]{:S(2)}) collective-permute-start(bf16[144,1024]{1,0:T(8,128)(2,1)} %pad_maximum_fusion.4), channel_id=1, source_target_pairs={{0,4},{2,6},{4,8},{6,10},{8,12},{10,14},{12,0},{14,2},{1,5},{3,7},... | collective-permute-start | bytes 884744 | tf_op jit(solution)/shard_map/ppermute | solution.py:36
  44.5 21.8 %collective-permute-start.4 = (bf16[96,1024]{1,0:T(8,128)(2,1)}, bf16[96,1024]{1,0:T(8,128)(2,1)}, u32[]{:S(2)}, u32[]{:S(2)}) collective-permute-start(bf16[96,1024]{1,0:T(8,128)(2,1)} %convolution_convert_fusion.11), channel_id=1, source_target_pairs={{0,2},{2,0},{4,6},{6,4},{8,10},{10,8},{12,14},{14,12},{1,3},{3,1},... | collective-permute-start | bytes 589832 | tf_op jit(solution)/shard_map/ppermute | solution.py:33
  47.7 22.8 %collective-permute-start.17 = (bf16[96,1024]{1,0:T(8,128)(2,1)}, bf16[96,1024]{1,0:T(8,128)(2,1)}, u32[]{:S(2)}, u32[]{:S(2)}) collective-permute-start(bf16[96,1024]{1,0:T(8,128)(2,1)} %convolution_convert_fusion.7), channel_id=1, source_target_pairs={{0,2},{2,0},{4,6},{6,4},{8,10},{10,8},{12,14},{14,12},{1,3},{3,1},... | collective-permute-start | bytes 589832 | tf_op jit(solution)/shard_map/ppermute | solution.py:33
  50.6 0.6 copy-start.19
  50.6 5.6 %copy-start.13 = (pred[128]{0:T(512)(128)(4,1)}, pred[128]{0:T(512)(128)(4,1)S(1)}, u32[]{:S(2)}) copy-start(pred[128]{0:T(512)(128)(4,1)S(1)} %get-tuple-element.25) | copy-start | bytes 388
  53.3 16.2 %collective-permute-start.7 = (bf16[96,1024]{1,0:T(8,128)(2,1)}, bf16[96,1024]{1,0:T(8,128)(2,1)}, u32[]{:S(2)}, u32[]{:S(2)}) collective-permute-start(bf16[96,1024]{1,0:T(8,128)(2,1)} %convolution_convert_fusion.8), channel_id=1, source_target_pairs={{0,2},{2,0},{4,6},{6,4},{8,10},{10,8},{12,14},{14,12},{1,3},{3,1},... | collective-permute-start | bytes 589832 | tf_op jit(solution)/shard_map/ppermute | solution.py:33
  55.5 0.6 copy-start.20
  58.4 10.1 %collective-permute-start.6 = (bf16[96,1024]{1,0:T(8,128)(2,1)}, bf16[96,1024]{1,0:T(8,128)(2,1)}, u32[]{:S(2)}, u32[]{:S(2)}) collective-permute-start(bf16[96,1024]{1,0:T(8,128)(2,1)} %convolution_convert_fusion.9), channel_id=1, source_target_pairs={{0,2},{2,0},{4,6},{6,4},{8,10},{10,8},{12,14},{14,12},{1,3},{3,1},... | collective-permute-start | bytes 589832 | tf_op jit(solution)/shard_map/ppermute | solution.py:33
  59.6 0.6 copy-start.21
  61.8 10.3 %copy-start.15 = (pred[128]{0:T(512)(128)(4,1)S(1)}, pred[128]{0:T(512)(128)(4,1)}, u32[]{:S(2)}) copy-start(pred[128]{0:T(512)(128)(4,1)} %get-tuple-element.27) | copy-start | bytes 388
  61.8 6.7 %collective-permute-start.5 = (bf16[96,1024]{1,0:T(8,128)(2,1)S(1)}, bf16[96,1024]{1,0:T(8,128)(2,1)S(1)}, u32[]{:S(2)}, u32[]{:S(2)}) collective-permute-start(bf16[96,1024]{1,0:T(8,128)(2,1)S(1)} %convolution_convert_fusion.10), channel_id=1, source_target_pairs={{0,2},{2,0},{4,6},{6,4},{8,10},{10,8},{12,14},{14,12},{1,3},{3,1},... | collective-permute-start | bytes 589832 | tf_op jit(solution)/shard_map/ppermute | solution.py:33
  64.3 9.6 %copy-start.16 = (pred[128]{0:T(512)(128)(4,1)S(1)}, pred[128]{0:T(512)(128)(4,1)}, u32[]{:S(2)}) copy-start(pred[128]{0:T(512)(128)(4,1)} %get-tuple-element.29) | copy-start | bytes 388
  65.3 11.3 %copy-start.14 = (pred[128]{0:T(512)(128)(4,1)S(1)}, pred[128]{0:T(512)(128)(4,1)}, u32[]{:S(2)}) copy-start(pred[128]{0:T(512)(128)(4,1)} %copy-done.13) | copy-start | bytes 388
  68.5 21.3 %copy-start.23 = (f32[896]{0:T(1024)S(1)}, f32[896]{0:T(1024)}, u32[]{:S(2)}) copy-start(f32[896]{0:T(1024)} %custom-call.2) | copy-start | bytes 10756
  70.4 23.5 %collective-permute-start.8 = (bf16[896,1024]{1,0:T(8,128)(2,1)S(1)}, bf16[896,1024]{1,0:T(8,128)(2,1)}, u32[]{:S(2)}, u32[]{:S(2)}) collective-permute-start(bf16[896,1024]{1,0:T(8,128)(2,1)S(1)} %constant_dynamic-update-slice_fusion.1), channel_id=1, source_target_pairs={{0,1},{1,0},{2,3},{3,2},{4,5},{5,4},{6,7},{7,6},{8,9},{9,8},{10,11... | collective-permute-start | bytes 5505032 | tf_op jit(solution)/shard_map/ppermute | solution.py:42
  73.3 12.7 %collective-permute-start.19 = (bf16[96,1024]{1,0:T(8,128)(2,1)S(1)}, bf16[96,1024]{1,0:T(8,128)(2,1)S(1)}, u32[]{:S(2)}, u32[]{:S(2)}) collective-permute-start(bf16[96,1024]{1,0:T(8,128)(2,1)S(1)} %convolution_convert_fusion.5), channel_id=1, source_target_pairs={{0,2},{2,0},{4,6},{6,4},{8,10},{10,8},{12,14},{14,12},{1,3},{3,1},... | collective-permute-start | bytes 589832 | tf_op jit(solution)/shard_map/ppermute | solution.py:33
  75.1 10.1 %collective-permute-start.18 = (bf16[96,1024]{1,0:T(8,128)(2,1)S(1)}, bf16[96,1024]{1,0:T(8,128)(2,1)S(1)}, u32[]{:S(2)}, u32[]{:S(2)}) collective-permute-start(bf16[96,1024]{1,0:T(8,128)(2,1)S(1)} %convolution_convert_fusion.6), channel_id=1, source_target_pairs={{0,2},{2,0},{4,6},{6,4},{8,10},{10,8},{12,14},{14,12},{1,3},{3,1},... | collective-permute-start | bytes 589832 | tf_op jit(solution)/shard_map/ppermute | solution.py:33
  77.7 11.3 %collective-permute-start.20 = (bf16[96,1024]{1,0:T(8,128)(2,1)S(1)}, bf16[96,1024]{1,0:T(8,128)(2,1)S(1)}, u32[]{:S(2)}, u32[]{:S(2)}) collective-permute-start(bf16[96,1024]{1,0:T(8,128)(2,1)S(1)} %convolution_convert_fusion.4), channel_id=1, source_target_pairs={{0,2},{2,0},{4,6},{6,4},{8,10},{10,8},{12,14},{14,12},{1,3},{3,1},... | collective-permute-start | bytes 589832 | tf_op jit(solution)/shard_map/ppermute | solution.py:33
  89.8 10.5 %collective-permute-start.21 = (bf16[896,1024]{1,0:T(8,128)(2,1)}, bf16[896,1024]{1,0:T(8,128)(2,1)}, u32[]{:S(2)}, u32[]{:S(2)}) collective-permute-start(bf16[896,1024]{1,0:T(8,128)(2,1)} %constant_dynamic-update-slice_fusion.6), channel_id=1, source_target_pairs={{0,1},{1,0},{2,3},{3,2},{4,5},{5,4},{6,7},{7,6},{8,9},{9,8},{10,11... | collective-permute-start | bytes 5505032 | tf_op jit(solution)/shard_map/ppermute | solution.py:42
  93.9 2.0 copy-start.9
  95.7 1.9 copy-start.3
  95.8 1.9 copy-start.5
  95.8 2.6 %copy-start.7 = (bf16[1,2048,384]{2,1,0:T(8,128)(2,1)S(1)}, bf16[1,2048,384]{2,1,0:T(8,128)(2,1)}, u32[]{:S(2)}) copy-start(bf16[1,2048,384]{2,1,0:T(8,128)(2,1)} %param.10) | copy-start | bytes 4718596
  98.4 4.7 %copy-start.11 = (f32[896,384]{0,1:T(8,128)}, f32[896,384]{0,1:T(8,128)S(1)}, u32[]{:S(2)}) copy-start(f32[896,384]{0,1:T(8,128)S(1)} %fusion.5) | copy-start | bytes 4128772
  100.3 2.8 %copy-start.12 = (f32[896,384]{0,1:T(8,128)}, f32[896,384]{0,1:T(8,128)S(1)}, u32[]{:S(2)}) copy-start(f32[896,384]{0,1:T(8,128)S(1)} %fusion.7) | copy-start | bytes 4128772
  103.1 3.0 %copy-start.1 = (bf16[896,1024]{1,0:T(8,128)(2,1)}, bf16[896,1024]{1,0:T(8,128)(2,1)S(1)}, u32[]{:S(2)}) copy-start(bf16[896,1024]{1,0:T(8,128)(2,1)S(1)} %get-tuple-element.17) | copy-start | bytes 5505028
  103.1 11.6 %copy-start.24 = (f32[128]{0:T(128)S(1)}, f32[128]{0:T(128)}, u32[]{:S(2)}) copy-start(f32[128]{0:T(128)} %fusion.156) | copy-start | bytes 1540
  106.1 1.3 collective-permute-start.27
  107.4 3.6 %collective-permute-start.28 = (f32[384]{0:T(512)S(1)}, f32[384]{0:T(512)S(1)}, u32[]{:S(2)}, u32[]{:S(2)}) collective-permute-start(f32[384]{0:T(512)S(1)} %slice.130), channel_id=1, source_target_pairs={{0,2},{2,0},{4,6},{6,4},{8,10},{10,8},{12,14},{14,12},{1,3},{3,1},... | collective-permute-start | bytes 4616 | tf_op jit(solution)/shard_map/ppermute | solution.py:33
  111.2 14.9 %collective-permute-start.29 = (f32[2,128]{1,0:T(2,128)S(1)}, f32[2,128]{1,0:T(2,128)S(1)}, u32[]{:S(2)}, u32[]{:S(2)}) collective-permute-start(f32[2,128]{1,0:T(2,128)S(1)} %pad_maximum_fusion.7), channel_id=1, source_target_pairs={{0,12},{2,14},{4,0},{6,2},{8,4},{10,6},{12,8},{14,10},{1,13},{3,15... | collective-permute-start | bytes 3080 | tf_op jit(solution)/shard_map/ppermute | solution.py:36
  111.5 14.7 %collective-permute-start.30 = (f32[2,128]{1,0:T(2,128)S(1)}, f32[2,128]{1,0:T(2,128)S(1)}, u32[]{:S(2)}, u32[]{:S(2)}) collective-permute-start(f32[2,128]{1,0:T(2,128)S(1)} %pad_maximum_fusion.8), channel_id=1, source_target_pairs={{0,8},{2,10},{4,12},{6,14},{8,0},{10,2},{12,4},{14,6},{1,9},{3,11}... | collective-permute-start | bytes 3080 | tf_op jit(solution)/shard_map/ppermute | solution.py:36
  115.0 3.7 %collective-permute-start.3 = (f32[4,96]{1,0:T(4,128)S(1)}, f32[4,96]{1,0:T(4,128)S(1)}, u32[]{:S(2)}, u32[]{:S(2)}) collective-permute-start(f32[4,96]{1,0:T(4,128)S(1)} %pad_maximum_fusion.6), channel_id=1, source_target_pairs={{0,2},{2,0},{4,6},{6,4},{8,10},{10,8},{12,14},{14,12},{1,3},{3,1},... | collective-permute-start | bytes 4616 | tf_op jit(solution)/shard_map/ppermute | solution.py:33
  116.5 9.7 %collective-permute-start.31 = (f32[2,128]{1,0:T(2,128)S(1)}, f32[2,128]{1,0:T(2,128)S(1)}, u32[]{:S(2)}, u32[]{:S(2)}) collective-permute-start(f32[2,128]{1,0:T(2,128)S(1)} %pad_maximum_fusion.9), channel_id=1, source_target_pairs={{0,4},{2,6},{4,8},{6,10},{8,12},{10,14},{12,0},{14,2},{1,5},{3,7},... | collective-permute-start | bytes 3080 | tf_op jit(solution)/shard_map/ppermute | solution.py:36
  121.7 1.4 copy-start.8
  122.9 12.8 %collective-permute-start.9 = (bf16[896,1024]{1,0:T(8,128)(2,1)S(1)}, bf16[896,1024]{1,0:T(8,128)(2,1)S(1)}, u32[]{:S(2)}, u32[]{:S(2)}) collective-permute-start(bf16[896,1024]{1,0:T(8,128)(2,1)S(1)} %convolution_convert_fusion.3), channel_id=1, source_target_pairs={{0,1},{1,0},{2,3},{3,2},{4,5},{5,4},{6,7},{7,6},{8,9},{9,8},{10,11... | collective-permute-start | bytes 5505032 | tf_op jit(solution)/shard_map/ppermute | solution.py:42
  123.2 1.4 copy-start.10
  124.6 1.6 copy-start.18
  125.8 12.7 %collective-permute-start.22 = (bf16[896,1024]{1,0:T(8,128)(2,1)S(1)}, bf16[896,1024]{1,0:T(8,128)(2,1)S(1)}, u32[]{:S(2)}, u32[]{:S(2)}) collective-permute-start(bf16[896,1024]{1,0:T(8,128)(2,1)S(1)} %add_convert_fusion), channel_id=1, source_target_pairs={{0,1},{1,0},{2,3},{3,2},{4,5},{5,4},{6,7},{7,6},{8,9},{9,8},{10,11... | collective-permute-start | bytes 5505032 | tf_op jit(solution)/shard_map/ppermute | solution.py:42
  126.8 1.5 copy-start.4
  126.8 2.0 %copy-start.6 = (bf16[896,1024]{1,0:T(8,128)(2,1)S(1)}, bf16[896,1024]{1,0:T(8,128)(2,1)}, u32[]{:S(2)}) copy-start(bf16[896,1024]{1,0:T(8,128)(2,1)} %copy-done.5) | copy-start | bytes 5505028
  137.0 3.5 %copy-start.2 = (bf16[896,1024]{1,0:T(8,128)(2,1)S(1)}, bf16[896,1024]{1,0:T(8,128)(2,1)}, u32[]{:S(2)}) copy-start(bf16[896,1024]{1,0:T(8,128)(2,1)} %copy-done.1) | copy-start | bytes 5505028
  137.0 20.5 %collective-permute-start.10 = (bf16[384,1024]{1,0:T(8,128)(2,1)S(1)}, bf16[384,1024]{1,0:T(8,128)(2,1)S(1)}, u32[]{:S(2)}, u32[]{:S(2)}) collective-permute-start(bf16[384,1024]{1,0:T(8,128)(2,1)S(1)} %slice.249), channel_id=1, source_target_pairs={{0,2},{2,0},{4,6},{6,4},{8,10},{10,8},{12,14},{14,12},{1,3},{3,1},... | collective-permute-start | bytes 2359304 | tf_op jit(solution)/shard_map/ppermute | solution.py:33
  139.7 33.8 %collective-permute-start.23 = (bf16[384,1024]{1,0:T(8,128)(2,1)S(1)}, bf16[384,1024]{1,0:T(8,128)(2,1)S(1)}, u32[]{:S(2)}, u32[]{:S(2)}) collective-permute-start(bf16[384,1024]{1,0:T(8,128)(2,1)S(1)} %slice.248), channel_id=1, source_target_pairs={{0,2},{2,0},{4,6},{6,4},{8,10},{10,8},{12,14},{14,12},{1,3},{3,1},... | collective-permute-start | bytes 2359304 | tf_op jit(solution)/shard_map/ppermute | solution.py:33
  157.7 18.5 %collective-permute-start.11 = (bf16[128,1024]{1,0:T(8,128)(2,1)S(1)}, bf16[128,1024]{1,0:T(8,128)(2,1)S(1)}, u32[]{:S(2)}, u32[]{:S(2)}) collective-permute-start(bf16[128,1024]{1,0:T(8,128)(2,1)S(1)} %fusion.35), channel_id=1, source_target_pairs={{0,12},{2,14},{4,0},{6,2},{8,4},{10,6},{12,8},{14,10},{1,13},{3,15... | collective-permute-start | bytes 786440 | tf_op jit(solution)/shard_map/ppermute | solution.py:36
  159.7 35.1 %collective-permute-start.12 = (bf16[128,1024]{1,0:T(8,128)(2,1)S(1)}, bf16[128,1024]{1,0:T(8,128)(2,1)S(1)}, u32[]{:S(2)}, u32[]{:S(2)}) collective-permute-start(bf16[128,1024]{1,0:T(8,128)(2,1)S(1)} %fusion.34), channel_id=1, source_target_pairs={{0,8},{2,10},{4,12},{6,14},{8,0},{10,2},{12,4},{14,6},{1,9},{3,11}... | collective-permute-start | bytes 786440 | tf_op jit(solution)/shard_map/ppermute | solution.py:36
  160.1 34.7 %collective-permute-start.13 = (bf16[128,1024]{1,0:T(8,128)(2,1)S(1)}, bf16[128,1024]{1,0:T(8,128)(2,1)S(1)}, u32[]{:S(2)}, u32[]{:S(2)}) collective-permute-start(bf16[128,1024]{1,0:T(8,128)(2,1)S(1)} %fusion.33), channel_id=1, source_target_pairs={{0,4},{2,6},{4,8},{6,10},{8,12},{10,14},{12,0},{14,2},{1,5},{3,7},... | collective-permute-start | bytes 786440 | tf_op jit(solution)/shard_map/ppermute | solution.py:36
  173.8 22.0 %collective-permute-start.24 = (bf16[128,1024]{1,0:T(8,128)(2,1)S(1)}, bf16[128,1024]{1,0:T(8,128)(2,1)S(1)}, u32[]{:S(2)}, u32[]{:S(2)}) collective-permute-start(bf16[128,1024]{1,0:T(8,128)(2,1)S(1)} %fusion.28), channel_id=1, source_target_pairs={{0,12},{2,14},{4,0},{6,2},{8,4},{10,6},{12,8},{14,10},{1,13},{3,15... | collective-permute-start | bytes 786440 | tf_op jit(solution)/shard_map/ppermute | solution.py:36
  175.7 27.8 %collective-permute-start.25 = (bf16[128,1024]{1,0:T(8,128)(2,1)S(1)}, bf16[128,1024]{1,0:T(8,128)(2,1)S(1)}, u32[]{:S(2)}, u32[]{:S(2)}) collective-permute-start(bf16[128,1024]{1,0:T(8,128)(2,1)S(1)} %fusion.27), channel_id=1, source_target_pairs={{0,8},{2,10},{4,12},{6,14},{8,0},{10,2},{12,4},{14,6},{1,9},{3,11}... | collective-permute-start | bytes 786440 | tf_op jit(solution)/shard_map/ppermute | solution.py:36
  176.2 27.4 %collective-permute-start.26 = (bf16[128,1024]{1,0:T(8,128)(2,1)S(1)}, bf16[128,1024]{1,0:T(8,128)(2,1)S(1)}, u32[]{:S(2)}, u32[]{:S(2)}) collective-permute-start(bf16[128,1024]{1,0:T(8,128)(2,1)S(1)} %fusion.26), channel_id=1, source_target_pairs={{0,4},{2,6},{4,8},{6,10},{8,12},{10,14},{12,0},{14,2},{1,5},{3,7},... | collective-permute-start | bytes 786440 | tf_op jit(solution)/shard_map/ppermute | solution.py:36

commit v2 on v1

v2 whole, which is shorter than its diff:
```python
import functools

import jax
import jax.numpy as jnp
import numpy as np
from jax import lax
from jax.experimental import pallas as pl
from jax.experimental.pallas import tpu as pltpu
from jax.sharding import PartitionSpec as P

BF = jnp.bfloat16
F32 = jnp.float32
I32 = jnp.int32
TAIL = 16


def dot(a, b, contract):
    return lax.dot_general(a, b, (contract, ((), ())), preferred_element_type=F32)


def split_three(values):
    high = lax.reduce_precision(values, 8, 7)
    rest = values - high
    middle = lax.reduce_precision(rest, 8, 7)
    low = rest - middle
    return [part.astype(BF) for part in (high, middle, low)]


def slot_source(lines, z, slot):
    if z < lines // 2:
        above = lines - 1 - z
        return ("down", slot) if slot <= above else ("up", slot - above)
    return ("up", slot) if slot <= z else ("down", slot - z)


def slot_place(lines, z, slot):
    if slot == 0:
        return 0
    direction, distance = slot_source(lines, z, slot)
    return distance if direction == "up" else lines - distance


def vmem_params(limit=48 * 1024 * 1024):
    return pltpu.CompilerParams(vmem_limit_bytes=limit)


SMEM_SPEC = pl.BlockSpec(memory_space=pltpu.SMEM)
VMEM_SPEC = pl.BlockSpec(memory_space=pltpu.VMEM)
ANY_SPEC = pl.BlockSpec(memory_space=pl.ANY)


def token_slot_kernel(count, part_rows, capacity, padded, info, *refs):
    blocks = refs[:count]
    dense, compact, place, table, parts = refs[count:]
    tokens = dense.shape[0] - TAIL
    width = dense.shape[1]
    per_row = width // tokens
    for i, block in enumerate(blocks):
        @pl.when(info[0] == i)
        def _():
            dense[:tokens, :] = block[:tokens, :]
            table[...] = block[tokens:, :].astype(F32)

    def parts_of(expert):
        row, lane = expert // per_row, pl.multiple_of((expert % per_row) * tokens, tokens)
        parts[...] = jnp.zeros_like(parts)
        for p in range(3):
            found = lax.broadcasted_iota(I32, (table.shape[0], tokens), 0) == p * part_rows + row
            parts[p:p + 1, :] = jnp.sum(
                jnp.where(found, table[:, pl.ds(lane, tokens)], 0.0), axis=0, keepdims=True)
        return parts[...]

    dense[tokens:, :] = jnp.zeros((TAIL, width), BF)
    dense[tokens:, :tokens] = parts_of(info[1]).astype(BF)
    theirs = parts_of(info[2])
    named = jnp.sum(theirs, axis=0, keepdims=True) > 0.0
    row_at = lax.broadcasted_iota(I32, (tokens, tokens), 0)
    column_at = lax.broadcasted_iota(I32, (tokens, tokens), 1)
    until = (row_at <= column_at).astype(F32).astype(BF)
    ones = jnp.broadcast_to(named.astype(F32), (TAIL, tokens)).astype(BF)
    rank = jnp.dot(ones, until, preferred_element_type=F32)[:1, :].astype(I32) - 1
    picked = ((row_at == rank) & named & (row_at < capacity)).astype(F32).astype(BF)
    place[...] = picked[:padded, :]
    compact[:padded, :] = jnp.dot(
        picked[:padded, :], dense[:tokens, :], preferred_element_type=F32).astype(BF)
    compact[padded:, :] = jnp.zeros((TAIL, width), BF)
    compact[padded:, :tokens] = dot(theirs.astype(BF), picked, ((1,), (1,))).astype(BF)


def grad_slot_kernel(count, info, *refs):
    blocks = refs[:count]
    place, dense, compact = refs[count:]
    for i, block in enumerate(blocks):
        @pl.when(info[0] == i)
        def _():
            dense[...] = block[...]
    compact[...] = jnp.dot(place[...], dense[...], preferred_element_type=F32).astype(BF)


def gather_rows(lines, tokens, padded, width, info, mine, other, rows, sems):
    core = info[lines]
    copies = []
    for half, blocks in enumerate((mine, other)):
        which = core if half == 0 else 1 - core
        lane = pl.multiple_of(which * width, width)
        for j in range(lines):
            at = info[j]
            dense, compact = blocks[j], blocks[lines + j]
            copies.append(pltpu.make_async_copy(
                dense.at[pl.ds(0, tokens), :],
                rows.at[pl.ds(pl.multiple_of(at * tokens, tokens), tokens), pl.ds(lane, width)],
                sems.at[len(copies)]))
            copies.append(pltpu.make_async_copy(
                compact.at[pl.ds(0, padded), :],
                rows.at[pl.ds(pl.multiple_of(lines * tokens + at * padded, 16), padded),
                        pl.ds(lane, width)],
                sems.at[len(copies)]))
    for copy in copies:
        copy.start()
    return copies


def gather_tokens_kernel(lines, tokens, padded, width, info, *refs):
    mine, other = refs[:2 * lines], refs[2 * lines:4 * lines]
    tails = refs[4 * lines:6 * lines]
    places = refs[6 * lines:7 * lines]
    rows, weights, ring, sems = refs[7 * lines:]
    copies = gather_rows(lines, tokens, padded, width, info, mine, other, rows, sems)
    eye = (lax.broadcasted_iota(I32, (tokens, tokens), 0)
           == lax.broadcasted_iota(I32, (tokens, tokens), 1))
    for j in range(lines):
        at = info[j]
        for i, (first, size) in enumerate(((0, tokens), (lines * tokens, padded))):
            row = jnp.sum(tails[i * lines + j][...].astype(F32), axis=0, keepdims=True)
            column = jnp.sum(jnp.where(eye, row, 0.0), axis=1, keepdims=True)
            weights[pl.ds(pl.multiple_of(first + at * size, 16), size), :] = column[:size]
        ring[at] = places[j][...]
    for copy in copies:
        copy.wait()


def gather_grads_kernel(lines, tokens, padded, width, info, *refs):
    mine, other = refs[:2 * lines], refs[2 * lines:4 * lines]
    rows, sems = refs[4 * lines:]
    for copy in gather_rows(lines, tokens, padded, width, info, mine, other, rows, sems):
        copy.wait()


def per_device(tokens, expert_ids, router_weights, gate_weight, up_weight, down_weight, grad_out):
    token_count, half_width = tokens.shape
    top_count = expert_ids.shape[1]
    experts = lax.axis_size("expert")
    capacity = min(token_count, 3 * token_count * top_count // (2 * experts))
    padded = -(-capacity // 16) * 16
    lines = experts // 2
    mine = lax.axis_index("expert")
    core = lax.axis_index("tensor")
    at_line = mine // 2
    peer = mine + 1 - 2 * (mine % 2)

    def over_pair(x):
        return lax.ppermute(x, "expert", [(i, i + 1 - 2 * (i % 2)) for i in range(experts)])

    def over_line(x, k):
        return lax.ppermute(
            x, "expert",
            [(i, ((i // 2 + k) % lines) * 2 + i % 2) for i in range(experts)],
        )

    def hop(x, k, step):
        low, high = (k - 1, lines - 1) if step > 0 else (1, lines - k + 1)
        return lax.ppermute(
            x, "expert",
            [(2 * z + y, 2 * (z + step) + y) for z in range(low, high) for y in range(2)],
        )

    def over_core(x):
        return lax.ppermute(x, "tensor", [(0, 1), (1, 0)])

    chosen = expert_ids[:, :, None] == jnp.arange(experts, dtype=I32)[None, None, :]
    table = jnp.sum(jnp.where(chosen, router_weights[:, :, None], 0.0), axis=1).T
    part_rows = experts * token_count // half_width
    parts = jnp.concatenate([p.reshape(part_rows, half_width) for p in split_three(table)])
    tail = -(-3 * part_rows // TAIL) * TAIL
    parts = jnp.pad(parts, ((0, tail - 3 * part_rows), (0, 0)))
    first = jnp.concatenate([tokens, parts])

    def along_line(start):
        up, down = {0: start}, {0: start}
        for k in range(1, lines):
            up[k] = hop(up[k - 1], k, 1)
            down[k] = hop(down[k - 1], k, -1)
        return up, down

    up, down = along_line(first)
    held_back, _, _ = lax.optimization_barrier((grad_out, up[min(2, lines - 1)], down[min(2, lines - 1)]))
    grad_up_line, grad_down_line = along_line(held_back)

    def candidates(slot, ups, downs):
        if slot == 0:
            return [ups[0]], jnp.zeros((), I32)
        sources = [slot_source(lines, z, slot) for z in range(lines)]
        names = sorted(set(sources))
        which = jnp.asarray(np.array([names.index(s) for s in sources], np.int32))[at_line]
        return [(ups if d == "up" else downs)[n] for d, n in names], which

    dense_blocks, compact_blocks, places = [], [], []
    for slot in range(lines):
        blocks, which = candidates(slot, up, down)
        info = jnp.stack([which, mine, peer]).astype(I32)
        dense, compact, place = pl.pallas_call(
            functools.partial(token_slot_kernel, len(blocks), part_rows, capacity, padded),
            out_shape=(
                jax.ShapeDtypeStruct((token_count + TAIL, half_width), BF),
                jax.ShapeDtypeStruct((padded + TAIL, half_width), BF),
                jax.ShapeDtypeStruct((padded, token_count), BF),
            ),
            in_specs=[SMEM_SPEC] + [VMEM_SPEC] * len(blocks),
            out_specs=(VMEM_SPEC,) * 3,
            scratch_shapes=[pltpu.VMEM((tail, half_width), F32), pltpu.VMEM((TAIL, token_count), F32)],
            compiler_params=vmem_params(),
            cost_estimate=pl.CostEstimate(flops=10**8, bytes_accessed=10**6, transcendentals=0),
        )(info, *blocks)
        dense_blocks.append(dense)
        compact_blocks.append(over_pair(compact))
        places.append(place)

    grad_dense, grad_compact = [], []
    for slot in range(lines):
        blocks, which = candidates(slot, grad_up_line, grad_down_line)
        if slot == 0:
            blocks = [grad_out]
        dense, compact = pl.pallas_call(
            functools.partial(grad_slot_kernel, len(blocks)),
            out_shape=(
                jax.ShapeDtypeStruct((token_count, half_width), BF),
                jax.ShapeDtypeStruct((padded, half_width), BF),
            ),
            in_specs=[SMEM_SPEC] + [VMEM_SPEC] * (len(blocks) + 1),
            out_specs=(VMEM_SPEC,) * 2,
            compiler_params=vmem_params(),
            cost_estimate=pl.CostEstimate(flops=10**8, bytes_accessed=10**6, transcendentals=0),
        )(which[None], *blocks, places[slot])
        grad_dense.append(dense)
        grad_compact.append(over_pair(compact))

    place_of = np.array([[slot_place(lines, z, s) for s in range(lines)] for z in range(lines)], np.int32)
    order = jnp.concatenate([jnp.asarray(place_of)[at_line], core[None].astype(I32)])
    dense_rows = lines * token_count
    row_count = lines * (token_count + padded)
    rows_shape = jax.ShapeDtypeStruct((row_count, 2 * half_width), BF)
    sem_shape = pltpu.SemaphoreType.DMA((4 * lines,))

    blocks = dense_blocks + compact_blocks
    other = [over_core(b) for b in blocks]
    tails = ([b[token_count:, :token_count] for b in dense_blocks]
             + [b[padded:, :token_count] for b in compact_blocks])
    rows, weights, ring = pl.pallas_call(
        functools.partial(gather_tokens_kernel, lines, token_count, padded, half_width),
        out_shape=(
            rows_shape,
            jax.ShapeDtypeStruct((row_count, 1), F32),
            jax.ShapeDtypeStruct((lines, padded, token_count), BF),
        ),
        in_specs=[SMEM_SPEC] + [ANY_SPEC] * (4 * lines) + [VMEM_SPEC] * (3 * lines),
        out_specs=(VMEM_SPEC,) * 3,
        scratch_shapes=[sem_shape],
        compiler_params=vmem_params(),
        cost_estimate=pl.CostEstimate(flops=10**6, bytes_accessed=8 * 10**6, transcendentals=0),
    )(order, *blocks, *other, *tails, *places)

    gate_local = gate_weight[0]
    up_local = up_weight[0]
    down_local = down_weight[0]
    gate = dot(rows, gate_local, ((1,), (0,)))
    upward = dot(rows, up_local, ((1,), (0,)))
    sig = jax.nn.sigmoid(gate)
    hidden = gate * sig * upward
    scaled_hidden = (weights * hidden).astype(BF)

    def summed_over_cores(make):
        sent = over_core(make(1 - core).astype(BF))
        return make(core) + sent.astype(F32)

    def half_of(x, which, axis):
        return lax.dynamic_slice_in_dim(x, which * half_width, half_width, axis)

    def go_home(both):
        total = None
        for k in list(range(1, lines)) + [0]:
            at = dense_rows + k * padded
            back = over_pair(both[at:at + padded].astype(BF))
            block = both[k * token_count:(k + 1) * token_count]
            block = block + dot(ring[k], back, ((0,), (0,)))
            if k:
                block = over_line(block.astype(BF), lines - k).astype(F32)
            total = block if total is None else total + block
        return total.astype(BF)

    layer_out = go_home(summed_over_cores(
        lambda c: dot(scaled_hidden, half_of(down_local, c, 1), ((1,), (0,)))))

    blocks = grad_dense + grad_compact
    other = [over_core(b) for b in blocks]
    grads = pl.pallas_call(
        functools.partial(gather_grads_kernel, lines, token_count, padded, half_width),
        out_shape=rows_shape,
        in_specs=[SMEM_SPEC] + [ANY_SPEC] * (4 * lines),
        out_specs=VMEM_SPEC,
        scratch_shapes=[sem_shape],
        compiler_params=vmem_params(),
        cost_estimate=pl.CostEstimate(flops=10**6, bytes_accessed=8 * 10**6, transcendentals=0),
    )(order, *blocks, *other)

    grad_plain = dot(grads, down_local, ((1,), (1,)))
    row_value = jnp.sum(hidden * grad_plain, axis=1)
    grad_hidden = weights * grad_plain
    grad_gate = (grad_hidden * upward * sig * (1.0 + gate * (1.0 - sig))).astype(BF)
    grad_up = (grad_hidden * gate * sig).astype(BF)
    input_grad = go_home(summed_over_cores(
        lambda c: dot(grad_gate, half_of(gate_local, c, 0), ((1,), (1,)))
        + dot(grad_up, half_of(up_local, c, 0), ((1,), (1,)))))

    down_grad = dot(scaled_hidden, grads, ((0,), (0,))).astype(BF)
    gate_grad = dot(rows, grad_gate, ((0,), (0,))).astype(BF)
    up_grad = dot(rows, grad_up, ((0,), (0,))).astype(BF)

    row_value = row_value + over_core(row_value)
    back_value = over_pair(row_value[dense_rows:])
    by_line = []
    for k in range(lines):
        own = row_value[k * token_count:(k + 1) * token_count]
        value = back_value[k * padded:(k + 1) * padded]
        value = jnp.sum(ring[k].astype(F32) * value[:, None], axis=0)
        both = jnp.stack([own, value])
        by_line.append(over_line(both, lines - k) if k else both)
    held = jnp.stack(by_line)
    ids_line = expert_ids // 2
    place = (ids_line - mine // 2) % lines
    is_peer = (expert_ids % 2) != (mine % 2)
    slot = place * 2 + is_peer.astype(jnp.int32)
    flat = held.reshape(experts, token_count)
    match = slot[:, :, None] == jnp.arange(experts, dtype=jnp.int32)[None, None, :]
    weight_grad = jnp.sum(jnp.where(match, flat.T[:, None, :], 0.0), axis=2)
    return (layer_out, input_grad, weight_grad, gate_grad[None], up_grad[None], down_grad[None])


def solution(mesh):
    in_specs = (
        P(("group", "expert"), "tensor"),
        P(("group", "expert"), None),
        P(("group", "expert"), None),
        P("expert", None, "tensor"),
        P("expert", None, "tensor"),
        P("expert", "tensor", None),
        P(("group", "expert"), "tensor"),
    )
    out_specs = (
        P(("group", "expert"), "tensor"),
        P(("group", "expert"), "tensor"),
        P(("group", "expert"), None),
        P(("group", "expert"), None, "tensor"),
        P(("group", "expert"), None, "tensor"),
        P(("group", "expert"), "tensor", None),
    )
    return jax.shard_map(
        per_device, mesh=mesh, in_specs=in_specs, out_specs=out_specs, check_vma=False
    )
```

time: 206 us -> 220 us (1.068)
  Pallas kernels: 0 us -> 18.9 us
  other arithmetic: 16.3 us -> 4.32 us
  starting transfers between devices: 51.4 us -> 62.2 us
  matrix products: 39.2 us -> 33.1 us
    ppermute x0 -> x12, starting transfers between devices: none -> 22.5 us  [hop(): lax.ppermute(x, 'expert', [(2 * z + y, 2 * (z + step) + y) for z in range...]
    ppermute x15 -> x9, starting transfers between devices: 37.6 us -> 15.1 us  [over_line(): lax.ppermute(x, 'expert', [(i, (i // 2 + k) % lines * 2 + i % 2) for i in...]
    ppermute x0 -> x12, waiting for transfers between devices: none -> 19.3 us  [hop(): lax.ppermute(x, 'expert', [(2 * z + y, 2 * (z + step) + y) for z in range...]
    pallas_call x0 -> x10, Pallas kernels: none -> 18.9 us  [the longest x4 5.47 us: per_device(): pl.pallas_call(functools.partial(token_slot_kernel, len(blocks), part_row...]
    ppermute x12 -> x17, waiting for transfers between devices: 42.3 us -> 24.4 us  [over_pair(): lax.ppermute(x, 'expert', [(i, i + 1 - 2 * (i % 2)) for i in range(expert...]
    ppermute x12 -> x17, starting transfers between devices: 12.7 us -> 20.3 us  [over_pair(): lax.ppermute(x, 'expert', [(i, i + 1 - 2 * (i % 2)) for i in range(expert...]
    dot_general x28 -> x20, matrix products: 39.2 us -> 33.1 us  [dot(): lax.dot_general(a, b, (contract, ((), ())), preferred_element_type=F32)]
    select_n x2 -> x0, other arithmetic: 4.65 us -> none  [whole(): lower = jnp.where(core == 0, held, other)]
  transfers between devices with their start and end apart: 32 -> 57, of which waited for: 11 -> 17; matrix products, arithmetic and copies ran while one was open for 35% -> 13% of each run, Pallas kernels for 0% -> 7%
where the time goes in v2:
time: 220 us; the launch traced here: 219 us
  waiting for transfers between devices  72.4 us (33%)
  starting transfers between devices  62.2 us (28%)
  matrix products  33.1 us (15%)
  local copies, waits for them, and re-layouts  26.5 us (12%)
  Pallas kernels  18.9 us (9%)
  other arithmetic  4.32 us (2%)
    dot_general x20, matrix products, dot(): lax.dot_general(a, b, (contract, ((), ())), preferred_element_type=F32)  33.1 us
    ppermute x9, waiting for transfers between devices, over_line(): lax.ppermute(x, 'expert', [(i, (i // 2 + k) % lines * 2 + i % 2) for i in...  28.6 us
    ppermute x17, waiting for transfers between devices, over_pair(): lax.ppermute(x, 'expert', [(i, i + 1 - 2 * (i % 2)) for i in range(expert...  24.4 us
    ppermute x12, starting transfers between devices, hop(): lax.ppermute(x, 'expert', [(2 * z + y, 2 * (z + step) + y) for z in range...  22.5 us
    unnamed x91, local copies, waits for them, and re-layouts  20.3 us
    ppermute x17, starting transfers between devices, over_pair(): lax.ppermute(x, 'expert', [(i, i + 1 - 2 * (i % 2)) for i in range(expert...  20.3 us
    ppermute x12, waiting for transfers between devices, hop(): lax.ppermute(x, 'expert', [(2 * z + y, 2 * (z + step) + y) for z in range...  19.3 us
    ppermute x9, starting transfers between devices, over_line(): lax.ppermute(x, 'expert', [(i, (i // 2 + k) % lines * 2 + i % 2) for i in...  15.1 us
  transfers between devices with their start and end apart: 57, of which 17 were waited for; matrix products, arithmetic and copies ran while one was open for 13% of the time, Pallas kernels for 7%

profile of v2, /device:TPU:0, one launch (start us, length us, event | category | flops | bytes accessed | tf_op | source)
XLA Modules:
  0.0 218.9 jit_solution(16119649757459144490)
XLA Ops:
  1.6 1.0 pad_maximum_fusion.refs_0_
  2.5 4.9 %collective-permute-start.1 = (bf16[144,1024]{1,0:T(8,128)(2,1)S(1)}, bf16[144,1024]{1,0:T(8,128)(2,1)S(1)}, u32[]{:S(2)}, u32[]{:S(2)}) collective-permute-start(bf16[144,1024]{1,0:T(8,128)(2,1)S(1)} %pad_maximum_fusion.refs_0_), channel_id=1, source_target_pairs={{0,4},{2,6},{4,8},{6,10},{8,12},{10,14},{1,5},{3,7},{5,9},{7,11},{... | collective-permute-start | bytes 884744 | tf_op jit(solution)/shard_map/ppermute | solution.py:172
  7.5 1.3 collective-permute-start
  8.8 4.9 %collective-permute-done.1.refs_1_.refs_2_ = bf16[144,1024]{1,0:T(8,128)(2,1)S(1)} collective-permute-done((bf16[144,1024]{1,0:T(8,128)(2,1)S(1)}, bf16[144,1024]{1,0:T(8,128)(2,1)S(1)}, u32[]{:S(2)}, u32[]{:S(2)}) %collective-permute-start.1) | collective-permute-done | bytes 294944 | tf_op jit(solution)/shard_map/ppermute | solution.py:172
  13.7 1.4 collective-permute-start.3
  15.1 2.8 %collective-permute-done.refs_0_ = bf16[144,1024]{1,0:T(8,128)(2,1)S(1)} collective-permute-done((bf16[144,1024]{1,0:T(8,128)(2,1)S(1)}, bf16[144,1024]{1,0:T(8,128)(2,1)S(1)}, u32[]{:S(2)}, u32[]{:S(2)}) %collective-permute-start) | collective-permute-done | bytes 294944 | tf_op jit(solution)/shard_map/ppermute | solution.py:172
  17.9 1.3 collective-permute-start.2
  20.2 1.6 collective-permute-start.6
  21.7 1.2 dynamic_slice.52.info
  26.4 1.0 copy-done.33
  27.6 1.6 collective-permute-start.32
  29.8 2.0 shard_map.183
  32.5 3.0 %collective-permute-done.32.refs_4_ = bf16[96,1024]{1,0:T(8,128)(2,1)} collective-permute-done((bf16[96,1024]{1,0:T(8,128)(2,1)S(1)}, bf16[96,1024]{1,0:T(8,128)(2,1)}, u32[]{:S(2)}, u32[]{:S(2)}) %collective-permute-start.32) | collective-permute-done | bytes 196640 | tf_op jit(solution)/shard_map/ppermute | solution.py:162
  35.5 1.5 collective-permute-start.8
  37.8 5.1 %collective-permute-start.27 = (bf16[128,1024]{1,0:T(8,128)(2,1)}, bf16[128,1024]{1,0:T(8,128)(2,1)S(1)}, u32[]{:S(2)}, u32[]{:S(2)}) collective-permute-start(bf16[128,1024]{1,0:T(8,128)(2,1)} %refs_0_.1), channel_id=1, source_target_pairs={{0,4},{2,6},{4,8},{6,10},{8,12},{10,14},{1,5},{3,7},{5,9},{7,11},{... | collective-permute-start | bytes 786440 | tf_op jit(solution)/shard_map/ppermute | solution.py:172
  44.3 1.3 collective-permute-start.4
  46.3 1.3 collective-permute-start.26
  48.2 11.5 %collective-permute-done.26.refs_0_ = bf16[128,1024]{1,0:T(8,128)(2,1)S(1)} collective-permute-done((bf16[128,1024]{1,0:T(8,128)(2,1)}, bf16[128,1024]{1,0:T(8,128)(2,1)S(1)}, u32[]{:S(2)}, u32[]{:S(2)}) %collective-permute-start.26) | collective-permute-done | bytes 262176 | tf_op jit(solution)/shard_map/ppermute | solution.py:172
  59.7 1.4 collective-permute-start.29
  61.1 1.3 collective-permute-start.28
  63.7 1.6 shard_map.184
  69.0 1.4 collective-permute-start.31
  70.4 1.3 collective-permute-start.30
  71.8 3.8 %collective-permute-done.9.refs_7_ = bf16[112,1024]{1,0:T(8,128)(2,1)S(1)} collective-permute-done((bf16[112,1024]{1,0:T(8,128)(2,1)}, bf16[112,1024]{1,0:T(8,128)(2,1)S(1)}, u32[]{:S(2)}, u32[]{:S(2)}) %collective-permute-start.9) | collective-permute-done | bytes 229408 | tf_op jit(solution)/shard_map/ppermute | solution.py:162
  81.3 2.3 %shard_map.188 = (bf16[128,1024]{1,0:T(8,128)(2,1)}, bf16[96,1024]{1,0:T(8,128)(2,1)S(1)}) custom-call(s32[1]{0:T(128)} %dynamic_slice.52.info, bf16[128,1024]{1,0:T(8,128)(2,1)S(1)} %collective-permute-done.28.refs_0_, bf16[128,1024]{1,0:T(8,128)(2,1)} %collective-permute-done.29.refs_1_, bf16[96,128]{1,0:T(8,128)(2,1)S(1)} %copy-done.27), custom_call_target="tpu_custom_call" | custom-call | flops 100000000 | bytes 1000000 | tf_op jit(solution)/shard_map/pallas_call | solution.py:233
  85.3 1.0 copy-done.2
  95.9 3.9 %shard_map.185 = (bf16[896,2048]{1,0:T(8,128)(2,1)}, f32[896,1]{1,0:T(8,128)S(1)}, bf16[4,96,128]{2,1,0:T(8,128)(2,1)S(1)}) custom-call(s32[5]{0:T(128)S(1)} %pad_add_fusion.info, bf16[144,1024]{1,0:T(8,128)(2,1)S(1)} %get-tuple-element.30.refs_0_, bf16[144,1024]{1,0:T(8,128)(2,1)S(1)} %get-tuple-element.31.refs_1_, ...), custom_call_target="tpu_custom_call" | custom-call | flops 1000000 | bytes 8000000 | tf_op jit(solution)/shard_map/pallas_call | solution.py:258
  99.9 1.6 collective-permute-start.34
  101.5 1.9 shard_map.189
  104.0 5.1 %fusion.5 = f32[896,384]{0,1:T(8,128)} fusion(bf16[896,2048]{1,0:T(8,128)(2,1)} %get-tuple-element.43, bf16[1,2048,384]{2,1,0:T(8,128)(2,1)S(1)} %copy-done.35), kind=kOutput, calls=%fused_computation.12 | convolution fusion | flops 1409286144 | bytes 6619136 | tf_op jit(solution)/shard_map/dot_general | solution.py:18
  110.1 1.4 collective-permute-done.35.refs_7_
  111.5 2.9 %fusion.7 = f32[896,384]{0,1:T(8,128)} fusion(bf16[896,2048]{1,0:T(8,128)(2,1)S(1)} %copy-done.40, bf16[1,2048,384]{2,1,0:T(8,128)(2,1)S(1)} %copy-done.37), kind=kOutput, calls=%fused_computation.14 | convolution fusion | flops 1409286144 | bytes 6619136 | tf_op jit(solution)/shard_map/dot_general | solution.py:18
  115.7 4.4 %shard_map.190 = bf16[896,2048]{1,0:T(8,128)(2,1)} custom-call(s32[5]{0:T(128)S(1)} %pad_add_fusion.info, bf16[128,1024]{1,0:T(8,128)(2,1)S(1)} %copy-done.10, bf16[128,1024]{1,0:T(8,128)(2,1)S(1)} %copy-done.12, bf16[128,1024]{1,0:T(8,128)(2,1)} %get-tuple-element.48.refs_2_, bf16[128,1024]{1,0:T(8,128)(2,1)S(1)} %get-tuple-element.49.refs_3_, ...), custom_call_target="tpu_custom_call" | custom-call | flops 1000000 | bytes 8000000 | tf_op jit(solution)/shard_map/pallas_call | solution.py:305
  120.2 4.6 %multiply_reduce_fusion = (f32[896]{0:T(1024)S(1)}, bf16[896,384]{0,1:T(8,128)(2,1)S(1)}, bf16[896,384]{0,1:T(8,128)(2,1)S(1)}, bf16[896,384]{0,1:T(8,128)(2,1)S(1)}) fusion(f32[896,384]{0,1:T(8,128)S(1)} %copy-done.43, f32[896,384]{0,1:T(8,128)S(1)} %copy-done.44, f32[896]{0:T(1024)S(1)} %reduce, bf16[896,2048]{1,0:T(8,128)(2,1)} %shard_map.190, ...), kind=kOutput, calls=%fused_computation.16 | convolution fusion | flops 1416166528 | bytes 10066944 | tf_op jit(solution)/shard_map/dot_general | solution.py:18
  124.9 2.9 %fusion.2 = bf16[1,384,2048]{2,1,0:T(8,128)(2,1)} fusion(bf16[896,384]{0,1:T(8,128)(2,1)S(1)} %get-tuple-element.60, bf16[896,2048]{1,0:T(8,128)(2,1)S(1)} %copy-done.34), kind=kOutput, calls=%fused_computation.8 | convolution fusion | flops 1410072576 | bytes 5931008 | tf_op jit(solution)/shard_map/dot_general | solution.py:18
  127.8 3.5 %fusion = bf16[1,2048,384]{2,1,0:T(8,128)(2,1)} fusion(bf16[896,2048]{1,0:T(8,128)(2,1)S(1)} %copy-done.41, bf16[896,384]{0,1:T(8,128)(2,1)S(1)} %get-tuple-element.59), kind=kOutput, calls=%fused_computation.6 | convolution fusion | flops 1410072576 | bytes 5931008 | tf_op jit(solution)/shard_map/dot_general | solution.py:18
  131.3 1.1 convolution_convert_fusion.3
  132.7 1.2 fusion.10
  134.5 1.2 add_convert_fusion
  136.2 3.5 %fusion.1 = bf16[1,2048,384]{2,1,0:T(8,128)(2,1)} fusion(bf16[896,2048]{1,0:T(8,128)(2,1)S(1)} %copy-done.41, bf16[896,384]{0,1:T(8,128)(2,1)S(1)} %get-tuple-element.61), kind=kOutput, calls=%fused_computation.7 | convolution fusion | flops 1410072576 | bytes 5931008 | tf_op jit(solution)/shard_map/dot_general | solution.py:18
  139.6 1.4 fusion.13
  141.0 1.6 collective-permute-start.53
  142.6 2.1 collective-permute-done.53
  144.9 2.7 %collective-permute-start.56 = (f32[2,128]{1,0:T(2,128)S(1)}, f32[2,128]{1,0:T(2,128)S(1)}, u32[]{:S(2)}, u32[]{:S(2)}) collective-permute-start(f32[2,128]{1,0:T(2,128)S(1)} %pad_maximum_fusion.4), channel_id=1, source_target_pairs={{0,4},{2,6},{4,8},{6,10},{8,12},{10,14},{12,0},{14,2},{1,5},{3,7},... | collective-permute-start | bytes 3080 | tf_op jit(solution)/shard_map/ppermute | solution.py:165
  147.6 2.6 %collective-permute-start.54 = (f32[2,128]{1,0:T(2,128)S(1)}, f32[2,128]{1,0:T(2,128)S(1)}, u32[]{:S(2)}, u32[]{:S(2)}) collective-permute-start(f32[2,128]{1,0:T(2,128)S(1)} %pad_maximum_fusion.2), channel_id=1, source_target_pairs={{0,12},{2,14},{4,0},{6,2},{8,4},{10,6},{12,8},{14,10},{1,13},{3,15... | collective-permute-start | bytes 3080 | tf_op jit(solution)/shard_map/ppermute | solution.py:165
  150.3 1.7 collective-permute-done.55
  152.7 1.2 fusion.101
  153.9 1.6 collective-permute-start.25
  156.0 1.5 collective-permute-start.21
  158.0 1.2 fusion.102
  159.3 1.6 collective-permute-start.49
  160.9 5.2 %collective-permute-done.23 = bf16[96,1024]{1,0:T(8,128)(2,1)S(1)} collective-permute-done((bf16[96,1024]{1,0:T(8,128)(2,1)S(1)}, bf16[96,1024]{1,0:T(8,128)(2,1)S(1)}, u32[]{:S(2)}, u32[]{:S(2)}) %collective-permute-start.23) | collective-permute-done | bytes 196640 | tf_op jit(solution)/shard_map/ppermute | solution.py:162
  166.0 1.5 collective-permute-start.47
  167.8 6.7 %collective-permute-done.19 = bf16[96,1024]{1,0:T(8,128)(2,1)S(1)} collective-permute-done((bf16[96,1024]{1,0:T(8,128)(2,1)S(1)}, bf16[96,1024]{1,0:T(8,128)(2,1)S(1)}, u32[]{:S(2)}, u32[]{:S(2)}) %collective-permute-start.19) | collective-permute-done | bytes 196640 | tf_op jit(solution)/shard_map/ppermute | solution.py:162
  174.5 1.5 collective-permute-start.45
  176.2 3.6 %collective-permute-start.20 = (bf16[128,1024]{1,0:T(8,128)(2,1)S(1)}, bf16[128,1024]{1,0:T(8,128)(2,1)S(1)}, u32[]{:S(2)}, u32[]{:S(2)}) collective-permute-start(bf16[128,1024]{1,0:T(8,128)(2,1)S(1)} %fusion.35), channel_id=1, source_target_pairs={{0,12},{2,14},{4,0},{6,2},{8,4},{10,6},{12,8},{14,10},{1,13},{3,15... | collective-permute-start | bytes 786440 | tf_op jit(solution)/shard_map/ppermute | solution.py:165
  181.5 1.6 collective-permute-start.24
  183.4 1.0 collective-permute-done.45
  184.3 1.5 collective-permute-start.51
  186.1 3.6 %collective-permute-start.46 = (bf16[128,1024]{1,0:T(8,128)(2,1)S(1)}, bf16[128,1024]{1,0:T(8,128)(2,1)S(1)}, u32[]{:S(2)}, u32[]{:S(2)}) collective-permute-start(bf16[128,1024]{1,0:T(8,128)(2,1)S(1)} %fusion.30), channel_id=1, source_target_pairs={{0,12},{2,14},{4,0},{6,2},{8,4},{10,6},{12,8},{14,10},{1,13},{3,15... | collective-permute-start | bytes 786440 | tf_op jit(solution)/shard_map/ppermute | solution.py:165
  190.1 18.2 %collective-permute-done.22 = bf16[128,1024]{1,0:T(8,128)(2,1)S(1)} collective-permute-done((bf16[128,1024]{1,0:T(8,128)(2,1)S(1)}, bf16[128,1024]{1,0:T(8,128)(2,1)S(1)}, u32[]{:S(2)}, u32[]{:S(2)}) %collective-permute-start.22) | collective-permute-done | bytes 262176 | tf_op jit(solution)/shard_map/ppermute | solution.py:165
  208.3 1.0 fusion.32
  209.3 8.6 %collective-permute-done.48 = bf16[128,1024]{1,0:T(8,128)(2,1)S(1)} collective-permute-done((bf16[128,1024]{1,0:T(8,128)(2,1)S(1)}, bf16[128,1024]{1,0:T(8,128)(2,1)S(1)}, u32[]{:S(2)}, u32[]{:S(2)}) %collective-permute-start.48) | collective-permute-done | bytes 262176 | tf_op jit(solution)/shard_map/ppermute | solution.py:165
  217.9 1.0 fusion.27
  (206 shorter events, 41.5 us)
Async XLA Ops:
  0.6 119.5 %copy-start = (bf16[1,384,2048]{2,1,0:T(8,128)(2,1)S(1)}, bf16[1,384,2048]{2,1,0:T(8,128)(2,1)}, u32[]{:S(2)}) copy-start(bf16[1,384,2048]{2,1,0:T(8,128)(2,1)} %param.19) | copy-start | bytes 4718596
  0.6 61.7 %copy-start.42 = (s32[4]{0:T(128)S(1)}, s32[4]{0:T(128)}, u32[]{:S(2)}) copy-start(s32[4]{0:T(128)} %constant.92.clone) | copy-start | bytes 52
  1.6 74.0 %copy-start.39 = (s32[128,4]{0,1:T(4,128)S(1)}, s32[128,4]{0,1:T(4,128)}, u32[]{:S(2)}) copy-start(s32[128,4]{0,1:T(4,128)} %param.15) | copy-start | bytes 6148
  2.5 11.2 %collective-permute-start.1 = (bf16[144,1024]{1,0:T(8,128)(2,1)S(1)}, bf16[144,1024]{1,0:T(8,128)(2,1)S(1)}, u32[]{:S(2)}, u32[]{:S(2)}) collective-permute-start(bf16[144,1024]{1,0:T(8,128)(2,1)S(1)} %pad_maximum_fusion.refs_0_), channel_id=1, source_target_pairs={{0,4},{2,6},{4,8},{6,10},{8,12},{10,14},{1,5},{3,7},{5,9},{7,11},{... | collective-permute-start | bytes 884744 | tf_op jit(solution)/shard_map/ppermute | solution.py:172
  7.5 10.4 %collective-permute-start = (bf16[144,1024]{1,0:T(8,128)(2,1)S(1)}, bf16[144,1024]{1,0:T(8,128)(2,1)S(1)}, u32[]{:S(2)}, u32[]{:S(2)}) collective-permute-start(bf16[144,1024]{1,0:T(8,128)(2,1)S(1)} %pad_maximum_fusion.refs_0_), channel_id=1, source_target_pairs={{4,0},{6,2},{8,4},{10,6},{12,8},{14,10},{5,1},{7,3},{9,5},{11,7},{... | collective-permute-start | bytes 884744 | tf_op jit(solution)/shard_map/ppermute | solution.py:172
  13.7 13.9 %collective-permute-start.3 = (bf16[144,1024]{1,0:T(8,128)(2,1)S(1)}, bf16[144,1024]{1,0:T(8,128)(2,1)}, u32[]{:S(2)}, u32[]{:S(2)}) collective-permute-start(bf16[144,1024]{1,0:T(8,128)(2,1)S(1)} %collective-permute-done.1.refs_1_.refs_2_), channel_id=1, source_target_pairs={{4,8},{6,10},{8,12},{10,14},{5,9},{7,11},{9,13},{11,15},{20,24},{2... | collective-permute-start | bytes 884744 | tf_op jit(solution)/shard_map/ppermute | solution.py:172
  17.9 11.4 %collective-permute-start.2 = (bf16[144,1024]{1,0:T(8,128)(2,1)S(1)}, bf16[144,1024]{1,0:T(8,128)(2,1)}, u32[]{:S(2)}, u32[]{:S(2)}) collective-permute-start(bf16[144,1024]{1,0:T(8,128)(2,1)S(1)} %collective-permute-done.refs_0_), channel_id=1, source_target_pairs={{4,0},{6,2},{8,4},{10,6},{5,1},{7,3},{9,5},{11,7},{20,16},{22,18},... | collective-permute-start | bytes 884744 | tf_op jit(solution)/shard_map/ppermute | solution.py:172
  20.1 41.0 %copy-start.31 = (bf16[96,128]{1,0:T(8,128)(2,1)}, bf16[96,128]{1,0:T(8,128)(2,1)S(1)}, u32[]{:S(2)}) copy-start(bf16[96,128]{1,0:T(8,128)(2,1)S(1)} %get-tuple-element.38.refs_24_.refs_1_) | copy-start | bytes 73732
  20.2 6.2 %collective-permute-start.6 = (bf16[112,1024]{1,0:T(8,128)(2,1)S(1)}, bf16[112,1024]{1,0:T(8,128)(2,1)S(1)}, u32[]{:S(2)}, u32[]{:S(2)}) collective-permute-start(bf16[112,1024]{1,0:T(8,128)(2,1)S(1)} %get-tuple-element.34), channel_id=1, source_target_pairs={{0,2},{2,0},{4,6},{6,4},{8,10},{10,8},{12,14},{14,12},{1,3},{3,1},... | collective-permute-start | bytes 688136 | tf_op jit(solution)/shard_map/ppermute | solution.py:162
  21.7 15.3 %collective-permute-start.10 = (bf16[144,1024]{1,0:T(8,128)(2,1)S(1)}, bf16[144,1024]{1,0:T(8,128)(2,1)S(1)}, u32[]{:S(2)}, u32[]{:S(2)}) collective-permute-start(bf16[144,1024]{1,0:T(8,128)(2,1)S(1)} %get-tuple-element.30.refs_0_), channel_id=1, source_target_pairs={{0,1},{1,0},{2,3},{3,2},{4,5},{5,4},{6,7},{7,6},{8,9},{9,8},{10,11... | collective-permute-start | bytes 884744 | tf_op jit(solution)/shard_map/ppermute | solution.py:178
  25.1 20.5 %collective-permute-start.11 = (bf16[144,1024]{1,0:T(8,128)(2,1)S(1)}, bf16[144,1024]{1,0:T(8,128)(2,1)S(1)}, u32[]{:S(2)}, u32[]{:S(2)}) collective-permute-start(bf16[144,1024]{1,0:T(8,128)(2,1)S(1)} %get-tuple-element.31.refs_1_), channel_id=1, source_target_pairs={{0,1},{1,0},{2,3},{3,2},{4,5},{5,4},{6,7},{7,6},{8,9},{9,8},{10,11... | collective-permute-start | bytes 884744 | tf_op jit(solution)/shard_map/ppermute | solution.py:178
  26.4 19.2 %copy-start.13 = (bf16[112,1024]{1,0:T(8,128)(2,1)}, bf16[112,1024]{1,0:T(8,128)(2,1)S(1)}, u32[]{:S(2)}) copy-start(bf16[112,1024]{1,0:T(8,128)(2,1)S(1)} %collective-permute-done.6.refs_4_) | copy-start | bytes 688132
  26.4 16.5 %collective-permute-start.14 = (bf16[112,1024]{1,0:T(8,128)(2,1)S(1)}, bf16[112,1024]{1,0:T(8,128)(2,1)S(1)}, u32[]{:S(2)}, u32[]{:S(2)}) collective-permute-start(bf16[112,1024]{1,0:T(8,128)(2,1)S(1)} %collective-permute-done.6.refs_4_), channel_id=1, source_target_pairs={{0,1},{1,0},{2,3},{3,2},{4,5},{5,4},{6,7},{7,6},{8,9},{9,8},{10,11... | collective-permute-start | bytes 688136 | tf_op jit(solution)/shard_map/ppermute | solution.py:178
  27.6 7.9 %collective-permute-start.32 = (bf16[96,1024]{1,0:T(8,128)(2,1)S(1)}, bf16[96,1024]{1,0:T(8,128)(2,1)}, u32[]{:S(2)}, u32[]{:S(2)}) collective-permute-start(bf16[96,1024]{1,0:T(8,128)(2,1)S(1)} %get-tuple-element.50), channel_id=1, source_target_pairs={{0,2},{2,0},{4,6},{6,4},{8,10},{10,8},{12,14},{14,12},{1,3},{3,1},... | collective-permute-start | bytes 589832 | tf_op jit(solution)/shard_map/ppermute | solution.py:162
  29.2 15.0 %collective-permute-start.7 = (bf16[112,1024]{1,0:T(8,128)(2,1)S(1)}, bf16[112,1024]{1,0:T(8,128)(2,1)}, u32[]{:S(2)}, u32[]{:S(2)}) collective-permute-start(bf16[112,1024]{1,0:T(8,128)(2,1)S(1)} %get-tuple-element.35), channel_id=1, source_target_pairs={{0,2},{2,0},{4,6},{6,4},{8,10},{10,8},{12,14},{14,12},{1,3},{3,1},... | collective-permute-start | bytes 688136 | tf_op jit(solution)/shard_map/ppermute | solution.py:162
  35.5 12.1 %collective-permute-start.8 = (bf16[112,1024]{1,0:T(8,128)(2,1)S(1)}, bf16[112,1024]{1,0:T(8,128)(2,1)}, u32[]{:S(2)}, u32[]{:S(2)}) collective-permute-start(bf16[112,1024]{1,0:T(8,128)(2,1)S(1)} %get-tuple-element.36), channel_id=1, source_target_pairs={{0,2},{2,0},{4,6},{6,4},{8,10},{10,8},{12,14},{14,12},{1,3},{3,1},... | collective-permute-start | bytes 688136 | tf_op jit(solution)/shard_map/ppermute | solution.py:162
  37.8 10.0 %collective-permute-start.27 = (bf16[128,1024]{1,0:T(8,128)(2,1)}, bf16[128,1024]{1,0:T(8,128)(2,1)S(1)}, u32[]{:S(2)}, u32[]{:S(2)}) collective-permute-start(bf16[128,1024]{1,0:T(8,128)(2,1)} %refs_0_.1), channel_id=1, source_target_pairs={{0,4},{2,6},{4,8},{6,10},{8,12},{10,14},{1,5},{3,7},{5,9},{7,11},{... | collective-permute-start | bytes 786440 | tf_op jit(solution)/shard_map/ppermute | solution.py:172
  43.6 17.5 %collective-permute-start.5 = (bf16[144,1024]{1,0:T(8,128)(2,1)}, bf16[144,1024]{1,0:T(8,128)(2,1)S(1)}, u32[]{:S(2)}, u32[]{:S(2)}) collective-permute-start(bf16[144,1024]{1,0:T(8,128)(2,1)} %collective-permute-done.3.refs_1_), channel_id=1, source_target_pairs={{8,12},{10,14},{9,13},{11,15},{24,28},{26,30},{25,29},{27,31}} | collective-permute-start | bytes 884744 | tf_op jit(solution)/shard_map/ppermute | solution.py:172
  44.3 18.7 %collective-permute-start.4 = (bf16[144,1024]{1,0:T(8,128)(2,1)}, bf16[144,1024]{1,0:T(8,128)(2,1)S(1)}, u32[]{:S(2)}, u32[]{:S(2)}) collective-permute-start(bf16[144,1024]{1,0:T(8,128)(2,1)} %collective-permute-done.2.refs_0_), channel_id=1, source_target_pairs={{4,0},{6,2},{5,1},{7,3},{20,16},{22,18},{21,17},{23,19}} | collective-permute-start | bytes 884744 | tf_op jit(solution)/shard_map/ppermute | solution.py:172
  46.3 13.4 %collective-permute-start.26 = (bf16[128,1024]{1,0:T(8,128)(2,1)}, bf16[128,1024]{1,0:T(8,128)(2,1)S(1)}, u32[]{:S(2)}, u32[]{:S(2)}) collective-permute-start(bf16[128,1024]{1,0:T(8,128)(2,1)} %refs_0_.1), channel_id=1, source_target_pairs={{4,0},{6,2},{8,4},{10,6},{12,8},{14,10},{5,1},{7,3},{9,5},{11,7},{... | collective-permute-start | bytes 786440 | tf_op jit(solution)/shard_map/ppermute | solution.py:172
  47.6 19.0 %collective-permute-start.15 = (bf16[112,1024]{1,0:T(8,128)(2,1)}, bf16[112,1024]{1,0:T(8,128)(2,1)S(1)}, u32[]{:S(2)}, u32[]{:S(2)}) collective-permute-start(bf16[112,1024]{1,0:T(8,128)(2,1)} %collective-permute-done.7.refs_5_), channel_id=1, source_target_pairs={{0,1},{1,0},{2,3},{3,2},{4,5},{5,4},{6,7},{7,6},{8,9},{9,8},{10,11... | collective-permute-start | bytes 688136 | tf_op jit(solution)/shard_map/ppermute | solution.py:178
  47.8 20.7 %collective-permute-start.12 = (bf16[144,1024]{1,0:T(8,128)(2,1)}, bf16[144,1024]{1,0:T(8,128)(2,1)}, u32[]{:S(2)}, u32[]{:S(2)}) collective-permute-start(bf16[144,1024]{1,0:T(8,128)(2,1)} %get-tuple-element.32.refs_2_), channel_id=1, source_target_pairs={{0,1},{1,0},{2,3},{3,2},{4,5},{5,4},{6,7},{7,6},{8,9},{9,8},{10,11... | collective-permute-start | bytes 884744 | tf_op jit(solution)/shard_map/ppermute | solution.py:178
  59.7 9.3 %collective-permute-start.29 = (bf16[128,1024]{1,0:T(8,128)(2,1)S(1)}, bf16[128,1024]{1,0:T(8,128)(2,1)}, u32[]{:S(2)}, u32[]{:S(2)}) collective-permute-start(bf16[128,1024]{1,0:T(8,128)(2,1)S(1)} %collective-permute-done.27.refs_1_.refs_2_), channel_id=1, source_target_pairs={{4,8},{6,10},{8,12},{10,14},{5,9},{7,11},{9,13},{11,15},{20,24},{2... | collective-permute-start | bytes 786440 | tf_op jit(solution)/shard_map/ppermute | solution.py:172
  61.1 9.3 %collective-permute-start.28 = (bf16[128,1024]{1,0:T(8,128)(2,1)S(1)}, bf16[128,1024]{1,0:T(8,128)(2,1)S(1)}, u32[]{:S(2)}, u32[]{:S(2)}) collective-permute-start(bf16[128,1024]{1,0:T(8,128)(2,1)S(1)} %collective-permute-done.26.refs_0_), channel_id=1, source_target_pairs={{4,0},{6,2},{8,4},{10,6},{5,1},{7,3},{9,5},{11,7},{20,16},{22,18},... | collective-permute-start | bytes 786440 | tf_op jit(solution)/shard_map/ppermute | solution.py:172
  63.0 5.8 %collective-permute-start.16 = (bf16[112,1024]{1,0:T(8,128)(2,1)}, bf16[112,1024]{1,0:T(8,128)(2,1)}, u32[]{:S(2)}, u32[]{:S(2)}) collective-permute-start(bf16[112,1024]{1,0:T(8,128)(2,1)} %collective-permute-done.8.refs_6_), channel_id=1, source_target_pairs={{0,1},{1,0},{2,3},{3,2},{4,5},{5,4},{6,7},{7,6},{8,9},{9,8},{10,11... | collective-permute-start | bytes 688136 | tf_op jit(solution)/shard_map/ppermute | solution.py:178
  67.3 8.2 %collective-permute-start.9 = (bf16[112,1024]{1,0:T(8,128)(2,1)}, bf16[112,1024]{1,0:T(8,128)(2,1)S(1)}, u32[]{:S(2)}, u32[]{:S(2)}) collective-permute-start(bf16[112,1024]{1,0:T(8,128)(2,1)} %get-tuple-element.37), channel_id=1, source_target_pairs={{0,2},{2,0},{4,6},{6,4},{8,10},{10,8},{12,14},{14,12},{1,3},{3,1},... | collective-permute-start | bytes 688136 | tf_op jit(solution)/shard_map/ppermute | solution.py:162
  68.5 34.8 %collective-permute-start.36 = (bf16[128,1024]{1,0:T(8,128)(2,1)}, bf16[128,1024]{1,0:T(8,128)(2,1)}, u32[]{:S(2)}, u32[]{:S(2)}) collective-permute-start(bf16[128,1024]{1,0:T(8,128)(2,1)} %copy-done.9), channel_id=1, source_target_pairs={{0,1},{1,0},{2,3},{3,2},{4,5},{5,4},{6,7},{7,6},{8,9},{9,8},{10,11... | collective-permute-start | bytes 786440 | tf_op jit(solution)/shard_map/ppermute | solution.py:178
  68.8 14.8 %collective-permute-start.13 = (bf16[144,1024]{1,0:T(8,128)(2,1)}, bf16[144,1024]{1,0:T(8,128)(2,1)S(1)}, u32[]{:S(2)}, u32[]{:S(2)}) collective-permute-start(bf16[144,1024]{1,0:T(8,128)(2,1)} %copy-done.1), channel_id=1, source_target_pairs={{0,1},{1,0},{2,3},{3,2},{4,5},{5,4},{6,7},{7,6},{8,9},{9,8},{10,11... | collective-permute-start | bytes 884744 | tf_op jit(solution)/shard_map/ppermute | solution.py:178
  69.0 30.8 %collective-permute-start.31 = (bf16[128,1024]{1,0:T(8,128)(2,1)}, bf16[128,1024]{1,0:T(8,128)(2,1)}, u32[]{:S(2)}, u32[]{:S(2)}) collective-permute-start(bf16[128,1024]{1,0:T(8,128)(2,1)} %collective-permute-done.29.refs_1_), channel_id=1, source_target_pairs={{8,12},{10,14},{9,13},{11,15},{24,28},{26,30},{25,29},{27,31}} | collective-permute-start | bytes 786440 | tf_op jit(solution)/shard_map/ppermute | solution.py:172
  70.4 29.5 %collective-permute-start.30 = (bf16[128,1024]{1,0:T(8,128)(2,1)S(1)}, bf16[128,1024]{1,0:T(8,128)(2,1)}, u32[]{:S(2)}, u32[]{:S(2)}) collective-permute-start(bf16[128,1024]{1,0:T(8,128)(2,1)S(1)} %collective-permute-done.28.refs_0_), channel_id=1, source_target_pairs={{4,0},{6,2},{5,1},{7,3},{20,16},{22,18},{21,17},{23,19}} | collective-permute-start | bytes 786440 | tf_op jit(solution)/shard_map/ppermute | solution.py:172
  75.5 9.8 %copy-start.15 = (bf16[112,1024]{1,0:T(8,128)(2,1)}, bf16[112,1024]{1,0:T(8,128)(2,1)S(1)}, u32[]{:S(2)}) copy-start(bf16[112,1024]{1,0:T(8,128)(2,1)S(1)} %collective-permute-done.9.refs_7_) | copy-start | bytes 688132
  75.6 9.2 %collective-permute-start.17 = (bf16[112,1024]{1,0:T(8,128)(2,1)S(1)}, bf16[112,1024]{1,0:T(8,128)(2,1)S(1)}, u32[]{:S(2)}, u32[]{:S(2)}) collective-permute-start(bf16[112,1024]{1,0:T(8,128)(2,1)S(1)} %collective-permute-done.9.refs_7_), channel_id=1, source_target_pairs={{0,1},{1,0},{2,3},{3,2},{4,5},{5,4},{6,7},{7,6},{8,9},{9,8},{10,11... | collective-permute-start | bytes 688136 | tf_op jit(solution)/shard_map/ppermute | solution.py:178
  79.9 19.9 %copy-start.11 = (bf16[128,1024]{1,0:T(8,128)(2,1)}, bf16[128,1024]{1,0:T(8,128)(2,1)S(1)}, u32[]{:S(2)}) copy-start(bf16[128,1024]{1,0:T(8,128)(2,1)S(1)} %get-tuple-element.47.refs_1_) | copy-start | bytes 786436
  84.3 24.8 %collective-permute-start.40 = (bf16[96,1024]{1,0:T(8,128)(2,1)}, bf16[96,1024]{1,0:T(8,128)(2,1)S(1)}, u32[]{:S(2)}, u32[]{:S(2)}) collective-permute-start(bf16[96,1024]{1,0:T(8,128)(2,1)} %collective-permute-done.32.refs_4_), channel_id=1, source_target_pairs={{0,1},{1,0},{2,3},{3,2},{4,5},{5,4},{6,7},{7,6},{8,9},{9,8},{10,11... | collective-permute-start | bytes 589832 | tf_op jit(solution)/shard_map/ppermute | solution.py:178
  84.8 24.3 %collective-permute-start.33 = (bf16[96,1024]{1,0:T(8,128)(2,1)S(1)}, bf16[96,1024]{1,0:T(8,128)(2,1)}, u32[]{:S(2)}, u32[]{:S(2)}) collective-permute-start(bf16[96,1024]{1,0:T(8,128)(2,1)S(1)} %get-tuple-element.51), channel_id=1, source_target_pairs={{0,2},{2,0},{4,6},{6,4},{8,10},{10,8},{12,14},{14,12},{1,3},{3,1},... | collective-permute-start | bytes 589832 | tf_op jit(solution)/shard_map/ppermute | solution.py:162
  99.8 9.9 %collective-permute-start.37 = (bf16[128,1024]{1,0:T(8,128)(2,1)S(1)}, bf16[128,1024]{1,0:T(8,128)(2,1)S(1)}, u32[]{:S(2)}, u32[]{:S(2)}) collective-permute-start(bf16[128,1024]{1,0:T(8,128)(2,1)S(1)} %get-tuple-element.47.refs_1_), channel_id=1, source_target_pairs={{0,1},{1,0},{2,3},{3,2},{4,5},{5,4},{6,7},{7,6},{8,9},{9,8},{10,11... | collective-permute-start | bytes 786440 | tf_op jit(solution)/shard_map/ppermute | solution.py:178
  99.9 9.7 %collective-permute-start.34 = (bf16[96,1024]{1,0:T(8,128)(2,1)S(1)}, bf16[96,1024]{1,0:T(8,128)(2,1)}, u32[]{:S(2)}, u32[]{:S(2)}) collective-permute-start(bf16[96,1024]{1,0:T(8,128)(2,1)S(1)} %get-tuple-element.52), channel_id=1, source_target_pairs={{0,2},{2,0},{4,6},{6,4},{8,10},{10,8},{12,14},{14,12},{1,3},{3,1},... | collective-permute-start | bytes 589832 | tf_op jit(solution)/shard_map/ppermute | solution.py:162
  103.4 8.2 %collective-permute-start.35 = (bf16[96,1024]{1,0:T(8,128)(2,1)S(1)}, bf16[96,1024]{1,0:T(8,128)(2,1)}, u32[]{:S(2)}, u32[]{:S(2)}) collective-permute-start(bf16[96,1024]{1,0:T(8,128)(2,1)S(1)} %get-tuple-element.53), channel_id=1, source_target_pairs={{0,2},{2,0},{4,6},{6,4},{8,10},{10,8},{12,14},{14,12},{1,3},{3,1},... | collective-permute-start | bytes 589832 | tf_op jit(solution)/shard_map/ppermute | solution.py:162
  109.1 5.6 %collective-permute-start.41 = (bf16[96,1024]{1,0:T(8,128)(2,1)}, bf16[96,1024]{1,0:T(8,128)(2,1)}, u32[]{:S(2)}, u32[]{:S(2)}) collective-permute-start(bf16[96,1024]{1,0:T(8,128)(2,1)} %collective-permute-done.33.refs_5_), channel_id=1, source_target_pairs={{0,1},{1,0},{2,3},{3,2},{4,5},{5,4},{6,7},{7,6},{8,9},{9,8},{10,11... | collective-permute-start | bytes 589832 | tf_op jit(solution)/shard_map/ppermute | solution.py:178
  109.1 5.6 %collective-permute-start.38 = (bf16[128,1024]{1,0:T(8,128)(2,1)}, bf16[128,1024]{1,0:T(8,128)(2,1)S(1)}, u32[]{:S(2)}, u32[]{:S(2)}) collective-permute-start(bf16[128,1024]{1,0:T(8,128)(2,1)} %get-tuple-element.48.refs_2_), channel_id=1, source_target_pairs={{0,1},{1,0},{2,3},{3,2},{4,5},{5,4},{6,7},{7,6},{8,9},{9,8},{10,11... | collective-permute-start | bytes 786440 | tf_op jit(solution)/shard_map/ppermute | solution.py:178
  109.6 5.1 %collective-permute-start.42 = (bf16[96,1024]{1,0:T(8,128)(2,1)}, bf16[96,1024]{1,0:T(8,128)(2,1)}, u32[]{:S(2)}, u32[]{:S(2)}) collective-permute-start(bf16[96,1024]{1,0:T(8,128)(2,1)} %collective-permute-done.34.refs_6_), channel_id=1, source_target_pairs={{0,1},{1,0},{2,3},{3,2},{4,5},{5,4},{6,7},{7,6},{8,9},{9,8},{10,11... | collective-permute-start | bytes 589832 | tf_op jit(solution)/shard_map/ppermute | solution.py:178
  109.7 5.1 %collective-permute-start.39 = (bf16[128,1024]{1,0:T(8,128)(2,1)S(1)}, bf16[128,1024]{1,0:T(8,128)(2,1)}, u32[]{:S(2)}, u32[]{:S(2)}) collective-permute-start(bf16[128,1024]{1,0:T(8,128)(2,1)S(1)} %get-tuple-element.49.refs_3_), channel_id=1, source_target_pairs={{0,1},{1,0},{2,3},{3,2},{4,5},{5,4},{6,7},{7,6},{8,9},{9,8},{10,11... | collective-permute-start | bytes 786440 | tf_op jit(solution)/shard_map/ppermute | solution.py:178
  111.5 3.2 %collective-permute-start.43 = (bf16[96,1024]{1,0:T(8,128)(2,1)}, bf16[96,1024]{1,0:T(8,128)(2,1)}, u32[]{:S(2)}, u32[]{:S(2)}) collective-permute-start(bf16[96,1024]{1,0:T(8,128)(2,1)} %collective-permute-done.35.refs_7_), channel_id=1, source_target_pairs={{0,1},{1,0},{2,3},{3,2},{4,5},{5,4},{6,7},{7,6},{8,9},{9,8},{10,11... | collective-permute-start | bytes 589832 | tf_op jit(solution)/shard_map/ppermute | solution.py:178
  133.8 7.2 %collective-permute-start.52 = (f32[896]{0:T(1024)S(1)}, f32[896]{0:T(1024)S(1)}, u32[]{:S(2)}, u32[]{:S(2)}) collective-permute-start(f32[896]{0:T(1024)S(1)} %get-tuple-element.58), channel_id=1, source_target_pairs={{0,1},{1,0},{2,3},{3,2},{4,5},{5,4},{6,7},{7,6},{8,9},{9,8},{10,11... | collective-permute-start | bytes 10760 | tf_op jit(solution)/shard_map/ppermute | solution.py:178
  134.4 18.3 %collective-permute-start.18 = (bf16[896,1024]{1,0:T(8,128)(2,1)S(1)}, bf16[896,1024]{1,0:T(8,128)(2,1)S(1)}, u32[]{:S(2)}, u32[]{:S(2)}) collective-permute-start(bf16[896,1024]{1,0:T(8,128)(2,1)S(1)} %convolution_convert_fusion.3), channel_id=1, source_target_pairs={{0,1},{1,0},{2,3},{3,2},{4,5},{5,4},{6,7},{7,6},{8,9},{9,8},{10,11... | collective-permute-start | bytes 5505032 | tf_op jit(solution)/shard_map/ppermute | solution.py:178
  135.7 22.4 %collective-permute-start.44 = (bf16[896,1024]{1,0:T(8,128)(2,1)S(1)}, bf16[896,1024]{1,0:T(8,128)(2,1)S(1)}, u32[]{:S(2)}, u32[]{:S(2)}) collective-permute-start(bf16[896,1024]{1,0:T(8,128)(2,1)S(1)} %add_convert_fusion), channel_id=1, source_target_pairs={{0,1},{1,0},{2,3},{3,2},{4,5},{5,4},{6,7},{7,6},{8,9},{9,8},{10,11... | collective-permute-start | bytes 5505032 | tf_op jit(solution)/shard_map/ppermute | solution.py:178
  141.0 3.7 %collective-permute-start.53 = (f32[384]{0:T(512)S(1)}, f32[384]{0:T(512)S(1)}, u32[]{:S(2)}, u32[]{:S(2)}) collective-permute-start(f32[384]{0:T(512)S(1)} %slice.156), channel_id=1, source_target_pairs={{0,2},{2,0},{4,6},{6,4},{8,10},{10,8},{12,14},{14,12},{1,3},{3,1},... | collective-permute-start | bytes 4616 | tf_op jit(solution)/shard_map/ppermute | solution.py:162
  144.9 5.4 %collective-permute-start.56 = (f32[2,128]{1,0:T(2,128)S(1)}, f32[2,128]{1,0:T(2,128)S(1)}, u32[]{:S(2)}, u32[]{:S(2)}) collective-permute-start(f32[2,128]{1,0:T(2,128)S(1)} %pad_maximum_fusion.4), channel_id=1, source_target_pairs={{0,4},{2,6},{4,8},{6,10},{8,12},{10,14},{12,0},{14,2},{1,5},{3,7},... | collective-permute-start | bytes 3080 | tf_op jit(solution)/shard_map/ppermute | solution.py:165
  147.6 4.5 %collective-permute-start.55 = (f32[2,128]{1,0:T(2,128)S(1)}, f32[2,128]{1,0:T(2,128)S(1)}, u32[]{:S(2)}, u32[]{:S(2)}) collective-permute-start(f32[2,128]{1,0:T(2,128)S(1)} %pad_maximum_fusion.3), channel_id=1, source_target_pairs={{0,8},{2,10},{4,12},{6,14},{8,0},{10,2},{12,4},{14,6},{1,9},{3,11}... | collective-permute-start | bytes 3080 | tf_op jit(solution)/shard_map/ppermute | solution.py:165
  147.6 4.4 %collective-permute-start.54 = (f32[2,128]{1,0:T(2,128)S(1)}, f32[2,128]{1,0:T(2,128)S(1)}, u32[]{:S(2)}, u32[]{:S(2)}) collective-permute-start(f32[2,128]{1,0:T(2,128)S(1)} %pad_maximum_fusion.2), channel_id=1, source_target_pairs={{0,12},{2,14},{4,0},{6,2},{8,4},{10,6},{12,8},{14,10},{1,13},{3,15... | collective-permute-start | bytes 3080 | tf_op jit(solution)/shard_map/ppermute | solution.py:165
  153.9 32.2 %collective-permute-start.25 = (bf16[96,1024]{1,0:T(8,128)(2,1)S(1)}, bf16[96,1024]{1,0:T(8,128)(2,1)S(1)}, u32[]{:S(2)}, u32[]{:S(2)}) collective-permute-start(bf16[96,1024]{1,0:T(8,128)(2,1)S(1)} %get-tuple-element.66), channel_id=1, source_target_pairs={{0,2},{2,0},{4,6},{6,4},{8,10},{10,8},{12,14},{14,12},{1,3},{3,1},... | collective-permute-start | bytes 589832 | tf_op jit(solution)/shard_map/ppermute | solution.py:162
  155.5 10.5 %collective-permute-start.23 = (bf16[96,1024]{1,0:T(8,128)(2,1)S(1)}, bf16[96,1024]{1,0:T(8,128)(2,1)S(1)}, u32[]{:S(2)}, u32[]{:S(2)}) collective-permute-start(bf16[96,1024]{1,0:T(8,128)(2,1)S(1)} %get-tuple-element.67), channel_id=1, source_target_pairs={{0,2},{2,0},{4,6},{6,4},{8,10},{10,8},{12,14},{14,12},{1,3},{3,1},... | collective-permute-start | bytes 589832 | tf_op jit(solution)/shard_map/ppermute | solution.py:162
  156.0 20.2 %collective-permute-start.21 = (bf16[96,1024]{1,0:T(8,128)(2,1)S(1)}, bf16[96,1024]{1,0:T(8,128)(2,1)S(1)}, u32[]{:S(2)}, u32[]{:S(2)}) collective-permute-start(bf16[96,1024]{1,0:T(8,128)(2,1)S(1)} %get-tuple-element.68), channel_id=1, source_target_pairs={{0,2},{2,0},{4,6},{6,4},{8,10},{10,8},{12,14},{14,12},{1,3},{3,1},... | collective-permute-start | bytes 589832 | tf_op jit(solution)/shard_map/ppermute | solution.py:162
  157.5 16.9 %collective-permute-start.19 = (bf16[96,1024]{1,0:T(8,128)(2,1)S(1)}, bf16[96,1024]{1,0:T(8,128)(2,1)S(1)}, u32[]{:S(2)}, u32[]{:S(2)}) collective-permute-start(bf16[96,1024]{1,0:T(8,128)(2,1)S(1)} %get-tuple-element.69), channel_id=1, source_target_pairs={{0,2},{2,0},{4,6},{6,4},{8,10},{10,8},{12,14},{14,12},{1,3},{3,1},... | collective-permute-start | bytes 589832 | tf_op jit(solution)/shard_map/ppermute | solution.py:162
  159.3 20.8 %collective-permute-start.49 = (bf16[96,1024]{1,0:T(8,128)(2,1)S(1)}, bf16[96,1024]{1,0:T(8,128)(2,1)S(1)}, u32[]{:S(2)}, u32[]{:S(2)}) collective-permute-start(bf16[96,1024]{1,0:T(8,128)(2,1)S(1)} %get-tuple-element.63), channel_id=1, source_target_pairs={{0,2},{2,0},{4,6},{6,4},{8,10},{10,8},{12,14},{14,12},{1,3},{3,1},... | collective-permute-start | bytes 589832 | tf_op jit(solution)/shard_map/ppermute | solution.py:162
  166.0 15.4 %collective-permute-start.47 = (bf16[96,1024]{1,0:T(8,128)(2,1)S(1)}, bf16[96,1024]{1,0:T(8,128)(2,1)S(1)}, u32[]{:S(2)}, u32[]{:S(2)}) collective-permute-start(bf16[96,1024]{1,0:T(8,128)(2,1)S(1)} %get-tuple-element.64), channel_id=1, source_target_pairs={{0,2},{2,0},{4,6},{6,4},{8,10},{10,8},{12,14},{14,12},{1,3},{3,1},... | collective-permute-start | bytes 589832 | tf_op jit(solution)/shard_map/ppermute | solution.py:162
  174.5 9.9 %collective-permute-start.45 = (bf16[96,1024]{1,0:T(8,128)(2,1)S(1)}, bf16[96,1024]{1,0:T(8,128)(2,1)S(1)}, u32[]{:S(2)}, u32[]{:S(2)}) collective-permute-start(bf16[96,1024]{1,0:T(8,128)(2,1)S(1)} %get-tuple-element.65), channel_id=1, source_target_pairs={{0,2},{2,0},{4,6},{6,4},{8,10},{10,8},{12,14},{14,12},{1,3},{3,1},... | collective-permute-start | bytes 589832 | tf_op jit(solution)/shard_map/ppermute | solution.py:162
  176.2 13.5 %collective-permute-start.20 = (bf16[128,1024]{1,0:T(8,128)(2,1)S(1)}, bf16[128,1024]{1,0:T(8,128)(2,1)S(1)}, u32[]{:S(2)}, u32[]{:S(2)}) collective-permute-start(bf16[128,1024]{1,0:T(8,128)(2,1)S(1)} %fusion.35), channel_id=1, source_target_pairs={{0,12},{2,14},{4,0},{6,2},{8,4},{10,6},{12,8},{14,10},{1,13},{3,15... | collective-permute-start | bytes 786440 | tf_op jit(solution)/shard_map/ppermute | solution.py:165
  180.1 28.2 %collective-permute-start.22 = (bf16[128,1024]{1,0:T(8,128)(2,1)S(1)}, bf16[128,1024]{1,0:T(8,128)(2,1)S(1)}, u32[]{:S(2)}, u32[]{:S(2)}) collective-permute-start(bf16[128,1024]{1,0:T(8,128)(2,1)S(1)} %fusion.34), channel_id=1, source_target_pairs={{0,8},{2,10},{4,12},{6,14},{8,0},{10,2},{12,4},{14,6},{1,9},{3,11}... | collective-permute-start | bytes 786440 | tf_op jit(solution)/shard_map/ppermute | solution.py:165
  181.5 26.8 %collective-permute-start.24 = (bf16[128,1024]{1,0:T(8,128)(2,1)S(1)}, bf16[128,1024]{1,0:T(8,128)(2,1)S(1)}, u32[]{:S(2)}, u32[]{:S(2)}) collective-permute-start(bf16[128,1024]{1,0:T(8,128)(2,1)S(1)} %fusion.33), channel_id=1, source_target_pairs={{0,4},{2,6},{4,8},{6,10},{8,12},{10,14},{12,0},{14,2},{1,5},{3,7},... | collective-permute-start | bytes 786440 | tf_op jit(solution)/shard_map/ppermute | solution.py:165
  184.3 24.9 %collective-permute-start.51 = (bf16[96,1024]{1,0:T(8,128)(2,1)S(1)}, bf16[96,1024]{1,0:T(8,128)(2,1)S(1)}, u32[]{:S(2)}, u32[]{:S(2)}) collective-permute-start(bf16[96,1024]{1,0:T(8,128)(2,1)S(1)} %get-tuple-element.62), channel_id=1, source_target_pairs={{0,2},{2,0},{4,6},{6,4},{8,10},{10,8},{12,14},{14,12},{1,3},{3,1},... | collective-permute-start | bytes 589832 | tf_op jit(solution)/shard_map/ppermute | solution.py:162
  186.1 23.2 %collective-permute-start.46 = (bf16[128,1024]{1,0:T(8,128)(2,1)S(1)}, bf16[128,1024]{1,0:T(8,128)(2,1)S(1)}, u32[]{:S(2)}, u32[]{:S(2)}) collective-permute-start(bf16[128,1024]{1,0:T(8,128)(2,1)S(1)} %fusion.30), channel_id=1, source_target_pairs={{0,12},{2,14},{4,0},{6,2},{8,4},{10,6},{12,8},{14,10},{1,13},{3,15... | collective-permute-start | bytes 786440 | tf_op jit(solution)/shard_map/ppermute | solution.py:165
  189.7 28.2 %collective-permute-start.48 = (bf16[128,1024]{1,0:T(8,128)(2,1)S(1)}, bf16[128,1024]{1,0:T(8,128)(2,1)S(1)}, u32[]{:S(2)}, u32[]{:S(2)}) collective-permute-start(bf16[128,1024]{1,0:T(8,128)(2,1)S(1)} %fusion.29), channel_id=1, source_target_pairs={{0,8},{2,10},{4,12},{6,14},{8,0},{10,2},{12,4},{14,6},{1,9},{3,11}... | collective-permute-start | bytes 786440 | tf_op jit(solution)/shard_map/ppermute | solution.py:165
  208.3 9.6 %collective-permute-start.50 = (bf16[128,1024]{1,0:T(8,128)(2,1)S(1)}, bf16[128,1024]{1,0:T(8,128)(2,1)S(1)}, u32[]{:S(2)}, u32[]{:S(2)}) collective-permute-start(bf16[128,1024]{1,0:T(8,128)(2,1)S(1)} %fusion.28), channel_id=1, source_target_pairs={{0,4},{2,6},{4,8},{6,10},{8,12},{10,14},{12,0},{14,2},{1,5},{3,7},... | collective-permute-start | bytes 786440 | tf_op jit(solution)/shard_map/ppermute | solution.py:165
  (38 other events, 80.2 us)

commit v3 on v1

v3 whole, which is shorter than its diff:
```python
import functools

import jax
import jax.numpy as jnp
import numpy as np
from jax import lax
from jax.experimental import pallas as pl
from jax.experimental.pallas import tpu as pltpu
from jax.sharding import PartitionSpec as P

BF = jnp.bfloat16
F32 = jnp.float32
I32 = jnp.int32
TAIL = 16


def dot(a, b, contract):
    return lax.dot_general(a, b, (contract, ((), ())), preferred_element_type=F32)


def split_three(values):
    high = lax.reduce_precision(values, 8, 7)
    rest = values - high
    middle = lax.reduce_precision(rest, 8, 7)
    low = rest - middle
    return [part.astype(BF) for part in (high, middle, low)]


def slot_source(lines, z, slot):
    if z < lines // 2:
        above = lines - 1 - z
        return ("down", slot) if slot <= above else ("up", slot - above)
    return ("up", slot) if slot <= z else ("down", slot - z)


def slot_place(lines, z, slot):
    if slot == 0:
        return 0
    direction, distance = slot_source(lines, z, slot)
    return distance if direction == "up" else lines - distance


def vmem_params(*shapes):
    total = sum(int(np.prod(x.shape)) * x.dtype.itemsize for x in shapes)
    return pltpu.CompilerParams(vmem_limit_bytes=int(total * 1.3) + 3 * 1024 * 1024)


def shape_of(shape, dtype=BF):
    return jax.ShapeDtypeStruct(shape, dtype)


def local_call(kernel, outs, args, scratch=(), in_specs=None, flops=10**8):
    moved = sum(int(np.prod(x.shape)) * x.dtype.itemsize for x in tuple(args) + tuple(outs))
    return pl.pallas_call(
        kernel,
        out_shape=tuple(outs),
        in_specs=in_specs or [SMEM_SPEC] + [VMEM_SPEC] * (len(args) - 1),
        out_specs=(VMEM_SPEC,) * len(outs),
        scratch_shapes=list(scratch),
        compiler_params=vmem_params(*args, *outs),
        cost_estimate=pl.CostEstimate(flops=flops, bytes_accessed=moved, transcendentals=0),
    )(*args)


SMEM_SPEC = pl.BlockSpec(memory_space=pltpu.SMEM)
VMEM_SPEC = pl.BlockSpec(memory_space=pltpu.VMEM)


def token_slot_kernel(count, which_at, tokens, part_rows, capacity, padded, info, *refs):
    blocks = refs[:count]
    compact, place, own_parts, table, parts = refs[count:]
    width = compact.shape[1]
    per_row = width // tokens
    for i, block in enumerate(blocks):
        @pl.when(info[which_at] == i)
        def _():
            table[...] = block[tokens:, :].astype(F32)

    def parts_of(expert):
        row, lane = expert // per_row, pl.multiple_of((expert % per_row) * tokens, tokens)
        parts[...] = jnp.zeros_like(parts)
        for p in range(3):
            found = lax.broadcasted_iota(I32, (table.shape[0], tokens), 0) == p * part_rows + row
            parts[p:p + 1, :] = jnp.sum(
                jnp.where(found, table[:, pl.ds(lane, tokens)], 0.0), axis=0, keepdims=True)
        return parts[...]

    own_parts[...] = parts_of(info[0]).astype(BF)
    theirs = parts_of(info[1])
    named = jnp.sum(theirs, axis=0, keepdims=True) > 0.0
    row_at = lax.broadcasted_iota(I32, (tokens, tokens), 0)
    column_at = lax.broadcasted_iota(I32, (tokens, tokens), 1)
    until = (row_at <= column_at).astype(F32).astype(BF)
    ones = jnp.broadcast_to(named.astype(F32), (TAIL, tokens)).astype(BF)
    rank = jnp.dot(ones, until, preferred_element_type=F32)[:1, :].astype(I32) - 1
    picked = ((row_at == rank) & named & (row_at < capacity)).astype(F32).astype(BF)
    place[...] = picked[:padded, :]
    for i, block in enumerate(blocks):
        @pl.when(info[which_at] == i)
        def _():
            compact[:padded, :] = jnp.dot(
                place[...], block[:tokens, :], preferred_element_type=F32).astype(BF)
    compact[padded:, :] = jnp.zeros((TAIL, width), BF)
    compact[padded:, :tokens] = dot(theirs.astype(BF), picked, ((1,), (1,))).astype(BF)


def grad_slot_kernel(count, which_at, info, *refs):
    blocks = refs[:count]
    place, compact = refs[count:]
    for i, block in enumerate(blocks):
        @pl.when(info[which_at] == i)
        def _():
            compact[...] = jnp.dot(
                place[...], block[...], preferred_element_type=F32).astype(BF)


def line_kernel(counts, which_at, place_at, tokens, info, *refs):
    whole = refs[-1]
    at = 0
    for slot, count in enumerate(counts):
        first = pl.multiple_of(info[place_at + slot] * tokens, tokens)
        for i in range(count):
            block = refs[at + i]

            @pl.when(info[which_at + slot] == i)
            def _():
                whole[pl.ds(first, tokens), :] = block[:tokens, :]
        at += count


def rows_copies(lines, tokens, padded, width, place_at, info, dense, compact, rows, sems):
    core = info[2]
    copies = []
    for half in range(2):
        lane = pl.multiple_of((core if half == 0 else 1 - core) * width, width)
        copies.append(pltpu.make_async_copy(
            dense[half], rows.at[pl.ds(0, lines * tokens), pl.ds(lane, width)],
            sems.at[len(copies)]))
        for j in range(lines):
            first = pl.multiple_of(lines * tokens + info[place_at + j] * padded, 16)
            copies.append(pltpu.make_async_copy(
                compact[half][j].at[pl.ds(0, padded), :],
                rows.at[pl.ds(first, padded), pl.ds(lane, width)],
                sems.at[len(copies)]))
    for copy in copies:
        copy.start()
    return copies


def token_rows_kernel(lines, tokens, padded, width, place_at, info, *refs):
    n = lines
    dense = refs[:2]
    compact = (refs[2:2 + n], refs[2 + n:2 + 2 * n])
    own_parts = refs[2 + 2 * n:2 + 3 * n]
    places = refs[2 + 3 * n:2 + 4 * n]
    rows, weights, ring, sems = refs[2 + 4 * n:]
    copies = rows_copies(n, tokens, padded, width, place_at, info, dense, compact, rows, sems)
    eye = (lax.broadcasted_iota(I32, (tokens, tokens), 0)
           == lax.broadcasted_iota(I32, (tokens, tokens), 1))
    for j in range(n):
        at = info[place_at + j]
        for first, size, tail in (
            (0, tokens, own_parts[j][...]),
            (n * tokens, padded, compact[0][j][padded:, :tokens]),
        ):
            row = jnp.sum(tail.astype(F32), axis=0, keepdims=True)
            column = jnp.sum(jnp.where(eye, row, 0.0), axis=1, keepdims=True)
            weights[pl.ds(pl.multiple_of(first + at * size, 16), size), :] = column[:size]
        ring[at] = places[j][...]
    for copy in copies:
        copy.wait()


def grad_rows_kernel(lines, tokens, padded, width, place_at, info, *refs):
    n = lines
    dense = refs[:2]
    compact = (refs[2:2 + n], refs[2 + n:2 + 2 * n])
    rows, sems = refs[2 + 2 * n:]
    for copy in rows_copies(n, tokens, padded, width, place_at, info, dense, compact, rows, sems):
        copy.wait()


def pack_kernel(lines, tokens, padded, info, both, tails, *messages):
    for k in range(lines):
        at = lines * tokens + k * padded
        messages[k][:padded, :] = both[at:at + padded, :].astype(BF)
        messages[k][padded:, :] = jnp.zeros((TAIL, both.shape[1]), BF)
        messages[k][padded:, :tokens] = tails[k].astype(BF)


def home_kernel(k, tokens, padded, info, both, back, ring, tails, message):
    place = ring[k]
    block = both[k * tokens:(k + 1) * tokens, :] + dot(place, back[:padded, :], ((0,), (0,)))
    message[:tokens, :] = block.astype(BF)
    message[tokens:, :] = jnp.zeros((TAIL, both.shape[1]), BF)
    theirs = dot(back[padded:, :padded], place, ((1,), (0,)))
    message[tokens:, :tokens] = jnp.concatenate(
        [tails[k][:8], theirs[:8]], axis=0).astype(BF)


def per_device(tokens, expert_ids, router_weights, gate_weight, up_weight, down_weight, grad_out):
    token_count, half_width = tokens.shape
    top_count = expert_ids.shape[1]
    experts = lax.axis_size("expert")
    capacity = min(token_count, 3 * token_count * top_count // (2 * experts))
    padded = -(-capacity // 16) * 16
    lines = experts // 2
    mine = lax.axis_index("expert")
    core = lax.axis_index("tensor")
    at_line = mine // 2
    peer = mine + 1 - 2 * (mine % 2)

    def over_pair(x):
        return lax.ppermute(x, "expert", [(i, i + 1 - 2 * (i % 2)) for i in range(experts)])

    def over_line(x, k):
        return lax.ppermute(
            x, "expert",
            [(i, ((i // 2 + k) % lines) * 2 + i % 2) for i in range(experts)],
        )

    def hop(x, k, step):
        low, high = (k - 1, lines - 1) if step > 0 else (1, lines - k + 1)
        return lax.ppermute(
            x, "expert",
            [(2 * z + y, 2 * (z + step) + y) for z in range(low, high) for y in range(2)],
        )

    def over_core(x):
        return lax.ppermute(x, "tensor", [(0, 1), (1, 0)])

    chosen = expert_ids[:, :, None] == jnp.arange(experts, dtype=I32)[None, None, :]
    table = jnp.sum(jnp.where(chosen, router_weights[:, :, None], 0.0), axis=1).T
    part_rows = experts * token_count // half_width
    parts = jnp.concatenate([p.reshape(part_rows, half_width) for p in split_three(table)])
    tail = -(-3 * part_rows // TAIL) * TAIL
    parts = jnp.pad(parts, ((0, tail - 3 * part_rows), (0, 0)))
    first = jnp.concatenate([tokens, parts])

    def along_line(start):
        up, down = {0: start}, {0: start}
        for k in range(1, lines):
            up[k] = hop(up[k - 1], k, 1)
            down[k] = hop(down[k - 1], k, -1)
        return up, down

    up, down = along_line(first)

    def sources_of(slot):
        if slot == 0:
            return [(None, 0)], np.zeros(lines, np.int32)
        sources = [slot_source(lines, z, slot) for z in range(lines)]
        names = sorted(set(sources))
        return names, np.array([names.index(n) for n in sources], np.int32)

    names_of = [sources_of(slot)[0] for slot in range(lines)]
    which_of = np.stack([sources_of(slot)[1] for slot in range(lines)], 1)
    place_of = np.array([[slot_place(lines, z, n) for n in range(lines)] for z in range(lines)], np.int32)
    known = jnp.asarray(np.concatenate([which_of, place_of], 1))[at_line]
    info = jnp.concatenate([jnp.stack([mine, peer, core]).astype(I32), known])
    which_at, place_at = 3, 3 + lines

    def candidates(slot, ups, downs):
        return [(downs if d == "down" else ups)[n] for d, n in names_of[slot]]

    counts = [len(n) for n in names_of]
    compact_shape = shape_of((padded + TAIL, half_width))
    packed, compact_blocks, places, own_parts = [], [], [], []
    for slot in range(lines):
        blocks = candidates(slot, up, down)
        compact, place, parts = local_call(
            functools.partial(token_slot_kernel, len(blocks), which_at + slot, token_count,
                              part_rows, capacity, padded),
            (compact_shape, shape_of((padded, token_count)), shape_of((TAIL, token_count))),
            (info, *blocks),
            (pltpu.VMEM((tail, half_width), F32), pltpu.VMEM((TAIL, token_count), F32)),
        )
        packed.append(compact)
        compact_blocks.append(over_pair(compact))
        places.append(place)
        own_parts.append(parts)

    def lined(ups, downs):
        blocks = [x for slot in range(lines) for x in candidates(slot, ups, downs)]
        (whole,) = local_call(
            functools.partial(line_kernel, counts, which_at, place_at, token_count),
            (shape_of((lines * token_count, half_width)),), (info, *blocks), flops=10**6)
        return whole

    dense_rows = lines * token_count
    row_count = lines * (token_count + padded)
    rows_shape = shape_of((row_count, 2 * half_width))
    sems = (pltpu.SemaphoreType.DMA((2 * (lines + 1),)),)
    sizes = (lines, token_count, padded, half_width, place_at)

    dense_own = lined(up, down)
    rows, weights, ring = local_call(
        functools.partial(token_rows_kernel, *sizes),
        (rows_shape, shape_of((row_count, 1), F32), shape_of((lines, padded, token_count))),
        (info, dense_own, over_core(dense_own), *compact_blocks,
         *[over_core(x) for x in compact_blocks], *own_parts, *places),
        sems, flops=10**6)

    held_grad, _ = lax.optimization_barrier((grad_out, packed[min(2, lines - 1)]))
    grad_ups, grad_downs = along_line(held_grad)
    grad_compact = []
    for slot in range(lines):
        blocks = candidates(slot, grad_ups, grad_downs)
        (compact,) = local_call(
            functools.partial(grad_slot_kernel, len(blocks), which_at + slot),
            (shape_of((padded, half_width)),), (info, *blocks, places[slot]))
        grad_compact.append(over_pair(compact))

    gate_local = gate_weight[0]
    up_local = up_weight[0]
    down_local = down_weight[0]
    gate = dot(rows, gate_local, ((1,), (0,)))
    upward = dot(rows, up_local, ((1,), (0,)))
    sig = jax.nn.sigmoid(gate)
    hidden = gate * sig * upward
    scaled_hidden = (weights * hidden).astype(BF)

    def summed_over_cores(make):
        sent = over_core(make(1 - core).astype(BF))
        return make(core) + sent.astype(F32)

    def half_of(x, which, axis):
        return lax.dynamic_slice_in_dim(x, which * half_width, half_width, axis)

    message_shape = shape_of((token_count + TAIL, half_width))

    def crossed(both, compact_tails):
        messages = local_call(
            functools.partial(pack_kernel, lines, token_count, padded),
            (compact_shape,) * lines, (info, both, compact_tails), flops=10**6)
        return [over_pair(m) for m in messages]

    def to_home(both, backs, dense_tails):
        return [
            local_call(
                functools.partial(home_kernel, k, token_count, padded),
                (message_shape,), (info, both, backs[k], ring, dense_tails))[0]
            for k in range(lines)
        ]

    def go_home(blocks):
        return [blocks[0]] + [over_line(blocks[k], lines - k) for k in range(1, lines)]

    def summed(blocks):
        total = blocks[0][:token_count].astype(F32)
        for block in blocks[1:]:
            total = total + block[:token_count].astype(F32)
        return total.astype(BF)

    no_tails = jnp.zeros((lines, TAIL, token_count), F32)
    out_both = summed_over_cores(
        lambda c: dot(scaled_hidden, half_of(down_local, c, 1), ((1,), (0,))))
    out_backs = crossed(out_both, no_tails)
    out_blocks = to_home(out_both, out_backs, no_tails)
    layer_out = summed(go_home(out_blocks))

    grad_own = lined(grad_ups, grad_downs)
    grad_own, _ = lax.optimization_barrier((grad_own, out_both))
    (grads,) = local_call(
        functools.partial(grad_rows_kernel, *sizes), (rows_shape,),
        (info, grad_own, over_core(grad_own), *grad_compact, *[over_core(x) for x in grad_compact]),
        sems, flops=10**6)
    grad_plain = dot(grads, down_local, ((1,), (1,)))
    row_value = jnp.sum(hidden * grad_plain, axis=1)
    grad_hidden = weights * grad_plain
    grad_gate = (grad_hidden * upward * sig * (1.0 + gate * (1.0 - sig))).astype(BF)
    grad_up = (grad_hidden * gate * sig).astype(BF)
    in_both = summed_over_cores(
        lambda c: dot(grad_gate, half_of(gate_local, c, 0), ((1,), (1,)))
        + dot(grad_up, half_of(up_local, c, 0), ((1,), (1,))))
    in_both, _ = lax.optimization_barrier((in_both, out_blocks))

    def tails_of(values):
        values = jnp.pad(values, ((0, 0), (0, token_count - values.shape[1])))
        parts = jnp.stack([p.astype(F32) for p in split_three(values)], axis=1)
        return jnp.pad(parts, ((0, 0), (0, TAIL - 3), (0, 0)))

    dense_tails = tails_of(row_value[:dense_rows].reshape(lines, token_count))
    compact_tails = tails_of(row_value[dense_rows:].reshape(lines, padded))
    in_backs = crossed(in_both, compact_tails)
    in_blocks = to_home(in_both, in_backs, dense_tails)
    came_home = go_home(in_blocks)
    input_grad = summed(came_home)

    down_grad = dot(scaled_hidden, grads, ((0,), (0,))).astype(BF)
    gate_grad = dot(rows, grad_gate, ((0,), (0,))).astype(BF)
    up_grad = dot(rows, grad_up, ((0,), (0,))).astype(BF)

    held = []
    for block in came_home:
        rows_back = block[token_count:, :token_count].astype(F32)
        held.append(jnp.stack([jnp.sum(rows_back[:8], axis=0), jnp.sum(rows_back[8:], axis=0)]))
    flat = jnp.stack(held).reshape(experts, token_count)
    place = (expert_ids // 2 - at_line) % lines
    slot = place * 2 + ((expert_ids % 2) != (mine % 2)).astype(I32)
    match = slot[:, :, None] == jnp.arange(experts, dtype=I32)[None, None, :]
    half_value = jnp.sum(jnp.where(match, flat.T[:, None, :], 0.0), axis=2)
    weight_grad = half_value + over_core(half_value)
    return (layer_out, input_grad, weight_grad, gate_grad[None], up_grad[None], down_grad[None])


def solution(mesh):
    in_specs = (
        P(("group", "expert"), "tensor"),
        P(("group", "expert"), None),
        P(("group", "expert"), None),
        P("expert", None, "tensor"),
        P("expert", None, "tensor"),
        P("expert", "tensor", None),
        P(("group", "expert"), "tensor"),
    )
    out_specs = (
        P(("group", "expert"), "tensor"),
        P(("group", "expert"), "tensor"),
        P(("group", "expert"), None),
        P(("group", "expert"), None, "tensor"),
        P(("group", "expert"), None, "tensor"),
        P(("group", "expert"), "tensor", None),
    )
    return jax.shard_map(
        per_device, mesh=mesh, in_specs=in_specs, out_specs=out_specs, check_vma=False
    )
```

time: 206 us -> 236 us (1.15)
  the two profiles are of different devices: /device:TPU:0 before, /device:TPU:9 now
where the time goes in v3:
time: 236 us; the launch traced here: 234 us
  waiting for transfers between devices  102 us (43%)
  starting transfers between devices  60.9 us (26%)
  matrix products  30.9 us (13%)
  Pallas kernels  20.8 us (9%)
  local copies, waits for them, and re-layouts  13.4 us (6%)
  other arithmetic  4.65 us (2%)
    ppermute x16, waiting for transfers between devices, over_pair(): lax.ppermute(x, 'expert', [(i, i + 1 - 2 * (i % 2)) for i in range(expert...  51.1 us
    dot_general x12, matrix products, dot(): lax.dot_general(a, b, (contract, ((), ())), preferred_element_type=F32)  30.9 us
    ppermute x12, starting transfers between devices, hop(): lax.ppermute(x, 'expert', [(2 * z + y, 2 * (z + step) + y) for z in range...  26.8 us
    ppermute x6, waiting for transfers between devices, over_line(): lax.ppermute(x, 'expert', [(i, (i // 2 + k) % lines * 2 + i % 2) for i in...  26.4 us
    ppermute x12, waiting for transfers between devices, hop(): lax.ppermute(x, 'expert', [(2 * z + y, 2 * (z + step) + y) for z in range...  24.2 us
    pallas_call x22, Pallas kernels, local_call(): pl.pallas_call(kernel, out_shape=tuple(outs), in_specs=in_specs or [SMEM_...  20.8 us
    ppermute x13, starting transfers between devices, over_core(): return lax.ppermute(x, 'tensor', [(0, 1), (1, 0)])  16.4 us
    ppermute x16, starting transfers between devices, over_pair(): lax.ppermute(x, 'expert', [(i, i + 1 - 2 * (i % 2)) for i in range(expert...  14.1 us
  transfers between devices with their start and end apart: 47, of which 26 were waited for; matrix products, arithmetic and copies ran while one was open for 6% of the time, Pallas kernels for 6%

profile of v3, /device:TPU:9, one launch (start us, length us, event | category | flops | bytes accessed | tf_op | source)
XLA Modules:
  0.0 233.9 jit_solution(10483995024286226418)
XLA Ops:
  2.5 3.2 %collective-permute-start.1 = (bf16[144,1024]{1,0:T(8,128)(2,1)S(1)}, bf16[144,1024]{1,0:T(8,128)(2,1)S(1)}, u32[]{:S(2)}, u32[]{:S(2)}) collective-permute-start(bf16[144,1024]{1,0:T(8,128)(2,1)S(1)} %pad_maximum_fusion.refs_0_), channel_id=1, source_target_pairs={{0,4},{2,6},{4,8},{6,10},{8,12},{10,14},{1,5},{3,7},{5,9},{7,11},{... | collective-permute-start | bytes 884744 | tf_op jit(solution)/shard_map/ppermute | solution.py:224
  5.7 2.1 collective-permute-start
  7.8 4.5 %collective-permute-done.1.refs_2_.refs_7_.refs_1_ = bf16[144,1024]{1,0:T(8,128)(2,1)S(1)} collective-permute-done((bf16[144,1024]{1,0:T(8,128)(2,1)S(1)}, bf16[144,1024]{1,0:T(8,128)(2,1)S(1)}, u32[]{:S(2)}, u32[]{:S(2)}) %collective-permute-start.1) | collective-permute-done | bytes 294944 | tf_op jit(solution)/shard_map/ppermute | solution.py:224
  12.3 3.2 %collective-permute-start.3 = (bf16[144,1024]{1,0:T(8,128)(2,1)S(1)}, bf16[144,1024]{1,0:T(8,128)(2,1)S(1)}, u32[]{:S(2)}, u32[]{:S(2)}) collective-permute-start(bf16[144,1024]{1,0:T(8,128)(2,1)S(1)} %collective-permute-done.1.refs_2_.refs_7_.refs_1_), channel_id=1, source_target_pairs={{4,8},{6,10},{8,12},{10,14},{5,9},{7,11},{9,13},{11,15},{20,24},{2... | collective-permute-start | bytes 884744 | tf_op jit(solution)/shard_map/ppermute | solution.py:224
  15.5 1.9 collective-permute-start.2
  17.4 2.8 %collective-permute-done.3.refs_4_.refs_1_ = bf16[144,1024]{1,0:T(8,128)(2,1)S(1)} collective-permute-done((bf16[144,1024]{1,0:T(8,128)(2,1)S(1)}, bf16[144,1024]{1,0:T(8,128)(2,1)S(1)}, u32[]{:S(2)}, u32[]{:S(2)}) %collective-permute-start.3) | collective-permute-done | bytes 294944 | tf_op jit(solution)/shard_map/ppermute | solution.py:224
  21.6 2.5 %collective-permute-done.2.refs_3_.refs_0_ = bf16[144,1024]{1,0:T(8,128)(2,1)S(1)} collective-permute-done((bf16[144,1024]{1,0:T(8,128)(2,1)S(1)}, bf16[144,1024]{1,0:T(8,128)(2,1)S(1)}, u32[]{:S(2)}, u32[]{:S(2)}) %collective-permute-start.2) | collective-permute-done | bytes 294944 | tf_op jit(solution)/shard_map/ppermute | solution.py:224
  24.1 2.8 %collective-permute-start.4 = (bf16[144,1024]{1,0:T(8,128)(2,1)S(1)}, bf16[144,1024]{1,0:T(8,128)(2,1)}, u32[]{:S(2)}, u32[]{:S(2)}) collective-permute-start(bf16[144,1024]{1,0:T(8,128)(2,1)S(1)} %collective-permute-done.2.refs_3_.refs_0_), channel_id=1, source_target_pairs={{4,0},{6,2},{5,1},{7,3},{20,16},{22,18},{21,17},{23,19}} | collective-permute-start | bytes 884744 | tf_op jit(solution)/shard_map/ppermute | solution.py:224
  33.8 3.6 %collective-permute-start.6 = (bf16[512,1024]{1,0:T(8,128)(2,1)S(1)}, bf16[512,1024]{1,0:T(8,128)(2,1)}, u32[]{:S(2)}, u32[]{:S(2)}) collective-permute-start(bf16[512,1024]{1,0:T(8,128)(2,1)S(1)} %shard_map.127.refs_0_), channel_id=1, source_target_pairs={{0,1},{1,0},{2,3},{3,2},{4,5},{5,4},{6,7},{7,6},{8,9},{9,8},{10,11... | collective-permute-start | bytes 3145736 | tf_op jit(solution)/shard_map/ppermute | solution.py:230
  38.4 1.3 collective-permute-start.7
  42.0 1.3 collective-permute-start.9
  43.3 1.5 shard_map.131
  45.7 1.2 collective-permute-start.11
  46.9 3.8 %collective-permute-done.8.refs_3_ = bf16[112,1024]{1,0:T(8,128)(2,1)} collective-permute-done((bf16[112,1024]{1,0:T(8,128)(2,1)S(1)}, bf16[112,1024]{1,0:T(8,128)(2,1)}, u32[]{:S(2)}, u32[]{:S(2)}) %collective-permute-start.8) | collective-permute-done | bytes 229408 | tf_op jit(solution)/shard_map/ppermute | solution.py:214
  50.7 1.2 collective-permute-start.12
  51.9 3.7 %collective-permute-done.9.refs_4_ = bf16[112,1024]{1,0:T(8,128)(2,1)} collective-permute-done((bf16[112,1024]{1,0:T(8,128)(2,1)S(1)}, bf16[112,1024]{1,0:T(8,128)(2,1)}, u32[]{:S(2)}, u32[]{:S(2)}) %collective-permute-start.9) | collective-permute-done | bytes 229408 | tf_op jit(solution)/shard_map/ppermute | solution.py:214
  55.6 1.2 collective-permute-start.13
  56.8 3.6 %collective-permute-done.10.refs_5_ = bf16[112,1024]{1,0:T(8,128)(2,1)S(1)} collective-permute-done((bf16[112,1024]{1,0:T(8,128)(2,1)S(1)}, bf16[112,1024]{1,0:T(8,128)(2,1)S(1)}, u32[]{:S(2)}, u32[]{:S(2)}) %collective-permute-start.10) | collective-permute-done | bytes 229408 | tf_op jit(solution)/shard_map/ppermute | solution.py:214
  65.2 2.5 %shard_map.132 = (bf16[896,2048]{1,0:T(8,128)(2,1)S(1)}, f32[896,1]{1,0:T(8,128)S(1)}, bf16[4,96,128]{2,1,0:T(8,128)(2,1)S(1)}) custom-call(s32[11]{0:T(128)S(1)} %pad_add_fusion.info, bf16[512,1024]{1,0:T(8,128)(2,1)S(1)} %shard_map.127.refs_0_, bf16[512,1024]{1,0:T(8,128)(2,1)} %collective-permute-done.6.refs_1_, ...), custom_call_target="tpu_custom_call" | custom-call | flops 1000000 | bytes 7818796 | tf_op jit(solution)/shard_map/pallas_call | solution.py:54
  67.7 1.8 copy-done.21
  69.7 4.5 %fusion.7 = f32[896,384]{0,1:T(8,128)S(1)} fusion(bf16[896,2048]{1,0:T(8,128)(2,1)} %copy-done.21, bf16[1,2048,384]{2,1,0:T(8,128)(2,1)} %param.11), kind=kOutput, calls=%fused_computation.14 | convolution fusion | flops 1409286144 | bytes 6619136 | tf_op jit(solution)/shard_map/dot_general | solution.py:18
  74.3 3.0 %multiply_convert_fusion.2 = (bf16[896,384]{0,1:T(8,128)(2,1)S(1)}, f32[896,384]{0,1:T(8,128)}) fusion(f32[896]{0:T(1024)S(1)} %reduce, f32[896,384]{0,1:T(8,128)S(1)} %fusion.7, bf16[896,2048]{1,0:T(8,128)(2,1)S(1)} %copy-done.22, bf16[1,2048,384]{2,1,0:T(8,128)(2,1)S(1)} %copy-done.28), kind=kOutput, calls=%fused_computation.19 | convolution fusion | flops 1411694592 | bytes 8687104 | tf_op jit(solution)/shard_map/dot_general | solution.py:18
  77.3 2.4 %convolution_convert_fusion.3 = bf16[896,1024]{1,0:T(8,128)(2,1)} fusion(bf16[896,384]{0,1:T(8,128)(2,1)S(1)} %get-tuple-element.78, bf16[1,384,2048]{2,1,0:T(8,128)(2,1)S(1)} %copy-done, s32[]{:T(128)S(6)} %select_n.54), kind=kOutput, calls=%fused_computation.9 | convolution fusion | flops 705560576 | bytes 3309572 | tf_op jit(solution)/shard_map/dot_general | solution.py:18
  79.9 2.1 collective-permute-start.24
  82.1 3.4 %collective-permute-start.23 = (bf16[128,1024]{1,0:T(8,128)(2,1)S(1)}, bf16[128,1024]{1,0:T(8,128)(2,1)S(1)}, u32[]{:S(2)}, u32[]{:S(2)}) collective-permute-start(bf16[128,1024]{1,0:T(8,128)(2,1)S(1)} %copy-done.9), channel_id=1, source_target_pairs={{4,0},{6,2},{8,4},{10,6},{12,8},{14,10},{5,1},{7,3},{9,5},{11,7},{... | collective-permute-start | bytes 786440 | tf_op jit(solution)/shard_map/ppermute | solution.py:224
  85.5 4.5 %collective-permute-done.24.refs_2_.refs_7_.refs_1_ = bf16[128,1024]{1,0:T(8,128)(2,1)S(1)} collective-permute-done((bf16[128,1024]{1,0:T(8,128)(2,1)S(1)}, bf16[128,1024]{1,0:T(8,128)(2,1)S(1)}, u32[]{:S(2)}, u32[]{:S(2)}) %collective-permute-start.24) | collective-permute-done | bytes 262176 | tf_op jit(solution)/shard_map/ppermute | solution.py:224
  89.9 1.6 collective-permute-start.26
  92.3 2.6 %collective-permute-start.25 = (bf16[128,1024]{1,0:T(8,128)(2,1)S(1)}, bf16[128,1024]{1,0:T(8,128)(2,1)S(1)}, u32[]{:S(2)}, u32[]{:S(2)}) collective-permute-start(bf16[128,1024]{1,0:T(8,128)(2,1)S(1)} %collective-permute-done.23.refs_1_.refs_5_.refs_0_), channel_id=1, source_target_pairs={{4,0},{6,2},{8,4},{10,6},{5,1},{7,3},{9,5},{11,7},{20,16},{22,18},... | collective-permute-start | bytes 786440 | tf_op jit(solution)/shard_map/ppermute | solution.py:224
  96.7 4.2 %collective-permute-done.25.refs_3_.refs_0_ = bf16[128,1024]{1,0:T(8,128)(2,1)S(1)} collective-permute-done((bf16[128,1024]{1,0:T(8,128)(2,1)S(1)}, bf16[128,1024]{1,0:T(8,128)(2,1)S(1)}, u32[]{:S(2)}, u32[]{:S(2)}) %collective-permute-start.25) | collective-permute-done | bytes 262176 | tf_op jit(solution)/shard_map/ppermute | solution.py:224
  100.9 2.5 %collective-permute-start.27 = (bf16[128,1024]{1,0:T(8,128)(2,1)S(1)}, bf16[128,1024]{1,0:T(8,128)(2,1)S(1)}, u32[]{:S(2)}, u32[]{:S(2)}) collective-permute-start(bf16[128,1024]{1,0:T(8,128)(2,1)S(1)} %collective-permute-done.25.refs_3_.refs_0_), channel_id=1, source_target_pairs={{4,0},{6,2},{5,1},{7,3},{20,16},{22,18},{21,17},{23,19}} | collective-permute-start | bytes 786440 | tf_op jit(solution)/shard_map/ppermute | solution.py:224
  103.5 3.3 %collective-permute-done.27.refs_6_.refs_1_ = bf16[128,1024]{1,0:T(8,128)(2,1)S(1)} collective-permute-done((bf16[128,1024]{1,0:T(8,128)(2,1)S(1)}, bf16[128,1024]{1,0:T(8,128)(2,1)S(1)}, u32[]{:S(2)}, u32[]{:S(2)}) %collective-permute-start.27) | collective-permute-done | bytes 262176 | tf_op jit(solution)/shard_map/ppermute | solution.py:224
  107.4 2.7 %convert_add_fusion.1.both = f32[896,1024]{1,0:T(8,128)S(1)} fusion(bf16[896,1024]{1,0:T(8,128)(2,1)} %collective-permute-done.15, bf16[896,384]{0,1:T(8,128)(2,1)S(1)} %copy-done.25, bf16[1,384,2048]{2,1,0:T(8,128)(2,1)S(1)} %copy-done, s32[]{:T(128)S(6)} %select_n.53), kind=kOutput, calls=%fused_computation.2 | convolution fusion | flops 706478080 | bytes 6979588 | tf_op jit(solution)/shard_map/dot_general | solution.py:18
  110.1 3.3 %collective-permute-start.29 = (bf16[512,1024]{1,0:T(8,128)(2,1)S(1)}, bf16[512,1024]{1,0:T(8,128)(2,1)S(1)}, u32[]{:S(2)}, u32[]{:S(2)}) collective-permute-start(bf16[512,1024]{1,0:T(8,128)(2,1)S(1)} %shard_map.138.refs_0_), channel_id=1, source_target_pairs={{0,1},{1,0},{2,3},{3,2},{4,5},{5,4},{6,7},{7,6},{8,9},{9,8},{10,11... | collective-permute-start | bytes 3145736 | tf_op jit(solution)/shard_map/ppermute | solution.py:230
  114.0 1.3 collective-permute-start.17
  115.5 1.2 collective-permute-start.21
  119.3 1.9 collective-permute-done.17.back
  121.3 1.2 collective-permute-start.31
  122.5 3.7 %collective-permute-done.19.back = bf16[112,1024]{1,0:T(8,128)(2,1)S(1)} collective-permute-done((bf16[112,1024]{1,0:T(8,128)(2,1)S(1)}, bf16[112,1024]{1,0:T(8,128)(2,1)S(1)}, u32[]{:S(2)}, u32[]{:S(2)}) %collective-permute-start.19) | collective-permute-done | bytes 229408 | tf_op jit(solution)/shard_map/ppermute | solution.py:214
  126.2 1.2 collective-permute-start.32
  127.4 3.7 %collective-permute-done.21.back = bf16[112,1024]{1,0:T(8,128)(2,1)S(1)} collective-permute-done((bf16[112,1024]{1,0:T(8,128)(2,1)S(1)}, bf16[112,1024]{1,0:T(8,128)(2,1)S(1)}, u32[]{:S(2)}, u32[]{:S(2)}) %collective-permute-start.21) | collective-permute-done | bytes 229408 | tf_op jit(solution)/shard_map/ppermute | solution.py:214
  131.1 1.2 collective-permute-start.16
  135.3 4.2 %collective-permute-done.31.refs_3_ = bf16[96,1024]{1,0:T(8,128)(2,1)S(1)} collective-permute-done((bf16[96,1024]{1,0:T(8,128)(2,1)S(1)}, bf16[96,1024]{1,0:T(8,128)(2,1)S(1)}, u32[]{:S(2)}, u32[]{:S(2)}) %collective-permute-start.31) | collective-permute-done | bytes 196640 | tf_op jit(solution)/shard_map/ppermute | solution.py:214
  140.4 3.4 %collective-permute-done.32.refs_4_ = bf16[96,1024]{1,0:T(8,128)(2,1)S(1)} collective-permute-done((bf16[96,1024]{1,0:T(8,128)(2,1)S(1)}, bf16[96,1024]{1,0:T(8,128)(2,1)S(1)}, u32[]{:S(2)}, u32[]{:S(2)}) %collective-permute-start.32) | collective-permute-done | bytes 196640 | tf_op jit(solution)/shard_map/ppermute | solution.py:214
  143.7 2.2 collective-permute-start.18
  146.7 1.9 collective-permute-done.16.back
  148.6 1.2 collective-permute-start.33
  150.7 3.5 %collective-permute-done.33.refs_5_ = bf16[96,1024]{1,0:T(8,128)(2,1)S(1)} collective-permute-done((bf16[96,1024]{1,0:T(8,128)(2,1)S(1)}, bf16[96,1024]{1,0:T(8,128)(2,1)S(1)}, u32[]{:S(2)}, u32[]{:S(2)}) %collective-permute-start.33) | collective-permute-done | bytes 196640 | tf_op jit(solution)/shard_map/ppermute | solution.py:214
  154.2 1.7 collective-permute-start.34
  156.0 3.9 %collective-permute-done.20 = bf16[144,1024]{1,0:T(8,128)(2,1)S(1)} collective-permute-done((bf16[144,1024]{1,0:T(8,128)(2,1)S(1)}, bf16[144,1024]{1,0:T(8,128)(2,1)S(1)}, u32[]{:S(2)}, u32[]{:S(2)}) %collective-permute-start.20) | collective-permute-done | bytes 294944 | tf_op jit(solution)/shard_map/ppermute | solution.py:217
  159.9 1.6 collective-permute-start.36
  161.5 4.6 %collective-permute-done.18 = bf16[144,1024]{1,0:T(8,128)(2,1)S(1)} collective-permute-done((bf16[144,1024]{1,0:T(8,128)(2,1)S(1)}, bf16[144,1024]{1,0:T(8,128)(2,1)S(1)}, u32[]{:S(2)}, u32[]{:S(2)}) %collective-permute-start.18) | collective-permute-done | bytes 294944 | tf_op jit(solution)/shard_map/ppermute | solution.py:217
  167.6 1.4 shard_map.143
  169.2 2.4 %multiply_reduce_fusion = (f32[896]{0:T(1024)S(1)}, bf16[896,384]{0,1:T(8,128)(2,1)S(1)}, bf16[896,384]{0,1:T(8,128)(2,1)S(1)}) fusion(f32[896,384]{0,1:T(8,128)S(1)} %copy-done.33, f32[896,384]{0,1:T(8,128)S(1)} %copy-done.32, f32[896]{0:T(1024)S(1)} %reduce, bf16[896,2048]{1,0:T(8,128)(2,1)S(1)} %shard_map.143, bf16[1,384,2048]{2,1,0:T(8,128)(2,1)S(1)} %copy-done), kind=kOutput, calls=%fused_computation.16 | convolution fusion | flops 1415478400 | bytes 9378816 | tf_op jit(solution)/shard_map/dot_general | solution.py:18
  171.7 2.4 %fusion.10 = f32[896,1024]{1,0:T(8,128)S(1)} fusion(bf16[896,384]{0,1:T(8,128)(2,1)S(1)} %get-tuple-element.67, bf16[1,2048,384]{2,1,0:T(8,128)(2,1)} %param.11, s32[]{:T(128)S(6)} %select_n.54), kind=kOutput, calls=%fused_computation.23 | convolution fusion | flops 704643072 | bytes 5144580 | tf_op jit(solution)/shard_map/dot_general | solution.py:18
  174.2 1.2 add_convert_fusion
  178.0 2.9 %fusion.2 = bf16[1,384,2048]{2,1,0:T(8,128)(2,1)} fusion(bf16[896,384]{0,1:T(8,128)(2,1)S(1)} %copy-done.26, bf16[896,2048]{1,0:T(8,128)(2,1)S(1)} %copy-done.2), kind=kOutput, calls=%fused_computation.8 | convolution fusion | flops 1410072576 | bytes 5931008 | tf_op jit(solution)/shard_map/dot_general | solution.py:18
  180.9 3.5 %fusion = bf16[1,2048,384]{2,1,0:T(8,128)(2,1)} fusion(bf16[896,2048]{1,0:T(8,128)(2,1)S(1)} %copy-done.23, bf16[896,384]{0,1:T(8,128)(2,1)S(1)} %get-tuple-element.67), kind=kOutput, calls=%fused_computation.6 | convolution fusion | flops 1410072576 | bytes 5931008 | tf_op jit(solution)/shard_map/dot_general | solution.py:18
  184.4 3.5 %fusion.1 = bf16[1,2048,384]{2,1,0:T(8,128)(2,1)} fusion(bf16[896,2048]{1,0:T(8,128)(2,1)S(1)} %copy-done.23, bf16[896,384]{0,1:T(8,128)(2,1)S(1)} %get-tuple-element.68), kind=kOutput, calls=%fused_computation.7 | convolution fusion | flops 1410072576 | bytes 5931008 | tf_op jit(solution)/shard_map/dot_general | solution.py:18
  187.9 1.2 convert_add_fusion.both
  189.7 1.3 collective-permute-start.39
  191.3 1.3 collective-permute-start.40
  192.9 8.9 %collective-permute-done.44.back = bf16[112,1024]{1,0:T(8,128)(2,1)S(1)} collective-permute-done((bf16[112,1024]{1,0:T(8,128)(2,1)S(1)}, bf16[112,1024]{1,0:T(8,128)(2,1)S(1)}, u32[]{:S(2)}, u32[]{:S(2)}) %collective-permute-start.44) | collective-permute-done | bytes 229408 | tf_op jit(solution)/shard_map/ppermute | solution.py:214
  203.4 8.1 %collective-permute-done.42.back = bf16[112,1024]{1,0:T(8,128)(2,1)S(1)} collective-permute-done((bf16[112,1024]{1,0:T(8,128)(2,1)S(1)}, bf16[112,1024]{1,0:T(8,128)(2,1)S(1)}, u32[]{:S(2)}, u32[]{:S(2)}) %collective-permute-start.42) | collective-permute-done | bytes 229408 | tf_op jit(solution)/shard_map/ppermute | solution.py:214
  213.8 17.9 %collective-permute-done.43 = bf16[144,1024]{1,0:T(8,128)(2,1)S(1)} collective-permute-done((bf16[144,1024]{1,0:T(8,128)(2,1)S(1)}, bf16[144,1024]{1,0:T(8,128)(2,1)S(1)}, u32[]{:S(2)}, u32[]{:S(2)}) %collective-permute-start.43) | collective-permute-done | bytes 294944 | tf_op jit(solution)/shard_map/ppermute | solution.py:217
  (172 shorter events, 43.1 us)
Async XLA Ops:
  0.6 76.7 %copy-start = (bf16[1,384,2048]{2,1,0:T(8,128)(2,1)S(1)}, bf16[1,384,2048]{2,1,0:T(8,128)(2,1)}, u32[]{:S(2)}) copy-start(bf16[1,384,2048]{2,1,0:T(8,128)(2,1)} %param.13) | copy-start | bytes 4718596
  2.5 9.8 %collective-permute-start.1 = (bf16[144,1024]{1,0:T(8,128)(2,1)S(1)}, bf16[144,1024]{1,0:T(8,128)(2,1)S(1)}, u32[]{:S(2)}, u32[]{:S(2)}) collective-permute-start(bf16[144,1024]{1,0:T(8,128)(2,1)S(1)} %pad_maximum_fusion.refs_0_), channel_id=1, source_target_pairs={{0,4},{2,6},{4,8},{6,10},{8,12},{10,14},{1,5},{3,7},{5,9},{7,11},{... | collective-permute-start | bytes 884744 | tf_op jit(solution)/shard_map/ppermute | solution.py:224
  5.7 9.8 %collective-permute-start = (bf16[144,1024]{1,0:T(8,128)(2,1)S(1)}, bf16[144,1024]{1,0:T(8,128)(2,1)S(1)}, u32[]{:S(2)}, u32[]{:S(2)}) collective-permute-start(bf16[144,1024]{1,0:T(8,128)(2,1)S(1)} %pad_maximum_fusion.refs_0_), channel_id=1, source_target_pairs={{4,0},{6,2},{8,4},{10,6},{12,8},{14,10},{5,1},{7,3},{9,5},{11,7},{... | collective-permute-start | bytes 884744 | tf_op jit(solution)/shard_map/ppermute | solution.py:224
  12.3 7.9 %collective-permute-start.3 = (bf16[144,1024]{1,0:T(8,128)(2,1)S(1)}, bf16[144,1024]{1,0:T(8,128)(2,1)S(1)}, u32[]{:S(2)}, u32[]{:S(2)}) collective-permute-start(bf16[144,1024]{1,0:T(8,128)(2,1)S(1)} %collective-permute-done.1.refs_2_.refs_7_.refs_1_), channel_id=1, source_target_pairs={{4,8},{6,10},{8,12},{10,14},{5,9},{7,11},{9,13},{11,15},{20,24},{2... | collective-permute-start | bytes 884744 | tf_op jit(solution)/shard_map/ppermute | solution.py:224
  15.5 8.6 %collective-permute-start.2 = (bf16[144,1024]{1,0:T(8,128)(2,1)S(1)}, bf16[144,1024]{1,0:T(8,128)(2,1)S(1)}, u32[]{:S(2)}, u32[]{:S(2)}) collective-permute-start(bf16[144,1024]{1,0:T(8,128)(2,1)S(1)} %collective-permute-done.refs_1_.refs_5_.refs_0_), channel_id=1, source_target_pairs={{4,0},{6,2},{8,4},{10,6},{5,1},{7,3},{9,5},{11,7},{20,16},{22,18},... | collective-permute-start | bytes 884744 | tf_op jit(solution)/shard_map/ppermute | solution.py:224
  20.2 8.1 %collective-permute-start.5 = (bf16[144,1024]{1,0:T(8,128)(2,1)S(1)}, bf16[144,1024]{1,0:T(8,128)(2,1)S(1)}, u32[]{:S(2)}, u32[]{:S(2)}) collective-permute-start(bf16[144,1024]{1,0:T(8,128)(2,1)S(1)} %collective-permute-done.3.refs_4_.refs_1_), channel_id=1, source_target_pairs={{8,12},{10,14},{9,13},{11,15},{24,28},{26,30},{25,29},{27,31}} | collective-permute-start | bytes 884744 | tf_op jit(solution)/shard_map/ppermute | solution.py:224
  24.1 5.7 %collective-permute-start.4 = (bf16[144,1024]{1,0:T(8,128)(2,1)S(1)}, bf16[144,1024]{1,0:T(8,128)(2,1)}, u32[]{:S(2)}, u32[]{:S(2)}) collective-permute-start(bf16[144,1024]{1,0:T(8,128)(2,1)S(1)} %collective-permute-done.2.refs_3_.refs_0_), channel_id=1, source_target_pairs={{4,0},{6,2},{5,1},{7,3},{20,16},{22,18},{21,17},{23,19}} | collective-permute-start | bytes 884744 | tf_op jit(solution)/shard_map/ppermute | solution.py:224
  33.8 28.8 %collective-permute-start.6 = (bf16[512,1024]{1,0:T(8,128)(2,1)S(1)}, bf16[512,1024]{1,0:T(8,128)(2,1)}, u32[]{:S(2)}, u32[]{:S(2)}) collective-permute-start(bf16[512,1024]{1,0:T(8,128)(2,1)S(1)} %shard_map.127.refs_0_), channel_id=1, source_target_pairs={{0,1},{1,0},{2,3},{3,2},{4,5},{5,4},{6,7},{7,6},{8,9},{9,8},{10,11... | collective-permute-start | bytes 3145736 | tf_op jit(solution)/shard_map/ppermute | solution.py:230
  38.4 7.2 %collective-permute-start.7 = (bf16[112,1024]{1,0:T(8,128)(2,1)S(1)}, bf16[112,1024]{1,0:T(8,128)(2,1)S(1)}, u32[]{:S(2)}, u32[]{:S(2)}) collective-permute-start(bf16[112,1024]{1,0:T(8,128)(2,1)S(1)} %get-tuple-element.32), channel_id=1, source_target_pairs={{0,2},{2,0},{4,6},{6,4},{8,10},{10,8},{12,14},{14,12},{1,3},{3,1},... | collective-permute-start | bytes 688136 | tf_op jit(solution)/shard_map/ppermute | solution.py:214
  40.7 27.0 %copy-start.14 = (bf16[96,128]{1,0:T(8,128)(2,1)}, bf16[96,128]{1,0:T(8,128)(2,1)S(1)}, u32[]{:S(2)}) copy-start(bf16[96,128]{1,0:T(8,128)(2,1)S(1)} %get-tuple-element.41.refs_15_.refs_2_) | copy-start | bytes 73732
  40.7 10.0 %collective-permute-start.8 = (bf16[112,1024]{1,0:T(8,128)(2,1)S(1)}, bf16[112,1024]{1,0:T(8,128)(2,1)}, u32[]{:S(2)}, u32[]{:S(2)}) collective-permute-start(bf16[112,1024]{1,0:T(8,128)(2,1)S(1)} %get-tuple-element.33), channel_id=1, source_target_pairs={{0,2},{2,0},{4,6},{6,4},{8,10},{10,8},{12,14},{14,12},{1,3},{3,1},... | collective-permute-start | bytes 688136 | tf_op jit(solution)/shard_map/ppermute | solution.py:214
  42.0 25.7 %copy-start.16 = (bf16[96,128]{1,0:T(8,128)(2,1)}, bf16[96,128]{1,0:T(8,128)(2,1)S(1)}, u32[]{:S(2)}) copy-start(bf16[96,128]{1,0:T(8,128)(2,1)S(1)} %get-tuple-element.42.refs_16_.refs_2_) | copy-start | bytes 73732
  42.0 13.6 %collective-permute-start.9 = (bf16[112,1024]{1,0:T(8,128)(2,1)S(1)}, bf16[112,1024]{1,0:T(8,128)(2,1)}, u32[]{:S(2)}, u32[]{:S(2)}) collective-permute-start(bf16[112,1024]{1,0:T(8,128)(2,1)S(1)} %get-tuple-element.34), channel_id=1, source_target_pairs={{0,2},{2,0},{4,6},{6,4},{8,10},{10,8},{12,14},{14,12},{1,3},{3,1},... | collective-permute-start | bytes 688136 | tf_op jit(solution)/shard_map/ppermute | solution.py:214
  45.4 15.0 %collective-permute-start.10 = (bf16[112,1024]{1,0:T(8,128)(2,1)S(1)}, bf16[112,1024]{1,0:T(8,128)(2,1)S(1)}, u32[]{:S(2)}, u32[]{:S(2)}) collective-permute-start(bf16[112,1024]{1,0:T(8,128)(2,1)S(1)} %get-tuple-element.35), channel_id=1, source_target_pairs={{0,2},{2,0},{4,6},{6,4},{8,10},{10,8},{12,14},{14,12},{1,3},{3,1},... | collective-permute-start | bytes 688136 | tf_op jit(solution)/shard_map/ppermute | solution.py:214
  45.7 16.2 %collective-permute-start.11 = (bf16[112,1024]{1,0:T(8,128)(2,1)S(1)}, bf16[112,1024]{1,0:T(8,128)(2,1)S(1)}, u32[]{:S(2)}, u32[]{:S(2)}) collective-permute-start(bf16[112,1024]{1,0:T(8,128)(2,1)S(1)} %collective-permute-done.7.refs_2_), channel_id=1, source_target_pairs={{0,1},{1,0},{2,3},{3,2},{4,5},{5,4},{6,7},{7,6},{8,9},{9,8},{10,11... | collective-permute-start | bytes 688136 | tf_op jit(solution)/shard_map/ppermute | solution.py:230
  50.7 11.9 %collective-permute-start.12 = (bf16[112,1024]{1,0:T(8,128)(2,1)}, bf16[112,1024]{1,0:T(8,128)(2,1)}, u32[]{:S(2)}, u32[]{:S(2)}) collective-permute-start(bf16[112,1024]{1,0:T(8,128)(2,1)} %collective-permute-done.8.refs_3_), channel_id=1, source_target_pairs={{0,1},{1,0},{2,3},{3,2},{4,5},{5,4},{6,7},{7,6},{8,9},{9,8},{10,11... | collective-permute-start | bytes 688136 | tf_op jit(solution)/shard_map/ppermute | solution.py:230
  55.6 7.0 %collective-permute-start.13 = (bf16[112,1024]{1,0:T(8,128)(2,1)}, bf16[112,1024]{1,0:T(8,128)(2,1)}, u32[]{:S(2)}, u32[]{:S(2)}) collective-permute-start(bf16[112,1024]{1,0:T(8,128)(2,1)} %collective-permute-done.9.refs_4_), channel_id=1, source_target_pairs={{0,1},{1,0},{2,3},{3,2},{4,5},{5,4},{6,7},{7,6},{8,9},{9,8},{10,11... | collective-permute-start | bytes 688136 | tf_op jit(solution)/shard_map/ppermute | solution.py:230
  60.4 2.2 collective-permute-start.14
  69.7 4.5 %copy-start.22 = (bf16[896,2048]{1,0:T(8,128)(2,1)S(1)}, bf16[896,2048]{1,0:T(8,128)(2,1)}, u32[]{:S(2)}) copy-start(bf16[896,2048]{1,0:T(8,128)(2,1)} %copy-done.21) | copy-start | bytes 11010052
  69.7 4.5 %copy-start.28 = (bf16[1,2048,384]{2,1,0:T(8,128)(2,1)S(1)}, bf16[1,2048,384]{2,1,0:T(8,128)(2,1)}, u32[]{:S(2)}) copy-start(bf16[1,2048,384]{2,1,0:T(8,128)(2,1)} %param.12) | copy-start | bytes 4718596
  74.2 3.0 %copy-start.31 = (f32[896,384]{0,1:T(8,128)}, f32[896,384]{0,1:T(8,128)S(1)}, u32[]{:S(2)}) copy-start(f32[896,384]{0,1:T(8,128)S(1)} %fusion.7) | copy-start | bytes 4128772
  77.3 2.4 %copy-start.24 = (bf16[896,384]{0,1:T(8,128)(2,1)}, bf16[896,384]{0,1:T(8,128)(2,1)S(1)}, u32[]{:S(2)}) copy-start(bf16[896,384]{0,1:T(8,128)(2,1)S(1)} %get-tuple-element.78) | copy-start | bytes 2064388
  77.3 2.6 %copy-start.9 = (bf16[128,1024]{1,0:T(8,128)(2,1)S(1)}, bf16[128,1024]{1,0:T(8,128)(2,1)}, u32[]{:S(2)}) copy-start(bf16[128,1024]{1,0:T(8,128)(2,1)} %refs_0_.1) | copy-start | bytes 786436
  79.7 27.7 %collective-permute-start.15 = (bf16[896,1024]{1,0:T(8,128)(2,1)}, bf16[896,1024]{1,0:T(8,128)(2,1)}, u32[]{:S(2)}, u32[]{:S(2)}) collective-permute-start(bf16[896,1024]{1,0:T(8,128)(2,1)} %convolution_convert_fusion.3), channel_id=1, source_target_pairs={{0,1},{1,0},{2,3},{3,2},{4,5},{5,4},{6,7},{7,6},{8,9},{9,8},{10,11... | collective-permute-start | bytes 5505032 | tf_op jit(solution)/shard_map/ppermute | solution.py:230
  79.9 10.0 %collective-permute-start.24 = (bf16[128,1024]{1,0:T(8,128)(2,1)S(1)}, bf16[128,1024]{1,0:T(8,128)(2,1)S(1)}, u32[]{:S(2)}, u32[]{:S(2)}) collective-permute-start(bf16[128,1024]{1,0:T(8,128)(2,1)S(1)} %copy-done.9), channel_id=1, source_target_pairs={{0,4},{2,6},{4,8},{6,10},{8,12},{10,14},{1,5},{3,7},{5,9},{7,11},{... | collective-permute-start | bytes 786440 | tf_op jit(solution)/shard_map/ppermute | solution.py:224
  82.1 10.3 %collective-permute-start.23 = (bf16[128,1024]{1,0:T(8,128)(2,1)S(1)}, bf16[128,1024]{1,0:T(8,128)(2,1)S(1)}, u32[]{:S(2)}, u32[]{:S(2)}) collective-permute-start(bf16[128,1024]{1,0:T(8,128)(2,1)S(1)} %copy-done.9), channel_id=1, source_target_pairs={{4,0},{6,2},{8,4},{10,6},{12,8},{14,10},{5,1},{7,3},{9,5},{11,7},{... | collective-permute-start | bytes 786440 | tf_op jit(solution)/shard_map/ppermute | solution.py:224
  89.9 6.1 %collective-permute-start.26 = (bf16[128,1024]{1,0:T(8,128)(2,1)S(1)}, bf16[128,1024]{1,0:T(8,128)(2,1)S(1)}, u32[]{:S(2)}, u32[]{:S(2)}) collective-permute-start(bf16[128,1024]{1,0:T(8,128)(2,1)S(1)} %collective-permute-done.24.refs_2_.refs_7_.refs_1_), channel_id=1, source_target_pairs={{4,8},{6,10},{8,12},{10,14},{5,9},{7,11},{9,13},{11,15},{20,24},{2... | collective-permute-start | bytes 786440 | tf_op jit(solution)/shard_map/ppermute | solution.py:224
  92.3 8.6 %collective-permute-start.25 = (bf16[128,1024]{1,0:T(8,128)(2,1)S(1)}, bf16[128,1024]{1,0:T(8,128)(2,1)S(1)}, u32[]{:S(2)}, u32[]{:S(2)}) collective-permute-start(bf16[128,1024]{1,0:T(8,128)(2,1)S(1)} %collective-permute-done.23.refs_1_.refs_5_.refs_0_), channel_id=1, source_target_pairs={{4,0},{6,2},{8,4},{10,6},{5,1},{7,3},{9,5},{11,7},{20,16},{22,18},... | collective-permute-start | bytes 786440 | tf_op jit(solution)/shard_map/ppermute | solution.py:224
  96.0 7.4 %collective-permute-start.28 = (bf16[128,1024]{1,0:T(8,128)(2,1)S(1)}, bf16[128,1024]{1,0:T(8,128)(2,1)S(1)}, u32[]{:S(2)}, u32[]{:S(2)}) collective-permute-start(bf16[128,1024]{1,0:T(8,128)(2,1)S(1)} %collective-permute-done.26.refs_4_.refs_1_), channel_id=1, source_target_pairs={{8,12},{10,14},{9,13},{11,15},{24,28},{26,30},{25,29},{27,31}} | collective-permute-start | bytes 786440 | tf_op jit(solution)/shard_map/ppermute | solution.py:224
  100.9 5.8 %collective-permute-start.27 = (bf16[128,1024]{1,0:T(8,128)(2,1)S(1)}, bf16[128,1024]{1,0:T(8,128)(2,1)S(1)}, u32[]{:S(2)}, u32[]{:S(2)}) collective-permute-start(bf16[128,1024]{1,0:T(8,128)(2,1)S(1)} %collective-permute-done.25.refs_3_.refs_0_), channel_id=1, source_target_pairs={{4,0},{6,2},{5,1},{7,3},{20,16},{22,18},{21,17},{23,19}} | collective-permute-start | bytes 786440 | tf_op jit(solution)/shard_map/ppermute | solution.py:224
  103.4 4.0 %copy-start.25 = (bf16[896,384]{0,1:T(8,128)(2,1)S(1)}, bf16[896,384]{0,1:T(8,128)(2,1)}, u32[]{:S(2)}) copy-start(bf16[896,384]{0,1:T(8,128)(2,1)} %copy-done.24) | copy-start | bytes 2064388
  110.1 57.5 %collective-permute-start.29 = (bf16[512,1024]{1,0:T(8,128)(2,1)S(1)}, bf16[512,1024]{1,0:T(8,128)(2,1)S(1)}, u32[]{:S(2)}, u32[]{:S(2)}) collective-permute-start(bf16[512,1024]{1,0:T(8,128)(2,1)S(1)} %shard_map.138.refs_0_), channel_id=1, source_target_pairs={{0,1},{1,0},{2,3},{3,2},{4,5},{5,4},{6,7},{7,6},{8,9},{9,8},{10,11... | collective-permute-start | bytes 3145736 | tf_op jit(solution)/shard_map/ppermute | solution.py:230
  113.4 4.5 %copy-start.15 = (bf16[96,128]{1,0:T(8,128)(2,1)S(1)}, bf16[96,128]{1,0:T(8,128)(2,1)}, u32[]{:S(2)}) copy-start(bf16[96,128]{1,0:T(8,128)(2,1)} %copy-done.14) | copy-start | bytes 73732
  113.4 5.2 %copy-start.17 = (bf16[96,128]{1,0:T(8,128)(2,1)S(1)}, bf16[96,128]{1,0:T(8,128)(2,1)}, u32[]{:S(2)}) copy-start(bf16[96,128]{1,0:T(8,128)(2,1)} %copy-done.16) | copy-start | bytes 73732
  114.0 7.3 %collective-permute-start.17 = (bf16[112,1024]{1,0:T(8,128)(2,1)S(1)}, bf16[112,1024]{1,0:T(8,128)(2,1)S(1)}, u32[]{:S(2)}, u32[]{:S(2)}) collective-permute-start(bf16[112,1024]{1,0:T(8,128)(2,1)S(1)} %get-tuple-element.48), channel_id=1, source_target_pairs={{0,2},{2,0},{4,6},{6,4},{8,10},{10,8},{12,14},{14,12},{1,3},{3,1},... | collective-permute-start | bytes 688136 | tf_op jit(solution)/shard_map/ppermute | solution.py:214
  115.3 10.9 %collective-permute-start.19 = (bf16[112,1024]{1,0:T(8,128)(2,1)S(1)}, bf16[112,1024]{1,0:T(8,128)(2,1)S(1)}, u32[]{:S(2)}, u32[]{:S(2)}) collective-permute-start(bf16[112,1024]{1,0:T(8,128)(2,1)S(1)} %get-tuple-element.49), channel_id=1, source_target_pairs={{0,2},{2,0},{4,6},{6,4},{8,10},{10,8},{12,14},{14,12},{1,3},{3,1},... | collective-permute-start | bytes 688136 | tf_op jit(solution)/shard_map/ppermute | solution.py:214
  115.5 15.6 %collective-permute-start.21 = (bf16[112,1024]{1,0:T(8,128)(2,1)S(1)}, bf16[112,1024]{1,0:T(8,128)(2,1)S(1)}, u32[]{:S(2)}, u32[]{:S(2)}) collective-permute-start(bf16[112,1024]{1,0:T(8,128)(2,1)S(1)} %get-tuple-element.50), channel_id=1, source_target_pairs={{0,2},{2,0},{4,6},{6,4},{8,10},{10,8},{12,14},{14,12},{1,3},{3,1},... | collective-permute-start | bytes 688136 | tf_op jit(solution)/shard_map/ppermute | solution.py:214
  117.5 17.8 %collective-permute-start.30 = (bf16[96,1024]{1,0:T(8,128)(2,1)S(1)}, bf16[96,1024]{1,0:T(8,128)(2,1)S(1)}, u32[]{:S(2)}, u32[]{:S(2)}) collective-permute-start(bf16[96,1024]{1,0:T(8,128)(2,1)S(1)} %shard_map.139), channel_id=1, source_target_pairs={{0,2},{2,0},{4,6},{6,4},{8,10},{10,8},{12,14},{14,12},{1,3},{3,1},... | collective-permute-start | bytes 589832 | tf_op jit(solution)/shard_map/ppermute | solution.py:214
  121.3 18.3 %collective-permute-start.31 = (bf16[96,1024]{1,0:T(8,128)(2,1)S(1)}, bf16[96,1024]{1,0:T(8,128)(2,1)S(1)}, u32[]{:S(2)}, u32[]{:S(2)}) collective-permute-start(bf16[96,1024]{1,0:T(8,128)(2,1)S(1)} %shard_map.140), channel_id=1, source_target_pairs={{0,2},{2,0},{4,6},{6,4},{8,10},{10,8},{12,14},{14,12},{1,3},{3,1},... | collective-permute-start | bytes 589832 | tf_op jit(solution)/shard_map/ppermute | solution.py:214
  126.2 17.6 %collective-permute-start.32 = (bf16[96,1024]{1,0:T(8,128)(2,1)S(1)}, bf16[96,1024]{1,0:T(8,128)(2,1)S(1)}, u32[]{:S(2)}, u32[]{:S(2)}) collective-permute-start(bf16[96,1024]{1,0:T(8,128)(2,1)S(1)} %shard_map.141), channel_id=1, source_target_pairs={{0,2},{2,0},{4,6},{6,4},{8,10},{10,8},{12,14},{14,12},{1,3},{3,1},... | collective-permute-start | bytes 589832 | tf_op jit(solution)/shard_map/ppermute | solution.py:214
  131.1 17.6 %collective-permute-start.16 = (bf16[112,1024]{1,0:T(8,128)(2,1)S(1)}, bf16[112,1024]{1,0:T(8,128)(2,1)S(1)}, u32[]{:S(2)}, u32[]{:S(2)}) collective-permute-start(bf16[112,1024]{1,0:T(8,128)(2,1)S(1)} %get-tuple-element.46), channel_id=1, source_target_pairs={{0,2},{2,0},{4,6},{6,4},{8,10},{10,8},{12,14},{14,12},{1,3},{3,1},... | collective-permute-start | bytes 688136 | tf_op jit(solution)/shard_map/ppermute | solution.py:214
  133.9 12.0 %copy-start.20 = (bf16[96,128]{1,0:T(8,128)(2,1)S(1)}, bf16[96,128]{1,0:T(8,128)(2,1)}, u32[]{:S(2)}) copy-start(bf16[96,128]{1,0:T(8,128)(2,1)} %copy-done.18) | copy-start | bytes 73732
  133.9 15.9 %copy-start.30 = (s32[128,4]{0,1:T(4,128)S(1)}, s32[128,4]{0,1:T(4,128)}, u32[]{:S(2)}) copy-start(s32[128,4]{0,1:T(4,128)} %param.9) | copy-start | bytes 6148
  135.3 20.7 %collective-permute-start.22 = (bf16[144,1024]{1,0:T(8,128)(2,1)S(1)}, bf16[144,1024]{1,0:T(8,128)(2,1)S(1)}, u32[]{:S(2)}, u32[]{:S(2)}) collective-permute-start(bf16[144,1024]{1,0:T(8,128)(2,1)S(1)} %shard_map.137), channel_id=1, source_target_pairs={{0,4},{2,6},{4,8},{6,10},{8,12},{10,14},{12,0},{14,2},{1,5},{3,7},... | collective-permute-start | bytes 884744 | tf_op jit(solution)/shard_map/ppermute | solution.py:217
  139.5 20.4 %collective-permute-start.20 = (bf16[144,1024]{1,0:T(8,128)(2,1)S(1)}, bf16[144,1024]{1,0:T(8,128)(2,1)S(1)}, u32[]{:S(2)}, u32[]{:S(2)}) collective-permute-start(bf16[144,1024]{1,0:T(8,128)(2,1)S(1)} %shard_map.136), channel_id=1, source_target_pairs={{0,8},{2,10},{4,12},{6,14},{8,0},{10,2},{12,4},{14,6},{1,9},{3,11}... | collective-permute-start | bytes 884744 | tf_op jit(solution)/shard_map/ppermute | solution.py:217
  143.7 22.3 %collective-permute-start.18 = (bf16[144,1024]{1,0:T(8,128)(2,1)S(1)}, bf16[144,1024]{1,0:T(8,128)(2,1)S(1)}, u32[]{:S(2)}, u32[]{:S(2)}) collective-permute-start(bf16[144,1024]{1,0:T(8,128)(2,1)S(1)} %shard_map.135), channel_id=1, source_target_pairs={{0,12},{2,14},{4,0},{6,2},{8,4},{10,6},{12,8},{14,10},{1,13},{3,15... | collective-permute-start | bytes 884744 | tf_op jit(solution)/shard_map/ppermute | solution.py:217
  148.6 5.6 %collective-permute-start.33 = (bf16[96,1024]{1,0:T(8,128)(2,1)S(1)}, bf16[96,1024]{1,0:T(8,128)(2,1)S(1)}, u32[]{:S(2)}, u32[]{:S(2)}) collective-permute-start(bf16[96,1024]{1,0:T(8,128)(2,1)S(1)} %shard_map.142), channel_id=1, source_target_pairs={{0,2},{2,0},{4,6},{6,4},{8,10},{10,8},{12,14},{14,12},{1,3},{3,1},... | collective-permute-start | bytes 589832 | tf_op jit(solution)/shard_map/ppermute | solution.py:214
  154.2 13.2 %collective-permute-start.34 = (bf16[96,1024]{1,0:T(8,128)(2,1)S(1)}, bf16[96,1024]{1,0:T(8,128)(2,1)S(1)}, u32[]{:S(2)}, u32[]{:S(2)}) collective-permute-start(bf16[96,1024]{1,0:T(8,128)(2,1)S(1)} %collective-permute-done.30.refs_2_), channel_id=1, source_target_pairs={{0,1},{1,0},{2,3},{3,2},{4,5},{5,4},{6,7},{7,6},{8,9},{9,8},{10,11... | collective-permute-start | bytes 589832 | tf_op jit(solution)/shard_map/ppermute | solution.py:230
  156.0 11.5 %collective-permute-start.35 = (bf16[96,1024]{1,0:T(8,128)(2,1)S(1)}, bf16[96,1024]{1,0:T(8,128)(2,1)S(1)}, u32[]{:S(2)}, u32[]{:S(2)}) collective-permute-start(bf16[96,1024]{1,0:T(8,128)(2,1)S(1)} %collective-permute-done.31.refs_3_), channel_id=1, source_target_pairs={{0,1},{1,0},{2,3},{3,2},{4,5},{5,4},{6,7},{7,6},{8,9},{9,8},{10,11... | collective-permute-start | bytes 589832 | tf_op jit(solution)/shard_map/ppermute | solution.py:230
  159.9 7.5 %collective-permute-start.36 = (bf16[96,1024]{1,0:T(8,128)(2,1)S(1)}, bf16[96,1024]{1,0:T(8,128)(2,1)S(1)}, u32[]{:S(2)}, u32[]{:S(2)}) collective-permute-start(bf16[96,1024]{1,0:T(8,128)(2,1)S(1)} %collective-permute-done.32.refs_4_), channel_id=1, source_target_pairs={{0,1},{1,0},{2,3},{3,2},{4,5},{5,4},{6,7},{7,6},{8,9},{9,8},{10,11... | collective-permute-start | bytes 589832 | tf_op jit(solution)/shard_map/ppermute | solution.py:230
  166.1 1.6 collective-permute-start.37
  169.1 2.5 %copy-start.1 = (bf16[896,2048]{1,0:T(8,128)(2,1)}, bf16[896,2048]{1,0:T(8,128)(2,1)S(1)}, u32[]{:S(2)}) copy-start(bf16[896,2048]{1,0:T(8,128)(2,1)S(1)} %shard_map.143) | copy-start | bytes 11010052
  171.7 2.4 %copy-start.29 = (bf16[1,2048,384]{2,1,0:T(8,128)(2,1)S(1)}, bf16[1,2048,384]{2,1,0:T(8,128)(2,1)}, u32[]{:S(2)}) copy-start(bf16[1,2048,384]{2,1,0:T(8,128)(2,1)} %param.12) | copy-start | bytes 4718596
  175.4 12.5 %collective-permute-start.38 = (bf16[896,1024]{1,0:T(8,128)(2,1)S(1)}, bf16[896,1024]{1,0:T(8,128)(2,1)S(1)}, u32[]{:S(2)}, u32[]{:S(2)}) collective-permute-start(bf16[896,1024]{1,0:T(8,128)(2,1)S(1)} %add_convert_fusion), channel_id=1, source_target_pairs={{0,1},{1,0},{2,3},{3,2},{4,5},{5,4},{6,7},{7,6},{8,9},{9,8},{10,11... | collective-permute-start | bytes 5505032 | tf_op jit(solution)/shard_map/ppermute | solution.py:230
  175.8 2.2 copy-start.26
  178.0 2.9 %copy-start.23 = (bf16[896,2048]{1,0:T(8,128)(2,1)S(1)}, bf16[896,2048]{1,0:T(8,128)(2,1)}, u32[]{:S(2)}) copy-start(bf16[896,2048]{1,0:T(8,128)(2,1)} %copy-done.21) | copy-start | bytes 11010052
  189.7 12.8 %collective-permute-start.39 = (bf16[112,1024]{1,0:T(8,128)(2,1)S(1)}, bf16[112,1024]{1,0:T(8,128)(2,1)S(1)}, u32[]{:S(2)}, u32[]{:S(2)}) collective-permute-start(bf16[112,1024]{1,0:T(8,128)(2,1)S(1)} %get-tuple-element.54), channel_id=1, source_target_pairs={{0,2},{2,0},{4,6},{6,4},{8,10},{10,8},{12,14},{14,12},{1,3},{3,1},... | collective-permute-start | bytes 688136 | tf_op jit(solution)/shard_map/ppermute | solution.py:214
  191.0 10.7 %collective-permute-start.44 = (bf16[112,1024]{1,0:T(8,128)(2,1)S(1)}, bf16[112,1024]{1,0:T(8,128)(2,1)S(1)}, u32[]{:S(2)}, u32[]{:S(2)}) collective-permute-start(bf16[112,1024]{1,0:T(8,128)(2,1)S(1)} %get-tuple-element.57), channel_id=1, source_target_pairs={{0,2},{2,0},{4,6},{6,4},{8,10},{10,8},{12,14},{14,12},{1,3},{3,1},... | collective-permute-start | bytes 688136 | tf_op jit(solution)/shard_map/ppermute | solution.py:214
  191.3 21.1 %collective-permute-start.40 = (bf16[112,1024]{1,0:T(8,128)(2,1)S(1)}, bf16[112,1024]{1,0:T(8,128)(2,1)S(1)}, u32[]{:S(2)}, u32[]{:S(2)}) collective-permute-start(bf16[112,1024]{1,0:T(8,128)(2,1)S(1)} %get-tuple-element.55), channel_id=1, source_target_pairs={{0,2},{2,0},{4,6},{6,4},{8,10},{10,8},{12,14},{14,12},{1,3},{3,1},... | collective-permute-start | bytes 688136 | tf_op jit(solution)/shard_map/ppermute | solution.py:214
  192.6 18.9 %collective-permute-start.42 = (bf16[112,1024]{1,0:T(8,128)(2,1)S(1)}, bf16[112,1024]{1,0:T(8,128)(2,1)S(1)}, u32[]{:S(2)}, u32[]{:S(2)}) collective-permute-start(bf16[112,1024]{1,0:T(8,128)(2,1)S(1)} %get-tuple-element.56), channel_id=1, source_target_pairs={{0,2},{2,0},{4,6},{6,4},{8,10},{10,8},{12,14},{14,12},{1,3},{3,1},... | collective-permute-start | bytes 688136 | tf_op jit(solution)/shard_map/ppermute | solution.py:214
  202.5 11.2 %collective-permute-start.45 = (bf16[144,1024]{1,0:T(8,128)(2,1)S(1)}, bf16[144,1024]{1,0:T(8,128)(2,1)S(1)}, u32[]{:S(2)}, u32[]{:S(2)}) collective-permute-start(bf16[144,1024]{1,0:T(8,128)(2,1)S(1)} %shard_map.148), channel_id=1, source_target_pairs={{0,4},{2,6},{4,8},{6,10},{8,12},{10,14},{12,0},{14,2},{1,5},{3,7},... | collective-permute-start | bytes 884744 | tf_op jit(solution)/shard_map/ppermute | solution.py:217
  212.4 19.3 %collective-permute-start.43 = (bf16[144,1024]{1,0:T(8,128)(2,1)S(1)}, bf16[144,1024]{1,0:T(8,128)(2,1)S(1)}, u32[]{:S(2)}, u32[]{:S(2)}) collective-permute-start(bf16[144,1024]{1,0:T(8,128)(2,1)S(1)} %shard_map.147), channel_id=1, source_target_pairs={{0,8},{2,10},{4,12},{6,14},{8,0},{10,2},{12,4},{14,6},{1,9},{3,11}... | collective-permute-start | bytes 884744 | tf_op jit(solution)/shard_map/ppermute | solution.py:217
  213.2 18.4 %collective-permute-start.41 = (bf16[144,1024]{1,0:T(8,128)(2,1)S(1)}, bf16[144,1024]{1,0:T(8,128)(2,1)S(1)}, u32[]{:S(2)}, u32[]{:S(2)}) collective-permute-start(bf16[144,1024]{1,0:T(8,128)(2,1)S(1)} %shard_map.146), channel_id=1, source_target_pairs={{0,12},{2,14},{4,0},{6,2},{8,4},{10,6},{12,8},{14,10},{1,13},{3,15... | collective-permute-start | bytes 884744 | tf_op jit(solution)/shard_map/ppermute | solution.py:217
  231.8 1.6 collective-permute-start.46
  (17 other events, 18.5 us)

commit v4 on v3

--- a/solution.py
+++ b/solution.py
@@ -180,18 +180,24 @@
         copy.wait()
 
 
-def pack_kernel(lines, tokens, padded, info, both, tails, *messages):
+def pack_kernel(lines, tokens, padded, tailed, info, both, *refs):
+    tails, messages = (refs[0], refs[1:]) if tailed else (None, refs)
     for k in range(lines):
         at = lines * tokens + k * padded
         messages[k][:padded, :] = both[at:at + padded, :].astype(BF)
-        messages[k][padded:, :] = jnp.zeros((TAIL, both.shape[1]), BF)
-        messages[k][padded:, :tokens] = tails[k].astype(BF)
-
-
-def home_kernel(k, tokens, padded, info, both, back, ring, tails, message):
+        if tails is not None:
+            messages[k][padded:, :] = jnp.zeros((TAIL, both.shape[1]), BF)
+            messages[k][padded:, :tokens] = tails[k].astype(BF)
+
+
+def home_kernel(k, tokens, padded, tailed, info, both, back, ring, *refs):
+    message = refs[-1]
     place = ring[k]
     block = both[k * tokens:(k + 1) * tokens, :] + dot(place, back[:padded, :], ((0,), (0,)))
     message[:tokens, :] = block.astype(BF)
+    if not tailed:
+        return
+    tails = refs[0]
     message[tokens:, :] = jnp.zeros((TAIL, both.shape[1]), BF)
     theirs = dot(back[padded:, :padded], place, ((1,), (0,)))
     message[tokens:, :tokens] = jnp.concatenate(
@@ -237,15 +243,6 @@
     parts = jnp.pad(parts, ((0, tail - 3 * part_rows), (0, 0)))
     first = jnp.concatenate([tokens, parts])
 
-    def along_line(start):
-        up, down = {0: start}, {0: start}
-        for k in range(1, lines):
-            up[k] = hop(up[k - 1], k, 1)
-            down[k] = hop(down[k - 1], k, -1)
-        return up, down
-
-    up, down = along_line(first)
-
     def sources_of(slot):
         if slot == 0:
             return [(None, 0)], np.zeros(lines, np.int32)
@@ -259,66 +256,41 @@
     known = jnp.asarray(np.concatenate([which_of, place_of], 1))[at_line]
     info = jnp.concatenate([jnp.stack([mine, peer, core]).astype(I32), known])
     which_at, place_at = 3, 3 + lines
-
-    def candidates(slot, ups, downs):
-        return [(downs if d == "down" else ups)[n] for d, n in names_of[slot]]
-
     counts = [len(n) for n in names_of]
-    compact_shape = shape_of((padded + TAIL, half_width))
-    packed, compact_blocks, places, own_parts = [], [], [], []
-    for slot in range(lines):
-        blocks = candidates(slot, up, down)
-        compact, place, parts = local_call(
-            functools.partial(token_slot_kernel, len(blocks), which_at + slot, token_count,
-                              part_rows, capacity, padded),
-            (compact_shape, shape_of((padded, token_count)), shape_of((TAIL, token_count))),
-            (info, *blocks),
-            (pltpu.VMEM((tail, half_width), F32), pltpu.VMEM((TAIL, token_count), F32)),
-        )
-        packed.append(compact)
-        compact_blocks.append(over_pair(compact))
-        places.append(place)
-        own_parts.append(parts)
-
-    def lined(ups, downs):
-        blocks = [x for slot in range(lines) for x in candidates(slot, ups, downs)]
-        (whole,) = local_call(
-            functools.partial(line_kernel, counts, which_at, place_at, token_count),
-            (shape_of((lines * token_count, half_width)),), (info, *blocks), flops=10**6)
-        return whole
-
     dense_rows = lines * token_count
     row_count = lines * (token_count + padded)
     rows_shape = shape_of((row_count, 2 * half_width))
     sems = (pltpu.SemaphoreType.DMA((2 * (lines + 1),)),)
     sizes = (lines, token_count, padded, half_width, place_at)
-
-    dense_own = lined(up, down)
-    rows, weights, ring = local_call(
-        functools.partial(token_rows_kernel, *sizes),
-        (rows_shape, shape_of((row_count, 1), F32), shape_of((lines, padded, token_count))),
-        (info, dense_own, over_core(dense_own), *compact_blocks,
-         *[over_core(x) for x in compact_blocks], *own_parts, *places),
-        sems, flops=10**6)
-
-    held_grad, _ = lax.optimization_barrier((grad_out, packed[min(2, lines - 1)]))
-    grad_ups, grad_downs = along_line(held_grad)
-    grad_compact = []
-    for slot in range(lines):
-        blocks = candidates(slot, grad_ups, grad_downs)
-        (compact,) = local_call(
-            functools.partial(grad_slot_kernel, len(blocks), which_at + slot),
-            (shape_of((padded, half_width)),), (info, *blocks, places[slot]))
-        grad_compact.append(over_pair(compact))
-
     gate_local = gate_weight[0]
     up_local = up_weight[0]
     down_local = down_weight[0]
-    gate = dot(rows, gate_local, ((1,), (0,)))
-    upward = dot(rows, up_local, ((1,), (0,)))
-    sig = jax.nn.sigmoid(gate)
-    hidden = gate * sig * upward
-    scaled_hidden = (weights * hidden).astype(BF)
+
+    def candidates(slot, ups, downs):
+        return [(downs if d == "down" else ups)[n] for d, n in names_of[slot]]
+
+    def token_slot(slot, ups, downs):
+        blocks = candidates(slot, ups, downs)
+        return local_call(
+            functools.partial(token_slot_kernel, len(blocks), which_at + slot, token_count,
+                              part_rows, capacity, padded),
+            (shape_of((padded + TAIL, half_width)), shape_of((padded, token_count)),
+             shape_of((TAIL, token_count))),
+            (info, *blocks),
+            (pltpu.VMEM((tail, half_width), F32), pltpu.VMEM((TAIL, token_count), F32)),
+        )
+
+    def grad_slot(slot, ups, downs, place):
+        blocks = candidates(slot, ups, downs)
+        return local_call(
+            functools.partial(grad_slot_kernel, len(blocks), which_at + slot),
+            (shape_of((padded, half_width)),), (info, *blocks, place))[0]
+
+    def lined(ups, downs):
+        blocks = [x for slot in range(lines) for x in candidates(slot, ups, downs)]
+        return local_call(
+            functools.partial(line_kernel, counts, which_at, place_at, token_count),
+            (shape_of((lines * token_count, half_width)),), (info, *blocks), flops=10**6)[0]
 
     def summed_over_cores(make):
         sent = over_core(make(1 - core).astype(BF))
@@ -327,24 +299,17 @@
     def half_of(x, which, axis):
         return lax.dynamic_slice_in_dim(x, which * half_width, half_width, axis)
 
-    message_shape = shape_of((token_count + TAIL, half_width))
-
-    def crossed(both, compact_tails):
-        messages = local_call(
-            functools.partial(pack_kernel, lines, token_count, padded),
-            (compact_shape,) * lines, (info, both, compact_tails), flops=10**6)
-        return [over_pair(m) for m in messages]
-
-    def to_home(both, backs, dense_tails):
-        return [
-            local_call(
-                functools.partial(home_kernel, k, token_count, padded),
-                (message_shape,), (info, both, backs[k], ring, dense_tails))[0]
-            for k in range(lines)
-        ]
-
-    def go_home(blocks):
-        return [blocks[0]] + [over_line(blocks[k], lines - k) for k in range(1, lines)]
+    def packed_rows(both, *tails):
+        extra = TAIL if tails else 0
+        return list(local_call(
+            functools.partial(pack_kernel, lines, token_count, padded, bool(tails)),
+            (shape_of((padded + extra, half_width)),) * lines, (info, both, *tails), flops=10**6))
+
+    def to_home(k, both, back, ring, *tails):
+        extra = TAIL if tails else 0
+        return local_call(
+            functools.partial(home_kernel, k, token_count, padded, bool(tails)),
+            (shape_of((token_count + extra, half_width)),), (info, both, back, ring, *tails))[0]
 
     def summed(blocks):
         total = blocks[0][:token_count].astype(F32)
@@ -352,48 +317,135 @@
             total = total + block[:token_count].astype(F32)
         return total.astype(BF)
 
-    no_tails = jnp.zeros((lines, TAIL, token_count), F32)
+    def tails_of(values):
+        values = jnp.pad(values, ((0, 0), (0, token_count - values.shape[1])))
+        parts = jnp.stack([p.astype(F32) for p in split_three(values)], axis=1)
+        return jnp.pad(parts, ((0, 0), (0, TAIL - 3), (0, 0)))
+
+    settle = lax.optimization_barrier
+
+    up, down = {0: first}, {0: first}
+    grad_ups, grad_downs = {0: grad_out}, {0: grad_out}
+    compact, compact_other, places, own_parts = {}, {}, {}, {}
+
+    def token_pair(slot):
+        block, places[slot], own_parts[slot] = token_slot(slot, up, down)
+        compact[slot] = over_pair(block)
+
+    for k in range(1, lines):
+        up[k], down[k] = hop(up[k - 1], k, 1), hop(down[k - 1], k, -1)
+        token_pair(k - 1)
+        if k > 1:
+            compact_other[k - 2] = over_core(compact[k - 2])
+        up, down, grad_ups, grad_downs, compact, compact_other, places, own_parts = settle(
+            (up, down, grad_ups, grad_downs, compact, compact_other, places, own_parts))
+
+    def grad_hop(k):
+        grad_ups[k], grad_downs[k] = hop(grad_ups[k - 1], k, 1), hop(grad_downs[k - 1], k, -1)
+
+    grad_hop(1)
+    token_pair(lines - 1)
+    if lines > 1:
+        compact_other[lines - 2] = over_core(compact[lines - 2])
+    dense_own = lined(up, down)
+    dense_other = over_core(dense_own)
+    grad_ups, grad_downs, compact, compact_other, places, own_parts, dense_own, dense_other = settle(
+        (grad_ups, grad_downs, compact, compact_other, places, own_parts, dense_own, dense_other))
+
+    grad_compact, grad_other = {}, {}
+
+    def grad_pair(slot):
+        grad_compact[slot] = over_pair(grad_slot(slot, grad_ups, grad_downs, places[slot]))
+
+    grad_hop(2)
+    grad_pair(0)
+    compact_other[lines - 1] = over_core(compact[lines - 1])
+    order = range(lines)
+    rows, weights, ring = local_call(
+        functools.partial(token_rows_kernel, *sizes),
+        (rows_shape, shape_of((row_count, 1), F32), shape_of((lines, padded, token_count))),
+        (info, dense_own, dense_other, *[compact[j] for j in order],
+         *[compact_other[j] for j in order], *[own_parts[j] for j in order],
+         *[places[j] for j in order]),
+        sems, flops=10**6)
+    gate = dot(rows, gate_local, ((1,), (0,)))
+    upward = dot(rows, up_local, ((1,), (0,)))
+    hidden = gate * jax.nn.sigmoid(gate) * upward
+    scaled_hidden = (weights * hidden).astype(BF)
     out_both = summed_over_cores(
         lambda c: dot(scaled_hidden, half_of(down_local, c, 1), ((1,), (0,))))
-    out_backs = crossed(out_both, no_tails)
-    out_blocks = to_home(out_both, out_backs, no_tails)
-    layer_out = summed(go_home(out_blocks))
-
+    saved = (rows, weights, ring, gate, upward, scaled_hidden)
+    grad_ups, grad_downs, grad_compact, places, saved, out_both = settle(
+        (grad_ups, grad_downs, grad_compact, places, saved, out_both))
+
+    sent_order = sorted(range(1, lines), key=lambda k: -min(k, lines - k)) + [0]
+    out_packed = packed_rows(out_both)
+    out_back = {}
+    for k in range(3, lines):
+        grad_hop(k)
+        grad_pair(k - 2)
+        grad_other[k - 3] = over_core(grad_compact[k - 3])
+        if k == 3:
+            out_back[sent_order[0]] = over_pair(out_packed[sent_order[0]])
+        grad_ups, grad_downs, grad_compact, grad_other, places, saved, out_both, out_packed, out_back = settle(
+            (grad_ups, grad_downs, grad_compact, grad_other, places, saved, out_both, out_packed, out_back))
+
+    rows, weights, ring, gate, upward, scaled_hidden = saved
+    grad_pair(lines - 2)
+    grad_pair(lines - 1)
     grad_own = lined(grad_ups, grad_downs)
-    grad_own, _ = lax.optimization_barrier((grad_own, out_both))
+    grad_line_other = over_core(grad_own)
+    out_home = {}
+
+    def out_send(k):
+        block = to_home(k, out_both, out_back[k], ring)
+        out_home[k] = over_line(block, lines - k) if k else block
+
+    out_send(sent_order[0])
+    grad_other[lines - 3] = over_core(grad_compact[lines - 3])
+    (grad_compact, grad_other, grad_own, grad_line_other, saved, out_both, out_packed, out_home) = settle(
+        (grad_compact, grad_other, grad_own, grad_line_other, saved, out_both, out_packed, out_home))
+
+    rows, weights, ring, gate, upward, scaled_hidden = saved
+    for k in sent_order[1:]:
+        out_back[k] = over_pair(out_packed[k])
+        out_send(k)
+    for j in (lines - 2, lines - 1):
+        grad_other[j] = over_core(grad_compact[j])
     (grads,) = local_call(
         functools.partial(grad_rows_kernel, *sizes), (rows_shape,),
-        (info, grad_own, over_core(grad_own), *grad_compact, *[over_core(x) for x in grad_compact]),
+        (info, grad_own, grad_line_other, *[grad_compact[j] for j in order],
+         *[grad_other[j] for j in order]),
         sems, flops=10**6)
+    sig = jax.nn.sigmoid(gate)
     grad_plain = dot(grads, down_local, ((1,), (1,)))
-    row_value = jnp.sum(hidden * grad_plain, axis=1)
+    row_value = jnp.sum(gate * sig * upward * grad_plain, axis=1)
     grad_hidden = weights * grad_plain
     grad_gate = (grad_hidden * upward * sig * (1.0 + gate * (1.0 - sig))).astype(BF)
     grad_up = (grad_hidden * gate * sig).astype(BF)
     in_both = summed_over_cores(
         lambda c: dot(grad_gate, half_of(gate_local, c, 0), ((1,), (1,)))
         + dot(grad_up, half_of(up_local, c, 0), ((1,), (1,))))
-    in_both, _ = lax.optimization_barrier((in_both, out_blocks))
-
-    def tails_of(values):
-        values = jnp.pad(values, ((0, 0), (0, token_count - values.shape[1])))
-        parts = jnp.stack([p.astype(F32) for p in split_three(values)], axis=1)
-        return jnp.pad(parts, ((0, 0), (0, TAIL - 3), (0, 0)))
-
     dense_tails = tails_of(row_value[:dense_rows].reshape(lines, token_count))
     compact_tails = tails_of(row_value[dense_rows:].reshape(lines, padded))
-    in_backs = crossed(in_both, compact_tails)
-    in_blocks = to_home(in_both, in_backs, dense_tails)
-    came_home = go_home(in_blocks)
-    input_grad = summed(came_home)
+    in_packed = packed_rows(in_both, compact_tails)
+    in_packed, in_both, dense_tails, ring, out_home, rows, scaled_hidden, grad_gate, grad_up, grads = settle(
+        (in_packed, in_both, dense_tails, ring, out_home, rows, scaled_hidden, grad_gate, grad_up, grads))
+
+    layer_out = summed([out_home[k] for k in range(lines)])
+    came_home = {}
+    for k in sent_order:
+        block = to_home(k, in_both, over_pair(in_packed[k]), ring, dense_tails)
+        came_home[k] = over_line(block, lines - k) if k else block
+    input_grad = summed([came_home[k] for k in range(lines)])
 
     down_grad = dot(scaled_hidden, grads, ((0,), (0,))).astype(BF)
     gate_grad = dot(rows, grad_gate, ((0,), (0,))).astype(BF)
     up_grad = dot(rows, grad_up, ((0,), (0,))).astype(BF)
 
     held = []
-    for block in came_home:
-        rows_back = block[token_count:, :token_count].astype(F32)
+    for k in range(lines):
+        rows_back = came_home[k][token_count:, :token_count].astype(F32)
         held.append(jnp.stack([jnp.sum(rows_back[:8], axis=0), jnp.sum(rows_back[8:], axis=0)]))
     flat = jnp.stack(held).reshape(experts, token_count)
     place = (expert_ids // 2 - at_line) % lines

time: 236 us -> 234 us (level)
  local copies, waits for them, and re-layouts: 13.4 us -> 24.8 us
  waiting for transfers between devices: 102 us -> 93.1 us
  starting transfers between devices: 60.9 us -> 55.4 us
  matrix products: 30.9 us -> 33.4 us
    ppermute x12, waiting for transfers between devices: 24.2 us -> 4.23 us  [hop(): lax.ppermute(x, 'expert', [(2 * z + y, 2 * (z + step) + y) for z in range...]
    unnamed x69 -> x121, local copies, waits for them, and re-layouts: 12.6 us -> 23.9 us
    ppermute x13, starting transfers between devices: 16.4 us -> 11.3 us  [over_core(): return lax.ppermute(x, 'tensor', [(0, 1), (1, 0)])]
    ppermute x16, waiting for transfers between devices: 51.1 us -> 55.7 us  [over_pair(): lax.ppermute(x, 'expert', [(i, i + 1 - 2 * (i % 2)) for i in range(expert...]
    ppermute x6, waiting for transfers between devices: 26.4 us -> 30.4 us  [over_line(): lax.ppermute(x, 'expert', [(i, (i // 2 + k) % lines * 2 + i % 2) for i in...]
    ppermute x13, waiting for transfers between devices: 0.21 us -> 2.72 us  [over_core(): return lax.ppermute(x, 'tensor', [(0, 1), (1, 0)])]
    dot_general x12, matrix products: 30.9 us -> 33.4 us  [dot(): lax.dot_general(a, b, (contract, ((), ())), preferred_element_type=F32)]
  transfers between devices with their start and end apart: 47 -> 47, of which waited for: 26 -> 19; matrix products, arithmetic and copies ran while one was open for 6% -> 8% of each run, Pallas kernels for 6% -> 6%
where the time goes in v4:
time: 234 us; the launch traced here: 233 us
  waiting for transfers between devices  93.1 us (40%)
  starting transfers between devices  55.4 us (24%)
  matrix products  33.4 us (14%)
  local copies, waits for them, and re-layouts  24.8 us (11%)
  Pallas kernels  19.6 us (8%)
  other arithmetic  4.86 us (2%)
    ppermute x16, waiting for transfers between devices, over_pair(): lax.ppermute(x, 'expert', [(i, i + 1 - 2 * (i % 2)) for i in range(expert...  55.7 us
    dot_general x12, matrix products, dot(): lax.dot_general(a, b, (contract, ((), ())), preferred_element_type=F32)  33.4 us
    ppermute x6, waiting for transfers between devices, over_line(): lax.ppermute(x, 'expert', [(i, (i // 2 + k) % lines * 2 + i % 2) for i in...  30.4 us
    ppermute x12, starting transfers between devices, hop(): lax.ppermute(x, 'expert', [(2 * z + y, 2 * (z + step) + y) for z in range...  26.5 us
    unnamed x121, local copies, waits for them, and re-layouts  23.9 us
    pallas_call x22, Pallas kernels, local_call(): pl.pallas_call(kernel, out_shape=tuple(outs), in_specs=in_specs or [SMEM_...  19.6 us
    ppermute x16, starting transfers between devices, over_pair(): lax.ppermute(x, 'expert', [(i, i + 1 - 2 * (i % 2)) for i in range(expert...  14.3 us
    ppermute x13, starting transfers between devices, over_core(): return lax.ppermute(x, 'tensor', [(0, 1), (1, 0)])  11.3 us
  transfers between devices with their start and end apart: 47, of which 19 were waited for; matrix products, arithmetic and copies ran while one was open for 8% of the time, Pallas kernels for 6%

profile of v4, /device:TPU:9, one launch (start us, length us, event | category | flops | bytes accessed | tf_op | source)
XLA Modules:
  0.0 232.6 jit_solution(9636716163607700272)
XLA Ops:
  2.5 1.9 collective-permute-start.1
  4.4 3.4 %collective-permute-start = (bf16[144,1024]{1,0:T(8,128)(2,1)S(1)}, bf16[144,1024]{1,0:T(8,128)(2,1)S(1)}, u32[]{:S(2)}, u32[]{:S(2)}) collective-permute-start(bf16[144,1024]{1,0:T(8,128)(2,1)S(1)} %pad_maximum_fusion.refs_0_), channel_id=1, source_target_pairs={{0,4},{2,6},{4,8},{6,10},{8,12},{10,14},{1,5},{3,7},{5,9},{7,11},{... | collective-permute-start | bytes 884744 | tf_op jit(solution)/shard_map/ppermute | solution.py:230
  8.6 1.0 shard_map.127
  9.6 1.3 collective-permute-start.2
  10.9 4.6 %collective-permute-done.2.refs_2_ = bf16[112,1024]{1,0:T(8,128)(2,1)S(1)} collective-permute-done((bf16[112,1024]{1,0:T(8,128)(2,1)S(1)}, bf16[112,1024]{1,0:T(8,128)(2,1)S(1)}, u32[]{:S(2)}, u32[]{:S(2)}) %collective-permute-start.2) | collective-permute-done | bytes 229408 | tf_op jit(solution)/shard_map/ppermute | solution.py:220
  15.5 3.2 %collective-permute-start.3 = (bf16[144,1024]{1,0:T(8,128)(2,1)S(1)}, bf16[144,1024]{1,0:T(8,128)(2,1)S(1)}, u32[]{:S(2)}, u32[]{:S(2)}) collective-permute-start(bf16[144,1024]{1,0:T(8,128)(2,1)S(1)} %collective-permute-done.refs_1_.refs_2_.refs_7_), channel_id=1, source_target_pairs={{4,8},{6,10},{8,12},{10,14},{5,9},{7,11},{9,13},{11,15},{20,24},{2... | collective-permute-start | bytes 884744 | tf_op jit(solution)/shard_map/ppermute | solution.py:230
  18.8 1.9 collective-permute-start.4
  20.7 2.5 %collective-permute-start.6 = (bf16[112,1024]{1,0:T(8,128)(2,1)S(1)}, bf16[112,1024]{1,0:T(8,128)(2,1)S(1)}, u32[]{:S(2)}, u32[]{:S(2)}) collective-permute-start(bf16[112,1024]{1,0:T(8,128)(2,1)S(1)} %collective-permute-done.2.refs_2_), channel_id=1, source_target_pairs={{0,1},{1,0},{2,3},{3,2},{4,5},{5,4},{6,7},{7,6},{8,9},{9,8},{10,11... | collective-permute-start | bytes 688136 | tf_op jit(solution)/shard_map/ppermute | solution.py:236
  23.2 1.0 shard_map.128
  24.3 1.3 collective-permute-start.5
  25.5 6.0 %collective-permute-done.5.refs_3_ = bf16[112,1024]{1,0:T(8,128)(2,1)S(1)} collective-permute-done((bf16[112,1024]{1,0:T(8,128)(2,1)S(1)}, bf16[112,1024]{1,0:T(8,128)(2,1)S(1)}, u32[]{:S(2)}, u32[]{:S(2)}) %collective-permute-start.5) | collective-permute-done | bytes 229408 | tf_op jit(solution)/shard_map/ppermute | solution.py:220
  32.2 1.3 collective-permute-start.8
  34.4 1.0 shard_map.129
  35.4 1.3 collective-permute-start.9
  36.7 6.0 %collective-permute-done.9.refs_4_ = bf16[112,1024]{1,0:T(8,128)(2,1)S(1)} collective-permute-done((bf16[112,1024]{1,0:T(8,128)(2,1)S(1)}, bf16[112,1024]{1,0:T(8,128)(2,1)S(1)}, u32[]{:S(2)}, u32[]{:S(2)}) %collective-permute-start.9) | collective-permute-done | bytes 229408 | tf_op jit(solution)/shard_map/ppermute | solution.py:220
  44.3 3.6 %collective-permute-start.11 = (bf16[128,1024]{1,0:T(8,128)(2,1)S(1)}, bf16[128,1024]{1,0:T(8,128)(2,1)S(1)}, u32[]{:S(2)}, u32[]{:S(2)}) collective-permute-start(bf16[128,1024]{1,0:T(8,128)(2,1)S(1)} %copy-done.9), channel_id=1, source_target_pairs={{0,4},{2,6},{4,8},{6,10},{8,12},{10,14},{1,5},{3,7},{5,9},{7,11},{... | collective-permute-start | bytes 786440 | tf_op jit(solution)/shard_map/ppermute | solution.py:230
  47.9 1.9 collective-permute-start.12
  50.4 1.1 shard_map.130
  51.5 1.3 collective-permute-start.13
  53.5 5.3 %collective-permute-done.13.refs_5_ = bf16[112,1024]{1,0:T(8,128)(2,1)S(1)} collective-permute-done((bf16[112,1024]{1,0:T(8,128)(2,1)S(1)}, bf16[112,1024]{1,0:T(8,128)(2,1)S(1)}, u32[]{:S(2)}, u32[]{:S(2)}) %collective-permute-start.13) | collective-permute-done | bytes 229408 | tf_op jit(solution)/shard_map/ppermute | solution.py:220
  60.5 1.1 collective-permute-done.19.refs_9_
  61.7 1.2 copy-done.4
  62.9 1.2 copy-done.11
  69.7 1.5 shard_map.133
  71.2 1.8 copy-done.34
  73.3 4.7 %fusion.7 = f32[896,384]{1,0:T(8,128)S(1)} fusion(bf16[896,2048]{1,0:T(8,128)(2,1)} %copy-done.34, bf16[1,2048,384]{2,1,0:T(8,128)(2,1)} %param.11), kind=kOutput, calls=%fused_computation.14 | convolution fusion | flops 1409286144 | bytes 6619136 | tf_op jit(solution)/shard_map/dot_general | solution.py:18
  78.0 3.2 %multiply_convert_fusion.2 = (bf16[896,384]{1,0:T(8,128)(2,1)S(1)}, f32[896,384]{1,0:T(8,128)}) fusion(f32[896,384]{1,0:T(8,128)S(1)} %fusion.7, f32[896]{0:T(1024)S(1)} %reduce, bf16[896,2048]{1,0:T(8,128)(2,1)S(1)} %copy-done.35, bf16[1,2048,384]{2,1,0:T(8,128)(2,1)S(1)} %copy-done.49), kind=kOutput, calls=%fused_computation.20 | convolution fusion | flops 1411694592 | bytes 8687104 | tf_op jit(solution)/shard_map/dot_general | solution.py:18
  82.1 2.4 %convolution_convert_fusion.3 = bf16[896,1024]{1,0:T(8,128)(2,1)} fusion(bf16[896,384]{1,0:T(8,128)(2,1)S(1)} %get-tuple-element.322, bf16[1,384,2048]{2,1,0:T(8,128)(2,1)S(1)} %copy-done, s32[]{:T(128)S(6)} %select_n.54), kind=kOutput, calls=%fused_computation.9 | convolution fusion | flops 705560576 | bytes 3309572 | tf_op jit(solution)/shard_map/dot_general | solution.py:18
  85.6 1.3 collective-permute-start.18
  86.9 3.7 %collective-permute-start.16 = (bf16[128,1024]{1,0:T(8,128)(2,1)S(1)}, bf16[128,1024]{1,0:T(8,128)(2,1)S(1)}, u32[]{:S(2)}, u32[]{:S(2)}) collective-permute-start(bf16[128,1024]{1,0:T(8,128)(2,1)S(1)} %collective-permute-done.11.refs_1_.refs_2_.refs_7_), channel_id=1, source_target_pairs={{4,8},{6,10},{8,12},{10,14},{5,9},{7,11},{9,13},{11,15},{20,24},{2... | collective-permute-start | bytes 786440 | tf_op jit(solution)/shard_map/ppermute | solution.py:230
  90.6 1.9 collective-permute-start.17
  92.5 2.8 %convert_add_fusion.1.both = f32[896,1024]{1,0:T(8,128)S(1)} fusion(bf16[896,1024]{1,0:T(8,128)(2,1)} %collective-permute-done.20, bf16[896,384]{1,0:T(8,128)(2,1)} %copy-done.52, bf16[1,384,2048]{2,1,0:T(8,128)(2,1)S(1)} %copy-done, s32[]{:T(128)S(6)} %select_n.53), kind=kOutput, calls=%fused_computation.2 | convolution fusion | flops 706478080 | bytes 6979588 | tf_op jit(solution)/shard_map/dot_general | solution.py:18
  95.8 3.8 %collective-permute-done.17.refs_0_.refs_3_ = bf16[128,1024]{1,0:T(8,128)(2,1)S(1)} collective-permute-done((bf16[128,1024]{1,0:T(8,128)(2,1)S(1)}, bf16[128,1024]{1,0:T(8,128)(2,1)S(1)}, u32[]{:S(2)}, u32[]{:S(2)}) %collective-permute-start.17) | collective-permute-done | bytes 262176 | tf_op jit(solution)/shard_map/ppermute | solution.py:230
  100.3 2.2 collective-permute-start.22
  103.6 1.8 collective-permute-start.24
  106.7 1.2 collective-permute-start.25
  108.2 5.5 %collective-permute-done.25.back = bf16[96,1024]{1,0:T(8,128)(2,1)S(1)} collective-permute-done((bf16[96,1024]{1,0:T(8,128)(2,1)S(1)}, bf16[96,1024]{1,0:T(8,128)(2,1)S(1)}, u32[]{:S(2)}, u32[]{:S(2)}) %collective-permute-start.25) | collective-permute-done | bytes 196640 | tf_op jit(solution)/shard_map/ppermute | solution.py:220
  114.4 1.2 collective-permute-start.29
  118.7 1.1 collective-permute-start.26
  120.4 3.6 %collective-permute-done.27.refs_5_ = bf16[96,1024]{1,0:T(8,128)(2,1)} collective-permute-done((bf16[96,1024]{1,0:T(8,128)(2,1)S(1)}, bf16[96,1024]{1,0:T(8,128)(2,1)}, u32[]{:S(2)}, u32[]{:S(2)}) %collective-permute-start.27) | collective-permute-done | bytes 196640 | tf_op jit(solution)/shard_map/ppermute | solution.py:220
  124.0 4.2 %collective-permute-done.26.refs_4_ = bf16[96,1024]{1,0:T(8,128)(2,1)} collective-permute-done((bf16[96,1024]{1,0:T(8,128)(2,1)S(1)}, bf16[96,1024]{1,0:T(8,128)(2,1)}, u32[]{:S(2)}, u32[]{:S(2)}) %collective-permute-start.26) | collective-permute-done | bytes 196640 | tf_op jit(solution)/shard_map/ppermute | solution.py:220
  129.6 1.1 copy-done.12
  131.7 1.3 collective-permute-done.31.refs_8_
  133.3 1.2 copy-done.13
  138.2 1.9 shard_map.140
  140.3 2.8 %multiply_reduce_fusion = (f32[896]{0:T(1024)S(1)}, bf16[896,384]{1,0:T(8,128)(2,1)S(1)}, bf16[896,384]{1,0:T(8,128)(2,1)S(1)}) fusion(f32[896,384]{1,0:T(8,128)S(1)} %copy-done.59, f32[896,384]{1,0:T(8,128)S(1)} %copy-done.58, f32[896]{0:T(1024)S(1)} %reduce.1, bf16[896,2048]{1,0:T(8,128)(2,1)S(1)} %shard_map.140, bf16[1,384,2048]{2,1,0:T(8,128)(2,1)S(1)} %copy-done), kind=kOutput, calls=%fused_computation.16 | convolution fusion | flops 1415478400 | bytes 9378816 | tf_op jit(solution)/shard_map/dot_general | solution.py:18
  143.1 1.2 fusion.10
  145.0 2.5 %add_convert_fusion = bf16[896,1024]{1,0:T(8,128)(2,1)} fusion(f32[896,1024]{1,0:T(8,128)S(1)} %fusion.10, bf16[896,384]{1,0:T(8,128)(2,1)S(1)} %get-tuple-element.321, bf16[1,2048,384]{2,1,0:T(8,128)(2,1)S(1)} %copy-done.50, s32[]{:T(128)S(6)} %select_n.54), kind=kOutput, calls=%fused_computation.1 | convolution fusion | flops 706478080 | bytes 6979588 | tf_op jit(solution)/shard_map/dot_general | solution.py:18
  148.3 1.1 collective-permute-start.35
  149.9 12.6 %collective-permute-done.37.back = bf16[96,1024]{1,0:T(8,128)(2,1)S(1)} collective-permute-done((bf16[96,1024]{1,0:T(8,128)(2,1)S(1)}, bf16[96,1024]{1,0:T(8,128)(2,1)S(1)}, u32[]{:S(2)}, u32[]{:S(2)}) %collective-permute-start.37) | collective-permute-done | bytes 196640 | tf_op jit(solution)/shard_map/ppermute | solution.py:220
  162.6 2.0 copy-done.2
  168.7 1.2 fusion.13
  170.3 2.7 %convert_add_fusion.both = f32[896,1024]{1,0:T(8,128)S(1)} fusion(bf16[896,1024]{1,0:T(8,128)(2,1)} %collective-permute-done.33, f32[896,1024]{1,0:T(8,128)S(1)} %fusion.13, bf16[896,384]{1,0:T(8,128)(2,1)S(1)} %copy-done.46, bf16[1,2048,384]{2,1,0:T(8,128)(2,1)S(1)} %copy-done.51, s32[]{:T(128)S(6)} %select_n.53), kind=kOutput, calls=%fused_computation | convolution fusion | flops 707395584 | bytes 10649604 | tf_op jit(solution)/shard_map/dot_general | solution.py:18
  173.7 7.6 %collective-permute-done.36 = bf16[128,1024]{1,0:T(8,128)(2,1)S(1)} collective-permute-done((bf16[128,1024]{1,0:T(8,128)(2,1)S(1)}, bf16[128,1024]{1,0:T(8,128)(2,1)S(1)}, u32[]{:S(2)}, u32[]{:S(2)}) %collective-permute-start.36) | collective-permute-done | bytes 262176 | tf_op jit(solution)/shard_map/ppermute | solution.py:223
  181.5 1.2 collective-permute-start.40
  183.0 1.2 collective-permute-start.44
  184.2 3.5 %fusion = bf16[1,2048,384]{2,1,0:T(8,128)(2,1)} fusion(bf16[896,2048]{1,0:T(8,128)(2,1)S(1)} %copy-done.36, bf16[896,384]{1,0:T(8,128)(2,1)S(1)} %copy-done.44), kind=kOutput, calls=%fused_computation.6 | convolution fusion | flops 1410072576 | bytes 5931008 | tf_op jit(solution)/shard_map/dot_general | solution.py:18
  187.7 3.5 %fusion.1 = bf16[1,2048,384]{2,1,0:T(8,128)(2,1)} fusion(bf16[896,2048]{1,0:T(8,128)(2,1)S(1)} %copy-done.36, bf16[896,384]{1,0:T(8,128)(2,1)S(1)} %copy-done.46), kind=kOutput, calls=%fused_computation.7 | convolution fusion | flops 1410072576 | bytes 5931008 | tf_op jit(solution)/shard_map/dot_general | solution.py:18
  191.2 3.0 %fusion.2 = bf16[1,384,2048]{2,1,0:T(8,128)(2,1)} fusion(bf16[896,384]{1,0:T(8,128)(2,1)S(1)} %copy-done.53, bf16[896,2048]{1,0:T(8,128)(2,1)S(1)} %copy-done.8), kind=kOutput, calls=%fused_computation.8 | convolution fusion | flops 1410072576 | bytes 5931008 | tf_op jit(solution)/shard_map/dot_general | solution.py:18
  195.1 7.7 %collective-permute-done.44.back = bf16[112,1024]{1,0:T(8,128)(2,1)S(1)} collective-permute-done((bf16[112,1024]{1,0:T(8,128)(2,1)S(1)}, bf16[112,1024]{1,0:T(8,128)(2,1)S(1)}, u32[]{:S(2)}, u32[]{:S(2)}) %collective-permute-start.44) | collective-permute-done | bytes 229408 | tf_op jit(solution)/shard_map/ppermute | solution.py:220
  206.5 1.1 collective-permute-start.41
  207.6 3.1 %collective-permute-done.45 = bf16[144,1024]{1,0:T(8,128)(2,1)S(1)} collective-permute-done((bf16[144,1024]{1,0:T(8,128)(2,1)S(1)}, bf16[144,1024]{1,0:T(8,128)(2,1)S(1)}, u32[]{:S(2)}, u32[]{:S(2)}) %collective-permute-start.45) | collective-permute-done | bytes 294944 | tf_op jit(solution)/shard_map/ppermute | solution.py:223
  210.8 17.0 %collective-permute-done.43 = bf16[144,1024]{1,0:T(8,128)(2,1)S(1)} collective-permute-done((bf16[144,1024]{1,0:T(8,128)(2,1)S(1)}, bf16[144,1024]{1,0:T(8,128)(2,1)S(1)}, u32[]{:S(2)}, u32[]{:S(2)}) %collective-permute-start.43) | collective-permute-done | bytes 294944 | tf_op jit(solution)/shard_map/ppermute | solution.py:223
  227.8 2.6 %collective-permute-done.41 = bf16[144,1024]{1,0:T(8,128)(2,1)S(1)} collective-permute-done((bf16[144,1024]{1,0:T(8,128)(2,1)S(1)}, bf16[144,1024]{1,0:T(8,128)(2,1)S(1)}, u32[]{:S(2)}, u32[]{:S(2)}) %collective-permute-start.41) | collective-permute-done | bytes 294944 | tf_op jit(solution)/shard_map/ppermute | solution.py:223
  (224 shorter events, 45.3 us)
Async XLA Ops:
  0.6 81.4 %copy-start = (bf16[1,384,2048]{2,1,0:T(8,128)(2,1)S(1)}, bf16[1,384,2048]{2,1,0:T(8,128)(2,1)}, u32[]{:S(2)}) copy-start(bf16[1,384,2048]{2,1,0:T(8,128)(2,1)} %param.13) | copy-start | bytes 4718596
  2.5 13.0 %collective-permute-start.1 = (bf16[144,1024]{1,0:T(8,128)(2,1)S(1)}, bf16[144,1024]{1,0:T(8,128)(2,1)S(1)}, u32[]{:S(2)}, u32[]{:S(2)}) collective-permute-start(bf16[144,1024]{1,0:T(8,128)(2,1)S(1)} %pad_maximum_fusion.refs_0_), channel_id=1, source_target_pairs={{4,0},{6,2},{8,4},{10,6},{12,8},{14,10},{5,1},{7,3},{9,5},{11,7},{... | collective-permute-start | bytes 884744 | tf_op jit(solution)/shard_map/ppermute | solution.py:230
  4.4 11.1 %collective-permute-start = (bf16[144,1024]{1,0:T(8,128)(2,1)S(1)}, bf16[144,1024]{1,0:T(8,128)(2,1)S(1)}, u32[]{:S(2)}, u32[]{:S(2)}) collective-permute-start(bf16[144,1024]{1,0:T(8,128)(2,1)S(1)} %pad_maximum_fusion.refs_0_), channel_id=1, source_target_pairs={{0,4},{2,6},{4,8},{6,10},{8,12},{10,14},{1,5},{3,7},{5,9},{7,11},{... | collective-permute-start | bytes 884744 | tf_op jit(solution)/shard_map/ppermute | solution.py:230
  9.6 5.9 %collective-permute-start.2 = (bf16[112,1024]{1,0:T(8,128)(2,1)S(1)}, bf16[112,1024]{1,0:T(8,128)(2,1)S(1)}, u32[]{:S(2)}, u32[]{:S(2)}) collective-permute-start(bf16[112,1024]{1,0:T(8,128)(2,1)S(1)} %get-tuple-element.165), channel_id=1, source_target_pairs={{0,2},{2,0},{4,6},{6,4},{8,10},{10,8},{12,14},{14,12},{1,3},{3,1},... | collective-permute-start | bytes 688136 | tf_op jit(solution)/shard_map/ppermute | solution.py:220
  15.5 27.1 %copy-start.14 = (bf16[112,1024]{1,0:T(8,128)(2,1)}, bf16[112,1024]{1,0:T(8,128)(2,1)S(1)}, u32[]{:S(2)}) copy-start(bf16[112,1024]{1,0:T(8,128)(2,1)S(1)} %collective-permute-done.2.refs_2_) | copy-start | bytes 688132
  15.5 16.0 %collective-permute-start.3 = (bf16[144,1024]{1,0:T(8,128)(2,1)S(1)}, bf16[144,1024]{1,0:T(8,128)(2,1)S(1)}, u32[]{:S(2)}, u32[]{:S(2)}) collective-permute-start(bf16[144,1024]{1,0:T(8,128)(2,1)S(1)} %collective-permute-done.refs_1_.refs_2_.refs_7_), channel_id=1, source_target_pairs={{4,8},{6,10},{8,12},{10,14},{5,9},{7,11},{9,13},{11,15},{20,24},{2... | collective-permute-start | bytes 884744 | tf_op jit(solution)/shard_map/ppermute | solution.py:230
  18.8 12.7 %collective-permute-start.4 = (bf16[144,1024]{1,0:T(8,128)(2,1)S(1)}, bf16[144,1024]{1,0:T(8,128)(2,1)S(1)}, u32[]{:S(2)}, u32[]{:S(2)}) collective-permute-start(bf16[144,1024]{1,0:T(8,128)(2,1)S(1)} %collective-permute-done.1.refs_0_.refs_1_.refs_5_), channel_id=1, source_target_pairs={{4,0},{6,2},{8,4},{10,6},{5,1},{7,3},{9,5},{11,7},{20,16},{22,18},... | collective-permute-start | bytes 884744 | tf_op jit(solution)/shard_map/ppermute | solution.py:230
  20.7 4.8 %collective-permute-start.6 = (bf16[112,1024]{1,0:T(8,128)(2,1)S(1)}, bf16[112,1024]{1,0:T(8,128)(2,1)S(1)}, u32[]{:S(2)}, u32[]{:S(2)}) collective-permute-start(bf16[112,1024]{1,0:T(8,128)(2,1)S(1)} %collective-permute-done.2.refs_2_), channel_id=1, source_target_pairs={{0,1},{1,0},{2,3},{3,2},{4,5},{5,4},{6,7},{7,6},{8,9},{9,8},{10,11... | collective-permute-start | bytes 688136 | tf_op jit(solution)/shard_map/ppermute | solution.py:236
  24.3 7.2 %collective-permute-start.5 = (bf16[112,1024]{1,0:T(8,128)(2,1)S(1)}, bf16[112,1024]{1,0:T(8,128)(2,1)S(1)}, u32[]{:S(2)}, u32[]{:S(2)}) collective-permute-start(bf16[112,1024]{1,0:T(8,128)(2,1)S(1)} %get-tuple-element.174), channel_id=1, source_target_pairs={{0,2},{2,0},{4,6},{6,4},{8,10},{10,8},{12,14},{14,12},{1,3},{3,1},... | collective-permute-start | bytes 688136 | tf_op jit(solution)/shard_map/ppermute | solution.py:220
  25.5 17.2 %copy-start.16 = (bf16[112,1024]{1,0:T(8,128)(2,1)}, bf16[112,1024]{1,0:T(8,128)(2,1)S(1)}, u32[]{:S(2)}) copy-start(bf16[112,1024]{1,0:T(8,128)(2,1)S(1)} %collective-permute-done.6.refs_6_) | copy-start | bytes 688132
  31.5 11.9 %copy-start.18 = (bf16[112,1024]{1,0:T(8,128)(2,1)}, bf16[112,1024]{1,0:T(8,128)(2,1)S(1)}, u32[]{:S(2)}) copy-start(bf16[112,1024]{1,0:T(8,128)(2,1)S(1)} %collective-permute-done.5.refs_3_) | copy-start | bytes 688132
  31.5 11.2 %collective-permute-start.7 = (bf16[144,1024]{1,0:T(8,128)(2,1)S(1)}, bf16[144,1024]{1,0:T(8,128)(2,1)S(1)}, u32[]{:S(2)}, u32[]{:S(2)}) collective-permute-start(bf16[144,1024]{1,0:T(8,128)(2,1)S(1)} %collective-permute-done.3.refs_1_.refs_4_), channel_id=1, source_target_pairs={{8,12},{10,14},{9,13},{11,15},{24,28},{26,30},{25,29},{27,31}} | collective-permute-start | bytes 884744 | tf_op jit(solution)/shard_map/ppermute | solution.py:230
  32.2 10.5 %collective-permute-start.8 = (bf16[144,1024]{1,0:T(8,128)(2,1)S(1)}, bf16[144,1024]{1,0:T(8,128)(2,1)S(1)}, u32[]{:S(2)}, u32[]{:S(2)}) collective-permute-start(bf16[144,1024]{1,0:T(8,128)(2,1)S(1)} %collective-permute-done.4.refs_0_.refs_3_), channel_id=1, source_target_pairs={{4,0},{6,2},{5,1},{7,3},{20,16},{22,18},{21,17},{23,19}} | collective-permute-start | bytes 884744 | tf_op jit(solution)/shard_map/ppermute | solution.py:230
  33.5 3.2 %collective-permute-start.10 = (bf16[112,1024]{1,0:T(8,128)(2,1)S(1)}, bf16[112,1024]{1,0:T(8,128)(2,1)S(1)}, u32[]{:S(2)}, u32[]{:S(2)}) collective-permute-start(bf16[112,1024]{1,0:T(8,128)(2,1)S(1)} %collective-permute-done.5.refs_3_), channel_id=1, source_target_pairs={{0,1},{1,0},{2,3},{3,2},{4,5},{5,4},{6,7},{7,6},{8,9},{9,8},{10,11... | collective-permute-start | bytes 688136 | tf_op jit(solution)/shard_map/ppermute | solution.py:236
  35.4 7.2 %collective-permute-start.9 = (bf16[112,1024]{1,0:T(8,128)(2,1)S(1)}, bf16[112,1024]{1,0:T(8,128)(2,1)S(1)}, u32[]{:S(2)}, u32[]{:S(2)}) collective-permute-start(bf16[112,1024]{1,0:T(8,128)(2,1)S(1)} %get-tuple-element.188), channel_id=1, source_target_pairs={{0,2},{2,0},{4,6},{6,4},{8,10},{10,8},{12,14},{14,12},{1,3},{3,1},... | collective-permute-start | bytes 688136 | tf_op jit(solution)/shard_map/ppermute | solution.py:220
  36.7 6.7 %copy-start.20 = (bf16[112,1024]{1,0:T(8,128)(2,1)}, bf16[112,1024]{1,0:T(8,128)(2,1)S(1)}, u32[]{:S(2)}) copy-start(bf16[112,1024]{1,0:T(8,128)(2,1)S(1)} %collective-permute-done.10.refs_7_) | copy-start | bytes 688132
  42.7 7.2 %copy-start.22 = (bf16[112,1024]{1,0:T(8,128)(2,1)}, bf16[112,1024]{1,0:T(8,128)(2,1)S(1)}, u32[]{:S(2)}) copy-start(bf16[112,1024]{1,0:T(8,128)(2,1)S(1)} %collective-permute-done.9.refs_4_) | copy-start | bytes 688132
  43.4 15.3 %copy-start.3 = (bf16[512,1024]{1,0:T(8,128)(2,1)}, bf16[512,1024]{1,0:T(8,128)(2,1)S(1)}, u32[]{:S(2)}) copy-start(bf16[512,1024]{1,0:T(8,128)(2,1)S(1)} %shard_map.131.refs_0_) | copy-start | bytes 3145732
  43.4 15.3 %collective-permute-start.15 = (bf16[512,1024]{1,0:T(8,128)(2,1)S(1)}, bf16[512,1024]{1,0:T(8,128)(2,1)S(1)}, u32[]{:S(2)}, u32[]{:S(2)}) collective-permute-start(bf16[512,1024]{1,0:T(8,128)(2,1)S(1)} %shard_map.131.refs_0_), channel_id=1, source_target_pairs={{0,1},{1,0},{2,3},{3,2},{4,5},{5,4},{6,7},{7,6},{8,9},{9,8},{10,11... | collective-permute-start | bytes 3145736 | tf_op jit(solution)/shard_map/ppermute | solution.py:236
  44.3 14.5 %collective-permute-start.11 = (bf16[128,1024]{1,0:T(8,128)(2,1)S(1)}, bf16[128,1024]{1,0:T(8,128)(2,1)S(1)}, u32[]{:S(2)}, u32[]{:S(2)}) collective-permute-start(bf16[128,1024]{1,0:T(8,128)(2,1)S(1)} %copy-done.9), channel_id=1, source_target_pairs={{0,4},{2,6},{4,8},{6,10},{8,12},{10,14},{1,5},{3,7},{5,9},{7,11},{... | collective-permute-start | bytes 786440 | tf_op jit(solution)/shard_map/ppermute | solution.py:230
  47.9 10.8 %collective-permute-start.12 = (bf16[128,1024]{1,0:T(8,128)(2,1)S(1)}, bf16[128,1024]{1,0:T(8,128)(2,1)S(1)}, u32[]{:S(2)}, u32[]{:S(2)}) collective-permute-start(bf16[128,1024]{1,0:T(8,128)(2,1)S(1)} %copy-done.9), channel_id=1, source_target_pairs={{4,0},{6,2},{8,4},{10,6},{12,8},{14,10},{5,1},{7,3},{9,5},{11,7},{... | collective-permute-start | bytes 786440 | tf_op jit(solution)/shard_map/ppermute | solution.py:230
  49.9 2.9 %collective-permute-start.14 = (bf16[112,1024]{1,0:T(8,128)(2,1)S(1)}, bf16[112,1024]{1,0:T(8,128)(2,1)S(1)}, u32[]{:S(2)}, u32[]{:S(2)}) collective-permute-start(bf16[112,1024]{1,0:T(8,128)(2,1)S(1)} %collective-permute-done.9.refs_4_), channel_id=1, source_target_pairs={{0,1},{1,0},{2,3},{3,2},{4,5},{5,4},{6,7},{7,6},{8,9},{9,8},{10,11... | collective-permute-start | bytes 688136 | tf_op jit(solution)/shard_map/ppermute | solution.py:236
  51.5 7.2 %collective-permute-start.13 = (bf16[112,1024]{1,0:T(8,128)(2,1)S(1)}, bf16[112,1024]{1,0:T(8,128)(2,1)S(1)}, u32[]{:S(2)}, u32[]{:S(2)}) collective-permute-start(bf16[112,1024]{1,0:T(8,128)(2,1)S(1)} %get-tuple-element.205), channel_id=1, source_target_pairs={{0,2},{2,0},{4,6},{6,4},{8,10},{10,8},{12,14},{14,12},{1,3},{3,1},... | collective-permute-start | bytes 688136 | tf_op jit(solution)/shard_map/ppermute | solution.py:220
  59.7 1.9 collective-permute-start.19
  73.2 4.7 %copy-start.35 = (bf16[896,2048]{1,0:T(8,128)(2,1)S(1)}, bf16[896,2048]{1,0:T(8,128)(2,1)}, u32[]{:S(2)}) copy-start(bf16[896,2048]{1,0:T(8,128)(2,1)} %copy-done.34) | copy-start | bytes 11010052
  73.2 4.7 %copy-start.49 = (bf16[1,2048,384]{2,1,0:T(8,128)(2,1)S(1)}, bf16[1,2048,384]{2,1,0:T(8,128)(2,1)}, u32[]{:S(2)}) copy-start(bf16[1,2048,384]{2,1,0:T(8,128)(2,1)} %param.12) | copy-start | bytes 4718596
  84.5 8.0 %collective-permute-start.20 = (bf16[896,1024]{1,0:T(8,128)(2,1)}, bf16[896,1024]{1,0:T(8,128)(2,1)}, u32[]{:S(2)}, u32[]{:S(2)}) collective-permute-start(bf16[896,1024]{1,0:T(8,128)(2,1)} %convolution_convert_fusion.3), channel_id=1, source_target_pairs={{0,1},{1,0},{2,3},{3,2},{4,5},{5,4},{6,7},{7,6},{8,9},{9,8},{10,11... | collective-permute-start | bytes 5505032 | tf_op jit(solution)/shard_map/ppermute | solution.py:236
  85.6 9.8 %collective-permute-start.18 = (bf16[96,1024]{1,0:T(8,128)(2,1)S(1)}, bf16[96,1024]{1,0:T(8,128)(2,1)S(1)}, u32[]{:S(2)}, u32[]{:S(2)}) collective-permute-start(bf16[96,1024]{1,0:T(8,128)(2,1)S(1)} %shard_map.132), channel_id=1, source_target_pairs={{0,2},{2,0},{4,6},{6,4},{8,10},{10,8},{12,14},{14,12},{1,3},{3,1},... | collective-permute-start | bytes 589832 | tf_op jit(solution)/shard_map/ppermute | solution.py:220
  86.9 8.9 %collective-permute-start.16 = (bf16[128,1024]{1,0:T(8,128)(2,1)S(1)}, bf16[128,1024]{1,0:T(8,128)(2,1)S(1)}, u32[]{:S(2)}, u32[]{:S(2)}) collective-permute-start(bf16[128,1024]{1,0:T(8,128)(2,1)S(1)} %collective-permute-done.11.refs_1_.refs_2_.refs_7_), channel_id=1, source_target_pairs={{4,8},{6,10},{8,12},{10,14},{5,9},{7,11},{9,13},{11,15},{20,24},{2... | collective-permute-start | bytes 786440 | tf_op jit(solution)/shard_map/ppermute | solution.py:230
  90.6 9.0 %collective-permute-start.17 = (bf16[128,1024]{1,0:T(8,128)(2,1)S(1)}, bf16[128,1024]{1,0:T(8,128)(2,1)S(1)}, u32[]{:S(2)}, u32[]{:S(2)}) collective-permute-start(bf16[128,1024]{1,0:T(8,128)(2,1)S(1)} %collective-permute-done.12.refs_0_.refs_1_.refs_5_), channel_id=1, source_target_pairs={{4,0},{6,2},{8,4},{10,6},{5,1},{7,3},{9,5},{11,7},{20,16},{22,18},... | collective-permute-start | bytes 786440 | tf_op jit(solution)/shard_map/ppermute | solution.py:230
  95.4 20.3 %copy-start.1 = (f32[896,1024]{1,0:T(8,128)}, f32[896,1024]{1,0:T(8,128)S(1)}, u32[]{:S(2)}) copy-start(f32[896,1024]{1,0:T(8,128)S(1)} %convert_add_fusion.1.both) | copy-start | bytes 11010052
  95.4 10.7 %copy-start.26 = (bf16[96,1024]{1,0:T(8,128)(2,1)}, bf16[96,1024]{1,0:T(8,128)(2,1)S(1)}, u32[]{:S(2)}) copy-start(bf16[96,1024]{1,0:T(8,128)(2,1)S(1)} %collective-permute-done.18.refs_2_) | copy-start | bytes 589828
  99.6 14.1 %collective-permute-start.21 = (bf16[128,1024]{1,0:T(8,128)(2,1)S(1)}, bf16[128,1024]{1,0:T(8,128)(2,1)S(1)}, u32[]{:S(2)}, u32[]{:S(2)}) collective-permute-start(bf16[128,1024]{1,0:T(8,128)(2,1)S(1)} %collective-permute-done.16.refs_1_.refs_4_), channel_id=1, source_target_pairs={{8,12},{10,14},{9,13},{11,15},{24,28},{26,30},{25,29},{27,31}} | collective-permute-start | bytes 786440 | tf_op jit(solution)/shard_map/ppermute | solution.py:230
  100.3 13.4 %collective-permute-start.22 = (bf16[128,1024]{1,0:T(8,128)(2,1)S(1)}, bf16[128,1024]{1,0:T(8,128)(2,1)S(1)}, u32[]{:S(2)}, u32[]{:S(2)}) collective-permute-start(bf16[128,1024]{1,0:T(8,128)(2,1)S(1)} %collective-permute-done.17.refs_0_.refs_3_), channel_id=1, source_target_pairs={{4,0},{6,2},{5,1},{7,3},{20,16},{22,18},{21,17},{23,19}} | collective-permute-start | bytes 786440 | tf_op jit(solution)/shard_map/ppermute | solution.py:230
  103.3 4.9 %collective-permute-start.23 = (bf16[96,1024]{1,0:T(8,128)(2,1)S(1)}, bf16[96,1024]{1,0:T(8,128)(2,1)S(1)}, u32[]{:S(2)}, u32[]{:S(2)}) collective-permute-start(bf16[96,1024]{1,0:T(8,128)(2,1)S(1)} %shard_map.134), channel_id=1, source_target_pairs={{0,2},{2,0},{4,6},{6,4},{8,10},{10,8},{12,14},{14,12},{1,3},{3,1},... | collective-permute-start | bytes 589832 | tf_op jit(solution)/shard_map/ppermute | solution.py:220
  103.6 4.6 %collective-permute-start.24 = (bf16[96,1024]{1,0:T(8,128)(2,1)S(1)}, bf16[96,1024]{1,0:T(8,128)(2,1)S(1)}, u32[]{:S(2)}, u32[]{:S(2)}) collective-permute-start(bf16[96,1024]{1,0:T(8,128)(2,1)S(1)} %collective-permute-done.18.refs_2_), channel_id=1, source_target_pairs={{0,1},{1,0},{2,3},{3,2},{4,5},{5,4},{6,7},{7,6},{8,9},{9,8},{10,11... | collective-permute-start | bytes 589832 | tf_op jit(solution)/shard_map/ppermute | solution.py:236
  106.7 7.7 %copy-start.39 = (bf16[96,1024]{1,0:T(8,128)(2,1)}, bf16[96,1024]{1,0:T(8,128)(2,1)S(1)}, u32[]{:S(2)}) copy-start(bf16[96,1024]{1,0:T(8,128)(2,1)S(1)} %get-tuple-element.303) | copy-start | bytes 589828
  106.7 7.7 %copy-start.41 = (bf16[96,1024]{1,0:T(8,128)(2,1)}, bf16[96,1024]{1,0:T(8,128)(2,1)S(1)}, u32[]{:S(2)}) copy-start(bf16[96,1024]{1,0:T(8,128)(2,1)S(1)} %get-tuple-element.305) | copy-start | bytes 589828
  106.7 7.0 %collective-permute-start.25 = (bf16[96,1024]{1,0:T(8,128)(2,1)S(1)}, bf16[96,1024]{1,0:T(8,128)(2,1)S(1)}, u32[]{:S(2)}, u32[]{:S(2)}) collective-permute-start(bf16[96,1024]{1,0:T(8,128)(2,1)S(1)} %get-tuple-element.260), channel_id=1, source_target_pairs={{0,2},{2,0},{4,6},{6,4},{8,10},{10,8},{12,14},{14,12},{1,3},{3,1},... | collective-permute-start | bytes 589832 | tf_op jit(solution)/shard_map/ppermute | solution.py:220
  108.2 11.7 %copy-start.28 = (bf16[96,1024]{1,0:T(8,128)(2,1)}, bf16[96,1024]{1,0:T(8,128)(2,1)S(1)}, u32[]{:S(2)}) copy-start(bf16[96,1024]{1,0:T(8,128)(2,1)S(1)} %collective-permute-done.23.refs_3_) | copy-start | bytes 589828
  108.2 6.2 %copy-start.30 = (bf16[96,1024]{1,0:T(8,128)(2,1)}, bf16[96,1024]{1,0:T(8,128)(2,1)S(1)}, u32[]{:S(2)}) copy-start(bf16[96,1024]{1,0:T(8,128)(2,1)S(1)} %collective-permute-done.24.refs_6_) | copy-start | bytes 589828
  114.4 14.5 %collective-permute-start.29 = (bf16[512,1024]{1,0:T(8,128)(2,1)S(1)}, bf16[512,1024]{1,0:T(8,128)(2,1)S(1)}, u32[]{:S(2)}, u32[]{:S(2)}) collective-permute-start(bf16[512,1024]{1,0:T(8,128)(2,1)S(1)} %shard_map.138.refs_0_), channel_id=1, source_target_pairs={{0,1},{1,0},{2,3},{3,2},{4,5},{5,4},{6,7},{7,6},{8,9},{9,8},{10,11... | collective-permute-start | bytes 3145736 | tf_op jit(solution)/shard_map/ppermute | solution.py:236
  116.5 12.5 %collective-permute-start.30 = (bf16[128,1024]{1,0:T(8,128)(2,1)S(1)}, bf16[128,1024]{1,0:T(8,128)(2,1)S(1)}, u32[]{:S(2)}, u32[]{:S(2)}) collective-permute-start(bf16[128,1024]{1,0:T(8,128)(2,1)S(1)} %shard_map.139), channel_id=1, source_target_pairs={{0,8},{2,10},{4,12},{6,14},{8,0},{10,2},{12,4},{14,6},{1,9},{3,11}... | collective-permute-start | bytes 786440 | tf_op jit(solution)/shard_map/ppermute | solution.py:223
  117.3 16.0 %copy-start.6 = (bf16[512,1024]{1,0:T(8,128)(2,1)S(1)}, bf16[512,1024]{1,0:T(8,128)(2,1)}, u32[]{:S(2)}) copy-start(bf16[512,1024]{1,0:T(8,128)(2,1)} %copy-done.5) | copy-start | bytes 3145732
  117.3 6.7 %collective-permute-start.27 = (bf16[96,1024]{1,0:T(8,128)(2,1)S(1)}, bf16[96,1024]{1,0:T(8,128)(2,1)}, u32[]{:S(2)}, u32[]{:S(2)}) collective-permute-start(bf16[96,1024]{1,0:T(8,128)(2,1)S(1)} %shard_map.137), channel_id=1, source_target_pairs={{0,2},{2,0},{4,6},{6,4},{8,10},{10,8},{12,14},{14,12},{1,3},{3,1},... | collective-permute-start | bytes 589832 | tf_op jit(solution)/shard_map/ppermute | solution.py:220
  118.7 9.5 %collective-permute-start.26 = (bf16[96,1024]{1,0:T(8,128)(2,1)S(1)}, bf16[96,1024]{1,0:T(8,128)(2,1)}, u32[]{:S(2)}, u32[]{:S(2)}) collective-permute-start(bf16[96,1024]{1,0:T(8,128)(2,1)S(1)} %shard_map.136), channel_id=1, source_target_pairs={{0,2},{2,0},{4,6},{6,4},{8,10},{10,8},{12,14},{14,12},{1,3},{3,1},... | collective-permute-start | bytes 589832 | tf_op jit(solution)/shard_map/ppermute | solution.py:220
  119.9 8.4 %collective-permute-start.28 = (bf16[96,1024]{1,0:T(8,128)(2,1)S(1)}, bf16[96,1024]{1,0:T(8,128)(2,1)S(1)}, u32[]{:S(2)}, u32[]{:S(2)}) collective-permute-start(bf16[96,1024]{1,0:T(8,128)(2,1)S(1)} %collective-permute-done.23.refs_3_), channel_id=1, source_target_pairs={{0,1},{1,0},{2,3},{3,2},{4,5},{5,4},{6,7},{7,6},{8,9},{9,8},{10,11... | collective-permute-start | bytes 589832 | tf_op jit(solution)/shard_map/ppermute | solution.py:236
  130.7 2.3 collective-permute-start.31
  131.5 1.8 collective-permute-start.32
  147.5 22.4 %collective-permute-start.33 = (bf16[896,1024]{1,0:T(8,128)(2,1)}, bf16[896,1024]{1,0:T(8,128)(2,1)}, u32[]{:S(2)}, u32[]{:S(2)}) collective-permute-start(bf16[896,1024]{1,0:T(8,128)(2,1)} %add_convert_fusion), channel_id=1, source_target_pairs={{0,1},{1,0},{2,3},{3,2},{4,5},{5,4},{6,7},{7,6},{8,9},{9,8},{10,11... | collective-permute-start | bytes 5505032 | tf_op jit(solution)/shard_map/ppermute | solution.py:236
  147.8 20.0 %collective-permute-start.34 = (bf16[96,1024]{1,0:T(8,128)(2,1)S(1)}, bf16[96,1024]{1,0:T(8,128)(2,1)S(1)}, u32[]{:S(2)}, u32[]{:S(2)}) collective-permute-start(bf16[96,1024]{1,0:T(8,128)(2,1)S(1)} %copy-done.38), channel_id=1, source_target_pairs={{0,2},{2,0},{4,6},{6,4},{8,10},{10,8},{12,14},{14,12},{1,3},{3,1},... | collective-permute-start | bytes 589832 | tf_op jit(solution)/shard_map/ppermute | solution.py:220
  148.3 17.7 %collective-permute-start.35 = (bf16[96,1024]{1,0:T(8,128)(2,1)S(1)}, bf16[96,1024]{1,0:T(8,128)(2,1)S(1)}, u32[]{:S(2)}, u32[]{:S(2)}) collective-permute-start(bf16[96,1024]{1,0:T(8,128)(2,1)S(1)} %copy-done.40), channel_id=1, source_target_pairs={{0,2},{2,0},{4,6},{6,4},{8,10},{10,8},{12,14},{14,12},{1,3},{3,1},... | collective-permute-start | bytes 589832 | tf_op jit(solution)/shard_map/ppermute | solution.py:220
  149.3 13.2 %collective-permute-start.37 = (bf16[96,1024]{1,0:T(8,128)(2,1)S(1)}, bf16[96,1024]{1,0:T(8,128)(2,1)S(1)}, u32[]{:S(2)}, u32[]{:S(2)}) collective-permute-start(bf16[96,1024]{1,0:T(8,128)(2,1)S(1)} %copy-done.42), channel_id=1, source_target_pairs={{0,2},{2,0},{4,6},{6,4},{8,10},{10,8},{12,14},{14,12},{1,3},{3,1},... | collective-permute-start | bytes 589832 | tf_op jit(solution)/shard_map/ppermute | solution.py:220
  165.4 8.3 %collective-permute-start.38 = (bf16[128,1024]{1,0:T(8,128)(2,1)S(1)}, bf16[128,1024]{1,0:T(8,128)(2,1)S(1)}, u32[]{:S(2)}, u32[]{:S(2)}) collective-permute-start(bf16[128,1024]{1,0:T(8,128)(2,1)S(1)} %shard_map.144), channel_id=1, source_target_pairs={{0,4},{2,6},{4,8},{6,10},{8,12},{10,14},{12,0},{14,2},{1,5},{3,7},... | collective-permute-start | bytes 786440 | tf_op jit(solution)/shard_map/ppermute | solution.py:223
  166.8 14.5 %collective-permute-start.36 = (bf16[128,1024]{1,0:T(8,128)(2,1)S(1)}, bf16[128,1024]{1,0:T(8,128)(2,1)S(1)}, u32[]{:S(2)}, u32[]{:S(2)}) collective-permute-start(bf16[128,1024]{1,0:T(8,128)(2,1)S(1)} %shard_map.143), channel_id=1, source_target_pairs={{0,12},{2,14},{4,0},{6,2},{8,4},{10,6},{12,8},{14,10},{1,13},{3,15... | collective-permute-start | bytes 786440 | tf_op jit(solution)/shard_map/ppermute | solution.py:223
  173.0 11.2 %copy-start.36 = (bf16[896,2048]{1,0:T(8,128)(2,1)S(1)}, bf16[896,2048]{1,0:T(8,128)(2,1)}, u32[]{:S(2)}) copy-start(bf16[896,2048]{1,0:T(8,128)(2,1)} %copy-done.34) | copy-start | bytes 11010052
  181.3 22.3 %collective-permute-start.39 = (bf16[112,1024]{1,0:T(8,128)(2,1)S(1)}, bf16[112,1024]{1,0:T(8,128)(2,1)S(1)}, u32[]{:S(2)}, u32[]{:S(2)}) collective-permute-start(bf16[112,1024]{1,0:T(8,128)(2,1)S(1)} %get-tuple-element.313), channel_id=1, source_target_pairs={{0,2},{2,0},{4,6},{6,4},{8,10},{10,8},{12,14},{14,12},{1,3},{3,1},... | collective-permute-start | bytes 688136 | tf_op jit(solution)/shard_map/ppermute | solution.py:220
  181.5 24.1 %collective-permute-start.40 = (bf16[112,1024]{1,0:T(8,128)(2,1)S(1)}, bf16[112,1024]{1,0:T(8,128)(2,1)S(1)}, u32[]{:S(2)}, u32[]{:S(2)}) collective-permute-start(bf16[112,1024]{1,0:T(8,128)(2,1)S(1)} %get-tuple-element.316), channel_id=1, source_target_pairs={{0,2},{2,0},{4,6},{6,4},{8,10},{10,8},{12,14},{14,12},{1,3},{3,1},... | collective-permute-start | bytes 688136 | tf_op jit(solution)/shard_map/ppermute | solution.py:220
  182.8 21.6 %collective-permute-start.42 = (bf16[112,1024]{1,0:T(8,128)(2,1)S(1)}, bf16[112,1024]{1,0:T(8,128)(2,1)S(1)}, u32[]{:S(2)}, u32[]{:S(2)}) collective-permute-start(bf16[112,1024]{1,0:T(8,128)(2,1)S(1)} %get-tuple-element.317), channel_id=1, source_target_pairs={{0,2},{2,0},{4,6},{6,4},{8,10},{10,8},{12,14},{14,12},{1,3},{3,1},... | collective-permute-start | bytes 688136 | tf_op jit(solution)/shard_map/ppermute | solution.py:220
  183.0 19.7 %collective-permute-start.44 = (bf16[112,1024]{1,0:T(8,128)(2,1)S(1)}, bf16[112,1024]{1,0:T(8,128)(2,1)S(1)}, u32[]{:S(2)}, u32[]{:S(2)}) collective-permute-start(bf16[112,1024]{1,0:T(8,128)(2,1)S(1)} %get-tuple-element.318), channel_id=1, source_target_pairs={{0,2},{2,0},{4,6},{6,4},{8,10},{10,8},{12,14},{14,12},{1,3},{3,1},... | collective-permute-start | bytes 688136 | tf_op jit(solution)/shard_map/ppermute | solution.py:220
  203.5 7.2 %collective-permute-start.45 = (bf16[144,1024]{1,0:T(8,128)(2,1)S(1)}, bf16[144,1024]{1,0:T(8,128)(2,1)S(1)}, u32[]{:S(2)}, u32[]{:S(2)}) collective-permute-start(bf16[144,1024]{1,0:T(8,128)(2,1)S(1)} %shard_map.148), channel_id=1, source_target_pairs={{0,4},{2,6},{4,8},{6,10},{8,12},{10,14},{12,0},{14,2},{1,5},{3,7},... | collective-permute-start | bytes 884744 | tf_op jit(solution)/shard_map/ppermute | solution.py:223
  205.2 22.6 %collective-permute-start.43 = (bf16[144,1024]{1,0:T(8,128)(2,1)S(1)}, bf16[144,1024]{1,0:T(8,128)(2,1)S(1)}, u32[]{:S(2)}, u32[]{:S(2)}) collective-permute-start(bf16[144,1024]{1,0:T(8,128)(2,1)S(1)} %shard_map.147), channel_id=1, source_target_pairs={{0,8},{2,10},{4,12},{6,14},{8,0},{10,2},{12,4},{14,6},{1,9},{3,11}... | collective-permute-start | bytes 884744 | tf_op jit(solution)/shard_map/ppermute | solution.py:223
  206.5 24.0 %collective-permute-start.41 = (bf16[144,1024]{1,0:T(8,128)(2,1)S(1)}, bf16[144,1024]{1,0:T(8,128)(2,1)S(1)}, u32[]{:S(2)}, u32[]{:S(2)}) collective-permute-start(bf16[144,1024]{1,0:T(8,128)(2,1)S(1)} %shard_map.146), channel_id=1, source_target_pairs={{0,12},{2,14},{4,0},{6,2},{8,4},{10,6},{12,8},{14,10},{1,13},{3,15... | collective-permute-start | bytes 884744 | tf_op jit(solution)/shard_map/ppermute | solution.py:223
  230.5 1.4 collective-permute-start.46
  (43 other events, 72.9 us)

commit v5 on v1

v5 whole, which is shorter than its diff:
```python
import functools

import jax
import jax.numpy as jnp
import numpy as np
from jax import lax
from jax.experimental import pallas as pl
from jax.experimental.pallas import tpu as pltpu
from jax.sharding import PartitionSpec as P

BF = jnp.bfloat16
F32 = jnp.float32
I32 = jnp.int32
TAIL = 16
ROWS = ((1,), (0,))
LAST = ((1,), (1,))
FIRST = ((0,), (0,))

SMEM_SPEC = pl.BlockSpec(memory_space=pltpu.SMEM)
VMEM_SPEC = pl.BlockSpec(memory_space=pltpu.VMEM)


def dot(a, b, contract):
    return lax.dot_general(a, b, (contract, ((), ())), preferred_element_type=F32)


def split_three(values):
    high = lax.reduce_precision(values, 8, 7)
    rest = values - high
    middle = lax.reduce_precision(rest, 8, 7)
    low = rest - middle
    return [part.astype(BF) for part in (high, middle, low)]


def shape_of(shape, dtype=BF):
    return jax.ShapeDtypeStruct(shape, dtype)


def local_call(kernel, outs, args, scratch=()):
    total = sum(int(np.prod(x.shape)) * x.dtype.itemsize for x in tuple(args) + tuple(outs))
    return pl.pallas_call(
        kernel,
        out_shape=tuple(outs),
        in_specs=[SMEM_SPEC] + [VMEM_SPEC] * (len(args) - 1),
        out_specs=(VMEM_SPEC,) * len(outs),
        scratch_shapes=list(scratch),
        compiler_params=pltpu.CompilerParams(vmem_limit_bytes=int(total * 1.25) + 4 * 1024 * 1024),
        cost_estimate=pl.CostEstimate(flops=1000, bytes_accessed=1000, transcendentals=0),
    )(*args)


def row_chunks(count):
    pieces = -(-count // 256)
    if count % (16 * pieces):
        pieces = 1
    return pieces, count // pieces


def token_pack_kernel(tokens, part_rows, capacity, padded, info, block, compact, place, own_parts, table, parts):
    width = compact.shape[1]
    per_row = width // tokens
    table[...] = block[tokens:, :].astype(F32)

    def parts_of(expert):
        row, lane = expert // per_row, pl.multiple_of((expert % per_row) * tokens, tokens)
        parts[...] = jnp.zeros_like(parts)
        for p in range(3):
            found = lax.broadcasted_iota(I32, (table.shape[0], tokens), 0) == p * part_rows + row
            parts[p:p + 1, :] = jnp.sum(
                jnp.where(found, table[:, pl.ds(lane, tokens)], 0.0), axis=0, keepdims=True)
        return parts[...]

    own_parts[...] = parts_of(info[0]).astype(BF)
    theirs = parts_of(info[1])
    named = jnp.sum(theirs, axis=0, keepdims=True) > 0.0
    row_at = lax.broadcasted_iota(I32, (tokens, tokens), 0)
    column_at = lax.broadcasted_iota(I32, (tokens, tokens), 1)
    until = (row_at <= column_at).astype(F32).astype(BF)
    ones = jnp.broadcast_to(named.astype(F32), (TAIL, tokens)).astype(BF)
    rank = jnp.dot(ones, until, preferred_element_type=F32)[:1, :].astype(I32) - 1
    picked = ((row_at == rank) & named & (row_at < capacity)).astype(F32).astype(BF)
    place[...] = picked[:padded, :]
    compact[:padded, :] = dot(picked[:padded, :], block[:tokens, :], ROWS).astype(BF)
    compact[padded:, :] = jnp.zeros((TAIL, width), BF)
    compact[padded:, :tokens] = dot(theirs.astype(BF), picked, LAST).astype(BF)


def grad_pack_kernel(info, block, place, compact):
    compact[...] = dot(place[...], block[...], ROWS).astype(BF)


def lay_out(lines, tokens, padded, blocks, compact, rows):
    for k in range(lines):
        rows[k * tokens:(k + 1) * tokens, :] = blocks[k][:tokens, :]
        at = lines * tokens + k * padded
        rows[at:at + padded, :] = compact[k][:padded, :]


def token_rows_kernel(lines, tokens, padded, info, *refs):
    n = lines
    blocks, compact, own_parts = refs[:n], refs[n:2 * n], refs[2 * n:3 * n]
    rows, weights = refs[3 * n:]
    lay_out(n, tokens, padded, blocks, compact, rows)
    eye = (lax.broadcasted_iota(I32, (tokens, tokens), 0)
           == lax.broadcasted_iota(I32, (tokens, tokens), 1))
    for k in range(n):
        for first, size, tail in (
            (k * tokens, tokens, own_parts[k][...]),
            (n * tokens + k * padded, padded, compact[k][padded:, :tokens]),
        ):
            row = jnp.sum(tail.astype(F32), axis=0, keepdims=True)
            column = jnp.sum(jnp.where(eye, row, 0.0), axis=1, keepdims=True)
            weights[first:first + size, :] = column[:size]


def grad_rows_kernel(lines, tokens, padded, info, *refs):
    lay_out(lines, tokens, padded, refs[:lines], refs[lines:2 * lines], refs[2 * lines])


def halves(info, width):
    core = info[2]
    return pl.ds(pl.multiple_of(core * width, width), width), pl.ds(pl.multiple_of((1 - core) * width, width), width)


def forward_kernel(pieces, chunk, info, own, other, weights, gate_w, up_w, down_w, gate, upward, scaled, sent):
    mine, theirs = halves(info, own.shape[1])

    @pl.loop(0, pieces)
    def _(i):
        at = pl.ds(pl.multiple_of(i * chunk, 16), chunk)
        a, b = own[at, :], other[at, :]
        g = dot(a, gate_w[mine, :], ROWS) + dot(b, gate_w[theirs, :], ROWS)
        u = dot(a, up_w[mine, :], ROWS) + dot(b, up_w[theirs, :], ROWS)
        gate[at, :] = g
        upward[at, :] = u
        h = (weights[at, :] * (g * jax.nn.sigmoid(g) * u)).astype(BF)
        scaled[at, :] = h
        sent[at, :] = dot(h, down_w[:, theirs], ROWS).astype(BF)


def backward_kernel(pieces, chunk, lines, tokens, padded, info, own, other, weights, gate, upward, gate_w, up_w,
                    down_w, grad_gate, grad_up, sent, dense_tails, compact_tails, values):
    mine, theirs = halves(info, own.shape[1])

    @pl.loop(0, pieces)
    def _(i):
        at = pl.ds(pl.multiple_of(i * chunk, 16), chunk)
        plain = dot(own[at, :], down_w[:, mine], LAST) + dot(other[at, :], down_w[:, theirs], LAST)
        g, u = gate[at, :], upward[at, :]
        sig = jax.nn.sigmoid(g)
        through = g * sig
        values[at, :] = jnp.sum(through * u * plain, axis=1, keepdims=True)
        scaled = weights[at, :] * plain
        gg = (scaled * u * sig * (1.0 + g * (1.0 - sig))).astype(BF)
        gu = (scaled * through).astype(BF)
        grad_gate[at, :] = gg
        grad_up[at, :] = gu
        sent[at, :] = (dot(gg, gate_w[theirs, :], LAST) + dot(gu, up_w[theirs, :], LAST)).astype(BF)

    eye = (lax.broadcasted_iota(I32, (tokens, tokens), 0)
           == lax.broadcasted_iota(I32, (tokens, tokens), 1))
    for k in range(lines):
        for first, size, tails in (
            (k * tokens, tokens, dense_tails),
            (lines * tokens + k * padded, padded, compact_tails),
        ):
            column = values[first:first + size, :]
            row = jnp.sum(jnp.where(eye[:size, :], column, 0.0), axis=0, keepdims=True)
            high = row.astype(BF).astype(F32)
            middle = (row - high).astype(BF).astype(F32)
            low = row - high - middle
            at = lax.broadcasted_iota(I32, (TAIL, tokens), 0)
            tails[k] = jnp.where(at == 0, high, jnp.where(at == 1, middle, jnp.where(at == 2, low, 0.0)))


def join_kernel(lines, tokens, padded, forward, info, came, *refs):
    width = came.shape[1]
    mine, _ = halves(info, width)
    if forward:
        scaled, down_w = refs[:2]
        dense, messages = refs[2], refs[3:]

        def product(at):
            return dot(scaled[at, :], down_w[:, mine], ROWS)
    else:
        grad_gate, grad_up, gate_w, up_w, tails = refs[:5]
        dense, messages = refs[5], refs[6:]

        def product(at):
            return dot(grad_gate[at, :], gate_w[mine, :], LAST) + dot(grad_up[at, :], up_w[mine, :], LAST)

    for k in range(lines):
        at = slice(lines * tokens + k * padded, lines * tokens + (k + 1) * padded)
        messages[k][:padded, :] = (product(at) + came[at, :].astype(F32)).astype(BF)
        if not forward:
            messages[k][padded:, :] = jnp.zeros((TAIL, width), BF)
            messages[k][padded:, :tokens] = tails[k].astype(BF)
    for k in range(lines):
        at = slice(k * tokens, (k + 1) * tokens)
        dense[k] = product(at) + came[at, :].astype(F32)


def home_kernel(k, tokens, padded, tailed, info, dense, back, place, *refs):
    message = refs[-1]
    block = dense[k] + dot(place[...], back[:padded, :], FIRST)
    message[:tokens, :] = block.astype(BF)
    if not tailed:
        return
    tails = refs[0]
    message[tokens:, :] = jnp.zeros((TAIL, message.shape[1]), BF)
    theirs = dot(back[padded:, :padded], place[...], ROWS)
    message[tokens:, :tokens] = jnp.concatenate([tails[k][:8], theirs[:8]], axis=0).astype(BF)


def per_device(tokens, expert_ids, router_weights, gate_weight, up_weight, down_weight, grad_out):
    token_count, half_width = tokens.shape
    hidden_half = gate_weight.shape[2]
    top_count = expert_ids.shape[1]
    experts = lax.axis_size("expert")
    capacity = min(token_count, 3 * token_count * top_count // (2 * experts))
    padded = -(-capacity // 16) * 16
    lines = experts // 2
    mine = lax.axis_index("expert")
    core = lax.axis_index("tensor")
    at_line = mine // 2
    peer = mine + 1 - 2 * (mine % 2)
    settle = lax.optimization_barrier

    def over_pair(x):
        return lax.ppermute(x, "expert", [(i, i + 1 - 2 * (i % 2)) for i in range(experts)])

    def over_line(x, k):
        return lax.ppermute(
            x, "expert",
            [(i, ((i // 2 + k) % lines) * 2 + i % 2) for i in range(experts)],
        )

    def over_core(x):
        return lax.ppermute(x, "tensor", [(0, 1), (1, 0)])

    chosen = expert_ids[:, :, None] == jnp.arange(experts, dtype=I32)[None, None, :]
    table = jnp.sum(jnp.where(chosen, router_weights[:, :, None], 0.0), axis=1).T
    part_rows = experts * token_count // half_width
    parts = jnp.concatenate([p.reshape(part_rows, half_width) for p in split_three(table)])
    tail = -(-3 * part_rows // TAIL) * TAIL
    parts = jnp.pad(parts, ((0, tail - 3 * part_rows), (0, 0)))
    first = jnp.concatenate([tokens, parts])

    info = jnp.stack([mine, peer, core]).astype(I32)
    sizes = (lines, token_count, padded)
    row_count = lines * (token_count + padded)
    half_rows = shape_of((row_count, half_width))
    hidden_rows = (row_count, hidden_half)
    gate_local = gate_weight[0]
    up_local = up_weight[0]
    down_local = down_weight[0]
    pieces, chunk = row_chunks(row_count)
    every = range(lines)
    by_reach = sorted(range(1, lines), key=lambda k: min(k, lines - k))

    blocks = {0: first}
    for k in by_reach:
        blocks[k] = over_line(first, k)
    compact, places, own_parts = {}, {}, {}
    for k in [0] + by_reach:
        packed, places[k], own_parts[k] = local_call(
            functools.partial(token_pack_kernel, token_count, part_rows, capacity, padded),
            (shape_of((padded + TAIL, half_width)), shape_of((padded, token_count)),
             shape_of((TAIL, token_count))),
            (info, blocks[k]),
            (pltpu.VMEM((tail, half_width), F32), pltpu.VMEM((TAIL, token_count), F32)),
        )
        compact[k] = over_pair(packed)

    held_grad, blocks = settle((grad_out, blocks))
    grad_blocks = {0: held_grad}
    for k in by_reach:
        grad_blocks[k] = over_line(held_grad, k)

    rows, weights = local_call(
        functools.partial(token_rows_kernel, *sizes),
        (half_rows, shape_of((row_count, 1), F32)),
        (info, *[blocks[k] for k in every], *[compact[k] for k in every], *[own_parts[k] for k in every]))
    rows_other = over_core(rows)
    gate, upward, scaled, sent = local_call(
        functools.partial(forward_kernel, pieces, chunk),
        (shape_of(hidden_rows, F32), shape_of(hidden_rows, F32), shape_of(hidden_rows), half_rows),
        (info, rows, rows_other, weights, gate_local, up_local, down_local))
    out_dense, *out_packed = local_call(
        functools.partial(join_kernel, *sizes, True),
        (shape_of((lines, token_count, half_width), F32),
         *[shape_of((padded, half_width)) for _ in every]),
        (info, over_core(sent), scaled, down_local))

    grad_compact = {}
    for k in [0] + by_reach:
        (packed,) = local_call(
            grad_pack_kernel, (shape_of((padded, half_width)),), (info, grad_blocks[k], places[k]))
        grad_compact[k] = over_pair(packed)
    out_back = {k: over_pair(out_packed[k]) for k in every}
    (grad_rows,) = local_call(
        functools.partial(grad_rows_kernel, *sizes), (half_rows,),
        (info, *[grad_blocks[k] for k in every], *[grad_compact[k] for k in every]))
    grad_rows, out_packed = settle((grad_rows, out_packed))
    grad_other = over_core(grad_rows)
    grad_gate, grad_up, sent, dense_tails, compact_tails = local_call(
        functools.partial(backward_kernel, pieces, chunk, *sizes),
        (shape_of(hidden_rows), shape_of(hidden_rows), half_rows,
         shape_of((lines, TAIL, token_count), F32), shape_of((lines, TAIL, token_count), F32)),
        (info, grad_rows, grad_other, weights, gate, upward, gate_local, up_local, down_local),
        (pltpu.VMEM((row_count, 1), F32),))
    sent, out_back = settle((sent, out_back))
    out_home = {}
    for k in by_reach[::-1] + [0]:
        (block,) = local_call(
            functools.partial(home_kernel, k, token_count, padded, False),
            (shape_of((token_count, half_width)),), (info, out_dense, out_back[k], places[k]))
        out_home[k] = over_line(block, lines - k) if k else block
    in_dense, *in_packed = local_call(
        functools.partial(join_kernel, *sizes, False),
        (shape_of((lines, token_count, half_width), F32),
         *[shape_of((padded + TAIL, half_width)) for _ in every]),
        (info, over_core(sent), grad_gate, grad_up, gate_local, up_local, compact_tails))
    in_packed, rows, rows_other, grad_rows, grad_other, scaled, grad_gate, grad_up = settle(
        (in_packed, rows, rows_other, grad_rows, grad_other, scaled, grad_gate, grad_up))
    in_back = {k: over_pair(in_packed[k]) for k in every}

    def summed(blocks):
        total = blocks[0][:token_count].astype(F32)
        for k in range(1, lines):
            total = total + blocks[k][:token_count].astype(F32)
        return total.astype(BF)

    layer_out = summed(out_home)
    in_back = {k: settle((in_back[k], layer_out))[0] for k in every}
    in_home = {}
    for k in by_reach[::-1] + [0]:
        (block,) = local_call(
            functools.partial(home_kernel, k, token_count, padded, True),
            (shape_of((token_count + TAIL, half_width)),),
            (info, in_dense, in_back[k], places[k], dense_tails))
        in_home[k] = over_line(block, lines - k) if k else block
    input_grad = summed(in_home)

    def whole(own, other):
        return jnp.concatenate(
            [jnp.where(core == 0, own, other), jnp.where(core == 0, other, own)], axis=1)

    rows = whole(rows, rows_other)
    grads = whole(grad_rows, grad_other)
    down_grad = dot(scaled, grads, FIRST).astype(BF)
    gate_grad = dot(rows, grad_gate, FIRST).astype(BF)
    up_grad = dot(rows, grad_up, FIRST).astype(BF)

    held = []
    for k in every:
        values = in_home[k][token_count:, :token_count].astype(F32)
        held.append(jnp.stack([jnp.sum(values[:8], axis=0), jnp.sum(values[8:], axis=0)]))
    flat = jnp.stack(held).reshape(experts, token_count)
    place = (expert_ids // 2 - at_line) % lines
    slot = place * 2 + ((expert_ids % 2) != (mine % 2)).astype(I32)
    match = slot[:, :, None] == jnp.arange(experts, dtype=I32)[None, None, :]
    half_value = jnp.sum(jnp.where(match, flat.T[:, None, :], 0.0), axis=2)
    weight_grad = half_value + over_core(half_value)
    return (layer_out, input_grad, weight_grad, gate_grad[None], up_grad[None], down_grad[None])


def solution(mesh):
    in_specs = (
        P(("group", "expert"), "tensor"),
        P(("group", "expert"), None),
        P(("group", "expert"), None),
        P("expert", None, "tensor"),
        P("expert", None, "tensor"),
        P("expert", "tensor", None),
        P(("group", "expert"), "tensor"),
    )
    out_specs = (
        P(("group", "expert"), "tensor"),
        P(("group", "expert"), "tensor"),
        P(("group", "expert"), None),
        P(("group", "expert"), None, "tensor"),
        P(("group", "expert"), None, "tensor"),
        P(("group", "expert"), "tensor", None),
    )
    return jax.shard_map(
        per_device, mesh=mesh, in_specs=in_specs, out_specs=out_specs, check_vma=False
    )
```

time: 206 us -> 204 us (level)
  the two profiles are of different devices: /device:TPU:0 before, /device:TPU:9 now
where the time goes in v5:
time: 204 us; the launch traced here: 203 us
  waiting for transfers between devices  101 us (50%)
  starting transfers between devices  40.5 us (20%)
  Pallas kernels  39.7 us (19%)
  matrix products  9.79 us (5%)
  other arithmetic  6.03 us (3%)
  local copies, waits for them, and re-layouts  4.71 us (2%)
    ppermute x12, waiting for transfers between devices, over_line(): lax.ppermute(x, 'expert', [(i, (i // 2 + k) % lines * 2 + i % 2) for i in...  71.6 us
    pallas_call x22, Pallas kernels, local_call(): pl.pallas_call(kernel, out_shape=tuple(outs), in_specs=[SMEM_SPEC] + [VME...  39.7 us
    ppermute x16, waiting for transfers between devices, over_pair(): lax.ppermute(x, 'expert', [(i, i + 1 - 2 * (i % 2)) for i in range(expert...  25.7 us
    ppermute x12, starting transfers between devices, over_line(): lax.ppermute(x, 'expert', [(i, (i // 2 + k) % lines * 2 + i % 2) for i in...  18.7 us
    ppermute x16, starting transfers between devices, over_pair(): lax.ppermute(x, 'expert', [(i, i + 1 - 2 * (i % 2)) for i in range(expert...  16.4 us
    dot_general x3, matrix products, dot(): lax.dot_general(a, b, (contract, ((), ())), preferred_element_type=F32)  9.79 us
    ppermute x5, starting transfers between devices, over_core(): return lax.ppermute(x, 'tensor', [(0, 1), (1, 0)])  5.44 us
    unnamed x61, local copies, waits for them, and re-layouts  4.7 us
  transfers between devices with their start and end apart: 33, of which 19 were waited for; matrix products, arithmetic and copies ran while one was open for 7% of the time, Pallas kernels for 12%

profile of v5, /device:TPU:9, one launch (start us, length us, event | category | flops | bytes accessed | tf_op | source)
XLA Modules:
  0.0 203.1 jit_solution(7034465167228700957)
XLA Ops:
  1.4 1.1 pad_maximum_fusion.3.block.refs_0_
  2.6 2.5 %collective-permute-start.1 = (bf16[144,1024]{1,0:T(8,128)(2,1)S(1)}, bf16[144,1024]{1,0:T(8,128)(2,1)}, u32[]{:S(2)}, u32[]{:S(2)}) collective-permute-start(bf16[144,1024]{1,0:T(8,128)(2,1)S(1)} %pad_maximum_fusion.3.block.refs_0_), channel_id=1, source_target_pairs={{0,8},{2,10},{4,12},{6,14},{8,0},{10,2},{12,4},{14,6},{1,9},{3,11}... | collective-permute-start | bytes 884744 | tf_op jit(solution)/shard_map/ppermute | solution.py:233
  5.1 2.2 %collective-permute-start = (bf16[144,1024]{1,0:T(8,128)(2,1)S(1)}, bf16[144,1024]{1,0:T(8,128)(2,1)}, u32[]{:S(2)}, u32[]{:S(2)}) collective-permute-start(bf16[144,1024]{1,0:T(8,128)(2,1)S(1)} %pad_maximum_fusion.3.block.refs_0_), channel_id=1, source_target_pairs={{0,4},{2,6},{4,8},{6,10},{8,12},{10,14},{12,0},{14,2},{1,5},{3,7},... | collective-permute-start | bytes 884744 | tf_op jit(solution)/shard_map/ppermute | solution.py:233
  7.4 0.9 shard_map.118
  8.3 1.3 collective-permute-start.3
  9.6 1.0 collective-permute-done.2.block.refs_3_
  10.6 1.3 shard_map.121
  11.9 1.3 collective-permute-start.6
  13.2 10.5 %collective-permute-done.1.block.refs_2_ = bf16[144,1024]{1,0:T(8,128)(2,1)} collective-permute-done((bf16[144,1024]{1,0:T(8,128)(2,1)S(1)}, bf16[144,1024]{1,0:T(8,128)(2,1)}, u32[]{:S(2)}, u32[]{:S(2)}) %collective-permute-start.1) | collective-permute-done | bytes 294944 | tf_op jit(solution)/shard_map/ppermute | solution.py:233
  23.7 1.3 shard_map.120
  25.0 1.3 collective-permute-start.5
  26.3 3.7 %collective-permute-done.block.refs_1_ = bf16[144,1024]{1,0:T(8,128)(2,1)} collective-permute-done((bf16[144,1024]{1,0:T(8,128)(2,1)S(1)}, bf16[144,1024]{1,0:T(8,128)(2,1)}, u32[]{:S(2)}, u32[]{:S(2)}) %collective-permute-start) | collective-permute-done | bytes 294944 | tf_op jit(solution)/shard_map/ppermute | solution.py:233
  30.0 1.3 shard_map.119
  31.4 1.3 collective-permute-start.4
  32.7 6.3 %collective-permute-done.4.refs_5_ = bf16[112,1024]{1,0:T(8,128)(2,1)S(1)} collective-permute-done((bf16[112,1024]{1,0:T(8,128)(2,1)S(1)}, bf16[112,1024]{1,0:T(8,128)(2,1)S(1)}, u32[]{:S(2)}, u32[]{:S(2)}) %collective-permute-start.4) | collective-permute-done | bytes 229408 | tf_op jit(solution)/shard_map/ppermute | solution.py:230
  39.0 1.4 shard_map.122
  40.4 2.2 %collective-permute-start.7 = (bf16[896,1024]{1,0:T(8,128)(2,1)S(1)}, bf16[896,1024]{1,0:T(8,128)(2,1)S(1)}, u32[]{:S(2)}, u32[]{:S(2)}) collective-permute-start(bf16[896,1024]{1,0:T(8,128)(2,1)S(1)} %get-tuple-element.117.own), channel_id=1, source_target_pairs={{0,1},{1,0},{2,3},{3,2},{4,5},{5,4},{6,7},{7,6},{8,9},{9,8},{10,11... | collective-permute-start | bytes 5505032 | tf_op jit(solution)/shard_map/ppermute | solution.py:239
  42.6 3.4 %collective-permute-done.7.other = bf16[896,1024]{1,0:T(8,128)(2,1)S(1)} collective-permute-done((bf16[896,1024]{1,0:T(8,128)(2,1)S(1)}, bf16[896,1024]{1,0:T(8,128)(2,1)S(1)}, u32[]{:S(2)}, u32[]{:S(2)}) %collective-permute-start.7) | collective-permute-done | bytes 1835040 | tf_op jit(solution)/shard_map/ppermute | solution.py:239
  46.0 2.1 %copy-done.7 = bf16[1,2048,384]{2,1,0:T(8,128)(2,1)S(1)} copy-done((bf16[1,2048,384]{2,1,0:T(8,128)(2,1)S(1)}, bf16[1,2048,384]{2,1,0:T(8,128)(2,1)}, u32[]{:S(2)}) %copy-start.7) | copy-done | bytes 1572888
  48.1 6.4 %shard_map.123 = (f32[896,384]{1,0:T(8,128)S(1)}, f32[896,384]{1,0:T(8,128)S(1)}, bf16[896,384]{1,0:T(8,128)(2,1)S(1)}, bf16[896,1024]{1,0:T(8,128)(2,1)S(1)}) custom-call(s32[3]{0:T(128)S(1)} %pad_add_fusion.info, bf16[896,1024]{1,0:T(8,128)(2,1)S(1)} %get-tuple-element.117.own, bf16[896,1024]{1,0:T(8,128)(2,1)S(1)} %collective-permute-done.7.other, ...), custom_call_target="tpu_custom_call" | custom-call | flops 1000 | bytes 1000 | tf_op jit(solution)/shard_map/pallas_call | solution.py:41
  54.9 3.9 %collective-permute-start.11 = (bf16[128,1024]{1,0:T(8,128)(2,1)S(1)}, bf16[128,1024]{1,0:T(8,128)(2,1)S(1)}, u32[]{:S(2)}, u32[]{:S(2)}) collective-permute-start(bf16[128,1024]{1,0:T(8,128)(2,1)S(1)} %copy-done.15), channel_id=1, source_target_pairs={{0,12},{2,14},{4,0},{6,2},{8,4},{10,6},{12,8},{14,10},{1,13},{3,15... | collective-permute-start | bytes 786440 | tf_op jit(solution)/shard_map/ppermute | solution.py:233
  58.8 1.2 collective-permute-start.9
  60.8 1.3 collective-permute-start.12
  62.1 3.6 %collective-permute-done.11.block.refs_3_ = bf16[128,1024]{1,0:T(8,128)(2,1)S(1)} collective-permute-done((bf16[128,1024]{1,0:T(8,128)(2,1)S(1)}, bf16[128,1024]{1,0:T(8,128)(2,1)S(1)}, u32[]{:S(2)}, u32[]{:S(2)}) %collective-permute-start.11) | collective-permute-done | bytes 262176 | tf_op jit(solution)/shard_map/ppermute | solution.py:233
  66.4 1.3 collective-permute-start.15
  67.7 8.2 %collective-permute-done.10.block.refs_2_ = bf16[128,1024]{1,0:T(8,128)(2,1)S(1)} collective-permute-done((bf16[128,1024]{1,0:T(8,128)(2,1)S(1)}, bf16[128,1024]{1,0:T(8,128)(2,1)S(1)}, u32[]{:S(2)}, u32[]{:S(2)}) %collective-permute-start.10) | collective-permute-done | bytes 262176 | tf_op jit(solution)/shard_map/ppermute | solution.py:233
  76.6 1.3 collective-permute-start.14
  77.9 3.6 %collective-permute-done.9.block.refs_1_ = bf16[128,1024]{1,0:T(8,128)(2,1)S(1)} collective-permute-done((bf16[128,1024]{1,0:T(8,128)(2,1)S(1)}, bf16[128,1024]{1,0:T(8,128)(2,1)S(1)}, u32[]{:S(2)}, u32[]{:S(2)}) %collective-permute-start.9) | collective-permute-done | bytes 262176 | tf_op jit(solution)/shard_map/ppermute | solution.py:233
  82.3 1.3 collective-permute-start.13
  83.6 4.7 %collective-permute-done.13.refs_5_ = bf16[96,1024]{1,0:T(8,128)(2,1)S(1)} collective-permute-done((bf16[96,1024]{1,0:T(8,128)(2,1)S(1)}, bf16[96,1024]{1,0:T(8,128)(2,1)S(1)}, u32[]{:S(2)}, u32[]{:S(2)}) %collective-permute-start.13) | collective-permute-done | bytes 196640 | tf_op jit(solution)/shard_map/ppermute | solution.py:230
  89.0 1.9 shard_map.124
  91.0 1.4 collective-permute-start.16
  92.3 1.3 collective-permute-start.17
  93.8 1.2 collective-permute-start.19
  95.8 7.6 %shard_map.130 = (bf16[896,384]{1,0:T(8,128)(2,1)S(1)}, bf16[896,384]{1,0:T(8,128)(2,1)S(1)}, bf16[896,1024]{1,0:T(8,128)(2,1)}, f32[4,16,128]{2,1,0:T(8,128)S(1)}, f32[4,16,128]{2,1,0:T(8,128)S(1)}) custom-call(s32[3]{0:T(128)S(1)} %pad_add_fusion.info, bf16[896,1024]{1,0:T(8,128)(2,1)S(1)} %shard_map.129.own, ...), custom_call_target="tpu_custom_call" | custom-call | flops 1000 | bytes 1000 | tf_op jit(solution)/shard_map/pallas_call | solution.py:41
  103.4 3.8 %collective-permute-done.19.back = bf16[96,1024]{1,0:T(8,128)(2,1)S(1)} collective-permute-done((bf16[96,1024]{1,0:T(8,128)(2,1)S(1)}, bf16[96,1024]{1,0:T(8,128)(2,1)S(1)}, u32[]{:S(2)}, u32[]{:S(2)}) %collective-permute-start.19) | collective-permute-done | bytes 196640 | tf_op jit(solution)/shard_map/ppermute | solution.py:230
  107.2 4.2 %collective-permute-done.20.back = bf16[96,1024]{1,0:T(8,128)(2,1)S(1)} collective-permute-done((bf16[96,1024]{1,0:T(8,128)(2,1)S(1)}, bf16[96,1024]{1,0:T(8,128)(2,1)S(1)}, u32[]{:S(2)}, u32[]{:S(2)}) %collective-permute-start.20) | collective-permute-done | bytes 196640 | tf_op jit(solution)/shard_map/ppermute | solution.py:230
  111.5 0.8 collective-permute-start.24
  112.3 1.5 shard_map.133
  113.8 1.5 shard_map.132
  115.3 4.1 %collective-permute-start.21 = (bf16[128,1024]{1,0:T(8,128)(2,1)}, bf16[128,1024]{1,0:T(8,128)(2,1)}, u32[]{:S(2)}, u32[]{:S(2)}) collective-permute-start(bf16[128,1024]{1,0:T(8,128)(2,1)} %shard_map.132), channel_id=1, source_target_pairs={{0,12},{2,14},{4,0},{6,2},{8,4},{10,6},{12,8},{14,10},{1,13},{3,15... | collective-permute-start | bytes 786440 | tf_op jit(solution)/shard_map/ppermute | solution.py:233
  119.4 1.5 shard_map.134
  120.9 1.3 collective-permute-start.23
  123.0 0.9 copy-done.26
  124.7 2.1 %collective-permute-done.21 = bf16[128,1024]{1,0:T(8,128)(2,1)} collective-permute-done((bf16[128,1024]{1,0:T(8,128)(2,1)}, bf16[128,1024]{1,0:T(8,128)(2,1)}, u32[]{:S(2)}, u32[]{:S(2)}) %collective-permute-start.21) | collective-permute-done | bytes 262176 | tf_op jit(solution)/shard_map/ppermute | solution.py:233
  126.8 10.1 %collective-permute-done.22 = bf16[128,1024]{1,0:T(8,128)(2,1)} collective-permute-done((bf16[128,1024]{1,0:T(8,128)(2,1)}, bf16[128,1024]{1,0:T(8,128)(2,1)}, u32[]{:S(2)}, u32[]{:S(2)}) %collective-permute-start.22) | collective-permute-done | bytes 262176 | tf_op jit(solution)/shard_map/ppermute | solution.py:233
  136.8 5.6 %collective-permute-done.23 = bf16[128,1024]{1,0:T(8,128)(2,1)} collective-permute-done((bf16[128,1024]{1,0:T(8,128)(2,1)}, bf16[128,1024]{1,0:T(8,128)(2,1)}, u32[]{:S(2)}, u32[]{:S(2)}) %collective-permute-start.23) | collective-permute-done | bytes 262176 | tf_op jit(solution)/shard_map/ppermute | solution.py:233
  142.5 2.0 add_convert_fusion.1
  144.5 5.6 %shard_map.135 = (f32[4,128,1024]{2,1,0:T(8,128)S(1)}, bf16[112,1024]{1,0:T(8,128)(2,1)S(1)}, bf16[112,1024]{1,0:T(8,128)(2,1)S(1)}, bf16[112,1024]{1,0:T(8,128)(2,1)S(1)}, bf16[112,1024]{1,0:T(8,128)(2,1)S(1)}) custom-call(s32[3]{0:T(128)S(1)} %pad_add_fusion.info, bf16[896,1024]{1,0:T(8,128)(2,1)} %collective-permute-done.24.came, ...), custom_call_target="tpu_custom_call" | custom-call | flops 1000 | bytes 1000 | tf_op jit(solution)/shard_map/pallas_call | solution.py:41
  150.1 1.3 collective-permute-start.25
  151.6 1.2 collective-permute-start.28
  153.3 3.4 %fusion.8 = bf16[1,2048,384]{2,1,0:T(8,128)(2,1)} fusion(bf16[896,384]{1,0:T(8,128)(2,1)S(1)} %get-tuple-element.120.refs_1_, bf16[896,1024]{1,0:T(8,128)(2,1)S(1)} %get-tuple-element.135, bf16[896,1024]{1,0:T(8,128)(2,1)S(1)} %get-tuple-element.134), kind=kOutput, calls=%fused_computation.9 | convolution fusion | flops 1417412608 | bytes 5931008 | tf_op jit(solution)/shard_map/dot_general | solution.py:24
  156.8 3.4 %fusion.7 = bf16[1,2048,384]{2,1,0:T(8,128)(2,1)} fusion(bf16[896,384]{1,0:T(8,128)(2,1)S(1)} %get-tuple-element.119.refs_0_, bf16[896,1024]{1,0:T(8,128)(2,1)S(1)} %get-tuple-element.135, bf16[896,1024]{1,0:T(8,128)(2,1)S(1)} %get-tuple-element.134), kind=kOutput, calls=%fused_computation.8 | convolution fusion | flops 1417412608 | bytes 5931008 | tf_op jit(solution)/shard_map/dot_general | solution.py:24
  160.4 0.9 copy-done.17
  161.3 3.0 %fusion.9 = bf16[1,384,2048]{2,1,0:T(8,128)(2,1)} fusion(bf16[896,384]{1,0:T(8,128)(2,1)S(1)} %copy-done.17, bf16[896,1024]{1,0:T(8,128)(2,1)S(1)} %get-tuple-element.133, bf16[896,1024]{1,0:T(8,128)(2,1)S(1)} %get-tuple-element.132), kind=kOutput, calls=%fused_computation.10 | convolution fusion | flops 1417412608 | bytes 5931008 | tf_op jit(solution)/shard_map/dot_general | solution.py:24
  164.3 0.8 shard_map.136
  165.1 6.6 %collective-permute-done.30.back = bf16[112,1024]{1,0:T(8,128)(2,1)S(1)} collective-permute-done((bf16[112,1024]{1,0:T(8,128)(2,1)S(1)}, bf16[112,1024]{1,0:T(8,128)(2,1)S(1)}, u32[]{:S(2)}, u32[]{:S(2)}) %collective-permute-start.30) | collective-permute-done | bytes 229408 | tf_op jit(solution)/shard_map/ppermute | solution.py:230
  171.7 0.8 shard_map.139
  172.5 2.3 %collective-permute-start.31 = (bf16[144,1024]{1,0:T(8,128)(2,1)S(1)}, bf16[144,1024]{1,0:T(8,128)(2,1)S(1)}, u32[]{:S(2)}, u32[]{:S(2)}) collective-permute-start(bf16[144,1024]{1,0:T(8,128)(2,1)S(1)} %shard_map.139), channel_id=1, source_target_pairs={{0,4},{2,6},{4,8},{6,10},{8,12},{10,14},{12,0},{14,2},{1,5},{3,7},... | collective-permute-start | bytes 884744 | tf_op jit(solution)/shard_map/ppermute | solution.py:233
  176.4 1.2 collective-permute-start.27
  177.6 2.6 %collective-permute-done.31 = bf16[144,1024]{1,0:T(8,128)(2,1)S(1)} collective-permute-done((bf16[144,1024]{1,0:T(8,128)(2,1)S(1)}, bf16[144,1024]{1,0:T(8,128)(2,1)S(1)}, u32[]{:S(2)}, u32[]{:S(2)}) %collective-permute-start.31) | collective-permute-done | bytes 294944 | tf_op jit(solution)/shard_map/ppermute | solution.py:233
  180.3 18.4 %collective-permute-done.29 = bf16[144,1024]{1,0:T(8,128)(2,1)S(1)} collective-permute-done((bf16[144,1024]{1,0:T(8,128)(2,1)S(1)}, bf16[144,1024]{1,0:T(8,128)(2,1)S(1)}, u32[]{:S(2)}, u32[]{:S(2)}) %collective-permute-start.29) | collective-permute-done | bytes 294944 | tf_op jit(solution)/shard_map/ppermute | solution.py:233
  198.7 2.3 %collective-permute-done.27 = bf16[144,1024]{1,0:T(8,128)(2,1)S(1)} collective-permute-done((bf16[144,1024]{1,0:T(8,128)(2,1)S(1)}, bf16[144,1024]{1,0:T(8,128)(2,1)S(1)}, u32[]{:S(2)}, u32[]{:S(2)}) %collective-permute-start.27) | collective-permute-done | bytes 294944 | tf_op jit(solution)/shard_map/ppermute | solution.py:233
  201.6 0.9 add_convert_fusion
  (114 shorter events, 11.4 us)
Async XLA Ops:
  1.4 44.6 %copy-start.2 = (bf16[1,384,2048]{2,1,0:T(8,128)(2,1)S(1)}, bf16[1,384,2048]{2,1,0:T(8,128)(2,1)}, u32[]{:S(2)}) copy-start(bf16[1,384,2048]{2,1,0:T(8,128)(2,1)} %param.12) | copy-start | bytes 4718596
  1.4 44.6 %copy-start.4 = (bf16[1,2048,384]{2,1,0:T(8,128)(2,1)S(1)}, bf16[1,2048,384]{2,1,0:T(8,128)(2,1)}, u32[]{:S(2)}) copy-start(bf16[1,2048,384]{2,1,0:T(8,128)(2,1)} %param.10) | copy-start | bytes 4718596
  2.6 8.0 %collective-permute-start.2 = (bf16[144,1024]{1,0:T(8,128)(2,1)S(1)}, bf16[144,1024]{1,0:T(8,128)(2,1)}, u32[]{:S(2)}, u32[]{:S(2)}) collective-permute-start(bf16[144,1024]{1,0:T(8,128)(2,1)S(1)} %pad_maximum_fusion.3.block.refs_0_), channel_id=1, source_target_pairs={{0,12},{2,14},{4,0},{6,2},{8,4},{10,6},{12,8},{14,10},{1,13},{3,15... | collective-permute-start | bytes 884744 | tf_op jit(solution)/shard_map/ppermute | solution.py:233
  2.6 21.1 %collective-permute-start.1 = (bf16[144,1024]{1,0:T(8,128)(2,1)S(1)}, bf16[144,1024]{1,0:T(8,128)(2,1)}, u32[]{:S(2)}, u32[]{:S(2)}) collective-permute-start(bf16[144,1024]{1,0:T(8,128)(2,1)S(1)} %pad_maximum_fusion.3.block.refs_0_), channel_id=1, source_target_pairs={{0,8},{2,10},{4,12},{6,14},{8,0},{10,2},{12,4},{14,6},{1,9},{3,11}... | collective-permute-start | bytes 884744 | tf_op jit(solution)/shard_map/ppermute | solution.py:233
  5.1 24.9 %collective-permute-start = (bf16[144,1024]{1,0:T(8,128)(2,1)S(1)}, bf16[144,1024]{1,0:T(8,128)(2,1)}, u32[]{:S(2)}, u32[]{:S(2)}) collective-permute-start(bf16[144,1024]{1,0:T(8,128)(2,1)S(1)} %pad_maximum_fusion.3.block.refs_0_), channel_id=1, source_target_pairs={{0,4},{2,6},{4,8},{6,10},{8,12},{10,14},{12,0},{14,2},{1,5},{3,7},... | collective-permute-start | bytes 884744 | tf_op jit(solution)/shard_map/ppermute | solution.py:233
  8.2 51.8 %copy-start.18 = (bf16[96,128]{1,0:T(8,128)(2,1)}, bf16[96,128]{1,0:T(8,128)(2,1)S(1)}, u32[]{:S(2)}) copy-start(bf16[96,128]{1,0:T(8,128)(2,1)S(1)} %get-tuple-element.83.place) | copy-start | bytes 73732
  8.3 24.4 %collective-permute-start.3 = (bf16[112,1024]{1,0:T(8,128)(2,1)S(1)}, bf16[112,1024]{1,0:T(8,128)(2,1)S(1)}, u32[]{:S(2)}, u32[]{:S(2)}) collective-permute-start(bf16[112,1024]{1,0:T(8,128)(2,1)S(1)} %get-tuple-element.69), channel_id=1, source_target_pairs={{0,2},{2,0},{4,6},{6,4},{8,10},{10,8},{12,14},{14,12},{1,3},{3,1},... | collective-permute-start | bytes 688136 | tf_op jit(solution)/shard_map/ppermute | solution.py:230
  11.9 107.5 %copy-start.21 = (bf16[96,128]{1,0:T(8,128)(2,1)}, bf16[96,128]{1,0:T(8,128)(2,1)S(1)}, u32[]{:S(2)}) copy-start(bf16[96,128]{1,0:T(8,128)(2,1)S(1)} %get-tuple-element.86.place) | copy-start | bytes 73732
  11.9 20.8 %collective-permute-start.6 = (bf16[112,1024]{1,0:T(8,128)(2,1)S(1)}, bf16[112,1024]{1,0:T(8,128)(2,1)S(1)}, u32[]{:S(2)}, u32[]{:S(2)}) collective-permute-start(bf16[112,1024]{1,0:T(8,128)(2,1)S(1)} %get-tuple-element.72), channel_id=1, source_target_pairs={{0,2},{2,0},{4,6},{6,4},{8,10},{10,8},{12,14},{14,12},{1,3},{3,1},... | collective-permute-start | bytes 688136 | tf_op jit(solution)/shard_map/ppermute | solution.py:230
  25.0 7.6 %collective-permute-start.5 = (bf16[112,1024]{1,0:T(8,128)(2,1)S(1)}, bf16[112,1024]{1,0:T(8,128)(2,1)S(1)}, u32[]{:S(2)}, u32[]{:S(2)}) collective-permute-start(bf16[112,1024]{1,0:T(8,128)(2,1)S(1)} %get-tuple-element.71), channel_id=1, source_target_pairs={{0,2},{2,0},{4,6},{6,4},{8,10},{10,8},{12,14},{14,12},{1,3},{3,1},... | collective-permute-start | bytes 688136 | tf_op jit(solution)/shard_map/ppermute | solution.py:230
  31.3 82.5 %copy-start.23 = (bf16[96,128]{1,0:T(8,128)(2,1)}, bf16[96,128]{1,0:T(8,128)(2,1)S(1)}, u32[]{:S(2)}) copy-start(bf16[96,128]{1,0:T(8,128)(2,1)S(1)} %get-tuple-element.84.place) | copy-start | bytes 73732
  31.4 7.6 %collective-permute-start.4 = (bf16[112,1024]{1,0:T(8,128)(2,1)S(1)}, bf16[112,1024]{1,0:T(8,128)(2,1)S(1)}, u32[]{:S(2)}, u32[]{:S(2)}) collective-permute-start(bf16[112,1024]{1,0:T(8,128)(2,1)S(1)} %get-tuple-element.70), channel_id=1, source_target_pairs={{0,2},{2,0},{4,6},{6,4},{8,10},{10,8},{12,14},{14,12},{1,3},{3,1},... | collective-permute-start | bytes 688136 | tf_op jit(solution)/shard_map/ppermute | solution.py:230
  40.4 14.1 %copy-start.9 = (bf16[896,1024]{1,0:T(8,128)(2,1)}, bf16[896,1024]{1,0:T(8,128)(2,1)S(1)}, u32[]{:S(2)}) copy-start(bf16[896,1024]{1,0:T(8,128)(2,1)S(1)} %get-tuple-element.117.own) | copy-start | bytes 5505028
  40.4 5.6 %collective-permute-start.7 = (bf16[896,1024]{1,0:T(8,128)(2,1)S(1)}, bf16[896,1024]{1,0:T(8,128)(2,1)S(1)}, u32[]{:S(2)}, u32[]{:S(2)}) collective-permute-start(bf16[896,1024]{1,0:T(8,128)(2,1)S(1)} %get-tuple-element.117.own), channel_id=1, source_target_pairs={{0,1},{1,0},{2,3},{3,2},{4,5},{5,4},{6,7},{7,6},{8,9},{9,8},{10,11... | collective-permute-start | bytes 5505032 | tf_op jit(solution)/shard_map/ppermute | solution.py:239
  46.0 8.5 %copy-start.11 = (bf16[896,1024]{1,0:T(8,128)(2,1)}, bf16[896,1024]{1,0:T(8,128)(2,1)S(1)}, u32[]{:S(2)}) copy-start(bf16[896,1024]{1,0:T(8,128)(2,1)S(1)} %collective-permute-done.7.other) | copy-start | bytes 5505028
  46.0 2.1 %copy-start.7 = (bf16[1,2048,384]{2,1,0:T(8,128)(2,1)S(1)}, bf16[1,2048,384]{2,1,0:T(8,128)(2,1)}, u32[]{:S(2)}) copy-start(bf16[1,2048,384]{2,1,0:T(8,128)(2,1)} %param.11) | copy-start | bytes 4718596
  48.1 6.8 %copy-start.15 = (bf16[128,1024]{1,0:T(8,128)(2,1)S(1)}, bf16[128,1024]{1,0:T(8,128)(2,1)}, u32[]{:S(2)}) copy-start(bf16[128,1024]{1,0:T(8,128)(2,1)} %refs_0_) | copy-start | bytes 786436
  54.5 34.5 %copy-start.16 = (bf16[896,384]{1,0:T(8,128)(2,1)}, bf16[896,384]{1,0:T(8,128)(2,1)S(1)}, u32[]{:S(2)}) copy-start(bf16[896,384]{1,0:T(8,128)(2,1)S(1)} %get-tuple-element.121.refs_0_) | copy-start | bytes 2064388
  54.5 34.5 %collective-permute-start.8 = (bf16[896,1024]{1,0:T(8,128)(2,1)S(1)}, bf16[896,1024]{1,0:T(8,128)(2,1)S(1)}, u32[]{:S(2)}, u32[]{:S(2)}) collective-permute-start(bf16[896,1024]{1,0:T(8,128)(2,1)S(1)} %get-tuple-element.79), channel_id=1, source_target_pairs={{0,1},{1,0},{2,3},{3,2},{4,5},{5,4},{6,7},{7,6},{8,9},{9,8},{10,11... | collective-permute-start | bytes 5505032 | tf_op jit(solution)/shard_map/ppermute | solution.py:239
  54.9 10.7 %collective-permute-start.11 = (bf16[128,1024]{1,0:T(8,128)(2,1)S(1)}, bf16[128,1024]{1,0:T(8,128)(2,1)S(1)}, u32[]{:S(2)}, u32[]{:S(2)}) collective-permute-start(bf16[128,1024]{1,0:T(8,128)(2,1)S(1)} %copy-done.15), channel_id=1, source_target_pairs={{0,12},{2,14},{4,0},{6,2},{8,4},{10,6},{12,8},{14,10},{1,13},{3,15... | collective-permute-start | bytes 786440 | tf_op jit(solution)/shard_map/ppermute | solution.py:233
  58.8 17.1 %collective-permute-start.10 = (bf16[128,1024]{1,0:T(8,128)(2,1)S(1)}, bf16[128,1024]{1,0:T(8,128)(2,1)S(1)}, u32[]{:S(2)}, u32[]{:S(2)}) collective-permute-start(bf16[128,1024]{1,0:T(8,128)(2,1)S(1)} %copy-done.15), channel_id=1, source_target_pairs={{0,8},{2,10},{4,12},{6,14},{8,0},{10,2},{12,4},{14,6},{1,9},{3,11}... | collective-permute-start | bytes 786440 | tf_op jit(solution)/shard_map/ppermute | solution.py:233
  58.8 22.7 %collective-permute-start.9 = (bf16[128,1024]{1,0:T(8,128)(2,1)S(1)}, bf16[128,1024]{1,0:T(8,128)(2,1)S(1)}, u32[]{:S(2)}, u32[]{:S(2)}) collective-permute-start(bf16[128,1024]{1,0:T(8,128)(2,1)S(1)} %copy-done.15), channel_id=1, source_target_pairs={{0,4},{2,6},{4,8},{6,10},{8,12},{10,14},{12,0},{14,2},{1,5},{3,7},... | collective-permute-start | bytes 786440 | tf_op jit(solution)/shard_map/ppermute | solution.py:233
  60.8 22.8 %collective-permute-start.12 = (bf16[96,1024]{1,0:T(8,128)(2,1)S(1)}, bf16[96,1024]{1,0:T(8,128)(2,1)S(1)}, u32[]{:S(2)}, u32[]{:S(2)}) collective-permute-start(bf16[96,1024]{1,0:T(8,128)(2,1)S(1)} %shard_map.125), channel_id=1, source_target_pairs={{0,2},{2,0},{4,6},{6,4},{8,10},{10,8},{12,14},{14,12},{1,3},{3,1},... | collective-permute-start | bytes 589832 | tf_op jit(solution)/shard_map/ppermute | solution.py:230
  66.4 17.2 %collective-permute-start.15 = (bf16[96,1024]{1,0:T(8,128)(2,1)S(1)}, bf16[96,1024]{1,0:T(8,128)(2,1)S(1)}, u32[]{:S(2)}, u32[]{:S(2)}) collective-permute-start(bf16[96,1024]{1,0:T(8,128)(2,1)S(1)} %shard_map.128), channel_id=1, source_target_pairs={{0,2},{2,0},{4,6},{6,4},{8,10},{10,8},{12,14},{14,12},{1,3},{3,1},... | collective-permute-start | bytes 589832 | tf_op jit(solution)/shard_map/ppermute | solution.py:230
  76.6 6.9 %collective-permute-start.14 = (bf16[96,1024]{1,0:T(8,128)(2,1)S(1)}, bf16[96,1024]{1,0:T(8,128)(2,1)S(1)}, u32[]{:S(2)}, u32[]{:S(2)}) collective-permute-start(bf16[96,1024]{1,0:T(8,128)(2,1)S(1)} %shard_map.127), channel_id=1, source_target_pairs={{0,2},{2,0},{4,6},{6,4},{8,10},{10,8},{12,14},{14,12},{1,3},{3,1},... | collective-permute-start | bytes 589832 | tf_op jit(solution)/shard_map/ppermute | solution.py:230
  82.3 6.8 %copy-start.3 = (bf16[1,384,2048]{2,1,0:T(8,128)(2,1)S(1)}, bf16[1,384,2048]{2,1,0:T(8,128)(2,1)}, u32[]{:S(2)}) copy-start(bf16[1,384,2048]{2,1,0:T(8,128)(2,1)} %param.12) | copy-start | bytes 4718596
  82.3 6.1 %collective-permute-start.13 = (bf16[96,1024]{1,0:T(8,128)(2,1)S(1)}, bf16[96,1024]{1,0:T(8,128)(2,1)S(1)}, u32[]{:S(2)}, u32[]{:S(2)}) collective-permute-start(bf16[96,1024]{1,0:T(8,128)(2,1)S(1)} %shard_map.126), channel_id=1, source_target_pairs={{0,2},{2,0},{4,6},{6,4},{8,10},{10,8},{12,14},{14,12},{1,3},{3,1},... | collective-permute-start | bytes 589832 | tf_op jit(solution)/shard_map/ppermute | solution.py:230
  89.0 6.8 %copy-start = (bf16[896,1024]{1,0:T(8,128)(2,1)}, bf16[896,1024]{1,0:T(8,128)(2,1)S(1)}, u32[]{:S(2)}) copy-start(bf16[896,1024]{1,0:T(8,128)(2,1)S(1)} %shard_map.129.own) | copy-start | bytes 5505028
  89.0 6.7 %copy-start.5 = (bf16[1,2048,384]{2,1,0:T(8,128)(2,1)S(1)}, bf16[1,2048,384]{2,1,0:T(8,128)(2,1)}, u32[]{:S(2)}) copy-start(bf16[1,2048,384]{2,1,0:T(8,128)(2,1)} %param.10) | copy-start | bytes 4718596
  91.0 4.8 %collective-permute-start.16 = (bf16[896,1024]{1,0:T(8,128)(2,1)S(1)}, bf16[896,1024]{1,0:T(8,128)(2,1)S(1)}, u32[]{:S(2)}, u32[]{:S(2)}) collective-permute-start(bf16[896,1024]{1,0:T(8,128)(2,1)S(1)} %shard_map.129.own), channel_id=1, source_target_pairs={{0,1},{1,0},{2,3},{3,2},{4,5},{5,4},{6,7},{7,6},{8,9},{9,8},{10,11... | collective-permute-start | bytes 5505032 | tf_op jit(solution)/shard_map/ppermute | solution.py:239
  92.3 11.1 %collective-permute-start.17 = (bf16[96,1024]{1,0:T(8,128)(2,1)S(1)}, bf16[96,1024]{1,0:T(8,128)(2,1)S(1)}, u32[]{:S(2)}, u32[]{:S(2)}) collective-permute-start(bf16[96,1024]{1,0:T(8,128)(2,1)S(1)} %get-tuple-element.87), channel_id=1, source_target_pairs={{0,2},{2,0},{4,6},{6,4},{8,10},{10,8},{12,14},{14,12},{1,3},{3,1},... | collective-permute-start | bytes 589832 | tf_op jit(solution)/shard_map/ppermute | solution.py:230
  93.6 9.8 %collective-permute-start.18 = (bf16[96,1024]{1,0:T(8,128)(2,1)S(1)}, bf16[96,1024]{1,0:T(8,128)(2,1)S(1)}, u32[]{:S(2)}, u32[]{:S(2)}) collective-permute-start(bf16[96,1024]{1,0:T(8,128)(2,1)S(1)} %get-tuple-element.88), channel_id=1, source_target_pairs={{0,2},{2,0},{4,6},{6,4},{8,10},{10,8},{12,14},{14,12},{1,3},{3,1},... | collective-permute-start | bytes 589832 | tf_op jit(solution)/shard_map/ppermute | solution.py:230
  93.8 13.4 %collective-permute-start.19 = (bf16[96,1024]{1,0:T(8,128)(2,1)S(1)}, bf16[96,1024]{1,0:T(8,128)(2,1)S(1)}, u32[]{:S(2)}, u32[]{:S(2)}) collective-permute-start(bf16[96,1024]{1,0:T(8,128)(2,1)S(1)} %get-tuple-element.89), channel_id=1, source_target_pairs={{0,2},{2,0},{4,6},{6,4},{8,10},{10,8},{12,14},{14,12},{1,3},{3,1},... | collective-permute-start | bytes 589832 | tf_op jit(solution)/shard_map/ppermute | solution.py:230
  95.1 16.4 %collective-permute-start.20 = (bf16[96,1024]{1,0:T(8,128)(2,1)S(1)}, bf16[96,1024]{1,0:T(8,128)(2,1)S(1)}, u32[]{:S(2)}, u32[]{:S(2)}) collective-permute-start(bf16[96,1024]{1,0:T(8,128)(2,1)S(1)} %get-tuple-element.90), channel_id=1, source_target_pairs={{0,2},{2,0},{4,6},{6,4},{8,10},{10,8},{12,14},{14,12},{1,3},{3,1},... | collective-permute-start | bytes 589832 | tf_op jit(solution)/shard_map/ppermute | solution.py:230
  95.8 7.7 %copy-start.13 = (bf16[896,1024]{1,0:T(8,128)(2,1)}, bf16[896,1024]{1,0:T(8,128)(2,1)S(1)}, u32[]{:S(2)}) copy-start(bf16[896,1024]{1,0:T(8,128)(2,1)S(1)} %collective-permute-done.16.other) | copy-start | bytes 5505028
  103.4 11.9 %copy-start.27 = (f32[4,16,128]{2,1,0:T(8,128)}, f32[4,16,128]{2,1,0:T(8,128)S(1)}, u32[]{:S(2)}) copy-start(f32[4,16,128]{2,1,0:T(8,128)S(1)} %get-tuple-element.102.refs_4_) | copy-start | bytes 98308
  103.4 11.9 %copy-start.25 = (bf16[96,1024]{1,0:T(8,128)(2,1)}, bf16[96,1024]{1,0:T(8,128)(2,1)S(1)}, u32[]{:S(2)}) copy-start(bf16[96,1024]{1,0:T(8,128)(2,1)S(1)} %collective-permute-done.17.back) | copy-start | bytes 589828
  111.5 33.0 %collective-permute-start.24 = (bf16[896,1024]{1,0:T(8,128)(2,1)}, bf16[896,1024]{1,0:T(8,128)(2,1)}, u32[]{:S(2)}, u32[]{:S(2)}) collective-permute-start(bf16[896,1024]{1,0:T(8,128)(2,1)} %get-tuple-element.99), channel_id=1, source_target_pairs={{0,1},{1,0},{2,3},{3,2},{4,5},{5,4},{6,7},{7,6},{8,9},{9,8},{10,11... | collective-permute-start | bytes 5505032 | tf_op jit(solution)/shard_map/ppermute | solution.py:239
  115.3 6.9 %copy-start.29 = (s32[128,4]{0,1:T(4,128)S(1)}, s32[128,4]{0,1:T(4,128)}, u32[]{:S(2)}) copy-start(s32[128,4]{0,1:T(4,128)} %param.8) | copy-start | bytes 6148
  115.3 11.4 %collective-permute-start.21 = (bf16[128,1024]{1,0:T(8,128)(2,1)}, bf16[128,1024]{1,0:T(8,128)(2,1)}, u32[]{:S(2)}, u32[]{:S(2)}) collective-permute-start(bf16[128,1024]{1,0:T(8,128)(2,1)} %shard_map.132), channel_id=1, source_target_pairs={{0,12},{2,14},{4,0},{6,2},{8,4},{10,6},{12,8},{14,10},{1,13},{3,15... | collective-permute-start | bytes 786440 | tf_op jit(solution)/shard_map/ppermute | solution.py:233
  119.4 17.4 %collective-permute-start.22 = (bf16[128,1024]{1,0:T(8,128)(2,1)}, bf16[128,1024]{1,0:T(8,128)(2,1)}, u32[]{:S(2)}, u32[]{:S(2)}) collective-permute-start(bf16[128,1024]{1,0:T(8,128)(2,1)} %shard_map.133), channel_id=1, source_target_pairs={{0,8},{2,10},{4,12},{6,14},{8,0},{10,2},{12,4},{14,6},{1,9},{3,11}... | collective-permute-start | bytes 786440 | tf_op jit(solution)/shard_map/ppermute | solution.py:233
  120.9 21.5 %collective-permute-start.23 = (bf16[128,1024]{1,0:T(8,128)(2,1)}, bf16[128,1024]{1,0:T(8,128)(2,1)}, u32[]{:S(2)}, u32[]{:S(2)}) collective-permute-start(bf16[128,1024]{1,0:T(8,128)(2,1)} %shard_map.134), channel_id=1, source_target_pairs={{0,4},{2,6},{4,8},{6,10},{8,12},{10,14},{12,0},{14,2},{1,5},{3,7},... | collective-permute-start | bytes 786440 | tf_op jit(solution)/shard_map/ppermute | solution.py:233
  122.2 0.7 copy-start.19
  123.0 0.9 copy-start.26
  123.9 20.6 %copy-start.6 = (bf16[1,2048,384]{2,1,0:T(8,128)(2,1)S(1)}, bf16[1,2048,384]{2,1,0:T(8,128)(2,1)}, u32[]{:S(2)}) copy-start(bf16[1,2048,384]{2,1,0:T(8,128)(2,1)} %param.10) | copy-start | bytes 4718596
  123.9 20.6 %copy-start.8 = (bf16[1,2048,384]{2,1,0:T(8,128)(2,1)S(1)}, bf16[1,2048,384]{2,1,0:T(8,128)(2,1)}, u32[]{:S(2)}) copy-start(bf16[1,2048,384]{2,1,0:T(8,128)(2,1)} %param.11) | copy-start | bytes 4718596
  123.9 20.6 %copy-start.28 = (f32[4,16,128]{2,1,0:T(8,128)S(1)}, f32[4,16,128]{2,1,0:T(8,128)}, u32[]{:S(2)}) copy-start(f32[4,16,128]{2,1,0:T(8,128)} %copy-done.27) | copy-start | bytes 98308
  144.5 8.6 %copy-start.10 = (bf16[896,1024]{1,0:T(8,128)(2,1)S(1)}, bf16[896,1024]{1,0:T(8,128)(2,1)}, u32[]{:S(2)}) copy-start(bf16[896,1024]{1,0:T(8,128)(2,1)} %copy-done.9) | copy-start | bytes 5505028
  144.5 8.6 %copy-start.12 = (bf16[896,1024]{1,0:T(8,128)(2,1)S(1)}, bf16[896,1024]{1,0:T(8,128)(2,1)}, u32[]{:S(2)}) copy-start(bf16[896,1024]{1,0:T(8,128)(2,1)} %copy-done.11) | copy-start | bytes 5505028
  150.1 14.2 %collective-permute-start.25 = (bf16[112,1024]{1,0:T(8,128)(2,1)S(1)}, bf16[112,1024]{1,0:T(8,128)(2,1)S(1)}, u32[]{:S(2)}, u32[]{:S(2)}) collective-permute-start(bf16[112,1024]{1,0:T(8,128)(2,1)S(1)} %get-tuple-element.108), channel_id=1, source_target_pairs={{0,2},{2,0},{4,6},{6,4},{8,10},{10,8},{12,14},{14,12},{1,3},{3,1},... | collective-permute-start | bytes 688136 | tf_op jit(solution)/shard_map/ppermute | solution.py:230
  151.4 23.3 %collective-permute-start.26 = (bf16[112,1024]{1,0:T(8,128)(2,1)S(1)}, bf16[112,1024]{1,0:T(8,128)(2,1)S(1)}, u32[]{:S(2)}, u32[]{:S(2)}) collective-permute-start(bf16[112,1024]{1,0:T(8,128)(2,1)S(1)} %get-tuple-element.111), channel_id=1, source_target_pairs={{0,2},{2,0},{4,6},{6,4},{8,10},{10,8},{12,14},{14,12},{1,3},{3,1},... | collective-permute-start | bytes 688136 | tf_op jit(solution)/shard_map/ppermute | solution.py:230
  151.6 23.9 %collective-permute-start.28 = (bf16[112,1024]{1,0:T(8,128)(2,1)S(1)}, bf16[112,1024]{1,0:T(8,128)(2,1)S(1)}, u32[]{:S(2)}, u32[]{:S(2)}) collective-permute-start(bf16[112,1024]{1,0:T(8,128)(2,1)S(1)} %get-tuple-element.113), channel_id=1, source_target_pairs={{0,2},{2,0},{4,6},{6,4},{8,10},{10,8},{12,14},{14,12},{1,3},{3,1},... | collective-permute-start | bytes 688136 | tf_op jit(solution)/shard_map/ppermute | solution.py:230
  152.9 18.8 %collective-permute-start.30 = (bf16[112,1024]{1,0:T(8,128)(2,1)S(1)}, bf16[112,1024]{1,0:T(8,128)(2,1)S(1)}, u32[]{:S(2)}, u32[]{:S(2)}) collective-permute-start(bf16[112,1024]{1,0:T(8,128)(2,1)S(1)} %get-tuple-element.115), channel_id=1, source_target_pairs={{0,2},{2,0},{4,6},{6,4},{8,10},{10,8},{12,14},{14,12},{1,3},{3,1},... | collective-permute-start | bytes 688136 | tf_op jit(solution)/shard_map/ppermute | solution.py:230
  156.8 3.4 %copy-start.1 = (bf16[896,1024]{1,0:T(8,128)(2,1)S(1)}, bf16[896,1024]{1,0:T(8,128)(2,1)}, u32[]{:S(2)}) copy-start(bf16[896,1024]{1,0:T(8,128)(2,1)} %copy-done) | copy-start | bytes 5505028
  156.8 3.4 %copy-start.14 = (bf16[896,1024]{1,0:T(8,128)(2,1)S(1)}, bf16[896,1024]{1,0:T(8,128)(2,1)}, u32[]{:S(2)}) copy-start(bf16[896,1024]{1,0:T(8,128)(2,1)} %copy-done.13) | copy-start | bytes 5505028
  160.2 1.1 copy-start.17
  161.3 3.0 %copy-start.20 = (bf16[96,128]{1,0:T(8,128)(2,1)S(1)}, bf16[96,128]{1,0:T(8,128)(2,1)}, u32[]{:S(2)}) copy-start(bf16[96,128]{1,0:T(8,128)(2,1)} %copy-done.18) | copy-start | bytes 73732
  164.3 7.4 %copy-start.22 = (bf16[96,128]{1,0:T(8,128)(2,1)S(1)}, bf16[96,128]{1,0:T(8,128)(2,1)}, u32[]{:S(2)}) copy-start(bf16[96,128]{1,0:T(8,128)(2,1)} %copy-done.21) | copy-start | bytes 73732
  165.1 9.7 %copy-start.24 = (bf16[96,128]{1,0:T(8,128)(2,1)S(1)}, bf16[96,128]{1,0:T(8,128)(2,1)}, u32[]{:S(2)}) copy-start(bf16[96,128]{1,0:T(8,128)(2,1)} %copy-done.23) | copy-start | bytes 73732
  172.5 7.8 %collective-permute-start.31 = (bf16[144,1024]{1,0:T(8,128)(2,1)S(1)}, bf16[144,1024]{1,0:T(8,128)(2,1)S(1)}, u32[]{:S(2)}, u32[]{:S(2)}) collective-permute-start(bf16[144,1024]{1,0:T(8,128)(2,1)S(1)} %shard_map.139), channel_id=1, source_target_pairs={{0,4},{2,6},{4,8},{6,10},{8,12},{10,14},{12,0},{14,2},{1,5},{3,7},... | collective-permute-start | bytes 884744 | tf_op jit(solution)/shard_map/ppermute | solution.py:233
  176.3 22.4 %collective-permute-start.29 = (bf16[144,1024]{1,0:T(8,128)(2,1)S(1)}, bf16[144,1024]{1,0:T(8,128)(2,1)S(1)}, u32[]{:S(2)}, u32[]{:S(2)}) collective-permute-start(bf16[144,1024]{1,0:T(8,128)(2,1)S(1)} %shard_map.138), channel_id=1, source_target_pairs={{0,8},{2,10},{4,12},{6,14},{8,0},{10,2},{12,4},{14,6},{1,9},{3,11}... | collective-permute-start | bytes 884744 | tf_op jit(solution)/shard_map/ppermute | solution.py:233
  176.4 24.6 %collective-permute-start.27 = (bf16[144,1024]{1,0:T(8,128)(2,1)S(1)}, bf16[144,1024]{1,0:T(8,128)(2,1)S(1)}, u32[]{:S(2)}, u32[]{:S(2)}) collective-permute-start(bf16[144,1024]{1,0:T(8,128)(2,1)S(1)} %shard_map.137), channel_id=1, source_target_pairs={{0,12},{2,14},{4,0},{6,2},{8,4},{10,6},{12,8},{14,10},{1,13},{3,15... | collective-permute-start | bytes 884744 | tf_op jit(solution)/shard_map/ppermute | solution.py:233
  201.1 1.4 collective-permute-start.32

commit v6 on v5

--- a/solution.py
+++ b/solution.py
@@ -50,7 +50,7 @@
 
 
 def row_chunks(count):
-    pieces = -(-count // 256)
+    pieces = -(-count // 512)
     if count % (16 * pieces):
         pieces = 1
     return pieces, count // pieces
@@ -180,24 +180,33 @@
         scaled, down_w = refs[:2]
         dense, messages = refs[2], refs[3:]
 
-        def product(at):
-            return dot(scaled[at, :], down_w[:, mine], ROWS)
+        def product(first, size):
+            return dot(scaled[first:first + size, :], down_w[:, mine], ROWS)
     else:
         grad_gate, grad_up, gate_w, up_w, tails = refs[:5]
         dense, messages = refs[5], refs[6:]
 
-        def product(at):
+        def product(first, size):
+            at = slice(first, first + size)
             return dot(grad_gate[at, :], gate_w[mine, :], LAST) + dot(grad_up[at, :], up_w[mine, :], LAST)
 
-    for k in range(lines):
-        at = slice(lines * tokens + k * padded, lines * tokens + (k + 1) * padded)
-        messages[k][:padded, :] = (product(at) + came[at, :].astype(F32)).astype(BF)
-        if not forward:
-            messages[k][padded:, :] = jnp.zeros((TAIL, width), BF)
-            messages[k][padded:, :tokens] = tails[k].astype(BF)
-    for k in range(lines):
-        at = slice(k * tokens, (k + 1) * tokens)
-        dense[k] = product(at) + came[at, :].astype(F32)
+    def joined(first, size):
+        return product(first, size) + came[first:first + size, :].astype(F32)
+
+    start = lines * tokens
+    for first in range(0, lines, 4):
+        count = min(4, lines - first)
+        total = joined(start + first * padded, count * padded).astype(BF)
+        for k in range(first, first + count):
+            messages[k][:padded, :] = total[(k - first) * padded:(k - first + 1) * padded]
+            if not forward:
+                messages[k][padded:, :] = jnp.zeros((TAIL, width), BF)
+                messages[k][padded:, :tokens] = tails[k].astype(BF)
+    for first in range(0, lines, 4):
+        count = min(4, lines - first)
+        total = joined(first * tokens, count * tokens)
+        for k in range(first, first + count):
+            dense[k] = total[(k - first) * tokens:(k - first + 1) * tokens]
 
 
 def home_kernel(k, tokens, padded, tailed, info, dense, back, place, *refs):
@@ -261,7 +270,7 @@
     blocks = {0: first}
     for k in by_reach:
         blocks[k] = over_line(first, k)
-    compact, places, own_parts = {}, {}, {}
+    compact, places, own_parts, early = {}, {}, {}, []
     for k in [0] + by_reach:
         packed, places[k], own_parts[k] = local_call(
             functools.partial(token_pack_kernel, token_count, part_rows, capacity, padded),
@@ -270,34 +279,47 @@
             (info, blocks[k]),
             (pltpu.VMEM((tail, half_width), F32), pltpu.VMEM((TAIL, token_count), F32)),
         )
+        if k != by_reach[-1]:
+            early.append(packed)
         compact[k] = over_pair(packed)
 
-    held_grad, blocks = settle((grad_out, blocks))
+    held_grad, blocks, early, compact[0] = settle((grad_out, blocks, early, compact[0]))
     grad_blocks = {0: held_grad}
     for k in by_reach:
         grad_blocks[k] = over_line(held_grad, k)
 
+    grad_packed = {
+        k: local_call(
+            grad_pack_kernel, (shape_of((padded, half_width)),), (info, grad_blocks[k], places[k]))[0]
+        for k in [0] + by_reach
+    }
+    grad_compact = {k: over_pair(grad_packed[k]) for k in [0] + by_reach}
+    ahead = {k: grad_compact[k] for k in [0] + by_reach[:1]}
+    compact, grad_blocks, grad_packed, ahead = settle((compact, grad_blocks, grad_packed, ahead))
+    grad_compact.update(ahead)
     rows, weights = local_call(
         functools.partial(token_rows_kernel, *sizes),
         (half_rows, shape_of((row_count, 1), F32)),
         (info, *[blocks[k] for k in every], *[compact[k] for k in every], *[own_parts[k] for k in every]))
     rows_other = over_core(rows)
+    ahead = {k: grad_compact[k] for k in by_reach[1:-1]}
+    rows_other, ahead = settle((rows_other, ahead))
+    grad_compact.update(ahead)
     gate, upward, scaled, sent = local_call(
         functools.partial(forward_kernel, pieces, chunk),
         (shape_of(hidden_rows, F32), shape_of(hidden_rows, F32), shape_of(hidden_rows), half_rows),
         (info, rows, rows_other, weights, gate_local, up_local, down_local))
+    sent, grad_compact = settle((sent, grad_compact))
     out_dense, *out_packed = local_call(
         functools.partial(join_kernel, *sizes, True),
         (shape_of((lines, token_count, half_width), F32),
          *[shape_of((padded, half_width)) for _ in every]),
         (info, over_core(sent), scaled, down_local))
 
-    grad_compact = {}
-    for k in [0] + by_reach:
-        (packed,) = local_call(
-            grad_pack_kernel, (shape_of((padded, half_width)),), (info, grad_blocks[k], places[k]))
-        grad_compact[k] = over_pair(packed)
-    out_back = {k: over_pair(out_packed[k]) for k in every}
+    outward = by_reach[::-1]
+    out_back = {k: over_pair(out_packed[k]) for k in by_reach}
+    last, _ = settle((out_packed[0], out_back[by_reach[0]]))
+    out_back[0] = over_pair(last)
     (grad_rows,) = local_call(
         functools.partial(grad_rows_kernel, *sizes), (half_rows,),
         (info, *[grad_blocks[k] for k in every], *[grad_compact[k] for k in every]))
@@ -309,37 +331,43 @@
          shape_of((lines, TAIL, token_count), F32), shape_of((lines, TAIL, token_count), F32)),
         (info, grad_rows, grad_other, weights, gate, upward, gate_local, up_local, down_local),
         (pltpu.VMEM((row_count, 1), F32),))
-    sent, out_back = settle((sent, out_back))
-    out_home = {}
-    for k in by_reach[::-1] + [0]:
-        (block,) = local_call(
-            functools.partial(home_kernel, k, token_count, padded, False),
-            (shape_of((token_count, half_width)),), (info, out_dense, out_back[k], places[k]))
-        out_home[k] = over_line(block, lines - k) if k else block
+
+    def to_home(k, dense, back, *tails):
+        extra = TAIL if tails else 0
+        return local_call(
+            functools.partial(home_kernel, k, token_count, padded, bool(tails)),
+            (shape_of((token_count + extra, half_width)),), (info, dense, back[k], places[k], *tails))[0]
+
+    def summed(blocks):
+        total = blocks[0][:token_count].astype(F32)
+        for k in range(1, lines):
+            total = total + blocks[k][:token_count].astype(F32)
+        return total.astype(BF)
+
+    sent, some = settle((sent, {k: out_back[k] for k in by_reach}))
+    out_back.update(some)
+    out_home = {k: to_home(k, out_dense, out_back) for k in by_reach + [0]}
+    out_came = {k: over_line(out_home[k], lines - k) for k in by_reach}
+    out_came[0] = out_home[0]
     in_dense, *in_packed = local_call(
         functools.partial(join_kernel, *sizes, False),
         (shape_of((lines, token_count, half_width), F32),
          *[shape_of((padded + TAIL, half_width)) for _ in every]),
         (info, over_core(sent), grad_gate, grad_up, gate_local, up_local, compact_tails))
-    in_packed, rows, rows_other, grad_rows, grad_other, scaled, grad_gate, grad_up = settle(
-        (in_packed, rows, rows_other, grad_rows, grad_other, scaled, grad_gate, grad_up))
-    in_back = {k: over_pair(in_packed[k]) for k in every}
-
-    def summed(blocks):
-        total = blocks[0][:token_count].astype(F32)
-        for k in range(1, lines):
-            total = total + blocks[k][:token_count].astype(F32)
-        return total.astype(BF)
-
-    layer_out = summed(out_home)
-    in_back = {k: settle((in_back[k], layer_out))[0] for k in every}
-    in_home = {}
-    for k in by_reach[::-1] + [0]:
-        (block,) = local_call(
-            functools.partial(home_kernel, k, token_count, padded, True),
-            (shape_of((token_count + TAIL, half_width)),),
-            (info, in_dense, in_back[k], places[k], dense_tails))
-        in_home[k] = over_line(block, lines - k) if k else block
+    in_packed, early = settle((in_packed, {k: out_came[k] for k in by_reach[:-1]}))
+    out_came.update(early)
+    in_back, in_home, sequence = {}, {}, outward + [0]
+    for i, k in enumerate(sequence):
+        packed = in_packed[k]
+        if i >= 2:
+            packed, in_home[sequence[i - 2]] = settle((packed, in_home[sequence[i - 2]]))
+        in_back[k] = over_pair(packed)
+        in_home[k] = to_home(k, in_dense, in_back, dense_tails)
+    in_home[outward[-1]], out_came = settle((in_home[outward[-1]], out_came))
+    layer_out = summed(out_came)
+    last_home, rows, rows_other, grad_rows, grad_other, scaled, grad_gate, grad_up = settle(
+        ([in_home[k] for k in outward], rows, rows_other, grad_rows, grad_other, scaled, grad_gate, grad_up))
+    in_home = {k: over_line(in_home[k], lines - k) if k else in_home[0] for k in every}
     input_grad = summed(in_home)
 
     def whole(own, other):

time: 204 us -> 177 us (0.87)
  starting transfers between devices: 40.5 us -> 30.1 us
  Pallas kernels: 39.7 us -> 32.1 us
  waiting for transfers between devices: 101 us -> 95.5 us
  local copies, waits for them, and re-layouts: 4.71 us -> 2.34 us
    ppermute x12, waiting for transfers between devices: 71.6 us -> 59.4 us  [over_line(): lax.ppermute(x, 'expert', [(i, (i // 2 + k) % lines * 2 + i % 2) for i in...]
    ppermute x12, starting transfers between devices: 18.7 us -> 10.8 us  [over_line(): lax.ppermute(x, 'expert', [(i, (i // 2 + k) % lines * 2 + i % 2) for i in...]
    pallas_call x22, Pallas kernels: 39.7 us -> 32.1 us  [local_call(): pl.pallas_call(kernel, out_shape=tuple(outs), in_specs=[SMEM_SPEC] + [VME...]
    ppermute x16, waiting for transfers between devices: 25.7 us -> 32.4 us  [over_pair(): lax.ppermute(x, 'expert', [(i, i + 1 - 2 * (i % 2)) for i in range(expert...]
    unnamed x61 -> x55, local copies, waits for them, and re-layouts: 4.7 us -> 2.33 us
    ppermute x16, starting transfers between devices: 16.4 us -> 14 us  [over_pair(): lax.ppermute(x, 'expert', [(i, i + 1 - 2 * (i % 2)) for i in range(expert...]
  transfers between devices with their start and end apart: 33 -> 33, of which waited for: 19 -> 19; matrix products, arithmetic and copies ran while one was open for 7% -> 7% of each run, Pallas kernels for 12% -> 17%
where the time goes in v6:
time: 177 us
  waiting for transfers between devices  95.5 us (54%)
  Pallas kernels  32.1 us (18%)
  starting transfers between devices  30.1 us (17%)
  matrix products  9.82 us (6%)
  other arithmetic  5.77 us (3%)
  local copies, waits for them, and re-layouts  2.34 us (1%)
    ppermute x12, waiting for transfers between devices, over_line(): lax.ppermute(x, 'expert', [(i, (i // 2 + k) % lines * 2 + i % 2) for i in...  59.4 us
    ppermute x16, waiting for transfers between devices, over_pair(): lax.ppermute(x, 'expert', [(i, i + 1 - 2 * (i % 2)) for i in range(expert...  32.4 us
    pallas_call x22, Pallas kernels, local_call(): pl.pallas_call(kernel, out_shape=tuple(outs), in_specs=[SMEM_SPEC] + [VME...  32.1 us
    ppermute x16, starting transfers between devices, over_pair(): lax.ppermute(x, 'expert', [(i, i + 1 - 2 * (i % 2)) for i in range(expert...  14 us
    ppermute x12, starting transfers between devices, over_line(): lax.ppermute(x, 'expert', [(i, (i // 2 + k) % lines * 2 + i % 2) for i in...  10.8 us
    dot_general x3, matrix products, dot(): lax.dot_general(a, b, (contract, ((), ())), preferred_element_type=F32)  9.82 us
    ppermute x5, starting transfers between devices, over_core(): return lax.ppermute(x, 'tensor', [(0, 1), (1, 0)])  5.29 us
    ppermute x5, waiting for transfers between devices, over_core(): return lax.ppermute(x, 'tensor', [(0, 1), (1, 0)])  3.69 us
  transfers between devices with their start and end apart: 33, of which 19 were waited for; matrix products, arithmetic and copies ran while one was open for 7% of the time, Pallas kernels for 17%

profile of v6, /device:TPU:9, one launch (start us, length us, event | category | flops | bytes accessed | tf_op | source)
XLA Modules:
  0.0 176.8 jit_solution(667823718676811832)
XLA Ops:
  0.6 0.8 select_reduce_fusion.1
  1.5 1.0 pad_maximum_fusion.3.block.refs_0_
  2.4 1.3 collective-permute-start
  3.8 1.1 collective-permute-start.1
  4.9 1.4 collective-permute-start.2
  6.3 0.9 shard_map.118
  7.2 1.3 collective-permute-start.3
  8.5 1.8 %collective-permute-done.block.refs_1_ = bf16[144,1024]{1,0:T(8,128)(2,1)S(1)} collective-permute-done((bf16[144,1024]{1,0:T(8,128)(2,1)S(1)}, bf16[144,1024]{1,0:T(8,128)(2,1)S(1)}, u32[]{:S(2)}, u32[]{:S(2)}) %collective-permute-start) | collective-permute-done | bytes 294944 | tf_op jit(solution)/shard_map/ppermute | solution.py:242
  10.4 0.9 shard_map.119
  11.3 20.0 %collective-permute-done.2.block.refs_3_ = bf16[144,1024]{1,0:T(8,128)(2,1)S(1)} collective-permute-done((bf16[144,1024]{1,0:T(8,128)(2,1)S(1)}, bf16[144,1024]{1,0:T(8,128)(2,1)S(1)}, u32[]{:S(2)}, u32[]{:S(2)}) %collective-permute-start.2) | collective-permute-done | bytes 294944 | tf_op jit(solution)/shard_map/ppermute | solution.py:242
  31.3 0.9 shard_map.120
  32.3 1.4 collective-permute-start.9
  33.7 1.2 collective-permute-start.4
  34.9 0.9 shard_map.121
  36.1 3.7 %collective-permute-done.7.block.refs_1_ = bf16[128,1024]{1,0:T(8,128)(2,1)S(1)} collective-permute-done((bf16[128,1024]{1,0:T(8,128)(2,1)}, bf16[128,1024]{1,0:T(8,128)(2,1)S(1)}, u32[]{:S(2)}, u32[]{:S(2)}) %collective-permute-start.7) | collective-permute-done | bytes 262176 | tf_op jit(solution)/shard_map/ppermute | solution.py:242
  39.8 1.2 collective-permute-start.6
  41.8 13.1 %collective-permute-done.8.block.refs_2_ = bf16[128,1024]{1,0:T(8,128)(2,1)S(1)} collective-permute-done((bf16[128,1024]{1,0:T(8,128)(2,1)}, bf16[128,1024]{1,0:T(8,128)(2,1)S(1)}, u32[]{:S(2)}, u32[]{:S(2)}) %collective-permute-start.8) | collective-permute-done | bytes 262176 | tf_op jit(solution)/shard_map/ppermute | solution.py:242
  54.9 1.2 collective-permute-start.10
  57.2 0.7 shard_map.124
  57.9 0.7 shard_map.125
  58.7 1.6 collective-permute-done.10.refs_4_
  60.3 4.2 %collective-permute-done.11.refs_5_ = bf16[96,1024]{1,0:T(8,128)(2,1)S(1)} collective-permute-done((bf16[96,1024]{1,0:T(8,128)(2,1)S(1)}, bf16[96,1024]{1,0:T(8,128)(2,1)S(1)}, u32[]{:S(2)}, u32[]{:S(2)}) %collective-permute-start.11) | collective-permute-done | bytes 196640 | tf_op jit(solution)/shard_map/ppermute | solution.py:239
  64.5 0.8 shard_map.126
  65.3 2.0 %collective-permute-start.12 = (bf16[896,1024]{1,0:T(8,128)(2,1)S(1)}, bf16[896,1024]{1,0:T(8,128)(2,1)S(1)}, u32[]{:S(2)}, u32[]{:S(2)}) collective-permute-start(bf16[896,1024]{1,0:T(8,128)(2,1)S(1)} %get-tuple-element.167.own), channel_id=1, source_target_pairs={{0,1},{1,0},{2,3},{3,2},{4,5},{5,4},{6,7},{7,6},{8,9},{9,8},{10,11... | collective-permute-start | bytes 5505032 | tf_op jit(solution)/shard_map/ppermute | solution.py:248
  67.3 1.3 collective-permute-start.13
  68.8 5.0 %collective-permute-done.13.refs_7_ = bf16[96,1024]{1,0:T(8,128)(2,1)S(1)} collective-permute-done((bf16[96,1024]{1,0:T(8,128)(2,1)S(1)}, bf16[96,1024]{1,0:T(8,128)(2,1)S(1)}, u32[]{:S(2)}, u32[]{:S(2)}) %collective-permute-start.13) | collective-permute-done | bytes 196640 | tf_op jit(solution)/shard_map/ppermute | solution.py:239
  73.8 5.7 %shard_map.127 = (f32[896,384]{1,0:T(8,128)S(1)}, f32[896,384]{1,0:T(8,128)S(1)}, bf16[896,384]{1,0:T(8,128)(2,1)S(1)}, bf16[896,1024]{1,0:T(8,128)(2,1)S(1)}) custom-call(s32[3]{0:T(128)S(1)} %pad_add_fusion.info, bf16[896,1024]{1,0:T(8,128)(2,1)S(1)} %get-tuple-element.167.own, bf16[896,1024]{1,0:T(8,128)(2,1)S(1)} %collective-permute-done.12.other, ...), custom_call_target="tpu_custom_call" | custom-call | flops 1000 | bytes 1000 | tf_op jit(solution)/shard_map/pallas_call | solution.py:41
  79.5 1.4 collective-permute-start.15
  81.5 2.7 %collective-permute-done.15.came = bf16[896,1024]{1,0:T(8,128)(2,1)S(1)} collective-permute-done((bf16[896,1024]{1,0:T(8,128)(2,1)S(1)}, bf16[896,1024]{1,0:T(8,128)(2,1)S(1)}, u32[]{:S(2)}, u32[]{:S(2)}) %collective-permute-start.15) | collective-permute-done | bytes 1835040 | tf_op jit(solution)/shard_map/ppermute | solution.py:248
  84.3 1.7 shard_map.129
  87.0 1.2 collective-permute-start.17
  88.5 1.2 collective-permute-start.19
  90.4 5.4 %shard_map.130 = (bf16[896,384]{1,0:T(8,128)(2,1)S(1)}, bf16[896,384]{1,0:T(8,128)(2,1)S(1)}, bf16[896,1024]{1,0:T(8,128)(2,1)S(1)}, f32[4,16,128]{2,1,0:T(8,128)S(1)}, f32[4,16,128]{2,1,0:T(8,128)S(1)}) custom-call(s32[3]{0:T(128)S(1)} %pad_add_fusion.info, bf16[896,1024]{1,0:T(8,128)(2,1)S(1)} %shard_map.128.own, ...), custom_call_target="tpu_custom_call" | custom-call | flops 1000 | bytes 1000 | tf_op jit(solution)/shard_map/pallas_call | solution.py:41
  95.9 1.7 collective-permute-done.18.back
  97.6 4.2 %collective-permute-done.19.back = bf16[96,1024]{1,0:T(8,128)(2,1)S(1)} collective-permute-done((bf16[96,1024]{1,0:T(8,128)(2,1)S(1)}, bf16[96,1024]{1,0:T(8,128)(2,1)S(1)}, u32[]{:S(2)}, u32[]{:S(2)}) %collective-permute-start.19) | collective-permute-done | bytes 196640 | tf_op jit(solution)/shard_map/ppermute | solution.py:239
  101.8 1.0 collective-permute-start.20
  102.8 0.8 shard_map.132
  103.6 0.8 shard_map.133
  104.4 1.5 collective-permute-start.22
  106.2 3.4 %shard_map.131 = (f32[4,128,1024]{2,1,0:T(8,128)S(1)}, bf16[112,1024]{1,0:T(8,128)(2,1)}, bf16[112,1024]{1,0:T(8,128)(2,1)}, bf16[112,1024]{1,0:T(8,128)(2,1)S(1)}, bf16[112,1024]{1,0:T(8,128)(2,1)S(1)}) custom-call(s32[3]{0:T(128)S(1)} %pad_add_fusion.info, bf16[896,1024]{1,0:T(8,128)(2,1)S(1)} %collective-permute-done.20.came, ...), custom_call_target="tpu_custom_call" | custom-call | flops 1000 | bytes 1000 | tf_op jit(solution)/shard_map/pallas_call | solution.py:41
  109.5 2.0 %collective-permute-done.21 = bf16[128,1024]{1,0:T(8,128)(2,1)S(1)} collective-permute-done((bf16[128,1024]{1,0:T(8,128)(2,1)S(1)}, bf16[128,1024]{1,0:T(8,128)(2,1)S(1)}, u32[]{:S(2)}, u32[]{:S(2)}) %collective-permute-start.21) | collective-permute-done | bytes 262176 | tf_op jit(solution)/shard_map/ppermute | solution.py:242
  111.6 8.4 %collective-permute-done.22 = bf16[128,1024]{1,0:T(8,128)(2,1)S(1)} collective-permute-done((bf16[128,1024]{1,0:T(8,128)(2,1)S(1)}, bf16[128,1024]{1,0:T(8,128)(2,1)S(1)}, u32[]{:S(2)}, u32[]{:S(2)}) %collective-permute-start.22) | collective-permute-done | bytes 262176 | tf_op jit(solution)/shard_map/ppermute | solution.py:242
  119.9 1.2 collective-permute-start.23
  121.4 1.5 shard_map.137
  122.9 1.1 collective-permute-start.26
  124.0 2.3 %collective-permute-done.23.back = bf16[112,1024]{1,0:T(8,128)(2,1)S(1)} collective-permute-done((bf16[112,1024]{1,0:T(8,128)(2,1)S(1)}, bf16[112,1024]{1,0:T(8,128)(2,1)S(1)}, u32[]{:S(2)}, u32[]{:S(2)}) %collective-permute-start.23) | collective-permute-done | bytes 229408 | tf_op jit(solution)/shard_map/ppermute | solution.py:239
  126.3 0.8 shard_map.134
  127.1 1.3 collective-permute-start.24
  128.4 2.9 %collective-permute-done.27.back = bf16[112,1024]{1,0:T(8,128)(2,1)S(1)} collective-permute-done((bf16[112,1024]{1,0:T(8,128)(2,1)S(1)}, bf16[112,1024]{1,0:T(8,128)(2,1)S(1)}, u32[]{:S(2)}, u32[]{:S(2)}) %collective-permute-start.27) | collective-permute-done | bytes 229408 | tf_op jit(solution)/shard_map/ppermute | solution.py:239
  131.3 0.8 shard_map.138
  132.8 1.2 collective-permute-start.28
  134.3 10.5 %collective-permute-done.25.back = bf16[96,1024]{1,0:T(8,128)(2,1)S(1)} collective-permute-done((bf16[96,1024]{1,0:T(8,128)(2,1)}, bf16[96,1024]{1,0:T(8,128)(2,1)S(1)}, u32[]{:S(2)}, u32[]{:S(2)}) %collective-permute-start.25) | collective-permute-done | bytes 196640 | tf_op jit(solution)/shard_map/ppermute | solution.py:239
  144.8 0.8 shard_map.136
  145.7 2.4 %collective-permute-start.30 = (bf16[144,1024]{1,0:T(8,128)(2,1)S(1)}, bf16[144,1024]{1,0:T(8,128)(2,1)S(1)}, u32[]{:S(2)}, u32[]{:S(2)}) collective-permute-start(bf16[144,1024]{1,0:T(8,128)(2,1)S(1)} %copy-done.17), channel_id=1, source_target_pairs={{0,8},{2,10},{4,12},{6,14},{8,0},{10,2},{12,4},{14,6},{1,9},{3,11}... | collective-permute-start | bytes 884744 | tf_op jit(solution)/shard_map/ppermute | solution.py:242
  148.1 1.3 shard_map.135
  149.8 1.4 shard_map.139
  151.5 3.4 %fusion.7 = bf16[1,2048,384]{2,1,0:T(8,128)(2,1)} fusion(bf16[896,384]{1,0:T(8,128)(2,1)S(1)} %get-tuple-element.169.refs_0_, bf16[896,1024]{1,0:T(8,128)(2,1)S(1)} %get-tuple-element.185, bf16[896,1024]{1,0:T(8,128)(2,1)S(1)} %get-tuple-element.184), kind=kOutput, calls=%fused_computation.8 | convolution fusion | flops 1417412608 | bytes 5931008 | tf_op jit(solution)/shard_map/dot_general | solution.py:24
  154.9 3.4 %fusion.8 = bf16[1,2048,384]{2,1,0:T(8,128)(2,1)} fusion(bf16[896,384]{1,0:T(8,128)(2,1)S(1)} %get-tuple-element.170.refs_1_, bf16[896,1024]{1,0:T(8,128)(2,1)S(1)} %get-tuple-element.185, bf16[896,1024]{1,0:T(8,128)(2,1)S(1)} %get-tuple-element.184), kind=kOutput, calls=%fused_computation.9 | convolution fusion | flops 1417412608 | bytes 5931008 | tf_op jit(solution)/shard_map/dot_general | solution.py:24
  158.6 0.9 copy-done.15
  159.5 3.0 %fusion.9 = bf16[1,384,2048]{2,1,0:T(8,128)(2,1)} fusion(bf16[896,384]{1,0:T(8,128)(2,1)S(1)} %copy-done.15, bf16[896,1024]{1,0:T(8,128)(2,1)S(1)} %get-tuple-element.183, bf16[896,1024]{1,0:T(8,128)(2,1)S(1)} %get-tuple-element.182), kind=kOutput, calls=%fused_computation.10 | convolution fusion | flops 1417412608 | bytes 5931008 | tf_op jit(solution)/shard_map/dot_general | solution.py:24
  162.4 1.8 %add_convert_fusion.1 = bf16[128,1024]{1,0:T(8,128)(2,1)} fusion(bf16[128,1024]{1,0:T(8,128)(2,1)S(1)} %copy-done.25, bf16[128,1024]{1,0:T(8,128)(2,1)} %collective-permute-done.26, bf16[128,1024]{1,0:T(8,128)(2,1)S(1)} %copy-done.23, bf16[128,1024]{1,0:T(8,128)(2,1)S(1)} %shard_map.136), kind=kLoop, calls=%fused_computation.16 | loop fusion | flops 1048576 | bytes 1310720 | tf_op jit(solution)/shard_map/convert_element_type | solution.py:345
  164.3 5.0 %collective-permute-done.30 = bf16[144,1024]{1,0:T(8,128)(2,1)S(1)} collective-permute-done((bf16[144,1024]{1,0:T(8,128)(2,1)S(1)}, bf16[144,1024]{1,0:T(8,128)(2,1)S(1)}, u32[]{:S(2)}, u32[]{:S(2)}) %collective-permute-start.30) | collective-permute-done | bytes 294944 | tf_op jit(solution)/shard_map/ppermute | solution.py:242
  169.3 5.4 %collective-permute-done.29 = bf16[144,1024]{1,0:T(8,128)(2,1)S(1)} collective-permute-done((bf16[144,1024]{1,0:T(8,128)(2,1)S(1)}, bf16[144,1024]{1,0:T(8,128)(2,1)S(1)}, u32[]{:S(2)}, u32[]{:S(2)}) %collective-permute-start.29) | collective-permute-done | bytes 294944 | tf_op jit(solution)/shard_map/ppermute | solution.py:242
  175.4 0.9 add_convert_fusion
  (108 shorter events, 9.0 us)
Async XLA Ops:
  0.6 40.4 %copy-start.13 = (bf16[128,1024]{1,0:T(8,128)(2,1)S(1)}, bf16[128,1024]{1,0:T(8,128)(2,1)}, u32[]{:S(2)}) copy-start(bf16[128,1024]{1,0:T(8,128)(2,1)} %refs_0_) | copy-start | bytes 786436
  2.4 7.9 %collective-permute-start = (bf16[144,1024]{1,0:T(8,128)(2,1)S(1)}, bf16[144,1024]{1,0:T(8,128)(2,1)S(1)}, u32[]{:S(2)}, u32[]{:S(2)}) collective-permute-start(bf16[144,1024]{1,0:T(8,128)(2,1)S(1)} %pad_maximum_fusion.3.block.refs_0_), channel_id=1, source_target_pairs={{0,4},{2,6},{4,8},{6,10},{8,12},{10,14},{12,0},{14,2},{1,5},{3,7},... | collective-permute-start | bytes 884744 | tf_op jit(solution)/shard_map/ppermute | solution.py:242
  3.8 28.4 %collective-permute-start.1 = (bf16[144,1024]{1,0:T(8,128)(2,1)S(1)}, bf16[144,1024]{1,0:T(8,128)(2,1)S(1)}, u32[]{:S(2)}, u32[]{:S(2)}) collective-permute-start(bf16[144,1024]{1,0:T(8,128)(2,1)S(1)} %pad_maximum_fusion.3.block.refs_0_), channel_id=1, source_target_pairs={{0,8},{2,10},{4,12},{6,14},{8,0},{10,2},{12,4},{14,6},{1,9},{3,11}... | collective-permute-start | bytes 884744 | tf_op jit(solution)/shard_map/ppermute | solution.py:242
  4.9 26.4 %collective-permute-start.2 = (bf16[144,1024]{1,0:T(8,128)(2,1)S(1)}, bf16[144,1024]{1,0:T(8,128)(2,1)S(1)}, u32[]{:S(2)}, u32[]{:S(2)}) collective-permute-start(bf16[144,1024]{1,0:T(8,128)(2,1)S(1)} %pad_maximum_fusion.3.block.refs_0_), channel_id=1, source_target_pairs={{0,12},{2,14},{4,0},{6,2},{8,4},{10,6},{12,8},{14,10},{1,13},{3,15... | collective-permute-start | bytes 884744 | tf_op jit(solution)/shard_map/ppermute | solution.py:242
  7.2 24.9 %collective-permute-start.3 = (bf16[112,1024]{1,0:T(8,128)(2,1)S(1)}, bf16[112,1024]{1,0:T(8,128)(2,1)S(1)}, u32[]{:S(2)}, u32[]{:S(2)}) collective-permute-start(bf16[112,1024]{1,0:T(8,128)(2,1)S(1)} %get-tuple-element.90), channel_id=1, source_target_pairs={{0,2},{2,0},{4,6},{6,4},{8,10},{10,8},{12,14},{14,12},{1,3},{3,1},... | collective-permute-start | bytes 688136 | tf_op jit(solution)/shard_map/ppermute | solution.py:239
  10.4 63.4 %copy-start.6 = (bf16[1,2048,384]{2,1,0:T(8,128)(2,1)S(1)}, bf16[1,2048,384]{2,1,0:T(8,128)(2,1)}, u32[]{:S(2)}) copy-start(bf16[1,2048,384]{2,1,0:T(8,128)(2,1)} %param.11) | copy-start | bytes 4718596
  11.3 91.5 %copy-start.19 = (bf16[96,128]{1,0:T(8,128)(2,1)}, bf16[96,128]{1,0:T(8,128)(2,1)S(1)}, u32[]{:S(2)}) copy-start(bf16[96,128]{1,0:T(8,128)(2,1)S(1)} %get-tuple-element.97.place) | copy-start | bytes 73732
  32.2 7.6 %collective-permute-start.7 = (bf16[128,1024]{1,0:T(8,128)(2,1)}, bf16[128,1024]{1,0:T(8,128)(2,1)S(1)}, u32[]{:S(2)}, u32[]{:S(2)}) collective-permute-start(bf16[128,1024]{1,0:T(8,128)(2,1)} %refs_0_), channel_id=1, source_target_pairs={{0,4},{2,6},{4,8},{6,10},{8,12},{10,14},{12,0},{14,2},{1,5},{3,7},... | collective-permute-start | bytes 786440 | tf_op jit(solution)/shard_map/ppermute | solution.py:242
  32.2 22.7 %collective-permute-start.8 = (bf16[128,1024]{1,0:T(8,128)(2,1)}, bf16[128,1024]{1,0:T(8,128)(2,1)S(1)}, u32[]{:S(2)}, u32[]{:S(2)}) collective-permute-start(bf16[128,1024]{1,0:T(8,128)(2,1)} %refs_0_), channel_id=1, source_target_pairs={{0,8},{2,10},{4,12},{6,14},{8,0},{10,2},{12,4},{14,6},{1,9},{3,11}... | collective-permute-start | bytes 786440 | tf_op jit(solution)/shard_map/ppermute | solution.py:242
  32.3 24.6 %collective-permute-start.9 = (bf16[128,1024]{1,0:T(8,128)(2,1)}, bf16[128,1024]{1,0:T(8,128)(2,1)S(1)}, u32[]{:S(2)}, u32[]{:S(2)}) collective-permute-start(bf16[128,1024]{1,0:T(8,128)(2,1)} %refs_0_), channel_id=1, source_target_pairs={{0,12},{2,14},{4,0},{6,2},{8,4},{10,6},{12,8},{14,10},{1,13},{3,15... | collective-permute-start | bytes 786440 | tf_op jit(solution)/shard_map/ppermute | solution.py:242
  33.7 26.6 %collective-permute-start.4 = (bf16[112,1024]{1,0:T(8,128)(2,1)S(1)}, bf16[112,1024]{1,0:T(8,128)(2,1)S(1)}, u32[]{:S(2)}, u32[]{:S(2)}) collective-permute-start(bf16[112,1024]{1,0:T(8,128)(2,1)S(1)} %get-tuple-element.91), channel_id=1, source_target_pairs={{0,2},{2,0},{4,6},{6,4},{8,10},{10,8},{12,14},{14,12},{1,3},{3,1},... | collective-permute-start | bytes 688136 | tf_op jit(solution)/shard_map/ppermute | solution.py:239
  35.8 24.5 %collective-permute-start.5 = (bf16[112,1024]{1,0:T(8,128)(2,1)S(1)}, bf16[112,1024]{1,0:T(8,128)(2,1)S(1)}, u32[]{:S(2)}, u32[]{:S(2)}) collective-permute-start(bf16[112,1024]{1,0:T(8,128)(2,1)S(1)} %get-tuple-element.94), channel_id=1, source_target_pairs={{0,2},{2,0},{4,6},{6,4},{8,10},{10,8},{12,14},{14,12},{1,3},{3,1},... | collective-permute-start | bytes 688136 | tf_op jit(solution)/shard_map/ppermute | solution.py:239
  39.8 20.5 %collective-permute-start.6 = (bf16[112,1024]{1,0:T(8,128)(2,1)S(1)}, bf16[112,1024]{1,0:T(8,128)(2,1)S(1)}, u32[]{:S(2)}, u32[]{:S(2)}) collective-permute-start(bf16[112,1024]{1,0:T(8,128)(2,1)S(1)} %get-tuple-element.92), channel_id=1, source_target_pairs={{0,2},{2,0},{4,6},{6,4},{8,10},{10,8},{12,14},{14,12},{1,3},{3,1},... | collective-permute-start | bytes 688136 | tf_op jit(solution)/shard_map/ppermute | solution.py:239
  41.8 32.0 %copy-start.4 = (bf16[1,384,2048]{2,1,0:T(8,128)(2,1)S(1)}, bf16[1,384,2048]{2,1,0:T(8,128)(2,1)}, u32[]{:S(2)}) copy-start(bf16[1,384,2048]{2,1,0:T(8,128)(2,1)} %param.12) | copy-start | bytes 4718596
  41.8 32.0 %copy-start.5 = (bf16[1,2048,384]{2,1,0:T(8,128)(2,1)S(1)}, bf16[1,2048,384]{2,1,0:T(8,128)(2,1)}, u32[]{:S(2)}) copy-start(bf16[1,2048,384]{2,1,0:T(8,128)(2,1)} %param.10) | copy-start | bytes 4718596
  54.9 5.4 %collective-permute-start.10 = (bf16[96,1024]{1,0:T(8,128)(2,1)S(1)}, bf16[96,1024]{1,0:T(8,128)(2,1)S(1)}, u32[]{:S(2)}, u32[]{:S(2)}) collective-permute-start(bf16[96,1024]{1,0:T(8,128)(2,1)S(1)} %shard_map.122), channel_id=1, source_target_pairs={{0,2},{2,0},{4,6},{6,4},{8,10},{10,8},{12,14},{14,12},{1,3},{3,1},... | collective-permute-start | bytes 589832 | tf_op jit(solution)/shard_map/ppermute | solution.py:239
  56.9 7.6 %collective-permute-start.11 = (bf16[96,1024]{1,0:T(8,128)(2,1)S(1)}, bf16[96,1024]{1,0:T(8,128)(2,1)S(1)}, u32[]{:S(2)}, u32[]{:S(2)}) collective-permute-start(bf16[96,1024]{1,0:T(8,128)(2,1)S(1)} %shard_map.123), channel_id=1, source_target_pairs={{0,2},{2,0},{4,6},{6,4},{8,10},{10,8},{12,14},{14,12},{1,3},{3,1},... | collective-permute-start | bytes 589832 | tf_op jit(solution)/shard_map/ppermute | solution.py:239
  65.3 14.2 %copy-start.7 = (bf16[896,1024]{1,0:T(8,128)(2,1)}, bf16[896,1024]{1,0:T(8,128)(2,1)S(1)}, u32[]{:S(2)}) copy-start(bf16[896,1024]{1,0:T(8,128)(2,1)S(1)} %get-tuple-element.167.own) | copy-start | bytes 5505028
  65.3 8.5 %collective-permute-start.12 = (bf16[896,1024]{1,0:T(8,128)(2,1)S(1)}, bf16[896,1024]{1,0:T(8,128)(2,1)S(1)}, u32[]{:S(2)}, u32[]{:S(2)}) collective-permute-start(bf16[896,1024]{1,0:T(8,128)(2,1)S(1)} %get-tuple-element.167.own), channel_id=1, source_target_pairs={{0,1},{1,0},{2,3},{3,2},{4,5},{5,4},{6,7},{7,6},{8,9},{9,8},{10,11... | collective-permute-start | bytes 5505032 | tf_op jit(solution)/shard_map/ppermute | solution.py:248
  67.3 6.5 %collective-permute-start.13 = (bf16[96,1024]{1,0:T(8,128)(2,1)S(1)}, bf16[96,1024]{1,0:T(8,128)(2,1)S(1)}, u32[]{:S(2)}, u32[]{:S(2)}) collective-permute-start(bf16[96,1024]{1,0:T(8,128)(2,1)S(1)} %shard_map.125), channel_id=1, source_target_pairs={{0,2},{2,0},{4,6},{6,4},{8,10},{10,8},{12,14},{14,12},{1,3},{3,1},... | collective-permute-start | bytes 589832 | tf_op jit(solution)/shard_map/ppermute | solution.py:239
  68.5 11.0 %collective-permute-start.14 = (bf16[96,1024]{1,0:T(8,128)(2,1)S(1)}, bf16[96,1024]{1,0:T(8,128)(2,1)S(1)}, u32[]{:S(2)}, u32[]{:S(2)}) collective-permute-start(bf16[96,1024]{1,0:T(8,128)(2,1)S(1)} %shard_map.124), channel_id=1, source_target_pairs={{0,2},{2,0},{4,6},{6,4},{8,10},{10,8},{12,14},{14,12},{1,3},{3,1},... | collective-permute-start | bytes 589832 | tf_op jit(solution)/shard_map/ppermute | solution.py:239
  73.8 5.7 %copy-start.9 = (bf16[896,1024]{1,0:T(8,128)(2,1)}, bf16[896,1024]{1,0:T(8,128)(2,1)S(1)}, u32[]{:S(2)}) copy-start(bf16[896,1024]{1,0:T(8,128)(2,1)S(1)} %collective-permute-done.12.other) | copy-start | bytes 5505028
  79.5 4.8 %copy-start.14 = (bf16[896,384]{1,0:T(8,128)(2,1)}, bf16[896,384]{1,0:T(8,128)(2,1)S(1)}, u32[]{:S(2)}) copy-start(bf16[896,384]{1,0:T(8,128)(2,1)S(1)} %get-tuple-element.171.refs_0_) | copy-start | bytes 2064388
  79.5 4.8 %collective-permute-start.15 = (bf16[896,1024]{1,0:T(8,128)(2,1)S(1)}, bf16[896,1024]{1,0:T(8,128)(2,1)S(1)}, u32[]{:S(2)}, u32[]{:S(2)}) collective-permute-start(bf16[896,1024]{1,0:T(8,128)(2,1)S(1)} %get-tuple-element.127), channel_id=1, source_target_pairs={{0,1},{1,0},{2,3},{3,2},{4,5},{5,4},{6,7},{7,6},{8,9},{9,8},{10,11... | collective-permute-start | bytes 5505032 | tf_op jit(solution)/shard_map/ppermute | solution.py:248
  81.5 8.9 %copy-start.2 = (bf16[896,1024]{1,0:T(8,128)(2,1)}, bf16[896,1024]{1,0:T(8,128)(2,1)S(1)}, u32[]{:S(2)}) copy-start(bf16[896,1024]{1,0:T(8,128)(2,1)S(1)} %shard_map.128.own) | copy-start | bytes 5505028
  86.0 0.7 copy-start.21
  86.6 3.8 %collective-permute-start.16 = (bf16[896,1024]{1,0:T(8,128)(2,1)S(1)}, bf16[896,1024]{1,0:T(8,128)(2,1)S(1)}, u32[]{:S(2)}, u32[]{:S(2)}) collective-permute-start(bf16[896,1024]{1,0:T(8,128)(2,1)S(1)} %shard_map.128.own), channel_id=1, source_target_pairs={{0,1},{1,0},{2,3},{3,2},{4,5},{5,4},{6,7},{7,6},{8,9},{9,8},{10,11... | collective-permute-start | bytes 5505032 | tf_op jit(solution)/shard_map/ppermute | solution.py:248
  87.0 8.9 %collective-permute-start.17 = (bf16[96,1024]{1,0:T(8,128)(2,1)S(1)}, bf16[96,1024]{1,0:T(8,128)(2,1)S(1)}, u32[]{:S(2)}, u32[]{:S(2)}) collective-permute-start(bf16[96,1024]{1,0:T(8,128)(2,1)S(1)} %get-tuple-element.130), channel_id=1, source_target_pairs={{0,2},{2,0},{4,6},{6,4},{8,10},{10,8},{12,14},{14,12},{1,3},{3,1},... | collective-permute-start | bytes 589832 | tf_op jit(solution)/shard_map/ppermute | solution.py:239
  88.3 9.3 %collective-permute-start.18 = (bf16[96,1024]{1,0:T(8,128)(2,1)S(1)}, bf16[96,1024]{1,0:T(8,128)(2,1)S(1)}, u32[]{:S(2)}, u32[]{:S(2)}) collective-permute-start(bf16[96,1024]{1,0:T(8,128)(2,1)S(1)} %get-tuple-element.131), channel_id=1, source_target_pairs={{0,2},{2,0},{4,6},{6,4},{8,10},{10,8},{12,14},{14,12},{1,3},{3,1},... | collective-permute-start | bytes 589832 | tf_op jit(solution)/shard_map/ppermute | solution.py:239
  88.5 13.3 %collective-permute-start.19 = (bf16[96,1024]{1,0:T(8,128)(2,1)S(1)}, bf16[96,1024]{1,0:T(8,128)(2,1)S(1)}, u32[]{:S(2)}, u32[]{:S(2)}) collective-permute-start(bf16[96,1024]{1,0:T(8,128)(2,1)S(1)} %get-tuple-element.132), channel_id=1, source_target_pairs={{0,2},{2,0},{4,6},{6,4},{8,10},{10,8},{12,14},{14,12},{1,3},{3,1},... | collective-permute-start | bytes 589832 | tf_op jit(solution)/shard_map/ppermute | solution.py:239
  90.4 5.4 %copy-start.11 = (bf16[896,1024]{1,0:T(8,128)(2,1)}, bf16[896,1024]{1,0:T(8,128)(2,1)S(1)}, u32[]{:S(2)}) copy-start(bf16[896,1024]{1,0:T(8,128)(2,1)S(1)} %collective-permute-done.16.other) | copy-start | bytes 5505028
  101.8 4.4 %collective-permute-start.20 = (bf16[896,1024]{1,0:T(8,128)(2,1)S(1)}, bf16[896,1024]{1,0:T(8,128)(2,1)S(1)}, u32[]{:S(2)}, u32[]{:S(2)}) collective-permute-start(bf16[896,1024]{1,0:T(8,128)(2,1)S(1)} %get-tuple-element.137), channel_id=1, source_target_pairs={{0,1},{1,0},{2,3},{3,2},{4,5},{5,4},{6,7},{7,6},{8,9},{9,8},{10,11... | collective-permute-start | bytes 5505032 | tf_op jit(solution)/shard_map/ppermute | solution.py:248
  103.6 8.0 %collective-permute-start.21 = (bf16[128,1024]{1,0:T(8,128)(2,1)S(1)}, bf16[128,1024]{1,0:T(8,128)(2,1)S(1)}, u32[]{:S(2)}, u32[]{:S(2)}) collective-permute-start(bf16[128,1024]{1,0:T(8,128)(2,1)S(1)} %shard_map.132), channel_id=1, source_target_pairs={{0,12},{2,14},{4,0},{6,2},{8,4},{10,6},{12,8},{14,10},{1,13},{3,15... | collective-permute-start | bytes 786440 | tf_op jit(solution)/shard_map/ppermute | solution.py:242
  104.4 15.5 %collective-permute-start.22 = (bf16[128,1024]{1,0:T(8,128)(2,1)S(1)}, bf16[128,1024]{1,0:T(8,128)(2,1)S(1)}, u32[]{:S(2)}, u32[]{:S(2)}) collective-permute-start(bf16[128,1024]{1,0:T(8,128)(2,1)S(1)} %shard_map.133), channel_id=1, source_target_pairs={{0,4},{2,6},{4,8},{6,10},{8,12},{10,14},{12,0},{14,2},{1,5},{3,7},... | collective-permute-start | bytes 786440 | tf_op jit(solution)/shard_map/ppermute | solution.py:242
  109.5 21.7 %copy-start = (f32[4,128,1024]{2,1,0:T(8,128)}, f32[4,128,1024]{2,1,0:T(8,128)S(1)}, u32[]{:S(2)}) copy-start(f32[4,128,1024]{2,1,0:T(8,128)S(1)} %get-tuple-element.141.dense) | copy-start | bytes 6291460
  111.6 15.5 %copy-start.22 = (bf16[128,1024]{1,0:T(8,128)(2,1)}, bf16[128,1024]{1,0:T(8,128)(2,1)S(1)}, u32[]{:S(2)}) copy-start(bf16[128,1024]{1,0:T(8,128)(2,1)S(1)} %collective-permute-done.21) | copy-start | bytes 786436
  119.9 7.2 %copy-start.24 = (bf16[128,1024]{1,0:T(8,128)(2,1)}, bf16[128,1024]{1,0:T(8,128)(2,1)S(1)}, u32[]{:S(2)}) copy-start(bf16[128,1024]{1,0:T(8,128)(2,1)S(1)} %collective-permute-done.22) | copy-start | bytes 786436
  119.9 6.3 %collective-permute-start.23 = (bf16[112,1024]{1,0:T(8,128)(2,1)S(1)}, bf16[112,1024]{1,0:T(8,128)(2,1)S(1)}, u32[]{:S(2)}, u32[]{:S(2)}) collective-permute-start(bf16[112,1024]{1,0:T(8,128)(2,1)S(1)} %get-tuple-element.150), channel_id=1, source_target_pairs={{0,2},{2,0},{4,6},{6,4},{8,10},{10,8},{12,14},{14,12},{1,3},{3,1},... | collective-permute-start | bytes 688136 | tf_op jit(solution)/shard_map/ppermute | solution.py:239
  121.2 10.1 %collective-permute-start.27 = (bf16[112,1024]{1,0:T(8,128)(2,1)S(1)}, bf16[112,1024]{1,0:T(8,128)(2,1)S(1)}, u32[]{:S(2)}, u32[]{:S(2)}) collective-permute-start(bf16[112,1024]{1,0:T(8,128)(2,1)S(1)} %get-tuple-element.162), channel_id=1, source_target_pairs={{0,2},{2,0},{4,6},{6,4},{8,10},{10,8},{12,14},{14,12},{1,3},{3,1},... | collective-permute-start | bytes 688136 | tf_op jit(solution)/shard_map/ppermute | solution.py:239
  122.9 26.6 %collective-permute-start.26 = (bf16[128,1024]{1,0:T(8,128)(2,1)}, bf16[128,1024]{1,0:T(8,128)(2,1)}, u32[]{:S(2)}, u32[]{:S(2)}) collective-permute-start(bf16[128,1024]{1,0:T(8,128)(2,1)} %shard_map.137), channel_id=1, source_target_pairs={{0,8},{2,10},{4,12},{6,14},{8,0},{10,2},{12,4},{14,6},{1,9},{3,11}... | collective-permute-start | bytes 786440 | tf_op jit(solution)/shard_map/ppermute | solution.py:242
  127.1 5.0 %copy-start.16 = (bf16[144,1024]{1,0:T(8,128)(2,1)}, bf16[144,1024]{1,0:T(8,128)(2,1)S(1)}, u32[]{:S(2)}) copy-start(bf16[144,1024]{1,0:T(8,128)(2,1)S(1)} %shard_map.134) | copy-start | bytes 884740
  127.1 7.2 %copy-start.26 = (s32[128,4]{0,1:T(4,128)S(1)}, s32[128,4]{0,1:T(4,128)}, u32[]{:S(2)}) copy-start(s32[128,4]{0,1:T(4,128)} %param.8) | copy-start | bytes 6148
  127.1 21.0 %collective-permute-start.24 = (bf16[112,1024]{1,0:T(8,128)(2,1)}, bf16[112,1024]{1,0:T(8,128)(2,1)}, u32[]{:S(2)}, u32[]{:S(2)}) collective-permute-start(bf16[112,1024]{1,0:T(8,128)(2,1)} %get-tuple-element.152), channel_id=1, source_target_pairs={{0,2},{2,0},{4,6},{6,4},{8,10},{10,8},{12,14},{14,12},{1,3},{3,1},... | collective-permute-start | bytes 688136 | tf_op jit(solution)/shard_map/ppermute | solution.py:239
  132.1 0.7 copy-start.18
  132.8 17.0 %collective-permute-start.28 = (bf16[112,1024]{1,0:T(8,128)(2,1)}, bf16[112,1024]{1,0:T(8,128)(2,1)}, u32[]{:S(2)}, u32[]{:S(2)}) collective-permute-start(bf16[112,1024]{1,0:T(8,128)(2,1)} %get-tuple-element.163), channel_id=1, source_target_pairs={{0,2},{2,0},{4,6},{6,4},{8,10},{10,8},{12,14},{14,12},{1,3},{3,1},... | collective-permute-start | bytes 688136 | tf_op jit(solution)/shard_map/ppermute | solution.py:239
  134.0 11.6 %copy-start.17 = (bf16[144,1024]{1,0:T(8,128)(2,1)S(1)}, bf16[144,1024]{1,0:T(8,128)(2,1)}, u32[]{:S(2)}) copy-start(bf16[144,1024]{1,0:T(8,128)(2,1)} %copy-done.16) | copy-start | bytes 884740
  134.1 14.1 %copy-start.1 = (f32[4,128,1024]{2,1,0:T(8,128)S(1)}, f32[4,128,1024]{2,1,0:T(8,128)}, u32[]{:S(2)}) copy-start(f32[4,128,1024]{2,1,0:T(8,128)} %copy-done) | copy-start | bytes 6291460
  134.1 14.1 %copy-start.20 = (bf16[96,128]{1,0:T(8,128)(2,1)S(1)}, bf16[96,128]{1,0:T(8,128)(2,1)}, u32[]{:S(2)}) copy-start(bf16[96,128]{1,0:T(8,128)(2,1)} %copy-done.19) | copy-start | bytes 73732
  134.1 10.7 %collective-permute-start.25 = (bf16[96,1024]{1,0:T(8,128)(2,1)}, bf16[96,1024]{1,0:T(8,128)(2,1)S(1)}, u32[]{:S(2)}, u32[]{:S(2)}) collective-permute-start(bf16[96,1024]{1,0:T(8,128)(2,1)} %copy-done.21), channel_id=1, source_target_pairs={{0,2},{2,0},{4,6},{6,4},{8,10},{10,8},{12,14},{14,12},{1,3},{3,1},... | collective-permute-start | bytes 589832 | tf_op jit(solution)/shard_map/ppermute | solution.py:239
  145.6 18.7 %collective-permute-start.31 = (bf16[144,1024]{1,0:T(8,128)(2,1)}, bf16[144,1024]{1,0:T(8,128)(2,1)S(1)}, u32[]{:S(2)}, u32[]{:S(2)}) collective-permute-start(bf16[144,1024]{1,0:T(8,128)(2,1)} %copy-done.18), channel_id=1, source_target_pairs={{0,4},{2,6},{4,8},{6,10},{8,12},{10,14},{12,0},{14,2},{1,5},{3,7},... | collective-permute-start | bytes 884744 | tf_op jit(solution)/shard_map/ppermute | solution.py:242
  145.7 23.6 %collective-permute-start.30 = (bf16[144,1024]{1,0:T(8,128)(2,1)S(1)}, bf16[144,1024]{1,0:T(8,128)(2,1)S(1)}, u32[]{:S(2)}, u32[]{:S(2)}) collective-permute-start(bf16[144,1024]{1,0:T(8,128)(2,1)S(1)} %copy-done.17), channel_id=1, source_target_pairs={{0,8},{2,10},{4,12},{6,14},{8,0},{10,2},{12,4},{14,6},{1,9},{3,11}... | collective-permute-start | bytes 884744 | tf_op jit(solution)/shard_map/ppermute | solution.py:242
  148.1 3.1 %copy-start.10 = (bf16[896,1024]{1,0:T(8,128)(2,1)S(1)}, bf16[896,1024]{1,0:T(8,128)(2,1)}, u32[]{:S(2)}) copy-start(bf16[896,1024]{1,0:T(8,128)(2,1)} %copy-done.9) | copy-start | bytes 5505028
  149.5 1.8 copy-start.8
  149.5 25.2 %collective-permute-start.29 = (bf16[144,1024]{1,0:T(8,128)(2,1)S(1)}, bf16[144,1024]{1,0:T(8,128)(2,1)S(1)}, u32[]{:S(2)}, u32[]{:S(2)}) collective-permute-start(bf16[144,1024]{1,0:T(8,128)(2,1)S(1)} %shard_map.135), channel_id=1, source_target_pairs={{0,12},{2,14},{4,0},{6,2},{8,4},{10,6},{12,8},{14,10},{1,13},{3,15... | collective-permute-start | bytes 884744 | tf_op jit(solution)/shard_map/ppermute | solution.py:242
  154.9 3.4 %copy-start.3 = (bf16[896,1024]{1,0:T(8,128)(2,1)S(1)}, bf16[896,1024]{1,0:T(8,128)(2,1)}, u32[]{:S(2)}) copy-start(bf16[896,1024]{1,0:T(8,128)(2,1)} %copy-done.2) | copy-start | bytes 5505028
  154.9 3.4 %copy-start.12 = (bf16[896,1024]{1,0:T(8,128)(2,1)S(1)}, bf16[896,1024]{1,0:T(8,128)(2,1)}, u32[]{:S(2)}) copy-start(bf16[896,1024]{1,0:T(8,128)(2,1)} %copy-done.11) | copy-start | bytes 5505028
  158.4 1.1 copy-start.15
  159.5 3.0 %copy-start.23 = (bf16[128,1024]{1,0:T(8,128)(2,1)S(1)}, bf16[128,1024]{1,0:T(8,128)(2,1)}, u32[]{:S(2)}) copy-start(bf16[128,1024]{1,0:T(8,128)(2,1)} %copy-done.22) | copy-start | bytes 786436
  159.5 3.0 %copy-start.25 = (bf16[128,1024]{1,0:T(8,128)(2,1)S(1)}, bf16[128,1024]{1,0:T(8,128)(2,1)}, u32[]{:S(2)}) copy-start(bf16[128,1024]{1,0:T(8,128)(2,1)} %copy-done.24) | copy-start | bytes 786436
  174.8 1.5 collective-permute-start.32

commit v7 on v6

--- a/solution.py
+++ b/solution.py
@@ -283,7 +283,12 @@
             early.append(packed)
         compact[k] = over_pair(packed)
 
-    held_grad, blocks, early, compact[0] = settle((grad_out, blocks, early, compact[0]))
+    (first_packed,) = local_call(
+        grad_pack_kernel, (shape_of((padded, half_width)),), (info, grad_out, places[0]))
+    grad_first = over_pair(first_packed)
+    soon = {k: compact[k] for k in [0] + by_reach[:1]}
+    held_grad, blocks, early, soon, grad_first = settle((grad_out, blocks, early, soon, grad_first))
+    compact.update(soon)
     grad_blocks = {0: held_grad}
     for k in by_reach:
         grad_blocks[k] = over_line(held_grad, k)
@@ -291,10 +296,11 @@
     grad_packed = {
         k: local_call(
             grad_pack_kernel, (shape_of((padded, half_width)),), (info, grad_blocks[k], places[k]))[0]
-        for k in [0] + by_reach
+        for k in by_reach
     }
-    grad_compact = {k: over_pair(grad_packed[k]) for k in [0] + by_reach}
-    ahead = {k: grad_compact[k] for k in [0] + by_reach[:1]}
+    grad_compact = {k: over_pair(grad_packed[k]) for k in by_reach}
+    grad_compact[0] = grad_first
+    ahead = {k: grad_compact[k] for k in by_reach[:1]}
     compact, grad_blocks, grad_packed, ahead = settle((compact, grad_blocks, grad_packed, ahead))
     grad_compact.update(ahead)
     rows, weights = local_call(
@@ -317,9 +323,7 @@
         (info, over_core(sent), scaled, down_local))
 
     outward = by_reach[::-1]
-    out_back = {k: over_pair(out_packed[k]) for k in by_reach}
-    last, _ = settle((out_packed[0], out_back[by_reach[0]]))
-    out_back[0] = over_pair(last)
+    out_back = {k: over_pair(out_packed[k]) for k in every}
     (grad_rows,) = local_call(
         functools.partial(grad_rows_kernel, *sizes), (half_rows,),
         (info, *[grad_blocks[k] for k in every], *[grad_compact[k] for k in every]))
@@ -354,16 +358,15 @@
         (shape_of((lines, token_count, half_width), F32),
          *[shape_of((padded + TAIL, half_width)) for _ in every]),
         (info, over_core(sent), grad_gate, grad_up, gate_local, up_local, compact_tails))
-    in_packed, early = settle((in_packed, {k: out_came[k] for k in by_reach[:-1]}))
-    out_came.update(early)
+    in_packed, out_came[0] = settle((in_packed, out_came[0]))
     in_back, in_home, sequence = {}, {}, outward + [0]
     for i, k in enumerate(sequence):
         packed = in_packed[k]
         if i >= 2:
-            packed, in_home[sequence[i - 2]] = settle((packed, in_home[sequence[i - 2]]))
+            packed, _ = settle((packed, in_home[sequence[i - 2]]))
         in_back[k] = over_pair(packed)
         in_home[k] = to_home(k, in_dense, in_back, dense_tails)
-    in_home[outward[-1]], out_came = settle((in_home[outward[-1]], out_came))
+    in_home[sequence[0]], out_came = settle((in_home[sequence[0]], out_came))
     layer_out = summed(out_came)
     last_home, rows, rows_other, grad_rows, grad_other, scaled, grad_gate, grad_up = settle(
         ([in_home[k] for k in outward], rows, rows_other, grad_rows, grad_other, scaled, grad_gate, grad_up))

time: 177 us -> 156 us (0.88)
  waiting for transfers between devices: 95.5 us -> 65.7 us
  starting transfers between devices: 30.1 us -> 35.7 us
    ppermute x12, waiting for transfers between devices: 59.4 us -> 40.4 us  [over_line(): lax.ppermute(x, 'expert', [(i, (i // 2 + k) % lines * 2 + i % 2) for i in...]
    ppermute x16, waiting for transfers between devices: 32.4 us -> 21.9 us  [over_pair(): lax.ppermute(x, 'expert', [(i, i + 1 - 2 * (i % 2)) for i in range(expert...]
    ppermute x5, starting transfers between devices: 5.29 us -> 7.62 us  [over_core(): return lax.ppermute(x, 'tensor', [(0, 1), (1, 0)])]
    ppermute x12, starting transfers between devices: 10.8 us -> 13.1 us  [over_line(): lax.ppermute(x, 'expert', [(i, (i // 2 + k) % lines * 2 + i % 2) for i in...]
    unnamed x55 -> x45, local copies, waits for them, and re-layouts: 2.33 us -> 4.09 us
  transfers between devices with their start and end apart: 33 -> 33, of which waited for: 19 -> 15; matrix products, arithmetic and copies ran while one was open for 7% -> 9% of each run, Pallas kernels for 17% -> 19%
where the time goes in v7:
time: 156 us; the launch traced here: 155 us
  waiting for transfers between devices  65.7 us (42%)
  starting transfers between devices  35.7 us (23%)
  Pallas kernels  32.6 us (21%)
  matrix products  9.79 us (6%)
  other arithmetic  5.92 us (4%)
  local copies, waits for them, and re-layouts  4.1 us (3%)
    ppermute x12, waiting for transfers between devices, over_line(): lax.ppermute(x, 'expert', [(i, (i // 2 + k) % lines * 2 + i % 2) for i in...  40.4 us
    pallas_call x22, Pallas kernels, local_call(): pl.pallas_call(kernel, out_shape=tuple(outs), in_specs=[SMEM_SPEC] + [VME...  32.6 us
    ppermute x16, waiting for transfers between devices, over_pair(): lax.ppermute(x, 'expert', [(i, i + 1 - 2 * (i % 2)) for i in range(expert...  21.9 us
    ppermute x16, starting transfers between devices, over_pair(): lax.ppermute(x, 'expert', [(i, i + 1 - 2 * (i % 2)) for i in range(expert...  15 us
    ppermute x12, starting transfers between devices, over_line(): lax.ppermute(x, 'expert', [(i, (i // 2 + k) % lines * 2 + i % 2) for i in...  13.1 us
    dot_general x3, matrix products, dot(): lax.dot_general(a, b, (contract, ((), ())), preferred_element_type=F32)  9.79 us
    ppermute x5, starting transfers between devices, over_core(): return lax.ppermute(x, 'tensor', [(0, 1), (1, 0)])  7.62 us
    unnamed x45, local copies, waits for them, and re-layouts  4.09 us
  transfers between devices with their start and end apart: 33, of which 15 were waited for; matrix products, arithmetic and copies ran while one was open for 9% of the time, Pallas kernels for 19%

profile of v7, /device:TPU:9, one launch (start us, length us, event | category | flops | bytes accessed | tf_op | source)
XLA Modules:
  0.0 155.0 jit_solution(7290670248073884328)
XLA Ops:
  0.6 0.8 select_reduce_fusion.1
  1.5 1.0 pad_maximum_fusion.3.block.refs_0_
  2.4 1.3 collective-permute-start
  3.8 1.1 collective-permute-start.1
  4.9 1.4 collective-permute-start.2
  6.3 0.9 shard_map.118
  7.2 1.3 collective-permute-start.3
  8.5 1.8 %collective-permute-done.block.refs_1_ = bf16[144,1024]{1,0:T(8,128)(2,1)S(1)} collective-permute-done((bf16[144,1024]{1,0:T(8,128)(2,1)S(1)}, bf16[144,1024]{1,0:T(8,128)(2,1)S(1)}, u32[]{:S(2)}, u32[]{:S(2)}) %collective-permute-start) | collective-permute-done | bytes 294944 | tf_op jit(solution)/shard_map/ppermute | solution.py:242
  10.4 0.9 shard_map.119
  11.3 1.3 collective-permute-start.4
  12.6 0.9 copy-done.11
  14.5 16.7 %collective-permute-done.2.block.refs_3_ = bf16[144,1024]{1,0:T(8,128)(2,1)S(1)} collective-permute-done((bf16[144,1024]{1,0:T(8,128)(2,1)S(1)}, bf16[144,1024]{1,0:T(8,128)(2,1)S(1)}, u32[]{:S(2)}, u32[]{:S(2)}) %collective-permute-start.2) | collective-permute-done | bytes 294944 | tf_op jit(solution)/shard_map/ppermute | solution.py:242
  31.3 0.9 shard_map.120
  32.4 1.4 collective-permute-start.10
  33.7 0.9 shard_map.122
  34.6 1.3 collective-permute-start.6
  36.2 1.3 collective-permute-done.8.block.refs_1_
  37.5 0.7 shard_map.123
  38.2 2.2 %collective-permute-start.11 = (bf16[96,1024]{1,0:T(8,128)(2,1)S(1)}, bf16[96,1024]{1,0:T(8,128)(2,1)S(1)}, u32[]{:S(2)}, u32[]{:S(2)}) collective-permute-start(bf16[96,1024]{1,0:T(8,128)(2,1)S(1)} %shard_map.123), channel_id=1, source_target_pairs={{0,2},{2,0},{4,6},{6,4},{8,10},{10,8},{12,14},{14,12},{1,3},{3,1},... | collective-permute-start | bytes 589832 | tf_op jit(solution)/shard_map/ppermute | solution.py:239
  40.4 1.5 collective-permute-done.9.block.refs_2_
  41.9 0.7 shard_map.124
  42.7 12.5 %collective-permute-done.10.block.refs_3_ = bf16[128,1024]{1,0:T(8,128)(2,1)S(1)} collective-permute-done((bf16[128,1024]{1,0:T(8,128)(2,1)S(1)}, bf16[128,1024]{1,0:T(8,128)(2,1)S(1)}, u32[]{:S(2)}, u32[]{:S(2)}) %collective-permute-start.10) | collective-permute-done | bytes 262176 | tf_op jit(solution)/shard_map/ppermute | solution.py:242
  55.9 0.8 shard_map.126
  56.7 3.4 %collective-permute-start.12 = (bf16[896,1024]{1,0:T(8,128)(2,1)S(1)}, bf16[896,1024]{1,0:T(8,128)(2,1)S(1)}, u32[]{:S(2)}, u32[]{:S(2)}) collective-permute-start(bf16[896,1024]{1,0:T(8,128)(2,1)S(1)} %get-tuple-element.161.own), channel_id=1, source_target_pairs={{0,1},{1,0},{2,3},{3,2},{4,5},{5,4},{6,7},{7,6},{8,9},{9,8},{10,11... | collective-permute-start | bytes 5505032 | tf_op jit(solution)/shard_map/ppermute | solution.py:248
  60.2 1.3 collective-permute-start.13
  61.6 5.0 %collective-permute-done.13.refs_7_ = bf16[96,1024]{1,0:T(8,128)(2,1)S(1)} collective-permute-done((bf16[96,1024]{1,0:T(8,128)(2,1)S(1)}, bf16[96,1024]{1,0:T(8,128)(2,1)S(1)}, u32[]{:S(2)}, u32[]{:S(2)}) %collective-permute-start.13) | collective-permute-done | bytes 196640 | tf_op jit(solution)/shard_map/ppermute | solution.py:239
  66.7 5.7 %shard_map.127 = (f32[896,384]{1,0:T(8,128)S(1)}, f32[896,384]{1,0:T(8,128)S(1)}, bf16[896,384]{1,0:T(8,128)(2,1)S(1)}, bf16[896,1024]{1,0:T(8,128)(2,1)S(1)}) custom-call(s32[3]{0:T(128)S(1)} %pad_add_fusion.info, bf16[896,1024]{1,0:T(8,128)(2,1)S(1)} %get-tuple-element.161.own, bf16[896,1024]{1,0:T(8,128)(2,1)S(1)} %collective-permute-done.12.other, ...), custom_call_target="tpu_custom_call" | custom-call | flops 1000 | bytes 1000 | tf_op jit(solution)/shard_map/pallas_call | solution.py:41
  72.4 1.4 collective-permute-start.15
  74.4 2.7 %collective-permute-done.15.came = bf16[896,1024]{1,0:T(8,128)(2,1)S(1)} collective-permute-done((bf16[896,1024]{1,0:T(8,128)(2,1)S(1)}, bf16[896,1024]{1,0:T(8,128)(2,1)S(1)}, u32[]{:S(2)}, u32[]{:S(2)}) %collective-permute-start.15) | collective-permute-done | bytes 1835040 | tf_op jit(solution)/shard_map/ppermute | solution.py:248
  77.2 1.7 %shard_map.129 = (f32[4,128,1024]{2,1,0:T(8,128)S(1)}, bf16[96,1024]{1,0:T(8,128)(2,1)S(1)}, bf16[96,1024]{1,0:T(8,128)(2,1)S(1)}, bf16[96,1024]{1,0:T(8,128)(2,1)S(1)}, bf16[96,1024]{1,0:T(8,128)(2,1)S(1)}) custom-call(s32[3]{0:T(128)S(1)} %pad_add_fusion.info, bf16[896,1024]{1,0:T(8,128)(2,1)S(1)} %collective-permute-done.15.came, ...), custom_call_target="tpu_custom_call" | custom-call | flops 1000 | bytes 1000 | tf_op jit(solution)/shard_map/pallas_call | solution.py:41
  79.3 1.2 collective-permute-start.17
  80.8 1.2 collective-permute-start.19
  82.7 5.5 %shard_map.130 = (bf16[896,384]{1,0:T(8,128)(2,1)S(1)}, bf16[896,384]{1,0:T(8,128)(2,1)S(1)}, bf16[896,1024]{1,0:T(8,128)(2,1)S(1)}, f32[4,16,128]{2,1,0:T(8,128)S(1)}, f32[4,16,128]{2,1,0:T(8,128)S(1)}) custom-call(s32[3]{0:T(128)S(1)} %pad_add_fusion.info, bf16[896,1024]{1,0:T(8,128)(2,1)S(1)} %shard_map.128.own, ...), custom_call_target="tpu_custom_call" | custom-call | flops 1000 | bytes 1000 | tf_op jit(solution)/shard_map/pallas_call | solution.py:41
  88.3 1.6 %collective-permute-done.18.back = bf16[96,1024]{1,0:T(8,128)(2,1)S(1)} collective-permute-done((bf16[96,1024]{1,0:T(8,128)(2,1)S(1)}, bf16[96,1024]{1,0:T(8,128)(2,1)S(1)}, u32[]{:S(2)}, u32[]{:S(2)}) %collective-permute-start.18) | collective-permute-done | bytes 196640 | tf_op jit(solution)/shard_map/ppermute | solution.py:239
  89.9 4.2 %collective-permute-done.19.back = bf16[96,1024]{1,0:T(8,128)(2,1)S(1)} collective-permute-done((bf16[96,1024]{1,0:T(8,128)(2,1)S(1)}, bf16[96,1024]{1,0:T(8,128)(2,1)S(1)}, u32[]{:S(2)}, u32[]{:S(2)}) %collective-permute-start.19) | collective-permute-done | bytes 196640 | tf_op jit(solution)/shard_map/ppermute | solution.py:239
  94.1 0.9 collective-permute-start.20
  95.1 1.2 collective-permute-start.21
  96.3 0.8 shard_map.134
  97.2 1.5 shard_map.135
  98.7 3.4 %collective-permute-start.24 = (bf16[128,1024]{1,0:T(8,128)(2,1)}, bf16[128,1024]{1,0:T(8,128)(2,1)}, u32[]{:S(2)}, u32[]{:S(2)}) collective-permute-start(bf16[128,1024]{1,0:T(8,128)(2,1)} %shard_map.135), channel_id=1, source_target_pairs={{0,8},{2,10},{4,12},{6,14},{8,0},{10,2},{12,4},{14,6},{1,9},{3,11}... | collective-permute-start | bytes 786440 | tf_op jit(solution)/shard_map/ppermute | solution.py:242
  102.0 1.5 shard_map.136
  103.5 0.8 shard_map.132
  104.4 3.4 %shard_map.131 = (f32[4,128,1024]{2,1,0:T(8,128)S(1)}, bf16[112,1024]{1,0:T(8,128)(2,1)S(1)}, bf16[112,1024]{1,0:T(8,128)(2,1)S(1)}, bf16[112,1024]{1,0:T(8,128)(2,1)}, bf16[112,1024]{1,0:T(8,128)(2,1)}) custom-call(s32[3]{0:T(128)S(1)} %pad_add_fusion.info, bf16[896,1024]{1,0:T(8,128)(2,1)S(1)} %collective-permute-done.20.came, ...), custom_call_target="tpu_custom_call" | custom-call | flops 1000 | bytes 1000 | tf_op jit(solution)/shard_map/pallas_call | solution.py:41
  109.3 1.2 collective-permute-start.26
  110.6 4.9 %collective-permute-done.22.back = bf16[112,1024]{1,0:T(8,128)(2,1)} collective-permute-done((bf16[112,1024]{1,0:T(8,128)(2,1)}, bf16[112,1024]{1,0:T(8,128)(2,1)}, u32[]{:S(2)}, u32[]{:S(2)}) %collective-permute-start.22) | collective-permute-done | bytes 229408 | tf_op jit(solution)/shard_map/ppermute | solution.py:239
  115.4 1.2 shard_map.133
  116.7 5.3 %collective-permute-done.25 = bf16[128,1024]{1,0:T(8,128)(2,1)} collective-permute-done((bf16[128,1024]{1,0:T(8,128)(2,1)}, bf16[128,1024]{1,0:T(8,128)(2,1)}, u32[]{:S(2)}, u32[]{:S(2)}) %collective-permute-start.25) | collective-permute-done | bytes 262176 | tf_op jit(solution)/shard_map/ppermute | solution.py:242
  122.0 1.2 shard_map.137
  123.2 2.3 %collective-permute-start.31 = (bf16[144,1024]{1,0:T(8,128)(2,1)S(1)}, bf16[144,1024]{1,0:T(8,128)(2,1)S(1)}, u32[]{:S(2)}, u32[]{:S(2)}) collective-permute-start(bf16[144,1024]{1,0:T(8,128)(2,1)S(1)} %shard_map.137), channel_id=1, source_target_pairs={{0,4},{2,6},{4,8},{6,10},{8,12},{10,14},{12,0},{14,2},{1,5},{3,7},... | collective-permute-start | bytes 884744 | tf_op jit(solution)/shard_map/ppermute | solution.py:242
  125.5 1.9 %collective-permute-start.30 = (bf16[144,1024]{1,0:T(8,128)(2,1)S(1)}, bf16[144,1024]{1,0:T(8,128)(2,1)S(1)}, u32[]{:S(2)}, u32[]{:S(2)}) collective-permute-start(bf16[144,1024]{1,0:T(8,128)(2,1)S(1)} %shard_map.133), channel_id=1, source_target_pairs={{0,8},{2,10},{4,12},{6,14},{8,0},{10,2},{12,4},{14,6},{1,9},{3,11}... | collective-permute-start | bytes 884744 | tf_op jit(solution)/shard_map/ppermute | solution.py:242
  127.6 1.3 collective-permute-start.27
  128.8 2.0 %add_convert_fusion.1 = bf16[128,1024]{1,0:T(8,128)(2,1)} fusion(bf16[128,1024]{1,0:T(8,128)(2,1)} %collective-permute-done.25, bf16[128,1024]{1,0:T(8,128)(2,1)} %collective-permute-done.24, bf16[128,1024]{1,0:T(8,128)(2,1)} %collective-permute-done.23, bf16[128,1024]{1,0:T(8,128)(2,1)S(1)} %shard_map.132), kind=kLoop, calls=%fused_computation.16 | loop fusion | flops 1048576 | bytes 1310720 | tf_op jit(solution)/shard_map/convert_element_type | solution.py:349
  130.8 2.3 %collective-permute-done.28.back = bf16[112,1024]{1,0:T(8,128)(2,1)S(1)} collective-permute-done((bf16[112,1024]{1,0:T(8,128)(2,1)S(1)}, bf16[112,1024]{1,0:T(8,128)(2,1)S(1)}, u32[]{:S(2)}, u32[]{:S(2)}) %collective-permute-start.28) | collective-permute-done | bytes 229408 | tf_op jit(solution)/shard_map/ppermute | solution.py:239
  133.1 0.8 shard_map.139
  134.1 3.9 %collective-permute-done.27.back = bf16[112,1024]{1,0:T(8,128)(2,1)S(1)} collective-permute-done((bf16[112,1024]{1,0:T(8,128)(2,1)S(1)}, bf16[112,1024]{1,0:T(8,128)(2,1)S(1)}, u32[]{:S(2)}, u32[]{:S(2)}) %collective-permute-start.27) | collective-permute-done | bytes 229408 | tf_op jit(solution)/shard_map/ppermute | solution.py:239
  138.0 0.8 shard_map.138
  139.1 0.8 copy-done.14
  139.9 3.4 %fusion.7 = bf16[1,2048,384]{2,1,0:T(8,128)(2,1)} fusion(bf16[896,384]{1,0:T(8,128)(2,1)S(1)} %copy-done.14, bf16[896,1024]{1,0:T(8,128)(2,1)S(1)} %get-tuple-element.179, bf16[896,1024]{1,0:T(8,128)(2,1)S(1)} %get-tuple-element.178), kind=kOutput, calls=%fused_computation.8 | convolution fusion | flops 1417412608 | bytes 5931008 | tf_op jit(solution)/shard_map/dot_general | solution.py:24
  143.4 3.4 %fusion.8 = bf16[1,2048,384]{2,1,0:T(8,128)(2,1)} fusion(bf16[896,384]{1,0:T(8,128)(2,1)S(1)} %get-tuple-element.164.refs_1_, bf16[896,1024]{1,0:T(8,128)(2,1)S(1)} %get-tuple-element.179, bf16[896,1024]{1,0:T(8,128)(2,1)S(1)} %get-tuple-element.178), kind=kOutput, calls=%fused_computation.9 | convolution fusion | flops 1417412608 | bytes 5931008 | tf_op jit(solution)/shard_map/dot_general | solution.py:24
  147.0 0.8 copy-done.16
  147.9 3.0 %fusion.9 = bf16[1,384,2048]{2,1,0:T(8,128)(2,1)} fusion(bf16[896,384]{1,0:T(8,128)(2,1)S(1)} %copy-done.16, bf16[896,1024]{1,0:T(8,128)(2,1)S(1)} %get-tuple-element.177, bf16[896,1024]{1,0:T(8,128)(2,1)S(1)} %get-tuple-element.176), kind=kOutput, calls=%fused_computation.10 | convolution fusion | flops 1417412608 | bytes 5931008 | tf_op jit(solution)/shard_map/dot_general | solution.py:24
  150.9 1.2 collective-permute-done.29
  152.2 1.4 collective-permute-start.32
  153.6 0.9 add_convert_fusion
  (98 shorter events, 8.0 us)
Async XLA Ops:
  0.6 31.6 %copy-start.12 = (bf16[128,1024]{1,0:T(8,128)(2,1)S(1)}, bf16[128,1024]{1,0:T(8,128)(2,1)}, u32[]{:S(2)}) copy-start(bf16[128,1024]{1,0:T(8,128)(2,1)} %refs_0_) | copy-start | bytes 786436
  2.4 7.9 %collective-permute-start = (bf16[144,1024]{1,0:T(8,128)(2,1)S(1)}, bf16[144,1024]{1,0:T(8,128)(2,1)S(1)}, u32[]{:S(2)}, u32[]{:S(2)}) collective-permute-start(bf16[144,1024]{1,0:T(8,128)(2,1)S(1)} %pad_maximum_fusion.3.block.refs_0_), channel_id=1, source_target_pairs={{0,4},{2,6},{4,8},{6,10},{8,12},{10,14},{12,0},{14,2},{1,5},{3,7},... | collective-permute-start | bytes 884744 | tf_op jit(solution)/shard_map/ppermute | solution.py:242
  3.8 28.4 %collective-permute-start.1 = (bf16[144,1024]{1,0:T(8,128)(2,1)S(1)}, bf16[144,1024]{1,0:T(8,128)(2,1)S(1)}, u32[]{:S(2)}, u32[]{:S(2)}) collective-permute-start(bf16[144,1024]{1,0:T(8,128)(2,1)S(1)} %pad_maximum_fusion.3.block.refs_0_), channel_id=1, source_target_pairs={{0,8},{2,10},{4,12},{6,14},{8,0},{10,2},{12,4},{14,6},{1,9},{3,11}... | collective-permute-start | bytes 884744 | tf_op jit(solution)/shard_map/ppermute | solution.py:242
  4.9 26.4 %collective-permute-start.2 = (bf16[144,1024]{1,0:T(8,128)(2,1)S(1)}, bf16[144,1024]{1,0:T(8,128)(2,1)S(1)}, u32[]{:S(2)}, u32[]{:S(2)}) collective-permute-start(bf16[144,1024]{1,0:T(8,128)(2,1)S(1)} %pad_maximum_fusion.3.block.refs_0_), channel_id=1, source_target_pairs={{0,12},{2,14},{4,0},{6,2},{8,4},{10,6},{12,8},{14,10},{1,13},{3,15... | collective-permute-start | bytes 884744 | tf_op jit(solution)/shard_map/ppermute | solution.py:242
  7.2 24.9 %collective-permute-start.3 = (bf16[112,1024]{1,0:T(8,128)(2,1)S(1)}, bf16[112,1024]{1,0:T(8,128)(2,1)S(1)}, u32[]{:S(2)}, u32[]{:S(2)}) collective-permute-start(bf16[112,1024]{1,0:T(8,128)(2,1)S(1)} %get-tuple-element.87), channel_id=1, source_target_pairs={{0,2},{2,0},{4,6},{6,4},{8,10},{10,8},{12,14},{14,12},{1,3},{3,1},... | collective-permute-start | bytes 688136 | tf_op jit(solution)/shard_map/ppermute | solution.py:239
  10.4 56.3 %copy-start.4 = (bf16[1,2048,384]{2,1,0:T(8,128)(2,1)S(1)}, bf16[1,2048,384]{2,1,0:T(8,128)(2,1)}, u32[]{:S(2)}) copy-start(bf16[1,2048,384]{2,1,0:T(8,128)(2,1)} %param.11) | copy-start | bytes 4718596
  11.3 20.9 %collective-permute-start.4 = (bf16[112,1024]{1,0:T(8,128)(2,1)S(1)}, bf16[112,1024]{1,0:T(8,128)(2,1)S(1)}, u32[]{:S(2)}, u32[]{:S(2)}) collective-permute-start(bf16[112,1024]{1,0:T(8,128)(2,1)S(1)} %get-tuple-element.88), channel_id=1, source_target_pairs={{0,2},{2,0},{4,6},{6,4},{8,10},{10,8},{12,14},{14,12},{1,3},{3,1},... | collective-permute-start | bytes 688136 | tf_op jit(solution)/shard_map/ppermute | solution.py:239
  12.6 0.9 copy-start.11
  14.2 17.9 %collective-permute-start.5 = (bf16[96,1024]{1,0:T(8,128)(2,1)S(1)}, bf16[96,1024]{1,0:T(8,128)(2,1)S(1)}, u32[]{:S(2)}, u32[]{:S(2)}) collective-permute-start(bf16[96,1024]{1,0:T(8,128)(2,1)S(1)} %shard_map.121), channel_id=1, source_target_pairs={{0,2},{2,0},{4,6},{6,4},{8,10},{10,8},{12,14},{14,12},{1,3},{3,1},... | collective-permute-start | bytes 589832 | tf_op jit(solution)/shard_map/ppermute | solution.py:239
  32.2 5.3 %collective-permute-start.8 = (bf16[128,1024]{1,0:T(8,128)(2,1)S(1)}, bf16[128,1024]{1,0:T(8,128)(2,1)S(1)}, u32[]{:S(2)}, u32[]{:S(2)}) collective-permute-start(bf16[128,1024]{1,0:T(8,128)(2,1)S(1)} %copy-done.12), channel_id=1, source_target_pairs={{0,4},{2,6},{4,8},{6,10},{8,12},{10,14},{12,0},{14,2},{1,5},{3,7},... | collective-permute-start | bytes 786440 | tf_op jit(solution)/shard_map/ppermute | solution.py:242
  32.3 9.6 %collective-permute-start.9 = (bf16[128,1024]{1,0:T(8,128)(2,1)S(1)}, bf16[128,1024]{1,0:T(8,128)(2,1)S(1)}, u32[]{:S(2)}, u32[]{:S(2)}) collective-permute-start(bf16[128,1024]{1,0:T(8,128)(2,1)S(1)} %copy-done.12), channel_id=1, source_target_pairs={{0,8},{2,10},{4,12},{6,14},{8,0},{10,2},{12,4},{14,6},{1,9},{3,11}... | collective-permute-start | bytes 786440 | tf_op jit(solution)/shard_map/ppermute | solution.py:242
  32.4 22.8 %collective-permute-start.10 = (bf16[128,1024]{1,0:T(8,128)(2,1)S(1)}, bf16[128,1024]{1,0:T(8,128)(2,1)S(1)}, u32[]{:S(2)}, u32[]{:S(2)}) collective-permute-start(bf16[128,1024]{1,0:T(8,128)(2,1)S(1)} %copy-done.12), channel_id=1, source_target_pairs={{0,12},{2,14},{4,0},{6,2},{8,4},{10,6},{12,8},{14,10},{1,13},{3,15... | collective-permute-start | bytes 786440 | tf_op jit(solution)/shard_map/ppermute | solution.py:242
  34.6 32.0 %copy-start.2 = (bf16[1,384,2048]{2,1,0:T(8,128)(2,1)S(1)}, bf16[1,384,2048]{2,1,0:T(8,128)(2,1)}, u32[]{:S(2)}) copy-start(bf16[1,384,2048]{2,1,0:T(8,128)(2,1)} %param.12) | copy-start | bytes 4718596
  34.6 32.0 %copy-start.3 = (bf16[1,2048,384]{2,1,0:T(8,128)(2,1)S(1)}, bf16[1,2048,384]{2,1,0:T(8,128)(2,1)}, u32[]{:S(2)}) copy-start(bf16[1,2048,384]{2,1,0:T(8,128)(2,1)} %param.10) | copy-start | bytes 4718596
  34.6 21.2 %collective-permute-start.6 = (bf16[112,1024]{1,0:T(8,128)(2,1)S(1)}, bf16[112,1024]{1,0:T(8,128)(2,1)S(1)}, u32[]{:S(2)}, u32[]{:S(2)}) collective-permute-start(bf16[112,1024]{1,0:T(8,128)(2,1)S(1)} %get-tuple-element.93), channel_id=1, source_target_pairs={{0,2},{2,0},{4,6},{6,4},{8,10},{10,8},{12,14},{14,12},{1,3},{3,1},... | collective-permute-start | bytes 688136 | tf_op jit(solution)/shard_map/ppermute | solution.py:239
  35.9 20.0 %collective-permute-start.7 = (bf16[112,1024]{1,0:T(8,128)(2,1)S(1)}, bf16[112,1024]{1,0:T(8,128)(2,1)S(1)}, u32[]{:S(2)}, u32[]{:S(2)}) collective-permute-start(bf16[112,1024]{1,0:T(8,128)(2,1)S(1)} %get-tuple-element.89), channel_id=1, source_target_pairs={{0,2},{2,0},{4,6},{6,4},{8,10},{10,8},{12,14},{14,12},{1,3},{3,1},... | collective-permute-start | bytes 688136 | tf_op jit(solution)/shard_map/ppermute | solution.py:239
  38.2 17.7 %collective-permute-start.11 = (bf16[96,1024]{1,0:T(8,128)(2,1)S(1)}, bf16[96,1024]{1,0:T(8,128)(2,1)S(1)}, u32[]{:S(2)}, u32[]{:S(2)}) collective-permute-start(bf16[96,1024]{1,0:T(8,128)(2,1)S(1)} %shard_map.123), channel_id=1, source_target_pairs={{0,2},{2,0},{4,6},{6,4},{8,10},{10,8},{12,14},{14,12},{1,3},{3,1},... | collective-permute-start | bytes 589832 | tf_op jit(solution)/shard_map/ppermute | solution.py:239
  56.7 15.7 %copy-start.5 = (bf16[896,1024]{1,0:T(8,128)(2,1)}, bf16[896,1024]{1,0:T(8,128)(2,1)S(1)}, u32[]{:S(2)}) copy-start(bf16[896,1024]{1,0:T(8,128)(2,1)S(1)} %get-tuple-element.161.own) | copy-start | bytes 5505028
  56.7 9.9 %collective-permute-start.12 = (bf16[896,1024]{1,0:T(8,128)(2,1)S(1)}, bf16[896,1024]{1,0:T(8,128)(2,1)S(1)}, u32[]{:S(2)}, u32[]{:S(2)}) collective-permute-start(bf16[896,1024]{1,0:T(8,128)(2,1)S(1)} %get-tuple-element.161.own), channel_id=1, source_target_pairs={{0,1},{1,0},{2,3},{3,2},{4,5},{5,4},{6,7},{7,6},{8,9},{9,8},{10,11... | collective-permute-start | bytes 5505032 | tf_op jit(solution)/shard_map/ppermute | solution.py:248
  60.2 6.5 %collective-permute-start.13 = (bf16[96,1024]{1,0:T(8,128)(2,1)S(1)}, bf16[96,1024]{1,0:T(8,128)(2,1)S(1)}, u32[]{:S(2)}, u32[]{:S(2)}) collective-permute-start(bf16[96,1024]{1,0:T(8,128)(2,1)S(1)} %shard_map.125), channel_id=1, source_target_pairs={{0,2},{2,0},{4,6},{6,4},{8,10},{10,8},{12,14},{14,12},{1,3},{3,1},... | collective-permute-start | bytes 589832 | tf_op jit(solution)/shard_map/ppermute | solution.py:239
  61.4 11.0 %collective-permute-start.14 = (bf16[96,1024]{1,0:T(8,128)(2,1)S(1)}, bf16[96,1024]{1,0:T(8,128)(2,1)S(1)}, u32[]{:S(2)}, u32[]{:S(2)}) collective-permute-start(bf16[96,1024]{1,0:T(8,128)(2,1)S(1)} %shard_map.124), channel_id=1, source_target_pairs={{0,2},{2,0},{4,6},{6,4},{8,10},{10,8},{12,14},{14,12},{1,3},{3,1},... | collective-permute-start | bytes 589832 | tf_op jit(solution)/shard_map/ppermute | solution.py:239
  66.6 5.7 %copy-start.7 = (bf16[896,1024]{1,0:T(8,128)(2,1)}, bf16[896,1024]{1,0:T(8,128)(2,1)S(1)}, u32[]{:S(2)}) copy-start(bf16[896,1024]{1,0:T(8,128)(2,1)S(1)} %collective-permute-done.12.other) | copy-start | bytes 5505028
  72.4 4.8 %copy-start.15 = (bf16[896,384]{1,0:T(8,128)(2,1)}, bf16[896,384]{1,0:T(8,128)(2,1)S(1)}, u32[]{:S(2)}) copy-start(bf16[896,384]{1,0:T(8,128)(2,1)S(1)} %get-tuple-element.165.refs_0_) | copy-start | bytes 2064388
  72.4 4.8 %collective-permute-start.15 = (bf16[896,1024]{1,0:T(8,128)(2,1)S(1)}, bf16[896,1024]{1,0:T(8,128)(2,1)S(1)}, u32[]{:S(2)}, u32[]{:S(2)}) collective-permute-start(bf16[896,1024]{1,0:T(8,128)(2,1)S(1)} %get-tuple-element.125), channel_id=1, source_target_pairs={{0,1},{1,0},{2,3},{3,2},{4,5},{5,4},{6,7},{7,6},{8,9},{9,8},{10,11... | collective-permute-start | bytes 5505032 | tf_op jit(solution)/shard_map/ppermute | solution.py:248
  74.4 8.3 %copy-start = (bf16[896,1024]{1,0:T(8,128)(2,1)}, bf16[896,1024]{1,0:T(8,128)(2,1)S(1)}, u32[]{:S(2)}) copy-start(bf16[896,1024]{1,0:T(8,128)(2,1)S(1)} %shard_map.128.own) | copy-start | bytes 5505028
  78.9 3.9 %collective-permute-start.16 = (bf16[896,1024]{1,0:T(8,128)(2,1)S(1)}, bf16[896,1024]{1,0:T(8,128)(2,1)S(1)}, u32[]{:S(2)}, u32[]{:S(2)}) collective-permute-start(bf16[896,1024]{1,0:T(8,128)(2,1)S(1)} %shard_map.128.own), channel_id=1, source_target_pairs={{0,1},{1,0},{2,3},{3,2},{4,5},{5,4},{6,7},{7,6},{8,9},{9,8},{10,11... | collective-permute-start | bytes 5505032 | tf_op jit(solution)/shard_map/ppermute | solution.py:248
  79.3 8.9 %collective-permute-start.17 = (bf16[96,1024]{1,0:T(8,128)(2,1)S(1)}, bf16[96,1024]{1,0:T(8,128)(2,1)S(1)}, u32[]{:S(2)}, u32[]{:S(2)}) collective-permute-start(bf16[96,1024]{1,0:T(8,128)(2,1)S(1)} %get-tuple-element.128), channel_id=1, source_target_pairs={{0,2},{2,0},{4,6},{6,4},{8,10},{10,8},{12,14},{14,12},{1,3},{3,1},... | collective-permute-start | bytes 589832 | tf_op jit(solution)/shard_map/ppermute | solution.py:239
  80.6 9.3 %collective-permute-start.18 = (bf16[96,1024]{1,0:T(8,128)(2,1)S(1)}, bf16[96,1024]{1,0:T(8,128)(2,1)S(1)}, u32[]{:S(2)}, u32[]{:S(2)}) collective-permute-start(bf16[96,1024]{1,0:T(8,128)(2,1)S(1)} %get-tuple-element.129), channel_id=1, source_target_pairs={{0,2},{2,0},{4,6},{6,4},{8,10},{10,8},{12,14},{14,12},{1,3},{3,1},... | collective-permute-start | bytes 589832 | tf_op jit(solution)/shard_map/ppermute | solution.py:239
  80.8 13.3 %collective-permute-start.19 = (bf16[96,1024]{1,0:T(8,128)(2,1)S(1)}, bf16[96,1024]{1,0:T(8,128)(2,1)S(1)}, u32[]{:S(2)}, u32[]{:S(2)}) collective-permute-start(bf16[96,1024]{1,0:T(8,128)(2,1)S(1)} %get-tuple-element.130), channel_id=1, source_target_pairs={{0,2},{2,0},{4,6},{6,4},{8,10},{10,8},{12,14},{14,12},{1,3},{3,1},... | collective-permute-start | bytes 589832 | tf_op jit(solution)/shard_map/ppermute | solution.py:239
  82.7 5.5 %copy-start.9 = (bf16[896,1024]{1,0:T(8,128)(2,1)}, bf16[896,1024]{1,0:T(8,128)(2,1)S(1)}, u32[]{:S(2)}) copy-start(bf16[896,1024]{1,0:T(8,128)(2,1)S(1)} %collective-permute-done.16.other) | copy-start | bytes 5505028
  88.2 16.1 %copy-start.13 = (bf16[896,384]{1,0:T(8,128)(2,1)}, bf16[896,384]{1,0:T(8,128)(2,1)S(1)}, u32[]{:S(2)}) copy-start(bf16[896,384]{1,0:T(8,128)(2,1)S(1)} %get-tuple-element.163.refs_0_) | copy-start | bytes 2064388
  94.1 10.2 %collective-permute-start.20 = (bf16[896,1024]{1,0:T(8,128)(2,1)S(1)}, bf16[896,1024]{1,0:T(8,128)(2,1)S(1)}, u32[]{:S(2)}, u32[]{:S(2)}) collective-permute-start(bf16[896,1024]{1,0:T(8,128)(2,1)S(1)} %get-tuple-element.135), channel_id=1, source_target_pairs={{0,1},{1,0},{2,3},{3,2},{4,5},{5,4},{6,7},{7,6},{8,9},{9,8},{10,11... | collective-permute-start | bytes 5505032 | tf_op jit(solution)/shard_map/ppermute | solution.py:248
  95.1 8.5 %collective-permute-start.21 = (bf16[96,1024]{1,0:T(8,128)(2,1)S(1)}, bf16[96,1024]{1,0:T(8,128)(2,1)S(1)}, u32[]{:S(2)}, u32[]{:S(2)}) collective-permute-start(bf16[96,1024]{1,0:T(8,128)(2,1)S(1)} %get-tuple-element.127), channel_id=1, source_target_pairs={{0,2},{2,0},{4,6},{6,4},{8,10},{10,8},{12,14},{14,12},{1,3},{3,1},... | collective-permute-start | bytes 589832 | tf_op jit(solution)/shard_map/ppermute | solution.py:239
  97.1 19.6 %collective-permute-start.23 = (bf16[128,1024]{1,0:T(8,128)(2,1)S(1)}, bf16[128,1024]{1,0:T(8,128)(2,1)}, u32[]{:S(2)}, u32[]{:S(2)}) collective-permute-start(bf16[128,1024]{1,0:T(8,128)(2,1)S(1)} %shard_map.134), channel_id=1, source_target_pairs={{0,12},{2,14},{4,0},{6,2},{8,4},{10,6},{12,8},{14,10},{1,13},{3,15... | collective-permute-start | bytes 786440 | tf_op jit(solution)/shard_map/ppermute | solution.py:242
  98.7 18.0 %collective-permute-start.24 = (bf16[128,1024]{1,0:T(8,128)(2,1)}, bf16[128,1024]{1,0:T(8,128)(2,1)}, u32[]{:S(2)}, u32[]{:S(2)}) collective-permute-start(bf16[128,1024]{1,0:T(8,128)(2,1)} %shard_map.135), channel_id=1, source_target_pairs={{0,8},{2,10},{4,12},{6,14},{8,0},{10,2},{12,4},{14,6},{1,9},{3,11}... | collective-permute-start | bytes 786440 | tf_op jit(solution)/shard_map/ppermute | solution.py:242
  103.5 18.5 %collective-permute-start.25 = (bf16[128,1024]{1,0:T(8,128)(2,1)}, bf16[128,1024]{1,0:T(8,128)(2,1)}, u32[]{:S(2)}, u32[]{:S(2)}) collective-permute-start(bf16[128,1024]{1,0:T(8,128)(2,1)} %shard_map.136), channel_id=1, source_target_pairs={{0,4},{2,6},{4,8},{6,10},{8,12},{10,14},{12,0},{14,2},{1,5},{3,7},... | collective-permute-start | bytes 786440 | tf_op jit(solution)/shard_map/ppermute | solution.py:242
  104.4 6.2 %copy-start.21 = (s32[128,4]{0,1:T(4,128)S(1)}, s32[128,4]{0,1:T(4,128)}, u32[]{:S(2)}) copy-start(s32[128,4]{0,1:T(4,128)} %param.8) | copy-start | bytes 6148
  107.7 0.7 copy-start.17
  108.4 0.7 copy-start.19
  109.1 6.3 %collective-permute-start.22 = (bf16[112,1024]{1,0:T(8,128)(2,1)}, bf16[112,1024]{1,0:T(8,128)(2,1)}, u32[]{:S(2)}, u32[]{:S(2)}) collective-permute-start(bf16[112,1024]{1,0:T(8,128)(2,1)} %get-tuple-element.145), channel_id=1, source_target_pairs={{0,2},{2,0},{4,6},{6,4},{8,10},{10,8},{12,14},{14,12},{1,3},{3,1},... | collective-permute-start | bytes 688136 | tf_op jit(solution)/shard_map/ppermute | solution.py:239
  109.3 12.7 %collective-permute-start.26 = (bf16[112,1024]{1,0:T(8,128)(2,1)}, bf16[112,1024]{1,0:T(8,128)(2,1)}, u32[]{:S(2)}, u32[]{:S(2)}) collective-permute-start(bf16[112,1024]{1,0:T(8,128)(2,1)} %get-tuple-element.156), channel_id=1, source_target_pairs={{0,2},{2,0},{4,6},{6,4},{8,10},{10,8},{12,14},{14,12},{1,3},{3,1},... | collective-permute-start | bytes 688136 | tf_op jit(solution)/shard_map/ppermute | solution.py:239
  116.6 10.7 %copy-start.20 = (bf16[112,1024]{1,0:T(8,128)(2,1)S(1)}, bf16[112,1024]{1,0:T(8,128)(2,1)}, u32[]{:S(2)}) copy-start(bf16[112,1024]{1,0:T(8,128)(2,1)} %copy-done.19) | copy-start | bytes 688132
  116.7 10.9 %copy-start.18 = (bf16[112,1024]{1,0:T(8,128)(2,1)S(1)}, bf16[112,1024]{1,0:T(8,128)(2,1)}, u32[]{:S(2)}) copy-start(bf16[112,1024]{1,0:T(8,128)(2,1)} %copy-done.17) | copy-start | bytes 688132
  123.2 27.7 %collective-permute-start.31 = (bf16[144,1024]{1,0:T(8,128)(2,1)S(1)}, bf16[144,1024]{1,0:T(8,128)(2,1)S(1)}, u32[]{:S(2)}, u32[]{:S(2)}) collective-permute-start(bf16[144,1024]{1,0:T(8,128)(2,1)S(1)} %shard_map.137), channel_id=1, source_target_pairs={{0,4},{2,6},{4,8},{6,10},{8,12},{10,14},{12,0},{14,2},{1,5},{3,7},... | collective-permute-start | bytes 884744 | tf_op jit(solution)/shard_map/ppermute | solution.py:242
  125.5 25.4 %collective-permute-start.30 = (bf16[144,1024]{1,0:T(8,128)(2,1)S(1)}, bf16[144,1024]{1,0:T(8,128)(2,1)S(1)}, u32[]{:S(2)}, u32[]{:S(2)}) collective-permute-start(bf16[144,1024]{1,0:T(8,128)(2,1)S(1)} %shard_map.133), channel_id=1, source_target_pairs={{0,8},{2,10},{4,12},{6,14},{8,0},{10,2},{12,4},{14,6},{1,9},{3,11}... | collective-permute-start | bytes 884744 | tf_op jit(solution)/shard_map/ppermute | solution.py:242
  127.3 5.8 %collective-permute-start.28 = (bf16[112,1024]{1,0:T(8,128)(2,1)S(1)}, bf16[112,1024]{1,0:T(8,128)(2,1)S(1)}, u32[]{:S(2)}, u32[]{:S(2)}) collective-permute-start(bf16[112,1024]{1,0:T(8,128)(2,1)S(1)} %copy-done.20), channel_id=1, source_target_pairs={{0,2},{2,0},{4,6},{6,4},{8,10},{10,8},{12,14},{14,12},{1,3},{3,1},... | collective-permute-start | bytes 688136 | tf_op jit(solution)/shard_map/ppermute | solution.py:239
  127.6 10.4 %collective-permute-start.27 = (bf16[112,1024]{1,0:T(8,128)(2,1)S(1)}, bf16[112,1024]{1,0:T(8,128)(2,1)S(1)}, u32[]{:S(2)}, u32[]{:S(2)}) collective-permute-start(bf16[112,1024]{1,0:T(8,128)(2,1)S(1)} %copy-done.18), channel_id=1, source_target_pairs={{0,2},{2,0},{4,6},{6,4},{8,10},{10,8},{12,14},{14,12},{1,3},{3,1},... | collective-permute-start | bytes 688136 | tf_op jit(solution)/shard_map/ppermute | solution.py:239
  133.1 5.7 %copy-start.8 = (bf16[896,1024]{1,0:T(8,128)(2,1)S(1)}, bf16[896,1024]{1,0:T(8,128)(2,1)}, u32[]{:S(2)}) copy-start(bf16[896,1024]{1,0:T(8,128)(2,1)} %copy-done.7) | copy-start | bytes 5505028
  133.9 5.0 %copy-start.6 = (bf16[896,1024]{1,0:T(8,128)(2,1)S(1)}, bf16[896,1024]{1,0:T(8,128)(2,1)}, u32[]{:S(2)}) copy-start(bf16[896,1024]{1,0:T(8,128)(2,1)} %copy-done.5) | copy-start | bytes 5505028
  133.9 18.2 %collective-permute-start.29 = (bf16[144,1024]{1,0:T(8,128)(2,1)S(1)}, bf16[144,1024]{1,0:T(8,128)(2,1)S(1)}, u32[]{:S(2)}, u32[]{:S(2)}) collective-permute-start(bf16[144,1024]{1,0:T(8,128)(2,1)S(1)} %shard_map.139), channel_id=1, source_target_pairs={{0,12},{2,14},{4,0},{6,2},{8,4},{10,6},{12,8},{14,10},{1,13},{3,15... | collective-permute-start | bytes 884744 | tf_op jit(solution)/shard_map/ppermute | solution.py:242
  138.8 1.1 copy-start.14
  143.3 3.4 %copy-start.1 = (bf16[896,1024]{1,0:T(8,128)(2,1)S(1)}, bf16[896,1024]{1,0:T(8,128)(2,1)}, u32[]{:S(2)}) copy-start(bf16[896,1024]{1,0:T(8,128)(2,1)} %copy-done) | copy-start | bytes 5505028
  143.4 3.4 %copy-start.10 = (bf16[896,1024]{1,0:T(8,128)(2,1)S(1)}, bf16[896,1024]{1,0:T(8,128)(2,1)}, u32[]{:S(2)}) copy-start(bf16[896,1024]{1,0:T(8,128)(2,1)} %copy-done.9) | copy-start | bytes 5505028
  146.8 1.1 copy-start.16
  152.2 2.3 %collective-permute-start.32 = (f32[128,4]{0,1:T(4,128)S(1)}, f32[128,4]{0,1:T(4,128)S(1)}, u32[]{:S(2)}, u32[]{:S(2)}) collective-permute-start(f32[128,4]{0,1:T(4,128)S(1)} %select_reduce_fusion), channel_id=1, source_target_pairs={{0,1},{1,0},{2,3},{3,2},{4,5},{5,4},{6,7},{7,6},{8,9},{9,8},{10,11... | collective-permute-start | bytes 6152 | tf_op jit(solution)/shard_map/ppermute | solution.py:248

commit v8 on v7

--- a/solution.py
+++ b/solution.py
@@ -286,36 +286,35 @@
     (first_packed,) = local_call(
         grad_pack_kernel, (shape_of((padded, half_width)),), (info, grad_out, places[0]))
     grad_first = over_pair(first_packed)
-    soon = {k: compact[k] for k in [0] + by_reach[:1]}
+    soon = {k: compact[k] for k in [0] + by_reach[:-1]}
     held_grad, blocks, early, soon, grad_first = settle((grad_out, blocks, early, soon, grad_first))
     compact.update(soon)
     grad_blocks = {0: held_grad}
     for k in by_reach:
         grad_blocks[k] = over_line(held_grad, k)
 
-    grad_packed = {
-        k: local_call(
+    def grad_pack(k):
+        return local_call(
             grad_pack_kernel, (shape_of((padded, half_width)),), (info, grad_blocks[k], places[k]))[0]
-        for k in by_reach
-    }
-    grad_compact = {k: over_pair(grad_packed[k]) for k in by_reach}
+
+    near, far = by_reach[:-1], by_reach[-1]
+    grad_packed = {k: grad_pack(k) for k in near}
+    grad_compact = {k: over_pair(grad_packed[k]) for k in near}
     grad_compact[0] = grad_first
-    ahead = {k: grad_compact[k] for k in by_reach[:1]}
-    compact, grad_blocks, grad_packed, ahead = settle((compact, grad_blocks, grad_packed, ahead))
-    grad_compact.update(ahead)
+    compact, near_blocks, near_packed = settle(
+        (compact, {k: grad_blocks[k] for k in near}, {k: grad_packed[k] for k in near}))
+    grad_blocks.update(near_blocks)
     rows, weights = local_call(
         functools.partial(token_rows_kernel, *sizes),
         (half_rows, shape_of((row_count, 1), F32)),
         (info, *[blocks[k] for k in every], *[compact[k] for k in every], *[own_parts[k] for k in every]))
     rows_other = over_core(rows)
-    ahead = {k: grad_compact[k] for k in by_reach[1:-1]}
-    rows_other, ahead = settle((rows_other, ahead))
-    grad_compact.update(ahead)
     gate, upward, scaled, sent = local_call(
         functools.partial(forward_kernel, pieces, chunk),
         (shape_of(hidden_rows, F32), shape_of(hidden_rows, F32), shape_of(hidden_rows), half_rows),
         (info, rows, rows_other, weights, gate_local, up_local, down_local))
-    sent, grad_compact = settle((sent, grad_compact))
+    sent, grad_compact, grad_blocks = settle((sent, grad_compact, grad_blocks))
+    grad_compact[far] = over_pair(grad_pack(far))
     out_dense, *out_packed = local_call(
         functools.partial(join_kernel, *sizes, True),
         (shape_of((lines, token_count, half_width), F32),
@@ -323,7 +322,7 @@
         (info, over_core(sent), scaled, down_local))
 
     outward = by_reach[::-1]
-    out_back = {k: over_pair(out_packed[k]) for k in every}
+    out_back = {k: over_pair(out_packed[k]) for k in near}
     (grad_rows,) = local_call(
         functools.partial(grad_rows_kernel, *sizes), (half_rows,),
         (info, *[grad_blocks[k] for k in every], *[grad_compact[k] for k in every]))
@@ -348,17 +347,30 @@
             total = total + blocks[k][:token_count].astype(F32)
         return total.astype(BF)
 
-    sent, some = settle((sent, {k: out_back[k] for k in by_reach}))
-    out_back.update(some)
-    out_home = {k: to_home(k, out_dense, out_back) for k in by_reach + [0]}
+    sent, out_back = settle((sent, out_back))
+    out_home = {k: to_home(k, out_dense, out_back) for k in near}
+    last, first_home = settle((out_packed[far], out_home[near[0]]))
+    out_back[far] = over_pair(last)
+    out_home[near[0]] = first_home
+    last, out_back[far] = settle((out_packed[0], out_back[far]))
+    out_back[0] = over_pair(last)
+    for k in (far, 0):
+        out_home[k] = to_home(k, out_dense, out_back)
+
+    def whole(own, other):
+        return jnp.concatenate(
+            [jnp.where(core == 0, own, other), jnp.where(core == 0, other, own)], axis=1)
+
+    came = over_core(sent)
     out_came = {k: over_line(out_home[k], lines - k) for k in by_reach}
     out_came[0] = out_home[0]
     in_dense, *in_packed = local_call(
         functools.partial(join_kernel, *sizes, False),
         (shape_of((lines, token_count, half_width), F32),
          *[shape_of((padded + TAIL, half_width)) for _ in every]),
-        (info, over_core(sent), grad_gate, grad_up, gate_local, up_local, compact_tails))
-    in_packed, out_came[0] = settle((in_packed, out_came[0]))
+        (info, came, grad_gate, grad_up, gate_local, up_local, compact_tails))
+    in_packed, ahead = settle((in_packed, {k: out_came[k] for k in near}))
+    out_came.update(ahead)
     in_back, in_home, sequence = {}, {}, outward + [0]
     for i, k in enumerate(sequence):
         packed = in_packed[k]
@@ -366,21 +378,19 @@
             packed, _ = settle((packed, in_home[sequence[i - 2]]))
         in_back[k] = over_pair(packed)
         in_home[k] = to_home(k, in_dense, in_back, dense_tails)
-    in_home[sequence[0]], out_came = settle((in_home[sequence[0]], out_came))
+    ready, out_came = settle(({k: in_home[k] for k in sequence[:2]}, out_came))
+    in_home.update(ready)
     layer_out = summed(out_came)
-    last_home, rows, rows_other, grad_rows, grad_other, scaled, grad_gate, grad_up = settle(
-        ([in_home[k] for k in outward], rows, rows_other, grad_rows, grad_other, scaled, grad_gate, grad_up))
+    rows, rows_other, grad_rows, _ = settle((rows, rows_other, grad_rows, in_packed))
+    rows = whole(rows, rows_other)
+    gate_grad = dot(rows, grad_gate, FIRST).astype(BF)
+    down_grad = dot(scaled, whole(grad_rows, grad_other), FIRST).astype(BF)
+    in_home[sequence[0]], gate_grad = settle((in_home[sequence[0]], gate_grad))
+    in_home[sequence[1]], down_grad = settle((in_home[sequence[1]], down_grad))
+    last_home, rows, grad_up = settle(([in_home[k] for k in outward], rows, grad_up))
     in_home = {k: over_line(in_home[k], lines - k) if k else in_home[0] for k in every}
     input_grad = summed(in_home)
 
-    def whole(own, other):
-        return jnp.concatenate(
-            [jnp.where(core == 0, own, other), jnp.where(core == 0, other, own)], axis=1)
-
-    rows = whole(rows, rows_other)
-    grads = whole(grad_rows, grad_other)
-    down_grad = dot(scaled, grads, FIRST).astype(BF)
-    gate_grad = dot(rows, grad_gate, FIRST).astype(BF)
     up_grad = dot(rows, grad_up, FIRST).astype(BF)
 
     held = []

time: 156 us -> 151 us (0.968)
  waiting for transfers between devices: 65.7 us -> 48.4 us
  starting transfers between devices: 35.7 us -> 48.2 us
  Pallas kernels: 32.6 us -> 35 us
  local copies, waits for them, and re-layouts: 4.1 us -> 2.35 us
    ppermute x16, waiting for transfers between devices: 21.9 us -> 10.3 us  [over_pair(): lax.ppermute(x, 'expert', [(i, i + 1 - 2 * (i % 2)) for i in range(expert...]
    ppermute x12, starting transfers between devices: 13.1 us -> 23.3 us  [over_line(): lax.ppermute(x, 'expert', [(i, (i // 2 + k) % lines * 2 + i % 2) for i in...]
    ppermute x12, waiting for transfers between devices: 40.4 us -> 34.2 us  [over_line(): lax.ppermute(x, 'expert', [(i, (i // 2 + k) % lines * 2 + i % 2) for i in...]
    pallas_call x22, Pallas kernels: 32.6 us -> 35 us  [local_call(): pl.pallas_call(kernel, out_shape=tuple(outs), in_specs=[SMEM_SPEC] + [VME...]
    ppermute x5, starting transfers between devices: 7.62 us -> 9.72 us  [over_core(): return lax.ppermute(x, 'tensor', [(0, 1), (1, 0)])]
    unnamed x45 -> x53, local copies, waits for them, and re-layouts: 4.09 us -> 2.34 us
  transfers between devices with their start and end apart: 33 -> 33, of which waited for: 15 -> 13; matrix products, arithmetic and copies ran while one was open for 9% -> 9% of each run, Pallas kernels for 19% -> 21%
where the time goes in v8:
time: 151 us
  waiting for transfers between devices  48.4 us (32%)
  starting transfers between devices  48.2 us (32%)
  Pallas kernels  35 us (23%)
  matrix products  9.92 us (7%)
  other arithmetic  6.13 us (4%)
  local copies, waits for them, and re-layouts  2.35 us (2%)
    pallas_call x22, Pallas kernels, local_call(): pl.pallas_call(kernel, out_shape=tuple(outs), in_specs=[SMEM_SPEC] + [VME...  35 us
    ppermute x12, waiting for transfers between devices, over_line(): lax.ppermute(x, 'expert', [(i, (i // 2 + k) % lines * 2 + i % 2) for i in...  34.2 us
    ppermute x12, starting transfers between devices, over_line(): lax.ppermute(x, 'expert', [(i, (i // 2 + k) % lines * 2 + i % 2) for i in...  23.3 us
    ppermute x16, starting transfers between devices, over_pair(): lax.ppermute(x, 'expert', [(i, i + 1 - 2 * (i % 2)) for i in range(expert...  15.1 us
    ppermute x16, waiting for transfers between devices, over_pair(): lax.ppermute(x, 'expert', [(i, i + 1 - 2 * (i % 2)) for i in range(expert...  10.3 us
    dot_general x3, matrix products, dot(): lax.dot_general(a, b, (contract, ((), ())), preferred_element_type=F32)  9.92 us
    ppermute x5, starting transfers between devices, over_core(): return lax.ppermute(x, 'tensor', [(0, 1), (1, 0)])  9.72 us
    ppermute x5, waiting for transfers between devices, over_core(): return lax.ppermute(x, 'tensor', [(0, 1), (1, 0)])  3.89 us
  transfers between devices with their start and end apart: 33, of which 13 were waited for; matrix products, arithmetic and copies ran while one was open for 9% of the time, Pallas kernels for 21%

profile of v8, /device:TPU:9, one launch (start us, length us, event | category | flops | bytes accessed | tf_op | source)
XLA Modules:
  0.0 151.1 jit_solution(7192068494391891614)
XLA Ops:
  1.4 1.0 pad_maximum_fusion.1.block.refs_0_
  2.4 1.5 collective-permute-start
  3.9 4.1 %collective-permute-start.1 = (bf16[144,1024]{1,0:T(8,128)(2,1)S(1)}, bf16[144,1024]{1,0:T(8,128)(2,1)S(1)}, u32[]{:S(2)}, u32[]{:S(2)}) collective-permute-start(bf16[144,1024]{1,0:T(8,128)(2,1)S(1)} %pad_maximum_fusion.1.block.refs_0_), channel_id=1, source_target_pairs={{0,8},{2,10},{4,12},{6,14},{8,0},{10,2},{12,4},{14,6},{1,9},{3,11}... | collective-permute-start | bytes 884744 | tf_op jit(solution)/shard_map/ppermute | solution.py:242
  8.1 0.9 shard_map.118
  9.0 1.3 collective-permute-start.3
  10.3 0.9 shard_map.120
  11.2 1.3 collective-permute-start.5
  12.5 6.2 %collective-permute-done.block.refs_1_ = bf16[144,1024]{1,0:T(8,128)(2,1)S(1)} collective-permute-done((bf16[144,1024]{1,0:T(8,128)(2,1)S(1)}, bf16[144,1024]{1,0:T(8,128)(2,1)S(1)}, u32[]{:S(2)}, u32[]{:S(2)}) %collective-permute-start) | collective-permute-done | bytes 294944 | tf_op jit(solution)/shard_map/ppermute | solution.py:242
  18.7 0.9 shard_map.119
  19.6 1.3 collective-permute-start.4
  20.9 1.3 shard_map.121
  22.5 4.3 %collective-permute-done.6.refs_4_ = bf16[96,1024]{1,0:T(8,128)(2,1)S(1)} collective-permute-done((bf16[96,1024]{1,0:T(8,128)(2,1)S(1)}, bf16[96,1024]{1,0:T(8,128)(2,1)S(1)}, u32[]{:S(2)}, u32[]{:S(2)}) %collective-permute-start.6) | collective-permute-done | bytes 196640 | tf_op jit(solution)/shard_map/ppermute | solution.py:239
  26.8 1.4 collective-permute-done.1.block.refs_2_
  28.2 2.2 %collective-permute-start.9 = (bf16[128,1024]{1,0:T(8,128)(2,1)}, bf16[128,1024]{1,0:T(8,128)(2,1)S(1)}, u32[]{:S(2)}, u32[]{:S(2)}) collective-permute-start(bf16[128,1024]{1,0:T(8,128)(2,1)} %refs_0_), channel_id=1, source_target_pairs={{0,12},{2,14},{4,0},{6,2},{8,4},{10,6},{12,8},{14,10},{1,13},{3,15... | collective-permute-start | bytes 786440 | tf_op jit(solution)/shard_map/ppermute | solution.py:242
  30.5 0.9 shard_map.122
  31.4 1.3 collective-permute-start.7
  32.7 1.4 collective-permute-done.9.block.refs_3_
  34.1 0.7 shard_map.124
  34.8 7.3 %collective-permute-done.8.block.refs_1_ = bf16[128,1024]{1,0:T(8,128)(2,1)S(1)} collective-permute-done((bf16[128,1024]{1,0:T(8,128)(2,1)}, bf16[128,1024]{1,0:T(8,128)(2,1)S(1)}, u32[]{:S(2)}, u32[]{:S(2)}) %collective-permute-start.8) | collective-permute-done | bytes 262176 | tf_op jit(solution)/shard_map/ppermute | solution.py:242
  42.1 0.7 shard_map.123
  42.9 0.8 shard_map.125
  43.7 5.9 %collective-permute-start.10 = (bf16[896,1024]{1,0:T(8,128)(2,1)S(1)}, bf16[896,1024]{1,0:T(8,128)(2,1)S(1)}, u32[]{:S(2)}, u32[]{:S(2)}) collective-permute-start(bf16[896,1024]{1,0:T(8,128)(2,1)S(1)} %get-tuple-element.174.own), channel_id=1, source_target_pairs={{0,1},{1,0},{2,3},{3,2},{4,5},{5,4},{6,7},{7,6},{8,9},{9,8},{10,11... | collective-permute-start | bytes 5505032 | tf_op jit(solution)/shard_map/ppermute | solution.py:248
  49.6 1.2 collective-permute-start.12
  51.1 1.9 %collective-permute-done.10.other = bf16[896,1024]{1,0:T(8,128)(2,1)S(1)} collective-permute-done((bf16[896,1024]{1,0:T(8,128)(2,1)S(1)}, bf16[896,1024]{1,0:T(8,128)(2,1)S(1)}, u32[]{:S(2)}, u32[]{:S(2)}) %collective-permute-start.10) | collective-permute-done | bytes 1835040 | tf_op jit(solution)/shard_map/ppermute | solution.py:248
  53.0 5.7 %shard_map.126 = (f32[896,384]{1,0:T(8,128)S(1)}, f32[896,384]{1,0:T(8,128)S(1)}, bf16[896,384]{1,0:T(8,128)(2,1)S(1)}, bf16[896,1024]{1,0:T(8,128)(2,1)S(1)}) custom-call(s32[3]{0:T(128)S(1)} %pad_add_fusion.info, bf16[896,1024]{1,0:T(8,128)(2,1)S(1)} %get-tuple-element.174.own, bf16[896,1024]{1,0:T(8,128)(2,1)S(1)} %collective-permute-done.10.other, ...), custom_call_target="tpu_custom_call" | custom-call | flops 1000 | bytes 1000 | tf_op jit(solution)/shard_map/pallas_call | solution.py:41
  58.7 2.7 %collective-permute-done.13.block.refs_2_ = bf16[128,1024]{1,0:T(8,128)(2,1)S(1)} collective-permute-done((bf16[128,1024]{1,0:T(8,128)(2,1)}, bf16[128,1024]{1,0:T(8,128)(2,1)S(1)}, u32[]{:S(2)}, u32[]{:S(2)}) %collective-permute-start.13) | collective-permute-done | bytes 262176 | tf_op jit(solution)/shard_map/ppermute | solution.py:242
  62.8 1.3 collective-permute-start.14
  64.1 5.3 %collective-permute-done.14.refs_6_ = bf16[96,1024]{1,0:T(8,128)(2,1)S(1)} collective-permute-done((bf16[96,1024]{1,0:T(8,128)(2,1)S(1)}, bf16[96,1024]{1,0:T(8,128)(2,1)S(1)}, u32[]{:S(2)}, u32[]{:S(2)}) %collective-permute-start.14) | collective-permute-done | bytes 196640 | tf_op jit(solution)/shard_map/ppermute | solution.py:239
  69.4 1.1 shard_map.128.own
  70.5 1.8 %shard_map.129 = (f32[4,128,1024]{2,1,0:T(8,128)S(1)}, bf16[96,1024]{1,0:T(8,128)(2,1)S(1)}, bf16[96,1024]{1,0:T(8,128)(2,1)S(1)}, bf16[96,1024]{1,0:T(8,128)(2,1)}, bf16[96,1024]{1,0:T(8,128)(2,1)S(1)}) custom-call(s32[3]{0:T(128)S(1)} %pad_add_fusion.info, bf16[896,1024]{1,0:T(8,128)(2,1)S(1)} %collective-permute-done.15.came, ...), custom_call_target="tpu_custom_call" | custom-call | flops 1000 | bytes 1000 | tf_op jit(solution)/shard_map/pallas_call | solution.py:41
  72.3 0.8 collective-permute-start.16
  73.1 1.2 collective-permute-start.17
  74.6 1.9 %collective-permute-done.16.other = bf16[896,1024]{1,0:T(8,128)(2,1)S(1)} collective-permute-done((bf16[896,1024]{1,0:T(8,128)(2,1)S(1)}, bf16[896,1024]{1,0:T(8,128)(2,1)S(1)}, u32[]{:S(2)}, u32[]{:S(2)}) %collective-permute-start.16) | collective-permute-done | bytes 1835040 | tf_op jit(solution)/shard_map/ppermute | solution.py:248
  76.5 6.6 %shard_map.130 = (bf16[896,384]{1,0:T(8,128)(2,1)S(1)}, bf16[896,384]{1,0:T(8,128)(2,1)S(1)}, bf16[896,1024]{1,0:T(8,128)(2,1)}, f32[4,16,128]{2,1,0:T(8,128)S(1)}, f32[4,16,128]{2,1,0:T(8,128)S(1)}) custom-call(s32[3]{0:T(128)S(1)} %pad_add_fusion.info, bf16[896,1024]{1,0:T(8,128)(2,1)S(1)} %shard_map.128.own, ...), custom_call_target="tpu_custom_call" | custom-call | flops 1000 | bytes 1000 | tf_op jit(solution)/shard_map/pallas_call | solution.py:41
  83.8 0.8 collective-permute-start.19
  84.7 1.5 shard_map.132
  86.2 1.2 collective-permute-start.24
  87.4 1.5 shard_map.133
  88.9 2.4 %collective-permute-start.21 = (bf16[128,1024]{1,0:T(8,128)(2,1)}, bf16[128,1024]{1,0:T(8,128)(2,1)}, u32[]{:S(2)}, u32[]{:S(2)}) collective-permute-start(bf16[128,1024]{1,0:T(8,128)(2,1)} %shard_map.133), channel_id=1, source_target_pairs={{0,4},{2,6},{4,8},{6,10},{8,12},{10,14},{12,0},{14,2},{1,5},{3,7},... | collective-permute-start | bytes 786440 | tf_op jit(solution)/shard_map/ppermute | solution.py:242
  91.2 1.8 %collective-permute-start.20 = (bf16[128,1024]{1,0:T(8,128)(2,1)}, bf16[128,1024]{1,0:T(8,128)(2,1)}, u32[]{:S(2)}, u32[]{:S(2)}) collective-permute-start(bf16[128,1024]{1,0:T(8,128)(2,1)} %shard_map.132), channel_id=1, source_target_pairs={{0,12},{2,14},{4,0},{6,2},{8,4},{10,6},{12,8},{14,10},{1,13},{3,15... | collective-permute-start | bytes 786440 | tf_op jit(solution)/shard_map/ppermute | solution.py:242
  93.1 1.2 collective-permute-start.25
  95.0 1.3 shard_map.137
  96.3 3.1 %collective-permute-start.26 = (bf16[128,1024]{1,0:T(8,128)(2,1)S(1)}, bf16[128,1024]{1,0:T(8,128)(2,1)S(1)}, u32[]{:S(2)}, u32[]{:S(2)}) collective-permute-start(bf16[128,1024]{1,0:T(8,128)(2,1)S(1)} %shard_map.137), channel_id=1, source_target_pairs={{0,8},{2,10},{4,12},{6,14},{8,0},{10,2},{12,4},{14,6},{1,9},{3,11}... | collective-permute-start | bytes 786440 | tf_op jit(solution)/shard_map/ppermute | solution.py:242
  99.4 0.8 shard_map.136
  100.2 3.8 %shard_map.131 = (f32[4,128,1024]{2,1,0:T(8,128)S(1)}, bf16[112,1024]{1,0:T(8,128)(2,1)S(1)}, bf16[112,1024]{1,0:T(8,128)(2,1)S(1)}, bf16[112,1024]{1,0:T(8,128)(2,1)S(1)}, bf16[112,1024]{1,0:T(8,128)(2,1)S(1)}) custom-call(s32[3]{0:T(128)S(1)} %pad_add_fusion.info, bf16[896,1024]{1,0:T(8,128)(2,1)} %collective-permute-done.19.came, ...), custom_call_target="tpu_custom_call" | custom-call | flops 1000 | bytes 1000 | tf_op jit(solution)/shard_map/pallas_call | solution.py:41
  104.0 0.8 collective-permute-done.20
  105.1 1.2 collective-permute-start.23
  107.2 0.9 copy-done.14
  108.0 3.0 %fusion.4 = bf16[384,2048]{1,0:T(8,128)(2,1)} fusion(bf16[896,384]{1,0:T(8,128)(2,1)S(1)} %copy-done.14, bf16[896,1024]{1,0:T(8,128)(2,1)S(1)} %get-tuple-element.195, bf16[896,1024]{1,0:T(8,128)(2,1)S(1)} %get-tuple-element.194), kind=kOutput, calls=%fused_computation.5 | convolution fusion | flops 1417412608 | bytes 5931008 | tf_op jit(solution)/shard_map/dot_general | solution.py:24
  111.0 3.5 %convolution_convert_fusion.1 = bf16[2048,384]{1,0:T(8,128)(2,1)} fusion(bf16[896,384]{1,0:T(8,128)(2,1)S(1)} %get-tuple-element.143.refs_0_, bf16[896,1024]{1,0:T(8,128)(2,1)S(1)} %get-tuple-element.193, bf16[896,1024]{1,0:T(8,128)(2,1)S(1)} %get-tuple-element.192), kind=kOutput, calls=%fused_computation.7 | convolution fusion | flops 1417412608 | bytes 5931008 | tf_op jit(solution)/shard_map/dot_general | solution.py:24
  115.2 0.8 shard_map.134
  116.3 0.8 shard_map.135
  117.1 1.3 collective-permute-start.27
  118.4 2.7 %collective-permute-start.31 = (bf16[144,1024]{1,0:T(8,128)(2,1)S(1)}, bf16[144,1024]{1,0:T(8,128)(2,1)S(1)}, u32[]{:S(2)}, u32[]{:S(2)}) collective-permute-start(bf16[144,1024]{1,0:T(8,128)(2,1)S(1)} %shard_map.135), channel_id=1, source_target_pairs={{0,4},{2,6},{4,8},{6,10},{8,12},{10,14},{12,0},{14,2},{1,5},{3,7},... | collective-permute-start | bytes 884744 | tf_op jit(solution)/shard_map/ppermute | solution.py:242
  121.1 2.3 %collective-permute-start.30 = (bf16[144,1024]{1,0:T(8,128)(2,1)S(1)}, bf16[144,1024]{1,0:T(8,128)(2,1)S(1)}, u32[]{:S(2)}, u32[]{:S(2)}) collective-permute-start(bf16[144,1024]{1,0:T(8,128)(2,1)S(1)} %shard_map.134), channel_id=1, source_target_pairs={{0,8},{2,10},{4,12},{6,14},{8,0},{10,2},{12,4},{14,6},{1,9},{3,11}... | collective-permute-start | bytes 884744 | tf_op jit(solution)/shard_map/ppermute | solution.py:242
  123.4 1.9 %add_convert_fusion.1 = bf16[128,1024]{1,0:T(8,128)(2,1)} fusion(bf16[128,1024]{1,0:T(8,128)(2,1)} %collective-permute-done.21, bf16[128,1024]{1,0:T(8,128)(2,1)S(1)} %collective-permute-done.26, bf16[128,1024]{1,0:T(8,128)(2,1)} %collective-permute-done.20, bf16[128,1024]{1,0:T(8,128)(2,1)S(1)} %shard_map.136), kind=kLoop, calls=%fused_computation.14 | loop fusion | flops 1048576 | bytes 1310720 | tf_op jit(solution)/shard_map/convert_element_type | solution.py:348
  125.3 0.8 shard_map.138
  126.1 0.8 shard_map.139
  126.9 3.2 %collective-permute-start.29 = (bf16[144,1024]{1,0:T(8,128)(2,1)S(1)}, bf16[144,1024]{1,0:T(8,128)(2,1)S(1)}, u32[]{:S(2)}, u32[]{:S(2)}) collective-permute-start(bf16[144,1024]{1,0:T(8,128)(2,1)S(1)} %shard_map.139), channel_id=1, source_target_pairs={{0,12},{2,14},{4,0},{6,2},{8,4},{10,6},{12,8},{14,10},{1,13},{3,15... | collective-permute-start | bytes 884744 | tf_op jit(solution)/shard_map/ppermute | solution.py:242
  130.1 3.5 %fusion.7 = bf16[1,2048,384]{2,1,0:T(8,128)(2,1)} fusion(bf16[896,2048]{1,0:T(8,128)(2,1)S(1)} %pad_maximum_fusion, bf16[896,384]{1,0:T(8,128)(2,1)S(1)} %get-tuple-element.182.refs_1_), kind=kOutput, calls=%fused_computation.8 | convolution fusion | flops 1410072576 | bytes 5931008 | tf_op jit(solution)/shard_map/dot_general | solution.py:24
  133.6 10.1 %collective-permute-done.30 = bf16[144,1024]{1,0:T(8,128)(2,1)S(1)} collective-permute-done((bf16[144,1024]{1,0:T(8,128)(2,1)S(1)}, bf16[144,1024]{1,0:T(8,128)(2,1)S(1)}, u32[]{:S(2)}, u32[]{:S(2)}) %collective-permute-start.30) | collective-permute-done | bytes 294944 | tf_op jit(solution)/shard_map/ppermute | solution.py:242
  143.8 4.2 %collective-permute-done.29 = bf16[144,1024]{1,0:T(8,128)(2,1)S(1)} collective-permute-done((bf16[144,1024]{1,0:T(8,128)(2,1)S(1)}, bf16[144,1024]{1,0:T(8,128)(2,1)S(1)}, u32[]{:S(2)}, u32[]{:S(2)}) %collective-permute-start.29) | collective-permute-done | bytes 294944 | tf_op jit(solution)/shard_map/ppermute | solution.py:242
  148.1 1.5 %collective-permute-start.32 = (f32[128,4]{0,1:T(4,128)S(1)}, f32[128,4]{0,1:T(4,128)S(1)}, u32[]{:S(2)}, u32[]{:S(2)}) collective-permute-start(f32[128,4]{0,1:T(4,128)S(1)} %select_reduce_fusion), channel_id=1, source_target_pairs={{0,1},{1,0},{2,3},{3,2},{4,5},{5,4},{6,7},{7,6},{8,9},{9,8},{10,11... | collective-permute-start | bytes 6152 | tf_op jit(solution)/shard_map/ppermute | solution.py:248
  149.6 0.9 add_convert_fusion
  (107 shorter events, 7.5 us)
Async XLA Ops:
  2.4 7.9 %collective-permute-start.2 = (bf16[144,1024]{1,0:T(8,128)(2,1)S(1)}, bf16[144,1024]{1,0:T(8,128)(2,1)S(1)}, u32[]{:S(2)}, u32[]{:S(2)}) collective-permute-start(bf16[144,1024]{1,0:T(8,128)(2,1)S(1)} %pad_maximum_fusion.1.block.refs_0_), channel_id=1, source_target_pairs={{0,12},{2,14},{4,0},{6,2},{8,4},{10,6},{12,8},{14,10},{1,13},{3,15... | collective-permute-start | bytes 884744 | tf_op jit(solution)/shard_map/ppermute | solution.py:242
  2.4 16.3 %collective-permute-start = (bf16[144,1024]{1,0:T(8,128)(2,1)S(1)}, bf16[144,1024]{1,0:T(8,128)(2,1)S(1)}, u32[]{:S(2)}, u32[]{:S(2)}) collective-permute-start(bf16[144,1024]{1,0:T(8,128)(2,1)S(1)} %pad_maximum_fusion.1.block.refs_0_), channel_id=1, source_target_pairs={{0,4},{2,6},{4,8},{6,10},{8,12},{10,14},{12,0},{14,2},{1,5},{3,7},... | collective-permute-start | bytes 884744 | tf_op jit(solution)/shard_map/ppermute | solution.py:242
  3.9 24.3 %collective-permute-start.1 = (bf16[144,1024]{1,0:T(8,128)(2,1)S(1)}, bf16[144,1024]{1,0:T(8,128)(2,1)S(1)}, u32[]{:S(2)}, u32[]{:S(2)}) collective-permute-start(bf16[144,1024]{1,0:T(8,128)(2,1)S(1)} %pad_maximum_fusion.1.block.refs_0_), channel_id=1, source_target_pairs={{0,8},{2,10},{4,12},{6,14},{8,0},{10,2},{12,4},{14,6},{1,9},{3,11}... | collective-permute-start | bytes 884744 | tf_op jit(solution)/shard_map/ppermute | solution.py:242
  8.1 44.9 %copy-start.5 = (bf16[1,2048,384]{2,1,0:T(8,128)(2,1)S(1)}, bf16[1,2048,384]{2,1,0:T(8,128)(2,1)}, u32[]{:S(2)}) copy-start(bf16[1,2048,384]{2,1,0:T(8,128)(2,1)} %param.11) | copy-start | bytes 4718596
  9.0 17.9 %collective-permute-start.3 = (bf16[112,1024]{1,0:T(8,128)(2,1)S(1)}, bf16[112,1024]{1,0:T(8,128)(2,1)S(1)}, u32[]{:S(2)}, u32[]{:S(2)}) collective-permute-start(bf16[112,1024]{1,0:T(8,128)(2,1)S(1)} %get-tuple-element.95), channel_id=1, source_target_pairs={{0,2},{2,0},{4,6},{6,4},{8,10},{10,8},{12,14},{14,12},{1,3},{3,1},... | collective-permute-start | bytes 688136 | tf_op jit(solution)/shard_map/ppermute | solution.py:239
  11.2 76.2 %copy-start.17 = (bf16[96,128]{1,0:T(8,128)(2,1)}, bf16[96,128]{1,0:T(8,128)(2,1)S(1)}, u32[]{:S(2)}) copy-start(bf16[96,128]{1,0:T(8,128)(2,1)S(1)} %get-tuple-element.109.place) | copy-start | bytes 73732
  11.2 17.0 %collective-permute-start.5 = (bf16[112,1024]{1,0:T(8,128)(2,1)S(1)}, bf16[112,1024]{1,0:T(8,128)(2,1)S(1)}, u32[]{:S(2)}, u32[]{:S(2)}) collective-permute-start(bf16[112,1024]{1,0:T(8,128)(2,1)S(1)} %get-tuple-element.97), channel_id=1, source_target_pairs={{0,2},{2,0},{4,6},{6,4},{8,10},{10,8},{12,14},{14,12},{1,3},{3,1},... | collective-permute-start | bytes 688136 | tf_op jit(solution)/shard_map/ppermute | solution.py:239
  19.6 65.0 %copy-start.15 = (bf16[96,128]{1,0:T(8,128)(2,1)}, bf16[96,128]{1,0:T(8,128)(2,1)S(1)}, u32[]{:S(2)}) copy-start(bf16[96,128]{1,0:T(8,128)(2,1)S(1)} %get-tuple-element.108.place) | copy-start | bytes 73732
  19.6 8.6 %collective-permute-start.4 = (bf16[112,1024]{1,0:T(8,128)(2,1)S(1)}, bf16[112,1024]{1,0:T(8,128)(2,1)S(1)}, u32[]{:S(2)}, u32[]{:S(2)}) collective-permute-start(bf16[112,1024]{1,0:T(8,128)(2,1)S(1)} %get-tuple-element.96), channel_id=1, source_target_pairs={{0,2},{2,0},{4,6},{6,4},{8,10},{10,8},{12,14},{14,12},{1,3},{3,1},... | collective-permute-start | bytes 688136 | tf_op jit(solution)/shard_map/ppermute | solution.py:239
  20.9 32.1 %copy-start.2 = (bf16[1,384,2048]{2,1,0:T(8,128)(2,1)S(1)}, bf16[1,384,2048]{2,1,0:T(8,128)(2,1)}, u32[]{:S(2)}) copy-start(bf16[1,384,2048]{2,1,0:T(8,128)(2,1)} %param.12) | copy-start | bytes 4718596
  20.9 32.1 %copy-start.3 = (bf16[1,2048,384]{2,1,0:T(8,128)(2,1)S(1)}, bf16[1,2048,384]{2,1,0:T(8,128)(2,1)}, u32[]{:S(2)}) copy-start(bf16[1,2048,384]{2,1,0:T(8,128)(2,1)} %param.10) | copy-start | bytes 4718596
  22.3 4.6 %collective-permute-start.6 = (bf16[96,1024]{1,0:T(8,128)(2,1)S(1)}, bf16[96,1024]{1,0:T(8,128)(2,1)S(1)}, u32[]{:S(2)}, u32[]{:S(2)}) collective-permute-start(bf16[96,1024]{1,0:T(8,128)(2,1)S(1)} %shard_map.121), channel_id=1, source_target_pairs={{0,2},{2,0},{4,6},{6,4},{8,10},{10,8},{12,14},{14,12},{1,3},{3,1},... | collective-permute-start | bytes 589832 | tf_op jit(solution)/shard_map/ppermute | solution.py:239
  28.2 5.9 %collective-permute-start.9 = (bf16[128,1024]{1,0:T(8,128)(2,1)}, bf16[128,1024]{1,0:T(8,128)(2,1)S(1)}, u32[]{:S(2)}, u32[]{:S(2)}) collective-permute-start(bf16[128,1024]{1,0:T(8,128)(2,1)} %refs_0_), channel_id=1, source_target_pairs={{0,12},{2,14},{4,0},{6,2},{8,4},{10,6},{12,8},{14,10},{1,13},{3,15... | collective-permute-start | bytes 786440 | tf_op jit(solution)/shard_map/ppermute | solution.py:242
  30.5 11.7 %collective-permute-start.8 = (bf16[128,1024]{1,0:T(8,128)(2,1)}, bf16[128,1024]{1,0:T(8,128)(2,1)S(1)}, u32[]{:S(2)}, u32[]{:S(2)}) collective-permute-start(bf16[128,1024]{1,0:T(8,128)(2,1)} %refs_0_), channel_id=1, source_target_pairs={{0,4},{2,6},{4,8},{6,10},{8,12},{10,14},{12,0},{14,2},{1,5},{3,7},... | collective-permute-start | bytes 786440 | tf_op jit(solution)/shard_map/ppermute | solution.py:242
  31.3 30.7 %copy-start.19 = (bf16[96,128]{1,0:T(8,128)(2,1)}, bf16[96,128]{1,0:T(8,128)(2,1)S(1)}, u32[]{:S(2)}) copy-start(bf16[96,128]{1,0:T(8,128)(2,1)S(1)} %get-tuple-element.130.place) | copy-start | bytes 73732
  31.4 11.5 %collective-permute-start.7 = (bf16[112,1024]{1,0:T(8,128)(2,1)S(1)}, bf16[112,1024]{1,0:T(8,128)(2,1)S(1)}, u32[]{:S(2)}, u32[]{:S(2)}) collective-permute-start(bf16[112,1024]{1,0:T(8,128)(2,1)S(1)} %get-tuple-element.105), channel_id=1, source_target_pairs={{0,2},{2,0},{4,6},{6,4},{8,10},{10,8},{12,14},{14,12},{1,3},{3,1},... | collective-permute-start | bytes 688136 | tf_op jit(solution)/shard_map/ppermute | solution.py:239
  43.7 15.0 %copy-start.7 = (bf16[896,1024]{1,0:T(8,128)(2,1)}, bf16[896,1024]{1,0:T(8,128)(2,1)S(1)}, u32[]{:S(2)}) copy-start(bf16[896,1024]{1,0:T(8,128)(2,1)S(1)} %get-tuple-element.174.own) | copy-start | bytes 5505028
  43.7 9.3 %collective-permute-start.10 = (bf16[896,1024]{1,0:T(8,128)(2,1)S(1)}, bf16[896,1024]{1,0:T(8,128)(2,1)S(1)}, u32[]{:S(2)}, u32[]{:S(2)}) collective-permute-start(bf16[896,1024]{1,0:T(8,128)(2,1)S(1)} %get-tuple-element.174.own), channel_id=1, source_target_pairs={{0,1},{1,0},{2,3},{3,2},{4,5},{5,4},{6,7},{7,6},{8,9},{9,8},{10,11... | collective-permute-start | bytes 5505032 | tf_op jit(solution)/shard_map/ppermute | solution.py:248
  49.6 11.8 %collective-permute-start.13 = (bf16[128,1024]{1,0:T(8,128)(2,1)}, bf16[128,1024]{1,0:T(8,128)(2,1)S(1)}, u32[]{:S(2)}, u32[]{:S(2)}) collective-permute-start(bf16[128,1024]{1,0:T(8,128)(2,1)} %refs_0_), channel_id=1, source_target_pairs={{0,8},{2,10},{4,12},{6,14},{8,0},{10,2},{12,4},{14,6},{1,9},{3,11}... | collective-permute-start | bytes 786440 | tf_op jit(solution)/shard_map/ppermute | solution.py:242
  49.6 11.8 %collective-permute-start.12 = (bf16[96,1024]{1,0:T(8,128)(2,1)S(1)}, bf16[96,1024]{1,0:T(8,128)(2,1)S(1)}, u32[]{:S(2)}, u32[]{:S(2)}) collective-permute-start(bf16[96,1024]{1,0:T(8,128)(2,1)S(1)} %shard_map.124), channel_id=1, source_target_pairs={{0,2},{2,0},{4,6},{6,4},{8,10},{10,8},{12,14},{14,12},{1,3},{3,1},... | collective-permute-start | bytes 589832 | tf_op jit(solution)/shard_map/ppermute | solution.py:239
  50.8 10.6 %collective-permute-start.11 = (bf16[96,1024]{1,0:T(8,128)(2,1)S(1)}, bf16[96,1024]{1,0:T(8,128)(2,1)S(1)}, u32[]{:S(2)}, u32[]{:S(2)}) collective-permute-start(bf16[96,1024]{1,0:T(8,128)(2,1)S(1)} %shard_map.123), channel_id=1, source_target_pairs={{0,2},{2,0},{4,6},{6,4},{8,10},{10,8},{12,14},{14,12},{1,3},{3,1},... | collective-permute-start | bytes 589832 | tf_op jit(solution)/shard_map/ppermute | solution.py:239
  53.0 5.7 %copy-start.9 = (bf16[896,1024]{1,0:T(8,128)(2,1)}, bf16[896,1024]{1,0:T(8,128)(2,1)S(1)}, u32[]{:S(2)}) copy-start(bf16[896,1024]{1,0:T(8,128)(2,1)S(1)} %collective-permute-done.10.other) | copy-start | bytes 5505028
  58.7 11.8 %copy-start.13 = (bf16[896,384]{1,0:T(8,128)(2,1)}, bf16[896,384]{1,0:T(8,128)(2,1)S(1)}, u32[]{:S(2)}) copy-start(bf16[896,384]{1,0:T(8,128)(2,1)S(1)} %get-tuple-element.133.refs_0_) | copy-start | bytes 2064388
  61.4 9.1 %collective-permute-start.15 = (bf16[896,1024]{1,0:T(8,128)(2,1)S(1)}, bf16[896,1024]{1,0:T(8,128)(2,1)S(1)}, u32[]{:S(2)}, u32[]{:S(2)}) collective-permute-start(bf16[896,1024]{1,0:T(8,128)(2,1)S(1)} %get-tuple-element.132), channel_id=1, source_target_pairs={{0,1},{1,0},{2,3},{3,2},{4,5},{5,4},{6,7},{7,6},{8,9},{9,8},{10,11... | collective-permute-start | bytes 5505032 | tf_op jit(solution)/shard_map/ppermute | solution.py:248
  62.8 6.6 %collective-permute-start.14 = (bf16[96,1024]{1,0:T(8,128)(2,1)S(1)}, bf16[96,1024]{1,0:T(8,128)(2,1)S(1)}, u32[]{:S(2)}, u32[]{:S(2)}) collective-permute-start(bf16[96,1024]{1,0:T(8,128)(2,1)S(1)} %shard_map.127), channel_id=1, source_target_pairs={{0,2},{2,0},{4,6},{6,4},{8,10},{10,8},{12,14},{14,12},{1,3},{3,1},... | collective-permute-start | bytes 589832 | tf_op jit(solution)/shard_map/ppermute | solution.py:239
  70.5 6.1 %copy-start = (bf16[896,1024]{1,0:T(8,128)(2,1)}, bf16[896,1024]{1,0:T(8,128)(2,1)S(1)}, u32[]{:S(2)}) copy-start(bf16[896,1024]{1,0:T(8,128)(2,1)S(1)} %shard_map.128.own) | copy-start | bytes 5505028
  72.3 10.8 %copy-start.24 = (bf16[96,1024]{1,0:T(8,128)(2,1)}, bf16[96,1024]{1,0:T(8,128)(2,1)S(1)}, u32[]{:S(2)}) copy-start(bf16[96,1024]{1,0:T(8,128)(2,1)S(1)} %get-tuple-element.161) | copy-start | bytes 589828
  72.3 4.2 %collective-permute-start.16 = (bf16[896,1024]{1,0:T(8,128)(2,1)S(1)}, bf16[896,1024]{1,0:T(8,128)(2,1)S(1)}, u32[]{:S(2)}, u32[]{:S(2)}) collective-permute-start(bf16[896,1024]{1,0:T(8,128)(2,1)S(1)} %shard_map.128.own), channel_id=1, source_target_pairs={{0,1},{1,0},{2,3},{3,2},{4,5},{5,4},{6,7},{7,6},{8,9},{9,8},{10,11... | collective-permute-start | bytes 5505032 | tf_op jit(solution)/shard_map/ppermute | solution.py:248
  73.1 10.0 %collective-permute-start.17 = (bf16[96,1024]{1,0:T(8,128)(2,1)S(1)}, bf16[96,1024]{1,0:T(8,128)(2,1)S(1)}, u32[]{:S(2)}, u32[]{:S(2)}) collective-permute-start(bf16[96,1024]{1,0:T(8,128)(2,1)S(1)} %get-tuple-element.135), channel_id=1, source_target_pairs={{0,2},{2,0},{4,6},{6,4},{8,10},{10,8},{12,14},{14,12},{1,3},{3,1},... | collective-permute-start | bytes 589832 | tf_op jit(solution)/shard_map/ppermute | solution.py:239
  74.3 9.5 %collective-permute-start.18 = (bf16[96,1024]{1,0:T(8,128)(2,1)S(1)}, bf16[96,1024]{1,0:T(8,128)(2,1)S(1)}, u32[]{:S(2)}, u32[]{:S(2)}) collective-permute-start(bf16[96,1024]{1,0:T(8,128)(2,1)S(1)} %get-tuple-element.137), channel_id=1, source_target_pairs={{0,2},{2,0},{4,6},{6,4},{8,10},{10,8},{12,14},{14,12},{1,3},{3,1},... | collective-permute-start | bytes 589832 | tf_op jit(solution)/shard_map/ppermute | solution.py:239
  76.5 6.6 %copy-start.11 = (bf16[896,1024]{1,0:T(8,128)(2,1)}, bf16[896,1024]{1,0:T(8,128)(2,1)S(1)}, u32[]{:S(2)}) copy-start(bf16[896,1024]{1,0:T(8,128)(2,1)S(1)} %collective-permute-done.16.other) | copy-start | bytes 5505028
  83.2 5.7 %copy-start.22 = (f32[4,16,128]{2,1,0:T(8,128)}, f32[4,16,128]{2,1,0:T(8,128)S(1)}, u32[]{:S(2)}) copy-start(f32[4,16,128]{2,1,0:T(8,128)S(1)} %get-tuple-element.145.refs_4_) | copy-start | bytes 98308
  83.8 16.3 %collective-permute-start.19 = (bf16[896,1024]{1,0:T(8,128)(2,1)}, bf16[896,1024]{1,0:T(8,128)(2,1)}, u32[]{:S(2)}, u32[]{:S(2)}) collective-permute-start(bf16[896,1024]{1,0:T(8,128)(2,1)} %get-tuple-element.142), channel_id=1, source_target_pairs={{0,1},{1,0},{2,3},{3,2},{4,5},{5,4},{6,7},{7,6},{8,9},{9,8},{10,11... | collective-permute-start | bytes 5505032 | tf_op jit(solution)/shard_map/ppermute | solution.py:248
  86.2 8.1 %copy-start.25 = (s32[128,4]{0,1:T(4,128)S(1)}, s32[128,4]{0,1:T(4,128)}, u32[]{:S(2)}) copy-start(s32[128,4]{0,1:T(4,128)} %param.8) | copy-start | bytes 6148
  86.2 6.9 %collective-permute-start.24 = (bf16[96,1024]{1,0:T(8,128)(2,1)}, bf16[96,1024]{1,0:T(8,128)(2,1)}, u32[]{:S(2)}, u32[]{:S(2)}) collective-permute-start(bf16[96,1024]{1,0:T(8,128)(2,1)} %get-tuple-element.160), channel_id=1, source_target_pairs={{0,2},{2,0},{4,6},{6,4},{8,10},{10,8},{12,14},{14,12},{1,3},{3,1},... | collective-permute-start | bytes 589832 | tf_op jit(solution)/shard_map/ppermute | solution.py:239
  88.9 15.1 %collective-permute-start.21 = (bf16[128,1024]{1,0:T(8,128)(2,1)}, bf16[128,1024]{1,0:T(8,128)(2,1)}, u32[]{:S(2)}, u32[]{:S(2)}) collective-permute-start(bf16[128,1024]{1,0:T(8,128)(2,1)} %shard_map.133), channel_id=1, source_target_pairs={{0,4},{2,6},{4,8},{6,10},{8,12},{10,14},{12,0},{14,2},{1,5},{3,7},... | collective-permute-start | bytes 786440 | tf_op jit(solution)/shard_map/ppermute | solution.py:242
  91.2 13.6 %collective-permute-start.20 = (bf16[128,1024]{1,0:T(8,128)(2,1)}, bf16[128,1024]{1,0:T(8,128)(2,1)}, u32[]{:S(2)}, u32[]{:S(2)}) collective-permute-start(bf16[128,1024]{1,0:T(8,128)(2,1)} %shard_map.132), channel_id=1, source_target_pairs={{0,12},{2,14},{4,0},{6,2},{8,4},{10,6},{12,8},{14,10},{1,13},{3,15... | collective-permute-start | bytes 786440 | tf_op jit(solution)/shard_map/ppermute | solution.py:242
  93.1 6.3 %collective-permute-start.25 = (bf16[96,1024]{1,0:T(8,128)(2,1)}, bf16[96,1024]{1,0:T(8,128)(2,1)S(1)}, u32[]{:S(2)}, u32[]{:S(2)}) collective-permute-start(bf16[96,1024]{1,0:T(8,128)(2,1)} %copy-done.24), channel_id=1, source_target_pairs={{0,2},{2,0},{4,6},{6,4},{8,10},{10,8},{12,14},{14,12},{1,3},{3,1},... | collective-permute-start | bytes 589832 | tf_op jit(solution)/shard_map/ppermute | solution.py:239
  94.2 0.7 copy-start.20
  95.0 5.2 %copy-start.6 = (bf16[1,2048,384]{2,1,0:T(8,128)(2,1)S(1)}, bf16[1,2048,384]{2,1,0:T(8,128)(2,1)}, u32[]{:S(2)}) copy-start(bf16[1,2048,384]{2,1,0:T(8,128)(2,1)} %param.11) | copy-start | bytes 4718596
  96.3 3.9 %copy-start.4 = (bf16[1,2048,384]{2,1,0:T(8,128)(2,1)S(1)}, bf16[1,2048,384]{2,1,0:T(8,128)(2,1)}, u32[]{:S(2)}) copy-start(bf16[1,2048,384]{2,1,0:T(8,128)(2,1)} %param.10) | copy-start | bytes 4718596
  96.3 3.9 %copy-start.23 = (f32[4,16,128]{2,1,0:T(8,128)S(1)}, f32[4,16,128]{2,1,0:T(8,128)}, u32[]{:S(2)}) copy-start(f32[4,16,128]{2,1,0:T(8,128)} %copy-done.22) | copy-start | bytes 98308
  96.3 20.8 %collective-permute-start.26 = (bf16[128,1024]{1,0:T(8,128)(2,1)S(1)}, bf16[128,1024]{1,0:T(8,128)(2,1)S(1)}, u32[]{:S(2)}, u32[]{:S(2)}) collective-permute-start(bf16[128,1024]{1,0:T(8,128)(2,1)S(1)} %shard_map.137), channel_id=1, source_target_pairs={{0,8},{2,10},{4,12},{6,14},{8,0},{10,2},{12,4},{14,6},{1,9},{3,11}... | collective-permute-start | bytes 786440 | tf_op jit(solution)/shard_map/ppermute | solution.py:242
  100.2 6.1 %copy-start.8 = (bf16[896,1024]{1,0:T(8,128)(2,1)S(1)}, bf16[896,1024]{1,0:T(8,128)(2,1)}, u32[]{:S(2)}) copy-start(bf16[896,1024]{1,0:T(8,128)(2,1)} %copy-done.7) | copy-start | bytes 5505028
  100.2 6.1 %copy-start.10 = (bf16[896,1024]{1,0:T(8,128)(2,1)S(1)}, bf16[896,1024]{1,0:T(8,128)(2,1)}, u32[]{:S(2)}) copy-start(bf16[896,1024]{1,0:T(8,128)(2,1)} %copy-done.9) | copy-start | bytes 5505028
  104.9 1.7 %copy-start.1 = (bf16[896,1024]{1,0:T(8,128)(2,1)S(1)}, bf16[896,1024]{1,0:T(8,128)(2,1)}, u32[]{:S(2)}) copy-start(bf16[896,1024]{1,0:T(8,128)(2,1)} %copy-done) | copy-start | bytes 5505028
  104.9 2.0 %copy-start.12 = (bf16[896,1024]{1,0:T(8,128)(2,1)S(1)}, bf16[896,1024]{1,0:T(8,128)(2,1)}, u32[]{:S(2)}) copy-start(bf16[896,1024]{1,0:T(8,128)(2,1)} %copy-done.11) | copy-start | bytes 5505028
  104.9 10.0 %collective-permute-start.22 = (bf16[112,1024]{1,0:T(8,128)(2,1)S(1)}, bf16[112,1024]{1,0:T(8,128)(2,1)S(1)}, u32[]{:S(2)}, u32[]{:S(2)}) collective-permute-start(bf16[112,1024]{1,0:T(8,128)(2,1)S(1)} %get-tuple-element.156), channel_id=1, source_target_pairs={{0,2},{2,0},{4,6},{6,4},{8,10},{10,8},{12,14},{14,12},{1,3},{3,1},... | collective-permute-start | bytes 688136 | tf_op jit(solution)/shard_map/ppermute | solution.py:239
  105.1 11.2 %collective-permute-start.23 = (bf16[112,1024]{1,0:T(8,128)(2,1)S(1)}, bf16[112,1024]{1,0:T(8,128)(2,1)S(1)}, u32[]{:S(2)}, u32[]{:S(2)}) collective-permute-start(bf16[112,1024]{1,0:T(8,128)(2,1)S(1)} %get-tuple-element.158), channel_id=1, source_target_pairs={{0,2},{2,0},{4,6},{6,4},{8,10},{10,8},{12,14},{14,12},{1,3},{3,1},... | collective-permute-start | bytes 688136 | tf_op jit(solution)/shard_map/ppermute | solution.py:239
  106.9 1.1 copy-start.14
  114.5 0.7 copy-start.21
  114.8 1.5 copy-start.18
  116.0 10.1 %collective-permute-start.28 = (bf16[112,1024]{1,0:T(8,128)(2,1)S(1)}, bf16[112,1024]{1,0:T(8,128)(2,1)S(1)}, u32[]{:S(2)}, u32[]{:S(2)}) collective-permute-start(bf16[112,1024]{1,0:T(8,128)(2,1)S(1)} %get-tuple-element.172), channel_id=1, source_target_pairs={{0,2},{2,0},{4,6},{6,4},{8,10},{10,8},{12,14},{14,12},{1,3},{3,1},... | collective-permute-start | bytes 688136 | tf_op jit(solution)/shard_map/ppermute | solution.py:239
  117.1 9.0 %copy-start.16 = (bf16[96,128]{1,0:T(8,128)(2,1)S(1)}, bf16[96,128]{1,0:T(8,128)(2,1)}, u32[]{:S(2)}) copy-start(bf16[96,128]{1,0:T(8,128)(2,1)} %copy-done.15) | copy-start | bytes 73732
  117.1 8.2 %collective-permute-start.27 = (bf16[112,1024]{1,0:T(8,128)(2,1)S(1)}, bf16[112,1024]{1,0:T(8,128)(2,1)S(1)}, u32[]{:S(2)}, u32[]{:S(2)}) collective-permute-start(bf16[112,1024]{1,0:T(8,128)(2,1)S(1)} %get-tuple-element.170), channel_id=1, source_target_pairs={{0,2},{2,0},{4,6},{6,4},{8,10},{10,8},{12,14},{14,12},{1,3},{3,1},... | collective-permute-start | bytes 688136 | tf_op jit(solution)/shard_map/ppermute | solution.py:239
  118.4 15.2 %collective-permute-start.31 = (bf16[144,1024]{1,0:T(8,128)(2,1)S(1)}, bf16[144,1024]{1,0:T(8,128)(2,1)S(1)}, u32[]{:S(2)}, u32[]{:S(2)}) collective-permute-start(bf16[144,1024]{1,0:T(8,128)(2,1)S(1)} %shard_map.135), channel_id=1, source_target_pairs={{0,4},{2,6},{4,8},{6,10},{8,12},{10,14},{12,0},{14,2},{1,5},{3,7},... | collective-permute-start | bytes 884744 | tf_op jit(solution)/shard_map/ppermute | solution.py:242
  121.1 22.6 %collective-permute-start.30 = (bf16[144,1024]{1,0:T(8,128)(2,1)S(1)}, bf16[144,1024]{1,0:T(8,128)(2,1)S(1)}, u32[]{:S(2)}, u32[]{:S(2)}) collective-permute-start(bf16[144,1024]{1,0:T(8,128)(2,1)S(1)} %shard_map.134), channel_id=1, source_target_pairs={{0,8},{2,10},{4,12},{6,14},{8,0},{10,2},{12,4},{14,6},{1,9},{3,11}... | collective-permute-start | bytes 884744 | tf_op jit(solution)/shard_map/ppermute | solution.py:242
  126.9 21.1 %collective-permute-start.29 = (bf16[144,1024]{1,0:T(8,128)(2,1)S(1)}, bf16[144,1024]{1,0:T(8,128)(2,1)S(1)}, u32[]{:S(2)}, u32[]{:S(2)}) collective-permute-start(bf16[144,1024]{1,0:T(8,128)(2,1)S(1)} %shard_map.139), channel_id=1, source_target_pairs={{0,12},{2,14},{4,0},{6,2},{8,4},{10,6},{12,8},{14,10},{1,13},{3,15... | collective-permute-start | bytes 884744 | tf_op jit(solution)/shard_map/ppermute | solution.py:242
  148.1 2.4 %collective-permute-start.32 = (f32[128,4]{0,1:T(4,128)S(1)}, f32[128,4]{0,1:T(4,128)S(1)}, u32[]{:S(2)}, u32[]{:S(2)}) collective-permute-start(f32[128,4]{0,1:T(4,128)S(1)} %select_reduce_fusion), channel_id=1, source_target_pairs={{0,1},{1,0},{2,3},{3,2},{4,5},{5,4},{6,7},{7,6},{8,9},{9,8},{10,11... | collective-permute-start | bytes 6152 | tf_op jit(solution)/shard_map/ppermute | solution.py:248

commit v9 on v8

--- a/solution.py
+++ b/solution.py
@@ -298,12 +298,12 @@
             grad_pack_kernel, (shape_of((padded, half_width)),), (info, grad_blocks[k], places[k]))[0]
 
     near, far = by_reach[:-1], by_reach[-1]
-    grad_packed = {k: grad_pack(k) for k in near}
-    grad_compact = {k: over_pair(grad_packed[k]) for k in near}
+    grad_packed = {k: grad_pack(k) for k in by_reach}
+    grad_compact = {k: over_pair(grad_packed[k]) for k in by_reach}
     grad_compact[0] = grad_first
-    compact, near_blocks, near_packed = settle(
-        (compact, {k: grad_blocks[k] for k in near}, {k: grad_packed[k] for k in near}))
-    grad_blocks.update(near_blocks)
+    ahead = {k: grad_compact[k] for k in near[:1]}
+    compact, grad_blocks, grad_packed, ahead = settle((compact, grad_blocks, grad_packed, ahead))
+    grad_compact.update(ahead)
     rows, weights = local_call(
         functools.partial(token_rows_kernel, *sizes),
         (half_rows, shape_of((row_count, 1), F32)),
@@ -313,8 +313,7 @@
         functools.partial(forward_kernel, pieces, chunk),
         (shape_of(hidden_rows, F32), shape_of(hidden_rows, F32), shape_of(hidden_rows), half_rows),
         (info, rows, rows_other, weights, gate_local, up_local, down_local))
-    sent, grad_compact, grad_blocks = settle((sent, grad_compact, grad_blocks))
-    grad_compact[far] = over_pair(grad_pack(far))
+    sent, grad_compact = settle((sent, grad_compact))
     out_dense, *out_packed = local_call(
         functools.partial(join_kernel, *sizes, True),
         (shape_of((lines, token_count, half_width), F32),
@@ -352,25 +351,21 @@
     last, first_home = settle((out_packed[far], out_home[near[0]]))
     out_back[far] = over_pair(last)
     out_home[near[0]] = first_home
-    last, out_back[far] = settle((out_packed[0], out_back[far]))
-    out_back[0] = over_pair(last)
-    for k in (far, 0):
-        out_home[k] = to_home(k, out_dense, out_back)
 
     def whole(own, other):
         return jnp.concatenate(
             [jnp.where(core == 0, own, other), jnp.where(core == 0, other, own)], axis=1)
 
     came = over_core(sent)
-    out_came = {k: over_line(out_home[k], lines - k) for k in by_reach}
-    out_came[0] = out_home[0]
+    out_came = {k: over_line(out_home[k], lines - k) for k in near}
     in_dense, *in_packed = local_call(
         functools.partial(join_kernel, *sizes, False),
         (shape_of((lines, token_count, half_width), F32),
          *[shape_of((padded + TAIL, half_width)) for _ in every]),
         (info, came, grad_gate, grad_up, gate_local, up_local, compact_tails))
-    in_packed, ahead = settle((in_packed, {k: out_came[k] for k in near}))
-    out_came.update(ahead)
+    in_packed, out_back[far], out_came = settle((in_packed, out_back[far], out_came))
+    far_home = to_home(far, out_dense, out_back)
+    out_came[far] = over_line(far_home, lines - far)
     in_back, in_home, sequence = {}, {}, outward + [0]
     for i, k in enumerate(sequence):
         packed = in_packed[k]
@@ -378,10 +373,13 @@
             packed, _ = settle((packed, in_home[sequence[i - 2]]))
         in_back[k] = over_pair(packed)
         in_home[k] = to_home(k, in_dense, in_back, dense_tails)
+    last, _ = settle((out_packed[0], in_back[sequence[2]]))
+    out_back[0] = over_pair(last)
     ready, out_came = settle(({k: in_home[k] for k in sequence[:2]}, out_came))
+    out_came[0] = to_home(0, out_dense, out_back)
     in_home.update(ready)
     layer_out = summed(out_came)
-    rows, rows_other, grad_rows, _ = settle((rows, rows_other, grad_rows, in_packed))
+    rows, rows_other, grad_rows, _ = settle((rows, rows_other, grad_rows, far_home))
     rows = whole(rows, rows_other)
     gate_grad = dot(rows, grad_gate, FIRST).astype(BF)
     down_grad = dot(scaled, whole(grad_rows, grad_other), FIRST).astype(BF)

time: 151 us -> 154 us (1.020)
  waiting for transfers between devices: 48.4 us -> 57.5 us
  starting transfers between devices: 48.2 us -> 39.2 us
  local copies, waits for them, and re-layouts: 2.35 us -> 5.19 us
    ppermute x12, waiting for transfers between devices: 34.2 us -> 43.6 us  [over_line(): lax.ppermute(x, 'expert', [(i, (i // 2 + k) % lines * 2 + i % 2) for i in...]
    ppermute x5, starting transfers between devices: 9.72 us -> 5.25 us  [over_core(): return lax.ppermute(x, 'tensor', [(0, 1), (1, 0)])]
    ppermute x12, starting transfers between devices: 23.3 us -> 19 us  [over_line(): lax.ppermute(x, 'expert', [(i, (i // 2 + k) % lines * 2 + i % 2) for i in...]
    unnamed x53 -> x55, local copies, waits for them, and re-layouts: 2.34 us -> 5.18 us
    ppermute x16, waiting for transfers between devices: 10.3 us -> 7.72 us  [over_pair(): lax.ppermute(x, 'expert', [(i, i + 1 - 2 * (i % 2)) for i in range(expert...]
    ppermute x5, waiting for transfers between devices: 3.89 us -> 6.2 us  [over_core(): return lax.ppermute(x, 'tensor', [(0, 1), (1, 0)])]
  transfers between devices with their start and end apart: 33 -> 33, of which waited for: 13 -> 16; matrix products, arithmetic and copies ran while one was open for 9% -> 9% of each run, Pallas kernels for 21% -> 21%
where the time goes in v9:
time: 154 us; the launch traced here: 153 us
  waiting for transfers between devices  57.5 us (37%)
  starting transfers between devices  39.2 us (25%)
  Pallas kernels  34.1 us (22%)
  matrix products  9.92 us (6%)
  other arithmetic  6.17 us (4%)
  local copies, waits for them, and re-layouts  5.19 us (3%)
    ppermute x12, waiting for transfers between devices, over_line(): lax.ppermute(x, 'expert', [(i, (i // 2 + k) % lines * 2 + i % 2) for i in...  43.6 us
    pallas_call x22, Pallas kernels, local_call(): pl.pallas_call(kernel, out_shape=tuple(outs), in_specs=[SMEM_SPEC] + [VME...  34.1 us
    ppermute x12, starting transfers between devices, over_line(): lax.ppermute(x, 'expert', [(i, (i // 2 + k) % lines * 2 + i % 2) for i in...  19 us
    ppermute x16, starting transfers between devices, over_pair(): lax.ppermute(x, 'expert', [(i, i + 1 - 2 * (i % 2)) for i in range(expert...  15 us
    dot_general x3, matrix products, dot(): lax.dot_general(a, b, (contract, ((), ())), preferred_element_type=F32)  9.92 us
    ppermute x16, waiting for transfers between devices, over_pair(): lax.ppermute(x, 'expert', [(i, i + 1 - 2 * (i % 2)) for i in range(expert...  7.72 us
    ppermute x5, waiting for transfers between devices, over_core(): return lax.ppermute(x, 'tensor', [(0, 1), (1, 0)])  6.2 us
    ppermute x5, starting transfers between devices, over_core(): return lax.ppermute(x, 'tensor', [(0, 1), (1, 0)])  5.25 us
  transfers between devices with their start and end apart: 33, of which 16 were waited for; matrix products, arithmetic and copies ran while one was open for 9% of the time, Pallas kernels for 21%

profile of v9, /device:TPU:9, one launch (start us, length us, event | category | flops | bytes accessed | tf_op | source)
XLA Modules:
  0.0 153.3 jit_solution(4479697083423307931)
XLA Ops:
  1.4 1.0 pad_maximum_fusion.1.block.refs_0_
  2.4 1.3 collective-permute-start
  3.9 2.3 %collective-permute-start.1 = (bf16[144,1024]{1,0:T(8,128)(2,1)S(1)}, bf16[144,1024]{1,0:T(8,128)(2,1)S(1)}, u32[]{:S(2)}, u32[]{:S(2)}) collective-permute-start(bf16[144,1024]{1,0:T(8,128)(2,1)S(1)} %pad_maximum_fusion.1.block.refs_0_), channel_id=1, source_target_pairs={{0,8},{2,10},{4,12},{6,14},{8,0},{10,2},{12,4},{14,6},{1,9},{3,11}... | collective-permute-start | bytes 884744 | tf_op jit(solution)/shard_map/ppermute | solution.py:242
  6.3 0.9 shard_map.118
  7.2 1.3 collective-permute-start.3
  8.5 1.8 %collective-permute-done.block.refs_1_ = bf16[144,1024]{1,0:T(8,128)(2,1)S(1)} collective-permute-done((bf16[144,1024]{1,0:T(8,128)(2,1)S(1)}, bf16[144,1024]{1,0:T(8,128)(2,1)S(1)}, u32[]{:S(2)}, u32[]{:S(2)}) %collective-permute-start) | collective-permute-done | bytes 294944 | tf_op jit(solution)/shard_map/ppermute | solution.py:242
  10.3 0.9 shard_map.119
  11.2 1.3 collective-permute-start.4
  12.5 6.7 %collective-permute-done.2.block.refs_3_ = bf16[144,1024]{1,0:T(8,128)(2,1)S(1)} collective-permute-done((bf16[144,1024]{1,0:T(8,128)(2,1)S(1)}, bf16[144,1024]{1,0:T(8,128)(2,1)S(1)}, u32[]{:S(2)}, u32[]{:S(2)}) %collective-permute-start.2) | collective-permute-done | bytes 294944 | tf_op jit(solution)/shard_map/ppermute | solution.py:242
  19.2 0.9 shard_map.120
  20.1 1.5 %collective-permute-start.5 = (bf16[112,1024]{1,0:T(8,128)(2,1)S(1)}, bf16[112,1024]{1,0:T(8,128)(2,1)S(1)}, u32[]{:S(2)}, u32[]{:S(2)}) collective-permute-start(bf16[112,1024]{1,0:T(8,128)(2,1)S(1)} %get-tuple-element.96), channel_id=1, source_target_pairs={{0,2},{2,0},{4,6},{6,4},{8,10},{10,8},{12,14},{14,12},{1,3},{3,1},... | collective-permute-start | bytes 688136 | tf_op jit(solution)/shard_map/ppermute | solution.py:239
  21.7 1.1 shard_map.121
  22.9 4.5 %collective-permute-done.6.refs_4_ = bf16[96,1024]{1,0:T(8,128)(2,1)S(1)} collective-permute-done((bf16[96,1024]{1,0:T(8,128)(2,1)S(1)}, bf16[96,1024]{1,0:T(8,128)(2,1)S(1)}, u32[]{:S(2)}, u32[]{:S(2)}) %collective-permute-start.6) | collective-permute-done | bytes 196640 | tf_op jit(solution)/shard_map/ppermute | solution.py:239
  27.4 1.0 collective-permute-done.1.block.refs_2_
  28.4 2.1 %collective-permute-start.8 = (bf16[128,1024]{1,0:T(8,128)(2,1)}, bf16[128,1024]{1,0:T(8,128)(2,1)S(1)}, u32[]{:S(2)}, u32[]{:S(2)}) collective-permute-start(bf16[128,1024]{1,0:T(8,128)(2,1)} %refs_0_), channel_id=1, source_target_pairs={{0,4},{2,6},{4,8},{6,10},{8,12},{10,14},{12,0},{14,2},{1,5},{3,7},... | collective-permute-start | bytes 786440 | tf_op jit(solution)/shard_map/ppermute | solution.py:242
  30.4 4.0 %collective-permute-start.9 = (bf16[128,1024]{1,0:T(8,128)(2,1)}, bf16[128,1024]{1,0:T(8,128)(2,1)S(1)}, u32[]{:S(2)}, u32[]{:S(2)}) collective-permute-start(bf16[128,1024]{1,0:T(8,128)(2,1)} %refs_0_), channel_id=1, source_target_pairs={{0,8},{2,10},{4,12},{6,14},{8,0},{10,2},{12,4},{14,6},{1,9},{3,11}... | collective-permute-start | bytes 786440 | tf_op jit(solution)/shard_map/ppermute | solution.py:242
  34.4 0.9 shard_map.122
  35.4 1.3 collective-permute-start.7
  37.4 1.0 collective-permute-start.11
  38.4 12.8 %collective-permute-done.9.block.refs_2_ = bf16[128,1024]{1,0:T(8,128)(2,1)S(1)} collective-permute-done((bf16[128,1024]{1,0:T(8,128)(2,1)}, bf16[128,1024]{1,0:T(8,128)(2,1)S(1)}, u32[]{:S(2)}, u32[]{:S(2)}) %collective-permute-start.9) | collective-permute-done | bytes 262176 | tf_op jit(solution)/shard_map/ppermute | solution.py:242
  51.9 4.7 %collective-permute-done.10.block.refs_3_ = bf16[128,1024]{1,0:T(8,128)(2,1)S(1)} collective-permute-done((bf16[128,1024]{1,0:T(8,128)(2,1)}, bf16[128,1024]{1,0:T(8,128)(2,1)S(1)}, u32[]{:S(2)}, u32[]{:S(2)}) %collective-permute-start.10) | collective-permute-done | bytes 262176 | tf_op jit(solution)/shard_map/ppermute | solution.py:242
  58.2 1.7 %collective-permute-start.12 = (bf16[896,1024]{1,0:T(8,128)(2,1)S(1)}, bf16[896,1024]{1,0:T(8,128)(2,1)S(1)}, u32[]{:S(2)}, u32[]{:S(2)}) collective-permute-start(bf16[896,1024]{1,0:T(8,128)(2,1)S(1)} %get-tuple-element.172.own), channel_id=1, source_target_pairs={{0,1},{1,0},{2,3},{3,2},{4,5},{5,4},{6,7},{7,6},{8,9},{9,8},{10,11... | collective-permute-start | bytes 5505032 | tf_op jit(solution)/shard_map/ppermute | solution.py:248
  59.9 1.3 collective-permute-start.13
  61.4 1.9 %collective-permute-done.12.other = bf16[896,1024]{1,0:T(8,128)(2,1)S(1)} collective-permute-done((bf16[896,1024]{1,0:T(8,128)(2,1)S(1)}, bf16[896,1024]{1,0:T(8,128)(2,1)S(1)}, u32[]{:S(2)}, u32[]{:S(2)}) %collective-permute-start.12) | collective-permute-done | bytes 1835040 | tf_op jit(solution)/shard_map/ppermute | solution.py:248
  63.3 5.7 %shard_map.127 = (f32[896,384]{1,0:T(8,128)S(1)}, f32[896,384]{1,0:T(8,128)S(1)}, bf16[896,384]{1,0:T(8,128)(2,1)S(1)}, bf16[896,1024]{1,0:T(8,128)(2,1)S(1)}) custom-call(s32[3]{0:T(128)S(1)} %pad_add_fusion.info, bf16[896,1024]{1,0:T(8,128)(2,1)S(1)} %get-tuple-element.172.own, bf16[896,1024]{1,0:T(8,128)(2,1)S(1)} %collective-permute-done.12.other, ...), custom_call_target="tpu_custom_call" | custom-call | flops 1000 | bytes 1000 | tf_op jit(solution)/shard_map/pallas_call | solution.py:41
  69.1 1.5 collective-permute-done.14.refs_7_
  70.6 0.8 collective-permute-start.15
  71.4 1.1 shard_map.129.own
  72.5 2.3 %collective-permute-done.15.came = bf16[896,1024]{1,0:T(8,128)(2,1)S(1)} collective-permute-done((bf16[896,1024]{1,0:T(8,128)(2,1)S(1)}, bf16[896,1024]{1,0:T(8,128)(2,1)S(1)}, u32[]{:S(2)}, u32[]{:S(2)}) %collective-permute-start.15) | collective-permute-done | bytes 1835040 | tf_op jit(solution)/shard_map/ppermute | solution.py:248
  74.9 1.7 %shard_map.128 = (f32[4,128,1024]{2,1,0:T(8,128)S(1)}, bf16[96,1024]{1,0:T(8,128)(2,1)S(1)}, bf16[96,1024]{1,0:T(8,128)(2,1)S(1)}, bf16[96,1024]{1,0:T(8,128)(2,1)S(1)}, bf16[96,1024]{1,0:T(8,128)(2,1)S(1)}) custom-call(s32[3]{0:T(128)S(1)} %pad_add_fusion.info, bf16[896,1024]{1,0:T(8,128)(2,1)S(1)} %collective-permute-done.15.came, ...), custom_call_target="tpu_custom_call" | custom-call | flops 1000 | bytes 1000 | tf_op jit(solution)/shard_map/pallas_call | solution.py:41
  77.6 1.2 collective-permute-start.17
  79.1 1.9 %collective-permute-done.16.other = bf16[896,1024]{1,0:T(8,128)(2,1)S(1)} collective-permute-done((bf16[896,1024]{1,0:T(8,128)(2,1)S(1)}, bf16[896,1024]{1,0:T(8,128)(2,1)S(1)}, u32[]{:S(2)}, u32[]{:S(2)}) %collective-permute-start.16) | collective-permute-done | bytes 1835040 | tf_op jit(solution)/shard_map/ppermute | solution.py:248
  81.0 6.6 %shard_map.130 = (bf16[896,384]{1,0:T(8,128)(2,1)S(1)}, bf16[896,384]{1,0:T(8,128)(2,1)S(1)}, bf16[896,1024]{1,0:T(8,128)(2,1)}, f32[4,16,128]{2,1,0:T(8,128)S(1)}, f32[4,16,128]{2,1,0:T(8,128)S(1)}) custom-call(s32[3]{0:T(128)S(1)} %pad_add_fusion.info, bf16[896,1024]{1,0:T(8,128)(2,1)S(1)} %shard_map.129.own, ...), custom_call_target="tpu_custom_call" | custom-call | flops 1000 | bytes 1000 | tf_op jit(solution)/shard_map/pallas_call | solution.py:41
  88.2 0.9 collective-permute-start.19
  89.1 1.5 shard_map.132
  90.6 1.5 shard_map.133
  92.1 2.1 %collective-permute-start.22 = (bf16[128,1024]{1,0:T(8,128)(2,1)}, bf16[128,1024]{1,0:T(8,128)(2,1)}, u32[]{:S(2)}, u32[]{:S(2)}) collective-permute-start(bf16[128,1024]{1,0:T(8,128)(2,1)} %shard_map.133), channel_id=1, source_target_pairs={{0,4},{2,6},{4,8},{6,10},{8,12},{10,14},{12,0},{14,2},{1,5},{3,7},... | collective-permute-start | bytes 786440 | tf_op jit(solution)/shard_map/ppermute | solution.py:242
  94.2 1.2 collective-permute-start.20
  95.5 1.4 copy-done.4
  96.9 1.4 copy-done.6
  99.1 3.7 %shard_map.131 = (f32[4,128,1024]{2,1,0:T(8,128)S(1)}, bf16[112,1024]{1,0:T(8,128)(2,1)S(1)}, bf16[112,1024]{1,0:T(8,128)(2,1)S(1)}, bf16[112,1024]{1,0:T(8,128)(2,1)S(1)}, bf16[112,1024]{1,0:T(8,128)(2,1)S(1)}) custom-call(s32[3]{0:T(128)S(1)} %pad_add_fusion.info, bf16[896,1024]{1,0:T(8,128)(2,1)} %collective-permute-done.19.came, ...), custom_call_target="tpu_custom_call" | custom-call | flops 1000 | bytes 1000 | tf_op jit(solution)/shard_map/pallas_call | solution.py:41
  102.9 2.2 %collective-permute-done.22 = bf16[128,1024]{1,0:T(8,128)(2,1)} collective-permute-done((bf16[128,1024]{1,0:T(8,128)(2,1)}, bf16[128,1024]{1,0:T(8,128)(2,1)}, u32[]{:S(2)}, u32[]{:S(2)}) %collective-permute-start.22) | collective-permute-done | bytes 262176 | tf_op jit(solution)/shard_map/ppermute | solution.py:242
  105.1 1.2 collective-permute-start.23
  106.6 0.8 shard_map.137
  107.4 2.4 %collective-permute-start.27 = (bf16[128,1024]{1,0:T(8,128)(2,1)S(1)}, bf16[128,1024]{1,0:T(8,128)(2,1)S(1)}, u32[]{:S(2)}, u32[]{:S(2)}) collective-permute-start(bf16[128,1024]{1,0:T(8,128)(2,1)S(1)} %shard_map.137), channel_id=1, source_target_pairs={{0,8},{2,10},{4,12},{6,14},{8,0},{10,2},{12,4},{14,6},{1,9},{3,11}... | collective-permute-start | bytes 786440 | tf_op jit(solution)/shard_map/ppermute | solution.py:242
  110.0 3.5 %convolution_convert_fusion.1 = bf16[2048,384]{1,0:T(8,128)(2,1)} fusion(bf16[896,384]{1,0:T(8,128)(2,1)S(1)} %get-tuple-element.144.refs_0_, bf16[896,1024]{1,0:T(8,128)(2,1)S(1)} %get-tuple-element.191, bf16[896,1024]{1,0:T(8,128)(2,1)S(1)} %get-tuple-element.190), kind=kOutput, calls=%fused_computation.7 | convolution fusion | flops 1417412608 | bytes 5931008 | tf_op jit(solution)/shard_map/dot_general | solution.py:24
  113.8 0.9 copy-done.14
  114.6 3.0 %fusion.4 = bf16[384,2048]{1,0:T(8,128)(2,1)} fusion(bf16[896,384]{1,0:T(8,128)(2,1)S(1)} %copy-done.14, bf16[896,1024]{1,0:T(8,128)(2,1)S(1)} %get-tuple-element.193, bf16[896,1024]{1,0:T(8,128)(2,1)S(1)} %get-tuple-element.192), kind=kOutput, calls=%fused_computation.5 | convolution fusion | flops 1417412608 | bytes 5931008 | tf_op jit(solution)/shard_map/dot_general | solution.py:24
  117.6 0.8 shard_map.134
  118.4 1.3 collective-permute-start.24
  119.7 0.8 shard_map.136
  121.4 1.1 collective-permute-start.31
  122.5 3.0 %collective-permute-start.30 = (bf16[144,1024]{1,0:T(8,128)(2,1)S(1)}, bf16[144,1024]{1,0:T(8,128)(2,1)S(1)}, u32[]{:S(2)}, u32[]{:S(2)}) collective-permute-start(bf16[144,1024]{1,0:T(8,128)(2,1)S(1)} %shard_map.134), channel_id=1, source_target_pairs={{0,8},{2,10},{4,12},{6,14},{8,0},{10,2},{12,4},{14,6},{1,9},{3,11}... | collective-permute-start | bytes 884744 | tf_op jit(solution)/shard_map/ppermute | solution.py:242
  125.5 1.2 collective-permute-start.25
  126.7 0.8 shard_map.139
  128.0 1.1 collective-permute-done.28.back
  129.1 0.8 shard_map.138
  130.0 3.5 %fusion.7 = bf16[1,2048,384]{2,1,0:T(8,128)(2,1)} fusion(bf16[896,2048]{1,0:T(8,128)(2,1)S(1)} %pad_maximum_fusion, bf16[896,384]{1,0:T(8,128)(2,1)S(1)} %get-tuple-element.180.refs_1_), kind=kOutput, calls=%fused_computation.8 | convolution fusion | flops 1410072576 | bytes 5931008 | tf_op jit(solution)/shard_map/dot_general | solution.py:24
  133.5 12.1 %collective-permute-done.30 = bf16[144,1024]{1,0:T(8,128)(2,1)S(1)} collective-permute-done((bf16[144,1024]{1,0:T(8,128)(2,1)S(1)}, bf16[144,1024]{1,0:T(8,128)(2,1)S(1)}, u32[]{:S(2)}, u32[]{:S(2)}) %collective-permute-start.30) | collective-permute-done | bytes 294944 | tf_op jit(solution)/shard_map/ppermute | solution.py:242
  145.6 0.8 shard_map.135
  146.4 1.9 %add_convert_fusion.1 = bf16[128,1024]{1,0:T(8,128)(2,1)} fusion(bf16[128,1024]{1,0:T(8,128)(2,1)} %collective-permute-done.22, bf16[128,1024]{1,0:T(8,128)(2,1)S(1)} %collective-permute-done.27, bf16[128,1024]{1,0:T(8,128)(2,1)} %collective-permute-done.21, bf16[128,1024]{1,0:T(8,128)(2,1)S(1)} %shard_map.135), kind=kLoop, calls=%fused_computation.14 | loop fusion | flops 1048576 | bytes 1310720 | tf_op jit(solution)/shard_map/convert_element_type | solution.py:347
  148.3 2.1 %collective-permute-done.29 = bf16[144,1024]{1,0:T(8,128)(2,1)S(1)} collective-permute-done((bf16[144,1024]{1,0:T(8,128)(2,1)S(1)}, bf16[144,1024]{1,0:T(8,128)(2,1)S(1)}, u32[]{:S(2)}, u32[]{:S(2)}) %collective-permute-start.29) | collective-permute-done | bytes 294944 | tf_op jit(solution)/shard_map/ppermute | solution.py:242
  150.5 1.3 collective-permute-start.32
  151.8 0.9 add_convert_fusion
  (109 shorter events, 9.8 us)
Async XLA Ops:
  2.4 7.9 %collective-permute-start = (bf16[144,1024]{1,0:T(8,128)(2,1)S(1)}, bf16[144,1024]{1,0:T(8,128)(2,1)S(1)}, u32[]{:S(2)}, u32[]{:S(2)}) collective-permute-start(bf16[144,1024]{1,0:T(8,128)(2,1)S(1)} %pad_maximum_fusion.1.block.refs_0_), channel_id=1, source_target_pairs={{0,4},{2,6},{4,8},{6,10},{8,12},{10,14},{12,0},{14,2},{1,5},{3,7},... | collective-permute-start | bytes 884744 | tf_op jit(solution)/shard_map/ppermute | solution.py:242
  3.7 15.5 %collective-permute-start.2 = (bf16[144,1024]{1,0:T(8,128)(2,1)S(1)}, bf16[144,1024]{1,0:T(8,128)(2,1)S(1)}, u32[]{:S(2)}, u32[]{:S(2)}) collective-permute-start(bf16[144,1024]{1,0:T(8,128)(2,1)S(1)} %pad_maximum_fusion.1.block.refs_0_), channel_id=1, source_target_pairs={{0,12},{2,14},{4,0},{6,2},{8,4},{10,6},{12,8},{14,10},{1,13},{3,15... | collective-permute-start | bytes 884744 | tf_op jit(solution)/shard_map/ppermute | solution.py:242
  3.9 24.5 %collective-permute-start.1 = (bf16[144,1024]{1,0:T(8,128)(2,1)S(1)}, bf16[144,1024]{1,0:T(8,128)(2,1)S(1)}, u32[]{:S(2)}, u32[]{:S(2)}) collective-permute-start(bf16[144,1024]{1,0:T(8,128)(2,1)S(1)} %pad_maximum_fusion.1.block.refs_0_), channel_id=1, source_target_pairs={{0,8},{2,10},{4,12},{6,14},{8,0},{10,2},{12,4},{14,6},{1,9},{3,11}... | collective-permute-start | bytes 884744 | tf_op jit(solution)/shard_map/ppermute | solution.py:242
  7.2 20.2 %collective-permute-start.3 = (bf16[112,1024]{1,0:T(8,128)(2,1)S(1)}, bf16[112,1024]{1,0:T(8,128)(2,1)S(1)}, u32[]{:S(2)}, u32[]{:S(2)}) collective-permute-start(bf16[112,1024]{1,0:T(8,128)(2,1)S(1)} %get-tuple-element.94), channel_id=1, source_target_pairs={{0,2},{2,0},{4,6},{6,4},{8,10},{10,8},{12,14},{14,12},{1,3},{3,1},... | collective-permute-start | bytes 688136 | tf_op jit(solution)/shard_map/ppermute | solution.py:239
  10.3 53.0 %copy-start.5 = (bf16[1,2048,384]{2,1,0:T(8,128)(2,1)S(1)}, bf16[1,2048,384]{2,1,0:T(8,128)(2,1)}, u32[]{:S(2)}) copy-start(bf16[1,2048,384]{2,1,0:T(8,128)(2,1)} %param.11) | copy-start | bytes 4718596
  11.2 77.9 %copy-start.15 = (bf16[96,128]{1,0:T(8,128)(2,1)}, bf16[96,128]{1,0:T(8,128)(2,1)S(1)}, u32[]{:S(2)}) copy-start(bf16[96,128]{1,0:T(8,128)(2,1)S(1)} %get-tuple-element.107.place) | copy-start | bytes 73732
  11.2 17.2 %collective-permute-start.4 = (bf16[112,1024]{1,0:T(8,128)(2,1)S(1)}, bf16[112,1024]{1,0:T(8,128)(2,1)S(1)}, u32[]{:S(2)}, u32[]{:S(2)}) collective-permute-start(bf16[112,1024]{1,0:T(8,128)(2,1)S(1)} %get-tuple-element.95), channel_id=1, source_target_pairs={{0,2},{2,0},{4,6},{6,4},{8,10},{10,8},{12,14},{14,12},{1,3},{3,1},... | collective-permute-start | bytes 688136 | tf_op jit(solution)/shard_map/ppermute | solution.py:239
  20.1 70.5 %copy-start.17 = (bf16[96,128]{1,0:T(8,128)(2,1)}, bf16[96,128]{1,0:T(8,128)(2,1)S(1)}, u32[]{:S(2)}) copy-start(bf16[96,128]{1,0:T(8,128)(2,1)S(1)} %get-tuple-element.109.place) | copy-start | bytes 73732
  20.1 8.3 %collective-permute-start.5 = (bf16[112,1024]{1,0:T(8,128)(2,1)S(1)}, bf16[112,1024]{1,0:T(8,128)(2,1)S(1)}, u32[]{:S(2)}, u32[]{:S(2)}) collective-permute-start(bf16[112,1024]{1,0:T(8,128)(2,1)S(1)} %get-tuple-element.96), channel_id=1, source_target_pairs={{0,2},{2,0},{4,6},{6,4},{8,10},{10,8},{12,14},{14,12},{1,3},{3,1},... | collective-permute-start | bytes 688136 | tf_op jit(solution)/shard_map/ppermute | solution.py:239
  22.8 4.6 %collective-permute-start.6 = (bf16[96,1024]{1,0:T(8,128)(2,1)S(1)}, bf16[96,1024]{1,0:T(8,128)(2,1)S(1)}, u32[]{:S(2)}, u32[]{:S(2)}) collective-permute-start(bf16[96,1024]{1,0:T(8,128)(2,1)S(1)} %shard_map.121), channel_id=1, source_target_pairs={{0,2},{2,0},{4,6},{6,4},{8,10},{10,8},{12,14},{14,12},{1,3},{3,1},... | collective-permute-start | bytes 589832 | tf_op jit(solution)/shard_map/ppermute | solution.py:239
  28.4 8.3 %collective-permute-start.8 = (bf16[128,1024]{1,0:T(8,128)(2,1)}, bf16[128,1024]{1,0:T(8,128)(2,1)S(1)}, u32[]{:S(2)}, u32[]{:S(2)}) collective-permute-start(bf16[128,1024]{1,0:T(8,128)(2,1)} %refs_0_), channel_id=1, source_target_pairs={{0,4},{2,6},{4,8},{6,10},{8,12},{10,14},{12,0},{14,2},{1,5},{3,7},... | collective-permute-start | bytes 786440 | tf_op jit(solution)/shard_map/ppermute | solution.py:242
  30.4 20.7 %collective-permute-start.9 = (bf16[128,1024]{1,0:T(8,128)(2,1)}, bf16[128,1024]{1,0:T(8,128)(2,1)S(1)}, u32[]{:S(2)}, u32[]{:S(2)}) collective-permute-start(bf16[128,1024]{1,0:T(8,128)(2,1)} %refs_0_), channel_id=1, source_target_pairs={{0,8},{2,10},{4,12},{6,14},{8,0},{10,2},{12,4},{14,6},{1,9},{3,11}... | collective-permute-start | bytes 786440 | tf_op jit(solution)/shard_map/ppermute | solution.py:242
  34.4 22.1 %collective-permute-start.10 = (bf16[128,1024]{1,0:T(8,128)(2,1)}, bf16[128,1024]{1,0:T(8,128)(2,1)S(1)}, u32[]{:S(2)}, u32[]{:S(2)}) collective-permute-start(bf16[128,1024]{1,0:T(8,128)(2,1)} %refs_0_), channel_id=1, source_target_pairs={{0,12},{2,14},{4,0},{6,2},{8,4},{10,6},{12,8},{14,10},{1,13},{3,15... | collective-permute-start | bytes 786440 | tf_op jit(solution)/shard_map/ppermute | solution.py:242
  35.3 22.0 %copy-start.19 = (bf16[96,128]{1,0:T(8,128)(2,1)}, bf16[96,128]{1,0:T(8,128)(2,1)S(1)}, u32[]{:S(2)}) copy-start(bf16[96,128]{1,0:T(8,128)(2,1)S(1)} %get-tuple-element.108.place) | copy-start | bytes 73732
  35.3 28.0 %copy-start.2 = (bf16[1,384,2048]{2,1,0:T(8,128)(2,1)S(1)}, bf16[1,384,2048]{2,1,0:T(8,128)(2,1)}, u32[]{:S(2)}) copy-start(bf16[1,384,2048]{2,1,0:T(8,128)(2,1)} %param.12) | copy-start | bytes 4718596
  35.4 28.0 %copy-start.3 = (bf16[1,2048,384]{2,1,0:T(8,128)(2,1)S(1)}, bf16[1,2048,384]{2,1,0:T(8,128)(2,1)}, u32[]{:S(2)}) copy-start(bf16[1,2048,384]{2,1,0:T(8,128)(2,1)} %param.10) | copy-start | bytes 4718596
  35.4 22.0 %collective-permute-start.7 = (bf16[112,1024]{1,0:T(8,128)(2,1)S(1)}, bf16[112,1024]{1,0:T(8,128)(2,1)S(1)}, u32[]{:S(2)}, u32[]{:S(2)}) collective-permute-start(bf16[112,1024]{1,0:T(8,128)(2,1)S(1)} %get-tuple-element.104), channel_id=1, source_target_pairs={{0,2},{2,0},{4,6},{6,4},{8,10},{10,8},{12,14},{14,12},{1,3},{3,1},... | collective-permute-start | bytes 688136 | tf_op jit(solution)/shard_map/ppermute | solution.py:239
  37.4 19.9 %collective-permute-start.11 = (bf16[96,1024]{1,0:T(8,128)(2,1)S(1)}, bf16[96,1024]{1,0:T(8,128)(2,1)S(1)}, u32[]{:S(2)}, u32[]{:S(2)}) collective-permute-start(bf16[96,1024]{1,0:T(8,128)(2,1)S(1)} %shard_map.123), channel_id=1, source_target_pairs={{0,2},{2,0},{4,6},{6,4},{8,10},{10,8},{12,14},{14,12},{1,3},{3,1},... | collective-permute-start | bytes 589832 | tf_op jit(solution)/shard_map/ppermute | solution.py:239
  58.1 10.9 %copy-start.7 = (bf16[896,1024]{1,0:T(8,128)(2,1)}, bf16[896,1024]{1,0:T(8,128)(2,1)S(1)}, u32[]{:S(2)}) copy-start(bf16[896,1024]{1,0:T(8,128)(2,1)S(1)} %get-tuple-element.172.own) | copy-start | bytes 5505028
  58.2 5.1 %collective-permute-start.12 = (bf16[896,1024]{1,0:T(8,128)(2,1)S(1)}, bf16[896,1024]{1,0:T(8,128)(2,1)S(1)}, u32[]{:S(2)}, u32[]{:S(2)}) collective-permute-start(bf16[896,1024]{1,0:T(8,128)(2,1)S(1)} %get-tuple-element.172.own), channel_id=1, source_target_pairs={{0,1},{1,0},{2,3},{3,2},{4,5},{5,4},{6,7},{7,6},{8,9},{9,8},{10,11... | collective-permute-start | bytes 5505032 | tf_op jit(solution)/shard_map/ppermute | solution.py:248
  59.9 9.2 %collective-permute-start.13 = (bf16[96,1024]{1,0:T(8,128)(2,1)S(1)}, bf16[96,1024]{1,0:T(8,128)(2,1)S(1)}, u32[]{:S(2)}, u32[]{:S(2)}) collective-permute-start(bf16[96,1024]{1,0:T(8,128)(2,1)S(1)} %shard_map.124), channel_id=1, source_target_pairs={{0,2},{2,0},{4,6},{6,4},{8,10},{10,8},{12,14},{14,12},{1,3},{3,1},... | collective-permute-start | bytes 589832 | tf_op jit(solution)/shard_map/ppermute | solution.py:239
  61.1 9.4 %collective-permute-start.14 = (bf16[96,1024]{1,0:T(8,128)(2,1)S(1)}, bf16[96,1024]{1,0:T(8,128)(2,1)S(1)}, u32[]{:S(2)}, u32[]{:S(2)}) collective-permute-start(bf16[96,1024]{1,0:T(8,128)(2,1)S(1)} %shard_map.125), channel_id=1, source_target_pairs={{0,2},{2,0},{4,6},{6,4},{8,10},{10,8},{12,14},{14,12},{1,3},{3,1},... | collective-permute-start | bytes 589832 | tf_op jit(solution)/shard_map/ppermute | solution.py:239
  63.3 5.7 %copy-start.9 = (bf16[896,1024]{1,0:T(8,128)(2,1)}, bf16[896,1024]{1,0:T(8,128)(2,1)S(1)}, u32[]{:S(2)}) copy-start(bf16[896,1024]{1,0:T(8,128)(2,1)S(1)} %collective-permute-done.12.other) | copy-start | bytes 5505028
  69.0 5.8 %copy-start.13 = (bf16[896,384]{1,0:T(8,128)(2,1)}, bf16[896,384]{1,0:T(8,128)(2,1)S(1)}, u32[]{:S(2)}) copy-start(bf16[896,384]{1,0:T(8,128)(2,1)S(1)} %get-tuple-element.124.refs_0_) | copy-start | bytes 2064388
  70.6 4.3 %collective-permute-start.15 = (bf16[896,1024]{1,0:T(8,128)(2,1)S(1)}, bf16[896,1024]{1,0:T(8,128)(2,1)S(1)}, u32[]{:S(2)}, u32[]{:S(2)}) collective-permute-start(bf16[896,1024]{1,0:T(8,128)(2,1)S(1)} %get-tuple-element.123), channel_id=1, source_target_pairs={{0,1},{1,0},{2,3},{3,2},{4,5},{5,4},{6,7},{7,6},{8,9},{9,8},{10,11... | collective-permute-start | bytes 5505032 | tf_op jit(solution)/shard_map/ppermute | solution.py:248
  72.5 8.5 %copy-start = (bf16[896,1024]{1,0:T(8,128)(2,1)}, bf16[896,1024]{1,0:T(8,128)(2,1)S(1)}, u32[]{:S(2)}) copy-start(bf16[896,1024]{1,0:T(8,128)(2,1)S(1)} %shard_map.129.own) | copy-start | bytes 5505028
  76.5 0.7 copy-start.23
  77.2 3.8 %copy-start.25 = (bf16[96,1024]{1,0:T(8,128)(2,1)}, bf16[96,1024]{1,0:T(8,128)(2,1)S(1)}, u32[]{:S(2)}) copy-start(bf16[96,1024]{1,0:T(8,128)(2,1)S(1)} %get-tuple-element.153) | copy-start | bytes 589828
  77.2 3.8 %collective-permute-start.16 = (bf16[896,1024]{1,0:T(8,128)(2,1)S(1)}, bf16[896,1024]{1,0:T(8,128)(2,1)S(1)}, u32[]{:S(2)}, u32[]{:S(2)}) collective-permute-start(bf16[896,1024]{1,0:T(8,128)(2,1)S(1)} %shard_map.129.own), channel_id=1, source_target_pairs={{0,1},{1,0},{2,3},{3,2},{4,5},{5,4},{6,7},{7,6},{8,9},{9,8},{10,11... | collective-permute-start | bytes 5505032 | tf_op jit(solution)/shard_map/ppermute | solution.py:248
  77.6 10.0 %collective-permute-start.17 = (bf16[96,1024]{1,0:T(8,128)(2,1)S(1)}, bf16[96,1024]{1,0:T(8,128)(2,1)S(1)}, u32[]{:S(2)}, u32[]{:S(2)}) collective-permute-start(bf16[96,1024]{1,0:T(8,128)(2,1)S(1)} %get-tuple-element.135), channel_id=1, source_target_pairs={{0,2},{2,0},{4,6},{6,4},{8,10},{10,8},{12,14},{14,12},{1,3},{3,1},... | collective-permute-start | bytes 589832 | tf_op jit(solution)/shard_map/ppermute | solution.py:239
  78.8 9.3 %collective-permute-start.18 = (bf16[96,1024]{1,0:T(8,128)(2,1)S(1)}, bf16[96,1024]{1,0:T(8,128)(2,1)S(1)}, u32[]{:S(2)}, u32[]{:S(2)}) collective-permute-start(bf16[96,1024]{1,0:T(8,128)(2,1)S(1)} %get-tuple-element.137), channel_id=1, source_target_pairs={{0,2},{2,0},{4,6},{6,4},{8,10},{10,8},{12,14},{14,12},{1,3},{3,1},... | collective-permute-start | bytes 589832 | tf_op jit(solution)/shard_map/ppermute | solution.py:239
  81.0 6.6 %copy-start.11 = (bf16[896,1024]{1,0:T(8,128)(2,1)}, bf16[896,1024]{1,0:T(8,128)(2,1)S(1)}, u32[]{:S(2)}) copy-start(bf16[896,1024]{1,0:T(8,128)(2,1)S(1)} %collective-permute-done.16.other) | copy-start | bytes 5505028
  87.6 4.5 %copy-start.21 = (f32[4,16,128]{2,1,0:T(8,128)}, f32[4,16,128]{2,1,0:T(8,128)S(1)}, u32[]{:S(2)}) copy-start(f32[4,16,128]{2,1,0:T(8,128)S(1)} %get-tuple-element.146.refs_4_) | copy-start | bytes 98308
  88.2 7.3 %collective-permute-start.19 = (bf16[896,1024]{1,0:T(8,128)(2,1)}, bf16[896,1024]{1,0:T(8,128)(2,1)}, u32[]{:S(2)}, u32[]{:S(2)}) collective-permute-start(bf16[896,1024]{1,0:T(8,128)(2,1)} %get-tuple-element.143), channel_id=1, source_target_pairs={{0,1},{1,0},{2,3},{3,2},{4,5},{5,4},{6,7},{7,6},{8,9},{9,8},{10,11... | collective-permute-start | bytes 5505032 | tf_op jit(solution)/shard_map/ppermute | solution.py:248
  90.6 4.8 %copy-start.26 = (s32[128,4]{0,1:T(4,128)S(1)}, s32[128,4]{0,1:T(4,128)}, u32[]{:S(2)}) copy-start(s32[128,4]{0,1:T(4,128)} %param.8) | copy-start | bytes 6148
  90.6 12.2 %collective-permute-start.21 = (bf16[128,1024]{1,0:T(8,128)(2,1)}, bf16[128,1024]{1,0:T(8,128)(2,1)}, u32[]{:S(2)}, u32[]{:S(2)}) collective-permute-start(bf16[128,1024]{1,0:T(8,128)(2,1)} %shard_map.132), channel_id=1, source_target_pairs={{0,12},{2,14},{4,0},{6,2},{8,4},{10,6},{12,8},{14,10},{1,13},{3,15... | collective-permute-start | bytes 786440 | tf_op jit(solution)/shard_map/ppermute | solution.py:242
  92.1 13.0 %collective-permute-start.22 = (bf16[128,1024]{1,0:T(8,128)(2,1)}, bf16[128,1024]{1,0:T(8,128)(2,1)}, u32[]{:S(2)}, u32[]{:S(2)}) collective-permute-start(bf16[128,1024]{1,0:T(8,128)(2,1)} %shard_map.133), channel_id=1, source_target_pairs={{0,4},{2,6},{4,8},{6,10},{8,12},{10,14},{12,0},{14,2},{1,5},{3,7},... | collective-permute-start | bytes 786440 | tf_op jit(solution)/shard_map/ppermute | solution.py:242
  94.2 8.6 %collective-permute-start.20 = (bf16[96,1024]{1,0:T(8,128)(2,1)}, bf16[96,1024]{1,0:T(8,128)(2,1)S(1)}, u32[]{:S(2)}, u32[]{:S(2)}) collective-permute-start(bf16[96,1024]{1,0:T(8,128)(2,1)} %copy-done.25), channel_id=1, source_target_pairs={{0,2},{2,0},{4,6},{6,4},{8,10},{10,8},{12,14},{14,12},{1,3},{3,1},... | collective-permute-start | bytes 589832 | tf_op jit(solution)/shard_map/ppermute | solution.py:239
  95.5 1.4 copy-start.4
  96.9 1.4 copy-start.6
  98.3 0.8 copy-start.22
  99.1 7.5 %copy-start.20 = (bf16[96,128]{1,0:T(8,128)(2,1)S(1)}, bf16[96,128]{1,0:T(8,128)(2,1)}, u32[]{:S(2)}) copy-start(bf16[96,128]{1,0:T(8,128)(2,1)} %copy-done.19) | copy-start | bytes 73732
  99.1 10.7 %copy-start.10 = (bf16[896,1024]{1,0:T(8,128)(2,1)S(1)}, bf16[896,1024]{1,0:T(8,128)(2,1)}, u32[]{:S(2)}) copy-start(bf16[896,1024]{1,0:T(8,128)(2,1)} %copy-done.9) | copy-start | bytes 5505028
  102.8 6.9 %copy-start.8 = (bf16[896,1024]{1,0:T(8,128)(2,1)S(1)}, bf16[896,1024]{1,0:T(8,128)(2,1)}, u32[]{:S(2)}) copy-start(bf16[896,1024]{1,0:T(8,128)(2,1)} %copy-done.7) | copy-start | bytes 5505028
  105.1 12.5 %collective-permute-start.23 = (bf16[112,1024]{1,0:T(8,128)(2,1)S(1)}, bf16[112,1024]{1,0:T(8,128)(2,1)S(1)}, u32[]{:S(2)}, u32[]{:S(2)}) collective-permute-start(bf16[112,1024]{1,0:T(8,128)(2,1)S(1)} %get-tuple-element.158), channel_id=1, source_target_pairs={{0,2},{2,0},{4,6},{6,4},{8,10},{10,8},{12,14},{14,12},{1,3},{3,1},... | collective-permute-start | bytes 688136 | tf_op jit(solution)/shard_map/ppermute | solution.py:239
  106.4 13.3 %collective-permute-start.26 = (bf16[112,1024]{1,0:T(8,128)(2,1)S(1)}, bf16[112,1024]{1,0:T(8,128)(2,1)S(1)}, u32[]{:S(2)}, u32[]{:S(2)}) collective-permute-start(bf16[112,1024]{1,0:T(8,128)(2,1)S(1)} %get-tuple-element.162), channel_id=1, source_target_pairs={{0,2},{2,0},{4,6},{6,4},{8,10},{10,8},{12,14},{14,12},{1,3},{3,1},... | collective-permute-start | bytes 688136 | tf_op jit(solution)/shard_map/ppermute | solution.py:239
  107.4 14.0 %collective-permute-start.27 = (bf16[128,1024]{1,0:T(8,128)(2,1)S(1)}, bf16[128,1024]{1,0:T(8,128)(2,1)S(1)}, u32[]{:S(2)}, u32[]{:S(2)}) collective-permute-start(bf16[128,1024]{1,0:T(8,128)(2,1)S(1)} %shard_map.137), channel_id=1, source_target_pairs={{0,8},{2,10},{4,12},{6,14},{8,0},{10,2},{12,4},{14,6},{1,9},{3,11}... | collective-permute-start | bytes 786440 | tf_op jit(solution)/shard_map/ppermute | solution.py:242
  110.0 3.5 %copy-start.1 = (bf16[896,1024]{1,0:T(8,128)(2,1)S(1)}, bf16[896,1024]{1,0:T(8,128)(2,1)}, u32[]{:S(2)}) copy-start(bf16[896,1024]{1,0:T(8,128)(2,1)} %copy-done) | copy-start | bytes 5505028
  110.0 3.5 %copy-start.12 = (bf16[896,1024]{1,0:T(8,128)(2,1)S(1)}, bf16[896,1024]{1,0:T(8,128)(2,1)}, u32[]{:S(2)}) copy-start(bf16[896,1024]{1,0:T(8,128)(2,1)} %copy-done.11) | copy-start | bytes 5505028
  113.5 1.1 copy-start.14
  117.6 2.1 %copy-start.18 = (bf16[96,128]{1,0:T(8,128)(2,1)S(1)}, bf16[96,128]{1,0:T(8,128)(2,1)}, u32[]{:S(2)}) copy-start(bf16[96,128]{1,0:T(8,128)(2,1)} %copy-done.17) | copy-start | bytes 73732
  118.4 7.1 %collective-permute-start.24 = (bf16[112,1024]{1,0:T(8,128)(2,1)S(1)}, bf16[112,1024]{1,0:T(8,128)(2,1)S(1)}, u32[]{:S(2)}, u32[]{:S(2)}) collective-permute-start(bf16[112,1024]{1,0:T(8,128)(2,1)S(1)} %get-tuple-element.160), channel_id=1, source_target_pairs={{0,2},{2,0},{4,6},{6,4},{8,10},{10,8},{12,14},{14,12},{1,3},{3,1},... | collective-permute-start | bytes 688136 | tf_op jit(solution)/shard_map/ppermute | solution.py:239
  120.5 5.0 %copy-start.24 = (bf16[96,1024]{1,0:T(8,128)(2,1)S(1)}, bf16[96,1024]{1,0:T(8,128)(2,1)}, u32[]{:S(2)}) copy-start(bf16[96,1024]{1,0:T(8,128)(2,1)} %copy-done.23) | copy-start | bytes 589828
  120.5 6.2 %copy-start.16 = (bf16[96,128]{1,0:T(8,128)(2,1)S(1)}, bf16[96,128]{1,0:T(8,128)(2,1)}, u32[]{:S(2)}) copy-start(bf16[96,128]{1,0:T(8,128)(2,1)} %copy-done.15) | copy-start | bytes 73732
  120.5 8.6 %collective-permute-start.28 = (bf16[112,1024]{1,0:T(8,128)(2,1)S(1)}, bf16[112,1024]{1,0:T(8,128)(2,1)S(1)}, u32[]{:S(2)}, u32[]{:S(2)}) collective-permute-start(bf16[112,1024]{1,0:T(8,128)(2,1)S(1)} %get-tuple-element.170), channel_id=1, source_target_pairs={{0,2},{2,0},{4,6},{6,4},{8,10},{10,8},{12,14},{14,12},{1,3},{3,1},... | collective-permute-start | bytes 688136 | tf_op jit(solution)/shard_map/ppermute | solution.py:239
  121.4 12.1 %collective-permute-start.31 = (bf16[144,1024]{1,0:T(8,128)(2,1)S(1)}, bf16[144,1024]{1,0:T(8,128)(2,1)S(1)}, u32[]{:S(2)}, u32[]{:S(2)}) collective-permute-start(bf16[144,1024]{1,0:T(8,128)(2,1)S(1)} %shard_map.136), channel_id=1, source_target_pairs={{0,4},{2,6},{4,8},{6,10},{8,12},{10,14},{12,0},{14,2},{1,5},{3,7},... | collective-permute-start | bytes 884744 | tf_op jit(solution)/shard_map/ppermute | solution.py:242
  122.5 23.1 %collective-permute-start.30 = (bf16[144,1024]{1,0:T(8,128)(2,1)S(1)}, bf16[144,1024]{1,0:T(8,128)(2,1)S(1)}, u32[]{:S(2)}, u32[]{:S(2)}) collective-permute-start(bf16[144,1024]{1,0:T(8,128)(2,1)S(1)} %shard_map.134), channel_id=1, source_target_pairs={{0,8},{2,10},{4,12},{6,14},{8,0},{10,2},{12,4},{14,6},{1,9},{3,11}... | collective-permute-start | bytes 884744 | tf_op jit(solution)/shard_map/ppermute | solution.py:242
  125.5 20.2 %collective-permute-start.25 = (bf16[96,1024]{1,0:T(8,128)(2,1)S(1)}, bf16[96,1024]{1,0:T(8,128)(2,1)S(1)}, u32[]{:S(2)}, u32[]{:S(2)}) collective-permute-start(bf16[96,1024]{1,0:T(8,128)(2,1)S(1)} %copy-done.24), channel_id=1, source_target_pairs={{0,2},{2,0},{4,6},{6,4},{8,10},{10,8},{12,14},{14,12},{1,3},{3,1},... | collective-permute-start | bytes 589832 | tf_op jit(solution)/shard_map/ppermute | solution.py:239
  127.5 22.9 %collective-permute-start.29 = (bf16[144,1024]{1,0:T(8,128)(2,1)S(1)}, bf16[144,1024]{1,0:T(8,128)(2,1)S(1)}, u32[]{:S(2)}, u32[]{:S(2)}) collective-permute-start(bf16[144,1024]{1,0:T(8,128)(2,1)S(1)} %shard_map.139), channel_id=1, source_target_pairs={{0,12},{2,14},{4,0},{6,2},{8,4},{10,6},{12,8},{14,10},{1,13},{3,15... | collective-permute-start | bytes 884744 | tf_op jit(solution)/shard_map/ppermute | solution.py:242
  150.5 2.2 %collective-permute-start.32 = (f32[128,4]{0,1:T(4,128)S(1)}, f32[128,4]{0,1:T(4,128)S(1)}, u32[]{:S(2)}, u32[]{:S(2)}) collective-permute-start(f32[128,4]{0,1:T(4,128)S(1)} %select_reduce_fusion), channel_id=1, source_target_pairs={{0,1},{1,0},{2,3},{3,2},{4,5},{5,4},{6,7},{7,6},{8,9},{9,8},{10,11... | collective-permute-start | bytes 6152 | tf_op jit(solution)/shard_map/ppermute | solution.py:248

commit v10 on v9

--- a/solution.py
+++ b/solution.py
@@ -325,8 +325,7 @@
     (grad_rows,) = local_call(
         functools.partial(grad_rows_kernel, *sizes), (half_rows,),
         (info, *[grad_blocks[k] for k in every], *[grad_compact[k] for k in every]))
-    grad_rows, out_packed = settle((grad_rows, out_packed))
-    grad_other = over_core(grad_rows)
+    grad_other, out_packed = settle((over_core(grad_rows), out_packed))
     grad_gate, grad_up, sent, dense_tails, compact_tails = local_call(
         functools.partial(backward_kernel, pieces, chunk, *sizes),
         (shape_of(hidden_rows), shape_of(hidden_rows), half_rows,
@@ -348,22 +347,20 @@
 
     sent, out_back = settle((sent, out_back))
     out_home = {k: to_home(k, out_dense, out_back) for k in near}
-    last, first_home = settle((out_packed[far], out_home[near[0]]))
-    out_back[far] = over_pair(last)
-    out_home[near[0]] = first_home
+    out_back[far] = over_pair(out_packed[far])
 
     def whole(own, other):
         return jnp.concatenate(
             [jnp.where(core == 0, own, other), jnp.where(core == 0, other, own)], axis=1)
 
-    came = over_core(sent)
+    came, out_back[far] = settle((over_core(sent), out_back[far]))
     out_came = {k: over_line(out_home[k], lines - k) for k in near}
     in_dense, *in_packed = local_call(
         functools.partial(join_kernel, *sizes, False),
         (shape_of((lines, token_count, half_width), F32),
          *[shape_of((padded + TAIL, half_width)) for _ in every]),
         (info, came, grad_gate, grad_up, gate_local, up_local, compact_tails))
-    in_packed, out_back[far], out_came = settle((in_packed, out_back[far], out_came))
+    in_packed, out_came = settle((in_packed, out_came))
     far_home = to_home(far, out_dense, out_back)
     out_came[far] = over_line(far_home, lines - far)
     in_back, in_home, sequence = {}, {}, outward + [0]
@@ -373,7 +370,7 @@
             packed, _ = settle((packed, in_home[sequence[i - 2]]))
         in_back[k] = over_pair(packed)
         in_home[k] = to_home(k, in_dense, in_back, dense_tails)
-    last, _ = settle((out_packed[0], in_back[sequence[2]]))
+    last, _ = settle((out_packed[0], in_back[sequence[1]]))
     out_back[0] = over_pair(last)
     ready, out_came = settle(({k: in_home[k] for k in sequence[:2]}, out_came))
     out_came[0] = to_home(0, out_dense, out_back)
@@ -385,7 +382,7 @@
     down_grad = dot(scaled, whole(grad_rows, grad_other), FIRST).astype(BF)
     in_home[sequence[0]], gate_grad = settle((in_home[sequence[0]], gate_grad))
     in_home[sequence[1]], down_grad = settle((in_home[sequence[1]], down_grad))
-    last_home, rows, grad_up = settle(([in_home[k] for k in outward], rows, grad_up))
+    last_home, layer_out, rows, grad_up = settle(([in_home[k] for k in outward], layer_out, rows, grad_up))
     in_home = {k: over_line(in_home[k], lines - k) if k else in_home[0] for k in every}
     input_grad = summed(in_home)
 

time: 154 us -> 153 us (level)
  starting transfers between devices: 39.2 us -> 42.1 us
  local copies, waits for them, and re-layouts: 5.19 us -> 2.51 us
    ppermute x16, waiting for transfers between devices: 7.72 us -> 19.9 us  [over_pair(): lax.ppermute(x, 'expert', [(i, i + 1 - 2 * (i % 2)) for i in range(expert...]
    ppermute x12, waiting for transfers between devices: 43.6 us -> 33 us  [over_line(): lax.ppermute(x, 'expert', [(i, (i // 2 + k) % lines * 2 + i % 2) for i in...]
    ppermute x5, starting transfers between devices: 5.25 us -> 9.89 us  [over_core(): return lax.ppermute(x, 'tensor', [(0, 1), (1, 0)])]
    unnamed x55 -> x57, local copies, waits for them, and re-layouts: 5.18 us -> 2.51 us
    ppermute x12, starting transfers between devices: 19 us -> 17 us  [over_line(): lax.ppermute(x, 'expert', [(i, (i // 2 + k) % lines * 2 + i % 2) for i in...]
    ppermute x5, waiting for transfers between devices: 6.2 us -> 4.18 us  [over_core(): return lax.ppermute(x, 'tensor', [(0, 1), (1, 0)])]
  transfers between devices with their start and end apart: 33 -> 33, of which waited for: 16 -> 13; matrix products, arithmetic and copies ran while one was open for 9% -> 9% of each run, Pallas kernels for 21% -> 22%
where the time goes in v10:
time: 153 us
  waiting for transfers between devices  57 us (37%)
  starting transfers between devices  42.1 us (28%)
  Pallas kernels  34.2 us (22%)
  matrix products  9.92 us (6%)
  other arithmetic  6.17 us (4%)
  local copies, waits for them, and re-layouts  2.51 us (2%)
    pallas_call x22, Pallas kernels, local_call(): pl.pallas_call(kernel, out_shape=tuple(outs), in_specs=[SMEM_SPEC] + [VME...  34.2 us
    ppermute x12, waiting for transfers between devices, over_line(): lax.ppermute(x, 'expert', [(i, (i // 2 + k) % lines * 2 + i % 2) for i in...  33 us
    ppermute x16, waiting for transfers between devices, over_pair(): lax.ppermute(x, 'expert', [(i, i + 1 - 2 * (i % 2)) for i in range(expert...  19.9 us
    ppermute x12, starting transfers between devices, over_line(): lax.ppermute(x, 'expert', [(i, (i // 2 + k) % lines * 2 + i % 2) for i in...  17 us
    ppermute x16, starting transfers between devices, over_pair(): lax.ppermute(x, 'expert', [(i, i + 1 - 2 * (i % 2)) for i in range(expert...  15.2 us
    dot_general x3, matrix products, dot(): lax.dot_general(a, b, (contract, ((), ())), preferred_element_type=F32)  9.92 us
    ppermute x5, starting transfers between devices, over_core(): return lax.ppermute(x, 'tensor', [(0, 1), (1, 0)])  9.89 us
    ppermute x5, waiting for transfers between devices, over_core(): return lax.ppermute(x, 'tensor', [(0, 1), (1, 0)])  4.18 us
  transfers between devices with their start and end apart: 33, of which 13 were waited for; matrix products, arithmetic and copies ran while one was open for 9% of the time, Pallas kernels for 22%

profile of v10, /device:TPU:9, one launch (start us, length us, event | category | flops | bytes accessed | tf_op | source)
XLA Modules:
  0.0 153.0 jit_solution(1193886802016502642)
XLA Ops:
  1.4 1.0 pad_maximum_fusion.1.block.refs_0_
  2.4 1.5 collective-permute-start
  3.9 4.1 %collective-permute-start.1 = (bf16[144,1024]{1,0:T(8,128)(2,1)S(1)}, bf16[144,1024]{1,0:T(8,128)(2,1)S(1)}, u32[]{:S(2)}, u32[]{:S(2)}) collective-permute-start(bf16[144,1024]{1,0:T(8,128)(2,1)S(1)} %pad_maximum_fusion.1.block.refs_0_), channel_id=1, source_target_pairs={{0,8},{2,10},{4,12},{6,14},{8,0},{10,2},{12,4},{14,6},{1,9},{3,11}... | collective-permute-start | bytes 884744 | tf_op jit(solution)/shard_map/ppermute | solution.py:242
  8.1 0.9 shard_map.118
  9.0 1.3 collective-permute-start.3
  10.3 0.9 shard_map.120
  11.2 1.3 collective-permute-start.5
  12.5 6.2 %collective-permute-done.block.refs_1_ = bf16[144,1024]{1,0:T(8,128)(2,1)S(1)} collective-permute-done((bf16[144,1024]{1,0:T(8,128)(2,1)S(1)}, bf16[144,1024]{1,0:T(8,128)(2,1)S(1)}, u32[]{:S(2)}, u32[]{:S(2)}) %collective-permute-start) | collective-permute-done | bytes 294944 | tf_op jit(solution)/shard_map/ppermute | solution.py:242
  18.7 0.9 shard_map.119
  19.6 1.3 collective-permute-start.4
  20.9 1.2 shard_map.121
  22.4 4.3 %collective-permute-done.6.refs_4_ = bf16[96,1024]{1,0:T(8,128)(2,1)S(1)} collective-permute-done((bf16[96,1024]{1,0:T(8,128)(2,1)S(1)}, bf16[96,1024]{1,0:T(8,128)(2,1)S(1)}, u32[]{:S(2)}, u32[]{:S(2)}) %collective-permute-start.6) | collective-permute-done | bytes 196640 | tf_op jit(solution)/shard_map/ppermute | solution.py:239
  26.7 1.5 collective-permute-done.1.block.refs_2_
  28.5 2.0 %collective-permute-start.10 = (bf16[128,1024]{1,0:T(8,128)(2,1)}, bf16[128,1024]{1,0:T(8,128)(2,1)S(1)}, u32[]{:S(2)}, u32[]{:S(2)}) collective-permute-start(bf16[128,1024]{1,0:T(8,128)(2,1)} %refs_0_), channel_id=1, source_target_pairs={{0,12},{2,14},{4,0},{6,2},{8,4},{10,6},{12,8},{14,10},{1,13},{3,15... | collective-permute-start | bytes 786440 | tf_op jit(solution)/shard_map/ppermute | solution.py:242
  30.5 2.3 %collective-permute-start.9 = (bf16[128,1024]{1,0:T(8,128)(2,1)}, bf16[128,1024]{1,0:T(8,128)(2,1)S(1)}, u32[]{:S(2)}, u32[]{:S(2)}) collective-permute-start(bf16[128,1024]{1,0:T(8,128)(2,1)} %refs_0_), channel_id=1, source_target_pairs={{0,8},{2,10},{4,12},{6,14},{8,0},{10,2},{12,4},{14,6},{1,9},{3,11}... | collective-permute-start | bytes 786440 | tf_op jit(solution)/shard_map/ppermute | solution.py:242
  32.8 0.9 shard_map.122
  33.7 1.3 collective-permute-start.7
  35.8 1.0 collective-permute-start.11
  36.8 4.5 %collective-permute-done.10.block.refs_3_ = bf16[128,1024]{1,0:T(8,128)(2,1)S(1)} collective-permute-done((bf16[128,1024]{1,0:T(8,128)(2,1)}, bf16[128,1024]{1,0:T(8,128)(2,1)S(1)}, u32[]{:S(2)}, u32[]{:S(2)}) %collective-permute-start.10) | collective-permute-done | bytes 262176 | tf_op jit(solution)/shard_map/ppermute | solution.py:242
  41.3 0.7 shard_map.125
  42.1 7.6 %collective-permute-done.9.block.refs_2_ = bf16[128,1024]{1,0:T(8,128)(2,1)S(1)} collective-permute-done((bf16[128,1024]{1,0:T(8,128)(2,1)}, bf16[128,1024]{1,0:T(8,128)(2,1)S(1)}, u32[]{:S(2)}, u32[]{:S(2)}) %collective-permute-start.9) | collective-permute-done | bytes 262176 | tf_op jit(solution)/shard_map/ppermute | solution.py:242
  49.7 0.7 shard_map.124
  50.5 0.8 shard_map.126
  51.3 7.0 %collective-permute-start.12 = (bf16[896,1024]{1,0:T(8,128)(2,1)S(1)}, bf16[896,1024]{1,0:T(8,128)(2,1)S(1)}, u32[]{:S(2)}, u32[]{:S(2)}) collective-permute-start(bf16[896,1024]{1,0:T(8,128)(2,1)S(1)} %get-tuple-element.162.own), channel_id=1, source_target_pairs={{0,1},{1,0},{2,3},{3,2},{4,5},{5,4},{6,7},{7,6},{8,9},{9,8},{10,11... | collective-permute-start | bytes 5505032 | tf_op jit(solution)/shard_map/ppermute | solution.py:248
  58.2 1.3 collective-permute-start.14
  59.7 1.9 %collective-permute-done.12.other = bf16[896,1024]{1,0:T(8,128)(2,1)S(1)} collective-permute-done((bf16[896,1024]{1,0:T(8,128)(2,1)S(1)}, bf16[896,1024]{1,0:T(8,128)(2,1)S(1)}, u32[]{:S(2)}, u32[]{:S(2)}) %collective-permute-start.12) | collective-permute-done | bytes 1835040 | tf_op jit(solution)/shard_map/ppermute | solution.py:248
  61.7 5.7 %shard_map.127 = (f32[896,384]{1,0:T(8,128)S(1)}, f32[896,384]{1,0:T(8,128)S(1)}, bf16[896,384]{1,0:T(8,128)(2,1)S(1)}, bf16[896,1024]{1,0:T(8,128)(2,1)S(1)}) custom-call(s32[3]{0:T(128)S(1)} %pad_add_fusion.info, bf16[896,1024]{1,0:T(8,128)(2,1)S(1)} %get-tuple-element.162.own, bf16[896,1024]{1,0:T(8,128)(2,1)S(1)} %collective-permute-done.12.other, ...), custom_call_target="tpu_custom_call" | custom-call | flops 1000 | bytes 1000 | tf_op jit(solution)/shard_map/pallas_call | solution.py:41
  67.4 1.5 %collective-permute-done.13.refs_6_ = bf16[96,1024]{1,0:T(8,128)(2,1)S(1)} collective-permute-done((bf16[96,1024]{1,0:T(8,128)(2,1)S(1)}, bf16[96,1024]{1,0:T(8,128)(2,1)S(1)}, u32[]{:S(2)}, u32[]{:S(2)}) %collective-permute-start.13) | collective-permute-done | bytes 196640 | tf_op jit(solution)/shard_map/ppermute | solution.py:239
  68.9 0.8 collective-permute-start.16
  69.8 1.1 shard_map.128.own
  71.0 2.2 %collective-permute-done.16.came = bf16[896,1024]{1,0:T(8,128)(2,1)S(1)} collective-permute-done((bf16[896,1024]{1,0:T(8,128)(2,1)S(1)}, bf16[896,1024]{1,0:T(8,128)(2,1)S(1)}, u32[]{:S(2)}, u32[]{:S(2)}) %collective-permute-start.16) | collective-permute-done | bytes 1835040 | tf_op jit(solution)/shard_map/ppermute | solution.py:248
  73.2 1.7 %shard_map.129 = (f32[4,128,1024]{2,1,0:T(8,128)S(1)}, bf16[96,1024]{1,0:T(8,128)(2,1)S(1)}, bf16[96,1024]{1,0:T(8,128)(2,1)S(1)}, bf16[96,1024]{1,0:T(8,128)(2,1)S(1)}, bf16[96,1024]{1,0:T(8,128)(2,1)S(1)}) custom-call(s32[3]{0:T(128)S(1)} %pad_add_fusion.info, bf16[896,1024]{1,0:T(8,128)(2,1)S(1)} %collective-permute-done.16.came, ...), custom_call_target="tpu_custom_call" | custom-call | flops 1000 | bytes 1000 | tf_op jit(solution)/shard_map/pallas_call | solution.py:41
  74.9 1.3 collective-permute-start.17
  76.5 6.6 %shard_map.130 = (bf16[896,384]{1,0:T(8,128)(2,1)S(1)}, bf16[896,384]{1,0:T(8,128)(2,1)S(1)}, bf16[896,1024]{1,0:T(8,128)(2,1)}, f32[4,16,128]{2,1,0:T(8,128)S(1)}, f32[4,16,128]{2,1,0:T(8,128)S(1)}) custom-call(s32[3]{0:T(128)S(1)} %pad_add_fusion.info, bf16[896,1024]{1,0:T(8,128)(2,1)S(1)} %shard_map.128.own, ...), custom_call_target="tpu_custom_call" | custom-call | flops 1000 | bytes 1000 | tf_op jit(solution)/shard_map/pallas_call | solution.py:41
  83.1 2.2 %collective-permute-done.18.back = bf16[96,1024]{1,0:T(8,128)(2,1)S(1)} collective-permute-done((bf16[96,1024]{1,0:T(8,128)(2,1)S(1)}, bf16[96,1024]{1,0:T(8,128)(2,1)S(1)}, u32[]{:S(2)}, u32[]{:S(2)}) %collective-permute-start.18) | collective-permute-done | bytes 196640 | tf_op jit(solution)/shard_map/ppermute | solution.py:239
  85.3 1.2 collective-permute-start.19
  86.5 1.5 shard_map.133
  88.0 2.1 %collective-permute-start.22 = (bf16[128,1024]{1,0:T(8,128)(2,1)}, bf16[128,1024]{1,0:T(8,128)(2,1)}, u32[]{:S(2)}, u32[]{:S(2)}) collective-permute-start(bf16[128,1024]{1,0:T(8,128)(2,1)} %shard_map.133), channel_id=1, source_target_pairs={{0,4},{2,6},{4,8},{6,10},{8,12},{10,14},{12,0},{14,2},{1,5},{3,7},... | collective-permute-start | bytes 786440 | tf_op jit(solution)/shard_map/ppermute | solution.py:242
  90.1 1.5 shard_map.132
  91.6 1.3 collective-permute-start.20
  92.9 5.3 %collective-permute-done.20.back = bf16[96,1024]{1,0:T(8,128)(2,1)S(1)} collective-permute-done((bf16[96,1024]{1,0:T(8,128)(2,1)}, bf16[96,1024]{1,0:T(8,128)(2,1)S(1)}, u32[]{:S(2)}, u32[]{:S(2)}) %collective-permute-start.20) | collective-permute-done | bytes 196640 | tf_op jit(solution)/shard_map/ppermute | solution.py:239
  98.2 0.7 copy-done.20
  98.9 0.8 shard_map.136
  99.7 1.2 collective-permute-start.25
  100.9 1.4 copy-done.6
  102.4 3.8 %shard_map.131 = (f32[4,128,1024]{2,1,0:T(8,128)S(1)}, bf16[112,1024]{1,0:T(8,128)(2,1)S(1)}, bf16[112,1024]{1,0:T(8,128)(2,1)S(1)}, bf16[112,1024]{1,0:T(8,128)(2,1)S(1)}, bf16[112,1024]{1,0:T(8,128)(2,1)S(1)}) custom-call(s32[3]{0:T(128)S(1)} %pad_add_fusion.info, bf16[896,1024]{1,0:T(8,128)(2,1)} %collective-permute-done.19.came, ...), custom_call_target="tpu_custom_call" | custom-call | flops 1000 | bytes 1000 | tf_op jit(solution)/shard_map/pallas_call | solution.py:41
  106.2 1.3 collective-permute-start.23
  108.4 3.5 %convolution_convert_fusion.1 = bf16[2048,384]{1,0:T(8,128)(2,1)} fusion(bf16[896,384]{1,0:T(8,128)(2,1)S(1)} %get-tuple-element.144.refs_0_, bf16[896,1024]{1,0:T(8,128)(2,1)S(1)} %get-tuple-element.193, bf16[896,1024]{1,0:T(8,128)(2,1)S(1)} %get-tuple-element.192), kind=kOutput, calls=%fused_computation.7 | convolution fusion | flops 1417412608 | bytes 5931008 | tf_op jit(solution)/shard_map/dot_general | solution.py:24
  111.9 3.0 %fusion.4 = bf16[384,2048]{1,0:T(8,128)(2,1)} fusion(bf16[896,384]{1,0:T(8,128)(2,1)S(1)} %copy-done.14, bf16[896,1024]{1,0:T(8,128)(2,1)S(1)} %get-tuple-element.191, bf16[896,1024]{1,0:T(8,128)(2,1)S(1)} %get-tuple-element.190), kind=kOutput, calls=%fused_computation.5 | convolution fusion | flops 1417412608 | bytes 5931008 | tf_op jit(solution)/shard_map/dot_general | solution.py:24
  114.9 2.1 %collective-permute-done.24.back = bf16[112,1024]{1,0:T(8,128)(2,1)S(1)} collective-permute-done((bf16[112,1024]{1,0:T(8,128)(2,1)S(1)}, bf16[112,1024]{1,0:T(8,128)(2,1)S(1)}, u32[]{:S(2)}, u32[]{:S(2)}) %collective-permute-start.24) | collective-permute-done | bytes 229408 | tf_op jit(solution)/shard_map/ppermute | solution.py:239
  117.0 1.2 collective-permute-start.27
  118.6 0.8 shard_map.134
  119.7 0.8 shard_map.135
  120.5 1.3 collective-permute-start.28
  121.8 2.9 %collective-permute-start.30 = (bf16[144,1024]{1,0:T(8,128)(2,1)S(1)}, bf16[144,1024]{1,0:T(8,128)(2,1)S(1)}, u32[]{:S(2)}, u32[]{:S(2)}) collective-permute-start(bf16[144,1024]{1,0:T(8,128)(2,1)S(1)} %shard_map.134), channel_id=1, source_target_pairs={{0,8},{2,10},{4,12},{6,14},{8,0},{10,2},{12,4},{14,6},{1,9},{3,11}... | collective-permute-start | bytes 884744 | tf_op jit(solution)/shard_map/ppermute | solution.py:242
  124.7 0.8 shard_map.138
  125.5 1.9 %add_convert_fusion.1 = bf16[128,1024]{1,0:T(8,128)(2,1)} fusion(bf16[128,1024]{1,0:T(8,128)(2,1)} %collective-permute-done.22, bf16[128,1024]{1,0:T(8,128)(2,1)S(1)} %collective-permute-done.25, bf16[128,1024]{1,0:T(8,128)(2,1)} %collective-permute-done.21, bf16[128,1024]{1,0:T(8,128)(2,1)S(1)} %shard_map.138), kind=kLoop, calls=%fused_computation.14 | loop fusion | flops 1048576 | bytes 1310720 | tf_op jit(solution)/shard_map/convert_element_type | solution.py:346
  127.4 4.5 %collective-permute-done.28.back = bf16[112,1024]{1,0:T(8,128)(2,1)S(1)} collective-permute-done((bf16[112,1024]{1,0:T(8,128)(2,1)S(1)}, bf16[112,1024]{1,0:T(8,128)(2,1)S(1)}, u32[]{:S(2)}, u32[]{:S(2)}) %collective-permute-start.28) | collective-permute-done | bytes 229408 | tf_op jit(solution)/shard_map/ppermute | solution.py:239
  131.9 0.8 shard_map.139
  132.7 0.8 shard_map.137
  134.1 3.5 %fusion.7 = bf16[1,2048,384]{2,1,0:T(8,128)(2,1)} fusion(bf16[896,2048]{1,0:T(8,128)(2,1)S(1)} %pad_maximum_fusion, bf16[896,384]{1,0:T(8,128)(2,1)S(1)} %get-tuple-element.180.refs_1_), kind=kOutput, calls=%fused_computation.8 | convolution fusion | flops 1410072576 | bytes 5931008 | tf_op jit(solution)/shard_map/dot_general | solution.py:24
  137.7 13.0 %collective-permute-done.29 = bf16[144,1024]{1,0:T(8,128)(2,1)S(1)} collective-permute-done((bf16[144,1024]{1,0:T(8,128)(2,1)S(1)}, bf16[144,1024]{1,0:T(8,128)(2,1)S(1)}, u32[]{:S(2)}, u32[]{:S(2)}) %collective-permute-start.29) | collective-permute-done | bytes 294944 | tf_op jit(solution)/shard_map/ppermute | solution.py:242
  150.8 0.8 collective-permute-start.32
  151.6 0.9 add_convert_fusion
  (111 shorter events, 5.9 us)
Async XLA Ops:
  2.4 7.9 %collective-permute-start.2 = (bf16[144,1024]{1,0:T(8,128)(2,1)S(1)}, bf16[144,1024]{1,0:T(8,128)(2,1)S(1)}, u32[]{:S(2)}, u32[]{:S(2)}) collective-permute-start(bf16[144,1024]{1,0:T(8,128)(2,1)S(1)} %pad_maximum_fusion.1.block.refs_0_), channel_id=1, source_target_pairs={{0,12},{2,14},{4,0},{6,2},{8,4},{10,6},{12,8},{14,10},{1,13},{3,15... | collective-permute-start | bytes 884744 | tf_op jit(solution)/shard_map/ppermute | solution.py:242
  2.4 16.3 %collective-permute-start = (bf16[144,1024]{1,0:T(8,128)(2,1)S(1)}, bf16[144,1024]{1,0:T(8,128)(2,1)S(1)}, u32[]{:S(2)}, u32[]{:S(2)}) collective-permute-start(bf16[144,1024]{1,0:T(8,128)(2,1)S(1)} %pad_maximum_fusion.1.block.refs_0_), channel_id=1, source_target_pairs={{0,4},{2,6},{4,8},{6,10},{8,12},{10,14},{12,0},{14,2},{1,5},{3,7},... | collective-permute-start | bytes 884744 | tf_op jit(solution)/shard_map/ppermute | solution.py:242
  3.9 24.3 %collective-permute-start.1 = (bf16[144,1024]{1,0:T(8,128)(2,1)S(1)}, bf16[144,1024]{1,0:T(8,128)(2,1)S(1)}, u32[]{:S(2)}, u32[]{:S(2)}) collective-permute-start(bf16[144,1024]{1,0:T(8,128)(2,1)S(1)} %pad_maximum_fusion.1.block.refs_0_), channel_id=1, source_target_pairs={{0,8},{2,10},{4,12},{6,14},{8,0},{10,2},{12,4},{14,6},{1,9},{3,11}... | collective-permute-start | bytes 884744 | tf_op jit(solution)/shard_map/ppermute | solution.py:242
  9.0 17.7 %collective-permute-start.3 = (bf16[112,1024]{1,0:T(8,128)(2,1)S(1)}, bf16[112,1024]{1,0:T(8,128)(2,1)S(1)}, u32[]{:S(2)}, u32[]{:S(2)}) collective-permute-start(bf16[112,1024]{1,0:T(8,128)(2,1)S(1)} %get-tuple-element.94), channel_id=1, source_target_pairs={{0,2},{2,0},{4,6},{6,4},{8,10},{10,8},{12,14},{14,12},{1,3},{3,1},... | collective-permute-start | bytes 688136 | tf_op jit(solution)/shard_map/ppermute | solution.py:239
  10.3 51.4 %copy-start.5 = (bf16[1,2048,384]{2,1,0:T(8,128)(2,1)S(1)}, bf16[1,2048,384]{2,1,0:T(8,128)(2,1)}, u32[]{:S(2)}) copy-start(bf16[1,2048,384]{2,1,0:T(8,128)(2,1)} %param.11) | copy-start | bytes 4718596
  11.2 75.3 %copy-start.17 = (bf16[96,128]{1,0:T(8,128)(2,1)}, bf16[96,128]{1,0:T(8,128)(2,1)S(1)}, u32[]{:S(2)}) copy-start(bf16[96,128]{1,0:T(8,128)(2,1)S(1)} %get-tuple-element.105.place) | copy-start | bytes 73732
  11.2 17.0 %collective-permute-start.5 = (bf16[112,1024]{1,0:T(8,128)(2,1)S(1)}, bf16[112,1024]{1,0:T(8,128)(2,1)S(1)}, u32[]{:S(2)}, u32[]{:S(2)}) collective-permute-start(bf16[112,1024]{1,0:T(8,128)(2,1)S(1)} %get-tuple-element.96), channel_id=1, source_target_pairs={{0,2},{2,0},{4,6},{6,4},{8,10},{10,8},{12,14},{14,12},{1,3},{3,1},... | collective-permute-start | bytes 688136 | tf_op jit(solution)/shard_map/ppermute | solution.py:239
  19.6 70.5 %copy-start.15 = (bf16[96,128]{1,0:T(8,128)(2,1)}, bf16[96,128]{1,0:T(8,128)(2,1)S(1)}, u32[]{:S(2)}) copy-start(bf16[96,128]{1,0:T(8,128)(2,1)S(1)} %get-tuple-element.103.place) | copy-start | bytes 73732
  19.6 8.6 %collective-permute-start.4 = (bf16[112,1024]{1,0:T(8,128)(2,1)S(1)}, bf16[112,1024]{1,0:T(8,128)(2,1)S(1)}, u32[]{:S(2)}, u32[]{:S(2)}) collective-permute-start(bf16[112,1024]{1,0:T(8,128)(2,1)S(1)} %get-tuple-element.95), channel_id=1, source_target_pairs={{0,2},{2,0},{4,6},{6,4},{8,10},{10,8},{12,14},{14,12},{1,3},{3,1},... | collective-permute-start | bytes 688136 | tf_op jit(solution)/shard_map/ppermute | solution.py:239
  22.1 4.6 %collective-permute-start.6 = (bf16[96,1024]{1,0:T(8,128)(2,1)S(1)}, bf16[96,1024]{1,0:T(8,128)(2,1)S(1)}, u32[]{:S(2)}, u32[]{:S(2)}) collective-permute-start(bf16[96,1024]{1,0:T(8,128)(2,1)S(1)} %shard_map.121), channel_id=1, source_target_pairs={{0,2},{2,0},{4,6},{6,4},{8,10},{10,8},{12,14},{14,12},{1,3},{3,1},... | collective-permute-start | bytes 589832 | tf_op jit(solution)/shard_map/ppermute | solution.py:239
  28.2 6.8 %collective-permute-start.8 = (bf16[128,1024]{1,0:T(8,128)(2,1)}, bf16[128,1024]{1,0:T(8,128)(2,1)S(1)}, u32[]{:S(2)}, u32[]{:S(2)}) collective-permute-start(bf16[128,1024]{1,0:T(8,128)(2,1)} %refs_0_), channel_id=1, source_target_pairs={{0,4},{2,6},{4,8},{6,10},{8,12},{10,14},{12,0},{14,2},{1,5},{3,7},... | collective-permute-start | bytes 786440 | tf_op jit(solution)/shard_map/ppermute | solution.py:242
  28.5 12.8 %collective-permute-start.10 = (bf16[128,1024]{1,0:T(8,128)(2,1)}, bf16[128,1024]{1,0:T(8,128)(2,1)S(1)}, u32[]{:S(2)}, u32[]{:S(2)}) collective-permute-start(bf16[128,1024]{1,0:T(8,128)(2,1)} %refs_0_), channel_id=1, source_target_pairs={{0,12},{2,14},{4,0},{6,2},{8,4},{10,6},{12,8},{14,10},{1,13},{3,15... | collective-permute-start | bytes 786440 | tf_op jit(solution)/shard_map/ppermute | solution.py:242
  30.5 19.2 %collective-permute-start.9 = (bf16[128,1024]{1,0:T(8,128)(2,1)}, bf16[128,1024]{1,0:T(8,128)(2,1)S(1)}, u32[]{:S(2)}, u32[]{:S(2)}) collective-permute-start(bf16[128,1024]{1,0:T(8,128)(2,1)} %refs_0_), channel_id=1, source_target_pairs={{0,8},{2,10},{4,12},{6,14},{8,0},{10,2},{12,4},{14,6},{1,9},{3,11}... | collective-permute-start | bytes 786440 | tf_op jit(solution)/shard_map/ppermute | solution.py:242
  33.7 16.8 %copy-start.19 = (bf16[96,128]{1,0:T(8,128)(2,1)}, bf16[96,128]{1,0:T(8,128)(2,1)S(1)}, u32[]{:S(2)}) copy-start(bf16[96,128]{1,0:T(8,128)(2,1)S(1)} %get-tuple-element.104.place) | copy-start | bytes 73732
  33.7 28.0 %copy-start.2 = (bf16[1,384,2048]{2,1,0:T(8,128)(2,1)S(1)}, bf16[1,384,2048]{2,1,0:T(8,128)(2,1)}, u32[]{:S(2)}) copy-start(bf16[1,384,2048]{2,1,0:T(8,128)(2,1)} %param.12) | copy-start | bytes 4718596
  33.7 28.0 %copy-start.3 = (bf16[1,2048,384]{2,1,0:T(8,128)(2,1)S(1)}, bf16[1,2048,384]{2,1,0:T(8,128)(2,1)}, u32[]{:S(2)}) copy-start(bf16[1,2048,384]{2,1,0:T(8,128)(2,1)} %param.10) | copy-start | bytes 4718596
  33.7 16.7 %collective-permute-start.7 = (bf16[112,1024]{1,0:T(8,128)(2,1)S(1)}, bf16[112,1024]{1,0:T(8,128)(2,1)S(1)}, u32[]{:S(2)}, u32[]{:S(2)}) collective-permute-start(bf16[112,1024]{1,0:T(8,128)(2,1)S(1)} %get-tuple-element.100), channel_id=1, source_target_pairs={{0,2},{2,0},{4,6},{6,4},{8,10},{10,8},{12,14},{14,12},{1,3},{3,1},... | collective-permute-start | bytes 688136 | tf_op jit(solution)/shard_map/ppermute | solution.py:239
  35.8 14.7 %collective-permute-start.11 = (bf16[96,1024]{1,0:T(8,128)(2,1)S(1)}, bf16[96,1024]{1,0:T(8,128)(2,1)S(1)}, u32[]{:S(2)}, u32[]{:S(2)}) collective-permute-start(bf16[96,1024]{1,0:T(8,128)(2,1)S(1)} %shard_map.123), channel_id=1, source_target_pairs={{0,2},{2,0},{4,6},{6,4},{8,10},{10,8},{12,14},{14,12},{1,3},{3,1},... | collective-permute-start | bytes 589832 | tf_op jit(solution)/shard_map/ppermute | solution.py:239
  51.3 16.1 %copy-start.7 = (bf16[896,1024]{1,0:T(8,128)(2,1)}, bf16[896,1024]{1,0:T(8,128)(2,1)S(1)}, u32[]{:S(2)}) copy-start(bf16[896,1024]{1,0:T(8,128)(2,1)S(1)} %get-tuple-element.162.own) | copy-start | bytes 5505028
  51.3 10.4 %collective-permute-start.12 = (bf16[896,1024]{1,0:T(8,128)(2,1)S(1)}, bf16[896,1024]{1,0:T(8,128)(2,1)S(1)}, u32[]{:S(2)}, u32[]{:S(2)}) collective-permute-start(bf16[896,1024]{1,0:T(8,128)(2,1)S(1)} %get-tuple-element.162.own), channel_id=1, source_target_pairs={{0,1},{1,0},{2,3},{3,2},{4,5},{5,4},{6,7},{7,6},{8,9},{9,8},{10,11... | collective-permute-start | bytes 5505032 | tf_op jit(solution)/shard_map/ppermute | solution.py:248
  58.2 9.2 %collective-permute-start.14 = (bf16[96,1024]{1,0:T(8,128)(2,1)S(1)}, bf16[96,1024]{1,0:T(8,128)(2,1)S(1)}, u32[]{:S(2)}, u32[]{:S(2)}) collective-permute-start(bf16[96,1024]{1,0:T(8,128)(2,1)S(1)} %shard_map.125), channel_id=1, source_target_pairs={{0,2},{2,0},{4,6},{6,4},{8,10},{10,8},{12,14},{14,12},{1,3},{3,1},... | collective-permute-start | bytes 589832 | tf_op jit(solution)/shard_map/ppermute | solution.py:239
  59.5 9.4 %collective-permute-start.13 = (bf16[96,1024]{1,0:T(8,128)(2,1)S(1)}, bf16[96,1024]{1,0:T(8,128)(2,1)S(1)}, u32[]{:S(2)}, u32[]{:S(2)}) collective-permute-start(bf16[96,1024]{1,0:T(8,128)(2,1)S(1)} %shard_map.124), channel_id=1, source_target_pairs={{0,2},{2,0},{4,6},{6,4},{8,10},{10,8},{12,14},{14,12},{1,3},{3,1},... | collective-permute-start | bytes 589832 | tf_op jit(solution)/shard_map/ppermute | solution.py:239
  61.7 5.7 %copy-start.9 = (bf16[896,1024]{1,0:T(8,128)(2,1)}, bf16[896,1024]{1,0:T(8,128)(2,1)S(1)}, u32[]{:S(2)}) copy-start(bf16[896,1024]{1,0:T(8,128)(2,1)S(1)} %collective-permute-done.12.other) | copy-start | bytes 5505028
  67.4 5.8 %copy-start.13 = (bf16[896,384]{1,0:T(8,128)(2,1)}, bf16[896,384]{1,0:T(8,128)(2,1)S(1)}, u32[]{:S(2)}) copy-start(bf16[896,384]{1,0:T(8,128)(2,1)S(1)} %get-tuple-element.132.refs_0_) | copy-start | bytes 2064388
  68.9 4.3 %collective-permute-start.16 = (bf16[896,1024]{1,0:T(8,128)(2,1)S(1)}, bf16[896,1024]{1,0:T(8,128)(2,1)S(1)}, u32[]{:S(2)}, u32[]{:S(2)}) collective-permute-start(bf16[896,1024]{1,0:T(8,128)(2,1)S(1)} %get-tuple-element.131), channel_id=1, source_target_pairs={{0,1},{1,0},{2,3},{3,2},{4,5},{5,4},{6,7},{7,6},{8,9},{9,8},{10,11... | collective-permute-start | bytes 5505032 | tf_op jit(solution)/shard_map/ppermute | solution.py:248
  70.9 5.6 %copy-start = (bf16[896,1024]{1,0:T(8,128)(2,1)}, bf16[896,1024]{1,0:T(8,128)(2,1)S(1)}, u32[]{:S(2)}) copy-start(bf16[896,1024]{1,0:T(8,128)(2,1)S(1)} %shard_map.128.own) | copy-start | bytes 5505028
  70.9 5.6 %collective-permute-start.15 = (bf16[896,1024]{1,0:T(8,128)(2,1)S(1)}, bf16[896,1024]{1,0:T(8,128)(2,1)S(1)}, u32[]{:S(2)}, u32[]{:S(2)}) collective-permute-start(bf16[896,1024]{1,0:T(8,128)(2,1)S(1)} %shard_map.128.own), channel_id=1, source_target_pairs={{0,1},{1,0},{2,3},{3,2},{4,5},{5,4},{6,7},{7,6},{8,9},{9,8},{10,11... | collective-permute-start | bytes 5505032 | tf_op jit(solution)/shard_map/ppermute | solution.py:248
  74.9 1.6 %copy-start.26 = (bf16[96,1024]{1,0:T(8,128)(2,1)}, bf16[96,1024]{1,0:T(8,128)(2,1)S(1)}, u32[]{:S(2)}) copy-start(bf16[96,1024]{1,0:T(8,128)(2,1)S(1)} %get-tuple-element.142) | copy-start | bytes 589828
  74.9 8.2 %copy-start.24 = (bf16[96,1024]{1,0:T(8,128)(2,1)}, bf16[96,1024]{1,0:T(8,128)(2,1)S(1)}, u32[]{:S(2)}) copy-start(bf16[96,1024]{1,0:T(8,128)(2,1)S(1)} %get-tuple-element.171) | copy-start | bytes 589828
  74.9 8.2 %collective-permute-start.17 = (bf16[96,1024]{1,0:T(8,128)(2,1)S(1)}, bf16[96,1024]{1,0:T(8,128)(2,1)S(1)}, u32[]{:S(2)}, u32[]{:S(2)}) collective-permute-start(bf16[96,1024]{1,0:T(8,128)(2,1)S(1)} %get-tuple-element.134), channel_id=1, source_target_pairs={{0,2},{2,0},{4,6},{6,4},{8,10},{10,8},{12,14},{14,12},{1,3},{3,1},... | collective-permute-start | bytes 589832 | tf_op jit(solution)/shard_map/ppermute | solution.py:239
  76.2 9.1 %collective-permute-start.18 = (bf16[96,1024]{1,0:T(8,128)(2,1)S(1)}, bf16[96,1024]{1,0:T(8,128)(2,1)S(1)}, u32[]{:S(2)}, u32[]{:S(2)}) collective-permute-start(bf16[96,1024]{1,0:T(8,128)(2,1)S(1)} %get-tuple-element.136), channel_id=1, source_target_pairs={{0,2},{2,0},{4,6},{6,4},{8,10},{10,8},{12,14},{14,12},{1,3},{3,1},... | collective-permute-start | bytes 589832 | tf_op jit(solution)/shard_map/ppermute | solution.py:239
  76.5 6.6 %copy-start.11 = (bf16[896,1024]{1,0:T(8,128)(2,1)}, bf16[896,1024]{1,0:T(8,128)(2,1)S(1)}, u32[]{:S(2)}) copy-start(bf16[896,1024]{1,0:T(8,128)(2,1)S(1)} %collective-permute-done.15.other) | copy-start | bytes 5505028
  83.1 8.5 %copy-start.22 = (f32[4,16,128]{2,1,0:T(8,128)}, f32[4,16,128]{2,1,0:T(8,128)S(1)}, u32[]{:S(2)}) copy-start(f32[4,16,128]{2,1,0:T(8,128)S(1)} %get-tuple-element.146.refs_4_) | copy-start | bytes 98308
  85.3 12.9 %collective-permute-start.19 = (bf16[896,1024]{1,0:T(8,128)(2,1)}, bf16[896,1024]{1,0:T(8,128)(2,1)}, u32[]{:S(2)}, u32[]{:S(2)}) collective-permute-start(bf16[896,1024]{1,0:T(8,128)(2,1)} %get-tuple-element.141), channel_id=1, source_target_pairs={{0,1},{1,0},{2,3},{3,2},{4,5},{5,4},{6,7},{7,6},{8,9},{9,8},{10,11... | collective-permute-start | bytes 5505032 | tf_op jit(solution)/shard_map/ppermute | solution.py:248
  88.0 4.9 %copy-start.27 = (s32[128,4]{0,1:T(4,128)S(1)}, s32[128,4]{0,1:T(4,128)}, u32[]{:S(2)}) copy-start(s32[128,4]{0,1:T(4,128)} %param.8) | copy-start | bytes 6148
  88.0 18.1 %collective-permute-start.22 = (bf16[128,1024]{1,0:T(8,128)(2,1)}, bf16[128,1024]{1,0:T(8,128)(2,1)}, u32[]{:S(2)}, u32[]{:S(2)}) collective-permute-start(bf16[128,1024]{1,0:T(8,128)(2,1)} %shard_map.133), channel_id=1, source_target_pairs={{0,4},{2,6},{4,8},{6,10},{8,12},{10,14},{12,0},{14,2},{1,5},{3,7},... | collective-permute-start | bytes 786440 | tf_op jit(solution)/shard_map/ppermute | solution.py:242
  91.6 14.5 %collective-permute-start.21 = (bf16[128,1024]{1,0:T(8,128)(2,1)}, bf16[128,1024]{1,0:T(8,128)(2,1)}, u32[]{:S(2)}, u32[]{:S(2)}) collective-permute-start(bf16[128,1024]{1,0:T(8,128)(2,1)} %shard_map.132), channel_id=1, source_target_pairs={{0,12},{2,14},{4,0},{6,2},{8,4},{10,6},{12,8},{14,10},{1,13},{3,15... | collective-permute-start | bytes 786440 | tf_op jit(solution)/shard_map/ppermute | solution.py:242
  91.6 9.3 %copy-start.4 = (bf16[1,2048,384]{2,1,0:T(8,128)(2,1)S(1)}, bf16[1,2048,384]{2,1,0:T(8,128)(2,1)}, u32[]{:S(2)}) copy-start(bf16[1,2048,384]{2,1,0:T(8,128)(2,1)} %param.10) | copy-start | bytes 4718596
  91.6 6.6 %collective-permute-start.20 = (bf16[96,1024]{1,0:T(8,128)(2,1)}, bf16[96,1024]{1,0:T(8,128)(2,1)S(1)}, u32[]{:S(2)}, u32[]{:S(2)}) collective-permute-start(bf16[96,1024]{1,0:T(8,128)(2,1)} %copy-done.26), channel_id=1, source_target_pairs={{0,2},{2,0},{4,6},{6,4},{8,10},{10,8},{12,14},{14,12},{1,3},{3,1},... | collective-permute-start | bytes 589832 | tf_op jit(solution)/shard_map/ppermute | solution.py:239
  98.2 0.7 copy-start.20
  98.9 2.0 %copy-start.23 = (f32[4,16,128]{2,1,0:T(8,128)S(1)}, f32[4,16,128]{2,1,0:T(8,128)}, u32[]{:S(2)}) copy-start(f32[4,16,128]{2,1,0:T(8,128)} %copy-done.22) | copy-start | bytes 98308
  99.7 22.1 %collective-permute-start.25 = (bf16[128,1024]{1,0:T(8,128)(2,1)S(1)}, bf16[128,1024]{1,0:T(8,128)(2,1)S(1)}, u32[]{:S(2)}, u32[]{:S(2)}) collective-permute-start(bf16[128,1024]{1,0:T(8,128)(2,1)S(1)} %shard_map.136), channel_id=1, source_target_pairs={{0,8},{2,10},{4,12},{6,14},{8,0},{10,2},{12,4},{14,6},{1,9},{3,11}... | collective-permute-start | bytes 786440 | tf_op jit(solution)/shard_map/ppermute | solution.py:242
  100.9 1.4 copy-start.6
  102.4 5.3 %copy-start.1 = (bf16[896,1024]{1,0:T(8,128)(2,1)S(1)}, bf16[896,1024]{1,0:T(8,128)(2,1)}, u32[]{:S(2)}) copy-start(bf16[896,1024]{1,0:T(8,128)(2,1)} %copy-done) | copy-start | bytes 5505028
  102.4 5.3 %copy-start.12 = (bf16[896,1024]{1,0:T(8,128)(2,1)S(1)}, bf16[896,1024]{1,0:T(8,128)(2,1)}, u32[]{:S(2)}) copy-start(bf16[896,1024]{1,0:T(8,128)(2,1)} %copy-done.11) | copy-start | bytes 5505028
  106.1 1.8 %copy-start.8 = (bf16[896,1024]{1,0:T(8,128)(2,1)S(1)}, bf16[896,1024]{1,0:T(8,128)(2,1)}, u32[]{:S(2)}) copy-start(bf16[896,1024]{1,0:T(8,128)(2,1)} %copy-done.7) | copy-start | bytes 5505028
  106.1 2.0 %copy-start.10 = (bf16[896,1024]{1,0:T(8,128)(2,1)S(1)}, bf16[896,1024]{1,0:T(8,128)(2,1)}, u32[]{:S(2)}) copy-start(bf16[896,1024]{1,0:T(8,128)(2,1)} %copy-done.9) | copy-start | bytes 5505028
  106.2 12.4 %collective-permute-start.23 = (bf16[112,1024]{1,0:T(8,128)(2,1)S(1)}, bf16[112,1024]{1,0:T(8,128)(2,1)S(1)}, u32[]{:S(2)}, u32[]{:S(2)}) collective-permute-start(bf16[112,1024]{1,0:T(8,128)(2,1)S(1)} %get-tuple-element.155), channel_id=1, source_target_pairs={{0,2},{2,0},{4,6},{6,4},{8,10},{10,8},{12,14},{14,12},{1,3},{3,1},... | collective-permute-start | bytes 688136 | tf_op jit(solution)/shard_map/ppermute | solution.py:239
  107.5 9.5 %collective-permute-start.24 = (bf16[112,1024]{1,0:T(8,128)(2,1)S(1)}, bf16[112,1024]{1,0:T(8,128)(2,1)S(1)}, u32[]{:S(2)}, u32[]{:S(2)}) collective-permute-start(bf16[112,1024]{1,0:T(8,128)(2,1)S(1)} %get-tuple-element.157), channel_id=1, source_target_pairs={{0,2},{2,0},{4,6},{6,4},{8,10},{10,8},{12,14},{14,12},{1,3},{3,1},... | collective-permute-start | bytes 688136 | tf_op jit(solution)/shard_map/ppermute | solution.py:239
  108.4 3.5 %copy-start.14 = (bf16[896,384]{1,0:T(8,128)(2,1)S(1)}, bf16[896,384]{1,0:T(8,128)(2,1)}, u32[]{:S(2)}) copy-start(bf16[896,384]{1,0:T(8,128)(2,1)} %copy-done.13) | copy-start | bytes 2064388
  111.9 5.0 %copy-start.25 = (bf16[96,1024]{1,0:T(8,128)(2,1)S(1)}, bf16[96,1024]{1,0:T(8,128)(2,1)}, u32[]{:S(2)}) copy-start(bf16[96,1024]{1,0:T(8,128)(2,1)} %copy-done.24) | copy-start | bytes 589828
  114.9 3.7 %copy-start.21 = (bf16[96,128]{1,0:T(8,128)(2,1)S(1)}, bf16[96,128]{1,0:T(8,128)(2,1)}, u32[]{:S(2)}) copy-start(bf16[96,128]{1,0:T(8,128)(2,1)} %copy-done.19) | copy-start | bytes 73732
  117.0 7.7 %collective-permute-start.27 = (bf16[96,1024]{1,0:T(8,128)(2,1)S(1)}, bf16[96,1024]{1,0:T(8,128)(2,1)S(1)}, u32[]{:S(2)}, u32[]{:S(2)}) collective-permute-start(bf16[96,1024]{1,0:T(8,128)(2,1)S(1)} %copy-done.25), channel_id=1, source_target_pairs={{0,2},{2,0},{4,6},{6,4},{8,10},{10,8},{12,14},{14,12},{1,3},{3,1},... | collective-permute-start | bytes 589832 | tf_op jit(solution)/shard_map/ppermute | solution.py:239
  118.6 1.1 copy-start.18
  119.4 13.3 %collective-permute-start.26 = (bf16[112,1024]{1,0:T(8,128)(2,1)S(1)}, bf16[112,1024]{1,0:T(8,128)(2,1)S(1)}, u32[]{:S(2)}, u32[]{:S(2)}) collective-permute-start(bf16[112,1024]{1,0:T(8,128)(2,1)S(1)} %get-tuple-element.169), channel_id=1, source_target_pairs={{0,2},{2,0},{4,6},{6,4},{8,10},{10,8},{12,14},{14,12},{1,3},{3,1},... | collective-permute-start | bytes 688136 | tf_op jit(solution)/shard_map/ppermute | solution.py:239
  120.5 11.4 %collective-permute-start.28 = (bf16[112,1024]{1,0:T(8,128)(2,1)S(1)}, bf16[112,1024]{1,0:T(8,128)(2,1)S(1)}, u32[]{:S(2)}, u32[]{:S(2)}) collective-permute-start(bf16[112,1024]{1,0:T(8,128)(2,1)S(1)} %get-tuple-element.177), channel_id=1, source_target_pairs={{0,2},{2,0},{4,6},{6,4},{8,10},{10,8},{12,14},{14,12},{1,3},{3,1},... | collective-permute-start | bytes 688136 | tf_op jit(solution)/shard_map/ppermute | solution.py:239
  121.8 15.8 %collective-permute-start.31 = (bf16[144,1024]{1,0:T(8,128)(2,1)S(1)}, bf16[144,1024]{1,0:T(8,128)(2,1)S(1)}, u32[]{:S(2)}, u32[]{:S(2)}) collective-permute-start(bf16[144,1024]{1,0:T(8,128)(2,1)S(1)} %shard_map.135), channel_id=1, source_target_pairs={{0,4},{2,6},{4,8},{6,10},{8,12},{10,14},{12,0},{14,2},{1,5},{3,7},... | collective-permute-start | bytes 884744 | tf_op jit(solution)/shard_map/ppermute | solution.py:242
  121.8 15.8 %collective-permute-start.30 = (bf16[144,1024]{1,0:T(8,128)(2,1)S(1)}, bf16[144,1024]{1,0:T(8,128)(2,1)S(1)}, u32[]{:S(2)}, u32[]{:S(2)}) collective-permute-start(bf16[144,1024]{1,0:T(8,128)(2,1)S(1)} %shard_map.134), channel_id=1, source_target_pairs={{0,8},{2,10},{4,12},{6,14},{8,0},{10,2},{12,4},{14,6},{1,9},{3,11}... | collective-permute-start | bytes 884744 | tf_op jit(solution)/shard_map/ppermute | solution.py:242
  125.5 7.2 %copy-start.16 = (bf16[96,128]{1,0:T(8,128)(2,1)S(1)}, bf16[96,128]{1,0:T(8,128)(2,1)}, u32[]{:S(2)}) copy-start(bf16[96,128]{1,0:T(8,128)(2,1)} %copy-done.15) | copy-start | bytes 73732
  133.5 17.2 %collective-permute-start.29 = (bf16[144,1024]{1,0:T(8,128)(2,1)S(1)}, bf16[144,1024]{1,0:T(8,128)(2,1)S(1)}, u32[]{:S(2)}, u32[]{:S(2)}) collective-permute-start(bf16[144,1024]{1,0:T(8,128)(2,1)S(1)} %shard_map.137), channel_id=1, source_target_pairs={{0,12},{2,14},{4,0},{6,2},{8,4},{10,6},{12,8},{14,10},{1,13},{3,15... | collective-permute-start | bytes 884744 | tf_op jit(solution)/shard_map/ppermute | solution.py:242
  150.8 1.7 %collective-permute-start.32 = (f32[128,4]{0,1:T(4,128)S(1)}, f32[128,4]{0,1:T(4,128)S(1)}, u32[]{:S(2)}, u32[]{:S(2)}) collective-permute-start(f32[128,4]{0,1:T(4,128)S(1)} %select_reduce_fusion), channel_id=1, source_target_pairs={{0,1},{1,0},{2,3},{3,2},{4,5},{5,4},{6,7},{7,6},{8,9},{9,8},{10,11... | collective-permute-start | bytes 6152 | tf_op jit(solution)/shard_map/ppermute | solution.py:248

commit v11 on v10

--- a/solution.py
+++ b/solution.py
@@ -298,12 +298,12 @@
             grad_pack_kernel, (shape_of((padded, half_width)),), (info, grad_blocks[k], places[k]))[0]
 
     near, far = by_reach[:-1], by_reach[-1]
-    grad_packed = {k: grad_pack(k) for k in by_reach}
-    grad_compact = {k: over_pair(grad_packed[k]) for k in by_reach}
+    grad_packed = {k: grad_pack(k) for k in near}
+    grad_compact = {k: over_pair(grad_packed[k]) for k in near}
     grad_compact[0] = grad_first
-    ahead = {k: grad_compact[k] for k in near[:1]}
-    compact, grad_blocks, grad_packed, ahead = settle((compact, grad_blocks, grad_packed, ahead))
-    grad_compact.update(ahead)
+    compact, near_blocks, near_packed = settle(
+        (compact, {k: grad_blocks[k] for k in near}, grad_packed))
+    grad_blocks.update(near_blocks)
     rows, weights = local_call(
         functools.partial(token_rows_kernel, *sizes),
         (half_rows, shape_of((row_count, 1), F32)),
@@ -322,6 +322,8 @@
 
     outward = by_reach[::-1]
     out_back = {k: over_pair(out_packed[k]) for k in near}
+    grad_blocks[far], out_back = settle((grad_blocks[far], out_back))
+    grad_compact[far] = over_pair(grad_pack(far))
     (grad_rows,) = local_call(
         functools.partial(grad_rows_kernel, *sizes), (half_rows,),
         (info, *[grad_blocks[k] for k in every], *[grad_compact[k] for k in every]))
@@ -345,8 +347,9 @@
             total = total + blocks[k][:token_count].astype(F32)
         return total.astype(BF)
 
-    sent, out_back = settle((sent, out_back))
     out_home = {k: to_home(k, out_dense, out_back) for k in near}
+    out_came = {k: over_line(out_home[k], lines - k) for k in near}
+    sent, out_came = settle((sent, out_came))
     out_back[far] = over_pair(out_packed[far])
 
     def whole(own, other):

time: 153 us -> 165 us (1.078)
  waiting for transfers between devices: 57 us -> 69.4 us
    ppermute x16, waiting for transfers between devices: 19.9 us -> 26.3 us  [over_pair(): lax.ppermute(x, 'expert', [(i, i + 1 - 2 * (i % 2)) for i in range(expert...]
    ppermute x12, waiting for transfers between devices: 33 us -> 37.7 us  [over_line(): lax.ppermute(x, 'expert', [(i, (i // 2 + k) % lines * 2 + i % 2) for i in...]
    unnamed x57 -> x65, local copies, waits for them, and re-layouts: 2.51 us -> 3.83 us
  transfers between devices with their start and end apart: 33 -> 33, of which waited for: 13 -> 18; matrix products, arithmetic and copies ran while one was open for 9% -> 8% of each run, Pallas kernels for 22% -> 18%
where the time goes in v11:
time: 165 us
  waiting for transfers between devices  69.4 us (42%)
  starting transfers between devices  42.1 us (26%)
  Pallas kernels  32.9 us (20%)
  matrix products  9.82 us (6%)
  other arithmetic  5.37 us (3%)
  local copies, waits for them, and re-layouts  3.84 us (2%)
    ppermute x12, waiting for transfers between devices, over_line(): lax.ppermute(x, 'expert', [(i, (i // 2 + k) % lines * 2 + i % 2) for i in...  37.7 us
    pallas_call x22, Pallas kernels, local_call(): pl.pallas_call(kernel, out_shape=tuple(outs), in_specs=[SMEM_SPEC] + [VME...  32.9 us
    ppermute x16, waiting for transfers between devices, over_pair(): lax.ppermute(x, 'expert', [(i, i + 1 - 2 * (i % 2)) for i in range(expert...  26.3 us
    ppermute x12, starting transfers between devices, over_line(): lax.ppermute(x, 'expert', [(i, (i // 2 + k) % lines * 2 + i % 2) for i in...  15.5 us
    ppermute x16, starting transfers between devices, over_pair(): lax.ppermute(x, 'expert', [(i, i + 1 - 2 * (i % 2)) for i in range(expert...  15.2 us
    ppermute x5, starting transfers between devices, over_core(): return lax.ppermute(x, 'tensor', [(0, 1), (1, 0)])  11.4 us
    dot_general x3, matrix products, dot(): lax.dot_general(a, b, (contract, ((), ())), preferred_element_type=F32)  9.82 us
    ppermute x5, waiting for transfers between devices, over_core(): return lax.ppermute(x, 'tensor', [(0, 1), (1, 0)])  5.41 us
  transfers between devices with their start and end apart: 33, of which 18 were waited for; matrix products, arithmetic and copies ran while one was open for 8% of the time, Pallas kernels for 18%

profile of v11, /device:TPU:9, one launch (start us, length us, event | category | flops | bytes accessed | tf_op | source)
XLA Modules:
  0.0 164.5 jit_solution(16749883754005068505)
XLA Ops:
  1.4 1.0 pad_maximum_fusion.1.block.refs_0_
  2.4 1.5 collective-permute-start
  3.9 4.1 %collective-permute-start.1 = (bf16[144,1024]{1,0:T(8,128)(2,1)S(1)}, bf16[144,1024]{1,0:T(8,128)(2,1)S(1)}, u32[]{:S(2)}, u32[]{:S(2)}) collective-permute-start(bf16[144,1024]{1,0:T(8,128)(2,1)S(1)} %pad_maximum_fusion.1.block.refs_0_), channel_id=1, source_target_pairs={{0,8},{2,10},{4,12},{6,14},{8,0},{10,2},{12,4},{14,6},{1,9},{3,11}... | collective-permute-start | bytes 884744 | tf_op jit(solution)/shard_map/ppermute | solution.py:242
  8.1 0.9 shard_map.118
  9.0 1.3 collective-permute-start.3
  10.3 0.9 shard_map.120
  11.2 1.3 collective-permute-start.5
  12.5 6.2 %collective-permute-done.block.refs_1_ = bf16[144,1024]{1,0:T(8,128)(2,1)S(1)} collective-permute-done((bf16[144,1024]{1,0:T(8,128)(2,1)S(1)}, bf16[144,1024]{1,0:T(8,128)(2,1)S(1)}, u32[]{:S(2)}, u32[]{:S(2)}) %collective-permute-start) | collective-permute-done | bytes 294944 | tf_op jit(solution)/shard_map/ppermute | solution.py:242
  18.7 0.9 shard_map.119
  19.6 1.3 collective-permute-start.4
  20.9 1.3 shard_map.121
  22.5 4.3 %collective-permute-done.6.refs_4_ = bf16[96,1024]{1,0:T(8,128)(2,1)S(1)} collective-permute-done((bf16[96,1024]{1,0:T(8,128)(2,1)S(1)}, bf16[96,1024]{1,0:T(8,128)(2,1)S(1)}, u32[]{:S(2)}, u32[]{:S(2)}) %collective-permute-start.6) | collective-permute-done | bytes 196640 | tf_op jit(solution)/shard_map/ppermute | solution.py:239
  26.8 1.4 collective-permute-done.1.block.refs_2_
  28.2 2.2 %collective-permute-start.9 = (bf16[128,1024]{1,0:T(8,128)(2,1)}, bf16[128,1024]{1,0:T(8,128)(2,1)S(1)}, u32[]{:S(2)}, u32[]{:S(2)}) collective-permute-start(bf16[128,1024]{1,0:T(8,128)(2,1)} %refs_0_), channel_id=1, source_target_pairs={{0,12},{2,14},{4,0},{6,2},{8,4},{10,6},{12,8},{14,10},{1,13},{3,15... | collective-permute-start | bytes 786440 | tf_op jit(solution)/shard_map/ppermute | solution.py:242
  30.5 0.9 shard_map.122
  31.4 1.3 collective-permute-start.7
  32.7 1.4 collective-permute-done.9.block.refs_3_
  34.8 7.3 %collective-permute-done.8.block.refs_1_ = bf16[128,1024]{1,0:T(8,128)(2,1)S(1)} collective-permute-done((bf16[128,1024]{1,0:T(8,128)(2,1)}, bf16[128,1024]{1,0:T(8,128)(2,1)S(1)}, u32[]{:S(2)}, u32[]{:S(2)}) %collective-permute-start.8) | collective-permute-done | bytes 262176 | tf_op jit(solution)/shard_map/ppermute | solution.py:242
  43.7 5.9 %collective-permute-start.11 = (bf16[896,1024]{1,0:T(8,128)(2,1)S(1)}, bf16[896,1024]{1,0:T(8,128)(2,1)S(1)}, u32[]{:S(2)}, u32[]{:S(2)}) collective-permute-start(bf16[896,1024]{1,0:T(8,128)(2,1)S(1)} %get-tuple-element.156.own), channel_id=1, source_target_pairs={{0,1},{1,0},{2,3},{3,2},{4,5},{5,4},{6,7},{7,6},{8,9},{9,8},{10,11... | collective-permute-start | bytes 5505032 | tf_op jit(solution)/shard_map/ppermute | solution.py:248
  49.6 1.2 collective-permute-start.13
  51.1 1.9 %collective-permute-done.11.other = bf16[896,1024]{1,0:T(8,128)(2,1)S(1)} collective-permute-done((bf16[896,1024]{1,0:T(8,128)(2,1)S(1)}, bf16[896,1024]{1,0:T(8,128)(2,1)S(1)}, u32[]{:S(2)}, u32[]{:S(2)}) %collective-permute-start.11) | collective-permute-done | bytes 1835040 | tf_op jit(solution)/shard_map/ppermute | solution.py:248
  53.0 5.7 %shard_map.126 = (f32[896,384]{1,0:T(8,128)S(1)}, f32[896,384]{1,0:T(8,128)S(1)}, bf16[896,384]{1,0:T(8,128)(2,1)S(1)}, bf16[896,1024]{1,0:T(8,128)(2,1)S(1)}) custom-call(s32[3]{0:T(128)S(1)} %pad_add_fusion.info, bf16[896,1024]{1,0:T(8,128)(2,1)S(1)} %get-tuple-element.156.own, bf16[896,1024]{1,0:T(8,128)(2,1)S(1)} %collective-permute-done.11.other, ...), custom_call_target="tpu_custom_call" | custom-call | flops 1000 | bytes 1000 | tf_op jit(solution)/shard_map/pallas_call | solution.py:41
  58.8 1.5 collective-permute-done.12.refs_5_
  60.3 0.8 collective-permute-start.14
  61.2 3.4 %collective-permute-done.14.came = bf16[896,1024]{1,0:T(8,128)(2,1)S(1)} collective-permute-done((bf16[896,1024]{1,0:T(8,128)(2,1)S(1)}, bf16[896,1024]{1,0:T(8,128)(2,1)S(1)}, u32[]{:S(2)}, u32[]{:S(2)}) %collective-permute-start.14) | collective-permute-done | bytes 1835040 | tf_op jit(solution)/shard_map/ppermute | solution.py:248
  64.6 1.7 %shard_map.127 = (f32[4,128,1024]{2,1,0:T(8,128)S(1)}, bf16[96,1024]{1,0:T(8,128)(2,1)S(1)}, bf16[96,1024]{1,0:T(8,128)(2,1)S(1)}, bf16[96,1024]{1,0:T(8,128)(2,1)S(1)}, bf16[96,1024]{1,0:T(8,128)(2,1)S(1)}) custom-call(s32[3]{0:T(128)S(1)} %pad_add_fusion.info, bf16[896,1024]{1,0:T(8,128)(2,1)S(1)} %collective-permute-done.14.came, ...), custom_call_target="tpu_custom_call" | custom-call | flops 1000 | bytes 1000 | tf_op jit(solution)/shard_map/pallas_call | solution.py:41
  66.3 1.3 collective-permute-start.15
  67.8 5.2 %collective-permute-done.10.block.refs_2_ = bf16[128,1024]{1,0:T(8,128)(2,1)S(1)} collective-permute-done((bf16[128,1024]{1,0:T(8,128)(2,1)}, bf16[128,1024]{1,0:T(8,128)(2,1)S(1)}, u32[]{:S(2)}, u32[]{:S(2)}) %collective-permute-start.10) | collective-permute-done | bytes 262176 | tf_op jit(solution)/shard_map/ppermute | solution.py:242
  73.0 3.6 %collective-permute-done.16.back = bf16[96,1024]{1,0:T(8,128)(2,1)S(1)} collective-permute-done((bf16[96,1024]{1,0:T(8,128)(2,1)S(1)}, bf16[96,1024]{1,0:T(8,128)(2,1)S(1)}, u32[]{:S(2)}, u32[]{:S(2)}) %collective-permute-start.16) | collective-permute-done | bytes 196640 | tf_op jit(solution)/shard_map/ppermute | solution.py:239
  77.4 1.2 collective-permute-start.17
  78.6 4.0 %collective-permute-done.17.refs_6_ = bf16[96,1024]{1,0:T(8,128)(2,1)S(1)} collective-permute-done((bf16[96,1024]{1,0:T(8,128)(2,1)S(1)}, bf16[96,1024]{1,0:T(8,128)(2,1)S(1)}, u32[]{:S(2)}, u32[]{:S(2)}) %collective-permute-start.17) | collective-permute-done | bytes 196640 | tf_op jit(solution)/shard_map/ppermute | solution.py:239
  82.7 1.1 shard_map.129.own
  83.8 2.2 %collective-permute-start.18 = (bf16[896,1024]{1,0:T(8,128)(2,1)S(1)}, bf16[896,1024]{1,0:T(8,128)(2,1)S(1)}, u32[]{:S(2)}, u32[]{:S(2)}) collective-permute-start(bf16[896,1024]{1,0:T(8,128)(2,1)S(1)} %shard_map.129.own), channel_id=1, source_target_pairs={{0,1},{1,0},{2,3},{3,2},{4,5},{5,4},{6,7},{7,6},{8,9},{9,8},{10,11... | collective-permute-start | bytes 5505032 | tf_op jit(solution)/shard_map/ppermute | solution.py:248
  86.9 0.8 shard_map.131
  87.7 1.6 %collective-permute-start.19 = (bf16[128,1024]{1,0:T(8,128)(2,1)S(1)}, bf16[128,1024]{1,0:T(8,128)(2,1)S(1)}, u32[]{:S(2)}, u32[]{:S(2)}) collective-permute-start(bf16[128,1024]{1,0:T(8,128)(2,1)S(1)} %shard_map.131), channel_id=1, source_target_pairs={{0,12},{2,14},{4,0},{6,2},{8,4},{10,6},{12,8},{14,10},{1,13},{3,15... | collective-permute-start | bytes 786440 | tf_op jit(solution)/shard_map/ppermute | solution.py:242
  89.4 6.6 %shard_map.130 = (bf16[896,384]{1,0:T(8,128)(2,1)S(1)}, bf16[896,384]{1,0:T(8,128)(2,1)S(1)}, bf16[896,1024]{1,0:T(8,128)(2,1)}, f32[4,16,128]{2,1,0:T(8,128)S(1)}, f32[4,16,128]{2,1,0:T(8,128)S(1)}) custom-call(s32[3]{0:T(128)S(1)} %pad_add_fusion.info, bf16[896,1024]{1,0:T(8,128)(2,1)S(1)} %shard_map.129.own, ...), custom_call_target="tpu_custom_call" | custom-call | flops 1000 | bytes 1000 | tf_op jit(solution)/shard_map/pallas_call | solution.py:41
  96.6 4.5 %collective-permute-done.19 = bf16[128,1024]{1,0:T(8,128)(2,1)S(1)} collective-permute-done((bf16[128,1024]{1,0:T(8,128)(2,1)S(1)}, bf16[128,1024]{1,0:T(8,128)(2,1)S(1)}, u32[]{:S(2)}, u32[]{:S(2)}) %collective-permute-start.19) | collective-permute-done | bytes 262176 | tf_op jit(solution)/shard_map/ppermute | solution.py:242
  101.8 1.1 collective-permute-start.21
  102.9 1.2 collective-permute-start.22
  104.2 5.5 %collective-permute-done.22.back = bf16[96,1024]{1,0:T(8,128)(2,1)S(1)} collective-permute-done((bf16[96,1024]{1,0:T(8,128)(2,1)}, bf16[96,1024]{1,0:T(8,128)(2,1)S(1)}, u32[]{:S(2)}, u32[]{:S(2)}) %collective-permute-start.22) | collective-permute-done | bytes 196640 | tf_op jit(solution)/shard_map/ppermute | solution.py:239
  111.2 1.1 collective-permute-start.25
  112.3 1.4 copy-done.6
  113.7 3.8 %shard_map.133 = (f32[4,128,1024]{2,1,0:T(8,128)S(1)}, bf16[112,1024]{1,0:T(8,128)(2,1)S(1)}, bf16[112,1024]{1,0:T(8,128)(2,1)S(1)}, bf16[112,1024]{1,0:T(8,128)(2,1)S(1)}, bf16[112,1024]{1,0:T(8,128)(2,1)S(1)}) custom-call(s32[3]{0:T(128)S(1)} %pad_add_fusion.info, bf16[896,1024]{1,0:T(8,128)(2,1)} %collective-permute-done.21.came, ...), custom_call_target="tpu_custom_call" | custom-call | flops 1000 | bytes 1000 | tf_op jit(solution)/shard_map/pallas_call | solution.py:41
  117.5 1.2 collective-permute-start.23
  120.0 3.4 %convolution_convert_fusion.1 = bf16[2048,384]{1,0:T(8,128)(2,1)} fusion(bf16[896,384]{1,0:T(8,128)(2,1)S(1)} %get-tuple-element.141.refs_0_, bf16[896,1024]{1,0:T(8,128)(2,1)S(1)} %get-tuple-element.187, bf16[896,1024]{1,0:T(8,128)(2,1)S(1)} %get-tuple-element.186), kind=kOutput, calls=%fused_computation.7 | convolution fusion | flops 1417412608 | bytes 5931008 | tf_op jit(solution)/shard_map/dot_general | solution.py:24
  123.5 3.0 %fusion.4 = bf16[384,2048]{1,0:T(8,128)(2,1)} fusion(bf16[896,384]{1,0:T(8,128)(2,1)S(1)} %copy-done.14, bf16[896,1024]{1,0:T(8,128)(2,1)S(1)} %get-tuple-element.185, bf16[896,1024]{1,0:T(8,128)(2,1)S(1)} %get-tuple-element.184), kind=kOutput, calls=%fused_computation.5 | convolution fusion | flops 1417412608 | bytes 5931008 | tf_op jit(solution)/shard_map/dot_general | solution.py:24
  126.4 2.1 %collective-permute-done.24.back = bf16[112,1024]{1,0:T(8,128)(2,1)S(1)} collective-permute-done((bf16[112,1024]{1,0:T(8,128)(2,1)S(1)}, bf16[112,1024]{1,0:T(8,128)(2,1)S(1)}, u32[]{:S(2)}, u32[]{:S(2)}) %collective-permute-start.24) | collective-permute-done | bytes 229408 | tf_op jit(solution)/shard_map/ppermute | solution.py:239
  128.5 1.2 collective-permute-start.27
  130.1 0.8 shard_map.134
  131.3 0.8 shard_map.135
  132.1 1.2 collective-permute-start.28
  133.3 1.6 collective-permute-start.31
  134.9 1.7 %collective-permute-start.30 = (bf16[144,1024]{1,0:T(8,128)(2,1)S(1)}, bf16[144,1024]{1,0:T(8,128)(2,1)S(1)}, u32[]{:S(2)}, u32[]{:S(2)}) collective-permute-start(bf16[144,1024]{1,0:T(8,128)(2,1)S(1)} %shard_map.134), channel_id=1, source_target_pairs={{0,8},{2,10},{4,12},{6,14},{8,0},{10,2},{12,4},{14,6},{1,9},{3,11}... | collective-permute-start | bytes 884744 | tf_op jit(solution)/shard_map/ppermute | solution.py:242
  136.6 0.8 shard_map.138
  137.5 0.9 add_convert_fusion.1
  138.3 5.1 %collective-permute-done.28.back = bf16[112,1024]{1,0:T(8,128)(2,1)S(1)} collective-permute-done((bf16[112,1024]{1,0:T(8,128)(2,1)S(1)}, bf16[112,1024]{1,0:T(8,128)(2,1)S(1)}, u32[]{:S(2)}, u32[]{:S(2)}) %collective-permute-start.28) | collective-permute-done | bytes 229408 | tf_op jit(solution)/shard_map/ppermute | solution.py:239
  143.5 0.8 shard_map.139
  144.3 0.8 shard_map.137
  145.1 1.5 collective-permute-start.29
  146.7 3.4 %fusion.7 = bf16[1,2048,384]{2,1,0:T(8,128)(2,1)} fusion(bf16[896,2048]{1,0:T(8,128)(2,1)S(1)} %pad_maximum_fusion, bf16[896,384]{1,0:T(8,128)(2,1)S(1)} %get-tuple-element.174.refs_1_), kind=kOutput, calls=%fused_computation.8 | convolution fusion | flops 1410072576 | bytes 5931008 | tf_op jit(solution)/shard_map/dot_general | solution.py:24
  150.1 7.6 %collective-permute-done.30 = bf16[144,1024]{1,0:T(8,128)(2,1)S(1)} collective-permute-done((bf16[144,1024]{1,0:T(8,128)(2,1)S(1)}, bf16[144,1024]{1,0:T(8,128)(2,1)S(1)}, u32[]{:S(2)}, u32[]{:S(2)}) %collective-permute-start.30) | collective-permute-done | bytes 294944 | tf_op jit(solution)/shard_map/ppermute | solution.py:242
  157.8 3.9 %collective-permute-done.29 = bf16[144,1024]{1,0:T(8,128)(2,1)S(1)} collective-permute-done((bf16[144,1024]{1,0:T(8,128)(2,1)S(1)}, bf16[144,1024]{1,0:T(8,128)(2,1)S(1)}, u32[]{:S(2)}, u32[]{:S(2)}) %collective-permute-start.29) | collective-permute-done | bytes 294944 | tf_op jit(solution)/shard_map/ppermute | solution.py:242
  161.8 1.3 collective-permute-start.32
  163.1 0.9 add_convert_fusion
  (119 shorter events, 11.4 us)
Async XLA Ops:
  2.4 7.9 %collective-permute-start.2 = (bf16[144,1024]{1,0:T(8,128)(2,1)S(1)}, bf16[144,1024]{1,0:T(8,128)(2,1)S(1)}, u32[]{:S(2)}, u32[]{:S(2)}) collective-permute-start(bf16[144,1024]{1,0:T(8,128)(2,1)S(1)} %pad_maximum_fusion.1.block.refs_0_), channel_id=1, source_target_pairs={{0,12},{2,14},{4,0},{6,2},{8,4},{10,6},{12,8},{14,10},{1,13},{3,15... | collective-permute-start | bytes 884744 | tf_op jit(solution)/shard_map/ppermute | solution.py:242
  2.4 16.3 %collective-permute-start = (bf16[144,1024]{1,0:T(8,128)(2,1)S(1)}, bf16[144,1024]{1,0:T(8,128)(2,1)S(1)}, u32[]{:S(2)}, u32[]{:S(2)}) collective-permute-start(bf16[144,1024]{1,0:T(8,128)(2,1)S(1)} %pad_maximum_fusion.1.block.refs_0_), channel_id=1, source_target_pairs={{0,4},{2,6},{4,8},{6,10},{8,12},{10,14},{12,0},{14,2},{1,5},{3,7},... | collective-permute-start | bytes 884744 | tf_op jit(solution)/shard_map/ppermute | solution.py:242
  3.9 24.3 %collective-permute-start.1 = (bf16[144,1024]{1,0:T(8,128)(2,1)S(1)}, bf16[144,1024]{1,0:T(8,128)(2,1)S(1)}, u32[]{:S(2)}, u32[]{:S(2)}) collective-permute-start(bf16[144,1024]{1,0:T(8,128)(2,1)S(1)} %pad_maximum_fusion.1.block.refs_0_), channel_id=1, source_target_pairs={{0,8},{2,10},{4,12},{6,14},{8,0},{10,2},{12,4},{14,6},{1,9},{3,11}... | collective-permute-start | bytes 884744 | tf_op jit(solution)/shard_map/ppermute | solution.py:242
  8.1 44.9 %copy-start.5 = (bf16[1,2048,384]{2,1,0:T(8,128)(2,1)S(1)}, bf16[1,2048,384]{2,1,0:T(8,128)(2,1)}, u32[]{:S(2)}) copy-start(bf16[1,2048,384]{2,1,0:T(8,128)(2,1)} %param.11) | copy-start | bytes 4718596
  9.0 17.9 %collective-permute-start.3 = (bf16[112,1024]{1,0:T(8,128)(2,1)S(1)}, bf16[112,1024]{1,0:T(8,128)(2,1)S(1)}, u32[]{:S(2)}, u32[]{:S(2)}) collective-permute-start(bf16[112,1024]{1,0:T(8,128)(2,1)S(1)} %get-tuple-element.91), channel_id=1, source_target_pairs={{0,2},{2,0},{4,6},{6,4},{8,10},{10,8},{12,14},{14,12},{1,3},{3,1},... | collective-permute-start | bytes 688136 | tf_op jit(solution)/shard_map/ppermute | solution.py:239
  11.2 74.8 %copy-start.17 = (bf16[96,128]{1,0:T(8,128)(2,1)}, bf16[96,128]{1,0:T(8,128)(2,1)S(1)}, u32[]{:S(2)}) copy-start(bf16[96,128]{1,0:T(8,128)(2,1)S(1)} %get-tuple-element.101.place) | copy-start | bytes 73732
  11.2 17.0 %collective-permute-start.5 = (bf16[112,1024]{1,0:T(8,128)(2,1)S(1)}, bf16[112,1024]{1,0:T(8,128)(2,1)S(1)}, u32[]{:S(2)}, u32[]{:S(2)}) collective-permute-start(bf16[112,1024]{1,0:T(8,128)(2,1)S(1)} %get-tuple-element.93), channel_id=1, source_target_pairs={{0,2},{2,0},{4,6},{6,4},{8,10},{10,8},{12,14},{14,12},{1,3},{3,1},... | collective-permute-start | bytes 688136 | tf_op jit(solution)/shard_map/ppermute | solution.py:239
  19.6 67.2 %copy-start.15 = (bf16[96,128]{1,0:T(8,128)(2,1)}, bf16[96,128]{1,0:T(8,128)(2,1)S(1)}, u32[]{:S(2)}) copy-start(bf16[96,128]{1,0:T(8,128)(2,1)S(1)} %get-tuple-element.100.place) | copy-start | bytes 73732
  19.6 8.6 %collective-permute-start.4 = (bf16[112,1024]{1,0:T(8,128)(2,1)S(1)}, bf16[112,1024]{1,0:T(8,128)(2,1)S(1)}, u32[]{:S(2)}, u32[]{:S(2)}) collective-permute-start(bf16[112,1024]{1,0:T(8,128)(2,1)S(1)} %get-tuple-element.92), channel_id=1, source_target_pairs={{0,2},{2,0},{4,6},{6,4},{8,10},{10,8},{12,14},{14,12},{1,3},{3,1},... | collective-permute-start | bytes 688136 | tf_op jit(solution)/shard_map/ppermute | solution.py:239
  20.9 32.1 %copy-start.2 = (bf16[1,384,2048]{2,1,0:T(8,128)(2,1)S(1)}, bf16[1,384,2048]{2,1,0:T(8,128)(2,1)}, u32[]{:S(2)}) copy-start(bf16[1,384,2048]{2,1,0:T(8,128)(2,1)} %param.12) | copy-start | bytes 4718596
  20.9 32.1 %copy-start.3 = (bf16[1,2048,384]{2,1,0:T(8,128)(2,1)S(1)}, bf16[1,2048,384]{2,1,0:T(8,128)(2,1)}, u32[]{:S(2)}) copy-start(bf16[1,2048,384]{2,1,0:T(8,128)(2,1)} %param.10) | copy-start | bytes 4718596
  22.3 4.6 %collective-permute-start.6 = (bf16[96,1024]{1,0:T(8,128)(2,1)S(1)}, bf16[96,1024]{1,0:T(8,128)(2,1)S(1)}, u32[]{:S(2)}, u32[]{:S(2)}) collective-permute-start(bf16[96,1024]{1,0:T(8,128)(2,1)S(1)} %shard_map.121), channel_id=1, source_target_pairs={{0,2},{2,0},{4,6},{6,4},{8,10},{10,8},{12,14},{14,12},{1,3},{3,1},... | collective-permute-start | bytes 589832 | tf_op jit(solution)/shard_map/ppermute | solution.py:239
  28.2 5.9 %collective-permute-start.9 = (bf16[128,1024]{1,0:T(8,128)(2,1)}, bf16[128,1024]{1,0:T(8,128)(2,1)S(1)}, u32[]{:S(2)}, u32[]{:S(2)}) collective-permute-start(bf16[128,1024]{1,0:T(8,128)(2,1)} %refs_0_), channel_id=1, source_target_pairs={{0,12},{2,14},{4,0},{6,2},{8,4},{10,6},{12,8},{14,10},{1,13},{3,15... | collective-permute-start | bytes 786440 | tf_op jit(solution)/shard_map/ppermute | solution.py:242
  30.5 11.7 %collective-permute-start.8 = (bf16[128,1024]{1,0:T(8,128)(2,1)}, bf16[128,1024]{1,0:T(8,128)(2,1)S(1)}, u32[]{:S(2)}, u32[]{:S(2)}) collective-permute-start(bf16[128,1024]{1,0:T(8,128)(2,1)} %refs_0_), channel_id=1, source_target_pairs={{0,4},{2,6},{4,8},{6,10},{8,12},{10,14},{12,0},{14,2},{1,5},{3,7},... | collective-permute-start | bytes 786440 | tf_op jit(solution)/shard_map/ppermute | solution.py:242
  31.3 45.3 %copy-start.19 = (bf16[96,128]{1,0:T(8,128)(2,1)}, bf16[96,128]{1,0:T(8,128)(2,1)S(1)}, u32[]{:S(2)}) copy-start(bf16[96,128]{1,0:T(8,128)(2,1)S(1)} %get-tuple-element.127.place) | copy-start | bytes 73732
  31.4 11.5 %collective-permute-start.7 = (bf16[112,1024]{1,0:T(8,128)(2,1)S(1)}, bf16[112,1024]{1,0:T(8,128)(2,1)S(1)}, u32[]{:S(2)}, u32[]{:S(2)}) collective-permute-start(bf16[112,1024]{1,0:T(8,128)(2,1)S(1)} %get-tuple-element.98), channel_id=1, source_target_pairs={{0,2},{2,0},{4,6},{6,4},{8,10},{10,8},{12,14},{14,12},{1,3},{3,1},... | collective-permute-start | bytes 688136 | tf_op jit(solution)/shard_map/ppermute | solution.py:239
  43.7 15.0 %copy-start.7 = (bf16[896,1024]{1,0:T(8,128)(2,1)}, bf16[896,1024]{1,0:T(8,128)(2,1)S(1)}, u32[]{:S(2)}) copy-start(bf16[896,1024]{1,0:T(8,128)(2,1)S(1)} %get-tuple-element.156.own) | copy-start | bytes 5505028
  43.7 9.3 %collective-permute-start.11 = (bf16[896,1024]{1,0:T(8,128)(2,1)S(1)}, bf16[896,1024]{1,0:T(8,128)(2,1)S(1)}, u32[]{:S(2)}, u32[]{:S(2)}) collective-permute-start(bf16[896,1024]{1,0:T(8,128)(2,1)S(1)} %get-tuple-element.156.own), channel_id=1, source_target_pairs={{0,1},{1,0},{2,3},{3,2},{4,5},{5,4},{6,7},{7,6},{8,9},{9,8},{10,11... | collective-permute-start | bytes 5505032 | tf_op jit(solution)/shard_map/ppermute | solution.py:248
  49.6 9.1 %collective-permute-start.13 = (bf16[96,1024]{1,0:T(8,128)(2,1)S(1)}, bf16[96,1024]{1,0:T(8,128)(2,1)S(1)}, u32[]{:S(2)}, u32[]{:S(2)}) collective-permute-start(bf16[96,1024]{1,0:T(8,128)(2,1)S(1)} %shard_map.124), channel_id=1, source_target_pairs={{0,2},{2,0},{4,6},{6,4},{8,10},{10,8},{12,14},{14,12},{1,3},{3,1},... | collective-permute-start | bytes 589832 | tf_op jit(solution)/shard_map/ppermute | solution.py:239
  50.8 9.5 %collective-permute-start.12 = (bf16[96,1024]{1,0:T(8,128)(2,1)S(1)}, bf16[96,1024]{1,0:T(8,128)(2,1)S(1)}, u32[]{:S(2)}, u32[]{:S(2)}) collective-permute-start(bf16[96,1024]{1,0:T(8,128)(2,1)S(1)} %shard_map.123), channel_id=1, source_target_pairs={{0,2},{2,0},{4,6},{6,4},{8,10},{10,8},{12,14},{14,12},{1,3},{3,1},... | collective-permute-start | bytes 589832 | tf_op jit(solution)/shard_map/ppermute | solution.py:239
  53.0 5.7 %copy-start.9 = (bf16[896,1024]{1,0:T(8,128)(2,1)}, bf16[896,1024]{1,0:T(8,128)(2,1)S(1)}, u32[]{:S(2)}) copy-start(bf16[896,1024]{1,0:T(8,128)(2,1)S(1)} %collective-permute-done.11.other) | copy-start | bytes 5505028
  58.7 7.5 %copy-start.13 = (bf16[896,384]{1,0:T(8,128)(2,1)}, bf16[896,384]{1,0:T(8,128)(2,1)S(1)}, u32[]{:S(2)}) copy-start(bf16[896,384]{1,0:T(8,128)(2,1)S(1)} %get-tuple-element.120.refs_0_) | copy-start | bytes 2064388
  60.3 4.3 %collective-permute-start.14 = (bf16[896,1024]{1,0:T(8,128)(2,1)S(1)}, bf16[896,1024]{1,0:T(8,128)(2,1)S(1)}, u32[]{:S(2)}, u32[]{:S(2)}) collective-permute-start(bf16[896,1024]{1,0:T(8,128)(2,1)S(1)} %get-tuple-element.119), channel_id=1, source_target_pairs={{0,1},{1,0},{2,3},{3,2},{4,5},{5,4},{6,7},{7,6},{8,9},{9,8},{10,11... | collective-permute-start | bytes 5505032 | tf_op jit(solution)/shard_map/ppermute | solution.py:248
  61.2 11.9 %collective-permute-start.10 = (bf16[128,1024]{1,0:T(8,128)(2,1)}, bf16[128,1024]{1,0:T(8,128)(2,1)S(1)}, u32[]{:S(2)}, u32[]{:S(2)}) collective-permute-start(bf16[128,1024]{1,0:T(8,128)(2,1)} %refs_0_), channel_id=1, source_target_pairs={{0,8},{2,10},{4,12},{6,14},{8,0},{10,2},{12,4},{14,6},{1,9},{3,11}... | collective-permute-start | bytes 786440 | tf_op jit(solution)/shard_map/ppermute | solution.py:242
  66.3 16.4 %copy-start.26 = (bf16[96,1024]{1,0:T(8,128)(2,1)}, bf16[96,1024]{1,0:T(8,128)(2,1)S(1)}, u32[]{:S(2)}) copy-start(bf16[96,1024]{1,0:T(8,128)(2,1)S(1)} %get-tuple-element.139) | copy-start | bytes 589828
  66.3 17.5 %copy-start.24 = (bf16[96,1024]{1,0:T(8,128)(2,1)}, bf16[96,1024]{1,0:T(8,128)(2,1)S(1)}, u32[]{:S(2)}) copy-start(bf16[96,1024]{1,0:T(8,128)(2,1)S(1)} %get-tuple-element.165) | copy-start | bytes 589828
  66.3 6.8 %collective-permute-start.15 = (bf16[96,1024]{1,0:T(8,128)(2,1)S(1)}, bf16[96,1024]{1,0:T(8,128)(2,1)S(1)}, u32[]{:S(2)}, u32[]{:S(2)}) collective-permute-start(bf16[96,1024]{1,0:T(8,128)(2,1)S(1)} %get-tuple-element.121), channel_id=1, source_target_pairs={{0,2},{2,0},{4,6},{6,4},{8,10},{10,8},{12,14},{14,12},{1,3},{3,1},... | collective-permute-start | bytes 589832 | tf_op jit(solution)/shard_map/ppermute | solution.py:239
  67.5 9.1 %collective-permute-start.16 = (bf16[96,1024]{1,0:T(8,128)(2,1)S(1)}, bf16[96,1024]{1,0:T(8,128)(2,1)S(1)}, u32[]{:S(2)}, u32[]{:S(2)}) collective-permute-start(bf16[96,1024]{1,0:T(8,128)(2,1)S(1)} %get-tuple-element.122), channel_id=1, source_target_pairs={{0,2},{2,0},{4,6},{6,4},{8,10},{10,8},{12,14},{14,12},{1,3},{3,1},... | collective-permute-start | bytes 589832 | tf_op jit(solution)/shard_map/ppermute | solution.py:239
  77.4 5.3 %collective-permute-start.17 = (bf16[96,1024]{1,0:T(8,128)(2,1)S(1)}, bf16[96,1024]{1,0:T(8,128)(2,1)S(1)}, u32[]{:S(2)}, u32[]{:S(2)}) collective-permute-start(bf16[96,1024]{1,0:T(8,128)(2,1)S(1)} %shard_map.128), channel_id=1, source_target_pairs={{0,2},{2,0},{4,6},{6,4},{8,10},{10,8},{12,14},{14,12},{1,3},{3,1},... | collective-permute-start | bytes 589832 | tf_op jit(solution)/shard_map/ppermute | solution.py:239
  83.8 5.6 %copy-start = (bf16[896,1024]{1,0:T(8,128)(2,1)}, bf16[896,1024]{1,0:T(8,128)(2,1)S(1)}, u32[]{:S(2)}) copy-start(bf16[896,1024]{1,0:T(8,128)(2,1)S(1)} %shard_map.129.own) | copy-start | bytes 5505028
  83.8 5.6 %collective-permute-start.18 = (bf16[896,1024]{1,0:T(8,128)(2,1)S(1)}, bf16[896,1024]{1,0:T(8,128)(2,1)S(1)}, u32[]{:S(2)}, u32[]{:S(2)}) collective-permute-start(bf16[896,1024]{1,0:T(8,128)(2,1)S(1)} %shard_map.129.own), channel_id=1, source_target_pairs={{0,1},{1,0},{2,3},{3,2},{4,5},{5,4},{6,7},{7,6},{8,9},{9,8},{10,11... | collective-permute-start | bytes 5505032 | tf_op jit(solution)/shard_map/ppermute | solution.py:248
  86.8 9.9 %collective-permute-start.20 = (bf16[128,1024]{1,0:T(8,128)(2,1)S(1)}, bf16[128,1024]{1,0:T(8,128)(2,1)S(1)}, u32[]{:S(2)}, u32[]{:S(2)}) collective-permute-start(bf16[128,1024]{1,0:T(8,128)(2,1)S(1)} %shard_map.132), channel_id=1, source_target_pairs={{0,4},{2,6},{4,8},{6,10},{8,12},{10,14},{12,0},{14,2},{1,5},{3,7},... | collective-permute-start | bytes 786440 | tf_op jit(solution)/shard_map/ppermute | solution.py:242
  87.7 13.5 %collective-permute-start.19 = (bf16[128,1024]{1,0:T(8,128)(2,1)S(1)}, bf16[128,1024]{1,0:T(8,128)(2,1)S(1)}, u32[]{:S(2)}, u32[]{:S(2)}) collective-permute-start(bf16[128,1024]{1,0:T(8,128)(2,1)S(1)} %shard_map.131), channel_id=1, source_target_pairs={{0,12},{2,14},{4,0},{6,2},{8,4},{10,6},{12,8},{14,10},{1,13},{3,15... | collective-permute-start | bytes 786440 | tf_op jit(solution)/shard_map/ppermute | solution.py:242
  89.4 6.6 %copy-start.11 = (bf16[896,1024]{1,0:T(8,128)(2,1)}, bf16[896,1024]{1,0:T(8,128)(2,1)S(1)}, u32[]{:S(2)}) copy-start(bf16[896,1024]{1,0:T(8,128)(2,1)S(1)} %collective-permute-done.18.other) | copy-start | bytes 5505028
  89.4 14.8 %copy-start.31 = (s32[128,4]{0,1:T(4,128)S(1)}, s32[128,4]{0,1:T(4,128)}, u32[]{:S(2)}) copy-start(s32[128,4]{0,1:T(4,128)} %param.8) | copy-start | bytes 6148
  96.6 4.5 %copy-start.27 = (bf16[128,1024]{1,0:T(8,128)(2,1)}, bf16[128,1024]{1,0:T(8,128)(2,1)S(1)}, u32[]{:S(2)}) copy-start(bf16[128,1024]{1,0:T(8,128)(2,1)S(1)} %collective-permute-done.20) | copy-start | bytes 786436
  101.1 0.7 copy-start.29
  101.8 7.9 %collective-permute-start.21 = (bf16[896,1024]{1,0:T(8,128)(2,1)}, bf16[896,1024]{1,0:T(8,128)(2,1)}, u32[]{:S(2)}, u32[]{:S(2)}) collective-permute-start(bf16[896,1024]{1,0:T(8,128)(2,1)} %get-tuple-element.138), channel_id=1, source_target_pairs={{0,1},{1,0},{2,3},{3,2},{4,5},{5,4},{6,7},{7,6},{8,9},{9,8},{10,11... | collective-permute-start | bytes 5505032 | tf_op jit(solution)/shard_map/ppermute | solution.py:248
  102.9 9.4 %copy-start.4 = (bf16[1,2048,384]{2,1,0:T(8,128)(2,1)S(1)}, bf16[1,2048,384]{2,1,0:T(8,128)(2,1)}, u32[]{:S(2)}) copy-start(bf16[1,2048,384]{2,1,0:T(8,128)(2,1)} %param.10) | copy-start | bytes 4718596
  102.9 6.7 %collective-permute-start.22 = (bf16[96,1024]{1,0:T(8,128)(2,1)}, bf16[96,1024]{1,0:T(8,128)(2,1)S(1)}, u32[]{:S(2)}, u32[]{:S(2)}) collective-permute-start(bf16[96,1024]{1,0:T(8,128)(2,1)} %copy-done.26), channel_id=1, source_target_pairs={{0,2},{2,0},{4,6},{6,4},{8,10},{10,8},{12,14},{14,12},{1,3},{3,1},... | collective-permute-start | bytes 589832 | tf_op jit(solution)/shard_map/ppermute | solution.py:239
  109.7 0.7 copy-start.20
  110.4 1.9 %copy-start.23 = (f32[4,16,128]{2,1,0:T(8,128)S(1)}, f32[4,16,128]{2,1,0:T(8,128)}, u32[]{:S(2)}) copy-start(f32[4,16,128]{2,1,0:T(8,128)} %copy-done.22) | copy-start | bytes 98308
  111.2 22.1 %collective-permute-start.25 = (bf16[128,1024]{1,0:T(8,128)(2,1)S(1)}, bf16[128,1024]{1,0:T(8,128)(2,1)S(1)}, u32[]{:S(2)}, u32[]{:S(2)}) collective-permute-start(bf16[128,1024]{1,0:T(8,128)(2,1)S(1)} %shard_map.136), channel_id=1, source_target_pairs={{0,8},{2,10},{4,12},{6,14},{8,0},{10,2},{12,4},{14,6},{1,9},{3,11}... | collective-permute-start | bytes 786440 | tf_op jit(solution)/shard_map/ppermute | solution.py:242
  112.3 1.4 copy-start.6
  113.7 5.3 %copy-start.1 = (bf16[896,1024]{1,0:T(8,128)(2,1)S(1)}, bf16[896,1024]{1,0:T(8,128)(2,1)}, u32[]{:S(2)}) copy-start(bf16[896,1024]{1,0:T(8,128)(2,1)} %copy-done) | copy-start | bytes 5505028
  113.7 5.3 %copy-start.12 = (bf16[896,1024]{1,0:T(8,128)(2,1)S(1)}, bf16[896,1024]{1,0:T(8,128)(2,1)}, u32[]{:S(2)}) copy-start(bf16[896,1024]{1,0:T(8,128)(2,1)} %copy-done.11) | copy-start | bytes 5505028
  117.5 1.8 %copy-start.8 = (bf16[896,1024]{1,0:T(8,128)(2,1)S(1)}, bf16[896,1024]{1,0:T(8,128)(2,1)}, u32[]{:S(2)}) copy-start(bf16[896,1024]{1,0:T(8,128)(2,1)} %copy-done.7) | copy-start | bytes 5505028
  117.5 2.0 %copy-start.10 = (bf16[896,1024]{1,0:T(8,128)(2,1)S(1)}, bf16[896,1024]{1,0:T(8,128)(2,1)}, u32[]{:S(2)}) copy-start(bf16[896,1024]{1,0:T(8,128)(2,1)} %copy-done.9) | copy-start | bytes 5505028
  117.5 12.6 %collective-permute-start.23 = (bf16[112,1024]{1,0:T(8,128)(2,1)S(1)}, bf16[112,1024]{1,0:T(8,128)(2,1)S(1)}, u32[]{:S(2)}, u32[]{:S(2)}) collective-permute-start(bf16[112,1024]{1,0:T(8,128)(2,1)S(1)} %get-tuple-element.149), channel_id=1, source_target_pairs={{0,2},{2,0},{4,6},{6,4},{8,10},{10,8},{12,14},{14,12},{1,3},{3,1},... | collective-permute-start | bytes 688136 | tf_op jit(solution)/shard_map/ppermute | solution.py:239
  118.7 9.8 %collective-permute-start.24 = (bf16[112,1024]{1,0:T(8,128)(2,1)S(1)}, bf16[112,1024]{1,0:T(8,128)(2,1)S(1)}, u32[]{:S(2)}, u32[]{:S(2)}) collective-permute-start(bf16[112,1024]{1,0:T(8,128)(2,1)S(1)} %get-tuple-element.151), channel_id=1, source_target_pairs={{0,2},{2,0},{4,6},{6,4},{8,10},{10,8},{12,14},{14,12},{1,3},{3,1},... | collective-permute-start | bytes 688136 | tf_op jit(solution)/shard_map/ppermute | solution.py:239
  120.0 3.4 %copy-start.14 = (bf16[896,384]{1,0:T(8,128)(2,1)S(1)}, bf16[896,384]{1,0:T(8,128)(2,1)}, u32[]{:S(2)}) copy-start(bf16[896,384]{1,0:T(8,128)(2,1)} %copy-done.13) | copy-start | bytes 2064388
  123.5 5.1 %copy-start.25 = (bf16[96,1024]{1,0:T(8,128)(2,1)S(1)}, bf16[96,1024]{1,0:T(8,128)(2,1)}, u32[]{:S(2)}) copy-start(bf16[96,1024]{1,0:T(8,128)(2,1)} %copy-done.24) | copy-start | bytes 589828
  126.4 3.7 %copy-start.21 = (bf16[96,128]{1,0:T(8,128)(2,1)S(1)}, bf16[96,128]{1,0:T(8,128)(2,1)}, u32[]{:S(2)}) copy-start(bf16[96,128]{1,0:T(8,128)(2,1)} %copy-done.19) | copy-start | bytes 73732
  128.5 8.1 %collective-permute-start.27 = (bf16[96,1024]{1,0:T(8,128)(2,1)S(1)}, bf16[96,1024]{1,0:T(8,128)(2,1)S(1)}, u32[]{:S(2)}, u32[]{:S(2)}) collective-permute-start(bf16[96,1024]{1,0:T(8,128)(2,1)S(1)} %copy-done.25), channel_id=1, source_target_pairs={{0,2},{2,0},{4,6},{6,4},{8,10},{10,8},{12,14},{14,12},{1,3},{3,1},... | collective-permute-start | bytes 589832 | tf_op jit(solution)/shard_map/ppermute | solution.py:239
  130.1 1.2 copy-start.18
  130.9 13.4 %collective-permute-start.26 = (bf16[112,1024]{1,0:T(8,128)(2,1)S(1)}, bf16[112,1024]{1,0:T(8,128)(2,1)S(1)}, u32[]{:S(2)}, u32[]{:S(2)}) collective-permute-start(bf16[112,1024]{1,0:T(8,128)(2,1)S(1)} %get-tuple-element.163), channel_id=1, source_target_pairs={{0,2},{2,0},{4,6},{6,4},{8,10},{10,8},{12,14},{14,12},{1,3},{3,1},... | collective-permute-start | bytes 688136 | tf_op jit(solution)/shard_map/ppermute | solution.py:239
  132.1 5.4 %copy-start.28 = (bf16[128,1024]{1,0:T(8,128)(2,1)S(1)}, bf16[128,1024]{1,0:T(8,128)(2,1)}, u32[]{:S(2)}) copy-start(bf16[128,1024]{1,0:T(8,128)(2,1)} %copy-done.27) | copy-start | bytes 786436
  132.1 5.4 %copy-start.30 = (bf16[128,1024]{1,0:T(8,128)(2,1)S(1)}, bf16[128,1024]{1,0:T(8,128)(2,1)}, u32[]{:S(2)}) copy-start(bf16[128,1024]{1,0:T(8,128)(2,1)} %copy-done.29) | copy-start | bytes 786436
  132.1 11.4 %collective-permute-start.28 = (bf16[112,1024]{1,0:T(8,128)(2,1)S(1)}, bf16[112,1024]{1,0:T(8,128)(2,1)S(1)}, u32[]{:S(2)}, u32[]{:S(2)}) collective-permute-start(bf16[112,1024]{1,0:T(8,128)(2,1)S(1)} %get-tuple-element.171), channel_id=1, source_target_pairs={{0,2},{2,0},{4,6},{6,4},{8,10},{10,8},{12,14},{14,12},{1,3},{3,1},... | collective-permute-start | bytes 688136 | tf_op jit(solution)/shard_map/ppermute | solution.py:239
  133.3 16.8 %collective-permute-start.31 = (bf16[144,1024]{1,0:T(8,128)(2,1)S(1)}, bf16[144,1024]{1,0:T(8,128)(2,1)S(1)}, u32[]{:S(2)}, u32[]{:S(2)}) collective-permute-start(bf16[144,1024]{1,0:T(8,128)(2,1)S(1)} %shard_map.135), channel_id=1, source_target_pairs={{0,4},{2,6},{4,8},{6,10},{8,12},{10,14},{12,0},{14,2},{1,5},{3,7},... | collective-permute-start | bytes 884744 | tf_op jit(solution)/shard_map/ppermute | solution.py:242
  134.9 22.8 %collective-permute-start.30 = (bf16[144,1024]{1,0:T(8,128)(2,1)S(1)}, bf16[144,1024]{1,0:T(8,128)(2,1)S(1)}, u32[]{:S(2)}, u32[]{:S(2)}) collective-permute-start(bf16[144,1024]{1,0:T(8,128)(2,1)S(1)} %shard_map.134), channel_id=1, source_target_pairs={{0,8},{2,10},{4,12},{6,14},{8,0},{10,2},{12,4},{14,6},{1,9},{3,11}... | collective-permute-start | bytes 884744 | tf_op jit(solution)/shard_map/ppermute | solution.py:242
  137.5 6.8 %copy-start.16 = (bf16[96,128]{1,0:T(8,128)(2,1)S(1)}, bf16[96,128]{1,0:T(8,128)(2,1)}, u32[]{:S(2)}) copy-start(bf16[96,128]{1,0:T(8,128)(2,1)} %copy-done.15) | copy-start | bytes 73732
  145.1 16.6 %collective-permute-start.29 = (bf16[144,1024]{1,0:T(8,128)(2,1)S(1)}, bf16[144,1024]{1,0:T(8,128)(2,1)S(1)}, u32[]{:S(2)}, u32[]{:S(2)}) collective-permute-start(bf16[144,1024]{1,0:T(8,128)(2,1)S(1)} %shard_map.137), channel_id=1, source_target_pairs={{0,12},{2,14},{4,0},{6,2},{8,4},{10,6},{12,8},{14,10},{1,13},{3,15... | collective-permute-start | bytes 884744 | tf_op jit(solution)/shard_map/ppermute | solution.py:242
  161.8 2.2 %collective-permute-start.32 = (f32[128,4]{0,1:T(4,128)S(1)}, f32[128,4]{0,1:T(4,128)S(1)}, u32[]{:S(2)}, u32[]{:S(2)}) collective-permute-start(f32[128,4]{0,1:T(4,128)S(1)} %select_reduce_fusion), channel_id=1, source_target_pairs={{0,1},{1,0},{2,3},{3,2},{4,5},{5,4},{6,7},{7,6},{8,9},{9,8},{10,11... | collective-permute-start | bytes 6152 | tf_op jit(solution)/shard_map/ppermute | solution.py:248
  (1 other events, 0.6 us)

commit v12 on v10

--- a/solution.py
+++ b/solution.py
@@ -321,7 +321,8 @@
         (info, over_core(sent), scaled, down_local))
 
     outward = by_reach[::-1]
-    out_back = {k: over_pair(out_packed[k]) for k in near}
+    leading, trailing = outward[:-1], outward[-1]
+    out_back = {k: over_pair(out_packed[k]) for k in leading}
     (grad_rows,) = local_call(
         functools.partial(grad_rows_kernel, *sizes), (half_rows,),
         (info, *[grad_blocks[k] for k in every], *[grad_compact[k] for k in every]))
@@ -346,23 +347,23 @@
         return total.astype(BF)
 
     sent, out_back = settle((sent, out_back))
-    out_home = {k: to_home(k, out_dense, out_back) for k in near}
-    out_back[far] = over_pair(out_packed[far])
+    out_home = {k: to_home(k, out_dense, out_back) for k in leading}
+    out_back[trailing] = over_pair(out_packed[trailing])
 
     def whole(own, other):
         return jnp.concatenate(
             [jnp.where(core == 0, own, other), jnp.where(core == 0, other, own)], axis=1)
 
-    came, out_back[far] = settle((over_core(sent), out_back[far]))
-    out_came = {k: over_line(out_home[k], lines - k) for k in near}
+    came = over_core(sent)
+    out_came = {k: over_line(out_home[k], lines - k) for k in leading}
     in_dense, *in_packed = local_call(
         functools.partial(join_kernel, *sizes, False),
         (shape_of((lines, token_count, half_width), F32),
          *[shape_of((padded + TAIL, half_width)) for _ in every]),
         (info, came, grad_gate, grad_up, gate_local, up_local, compact_tails))
-    in_packed, out_came = settle((in_packed, out_came))
-    far_home = to_home(far, out_dense, out_back)
-    out_came[far] = over_line(far_home, lines - far)
+    in_packed, out_back[trailing], out_came = settle((in_packed, out_back[trailing], out_came))
+    trailing_home = to_home(trailing, out_dense, out_back)
+    out_came[trailing] = over_line(trailing_home, lines - trailing)
     in_back, in_home, sequence = {}, {}, outward + [0]
     for i, k in enumerate(sequence):
         packed = in_packed[k]
@@ -376,13 +377,11 @@
     out_came[0] = to_home(0, out_dense, out_back)
     in_home.update(ready)
     layer_out = summed(out_came)
-    rows, rows_other, grad_rows, _ = settle((rows, rows_other, grad_rows, far_home))
+    last_home, layer_out, rows, rows_other, grad_rows, grad_up = settle(
+        ([in_home[k] for k in outward], layer_out, rows, rows_other, grad_rows, grad_up))
     rows = whole(rows, rows_other)
     gate_grad = dot(rows, grad_gate, FIRST).astype(BF)
     down_grad = dot(scaled, whole(grad_rows, grad_other), FIRST).astype(BF)
-    in_home[sequence[0]], gate_grad = settle((in_home[sequence[0]], gate_grad))
-    in_home[sequence[1]], down_grad = settle((in_home[sequence[1]], down_grad))
-    last_home, layer_out, rows, grad_up = settle(([in_home[k] for k in outward], layer_out, rows, grad_up))
     in_home = {k: over_line(in_home[k], lines - k) if k else in_home[0] for k in every}
     input_grad = summed(in_home)
 

time: 153 us -> 158 us (1.033); the launches traced: 153 us -> 156 us
  starting transfers between devices: 42.1 us -> 47.8 us
  waiting for transfers between devices: 57 us -> 55.1 us
    ppermute x12, starting transfers between devices: 17 us -> 22.9 us  [over_line(): lax.ppermute(x, 'expert', [(i, (i // 2 + k) % lines * 2 + i % 2) for i in...]
    ppermute x16, waiting for transfers between devices: 19.9 us -> 14.2 us  [over_pair(): lax.ppermute(x, 'expert', [(i, i + 1 - 2 * (i % 2)) for i in range(expert...]
    ppermute x12, waiting for transfers between devices: 33 us -> 36.7 us  [over_line(): lax.ppermute(x, 'expert', [(i, (i // 2 + k) % lines * 2 + i % 2) for i in...]
    unnamed x57 -> x65, local copies, waits for them, and re-layouts: 2.51 us -> 3.79 us
  transfers between devices with their start and end apart: 33 -> 33, of which waited for: 13 -> 15; matrix products, arithmetic and copies ran while one was open for 9% -> 8% of each run, Pallas kernels for 22% -> 20%
where the time goes in v12:
time: 158 us; the launch traced here: 156 us
  waiting for transfers between devices  55.1 us (35%)
  starting transfers between devices  47.8 us (30%)
  Pallas kernels  32.7 us (21%)
  matrix products  9.84 us (6%)
  other arithmetic  5.73 us (4%)
  local copies, waits for them, and re-layouts  3.8 us (2%)
    ppermute x12, waiting for transfers between devices, over_line(): lax.ppermute(x, 'expert', [(i, (i // 2 + k) % lines * 2 + i % 2) for i in...  36.7 us
    pallas_call x22, Pallas kernels, local_call(): pl.pallas_call(kernel, out_shape=tuple(outs), in_specs=[SMEM_SPEC] + [VME...  32.7 us
    ppermute x12, starting transfers between devices, over_line(): lax.ppermute(x, 'expert', [(i, (i // 2 + k) % lines * 2 + i % 2) for i in...  22.9 us
    ppermute x16, starting transfers between devices, over_pair(): lax.ppermute(x, 'expert', [(i, i + 1 - 2 * (i % 2)) for i in range(expert...  15.2 us
    ppermute x16, waiting for transfers between devices, over_pair(): lax.ppermute(x, 'expert', [(i, i + 1 - 2 * (i % 2)) for i in range(expert...  14.2 us
    dot_general x3, matrix products, dot(): lax.dot_general(a, b, (contract, ((), ())), preferred_element_type=F32)  9.84 us
    ppermute x5, starting transfers between devices, over_core(): return lax.ppermute(x, 'tensor', [(0, 1), (1, 0)])  9.66 us
    ppermute x5, waiting for transfers between devices, over_core(): return lax.ppermute(x, 'tensor', [(0, 1), (1, 0)])  4.18 us
  transfers between devices with their start and end apart: 33, of which 15 were waited for; matrix products, arithmetic and copies ran while one was open for 8% of the time, Pallas kernels for 20%

profile of v12, /device:TPU:9, one launch (start us, length us, event | category | flops | bytes accessed | tf_op | source)
XLA Modules:
  0.0 156.1 jit_solution(16141825631161023691)
XLA Ops:
  1.4 1.0 pad_maximum_fusion.3.block.refs_0_
  2.4 1.5 collective-permute-start
  3.9 4.1 %collective-permute-start.1 = (bf16[144,1024]{1,0:T(8,128)(2,1)S(1)}, bf16[144,1024]{1,0:T(8,128)(2,1)S(1)}, u32[]{:S(2)}, u32[]{:S(2)}) collective-permute-start(bf16[144,1024]{1,0:T(8,128)(2,1)S(1)} %pad_maximum_fusion.3.block.refs_0_), channel_id=1, source_target_pairs={{0,8},{2,10},{4,12},{6,14},{8,0},{10,2},{12,4},{14,6},{1,9},{3,11}... | collective-permute-start | bytes 884744 | tf_op jit(solution)/shard_map/ppermute | solution.py:242
  8.1 0.9 shard_map.118
  9.0 1.3 collective-permute-start.3
  10.3 0.9 shard_map.120
  11.2 1.3 collective-permute-start.5
  12.5 6.2 %collective-permute-done.block.refs_1_ = bf16[144,1024]{1,0:T(8,128)(2,1)S(1)} collective-permute-done((bf16[144,1024]{1,0:T(8,128)(2,1)S(1)}, bf16[144,1024]{1,0:T(8,128)(2,1)S(1)}, u32[]{:S(2)}, u32[]{:S(2)}) %collective-permute-start) | collective-permute-done | bytes 294944 | tf_op jit(solution)/shard_map/ppermute | solution.py:242
  18.7 0.9 shard_map.119
  19.6 1.3 collective-permute-start.4
  20.9 1.2 shard_map.121
  22.4 4.3 %collective-permute-done.6.refs_4_ = bf16[96,1024]{1,0:T(8,128)(2,1)S(1)} collective-permute-done((bf16[96,1024]{1,0:T(8,128)(2,1)S(1)}, bf16[96,1024]{1,0:T(8,128)(2,1)S(1)}, u32[]{:S(2)}, u32[]{:S(2)}) %collective-permute-start.6) | collective-permute-done | bytes 196640 | tf_op jit(solution)/shard_map/ppermute | solution.py:239
  26.7 1.5 collective-permute-done.1.block.refs_2_
  28.5 2.0 %collective-permute-start.10 = (bf16[128,1024]{1,0:T(8,128)(2,1)}, bf16[128,1024]{1,0:T(8,128)(2,1)S(1)}, u32[]{:S(2)}, u32[]{:S(2)}) collective-permute-start(bf16[128,1024]{1,0:T(8,128)(2,1)} %refs_0_), channel_id=1, source_target_pairs={{0,12},{2,14},{4,0},{6,2},{8,4},{10,6},{12,8},{14,10},{1,13},{3,15... | collective-permute-start | bytes 786440 | tf_op jit(solution)/shard_map/ppermute | solution.py:242
  30.5 2.3 %collective-permute-start.9 = (bf16[128,1024]{1,0:T(8,128)(2,1)}, bf16[128,1024]{1,0:T(8,128)(2,1)S(1)}, u32[]{:S(2)}, u32[]{:S(2)}) collective-permute-start(bf16[128,1024]{1,0:T(8,128)(2,1)} %refs_0_), channel_id=1, source_target_pairs={{0,8},{2,10},{4,12},{6,14},{8,0},{10,2},{12,4},{14,6},{1,9},{3,11}... | collective-permute-start | bytes 786440 | tf_op jit(solution)/shard_map/ppermute | solution.py:242
  32.8 0.9 shard_map.122
  33.7 1.3 collective-permute-start.7
  35.8 1.0 collective-permute-start.11
  36.8 4.5 %collective-permute-done.10.block.refs_3_ = bf16[128,1024]{1,0:T(8,128)(2,1)S(1)} collective-permute-done((bf16[128,1024]{1,0:T(8,128)(2,1)}, bf16[128,1024]{1,0:T(8,128)(2,1)S(1)}, u32[]{:S(2)}, u32[]{:S(2)}) %collective-permute-start.10) | collective-permute-done | bytes 262176 | tf_op jit(solution)/shard_map/ppermute | solution.py:242
  42.1 7.6 %collective-permute-done.9.block.refs_2_ = bf16[128,1024]{1,0:T(8,128)(2,1)S(1)} collective-permute-done((bf16[128,1024]{1,0:T(8,128)(2,1)}, bf16[128,1024]{1,0:T(8,128)(2,1)S(1)}, u32[]{:S(2)}, u32[]{:S(2)}) %collective-permute-start.9) | collective-permute-done | bytes 262176 | tf_op jit(solution)/shard_map/ppermute | solution.py:242
  51.3 7.0 %collective-permute-start.12 = (bf16[896,1024]{1,0:T(8,128)(2,1)S(1)}, bf16[896,1024]{1,0:T(8,128)(2,1)S(1)}, u32[]{:S(2)}, u32[]{:S(2)}) collective-permute-start(bf16[896,1024]{1,0:T(8,128)(2,1)S(1)} %get-tuple-element.166.own), channel_id=1, source_target_pairs={{0,1},{1,0},{2,3},{3,2},{4,5},{5,4},{6,7},{7,6},{8,9},{9,8},{10,11... | collective-permute-start | bytes 5505032 | tf_op jit(solution)/shard_map/ppermute | solution.py:248
  58.2 1.3 collective-permute-start.14
  59.7 1.9 %collective-permute-done.12.other = bf16[896,1024]{1,0:T(8,128)(2,1)S(1)} collective-permute-done((bf16[896,1024]{1,0:T(8,128)(2,1)S(1)}, bf16[896,1024]{1,0:T(8,128)(2,1)S(1)}, u32[]{:S(2)}, u32[]{:S(2)}) %collective-permute-start.12) | collective-permute-done | bytes 1835040 | tf_op jit(solution)/shard_map/ppermute | solution.py:248
  61.7 5.7 %shard_map.127 = (f32[896,384]{1,0:T(8,128)S(1)}, f32[896,384]{1,0:T(8,128)S(1)}, bf16[896,384]{1,0:T(8,128)(2,1)S(1)}, bf16[896,1024]{1,0:T(8,128)(2,1)S(1)}) custom-call(s32[3]{0:T(128)S(1)} %pad_add_fusion.info, bf16[896,1024]{1,0:T(8,128)(2,1)S(1)} %get-tuple-element.166.own, bf16[896,1024]{1,0:T(8,128)(2,1)S(1)} %collective-permute-done.12.other, ...), custom_call_target="tpu_custom_call" | custom-call | flops 1000 | bytes 1000 | tf_op jit(solution)/shard_map/pallas_call | solution.py:41
  67.4 1.6 %collective-permute-done.13.refs_6_ = bf16[96,1024]{1,0:T(8,128)(2,1)S(1)} collective-permute-done((bf16[96,1024]{1,0:T(8,128)(2,1)S(1)}, bf16[96,1024]{1,0:T(8,128)(2,1)S(1)}, u32[]{:S(2)}, u32[]{:S(2)}) %collective-permute-start.13) | collective-permute-done | bytes 196640 | tf_op jit(solution)/shard_map/ppermute | solution.py:239
  68.9 0.8 collective-permute-start.16
  69.8 1.1 shard_map.128.own
  71.0 2.2 %collective-permute-done.16.came = bf16[896,1024]{1,0:T(8,128)(2,1)S(1)} collective-permute-done((bf16[896,1024]{1,0:T(8,128)(2,1)S(1)}, bf16[896,1024]{1,0:T(8,128)(2,1)S(1)}, u32[]{:S(2)}, u32[]{:S(2)}) %collective-permute-start.16) | collective-permute-done | bytes 1835040 | tf_op jit(solution)/shard_map/ppermute | solution.py:248
  73.2 1.7 %shard_map.129 = (f32[4,128,1024]{2,1,0:T(8,128)S(1)}, bf16[96,1024]{1,0:T(8,128)(2,1)S(1)}, bf16[96,1024]{1,0:T(8,128)(2,1)S(1)}, bf16[96,1024]{1,0:T(8,128)(2,1)S(1)}, bf16[96,1024]{1,0:T(8,128)(2,1)S(1)}) custom-call(s32[3]{0:T(128)S(1)} %pad_add_fusion.info, bf16[896,1024]{1,0:T(8,128)(2,1)S(1)} %collective-permute-done.16.came, ...), custom_call_target="tpu_custom_call" | custom-call | flops 1000 | bytes 1000 | tf_op jit(solution)/shard_map/pallas_call | solution.py:41
  74.9 1.3 collective-permute-start.17
  76.4 5.4 %shard_map.130 = (bf16[896,384]{1,0:T(8,128)(2,1)S(1)}, bf16[896,384]{1,0:T(8,128)(2,1)S(1)}, bf16[896,1024]{1,0:T(8,128)(2,1)S(1)}, f32[4,16,128]{2,1,0:T(8,128)S(1)}, f32[4,16,128]{2,1,0:T(8,128)S(1)}) custom-call(s32[3]{0:T(128)S(1)} %pad_add_fusion.info, bf16[896,1024]{1,0:T(8,128)(2,1)S(1)} %shard_map.128.own, ...), custom_call_target="tpu_custom_call" | custom-call | flops 1000 | bytes 1000 | tf_op jit(solution)/shard_map/pallas_call | solution.py:41
  81.8 3.5 %collective-permute-done.18.back = bf16[96,1024]{1,0:T(8,128)(2,1)S(1)} collective-permute-done((bf16[96,1024]{1,0:T(8,128)(2,1)S(1)}, bf16[96,1024]{1,0:T(8,128)(2,1)S(1)}, u32[]{:S(2)}, u32[]{:S(2)}) %collective-permute-start.18) | collective-permute-done | bytes 196640 | tf_op jit(solution)/shard_map/ppermute | solution.py:239
  85.3 1.2 collective-permute-start.19
  86.5 0.8 shard_map.133
  87.3 2.1 %collective-permute-start.22 = (bf16[128,1024]{1,0:T(8,128)(2,1)S(1)}, bf16[128,1024]{1,0:T(8,128)(2,1)S(1)}, u32[]{:S(2)}, u32[]{:S(2)}) collective-permute-start(bf16[128,1024]{1,0:T(8,128)(2,1)S(1)} %shard_map.133), channel_id=1, source_target_pairs={{0,4},{2,6},{4,8},{6,10},{8,12},{10,14},{12,0},{14,2},{1,5},{3,7},... | collective-permute-start | bytes 786440 | tf_op jit(solution)/shard_map/ppermute | solution.py:242
  89.4 0.8 shard_map.132
  90.8 1.2 collective-permute-start.20
  92.0 3.4 %shard_map.131 = (f32[4,128,1024]{2,1,0:T(8,128)S(1)}, bf16[112,1024]{1,0:T(8,128)(2,1)S(1)}, bf16[112,1024]{1,0:T(8,128)(2,1)S(1)}, bf16[112,1024]{1,0:T(8,128)(2,1)}, bf16[112,1024]{1,0:T(8,128)(2,1)}) custom-call(s32[3]{0:T(128)S(1)} %pad_add_fusion.info, bf16[896,1024]{1,0:T(8,128)(2,1)S(1)} %collective-permute-done.19.came, ...), custom_call_target="tpu_custom_call" | custom-call | flops 1000 | bytes 1000 | tf_op jit(solution)/shard_map/pallas_call | solution.py:41
  95.4 1.3 copy-done
  96.8 3.9 %collective-permute-done.22 = bf16[128,1024]{1,0:T(8,128)(2,1)S(1)} collective-permute-done((bf16[128,1024]{1,0:T(8,128)(2,1)S(1)}, bf16[128,1024]{1,0:T(8,128)(2,1)S(1)}, u32[]{:S(2)}, u32[]{:S(2)}) %collective-permute-start.22) | collective-permute-done | bytes 262176 | tf_op jit(solution)/shard_map/ppermute | solution.py:242
  100.6 5.8 %collective-permute-done.21 = bf16[128,1024]{1,0:T(8,128)(2,1)S(1)} collective-permute-done((bf16[128,1024]{1,0:T(8,128)(2,1)S(1)}, bf16[128,1024]{1,0:T(8,128)(2,1)S(1)}, u32[]{:S(2)}, u32[]{:S(2)}) %collective-permute-start.21) | collective-permute-done | bytes 262176 | tf_op jit(solution)/shard_map/ppermute | solution.py:242
  106.4 1.3 collective-permute-start.24
  107.7 1.5 shard_map.136
  109.2 2.7 %collective-permute-start.25 = (bf16[128,1024]{1,0:T(8,128)(2,1)}, bf16[128,1024]{1,0:T(8,128)(2,1)}, u32[]{:S(2)}, u32[]{:S(2)}) collective-permute-start(bf16[128,1024]{1,0:T(8,128)(2,1)} %shard_map.136), channel_id=1, source_target_pairs={{0,12},{2,14},{4,0},{6,2},{8,4},{10,6},{12,8},{14,10},{1,13},{3,15... | collective-permute-start | bytes 786440 | tf_op jit(solution)/shard_map/ppermute | solution.py:242
  112.2 0.9 collective-permute-done.24.back
  113.1 1.3 collective-permute-start.27
  114.4 4.0 %collective-permute-done.23.back = bf16[112,1024]{1,0:T(8,128)(2,1)} collective-permute-done((bf16[112,1024]{1,0:T(8,128)(2,1)}, bf16[112,1024]{1,0:T(8,128)(2,1)}, u32[]{:S(2)}, u32[]{:S(2)}) %collective-permute-start.23) | collective-permute-done | bytes 229408 | tf_op jit(solution)/shard_map/ppermute | solution.py:239
  118.3 1.6 %copy-done.1 = f32[4,128,1024]{2,1,0:T(8,128)S(1)} copy-done((f32[4,128,1024]{2,1,0:T(8,128)S(1)}, f32[4,128,1024]{2,1,0:T(8,128)}, u32[]{:S(2)}) %copy-start.1) | copy-done | bytes 2097176
  120.7 1.2 shard_map.134
  121.9 1.1 collective-permute-start.26
  123.0 1.2 shard_map.135
  124.8 2.7 %collective-permute-start.30 = (bf16[144,1024]{1,0:T(8,128)(2,1)S(1)}, bf16[144,1024]{1,0:T(8,128)(2,1)S(1)}, u32[]{:S(2)}, u32[]{:S(2)}) collective-permute-start(bf16[144,1024]{1,0:T(8,128)(2,1)S(1)} %shard_map.134), channel_id=1, source_target_pairs={{0,8},{2,10},{4,12},{6,14},{8,0},{10,2},{12,4},{14,6},{1,9},{3,11}... | collective-permute-start | bytes 884744 | tf_op jit(solution)/shard_map/ppermute | solution.py:242
  127.6 1.1 collective-permute-start.31
  128.6 0.8 shard_map.138
  129.4 1.8 %add_convert_fusion.1 = bf16[128,1024]{1,0:T(8,128)(2,1)} fusion(bf16[128,1024]{1,0:T(8,128)(2,1)S(1)} %copy-done.28, bf16[128,1024]{1,0:T(8,128)(2,1)S(1)} %copy-done.30, bf16[128,1024]{1,0:T(8,128)(2,1)} %collective-permute-done.25, bf16[128,1024]{1,0:T(8,128)(2,1)S(1)} %shard_map.138), kind=kLoop, calls=%fused_computation.16 | loop fusion | flops 1048576 | bytes 1310720 | tf_op jit(solution)/shard_map/convert_element_type | solution.py:347
  131.3 0.8 shard_map.139
  132.1 0.8 shard_map.137
  133.0 3.5 %collective-permute-start.29 = (bf16[144,1024]{1,0:T(8,128)(2,1)S(1)}, bf16[144,1024]{1,0:T(8,128)(2,1)S(1)}, u32[]{:S(2)}, u32[]{:S(2)}) collective-permute-start(bf16[144,1024]{1,0:T(8,128)(2,1)S(1)} %shard_map.137), channel_id=1, source_target_pairs={{0,12},{2,14},{4,0},{6,2},{8,4},{10,6},{12,8},{14,10},{1,13},{3,15... | collective-permute-start | bytes 884744 | tf_op jit(solution)/shard_map/ppermute | solution.py:242
  137.0 3.4 %fusion.7 = bf16[1,2048,384]{2,1,0:T(8,128)(2,1)} fusion(bf16[896,384]{1,0:T(8,128)(2,1)S(1)} %get-tuple-element.136.refs_0_, bf16[896,1024]{1,0:T(8,128)(2,1)S(1)} %get-tuple-element.181, bf16[896,1024]{1,0:T(8,128)(2,1)S(1)} %get-tuple-element.180), kind=kOutput, calls=%fused_computation.8 | convolution fusion | flops 1417412608 | bytes 5931008 | tf_op jit(solution)/shard_map/dot_general | solution.py:24
  140.4 3.4 %fusion.8 = bf16[1,2048,384]{2,1,0:T(8,128)(2,1)} fusion(bf16[896,384]{1,0:T(8,128)(2,1)S(1)} %get-tuple-element.168.refs_1_, bf16[896,1024]{1,0:T(8,128)(2,1)S(1)} %get-tuple-element.181, bf16[896,1024]{1,0:T(8,128)(2,1)S(1)} %get-tuple-element.180), kind=kOutput, calls=%fused_computation.9 | convolution fusion | flops 1417412608 | bytes 5931008 | tf_op jit(solution)/shard_map/dot_general | solution.py:24
  143.8 3.0 %fusion.9 = bf16[1,384,2048]{2,1,0:T(8,128)(2,1)} fusion(bf16[896,384]{1,0:T(8,128)(2,1)S(1)} %copy-done.15, bf16[896,1024]{1,0:T(8,128)(2,1)S(1)} %get-tuple-element.179, bf16[896,1024]{1,0:T(8,128)(2,1)S(1)} %get-tuple-element.178), kind=kOutput, calls=%fused_computation.10 | convolution fusion | flops 1417412608 | bytes 5931008 | tf_op jit(solution)/shard_map/dot_general | solution.py:24
  146.9 5.2 %collective-permute-done.31 = bf16[144,1024]{1,0:T(8,128)(2,1)S(1)} collective-permute-done((bf16[144,1024]{1,0:T(8,128)(2,1)S(1)}, bf16[144,1024]{1,0:T(8,128)(2,1)S(1)}, u32[]{:S(2)}, u32[]{:S(2)}) %collective-permute-start.31) | collective-permute-done | bytes 294944 | tf_op jit(solution)/shard_map/ppermute | solution.py:242
  152.1 1.9 %collective-permute-done.29 = bf16[144,1024]{1,0:T(8,128)(2,1)S(1)} collective-permute-done((bf16[144,1024]{1,0:T(8,128)(2,1)S(1)}, bf16[144,1024]{1,0:T(8,128)(2,1)S(1)}, u32[]{:S(2)}, u32[]{:S(2)}) %collective-permute-start.29) | collective-permute-done | bytes 294944 | tf_op jit(solution)/shard_map/ppermute | solution.py:242
  154.6 0.9 add_convert_fusion
  (118 shorter events, 9.1 us)
Async XLA Ops:
  2.4 7.9 %collective-permute-start.2 = (bf16[144,1024]{1,0:T(8,128)(2,1)S(1)}, bf16[144,1024]{1,0:T(8,128)(2,1)S(1)}, u32[]{:S(2)}, u32[]{:S(2)}) collective-permute-start(bf16[144,1024]{1,0:T(8,128)(2,1)S(1)} %pad_maximum_fusion.3.block.refs_0_), channel_id=1, source_target_pairs={{0,12},{2,14},{4,0},{6,2},{8,4},{10,6},{12,8},{14,10},{1,13},{3,15... | collective-permute-start | bytes 884744 | tf_op jit(solution)/shard_map/ppermute | solution.py:242
  2.4 16.3 %collective-permute-start = (bf16[144,1024]{1,0:T(8,128)(2,1)S(1)}, bf16[144,1024]{1,0:T(8,128)(2,1)S(1)}, u32[]{:S(2)}, u32[]{:S(2)}) collective-permute-start(bf16[144,1024]{1,0:T(8,128)(2,1)S(1)} %pad_maximum_fusion.3.block.refs_0_), channel_id=1, source_target_pairs={{0,4},{2,6},{4,8},{6,10},{8,12},{10,14},{12,0},{14,2},{1,5},{3,7},... | collective-permute-start | bytes 884744 | tf_op jit(solution)/shard_map/ppermute | solution.py:242
  3.9 24.3 %collective-permute-start.1 = (bf16[144,1024]{1,0:T(8,128)(2,1)S(1)}, bf16[144,1024]{1,0:T(8,128)(2,1)S(1)}, u32[]{:S(2)}, u32[]{:S(2)}) collective-permute-start(bf16[144,1024]{1,0:T(8,128)(2,1)S(1)} %pad_maximum_fusion.3.block.refs_0_), channel_id=1, source_target_pairs={{0,8},{2,10},{4,12},{6,14},{8,0},{10,2},{12,4},{14,6},{1,9},{3,11}... | collective-permute-start | bytes 884744 | tf_op jit(solution)/shard_map/ppermute | solution.py:242
  9.0 17.7 %collective-permute-start.3 = (bf16[112,1024]{1,0:T(8,128)(2,1)S(1)}, bf16[112,1024]{1,0:T(8,128)(2,1)S(1)}, u32[]{:S(2)}, u32[]{:S(2)}) collective-permute-start(bf16[112,1024]{1,0:T(8,128)(2,1)S(1)} %get-tuple-element.88), channel_id=1, source_target_pairs={{0,2},{2,0},{4,6},{6,4},{8,10},{10,8},{12,14},{14,12},{1,3},{3,1},... | collective-permute-start | bytes 688136 | tf_op jit(solution)/shard_map/ppermute | solution.py:239
  10.3 51.4 %copy-start.7 = (bf16[1,2048,384]{2,1,0:T(8,128)(2,1)S(1)}, bf16[1,2048,384]{2,1,0:T(8,128)(2,1)}, u32[]{:S(2)}) copy-start(bf16[1,2048,384]{2,1,0:T(8,128)(2,1)} %param.11) | copy-start | bytes 4718596
  11.2 75.3 %copy-start.18 = (bf16[96,128]{1,0:T(8,128)(2,1)}, bf16[96,128]{1,0:T(8,128)(2,1)S(1)}, u32[]{:S(2)}) copy-start(bf16[96,128]{1,0:T(8,128)(2,1)S(1)} %get-tuple-element.99.place) | copy-start | bytes 73732
  11.2 17.0 %collective-permute-start.5 = (bf16[112,1024]{1,0:T(8,128)(2,1)S(1)}, bf16[112,1024]{1,0:T(8,128)(2,1)S(1)}, u32[]{:S(2)}, u32[]{:S(2)}) collective-permute-start(bf16[112,1024]{1,0:T(8,128)(2,1)S(1)} %get-tuple-element.90), channel_id=1, source_target_pairs={{0,2},{2,0},{4,6},{6,4},{8,10},{10,8},{12,14},{14,12},{1,3},{3,1},... | collective-permute-start | bytes 688136 | tf_op jit(solution)/shard_map/ppermute | solution.py:239
  19.6 88.0 %copy-start.16 = (bf16[96,128]{1,0:T(8,128)(2,1)}, bf16[96,128]{1,0:T(8,128)(2,1)S(1)}, u32[]{:S(2)}) copy-start(bf16[96,128]{1,0:T(8,128)(2,1)S(1)} %get-tuple-element.97.place) | copy-start | bytes 73732
  19.6 8.6 %collective-permute-start.4 = (bf16[112,1024]{1,0:T(8,128)(2,1)S(1)}, bf16[112,1024]{1,0:T(8,128)(2,1)S(1)}, u32[]{:S(2)}, u32[]{:S(2)}) collective-permute-start(bf16[112,1024]{1,0:T(8,128)(2,1)S(1)} %get-tuple-element.89), channel_id=1, source_target_pairs={{0,2},{2,0},{4,6},{6,4},{8,10},{10,8},{12,14},{14,12},{1,3},{3,1},... | collective-permute-start | bytes 688136 | tf_op jit(solution)/shard_map/ppermute | solution.py:239
  22.1 4.6 %collective-permute-start.6 = (bf16[96,1024]{1,0:T(8,128)(2,1)S(1)}, bf16[96,1024]{1,0:T(8,128)(2,1)S(1)}, u32[]{:S(2)}, u32[]{:S(2)}) collective-permute-start(bf16[96,1024]{1,0:T(8,128)(2,1)S(1)} %shard_map.121), channel_id=1, source_target_pairs={{0,2},{2,0},{4,6},{6,4},{8,10},{10,8},{12,14},{14,12},{1,3},{3,1},... | collective-permute-start | bytes 589832 | tf_op jit(solution)/shard_map/ppermute | solution.py:239
  28.2 6.8 %collective-permute-start.8 = (bf16[128,1024]{1,0:T(8,128)(2,1)}, bf16[128,1024]{1,0:T(8,128)(2,1)S(1)}, u32[]{:S(2)}, u32[]{:S(2)}) collective-permute-start(bf16[128,1024]{1,0:T(8,128)(2,1)} %refs_0_), channel_id=1, source_target_pairs={{0,4},{2,6},{4,8},{6,10},{8,12},{10,14},{12,0},{14,2},{1,5},{3,7},... | collective-permute-start | bytes 786440 | tf_op jit(solution)/shard_map/ppermute | solution.py:242
  28.5 12.8 %collective-permute-start.10 = (bf16[128,1024]{1,0:T(8,128)(2,1)}, bf16[128,1024]{1,0:T(8,128)(2,1)S(1)}, u32[]{:S(2)}, u32[]{:S(2)}) collective-permute-start(bf16[128,1024]{1,0:T(8,128)(2,1)} %refs_0_), channel_id=1, source_target_pairs={{0,12},{2,14},{4,0},{6,2},{8,4},{10,6},{12,8},{14,10},{1,13},{3,15... | collective-permute-start | bytes 786440 | tf_op jit(solution)/shard_map/ppermute | solution.py:242
  30.5 19.2 %collective-permute-start.9 = (bf16[128,1024]{1,0:T(8,128)(2,1)}, bf16[128,1024]{1,0:T(8,128)(2,1)S(1)}, u32[]{:S(2)}, u32[]{:S(2)}) collective-permute-start(bf16[128,1024]{1,0:T(8,128)(2,1)} %refs_0_), channel_id=1, source_target_pairs={{0,8},{2,10},{4,12},{6,14},{8,0},{10,2},{12,4},{14,6},{1,9},{3,11}... | collective-permute-start | bytes 786440 | tf_op jit(solution)/shard_map/ppermute | solution.py:242
  33.7 55.8 %copy-start.20 = (bf16[96,128]{1,0:T(8,128)(2,1)}, bf16[96,128]{1,0:T(8,128)(2,1)S(1)}, u32[]{:S(2)}) copy-start(bf16[96,128]{1,0:T(8,128)(2,1)S(1)} %get-tuple-element.98.place) | copy-start | bytes 73732
  33.7 28.0 %copy-start.5 = (bf16[1,384,2048]{2,1,0:T(8,128)(2,1)S(1)}, bf16[1,384,2048]{2,1,0:T(8,128)(2,1)}, u32[]{:S(2)}) copy-start(bf16[1,384,2048]{2,1,0:T(8,128)(2,1)} %param.12) | copy-start | bytes 4718596
  33.7 28.0 %copy-start.6 = (bf16[1,2048,384]{2,1,0:T(8,128)(2,1)S(1)}, bf16[1,2048,384]{2,1,0:T(8,128)(2,1)}, u32[]{:S(2)}) copy-start(bf16[1,2048,384]{2,1,0:T(8,128)(2,1)} %param.10) | copy-start | bytes 4718596
  33.7 16.7 %collective-permute-start.7 = (bf16[112,1024]{1,0:T(8,128)(2,1)S(1)}, bf16[112,1024]{1,0:T(8,128)(2,1)S(1)}, u32[]{:S(2)}, u32[]{:S(2)}) collective-permute-start(bf16[112,1024]{1,0:T(8,128)(2,1)S(1)} %get-tuple-element.94), channel_id=1, source_target_pairs={{0,2},{2,0},{4,6},{6,4},{8,10},{10,8},{12,14},{14,12},{1,3},{3,1},... | collective-permute-start | bytes 688136 | tf_op jit(solution)/shard_map/ppermute | solution.py:239
  35.8 14.7 %collective-permute-start.11 = (bf16[96,1024]{1,0:T(8,128)(2,1)S(1)}, bf16[96,1024]{1,0:T(8,128)(2,1)S(1)}, u32[]{:S(2)}, u32[]{:S(2)}) collective-permute-start(bf16[96,1024]{1,0:T(8,128)(2,1)S(1)} %shard_map.123), channel_id=1, source_target_pairs={{0,2},{2,0},{4,6},{6,4},{8,10},{10,8},{12,14},{14,12},{1,3},{3,1},... | collective-permute-start | bytes 589832 | tf_op jit(solution)/shard_map/ppermute | solution.py:239
  51.2 16.1 %copy-start.8 = (bf16[896,1024]{1,0:T(8,128)(2,1)}, bf16[896,1024]{1,0:T(8,128)(2,1)S(1)}, u32[]{:S(2)}) copy-start(bf16[896,1024]{1,0:T(8,128)(2,1)S(1)} %get-tuple-element.166.own) | copy-start | bytes 5505028
  51.3 10.4 %collective-permute-start.12 = (bf16[896,1024]{1,0:T(8,128)(2,1)S(1)}, bf16[896,1024]{1,0:T(8,128)(2,1)S(1)}, u32[]{:S(2)}, u32[]{:S(2)}) collective-permute-start(bf16[896,1024]{1,0:T(8,128)(2,1)S(1)} %get-tuple-element.166.own), channel_id=1, source_target_pairs={{0,1},{1,0},{2,3},{3,2},{4,5},{5,4},{6,7},{7,6},{8,9},{9,8},{10,11... | collective-permute-start | bytes 5505032 | tf_op jit(solution)/shard_map/ppermute | solution.py:248
  58.2 9.1 %collective-permute-start.14 = (bf16[96,1024]{1,0:T(8,128)(2,1)S(1)}, bf16[96,1024]{1,0:T(8,128)(2,1)S(1)}, u32[]{:S(2)}, u32[]{:S(2)}) collective-permute-start(bf16[96,1024]{1,0:T(8,128)(2,1)S(1)} %shard_map.125), channel_id=1, source_target_pairs={{0,2},{2,0},{4,6},{6,4},{8,10},{10,8},{12,14},{14,12},{1,3},{3,1},... | collective-permute-start | bytes 589832 | tf_op jit(solution)/shard_map/ppermute | solution.py:239
  59.5 9.4 %collective-permute-start.13 = (bf16[96,1024]{1,0:T(8,128)(2,1)S(1)}, bf16[96,1024]{1,0:T(8,128)(2,1)S(1)}, u32[]{:S(2)}, u32[]{:S(2)}) collective-permute-start(bf16[96,1024]{1,0:T(8,128)(2,1)S(1)} %shard_map.124), channel_id=1, source_target_pairs={{0,2},{2,0},{4,6},{6,4},{8,10},{10,8},{12,14},{14,12},{1,3},{3,1},... | collective-permute-start | bytes 589832 | tf_op jit(solution)/shard_map/ppermute | solution.py:239
  61.7 5.7 %copy-start.10 = (bf16[896,1024]{1,0:T(8,128)(2,1)}, bf16[896,1024]{1,0:T(8,128)(2,1)S(1)}, u32[]{:S(2)}) copy-start(bf16[896,1024]{1,0:T(8,128)(2,1)S(1)} %collective-permute-done.12.other) | copy-start | bytes 5505028
  67.3 5.9 %copy-start.14 = (bf16[896,384]{1,0:T(8,128)(2,1)}, bf16[896,384]{1,0:T(8,128)(2,1)S(1)}, u32[]{:S(2)}) copy-start(bf16[896,384]{1,0:T(8,128)(2,1)S(1)} %get-tuple-element.126.refs_0_) | copy-start | bytes 2064388
  68.9 4.3 %collective-permute-start.16 = (bf16[896,1024]{1,0:T(8,128)(2,1)S(1)}, bf16[896,1024]{1,0:T(8,128)(2,1)S(1)}, u32[]{:S(2)}, u32[]{:S(2)}) collective-permute-start(bf16[896,1024]{1,0:T(8,128)(2,1)S(1)} %get-tuple-element.125), channel_id=1, source_target_pairs={{0,1},{1,0},{2,3},{3,2},{4,5},{5,4},{6,7},{7,6},{8,9},{9,8},{10,11... | collective-permute-start | bytes 5505032 | tf_op jit(solution)/shard_map/ppermute | solution.py:248
  70.9 5.6 %copy-start.3 = (bf16[896,1024]{1,0:T(8,128)(2,1)}, bf16[896,1024]{1,0:T(8,128)(2,1)S(1)}, u32[]{:S(2)}) copy-start(bf16[896,1024]{1,0:T(8,128)(2,1)S(1)} %shard_map.128.own) | copy-start | bytes 5505028
  70.9 5.5 %collective-permute-start.15 = (bf16[896,1024]{1,0:T(8,128)(2,1)S(1)}, bf16[896,1024]{1,0:T(8,128)(2,1)S(1)}, u32[]{:S(2)}, u32[]{:S(2)}) collective-permute-start(bf16[896,1024]{1,0:T(8,128)(2,1)S(1)} %shard_map.128.own), channel_id=1, source_target_pairs={{0,1},{1,0},{2,3},{3,2},{4,5},{5,4},{6,7},{7,6},{8,9},{9,8},{10,11... | collective-permute-start | bytes 5505032 | tf_op jit(solution)/shard_map/ppermute | solution.py:248
  74.9 6.9 %copy-start.26 = (bf16[96,1024]{1,0:T(8,128)(2,1)}, bf16[96,1024]{1,0:T(8,128)(2,1)S(1)}, u32[]{:S(2)}) copy-start(bf16[96,1024]{1,0:T(8,128)(2,1)S(1)} %get-tuple-element.159) | copy-start | bytes 589828
  74.9 6.9 %collective-permute-start.17 = (bf16[96,1024]{1,0:T(8,128)(2,1)S(1)}, bf16[96,1024]{1,0:T(8,128)(2,1)S(1)}, u32[]{:S(2)}, u32[]{:S(2)}) collective-permute-start(bf16[96,1024]{1,0:T(8,128)(2,1)S(1)} %get-tuple-element.129), channel_id=1, source_target_pairs={{0,2},{2,0},{4,6},{6,4},{8,10},{10,8},{12,14},{14,12},{1,3},{3,1},... | collective-permute-start | bytes 589832 | tf_op jit(solution)/shard_map/ppermute | solution.py:239
  76.2 9.1 %collective-permute-start.18 = (bf16[96,1024]{1,0:T(8,128)(2,1)S(1)}, bf16[96,1024]{1,0:T(8,128)(2,1)S(1)}, u32[]{:S(2)}, u32[]{:S(2)}) collective-permute-start(bf16[96,1024]{1,0:T(8,128)(2,1)S(1)} %get-tuple-element.130), channel_id=1, source_target_pairs={{0,2},{2,0},{4,6},{6,4},{8,10},{10,8},{12,14},{14,12},{1,3},{3,1},... | collective-permute-start | bytes 589832 | tf_op jit(solution)/shard_map/ppermute | solution.py:239
  76.4 5.4 %copy-start.12 = (bf16[896,1024]{1,0:T(8,128)(2,1)}, bf16[896,1024]{1,0:T(8,128)(2,1)S(1)}, u32[]{:S(2)}) copy-start(bf16[896,1024]{1,0:T(8,128)(2,1)S(1)} %collective-permute-done.15.other) | copy-start | bytes 5505028
  85.3 6.8 %collective-permute-start.19 = (bf16[896,1024]{1,0:T(8,128)(2,1)S(1)}, bf16[896,1024]{1,0:T(8,128)(2,1)S(1)}, u32[]{:S(2)}, u32[]{:S(2)}) collective-permute-start(bf16[896,1024]{1,0:T(8,128)(2,1)S(1)} %get-tuple-element.135), channel_id=1, source_target_pairs={{0,1},{1,0},{2,3},{3,2},{4,5},{5,4},{6,7},{7,6},{8,9},{9,8},{10,11... | collective-permute-start | bytes 5505032 | tf_op jit(solution)/shard_map/ppermute | solution.py:248
  87.3 13.3 %collective-permute-start.22 = (bf16[128,1024]{1,0:T(8,128)(2,1)S(1)}, bf16[128,1024]{1,0:T(8,128)(2,1)S(1)}, u32[]{:S(2)}, u32[]{:S(2)}) collective-permute-start(bf16[128,1024]{1,0:T(8,128)(2,1)S(1)} %shard_map.133), channel_id=1, source_target_pairs={{0,4},{2,6},{4,8},{6,10},{8,12},{10,14},{12,0},{14,2},{1,5},{3,7},... | collective-permute-start | bytes 786440 | tf_op jit(solution)/shard_map/ppermute | solution.py:242
  90.2 16.2 %collective-permute-start.21 = (bf16[128,1024]{1,0:T(8,128)(2,1)S(1)}, bf16[128,1024]{1,0:T(8,128)(2,1)S(1)}, u32[]{:S(2)}, u32[]{:S(2)}) collective-permute-start(bf16[128,1024]{1,0:T(8,128)(2,1)S(1)} %shard_map.132), channel_id=1, source_target_pairs={{0,8},{2,10},{4,12},{6,14},{8,0},{10,2},{12,4},{14,6},{1,9},{3,11}... | collective-permute-start | bytes 786440 | tf_op jit(solution)/shard_map/ppermute | solution.py:242
  90.8 5.9 %collective-permute-start.20 = (bf16[96,1024]{1,0:T(8,128)(2,1)S(1)}, bf16[96,1024]{1,0:T(8,128)(2,1)S(1)}, u32[]{:S(2)}, u32[]{:S(2)}) collective-permute-start(bf16[96,1024]{1,0:T(8,128)(2,1)S(1)} %get-tuple-element.144), channel_id=1, source_target_pairs={{0,2},{2,0},{4,6},{6,4},{8,10},{10,8},{12,14},{14,12},{1,3},{3,1},... | collective-permute-start | bytes 589832 | tf_op jit(solution)/shard_map/ppermute | solution.py:239
  95.4 1.3 copy-start
  96.7 12.4 %copy-start.22 = (bf16[112,1024]{1,0:T(8,128)(2,1)}, bf16[112,1024]{1,0:T(8,128)(2,1)S(1)}, u32[]{:S(2)}) copy-start(bf16[112,1024]{1,0:T(8,128)(2,1)S(1)} %get-tuple-element.157) | copy-start | bytes 688132
  96.7 15.1 %copy-start.24 = (bf16[112,1024]{1,0:T(8,128)(2,1)}, bf16[112,1024]{1,0:T(8,128)(2,1)S(1)}, u32[]{:S(2)}) copy-start(bf16[112,1024]{1,0:T(8,128)(2,1)S(1)} %get-tuple-element.165) | copy-start | bytes 688132
  96.7 17.6 %copy-start.31 = (s32[128,4]{0,1:T(4,128)S(1)}, s32[128,4]{0,1:T(4,128)}, u32[]{:S(2)}) copy-start(s32[128,4]{0,1:T(4,128)} %param.8) | copy-start | bytes 6148
  100.6 11.3 %copy-start.27 = (bf16[128,1024]{1,0:T(8,128)(2,1)}, bf16[128,1024]{1,0:T(8,128)(2,1)S(1)}, u32[]{:S(2)}) copy-start(bf16[128,1024]{1,0:T(8,128)(2,1)S(1)} %collective-permute-done.22) | copy-start | bytes 786436
  106.4 5.5 %copy-start.29 = (bf16[128,1024]{1,0:T(8,128)(2,1)}, bf16[128,1024]{1,0:T(8,128)(2,1)S(1)}, u32[]{:S(2)}) copy-start(bf16[128,1024]{1,0:T(8,128)(2,1)S(1)} %collective-permute-done.21) | copy-start | bytes 786436
  106.4 6.7 %collective-permute-start.24 = (bf16[112,1024]{1,0:T(8,128)(2,1)}, bf16[112,1024]{1,0:T(8,128)(2,1)}, u32[]{:S(2)}, u32[]{:S(2)}) collective-permute-start(bf16[112,1024]{1,0:T(8,128)(2,1)} %get-tuple-element.150), channel_id=1, source_target_pairs={{0,2},{2,0},{4,6},{6,4},{8,10},{10,8},{12,14},{14,12},{1,3},{3,1},... | collective-permute-start | bytes 688136 | tf_op jit(solution)/shard_map/ppermute | solution.py:239
  109.2 15.7 %collective-permute-start.25 = (bf16[128,1024]{1,0:T(8,128)(2,1)}, bf16[128,1024]{1,0:T(8,128)(2,1)}, u32[]{:S(2)}, u32[]{:S(2)}) collective-permute-start(bf16[128,1024]{1,0:T(8,128)(2,1)} %shard_map.136), channel_id=1, source_target_pairs={{0,12},{2,14},{4,0},{6,2},{8,4},{10,6},{12,8},{14,10},{1,13},{3,15... | collective-permute-start | bytes 786440 | tf_op jit(solution)/shard_map/ppermute | solution.py:242
  111.9 6.4 %collective-permute-start.23 = (bf16[112,1024]{1,0:T(8,128)(2,1)}, bf16[112,1024]{1,0:T(8,128)(2,1)}, u32[]{:S(2)}, u32[]{:S(2)}) collective-permute-start(bf16[112,1024]{1,0:T(8,128)(2,1)} %get-tuple-element.148), channel_id=1, source_target_pairs={{0,2},{2,0},{4,6},{6,4},{8,10},{10,8},{12,14},{14,12},{1,3},{3,1},... | collective-permute-start | bytes 688136 | tf_op jit(solution)/shard_map/ppermute | solution.py:239
  113.1 15.6 %collective-permute-start.27 = (bf16[96,1024]{1,0:T(8,128)(2,1)}, bf16[96,1024]{1,0:T(8,128)(2,1)S(1)}, u32[]{:S(2)}, u32[]{:S(2)}) collective-permute-start(bf16[96,1024]{1,0:T(8,128)(2,1)} %copy-done.26), channel_id=1, source_target_pairs={{0,2},{2,0},{4,6},{6,4},{8,10},{10,8},{12,14},{14,12},{1,3},{3,1},... | collective-permute-start | bytes 589832 | tf_op jit(solution)/shard_map/ppermute | solution.py:239
  118.3 1.6 %copy-start.1 = (f32[4,128,1024]{2,1,0:T(8,128)S(1)}, f32[4,128,1024]{2,1,0:T(8,128)}, u32[]{:S(2)}) copy-start(f32[4,128,1024]{2,1,0:T(8,128)} %copy-done) | copy-start | bytes 6291460
  120.7 1.2 copy-start.23
  120.7 2.3 %copy-start.19 = (bf16[96,128]{1,0:T(8,128)(2,1)S(1)}, bf16[96,128]{1,0:T(8,128)(2,1)}, u32[]{:S(2)}) copy-start(bf16[96,128]{1,0:T(8,128)(2,1)} %copy-done.18) | copy-start | bytes 73732
  121.9 2.3 %copy-start.25 = (bf16[112,1024]{1,0:T(8,128)(2,1)S(1)}, bf16[112,1024]{1,0:T(8,128)(2,1)}, u32[]{:S(2)}) copy-start(bf16[112,1024]{1,0:T(8,128)(2,1)} %copy-done.24) | copy-start | bytes 688132
  121.9 10.2 %collective-permute-start.26 = (bf16[112,1024]{1,0:T(8,128)(2,1)S(1)}, bf16[112,1024]{1,0:T(8,128)(2,1)S(1)}, u32[]{:S(2)}, u32[]{:S(2)}) collective-permute-start(bf16[112,1024]{1,0:T(8,128)(2,1)S(1)} %copy-done.23), channel_id=1, source_target_pairs={{0,2},{2,0},{4,6},{6,4},{8,10},{10,8},{12,14},{14,12},{1,3},{3,1},... | collective-permute-start | bytes 688136 | tf_op jit(solution)/shard_map/ppermute | solution.py:239
  123.0 6.4 %copy-start.30 = (bf16[128,1024]{1,0:T(8,128)(2,1)S(1)}, bf16[128,1024]{1,0:T(8,128)(2,1)}, u32[]{:S(2)}) copy-start(bf16[128,1024]{1,0:T(8,128)(2,1)} %copy-done.29) | copy-start | bytes 786436
  124.3 5.2 %copy-start.28 = (bf16[128,1024]{1,0:T(8,128)(2,1)S(1)}, bf16[128,1024]{1,0:T(8,128)(2,1)}, u32[]{:S(2)}) copy-start(bf16[128,1024]{1,0:T(8,128)(2,1)} %copy-done.27) | copy-start | bytes 786436
  124.3 7.0 %copy-start.2 = (f32[4,128,1024]{2,1,0:T(8,128)S(1)}, f32[4,128,1024]{2,1,0:T(8,128)}, u32[]{:S(2)}) copy-start(f32[4,128,1024]{2,1,0:T(8,128)} %copy-done) | copy-start | bytes 6291460
  124.3 7.0 %collective-permute-start.28 = (bf16[112,1024]{1,0:T(8,128)(2,1)S(1)}, bf16[112,1024]{1,0:T(8,128)(2,1)S(1)}, u32[]{:S(2)}, u32[]{:S(2)}) collective-permute-start(bf16[112,1024]{1,0:T(8,128)(2,1)S(1)} %copy-done.25), channel_id=1, source_target_pairs={{0,2},{2,0},{4,6},{6,4},{8,10},{10,8},{12,14},{14,12},{1,3},{3,1},... | collective-permute-start | bytes 688136 | tf_op jit(solution)/shard_map/ppermute | solution.py:239
  124.8 22.0 %collective-permute-start.30 = (bf16[144,1024]{1,0:T(8,128)(2,1)S(1)}, bf16[144,1024]{1,0:T(8,128)(2,1)S(1)}, u32[]{:S(2)}, u32[]{:S(2)}) collective-permute-start(bf16[144,1024]{1,0:T(8,128)(2,1)S(1)} %shard_map.134), channel_id=1, source_target_pairs={{0,8},{2,10},{4,12},{6,14},{8,0},{10,2},{12,4},{14,6},{1,9},{3,11}... | collective-permute-start | bytes 884744 | tf_op jit(solution)/shard_map/ppermute | solution.py:242
  127.6 24.5 %collective-permute-start.31 = (bf16[144,1024]{1,0:T(8,128)(2,1)S(1)}, bf16[144,1024]{1,0:T(8,128)(2,1)S(1)}, u32[]{:S(2)}, u32[]{:S(2)}) collective-permute-start(bf16[144,1024]{1,0:T(8,128)(2,1)S(1)} %shard_map.135), channel_id=1, source_target_pairs={{0,4},{2,6},{4,8},{6,10},{8,12},{10,14},{12,0},{14,2},{1,5},{3,7},... | collective-permute-start | bytes 884744 | tf_op jit(solution)/shard_map/ppermute | solution.py:242
  129.4 2.7 %copy-start.17 = (bf16[96,128]{1,0:T(8,128)(2,1)S(1)}, bf16[96,128]{1,0:T(8,128)(2,1)}, u32[]{:S(2)}) copy-start(bf16[96,128]{1,0:T(8,128)(2,1)} %copy-done.16) | copy-start | bytes 73732
  131.3 5.2 %copy-start.13 = (bf16[896,1024]{1,0:T(8,128)(2,1)S(1)}, bf16[896,1024]{1,0:T(8,128)(2,1)}, u32[]{:S(2)}) copy-start(bf16[896,1024]{1,0:T(8,128)(2,1)} %copy-done.12) | copy-start | bytes 5505028
  132.1 4.4 %copy-start.4 = (bf16[896,1024]{1,0:T(8,128)(2,1)S(1)}, bf16[896,1024]{1,0:T(8,128)(2,1)}, u32[]{:S(2)}) copy-start(bf16[896,1024]{1,0:T(8,128)(2,1)} %copy-done.3) | copy-start | bytes 5505028
  132.9 3.8 %copy-start.9 = (bf16[896,1024]{1,0:T(8,128)(2,1)S(1)}, bf16[896,1024]{1,0:T(8,128)(2,1)}, u32[]{:S(2)}) copy-start(bf16[896,1024]{1,0:T(8,128)(2,1)} %copy-done.8) | copy-start | bytes 5505028
  132.9 3.8 %copy-start.11 = (bf16[896,1024]{1,0:T(8,128)(2,1)S(1)}, bf16[896,1024]{1,0:T(8,128)(2,1)}, u32[]{:S(2)}) copy-start(bf16[896,1024]{1,0:T(8,128)(2,1)} %copy-done.10) | copy-start | bytes 5505028
  133.0 21.1 %collective-permute-start.29 = (bf16[144,1024]{1,0:T(8,128)(2,1)S(1)}, bf16[144,1024]{1,0:T(8,128)(2,1)S(1)}, u32[]{:S(2)}, u32[]{:S(2)}) collective-permute-start(bf16[144,1024]{1,0:T(8,128)(2,1)S(1)} %shard_map.137), channel_id=1, source_target_pairs={{0,12},{2,14},{4,0},{6,2},{8,4},{10,6},{12,8},{14,10},{1,13},{3,15... | collective-permute-start | bytes 884744 | tf_op jit(solution)/shard_map/ppermute | solution.py:242
  140.4 3.4 %copy-start.15 = (bf16[896,384]{1,0:T(8,128)(2,1)S(1)}, bf16[896,384]{1,0:T(8,128)(2,1)}, u32[]{:S(2)}) copy-start(bf16[896,384]{1,0:T(8,128)(2,1)} %copy-done.14) | copy-start | bytes 2064388
  154.1 1.4 collective-permute-start.32
  (1 other events, 0.7 us)

commit v13 on v12

--- a/solution.py
+++ b/solution.py
@@ -361,8 +361,12 @@
         (shape_of((lines, token_count, half_width), F32),
          *[shape_of((padded + TAIL, half_width)) for _ in every]),
         (info, came, grad_gate, grad_up, gate_local, up_local, compact_tails))
+    distant = out_came.pop(outward[0])
     in_packed, out_back[trailing], out_came = settle((in_packed, out_back[trailing], out_came))
     trailing_home = to_home(trailing, out_dense, out_back)
+    later, out_came[outward[0]], _ = settle(
+        (in_packed[:outward[0]] + in_packed[outward[0] + 1:], distant, trailing_home))
+    in_packed = later[:outward[0]] + [in_packed[outward[0]]] + later[outward[0]:]
     out_came[trailing] = over_line(trailing_home, lines - trailing)
     in_back, in_home, sequence = {}, {}, outward + [0]
     for i, k in enumerate(sequence):

time: 158 us -> 158 us (level)
    ppermute x12, waiting for transfers between devices: 36.7 us -> 34.2 us  [over_line(): lax.ppermute(x, 'expert', [(i, (i // 2 + k) % lines * 2 + i % 2) for i in...]
    ppermute x16, waiting for transfers between devices: 14.2 us -> 16.4 us  [over_pair(): lax.ppermute(x, 'expert', [(i, i + 1 - 2 * (i % 2)) for i in range(expert...]
  transfers between devices with their start and end apart: 33 -> 33, of which waited for: 15 -> 16; matrix products, arithmetic and copies ran while one was open for 8% -> 8% of each run, Pallas kernels for 20% -> 20%
where the time goes in v13:
time: 158 us; the launch traced here: 156 us
  waiting for transfers between devices  54.8 us (35%)
  starting transfers between devices  47.4 us (30%)
  Pallas kernels  32.7 us (21%)
  matrix products  9.84 us (6%)
  other arithmetic  5.73 us (4%)
  local copies, waits for them, and re-layouts  4.5 us (3%)
    ppermute x12, waiting for transfers between devices, over_line(): lax.ppermute(x, 'expert', [(i, (i // 2 + k) % lines * 2 + i % 2) for i in...  34.2 us
    pallas_call x22, Pallas kernels, local_call(): pl.pallas_call(kernel, out_shape=tuple(outs), in_specs=[SMEM_SPEC] + [VME...  32.7 us
    ppermute x12, starting transfers between devices, over_line(): lax.ppermute(x, 'expert', [(i, (i // 2 + k) % lines * 2 + i % 2) for i in...  22.6 us
    ppermute x16, waiting for transfers between devices, over_pair(): lax.ppermute(x, 'expert', [(i, i + 1 - 2 * (i % 2)) for i in range(expert...  16.4 us
    ppermute x16, starting transfers between devices, over_pair(): lax.ppermute(x, 'expert', [(i, i + 1 - 2 * (i % 2)) for i in range(expert...  15.1 us
    dot_general x3, matrix products, dot(): lax.dot_general(a, b, (contract, ((), ())), preferred_element_type=F32)  9.84 us
    ppermute x5, starting transfers between devices, over_core(): return lax.ppermute(x, 'tensor', [(0, 1), (1, 0)])  9.66 us
    unnamed x65, local copies, waits for them, and re-layouts  4.49 us
  transfers between devices with their start and end apart: 33, of which 16 were waited for; matrix products, arithmetic and copies ran while one was open for 8% of the time, Pallas kernels for 20%

profile of v13, /device:TPU:9, one launch (start us, length us, event | category | flops | bytes accessed | tf_op | source)
XLA Modules:
  0.0 156.1 jit_solution(9178551052864819501)
XLA Ops:
  1.4 1.0 pad_maximum_fusion.3.block.refs_0_
  2.4 1.5 collective-permute-start
  3.9 4.1 %collective-permute-start.1 = (bf16[144,1024]{1,0:T(8,128)(2,1)S(1)}, bf16[144,1024]{1,0:T(8,128)(2,1)S(1)}, u32[]{:S(2)}, u32[]{:S(2)}) collective-permute-start(bf16[144,1024]{1,0:T(8,128)(2,1)S(1)} %pad_maximum_fusion.3.block.refs_0_), channel_id=1, source_target_pairs={{0,8},{2,10},{4,12},{6,14},{8,0},{10,2},{12,4},{14,6},{1,9},{3,11}... | collective-permute-start | bytes 884744 | tf_op jit(solution)/shard_map/ppermute | solution.py:242
  8.1 0.9 shard_map.118
  9.0 1.3 collective-permute-start.3
  10.3 0.9 shard_map.120
  11.2 1.3 collective-permute-start.5
  12.5 6.2 %collective-permute-done.block.refs_1_ = bf16[144,1024]{1,0:T(8,128)(2,1)S(1)} collective-permute-done((bf16[144,1024]{1,0:T(8,128)(2,1)S(1)}, bf16[144,1024]{1,0:T(8,128)(2,1)S(1)}, u32[]{:S(2)}, u32[]{:S(2)}) %collective-permute-start) | collective-permute-done | bytes 294944 | tf_op jit(solution)/shard_map/ppermute | solution.py:242
  18.7 0.9 shard_map.119
  19.6 1.3 collective-permute-start.4
  20.9 1.2 shard_map.121
  22.4 4.3 %collective-permute-done.6.refs_4_ = bf16[96,1024]{1,0:T(8,128)(2,1)S(1)} collective-permute-done((bf16[96,1024]{1,0:T(8,128)(2,1)S(1)}, bf16[96,1024]{1,0:T(8,128)(2,1)S(1)}, u32[]{:S(2)}, u32[]{:S(2)}) %collective-permute-start.6) | collective-permute-done | bytes 196640 | tf_op jit(solution)/shard_map/ppermute | solution.py:239
  26.7 1.5 collective-permute-done.1.block.refs_2_
  28.5 2.0 %collective-permute-start.10 = (bf16[128,1024]{1,0:T(8,128)(2,1)}, bf16[128,1024]{1,0:T(8,128)(2,1)S(1)}, u32[]{:S(2)}, u32[]{:S(2)}) collective-permute-start(bf16[128,1024]{1,0:T(8,128)(2,1)} %refs_0_), channel_id=1, source_target_pairs={{0,12},{2,14},{4,0},{6,2},{8,4},{10,6},{12,8},{14,10},{1,13},{3,15... | collective-permute-start | bytes 786440 | tf_op jit(solution)/shard_map/ppermute | solution.py:242
  30.5 2.3 %collective-permute-start.9 = (bf16[128,1024]{1,0:T(8,128)(2,1)}, bf16[128,1024]{1,0:T(8,128)(2,1)S(1)}, u32[]{:S(2)}, u32[]{:S(2)}) collective-permute-start(bf16[128,1024]{1,0:T(8,128)(2,1)} %refs_0_), channel_id=1, source_target_pairs={{0,8},{2,10},{4,12},{6,14},{8,0},{10,2},{12,4},{14,6},{1,9},{3,11}... | collective-permute-start | bytes 786440 | tf_op jit(solution)/shard_map/ppermute | solution.py:242
  32.8 0.9 shard_map.122
  33.7 1.3 collective-permute-start.7
  35.8 1.0 collective-permute-start.11
  36.8 4.5 %collective-permute-done.10.block.refs_3_ = bf16[128,1024]{1,0:T(8,128)(2,1)S(1)} collective-permute-done((bf16[128,1024]{1,0:T(8,128)(2,1)}, bf16[128,1024]{1,0:T(8,128)(2,1)S(1)}, u32[]{:S(2)}, u32[]{:S(2)}) %collective-permute-start.10) | collective-permute-done | bytes 262176 | tf_op jit(solution)/shard_map/ppermute | solution.py:242
  42.1 7.6 %collective-permute-done.9.block.refs_2_ = bf16[128,1024]{1,0:T(8,128)(2,1)S(1)} collective-permute-done((bf16[128,1024]{1,0:T(8,128)(2,1)}, bf16[128,1024]{1,0:T(8,128)(2,1)S(1)}, u32[]{:S(2)}, u32[]{:S(2)}) %collective-permute-start.9) | collective-permute-done | bytes 262176 | tf_op jit(solution)/shard_map/ppermute | solution.py:242
  51.3 7.0 %collective-permute-start.12 = (bf16[896,1024]{1,0:T(8,128)(2,1)S(1)}, bf16[896,1024]{1,0:T(8,128)(2,1)S(1)}, u32[]{:S(2)}, u32[]{:S(2)}) collective-permute-start(bf16[896,1024]{1,0:T(8,128)(2,1)S(1)} %get-tuple-element.172.own), channel_id=1, source_target_pairs={{0,1},{1,0},{2,3},{3,2},{4,5},{5,4},{6,7},{7,6},{8,9},{9,8},{10,11... | collective-permute-start | bytes 5505032 | tf_op jit(solution)/shard_map/ppermute | solution.py:248
  58.2 1.3 collective-permute-start.14
  59.7 1.9 %collective-permute-done.12.other = bf16[896,1024]{1,0:T(8,128)(2,1)S(1)} collective-permute-done((bf16[896,1024]{1,0:T(8,128)(2,1)S(1)}, bf16[896,1024]{1,0:T(8,128)(2,1)S(1)}, u32[]{:S(2)}, u32[]{:S(2)}) %collective-permute-start.12) | collective-permute-done | bytes 1835040 | tf_op jit(solution)/shard_map/ppermute | solution.py:248
  61.7 5.7 %shard_map.127 = (f32[896,384]{1,0:T(8,128)S(1)}, f32[896,384]{1,0:T(8,128)S(1)}, bf16[896,384]{1,0:T(8,128)(2,1)S(1)}, bf16[896,1024]{1,0:T(8,128)(2,1)S(1)}) custom-call(s32[3]{0:T(128)S(1)} %pad_add_fusion.info, bf16[896,1024]{1,0:T(8,128)(2,1)S(1)} %get-tuple-element.172.own, bf16[896,1024]{1,0:T(8,128)(2,1)S(1)} %collective-permute-done.12.other, ...), custom_call_target="tpu_custom_call" | custom-call | flops 1000 | bytes 1000 | tf_op jit(solution)/shard_map/pallas_call | solution.py:41
  67.4 1.6 %collective-permute-done.13.refs_6_ = bf16[96,1024]{1,0:T(8,128)(2,1)S(1)} collective-permute-done((bf16[96,1024]{1,0:T(8,128)(2,1)S(1)}, bf16[96,1024]{1,0:T(8,128)(2,1)S(1)}, u32[]{:S(2)}, u32[]{:S(2)}) %collective-permute-start.13) | collective-permute-done | bytes 196640 | tf_op jit(solution)/shard_map/ppermute | solution.py:239
  68.9 0.8 collective-permute-start.16
  69.8 1.1 shard_map.128.own
  71.0 2.2 %collective-permute-done.16.came = bf16[896,1024]{1,0:T(8,128)(2,1)S(1)} collective-permute-done((bf16[896,1024]{1,0:T(8,128)(2,1)S(1)}, bf16[896,1024]{1,0:T(8,128)(2,1)S(1)}, u32[]{:S(2)}, u32[]{:S(2)}) %collective-permute-start.16) | collective-permute-done | bytes 1835040 | tf_op jit(solution)/shard_map/ppermute | solution.py:248
  73.2 1.7 %shard_map.129 = (f32[4,128,1024]{2,1,0:T(8,128)S(1)}, bf16[96,1024]{1,0:T(8,128)(2,1)S(1)}, bf16[96,1024]{1,0:T(8,128)(2,1)S(1)}, bf16[96,1024]{1,0:T(8,128)(2,1)S(1)}, bf16[96,1024]{1,0:T(8,128)(2,1)S(1)}) custom-call(s32[3]{0:T(128)S(1)} %pad_add_fusion.info, bf16[896,1024]{1,0:T(8,128)(2,1)S(1)} %collective-permute-done.16.came, ...), custom_call_target="tpu_custom_call" | custom-call | flops 1000 | bytes 1000 | tf_op jit(solution)/shard_map/pallas_call | solution.py:41
  74.9 1.3 collective-permute-start.17
  76.4 5.4 %shard_map.130 = (bf16[896,384]{1,0:T(8,128)(2,1)S(1)}, bf16[896,384]{1,0:T(8,128)(2,1)S(1)}, bf16[896,1024]{1,0:T(8,128)(2,1)S(1)}, f32[4,16,128]{2,1,0:T(8,128)S(1)}, f32[4,16,128]{2,1,0:T(8,128)S(1)}) custom-call(s32[3]{0:T(128)S(1)} %pad_add_fusion.info, bf16[896,1024]{1,0:T(8,128)(2,1)S(1)} %shard_map.128.own, ...), custom_call_target="tpu_custom_call" | custom-call | flops 1000 | bytes 1000 | tf_op jit(solution)/shard_map/pallas_call | solution.py:41
  81.8 3.5 %collective-permute-done.18.back = bf16[96,1024]{1,0:T(8,128)(2,1)S(1)} collective-permute-done((bf16[96,1024]{1,0:T(8,128)(2,1)S(1)}, bf16[96,1024]{1,0:T(8,128)(2,1)S(1)}, u32[]{:S(2)}, u32[]{:S(2)}) %collective-permute-start.18) | collective-permute-done | bytes 196640 | tf_op jit(solution)/shard_map/ppermute | solution.py:239
  85.3 1.2 collective-permute-start.19
  86.5 0.8 shard_map.132
  87.3 2.1 %collective-permute-start.21 = (bf16[128,1024]{1,0:T(8,128)(2,1)S(1)}, bf16[128,1024]{1,0:T(8,128)(2,1)S(1)}, u32[]{:S(2)}, u32[]{:S(2)}) collective-permute-start(bf16[128,1024]{1,0:T(8,128)(2,1)S(1)} %shard_map.132), channel_id=1, source_target_pairs={{0,4},{2,6},{4,8},{6,10},{8,12},{10,14},{12,0},{14,2},{1,5},{3,7},... | collective-permute-start | bytes 786440 | tf_op jit(solution)/shard_map/ppermute | solution.py:242
  89.4 0.8 shard_map.134
  90.8 1.2 collective-permute-start.20
  92.0 3.4 %shard_map.131 = (f32[4,128,1024]{2,1,0:T(8,128)S(1)}, bf16[112,1024]{1,0:T(8,128)(2,1)S(1)}, bf16[112,1024]{1,0:T(8,128)(2,1)S(1)}, bf16[112,1024]{1,0:T(8,128)(2,1)}, bf16[112,1024]{1,0:T(8,128)(2,1)}) custom-call(s32[3]{0:T(128)S(1)} %pad_add_fusion.info, bf16[896,1024]{1,0:T(8,128)(2,1)S(1)} %collective-permute-done.19.came, ...), custom_call_target="tpu_custom_call" | custom-call | flops 1000 | bytes 1000 | tf_op jit(solution)/shard_map/pallas_call | solution.py:41
  95.4 1.3 copy-done
  96.8 3.9 %collective-permute-done.21 = bf16[128,1024]{1,0:T(8,128)(2,1)S(1)} collective-permute-done((bf16[128,1024]{1,0:T(8,128)(2,1)S(1)}, bf16[128,1024]{1,0:T(8,128)(2,1)S(1)}, u32[]{:S(2)}, u32[]{:S(2)}) %collective-permute-start.21) | collective-permute-done | bytes 262176 | tf_op jit(solution)/shard_map/ppermute | solution.py:242
  101.3 1.5 shard_map.135
  102.8 3.6 %collective-permute-done.23 = bf16[128,1024]{1,0:T(8,128)(2,1)S(1)} collective-permute-done((bf16[128,1024]{1,0:T(8,128)(2,1)S(1)}, bf16[128,1024]{1,0:T(8,128)(2,1)S(1)}, u32[]{:S(2)}, u32[]{:S(2)}) %collective-permute-start.23) | collective-permute-done | bytes 262176 | tf_op jit(solution)/shard_map/ppermute | solution.py:242
  106.4 1.3 collective-permute-start.24
  107.7 2.7 %collective-permute-start.25 = (bf16[128,1024]{1,0:T(8,128)(2,1)}, bf16[128,1024]{1,0:T(8,128)(2,1)}, u32[]{:S(2)}, u32[]{:S(2)}) collective-permute-start(bf16[128,1024]{1,0:T(8,128)(2,1)} %shard_map.135), channel_id=1, source_target_pairs={{0,12},{2,14},{4,0},{6,2},{8,4},{10,6},{12,8},{14,10},{1,13},{3,15... | collective-permute-start | bytes 786440 | tf_op jit(solution)/shard_map/ppermute | solution.py:242
  110.6 2.4 %collective-permute-done.24.back = bf16[112,1024]{1,0:T(8,128)(2,1)} collective-permute-done((bf16[112,1024]{1,0:T(8,128)(2,1)}, bf16[112,1024]{1,0:T(8,128)(2,1)}, u32[]{:S(2)}, u32[]{:S(2)}) %collective-permute-start.24) | collective-permute-done | bytes 229408 | tf_op jit(solution)/shard_map/ppermute | solution.py:239
  113.1 1.3 collective-permute-start.27
  114.4 4.0 %collective-permute-done.22.back = bf16[112,1024]{1,0:T(8,128)(2,1)} collective-permute-done((bf16[112,1024]{1,0:T(8,128)(2,1)}, bf16[112,1024]{1,0:T(8,128)(2,1)}, u32[]{:S(2)}, u32[]{:S(2)}) %collective-permute-start.22) | collective-permute-done | bytes 229408 | tf_op jit(solution)/shard_map/ppermute | solution.py:239
  118.4 1.6 %copy-done.1 = f32[4,128,1024]{2,1,0:T(8,128)S(1)} copy-done((f32[4,128,1024]{2,1,0:T(8,128)S(1)}, f32[4,128,1024]{2,1,0:T(8,128)}, u32[]{:S(2)}) %copy-start.1) | copy-done | bytes 2097176
  120.7 1.2 shard_map.133
  122.0 0.9 collective-permute-start.26
  122.9 1.2 shard_map.136
  124.9 2.7 %collective-permute-start.30 = (bf16[144,1024]{1,0:T(8,128)(2,1)S(1)}, bf16[144,1024]{1,0:T(8,128)(2,1)S(1)}, u32[]{:S(2)}, u32[]{:S(2)}) collective-permute-start(bf16[144,1024]{1,0:T(8,128)(2,1)S(1)} %shard_map.133), channel_id=1, source_target_pairs={{0,8},{2,10},{4,12},{6,14},{8,0},{10,2},{12,4},{14,6},{1,9},{3,11}... | collective-permute-start | bytes 884744 | tf_op jit(solution)/shard_map/ppermute | solution.py:242
  127.6 1.2 collective-permute-start.31
  128.8 0.8 shard_map.138
  129.6 1.8 %add_convert_fusion.1 = bf16[128,1024]{1,0:T(8,128)(2,1)} fusion(bf16[128,1024]{1,0:T(8,128)(2,1)S(1)} %copy-done.28, bf16[128,1024]{1,0:T(8,128)(2,1)S(1)} %copy-done.30, bf16[128,1024]{1,0:T(8,128)(2,1)} %collective-permute-done.25, bf16[128,1024]{1,0:T(8,128)(2,1)S(1)} %shard_map.138), kind=kLoop, calls=%fused_computation.16 | loop fusion | flops 1048576 | bytes 1310720 | tf_op jit(solution)/shard_map/convert_element_type | solution.py:347
  132.0 0.8 shard_map.139
  132.8 0.8 shard_map.137
  133.7 3.1 %collective-permute-start.29 = (bf16[144,1024]{1,0:T(8,128)(2,1)S(1)}, bf16[144,1024]{1,0:T(8,128)(2,1)S(1)}, u32[]{:S(2)}, u32[]{:S(2)}) collective-permute-start(bf16[144,1024]{1,0:T(8,128)(2,1)S(1)} %shard_map.137), channel_id=1, source_target_pairs={{0,12},{2,14},{4,0},{6,2},{8,4},{10,6},{12,8},{14,10},{1,13},{3,15... | collective-permute-start | bytes 884744 | tf_op jit(solution)/shard_map/ppermute | solution.py:242
  137.3 3.4 %fusion.7 = bf16[1,2048,384]{2,1,0:T(8,128)(2,1)} fusion(bf16[896,384]{1,0:T(8,128)(2,1)S(1)} %get-tuple-element.139.refs_0_, bf16[896,1024]{1,0:T(8,128)(2,1)S(1)} %get-tuple-element.187, bf16[896,1024]{1,0:T(8,128)(2,1)S(1)} %get-tuple-element.186), kind=kOutput, calls=%fused_computation.8 | convolution fusion | flops 1417412608 | bytes 5931008 | tf_op jit(solution)/shard_map/dot_general | solution.py:24
  140.7 3.4 %fusion.8 = bf16[1,2048,384]{2,1,0:T(8,128)(2,1)} fusion(bf16[896,384]{1,0:T(8,128)(2,1)S(1)} %get-tuple-element.174.refs_1_, bf16[896,1024]{1,0:T(8,128)(2,1)S(1)} %get-tuple-element.187, bf16[896,1024]{1,0:T(8,128)(2,1)S(1)} %get-tuple-element.186), kind=kOutput, calls=%fused_computation.9 | convolution fusion | flops 1417412608 | bytes 5931008 | tf_op jit(solution)/shard_map/dot_general | solution.py:24
  144.2 3.0 %fusion.9 = bf16[1,384,2048]{2,1,0:T(8,128)(2,1)} fusion(bf16[896,384]{1,0:T(8,128)(2,1)S(1)} %copy-done.15, bf16[896,1024]{1,0:T(8,128)(2,1)S(1)} %get-tuple-element.185, bf16[896,1024]{1,0:T(8,128)(2,1)S(1)} %get-tuple-element.184), kind=kOutput, calls=%fused_computation.10 | convolution fusion | flops 1417412608 | bytes 5931008 | tf_op jit(solution)/shard_map/dot_general | solution.py:24
  147.2 5.4 %collective-permute-done.31 = bf16[144,1024]{1,0:T(8,128)(2,1)S(1)} collective-permute-done((bf16[144,1024]{1,0:T(8,128)(2,1)S(1)}, bf16[144,1024]{1,0:T(8,128)(2,1)S(1)}, u32[]{:S(2)}, u32[]{:S(2)}) %collective-permute-start.31) | collective-permute-done | bytes 294944 | tf_op jit(solution)/shard_map/ppermute | solution.py:242
  152.6 1.4 collective-permute-done.29
  154.6 0.9 add_convert_fusion
  (118 shorter events, 10.5 us)
Async XLA Ops:
  2.4 7.9 %collective-permute-start.2 = (bf16[144,1024]{1,0:T(8,128)(2,1)S(1)}, bf16[144,1024]{1,0:T(8,128)(2,1)S(1)}, u32[]{:S(2)}, u32[]{:S(2)}) collective-permute-start(bf16[144,1024]{1,0:T(8,128)(2,1)S(1)} %pad_maximum_fusion.3.block.refs_0_), channel_id=1, source_target_pairs={{0,12},{2,14},{4,0},{6,2},{8,4},{10,6},{12,8},{14,10},{1,13},{3,15... | collective-permute-start | bytes 884744 | tf_op jit(solution)/shard_map/ppermute | solution.py:242
  2.4 16.3 %collective-permute-start = (bf16[144,1024]{1,0:T(8,128)(2,1)S(1)}, bf16[144,1024]{1,0:T(8,128)(2,1)S(1)}, u32[]{:S(2)}, u32[]{:S(2)}) collective-permute-start(bf16[144,1024]{1,0:T(8,128)(2,1)S(1)} %pad_maximum_fusion.3.block.refs_0_), channel_id=1, source_target_pairs={{0,4},{2,6},{4,8},{6,10},{8,12},{10,14},{12,0},{14,2},{1,5},{3,7},... | collective-permute-start | bytes 884744 | tf_op jit(solution)/shard_map/ppermute | solution.py:242
  3.9 24.3 %collective-permute-start.1 = (bf16[144,1024]{1,0:T(8,128)(2,1)S(1)}, bf16[144,1024]{1,0:T(8,128)(2,1)S(1)}, u32[]{:S(2)}, u32[]{:S(2)}) collective-permute-start(bf16[144,1024]{1,0:T(8,128)(2,1)S(1)} %pad_maximum_fusion.3.block.refs_0_), channel_id=1, source_target_pairs={{0,8},{2,10},{4,12},{6,14},{8,0},{10,2},{12,4},{14,6},{1,9},{3,11}... | collective-permute-start | bytes 884744 | tf_op jit(solution)/shard_map/ppermute | solution.py:242
  9.0 17.7 %collective-permute-start.3 = (bf16[112,1024]{1,0:T(8,128)(2,1)S(1)}, bf16[112,1024]{1,0:T(8,128)(2,1)S(1)}, u32[]{:S(2)}, u32[]{:S(2)}) collective-permute-start(bf16[112,1024]{1,0:T(8,128)(2,1)S(1)} %get-tuple-element.91), channel_id=1, source_target_pairs={{0,2},{2,0},{4,6},{6,4},{8,10},{10,8},{12,14},{14,12},{1,3},{3,1},... | collective-permute-start | bytes 688136 | tf_op jit(solution)/shard_map/ppermute | solution.py:239
  10.3 51.4 %copy-start.7 = (bf16[1,2048,384]{2,1,0:T(8,128)(2,1)S(1)}, bf16[1,2048,384]{2,1,0:T(8,128)(2,1)}, u32[]{:S(2)}) copy-start(bf16[1,2048,384]{2,1,0:T(8,128)(2,1)} %param.11) | copy-start | bytes 4718596
  11.2 75.3 %copy-start.18 = (bf16[96,128]{1,0:T(8,128)(2,1)}, bf16[96,128]{1,0:T(8,128)(2,1)S(1)}, u32[]{:S(2)}) copy-start(bf16[96,128]{1,0:T(8,128)(2,1)S(1)} %get-tuple-element.102.place) | copy-start | bytes 73732
  11.2 17.0 %collective-permute-start.5 = (bf16[112,1024]{1,0:T(8,128)(2,1)S(1)}, bf16[112,1024]{1,0:T(8,128)(2,1)S(1)}, u32[]{:S(2)}, u32[]{:S(2)}) collective-permute-start(bf16[112,1024]{1,0:T(8,128)(2,1)S(1)} %get-tuple-element.93), channel_id=1, source_target_pairs={{0,2},{2,0},{4,6},{6,4},{8,10},{10,8},{12,14},{14,12},{1,3},{3,1},... | collective-permute-start | bytes 688136 | tf_op jit(solution)/shard_map/ppermute | solution.py:239
  19.6 81.7 %copy-start.16 = (bf16[96,128]{1,0:T(8,128)(2,1)}, bf16[96,128]{1,0:T(8,128)(2,1)S(1)}, u32[]{:S(2)}) copy-start(bf16[96,128]{1,0:T(8,128)(2,1)S(1)} %get-tuple-element.100.place) | copy-start | bytes 73732
  19.6 8.6 %collective-permute-start.4 = (bf16[112,1024]{1,0:T(8,128)(2,1)S(1)}, bf16[112,1024]{1,0:T(8,128)(2,1)S(1)}, u32[]{:S(2)}, u32[]{:S(2)}) collective-permute-start(bf16[112,1024]{1,0:T(8,128)(2,1)S(1)} %get-tuple-element.92), channel_id=1, source_target_pairs={{0,2},{2,0},{4,6},{6,4},{8,10},{10,8},{12,14},{14,12},{1,3},{3,1},... | collective-permute-start | bytes 688136 | tf_op jit(solution)/shard_map/ppermute | solution.py:239
  22.1 4.6 %collective-permute-start.6 = (bf16[96,1024]{1,0:T(8,128)(2,1)S(1)}, bf16[96,1024]{1,0:T(8,128)(2,1)S(1)}, u32[]{:S(2)}, u32[]{:S(2)}) collective-permute-start(bf16[96,1024]{1,0:T(8,128)(2,1)S(1)} %shard_map.121), channel_id=1, source_target_pairs={{0,2},{2,0},{4,6},{6,4},{8,10},{10,8},{12,14},{14,12},{1,3},{3,1},... | collective-permute-start | bytes 589832 | tf_op jit(solution)/shard_map/ppermute | solution.py:239
  28.2 6.8 %collective-permute-start.8 = (bf16[128,1024]{1,0:T(8,128)(2,1)}, bf16[128,1024]{1,0:T(8,128)(2,1)S(1)}, u32[]{:S(2)}, u32[]{:S(2)}) collective-permute-start(bf16[128,1024]{1,0:T(8,128)(2,1)} %refs_0_), channel_id=1, source_target_pairs={{0,4},{2,6},{4,8},{6,10},{8,12},{10,14},{12,0},{14,2},{1,5},{3,7},... | collective-permute-start | bytes 786440 | tf_op jit(solution)/shard_map/ppermute | solution.py:242
  28.5 12.8 %collective-permute-start.10 = (bf16[128,1024]{1,0:T(8,128)(2,1)}, bf16[128,1024]{1,0:T(8,128)(2,1)S(1)}, u32[]{:S(2)}, u32[]{:S(2)}) collective-permute-start(bf16[128,1024]{1,0:T(8,128)(2,1)} %refs_0_), channel_id=1, source_target_pairs={{0,12},{2,14},{4,0},{6,2},{8,4},{10,6},{12,8},{14,10},{1,13},{3,15... | collective-permute-start | bytes 786440 | tf_op jit(solution)/shard_map/ppermute | solution.py:242
  30.5 19.2 %collective-permute-start.9 = (bf16[128,1024]{1,0:T(8,128)(2,1)}, bf16[128,1024]{1,0:T(8,128)(2,1)S(1)}, u32[]{:S(2)}, u32[]{:S(2)}) collective-permute-start(bf16[128,1024]{1,0:T(8,128)(2,1)} %refs_0_), channel_id=1, source_target_pairs={{0,8},{2,10},{4,12},{6,14},{8,0},{10,2},{12,4},{14,6},{1,9},{3,11}... | collective-permute-start | bytes 786440 | tf_op jit(solution)/shard_map/ppermute | solution.py:242
  33.7 55.8 %copy-start.20 = (bf16[96,128]{1,0:T(8,128)(2,1)}, bf16[96,128]{1,0:T(8,128)(2,1)S(1)}, u32[]{:S(2)}) copy-start(bf16[96,128]{1,0:T(8,128)(2,1)S(1)} %get-tuple-element.101.place) | copy-start | bytes 73732
  33.7 28.0 %copy-start.5 = (bf16[1,384,2048]{2,1,0:T(8,128)(2,1)S(1)}, bf16[1,384,2048]{2,1,0:T(8,128)(2,1)}, u32[]{:S(2)}) copy-start(bf16[1,384,2048]{2,1,0:T(8,128)(2,1)} %param.12) | copy-start | bytes 4718596
  33.7 28.0 %copy-start.6 = (bf16[1,2048,384]{2,1,0:T(8,128)(2,1)S(1)}, bf16[1,2048,384]{2,1,0:T(8,128)(2,1)}, u32[]{:S(2)}) copy-start(bf16[1,2048,384]{2,1,0:T(8,128)(2,1)} %param.10) | copy-start | bytes 4718596
  33.7 16.7 %collective-permute-start.7 = (bf16[112,1024]{1,0:T(8,128)(2,1)S(1)}, bf16[112,1024]{1,0:T(8,128)(2,1)S(1)}, u32[]{:S(2)}, u32[]{:S(2)}) collective-permute-start(bf16[112,1024]{1,0:T(8,128)(2,1)S(1)} %get-tuple-element.97), channel_id=1, source_target_pairs={{0,2},{2,0},{4,6},{6,4},{8,10},{10,8},{12,14},{14,12},{1,3},{3,1},... | collective-permute-start | bytes 688136 | tf_op jit(solution)/shard_map/ppermute | solution.py:239
  35.8 14.7 %collective-permute-start.11 = (bf16[96,1024]{1,0:T(8,128)(2,1)S(1)}, bf16[96,1024]{1,0:T(8,128)(2,1)S(1)}, u32[]{:S(2)}, u32[]{:S(2)}) collective-permute-start(bf16[96,1024]{1,0:T(8,128)(2,1)S(1)} %shard_map.123), channel_id=1, source_target_pairs={{0,2},{2,0},{4,6},{6,4},{8,10},{10,8},{12,14},{14,12},{1,3},{3,1},... | collective-permute-start | bytes 589832 | tf_op jit(solution)/shard_map/ppermute | solution.py:239
  51.2 16.1 %copy-start.8 = (bf16[896,1024]{1,0:T(8,128)(2,1)}, bf16[896,1024]{1,0:T(8,128)(2,1)S(1)}, u32[]{:S(2)}) copy-start(bf16[896,1024]{1,0:T(8,128)(2,1)S(1)} %get-tuple-element.172.own) | copy-start | bytes 5505028
  51.3 10.4 %collective-permute-start.12 = (bf16[896,1024]{1,0:T(8,128)(2,1)S(1)}, bf16[896,1024]{1,0:T(8,128)(2,1)S(1)}, u32[]{:S(2)}, u32[]{:S(2)}) collective-permute-start(bf16[896,1024]{1,0:T(8,128)(2,1)S(1)} %get-tuple-element.172.own), channel_id=1, source_target_pairs={{0,1},{1,0},{2,3},{3,2},{4,5},{5,4},{6,7},{7,6},{8,9},{9,8},{10,11... | collective-permute-start | bytes 5505032 | tf_op jit(solution)/shard_map/ppermute | solution.py:248
  58.2 9.1 %collective-permute-start.14 = (bf16[96,1024]{1,0:T(8,128)(2,1)S(1)}, bf16[96,1024]{1,0:T(8,128)(2,1)S(1)}, u32[]{:S(2)}, u32[]{:S(2)}) collective-permute-start(bf16[96,1024]{1,0:T(8,128)(2,1)S(1)} %shard_map.125), channel_id=1, source_target_pairs={{0,2},{2,0},{4,6},{6,4},{8,10},{10,8},{12,14},{14,12},{1,3},{3,1},... | collective-permute-start | bytes 589832 | tf_op jit(solution)/shard_map/ppermute | solution.py:239
  59.5 9.4 %collective-permute-start.13 = (bf16[96,1024]{1,0:T(8,128)(2,1)S(1)}, bf16[96,1024]{1,0:T(8,128)(2,1)S(1)}, u32[]{:S(2)}, u32[]{:S(2)}) collective-permute-start(bf16[96,1024]{1,0:T(8,128)(2,1)S(1)} %shard_map.124), channel_id=1, source_target_pairs={{0,2},{2,0},{4,6},{6,4},{8,10},{10,8},{12,14},{14,12},{1,3},{3,1},... | collective-permute-start | bytes 589832 | tf_op jit(solution)/shard_map/ppermute | solution.py:239
  61.7 5.7 %copy-start.10 = (bf16[896,1024]{1,0:T(8,128)(2,1)}, bf16[896,1024]{1,0:T(8,128)(2,1)S(1)}, u32[]{:S(2)}) copy-start(bf16[896,1024]{1,0:T(8,128)(2,1)S(1)} %collective-permute-done.12.other) | copy-start | bytes 5505028
  67.3 5.9 %copy-start.14 = (bf16[896,384]{1,0:T(8,128)(2,1)}, bf16[896,384]{1,0:T(8,128)(2,1)S(1)}, u32[]{:S(2)}) copy-start(bf16[896,384]{1,0:T(8,128)(2,1)S(1)} %get-tuple-element.129.refs_0_) | copy-start | bytes 2064388
  68.9 4.3 %collective-permute-start.16 = (bf16[896,1024]{1,0:T(8,128)(2,1)S(1)}, bf16[896,1024]{1,0:T(8,128)(2,1)S(1)}, u32[]{:S(2)}, u32[]{:S(2)}) collective-permute-start(bf16[896,1024]{1,0:T(8,128)(2,1)S(1)} %get-tuple-element.128), channel_id=1, source_target_pairs={{0,1},{1,0},{2,3},{3,2},{4,5},{5,4},{6,7},{7,6},{8,9},{9,8},{10,11... | collective-permute-start | bytes 5505032 | tf_op jit(solution)/shard_map/ppermute | solution.py:248
  70.9 5.6 %copy-start.3 = (bf16[896,1024]{1,0:T(8,128)(2,1)}, bf16[896,1024]{1,0:T(8,128)(2,1)S(1)}, u32[]{:S(2)}) copy-start(bf16[896,1024]{1,0:T(8,128)(2,1)S(1)} %shard_map.128.own) | copy-start | bytes 5505028
  70.9 5.5 %collective-permute-start.15 = (bf16[896,1024]{1,0:T(8,128)(2,1)S(1)}, bf16[896,1024]{1,0:T(8,128)(2,1)S(1)}, u32[]{:S(2)}, u32[]{:S(2)}) collective-permute-start(bf16[896,1024]{1,0:T(8,128)(2,1)S(1)} %shard_map.128.own), channel_id=1, source_target_pairs={{0,1},{1,0},{2,3},{3,2},{4,5},{5,4},{6,7},{7,6},{8,9},{9,8},{10,11... | collective-permute-start | bytes 5505032 | tf_op jit(solution)/shard_map/ppermute | solution.py:248
  74.9 6.9 %copy-start.26 = (bf16[96,1024]{1,0:T(8,128)(2,1)}, bf16[96,1024]{1,0:T(8,128)(2,1)S(1)}, u32[]{:S(2)}) copy-start(bf16[96,1024]{1,0:T(8,128)(2,1)S(1)} %get-tuple-element.165) | copy-start | bytes 589828
  74.9 6.9 %collective-permute-start.17 = (bf16[96,1024]{1,0:T(8,128)(2,1)S(1)}, bf16[96,1024]{1,0:T(8,128)(2,1)S(1)}, u32[]{:S(2)}, u32[]{:S(2)}) collective-permute-start(bf16[96,1024]{1,0:T(8,128)(2,1)S(1)} %get-tuple-element.132), channel_id=1, source_target_pairs={{0,2},{2,0},{4,6},{6,4},{8,10},{10,8},{12,14},{14,12},{1,3},{3,1},... | collective-permute-start | bytes 589832 | tf_op jit(solution)/shard_map/ppermute | solution.py:239
  76.2 9.1 %collective-permute-start.18 = (bf16[96,1024]{1,0:T(8,128)(2,1)S(1)}, bf16[96,1024]{1,0:T(8,128)(2,1)S(1)}, u32[]{:S(2)}, u32[]{:S(2)}) collective-permute-start(bf16[96,1024]{1,0:T(8,128)(2,1)S(1)} %get-tuple-element.133), channel_id=1, source_target_pairs={{0,2},{2,0},{4,6},{6,4},{8,10},{10,8},{12,14},{14,12},{1,3},{3,1},... | collective-permute-start | bytes 589832 | tf_op jit(solution)/shard_map/ppermute | solution.py:239
  76.4 5.4 %copy-start.12 = (bf16[896,1024]{1,0:T(8,128)(2,1)}, bf16[896,1024]{1,0:T(8,128)(2,1)S(1)}, u32[]{:S(2)}) copy-start(bf16[896,1024]{1,0:T(8,128)(2,1)S(1)} %collective-permute-done.15.other) | copy-start | bytes 5505028
  85.3 6.8 %collective-permute-start.19 = (bf16[896,1024]{1,0:T(8,128)(2,1)S(1)}, bf16[896,1024]{1,0:T(8,128)(2,1)S(1)}, u32[]{:S(2)}, u32[]{:S(2)}) collective-permute-start(bf16[896,1024]{1,0:T(8,128)(2,1)S(1)} %get-tuple-element.138), channel_id=1, source_target_pairs={{0,1},{1,0},{2,3},{3,2},{4,5},{5,4},{6,7},{7,6},{8,9},{9,8},{10,11... | collective-permute-start | bytes 5505032 | tf_op jit(solution)/shard_map/ppermute | solution.py:248
  87.3 13.3 %collective-permute-start.21 = (bf16[128,1024]{1,0:T(8,128)(2,1)S(1)}, bf16[128,1024]{1,0:T(8,128)(2,1)S(1)}, u32[]{:S(2)}, u32[]{:S(2)}) collective-permute-start(bf16[128,1024]{1,0:T(8,128)(2,1)S(1)} %shard_map.132), channel_id=1, source_target_pairs={{0,4},{2,6},{4,8},{6,10},{8,12},{10,14},{12,0},{14,2},{1,5},{3,7},... | collective-permute-start | bytes 786440 | tf_op jit(solution)/shard_map/ppermute | solution.py:242
  90.2 16.2 %collective-permute-start.23 = (bf16[128,1024]{1,0:T(8,128)(2,1)S(1)}, bf16[128,1024]{1,0:T(8,128)(2,1)S(1)}, u32[]{:S(2)}, u32[]{:S(2)}) collective-permute-start(bf16[128,1024]{1,0:T(8,128)(2,1)S(1)} %shard_map.134), channel_id=1, source_target_pairs={{0,8},{2,10},{4,12},{6,14},{8,0},{10,2},{12,4},{14,6},{1,9},{3,11}... | collective-permute-start | bytes 786440 | tf_op jit(solution)/shard_map/ppermute | solution.py:242
  90.8 5.9 %collective-permute-start.20 = (bf16[96,1024]{1,0:T(8,128)(2,1)S(1)}, bf16[96,1024]{1,0:T(8,128)(2,1)S(1)}, u32[]{:S(2)}, u32[]{:S(2)}) collective-permute-start(bf16[96,1024]{1,0:T(8,128)(2,1)S(1)} %get-tuple-element.147), channel_id=1, source_target_pairs={{0,2},{2,0},{4,6},{6,4},{8,10},{10,8},{12,14},{14,12},{1,3},{3,1},... | collective-permute-start | bytes 589832 | tf_op jit(solution)/shard_map/ppermute | solution.py:239
  95.4 1.3 copy-start
  96.7 9.7 %copy-start.22 = (bf16[112,1024]{1,0:T(8,128)(2,1)}, bf16[112,1024]{1,0:T(8,128)(2,1)S(1)}, u32[]{:S(2)}) copy-start(bf16[112,1024]{1,0:T(8,128)(2,1)S(1)} %get-tuple-element.163) | copy-start | bytes 688132
  96.7 10.9 %copy-start.24 = (bf16[112,1024]{1,0:T(8,128)(2,1)}, bf16[112,1024]{1,0:T(8,128)(2,1)S(1)}, u32[]{:S(2)}) copy-start(bf16[112,1024]{1,0:T(8,128)(2,1)S(1)} %get-tuple-element.171) | copy-start | bytes 688132
  96.7 17.6 %copy-start.31 = (s32[128,4]{0,1:T(4,128)S(1)}, s32[128,4]{0,1:T(4,128)}, u32[]{:S(2)}) copy-start(s32[128,4]{0,1:T(4,128)} %param.8) | copy-start | bytes 6148
  106.4 4.0 %copy-start.29 = (bf16[128,1024]{1,0:T(8,128)(2,1)}, bf16[128,1024]{1,0:T(8,128)(2,1)S(1)}, u32[]{:S(2)}) copy-start(bf16[128,1024]{1,0:T(8,128)(2,1)S(1)} %collective-permute-done.23) | copy-start | bytes 786436
  106.4 6.7 %collective-permute-start.24 = (bf16[112,1024]{1,0:T(8,128)(2,1)}, bf16[112,1024]{1,0:T(8,128)(2,1)}, u32[]{:S(2)}, u32[]{:S(2)}) collective-permute-start(bf16[112,1024]{1,0:T(8,128)(2,1)} %get-tuple-element.157), channel_id=1, source_target_pairs={{0,2},{2,0},{4,6},{6,4},{8,10},{10,8},{12,14},{14,12},{1,3},{3,1},... | collective-permute-start | bytes 688136 | tf_op jit(solution)/shard_map/ppermute | solution.py:239
  107.7 17.2 %collective-permute-start.25 = (bf16[128,1024]{1,0:T(8,128)(2,1)}, bf16[128,1024]{1,0:T(8,128)(2,1)}, u32[]{:S(2)}, u32[]{:S(2)}) collective-permute-start(bf16[128,1024]{1,0:T(8,128)(2,1)} %shard_map.135), channel_id=1, source_target_pairs={{0,12},{2,14},{4,0},{6,2},{8,4},{10,6},{12,8},{14,10},{1,13},{3,15... | collective-permute-start | bytes 786440 | tf_op jit(solution)/shard_map/ppermute | solution.py:242
  110.4 8.0 %collective-permute-start.22 = (bf16[112,1024]{1,0:T(8,128)(2,1)}, bf16[112,1024]{1,0:T(8,128)(2,1)}, u32[]{:S(2)}, u32[]{:S(2)}) collective-permute-start(bf16[112,1024]{1,0:T(8,128)(2,1)} %get-tuple-element.150), channel_id=1, source_target_pairs={{0,2},{2,0},{4,6},{6,4},{8,10},{10,8},{12,14},{14,12},{1,3},{3,1},... | collective-permute-start | bytes 688136 | tf_op jit(solution)/shard_map/ppermute | solution.py:239
  113.1 15.7 %collective-permute-start.27 = (bf16[96,1024]{1,0:T(8,128)(2,1)}, bf16[96,1024]{1,0:T(8,128)(2,1)S(1)}, u32[]{:S(2)}, u32[]{:S(2)}) collective-permute-start(bf16[96,1024]{1,0:T(8,128)(2,1)} %copy-done.26), channel_id=1, source_target_pairs={{0,2},{2,0},{4,6},{6,4},{8,10},{10,8},{12,14},{14,12},{1,3},{3,1},... | collective-permute-start | bytes 589832 | tf_op jit(solution)/shard_map/ppermute | solution.py:239
  118.4 1.6 %copy-start.1 = (f32[4,128,1024]{2,1,0:T(8,128)S(1)}, f32[4,128,1024]{2,1,0:T(8,128)}, u32[]{:S(2)}) copy-start(f32[4,128,1024]{2,1,0:T(8,128)} %copy-done) | copy-start | bytes 6291460
  120.0 0.7 copy-start.21
  120.7 1.2 copy-start.23
  120.7 2.2 %copy-start.19 = (bf16[96,128]{1,0:T(8,128)(2,1)S(1)}, bf16[96,128]{1,0:T(8,128)(2,1)}, u32[]{:S(2)}) copy-start(bf16[96,128]{1,0:T(8,128)(2,1)} %copy-done.18) | copy-start | bytes 73732
  122.0 2.2 %copy-start.25 = (bf16[112,1024]{1,0:T(8,128)(2,1)S(1)}, bf16[112,1024]{1,0:T(8,128)(2,1)}, u32[]{:S(2)}) copy-start(bf16[112,1024]{1,0:T(8,128)(2,1)} %copy-done.24) | copy-start | bytes 688132
  122.0 10.8 %collective-permute-start.26 = (bf16[112,1024]{1,0:T(8,128)(2,1)S(1)}, bf16[112,1024]{1,0:T(8,128)(2,1)S(1)}, u32[]{:S(2)}, u32[]{:S(2)}) collective-permute-start(bf16[112,1024]{1,0:T(8,128)(2,1)S(1)} %copy-done.23), channel_id=1, source_target_pairs={{0,2},{2,0},{4,6},{6,4},{8,10},{10,8},{12,14},{14,12},{1,3},{3,1},... | collective-permute-start | bytes 688136 | tf_op jit(solution)/shard_map/ppermute | solution.py:239
  122.9 6.6 %copy-start.30 = (bf16[128,1024]{1,0:T(8,128)(2,1)S(1)}, bf16[128,1024]{1,0:T(8,128)(2,1)}, u32[]{:S(2)}) copy-start(bf16[128,1024]{1,0:T(8,128)(2,1)} %copy-done.29) | copy-start | bytes 786436
  124.2 5.4 %copy-start.28 = (bf16[128,1024]{1,0:T(8,128)(2,1)S(1)}, bf16[128,1024]{1,0:T(8,128)(2,1)}, u32[]{:S(2)}) copy-start(bf16[128,1024]{1,0:T(8,128)(2,1)} %copy-done.27) | copy-start | bytes 786436
  124.2 7.8 %copy-start.2 = (f32[4,128,1024]{2,1,0:T(8,128)S(1)}, f32[4,128,1024]{2,1,0:T(8,128)}, u32[]{:S(2)}) copy-start(f32[4,128,1024]{2,1,0:T(8,128)} %copy-done) | copy-start | bytes 6291460
  124.2 7.8 %collective-permute-start.28 = (bf16[112,1024]{1,0:T(8,128)(2,1)S(1)}, bf16[112,1024]{1,0:T(8,128)(2,1)S(1)}, u32[]{:S(2)}, u32[]{:S(2)}) collective-permute-start(bf16[112,1024]{1,0:T(8,128)(2,1)S(1)} %copy-done.25), channel_id=1, source_target_pairs={{0,2},{2,0},{4,6},{6,4},{8,10},{10,8},{12,14},{14,12},{1,3},{3,1},... | collective-permute-start | bytes 688136 | tf_op jit(solution)/shard_map/ppermute | solution.py:239
  124.9 22.3 %collective-permute-start.30 = (bf16[144,1024]{1,0:T(8,128)(2,1)S(1)}, bf16[144,1024]{1,0:T(8,128)(2,1)S(1)}, u32[]{:S(2)}, u32[]{:S(2)}) collective-permute-start(bf16[144,1024]{1,0:T(8,128)(2,1)S(1)} %shard_map.133), channel_id=1, source_target_pairs={{0,8},{2,10},{4,12},{6,14},{8,0},{10,2},{12,4},{14,6},{1,9},{3,11}... | collective-permute-start | bytes 884744 | tf_op jit(solution)/shard_map/ppermute | solution.py:242
  127.6 25.0 %collective-permute-start.31 = (bf16[144,1024]{1,0:T(8,128)(2,1)S(1)}, bf16[144,1024]{1,0:T(8,128)(2,1)S(1)}, u32[]{:S(2)}, u32[]{:S(2)}) collective-permute-start(bf16[144,1024]{1,0:T(8,128)(2,1)S(1)} %shard_map.136), channel_id=1, source_target_pairs={{0,4},{2,6},{4,8},{6,10},{8,12},{10,14},{12,0},{14,2},{1,5},{3,7},... | collective-permute-start | bytes 884744 | tf_op jit(solution)/shard_map/ppermute | solution.py:242
  129.6 3.3 %copy-start.17 = (bf16[96,128]{1,0:T(8,128)(2,1)S(1)}, bf16[96,128]{1,0:T(8,128)(2,1)}, u32[]{:S(2)}) copy-start(bf16[96,128]{1,0:T(8,128)(2,1)} %copy-done.16) | copy-start | bytes 73732
  132.0 4.8 %copy-start.13 = (bf16[896,1024]{1,0:T(8,128)(2,1)S(1)}, bf16[896,1024]{1,0:T(8,128)(2,1)}, u32[]{:S(2)}) copy-start(bf16[896,1024]{1,0:T(8,128)(2,1)} %copy-done.12) | copy-start | bytes 5505028
  132.8 4.0 %copy-start.4 = (bf16[896,1024]{1,0:T(8,128)(2,1)S(1)}, bf16[896,1024]{1,0:T(8,128)(2,1)}, u32[]{:S(2)}) copy-start(bf16[896,1024]{1,0:T(8,128)(2,1)} %copy-done.3) | copy-start | bytes 5505028
  133.6 3.4 %copy-start.9 = (bf16[896,1024]{1,0:T(8,128)(2,1)S(1)}, bf16[896,1024]{1,0:T(8,128)(2,1)}, u32[]{:S(2)}) copy-start(bf16[896,1024]{1,0:T(8,128)(2,1)} %copy-done.8) | copy-start | bytes 5505028
  133.7 3.4 %copy-start.11 = (bf16[896,1024]{1,0:T(8,128)(2,1)S(1)}, bf16[896,1024]{1,0:T(8,128)(2,1)}, u32[]{:S(2)}) copy-start(bf16[896,1024]{1,0:T(8,128)(2,1)} %copy-done.10) | copy-start | bytes 5505028
  133.7 20.4 %collective-permute-start.29 = (bf16[144,1024]{1,0:T(8,128)(2,1)S(1)}, bf16[144,1024]{1,0:T(8,128)(2,1)S(1)}, u32[]{:S(2)}, u32[]{:S(2)}) collective-permute-start(bf16[144,1024]{1,0:T(8,128)(2,1)S(1)} %shard_map.137), channel_id=1, source_target_pairs={{0,12},{2,14},{4,0},{6,2},{8,4},{10,6},{12,8},{14,10},{1,13},{3,15... | collective-permute-start | bytes 884744 | tf_op jit(solution)/shard_map/ppermute | solution.py:242
  140.7 3.4 %copy-start.15 = (bf16[896,384]{1,0:T(8,128)(2,1)S(1)}, bf16[896,384]{1,0:T(8,128)(2,1)}, u32[]{:S(2)}) copy-start(bf16[896,384]{1,0:T(8,128)(2,1)} %copy-done.14) | copy-start | bytes 2064388
  154.1 1.4 collective-permute-start.32
  (1 other events, 0.7 us)

commit v14 on v8

--- a/solution.py
+++ b/solution.py
@@ -352,25 +352,26 @@
     last, first_home = settle((out_packed[far], out_home[near[0]]))
     out_back[far] = over_pair(last)
     out_home[near[0]] = first_home
-    last, out_back[far] = settle((out_packed[0], out_back[far]))
-    out_back[0] = over_pair(last)
-    for k in (far, 0):
-        out_home[k] = to_home(k, out_dense, out_back)
-
     def whole(own, other):
         return jnp.concatenate(
             [jnp.where(core == 0, own, other), jnp.where(core == 0, other, own)], axis=1)
 
     came = over_core(sent)
-    out_came = {k: over_line(out_home[k], lines - k) for k in by_reach}
-    out_came[0] = out_home[0]
+    out_came = {k: over_line(out_home[k], lines - k) for k in near}
     in_dense, *in_packed = local_call(
         functools.partial(join_kernel, *sizes, False),
         (shape_of((lines, token_count, half_width), F32),
          *[shape_of((padded + TAIL, half_width)) for _ in every]),
         (info, came, grad_gate, grad_up, gate_local, up_local, compact_tails))
-    in_packed, ahead = settle((in_packed, {k: out_came[k] for k in near}))
+    in_packed, out_back[far], ahead = settle((in_packed, out_back[far], out_came))
     out_came.update(ahead)
+    last, out_back[far] = settle((out_packed[0], out_back[far]))
+    out_back[0] = over_pair(last)
+    for k in (far, 0):
+        out_home[k] = to_home(k, out_dense, out_back)
+
+    out_came[far] = over_line(out_home[far], lines - far)
+    out_came[0] = out_home[0]
     in_back, in_home, sequence = {}, {}, outward + [0]
     for i, k in enumerate(sequence):
         packed = in_packed[k]

time: 151 us -> 157 us (1.040)
  waiting for transfers between devices: 48.4 us -> 58.4 us
  starting transfers between devices: 48.2 us -> 42.3 us
  local copies, waits for them, and re-layouts: 2.35 us -> 4.35 us
    ppermute x12, waiting for transfers between devices: 34.2 us -> 41.2 us  [over_line(): lax.ppermute(x, 'expert', [(i, (i // 2 + k) % lines * 2 + i % 2) for i in...]
    ppermute x12, starting transfers between devices: 23.3 us -> 17.1 us  [over_line(): lax.ppermute(x, 'expert', [(i, (i // 2 + k) % lines * 2 + i % 2) for i in...]
    ppermute x16, waiting for transfers between devices: 10.3 us -> 15.2 us  [over_pair(): lax.ppermute(x, 'expert', [(i, i + 1 - 2 * (i % 2)) for i in range(expert...]
    unnamed x53 -> x55, local copies, waits for them, and re-layouts: 2.34 us -> 4.34 us
    ppermute x5, waiting for transfers between devices: 3.89 us -> 1.96 us  [over_core(): return lax.ppermute(x, 'tensor', [(0, 1), (1, 0)])]
  transfers between devices with their start and end apart: 33 -> 33, of which waited for: 13 -> 15; matrix products, arithmetic and copies ran while one was open for 9% -> 9% of each run, Pallas kernels for 21% -> 20%
where the time goes in v14:
time: 157 us; the launch traced here: 156 us
  waiting for transfers between devices  58.4 us (37%)
  starting transfers between devices  42.3 us (27%)
  Pallas kernels  34.2 us (22%)
  matrix products  9.93 us (6%)
  other arithmetic  6.17 us (4%)
  local copies, waits for them, and re-layouts  4.35 us (3%)
    ppermute x12, waiting for transfers between devices, over_line(): lax.ppermute(x, 'expert', [(i, (i // 2 + k) % lines * 2 + i % 2) for i in...  41.2 us
    pallas_call x22, Pallas kernels, local_call(): pl.pallas_call(kernel, out_shape=tuple(outs), in_specs=[SMEM_SPEC] + [VME...  34.2 us
    ppermute x12, starting transfers between devices, over_line(): lax.ppermute(x, 'expert', [(i, (i // 2 + k) % lines * 2 + i % 2) for i in...  17.1 us
    ppermute x16, starting transfers between devices, over_pair(): lax.ppermute(x, 'expert', [(i, i + 1 - 2 * (i % 2)) for i in range(expert...  15.3 us
    ppermute x16, waiting for transfers between devices, over_pair(): lax.ppermute(x, 'expert', [(i, i + 1 - 2 * (i % 2)) for i in range(expert...  15.2 us
    ppermute x5, starting transfers between devices, over_core(): return lax.ppermute(x, 'tensor', [(0, 1), (1, 0)])  9.98 us
    dot_general x3, matrix products, dot(): lax.dot_general(a, b, (contract, ((), ())), preferred_element_type=F32)  9.93 us
    unnamed x55, local copies, waits for them, and re-layouts  4.34 us
  transfers between devices with their start and end apart: 33, of which 15 were waited for; matrix products, arithmetic and copies ran while one was open for 9% of the time, Pallas kernels for 20%

profile of v14, /device:TPU:9, one launch (start us, length us, event | category | flops | bytes accessed | tf_op | source)
XLA Modules:
  0.0 156.5 jit_solution(13565210350697822161)
XLA Ops:
  1.4 1.0 pad_maximum_fusion.1.block.refs_0_
  2.4 1.3 collective-permute-start
  3.9 2.3 %collective-permute-start.1 = (bf16[144,1024]{1,0:T(8,128)(2,1)S(1)}, bf16[144,1024]{1,0:T(8,128)(2,1)S(1)}, u32[]{:S(2)}, u32[]{:S(2)}) collective-permute-start(bf16[144,1024]{1,0:T(8,128)(2,1)S(1)} %pad_maximum_fusion.1.block.refs_0_), channel_id=1, source_target_pairs={{0,8},{2,10},{4,12},{6,14},{8,0},{10,2},{12,4},{14,6},{1,9},{3,11}... | collective-permute-start | bytes 884744 | tf_op jit(solution)/shard_map/ppermute | solution.py:242
  6.3 0.9 shard_map.118
  7.2 1.3 collective-permute-start.3
  8.5 1.8 %collective-permute-done.block.refs_1_ = bf16[144,1024]{1,0:T(8,128)(2,1)S(1)} collective-permute-done((bf16[144,1024]{1,0:T(8,128)(2,1)S(1)}, bf16[144,1024]{1,0:T(8,128)(2,1)S(1)}, u32[]{:S(2)}, u32[]{:S(2)}) %collective-permute-start) | collective-permute-done | bytes 294944 | tf_op jit(solution)/shard_map/ppermute | solution.py:242
  10.3 0.9 shard_map.119
  11.2 1.3 collective-permute-start.4
  12.5 6.7 %collective-permute-done.2.block.refs_3_ = bf16[144,1024]{1,0:T(8,128)(2,1)S(1)} collective-permute-done((bf16[144,1024]{1,0:T(8,128)(2,1)S(1)}, bf16[144,1024]{1,0:T(8,128)(2,1)S(1)}, u32[]{:S(2)}, u32[]{:S(2)}) %collective-permute-start.2) | collective-permute-done | bytes 294944 | tf_op jit(solution)/shard_map/ppermute | solution.py:242
  19.2 0.9 shard_map.120
  20.1 1.6 collective-permute-start.5
  21.7 1.3 shard_map.121
  23.1 4.5 %collective-permute-done.6.refs_4_ = bf16[96,1024]{1,0:T(8,128)(2,1)S(1)} collective-permute-done((bf16[96,1024]{1,0:T(8,128)(2,1)S(1)}, bf16[96,1024]{1,0:T(8,128)(2,1)S(1)}, u32[]{:S(2)}, u32[]{:S(2)}) %collective-permute-start.6) | collective-permute-done | bytes 196640 | tf_op jit(solution)/shard_map/ppermute | solution.py:239
  27.6 0.8 collective-permute-done.1.block.refs_2_
  28.4 2.1 %collective-permute-start.8 = (bf16[128,1024]{1,0:T(8,128)(2,1)}, bf16[128,1024]{1,0:T(8,128)(2,1)S(1)}, u32[]{:S(2)}, u32[]{:S(2)}) collective-permute-start(bf16[128,1024]{1,0:T(8,128)(2,1)} %refs_0_), channel_id=1, source_target_pairs={{0,4},{2,6},{4,8},{6,10},{8,12},{10,14},{12,0},{14,2},{1,5},{3,7},... | collective-permute-start | bytes 786440 | tf_op jit(solution)/shard_map/ppermute | solution.py:242
  30.4 2.0 %collective-permute-start.9 = (bf16[128,1024]{1,0:T(8,128)(2,1)}, bf16[128,1024]{1,0:T(8,128)(2,1)S(1)}, u32[]{:S(2)}, u32[]{:S(2)}) collective-permute-start(bf16[128,1024]{1,0:T(8,128)(2,1)} %refs_0_), channel_id=1, source_target_pairs={{0,12},{2,14},{4,0},{6,2},{8,4},{10,6},{12,8},{14,10},{1,13},{3,15... | collective-permute-start | bytes 786440 | tf_op jit(solution)/shard_map/ppermute | solution.py:242
  32.4 0.9 shard_map.122
  33.3 1.3 collective-permute-start.7
  34.6 1.7 %collective-permute-done.8.block.refs_1_ = bf16[128,1024]{1,0:T(8,128)(2,1)S(1)} collective-permute-done((bf16[128,1024]{1,0:T(8,128)(2,1)}, bf16[128,1024]{1,0:T(8,128)(2,1)S(1)}, u32[]{:S(2)}, u32[]{:S(2)}) %collective-permute-start.8) | collective-permute-done | bytes 262176 | tf_op jit(solution)/shard_map/ppermute | solution.py:242
  37.1 4.5 %collective-permute-done.9.block.refs_3_ = bf16[128,1024]{1,0:T(8,128)(2,1)S(1)} collective-permute-done((bf16[128,1024]{1,0:T(8,128)(2,1)}, bf16[128,1024]{1,0:T(8,128)(2,1)S(1)}, u32[]{:S(2)}, u32[]{:S(2)}) %collective-permute-start.9) | collective-permute-done | bytes 262176 | tf_op jit(solution)/shard_map/ppermute | solution.py:242
  43.2 7.0 %collective-permute-start.10 = (bf16[896,1024]{1,0:T(8,128)(2,1)S(1)}, bf16[896,1024]{1,0:T(8,128)(2,1)S(1)}, u32[]{:S(2)}, u32[]{:S(2)}) collective-permute-start(bf16[896,1024]{1,0:T(8,128)(2,1)S(1)} %get-tuple-element.176.own), channel_id=1, source_target_pairs={{0,1},{1,0},{2,3},{3,2},{4,5},{5,4},{6,7},{7,6},{8,9},{9,8},{10,11... | collective-permute-start | bytes 5505032 | tf_op jit(solution)/shard_map/ppermute | solution.py:248
  50.2 2.1 %collective-permute-start.13 = (bf16[128,1024]{1,0:T(8,128)(2,1)}, bf16[128,1024]{1,0:T(8,128)(2,1)S(1)}, u32[]{:S(2)}, u32[]{:S(2)}) collective-permute-start(bf16[128,1024]{1,0:T(8,128)(2,1)} %refs_0_), channel_id=1, source_target_pairs={{0,8},{2,10},{4,12},{6,14},{8,0},{10,2},{12,4},{14,6},{1,9},{3,11}... | collective-permute-start | bytes 786440 | tf_op jit(solution)/shard_map/ppermute | solution.py:242
  52.3 1.2 collective-permute-start.11
  53.7 5.7 %shard_map.126 = (f32[896,384]{1,0:T(8,128)S(1)}, f32[896,384]{1,0:T(8,128)S(1)}, bf16[896,384]{1,0:T(8,128)(2,1)S(1)}, bf16[896,1024]{1,0:T(8,128)(2,1)S(1)}) custom-call(s32[3]{0:T(128)S(1)} %pad_add_fusion.info, bf16[896,1024]{1,0:T(8,128)(2,1)S(1)} %get-tuple-element.176.own, bf16[896,1024]{1,0:T(8,128)(2,1)S(1)} %collective-permute-done.10.other, ...), custom_call_target="tpu_custom_call" | custom-call | flops 1000 | bytes 1000 | tf_op jit(solution)/shard_map/pallas_call | solution.py:41
  59.4 4.4 %collective-permute-done.13.block.refs_2_ = bf16[128,1024]{1,0:T(8,128)(2,1)S(1)} collective-permute-done((bf16[128,1024]{1,0:T(8,128)(2,1)}, bf16[128,1024]{1,0:T(8,128)(2,1)S(1)}, u32[]{:S(2)}, u32[]{:S(2)}) %collective-permute-start.13) | collective-permute-done | bytes 262176 | tf_op jit(solution)/shard_map/ppermute | solution.py:242
  63.9 0.9 collective-permute-start.15
  65.5 1.3 collective-permute-start.14
  66.7 5.3 %collective-permute-done.14.refs_6_ = bf16[96,1024]{1,0:T(8,128)(2,1)S(1)} collective-permute-done((bf16[96,1024]{1,0:T(8,128)(2,1)S(1)}, bf16[96,1024]{1,0:T(8,128)(2,1)S(1)}, u32[]{:S(2)}, u32[]{:S(2)}) %collective-permute-start.14) | collective-permute-done | bytes 196640 | tf_op jit(solution)/shard_map/ppermute | solution.py:239
  72.1 1.1 shard_map.128.own
  73.2 1.7 %shard_map.129 = (f32[4,128,1024]{2,1,0:T(8,128)S(1)}, bf16[96,1024]{1,0:T(8,128)(2,1)S(1)}, bf16[96,1024]{1,0:T(8,128)(2,1)S(1)}, bf16[96,1024]{1,0:T(8,128)(2,1)S(1)}, bf16[96,1024]{1,0:T(8,128)(2,1)S(1)}) custom-call(s32[3]{0:T(128)S(1)} %pad_add_fusion.info, bf16[896,1024]{1,0:T(8,128)(2,1)S(1)} %collective-permute-done.15.came, ...), custom_call_target="tpu_custom_call" | custom-call | flops 1000 | bytes 1000 | tf_op jit(solution)/shard_map/pallas_call | solution.py:41
  75.5 0.8 collective-permute-start.16
  76.3 1.2 collective-permute-start.17
  77.8 1.9 %collective-permute-done.16.other = bf16[896,1024]{1,0:T(8,128)(2,1)S(1)} collective-permute-done((bf16[896,1024]{1,0:T(8,128)(2,1)S(1)}, bf16[896,1024]{1,0:T(8,128)(2,1)S(1)}, u32[]{:S(2)}, u32[]{:S(2)}) %collective-permute-start.16) | collective-permute-done | bytes 1835040 | tf_op jit(solution)/shard_map/ppermute | solution.py:248
  79.7 6.6 %shard_map.130 = (bf16[896,384]{1,0:T(8,128)(2,1)S(1)}, bf16[896,384]{1,0:T(8,128)(2,1)S(1)}, bf16[896,1024]{1,0:T(8,128)(2,1)}, f32[4,16,128]{2,1,0:T(8,128)S(1)}, f32[4,16,128]{2,1,0:T(8,128)S(1)}) custom-call(s32[3]{0:T(128)S(1)} %pad_add_fusion.info, bf16[896,1024]{1,0:T(8,128)(2,1)S(1)} %shard_map.128.own, ...), custom_call_target="tpu_custom_call" | custom-call | flops 1000 | bytes 1000 | tf_op jit(solution)/shard_map/pallas_call | solution.py:41
  87.1 0.8 collective-permute-start.19
  87.9 1.5 shard_map.132
  89.4 1.8 %collective-permute-start.21 = (bf16[128,1024]{1,0:T(8,128)(2,1)}, bf16[128,1024]{1,0:T(8,128)(2,1)}, u32[]{:S(2)}, u32[]{:S(2)}) collective-permute-start(bf16[128,1024]{1,0:T(8,128)(2,1)} %shard_map.132), channel_id=1, source_target_pairs={{0,12},{2,14},{4,0},{6,2},{8,4},{10,6},{12,8},{14,10},{1,13},{3,15... | collective-permute-start | bytes 786440 | tf_op jit(solution)/shard_map/ppermute | solution.py:242
  91.2 1.5 shard_map.133
  92.7 1.2 collective-permute-start.20
  93.9 1.4 copy-done.4
  95.4 1.4 copy-done.6
  97.5 3.8 %shard_map.131 = (f32[4,128,1024]{2,1,0:T(8,128)S(1)}, bf16[112,1024]{1,0:T(8,128)(2,1)S(1)}, bf16[112,1024]{1,0:T(8,128)(2,1)S(1)}, bf16[112,1024]{1,0:T(8,128)(2,1)S(1)}, bf16[112,1024]{1,0:T(8,128)(2,1)S(1)}) custom-call(s32[3]{0:T(128)S(1)} %pad_add_fusion.info, bf16[896,1024]{1,0:T(8,128)(2,1)} %collective-permute-done.19.came, ...), custom_call_target="tpu_custom_call" | custom-call | flops 1000 | bytes 1000 | tf_op jit(solution)/shard_map/pallas_call | solution.py:41
  101.3 4.6 %collective-permute-done.22 = bf16[128,1024]{1,0:T(8,128)(2,1)} collective-permute-done((bf16[128,1024]{1,0:T(8,128)(2,1)}, bf16[128,1024]{1,0:T(8,128)(2,1)}, u32[]{:S(2)}, u32[]{:S(2)}) %collective-permute-start.22) | collective-permute-done | bytes 262176 | tf_op jit(solution)/shard_map/ppermute | solution.py:242
  106.0 1.2 collective-permute-start.23
  107.4 1.2 collective-permute-start.25
  108.6 0.8 shard_map.137
  109.5 1.9 %collective-permute-start.26 = (bf16[128,1024]{1,0:T(8,128)(2,1)S(1)}, bf16[128,1024]{1,0:T(8,128)(2,1)S(1)}, u32[]{:S(2)}, u32[]{:S(2)}) collective-permute-start(bf16[128,1024]{1,0:T(8,128)(2,1)S(1)} %shard_map.137), channel_id=1, source_target_pairs={{0,8},{2,10},{4,12},{6,14},{8,0},{10,2},{12,4},{14,6},{1,9},{3,11}... | collective-permute-start | bytes 786440 | tf_op jit(solution)/shard_map/ppermute | solution.py:242
  111.6 3.0 %fusion.4 = bf16[384,2048]{1,0:T(8,128)(2,1)} fusion(bf16[896,384]{1,0:T(8,128)(2,1)S(1)} %copy-done.14, bf16[896,1024]{1,0:T(8,128)(2,1)S(1)} %get-tuple-element.197, bf16[896,1024]{1,0:T(8,128)(2,1)S(1)} %get-tuple-element.196), kind=kOutput, calls=%fused_computation.5 | convolution fusion | flops 1417412608 | bytes 5931008 | tf_op jit(solution)/shard_map/dot_general | solution.py:24
  114.9 3.5 %convolution_convert_fusion.1 = bf16[2048,384]{1,0:T(8,128)(2,1)} fusion(bf16[896,384]{1,0:T(8,128)(2,1)S(1)} %get-tuple-element.144.refs_0_, bf16[896,1024]{1,0:T(8,128)(2,1)S(1)} %get-tuple-element.195, bf16[896,1024]{1,0:T(8,128)(2,1)S(1)} %get-tuple-element.194), kind=kOutput, calls=%fused_computation.7 | convolution fusion | flops 1417412608 | bytes 5931008 | tf_op jit(solution)/shard_map/dot_general | solution.py:24
  118.7 2.8 %collective-permute-done.25.back = bf16[96,1024]{1,0:T(8,128)(2,1)S(1)} collective-permute-done((bf16[96,1024]{1,0:T(8,128)(2,1)S(1)}, bf16[96,1024]{1,0:T(8,128)(2,1)S(1)}, u32[]{:S(2)}, u32[]{:S(2)}) %collective-permute-start.25) | collective-permute-done | bytes 196640 | tf_op jit(solution)/shard_map/ppermute | solution.py:239
  121.5 0.8 shard_map.136
  122.3 0.8 shard_map.134
  123.1 1.3 collective-permute-start.28
  124.3 0.8 shard_map.135
  126.0 1.9 %collective-permute-start.30 = (bf16[144,1024]{1,0:T(8,128)(2,1)S(1)}, bf16[144,1024]{1,0:T(8,128)(2,1)S(1)}, u32[]{:S(2)}, u32[]{:S(2)}) collective-permute-start(bf16[144,1024]{1,0:T(8,128)(2,1)S(1)} %shard_map.134), channel_id=1, source_target_pairs={{0,8},{2,10},{4,12},{6,14},{8,0},{10,2},{12,4},{14,6},{1,9},{3,11}... | collective-permute-start | bytes 884744 | tf_op jit(solution)/shard_map/ppermute | solution.py:242
  128.0 1.9 %add_convert_fusion.1 = bf16[128,1024]{1,0:T(8,128)(2,1)} fusion(bf16[128,1024]{1,0:T(8,128)(2,1)} %collective-permute-done.22, bf16[128,1024]{1,0:T(8,128)(2,1)S(1)} %collective-permute-done.26, bf16[128,1024]{1,0:T(8,128)(2,1)} %collective-permute-done.21, bf16[128,1024]{1,0:T(8,128)(2,1)S(1)} %shard_map.136), kind=kLoop, calls=%fused_computation.14 | loop fusion | flops 1048576 | bytes 1310720 | tf_op jit(solution)/shard_map/convert_element_type | solution.py:348
  129.9 0.8 shard_map.139
  130.7 0.9 collective-permute-start.29
  131.6 1.9 %collective-permute-done.27.back = bf16[112,1024]{1,0:T(8,128)(2,1)S(1)} collective-permute-done((bf16[112,1024]{1,0:T(8,128)(2,1)S(1)}, bf16[112,1024]{1,0:T(8,128)(2,1)S(1)}, u32[]{:S(2)}, u32[]{:S(2)}) %collective-permute-start.27) | collective-permute-done | bytes 229408 | tf_op jit(solution)/shard_map/ppermute | solution.py:239
  133.5 0.8 shard_map.138
  134.3 3.5 %fusion.7 = bf16[1,2048,384]{2,1,0:T(8,128)(2,1)} fusion(bf16[896,2048]{1,0:T(8,128)(2,1)S(1)} %pad_maximum_fusion, bf16[896,384]{1,0:T(8,128)(2,1)S(1)} %get-tuple-element.184.refs_1_), kind=kOutput, calls=%fused_computation.8 | convolution fusion | flops 1410072576 | bytes 5931008 | tf_op jit(solution)/shard_map/dot_general | solution.py:24
  137.8 11.2 %collective-permute-done.30 = bf16[144,1024]{1,0:T(8,128)(2,1)S(1)} collective-permute-done((bf16[144,1024]{1,0:T(8,128)(2,1)S(1)}, bf16[144,1024]{1,0:T(8,128)(2,1)S(1)}, u32[]{:S(2)}, u32[]{:S(2)}) %collective-permute-start.30) | collective-permute-done | bytes 294944 | tf_op jit(solution)/shard_map/ppermute | solution.py:242
  149.1 5.3 %collective-permute-done.29 = bf16[144,1024]{1,0:T(8,128)(2,1)S(1)} collective-permute-done((bf16[144,1024]{1,0:T(8,128)(2,1)S(1)}, bf16[144,1024]{1,0:T(8,128)(2,1)S(1)}, u32[]{:S(2)}, u32[]{:S(2)}) %collective-permute-start.29) | collective-permute-done | bytes 294944 | tf_op jit(solution)/shard_map/ppermute | solution.py:242
  155.0 0.9 add_convert_fusion
  (109 shorter events, 10.3 us)
Async XLA Ops:
  2.4 7.9 %collective-permute-start = (bf16[144,1024]{1,0:T(8,128)(2,1)S(1)}, bf16[144,1024]{1,0:T(8,128)(2,1)S(1)}, u32[]{:S(2)}, u32[]{:S(2)}) collective-permute-start(bf16[144,1024]{1,0:T(8,128)(2,1)S(1)} %pad_maximum_fusion.1.block.refs_0_), channel_id=1, source_target_pairs={{0,4},{2,6},{4,8},{6,10},{8,12},{10,14},{12,0},{14,2},{1,5},{3,7},... | collective-permute-start | bytes 884744 | tf_op jit(solution)/shard_map/ppermute | solution.py:242
  3.7 15.5 %collective-permute-start.2 = (bf16[144,1024]{1,0:T(8,128)(2,1)S(1)}, bf16[144,1024]{1,0:T(8,128)(2,1)S(1)}, u32[]{:S(2)}, u32[]{:S(2)}) collective-permute-start(bf16[144,1024]{1,0:T(8,128)(2,1)S(1)} %pad_maximum_fusion.1.block.refs_0_), channel_id=1, source_target_pairs={{0,12},{2,14},{4,0},{6,2},{8,4},{10,6},{12,8},{14,10},{1,13},{3,15... | collective-permute-start | bytes 884744 | tf_op jit(solution)/shard_map/ppermute | solution.py:242
  3.9 24.5 %collective-permute-start.1 = (bf16[144,1024]{1,0:T(8,128)(2,1)S(1)}, bf16[144,1024]{1,0:T(8,128)(2,1)S(1)}, u32[]{:S(2)}, u32[]{:S(2)}) collective-permute-start(bf16[144,1024]{1,0:T(8,128)(2,1)S(1)} %pad_maximum_fusion.1.block.refs_0_), channel_id=1, source_target_pairs={{0,8},{2,10},{4,12},{6,14},{8,0},{10,2},{12,4},{14,6},{1,9},{3,11}... | collective-permute-start | bytes 884744 | tf_op jit(solution)/shard_map/ppermute | solution.py:242
  6.3 47.4 %copy-start.5 = (bf16[1,2048,384]{2,1,0:T(8,128)(2,1)S(1)}, bf16[1,2048,384]{2,1,0:T(8,128)(2,1)}, u32[]{:S(2)}) copy-start(bf16[1,2048,384]{2,1,0:T(8,128)(2,1)} %param.11) | copy-start | bytes 4718596
  7.2 20.4 %collective-permute-start.3 = (bf16[112,1024]{1,0:T(8,128)(2,1)S(1)}, bf16[112,1024]{1,0:T(8,128)(2,1)S(1)}, u32[]{:S(2)}, u32[]{:S(2)}) collective-permute-start(bf16[112,1024]{1,0:T(8,128)(2,1)S(1)} %get-tuple-element.96), channel_id=1, source_target_pairs={{0,2},{2,0},{4,6},{6,4},{8,10},{10,8},{12,14},{14,12},{1,3},{3,1},... | collective-permute-start | bytes 688136 | tf_op jit(solution)/shard_map/ppermute | solution.py:239
  11.2 76.7 %copy-start.15 = (bf16[96,128]{1,0:T(8,128)(2,1)}, bf16[96,128]{1,0:T(8,128)(2,1)S(1)}, u32[]{:S(2)}) copy-start(bf16[96,128]{1,0:T(8,128)(2,1)S(1)} %get-tuple-element.109.place) | copy-start | bytes 73732
  11.2 17.2 %collective-permute-start.4 = (bf16[112,1024]{1,0:T(8,128)(2,1)S(1)}, bf16[112,1024]{1,0:T(8,128)(2,1)S(1)}, u32[]{:S(2)}, u32[]{:S(2)}) collective-permute-start(bf16[112,1024]{1,0:T(8,128)(2,1)S(1)} %get-tuple-element.97), channel_id=1, source_target_pairs={{0,2},{2,0},{4,6},{6,4},{8,10},{10,8},{12,14},{14,12},{1,3},{3,1},... | collective-permute-start | bytes 688136 | tf_op jit(solution)/shard_map/ppermute | solution.py:239
  20.1 71.1 %copy-start.17 = (bf16[96,128]{1,0:T(8,128)(2,1)}, bf16[96,128]{1,0:T(8,128)(2,1)S(1)}, u32[]{:S(2)}) copy-start(bf16[96,128]{1,0:T(8,128)(2,1)S(1)} %get-tuple-element.110.place) | copy-start | bytes 73732
  20.1 8.3 %collective-permute-start.5 = (bf16[112,1024]{1,0:T(8,128)(2,1)S(1)}, bf16[112,1024]{1,0:T(8,128)(2,1)S(1)}, u32[]{:S(2)}, u32[]{:S(2)}) collective-permute-start(bf16[112,1024]{1,0:T(8,128)(2,1)S(1)} %get-tuple-element.98), channel_id=1, source_target_pairs={{0,2},{2,0},{4,6},{6,4},{8,10},{10,8},{12,14},{14,12},{1,3},{3,1},... | collective-permute-start | bytes 688136 | tf_op jit(solution)/shard_map/ppermute | solution.py:239
  21.7 32.1 %copy-start.2 = (bf16[1,384,2048]{2,1,0:T(8,128)(2,1)S(1)}, bf16[1,384,2048]{2,1,0:T(8,128)(2,1)}, u32[]{:S(2)}) copy-start(bf16[1,384,2048]{2,1,0:T(8,128)(2,1)} %param.12) | copy-start | bytes 4718596
  21.7 32.1 %copy-start.3 = (bf16[1,2048,384]{2,1,0:T(8,128)(2,1)S(1)}, bf16[1,2048,384]{2,1,0:T(8,128)(2,1)}, u32[]{:S(2)}) copy-start(bf16[1,2048,384]{2,1,0:T(8,128)(2,1)} %param.10) | copy-start | bytes 4718596
  23.0 4.6 %collective-permute-start.6 = (bf16[96,1024]{1,0:T(8,128)(2,1)S(1)}, bf16[96,1024]{1,0:T(8,128)(2,1)S(1)}, u32[]{:S(2)}, u32[]{:S(2)}) collective-permute-start(bf16[96,1024]{1,0:T(8,128)(2,1)S(1)} %shard_map.121), channel_id=1, source_target_pairs={{0,2},{2,0},{4,6},{6,4},{8,10},{10,8},{12,14},{14,12},{1,3},{3,1},... | collective-permute-start | bytes 589832 | tf_op jit(solution)/shard_map/ppermute | solution.py:239
  28.4 8.0 %collective-permute-start.8 = (bf16[128,1024]{1,0:T(8,128)(2,1)}, bf16[128,1024]{1,0:T(8,128)(2,1)S(1)}, u32[]{:S(2)}, u32[]{:S(2)}) collective-permute-start(bf16[128,1024]{1,0:T(8,128)(2,1)} %refs_0_), channel_id=1, source_target_pairs={{0,4},{2,6},{4,8},{6,10},{8,12},{10,14},{12,0},{14,2},{1,5},{3,7},... | collective-permute-start | bytes 786440 | tf_op jit(solution)/shard_map/ppermute | solution.py:242
  30.4 11.2 %collective-permute-start.9 = (bf16[128,1024]{1,0:T(8,128)(2,1)}, bf16[128,1024]{1,0:T(8,128)(2,1)S(1)}, u32[]{:S(2)}, u32[]{:S(2)}) collective-permute-start(bf16[128,1024]{1,0:T(8,128)(2,1)} %refs_0_), channel_id=1, source_target_pairs={{0,12},{2,14},{4,0},{6,2},{8,4},{10,6},{12,8},{14,10},{1,13},{3,15... | collective-permute-start | bytes 786440 | tf_op jit(solution)/shard_map/ppermute | solution.py:242
  33.3 31.4 %copy-start.19 = (bf16[96,128]{1,0:T(8,128)(2,1)}, bf16[96,128]{1,0:T(8,128)(2,1)S(1)}, u32[]{:S(2)}) copy-start(bf16[96,128]{1,0:T(8,128)(2,1)S(1)} %get-tuple-element.131.place) | copy-start | bytes 73732
  33.3 9.0 %collective-permute-start.7 = (bf16[112,1024]{1,0:T(8,128)(2,1)S(1)}, bf16[112,1024]{1,0:T(8,128)(2,1)S(1)}, u32[]{:S(2)}, u32[]{:S(2)}) collective-permute-start(bf16[112,1024]{1,0:T(8,128)(2,1)S(1)} %get-tuple-element.106), channel_id=1, source_target_pairs={{0,2},{2,0},{4,6},{6,4},{8,10},{10,8},{12,14},{14,12},{1,3},{3,1},... | collective-permute-start | bytes 688136 | tf_op jit(solution)/shard_map/ppermute | solution.py:239
  43.2 16.3 %copy-start.7 = (bf16[896,1024]{1,0:T(8,128)(2,1)}, bf16[896,1024]{1,0:T(8,128)(2,1)S(1)}, u32[]{:S(2)}) copy-start(bf16[896,1024]{1,0:T(8,128)(2,1)S(1)} %get-tuple-element.176.own) | copy-start | bytes 5505028
  43.2 10.6 %collective-permute-start.10 = (bf16[896,1024]{1,0:T(8,128)(2,1)S(1)}, bf16[896,1024]{1,0:T(8,128)(2,1)S(1)}, u32[]{:S(2)}, u32[]{:S(2)}) collective-permute-start(bf16[896,1024]{1,0:T(8,128)(2,1)S(1)} %get-tuple-element.176.own), channel_id=1, source_target_pairs={{0,1},{1,0},{2,3},{3,2},{4,5},{5,4},{6,7},{7,6},{8,9},{9,8},{10,11... | collective-permute-start | bytes 5505032 | tf_op jit(solution)/shard_map/ppermute | solution.py:248
  50.2 13.7 %collective-permute-start.13 = (bf16[128,1024]{1,0:T(8,128)(2,1)}, bf16[128,1024]{1,0:T(8,128)(2,1)S(1)}, u32[]{:S(2)}, u32[]{:S(2)}) collective-permute-start(bf16[128,1024]{1,0:T(8,128)(2,1)} %refs_0_), channel_id=1, source_target_pairs={{0,8},{2,10},{4,12},{6,14},{8,0},{10,2},{12,4},{14,6},{1,9},{3,11}... | collective-permute-start | bytes 786440 | tf_op jit(solution)/shard_map/ppermute | solution.py:242
  52.3 11.6 %collective-permute-start.11 = (bf16[96,1024]{1,0:T(8,128)(2,1)S(1)}, bf16[96,1024]{1,0:T(8,128)(2,1)S(1)}, u32[]{:S(2)}, u32[]{:S(2)}) collective-permute-start(bf16[96,1024]{1,0:T(8,128)(2,1)S(1)} %shard_map.123), channel_id=1, source_target_pairs={{0,2},{2,0},{4,6},{6,4},{8,10},{10,8},{12,14},{14,12},{1,3},{3,1},... | collective-permute-start | bytes 589832 | tf_op jit(solution)/shard_map/ppermute | solution.py:239
  53.5 10.4 %collective-permute-start.12 = (bf16[96,1024]{1,0:T(8,128)(2,1)S(1)}, bf16[96,1024]{1,0:T(8,128)(2,1)S(1)}, u32[]{:S(2)}, u32[]{:S(2)}) collective-permute-start(bf16[96,1024]{1,0:T(8,128)(2,1)S(1)} %shard_map.124), channel_id=1, source_target_pairs={{0,2},{2,0},{4,6},{6,4},{8,10},{10,8},{12,14},{14,12},{1,3},{3,1},... | collective-permute-start | bytes 589832 | tf_op jit(solution)/shard_map/ppermute | solution.py:239
  53.7 5.7 %copy-start.9 = (bf16[896,1024]{1,0:T(8,128)(2,1)}, bf16[896,1024]{1,0:T(8,128)(2,1)S(1)}, u32[]{:S(2)}) copy-start(bf16[896,1024]{1,0:T(8,128)(2,1)S(1)} %collective-permute-done.10.other) | copy-start | bytes 5505028
  59.4 13.7 %copy-start.13 = (bf16[896,384]{1,0:T(8,128)(2,1)}, bf16[896,384]{1,0:T(8,128)(2,1)S(1)}, u32[]{:S(2)}) copy-start(bf16[896,384]{1,0:T(8,128)(2,1)S(1)} %get-tuple-element.134.refs_0_) | copy-start | bytes 2064388
  63.9 9.3 %collective-permute-start.15 = (bf16[896,1024]{1,0:T(8,128)(2,1)S(1)}, bf16[896,1024]{1,0:T(8,128)(2,1)S(1)}, u32[]{:S(2)}, u32[]{:S(2)}) collective-permute-start(bf16[896,1024]{1,0:T(8,128)(2,1)S(1)} %get-tuple-element.133), channel_id=1, source_target_pairs={{0,1},{1,0},{2,3},{3,2},{4,5},{5,4},{6,7},{7,6},{8,9},{9,8},{10,11... | collective-permute-start | bytes 5505032 | tf_op jit(solution)/shard_map/ppermute | solution.py:248
  65.5 6.6 %collective-permute-start.14 = (bf16[96,1024]{1,0:T(8,128)(2,1)S(1)}, bf16[96,1024]{1,0:T(8,128)(2,1)S(1)}, u32[]{:S(2)}, u32[]{:S(2)}) collective-permute-start(bf16[96,1024]{1,0:T(8,128)(2,1)S(1)} %shard_map.127), channel_id=1, source_target_pairs={{0,2},{2,0},{4,6},{6,4},{8,10},{10,8},{12,14},{14,12},{1,3},{3,1},... | collective-permute-start | bytes 589832 | tf_op jit(solution)/shard_map/ppermute | solution.py:239
  73.1 6.6 %copy-start = (bf16[896,1024]{1,0:T(8,128)(2,1)}, bf16[896,1024]{1,0:T(8,128)(2,1)S(1)}, u32[]{:S(2)}) copy-start(bf16[896,1024]{1,0:T(8,128)(2,1)S(1)} %shard_map.128.own) | copy-start | bytes 5505028
  74.8 0.7 copy-start.23
  75.5 10.8 %copy-start.25 = (bf16[96,1024]{1,0:T(8,128)(2,1)}, bf16[96,1024]{1,0:T(8,128)(2,1)S(1)}, u32[]{:S(2)}) copy-start(bf16[96,1024]{1,0:T(8,128)(2,1)S(1)} %get-tuple-element.155) | copy-start | bytes 589828
  75.5 4.2 %collective-permute-start.16 = (bf16[896,1024]{1,0:T(8,128)(2,1)S(1)}, bf16[896,1024]{1,0:T(8,128)(2,1)S(1)}, u32[]{:S(2)}, u32[]{:S(2)}) collective-permute-start(bf16[896,1024]{1,0:T(8,128)(2,1)S(1)} %shard_map.128.own), channel_id=1, source_target_pairs={{0,1},{1,0},{2,3},{3,2},{4,5},{5,4},{6,7},{7,6},{8,9},{9,8},{10,11... | collective-permute-start | bytes 5505032 | tf_op jit(solution)/shard_map/ppermute | solution.py:248
  76.3 10.0 %collective-permute-start.17 = (bf16[96,1024]{1,0:T(8,128)(2,1)S(1)}, bf16[96,1024]{1,0:T(8,128)(2,1)S(1)}, u32[]{:S(2)}, u32[]{:S(2)}) collective-permute-start(bf16[96,1024]{1,0:T(8,128)(2,1)S(1)} %get-tuple-element.136), channel_id=1, source_target_pairs={{0,2},{2,0},{4,6},{6,4},{8,10},{10,8},{12,14},{14,12},{1,3},{3,1},... | collective-permute-start | bytes 589832 | tf_op jit(solution)/shard_map/ppermute | solution.py:239
  77.5 9.5 %collective-permute-start.18 = (bf16[96,1024]{1,0:T(8,128)(2,1)S(1)}, bf16[96,1024]{1,0:T(8,128)(2,1)S(1)}, u32[]{:S(2)}, u32[]{:S(2)}) collective-permute-start(bf16[96,1024]{1,0:T(8,128)(2,1)S(1)} %get-tuple-element.138), channel_id=1, source_target_pairs={{0,2},{2,0},{4,6},{6,4},{8,10},{10,8},{12,14},{14,12},{1,3},{3,1},... | collective-permute-start | bytes 589832 | tf_op jit(solution)/shard_map/ppermute | solution.py:239
  79.7 6.6 %copy-start.11 = (bf16[896,1024]{1,0:T(8,128)(2,1)}, bf16[896,1024]{1,0:T(8,128)(2,1)S(1)}, u32[]{:S(2)}) copy-start(bf16[896,1024]{1,0:T(8,128)(2,1)S(1)} %collective-permute-done.16.other) | copy-start | bytes 5505028
  86.3 6.4 %copy-start.21 = (f32[4,16,128]{2,1,0:T(8,128)}, f32[4,16,128]{2,1,0:T(8,128)S(1)}, u32[]{:S(2)}) copy-start(f32[4,16,128]{2,1,0:T(8,128)S(1)} %get-tuple-element.146.refs_4_) | copy-start | bytes 98308
  87.1 6.9 %collective-permute-start.19 = (bf16[896,1024]{1,0:T(8,128)(2,1)}, bf16[896,1024]{1,0:T(8,128)(2,1)}, u32[]{:S(2)}, u32[]{:S(2)}) collective-permute-start(bf16[896,1024]{1,0:T(8,128)(2,1)} %get-tuple-element.143), channel_id=1, source_target_pairs={{0,1},{1,0},{2,3},{3,2},{4,5},{5,4},{6,7},{7,6},{8,9},{9,8},{10,11... | collective-permute-start | bytes 5505032 | tf_op jit(solution)/shard_map/ppermute | solution.py:248
  89.3 4.6 %copy-start.26 = (s32[128,4]{0,1:T(4,128)S(1)}, s32[128,4]{0,1:T(4,128)}, u32[]{:S(2)}) copy-start(s32[128,4]{0,1:T(4,128)} %param.8) | copy-start | bytes 6148
  89.4 12.0 %collective-permute-start.21 = (bf16[128,1024]{1,0:T(8,128)(2,1)}, bf16[128,1024]{1,0:T(8,128)(2,1)}, u32[]{:S(2)}, u32[]{:S(2)}) collective-permute-start(bf16[128,1024]{1,0:T(8,128)(2,1)} %shard_map.132), channel_id=1, source_target_pairs={{0,12},{2,14},{4,0},{6,2},{8,4},{10,6},{12,8},{14,10},{1,13},{3,15... | collective-permute-start | bytes 786440 | tf_op jit(solution)/shard_map/ppermute | solution.py:242
  92.7 13.3 %collective-permute-start.22 = (bf16[128,1024]{1,0:T(8,128)(2,1)}, bf16[128,1024]{1,0:T(8,128)(2,1)}, u32[]{:S(2)}, u32[]{:S(2)}) collective-permute-start(bf16[128,1024]{1,0:T(8,128)(2,1)} %shard_map.133), channel_id=1, source_target_pairs={{0,4},{2,6},{4,8},{6,10},{8,12},{10,14},{12,0},{14,2},{1,5},{3,7},... | collective-permute-start | bytes 786440 | tf_op jit(solution)/shard_map/ppermute | solution.py:242
  92.7 8.6 %collective-permute-start.20 = (bf16[96,1024]{1,0:T(8,128)(2,1)}, bf16[96,1024]{1,0:T(8,128)(2,1)S(1)}, u32[]{:S(2)}, u32[]{:S(2)}) collective-permute-start(bf16[96,1024]{1,0:T(8,128)(2,1)} %copy-done.25), channel_id=1, source_target_pairs={{0,2},{2,0},{4,6},{6,4},{8,10},{10,8},{12,14},{14,12},{1,3},{3,1},... | collective-permute-start | bytes 589832 | tf_op jit(solution)/shard_map/ppermute | solution.py:239
  93.9 1.4 copy-start.4
  95.3 1.4 copy-start.6
  96.8 0.8 copy-start.22
  97.5 9.9 %copy-start.24 = (bf16[96,1024]{1,0:T(8,128)(2,1)S(1)}, bf16[96,1024]{1,0:T(8,128)(2,1)}, u32[]{:S(2)}) copy-start(bf16[96,1024]{1,0:T(8,128)(2,1)} %copy-done.23) | copy-start | bytes 589828
  97.5 11.1 %copy-start.20 = (bf16[96,128]{1,0:T(8,128)(2,1)S(1)}, bf16[96,128]{1,0:T(8,128)(2,1)}, u32[]{:S(2)}) copy-start(bf16[96,128]{1,0:T(8,128)(2,1)} %copy-done.19) | copy-start | bytes 73732
  97.5 13.8 %copy-start.12 = (bf16[896,1024]{1,0:T(8,128)(2,1)S(1)}, bf16[896,1024]{1,0:T(8,128)(2,1)}, u32[]{:S(2)}) copy-start(bf16[896,1024]{1,0:T(8,128)(2,1)} %copy-done.11) | copy-start | bytes 5505028
  101.3 10.0 %copy-start.1 = (bf16[896,1024]{1,0:T(8,128)(2,1)S(1)}, bf16[896,1024]{1,0:T(8,128)(2,1)}, u32[]{:S(2)}) copy-start(bf16[896,1024]{1,0:T(8,128)(2,1)} %copy-done) | copy-start | bytes 5505028
  106.0 16.3 %collective-permute-start.23 = (bf16[112,1024]{1,0:T(8,128)(2,1)S(1)}, bf16[112,1024]{1,0:T(8,128)(2,1)S(1)}, u32[]{:S(2)}, u32[]{:S(2)}) collective-permute-start(bf16[112,1024]{1,0:T(8,128)(2,1)S(1)} %get-tuple-element.158), channel_id=1, source_target_pairs={{0,2},{2,0},{4,6},{6,4},{8,10},{10,8},{12,14},{14,12},{1,3},{3,1},... | collective-permute-start | bytes 688136 | tf_op jit(solution)/shard_map/ppermute | solution.py:239
  107.2 17.2 %collective-permute-start.24 = (bf16[112,1024]{1,0:T(8,128)(2,1)S(1)}, bf16[112,1024]{1,0:T(8,128)(2,1)S(1)}, u32[]{:S(2)}, u32[]{:S(2)}) collective-permute-start(bf16[112,1024]{1,0:T(8,128)(2,1)S(1)} %get-tuple-element.160), channel_id=1, source_target_pairs={{0,2},{2,0},{4,6},{6,4},{8,10},{10,8},{12,14},{14,12},{1,3},{3,1},... | collective-permute-start | bytes 688136 | tf_op jit(solution)/shard_map/ppermute | solution.py:239
  107.4 14.0 %collective-permute-start.25 = (bf16[96,1024]{1,0:T(8,128)(2,1)S(1)}, bf16[96,1024]{1,0:T(8,128)(2,1)S(1)}, u32[]{:S(2)}, u32[]{:S(2)}) collective-permute-start(bf16[96,1024]{1,0:T(8,128)(2,1)S(1)} %copy-done.24), channel_id=1, source_target_pairs={{0,2},{2,0},{4,6},{6,4},{8,10},{10,8},{12,14},{14,12},{1,3},{3,1},... | collective-permute-start | bytes 589832 | tf_op jit(solution)/shard_map/ppermute | solution.py:239
  109.4 2.1 %copy-start.14 = (bf16[896,384]{1,0:T(8,128)(2,1)S(1)}, bf16[896,384]{1,0:T(8,128)(2,1)}, u32[]{:S(2)}) copy-start(bf16[896,384]{1,0:T(8,128)(2,1)} %copy-done.13) | copy-start | bytes 2064388
  109.5 16.0 %collective-permute-start.26 = (bf16[128,1024]{1,0:T(8,128)(2,1)S(1)}, bf16[128,1024]{1,0:T(8,128)(2,1)S(1)}, u32[]{:S(2)}, u32[]{:S(2)}) collective-permute-start(bf16[128,1024]{1,0:T(8,128)(2,1)S(1)} %shard_map.137), channel_id=1, source_target_pairs={{0,8},{2,10},{4,12},{6,14},{8,0},{10,2},{12,4},{14,6},{1,9},{3,11}... | collective-permute-start | bytes 786440 | tf_op jit(solution)/shard_map/ppermute | solution.py:242
  111.6 3.0 %copy-start.8 = (bf16[896,1024]{1,0:T(8,128)(2,1)S(1)}, bf16[896,1024]{1,0:T(8,128)(2,1)}, u32[]{:S(2)}) copy-start(bf16[896,1024]{1,0:T(8,128)(2,1)} %copy-done.7) | copy-start | bytes 5505028
  111.6 3.0 %copy-start.10 = (bf16[896,1024]{1,0:T(8,128)(2,1)S(1)}, bf16[896,1024]{1,0:T(8,128)(2,1)}, u32[]{:S(2)}) copy-start(bf16[896,1024]{1,0:T(8,128)(2,1)} %copy-done.9) | copy-start | bytes 5505028
  122.2 2.1 %copy-start.18 = (bf16[96,128]{1,0:T(8,128)(2,1)S(1)}, bf16[96,128]{1,0:T(8,128)(2,1)}, u32[]{:S(2)}) copy-start(bf16[96,128]{1,0:T(8,128)(2,1)} %copy-done.17) | copy-start | bytes 73732
  123.1 6.8 %copy-start.16 = (bf16[96,128]{1,0:T(8,128)(2,1)S(1)}, bf16[96,128]{1,0:T(8,128)(2,1)}, u32[]{:S(2)}) copy-start(bf16[96,128]{1,0:T(8,128)(2,1)} %copy-done.15) | copy-start | bytes 73732
  123.1 6.8 %collective-permute-start.28 = (bf16[112,1024]{1,0:T(8,128)(2,1)S(1)}, bf16[112,1024]{1,0:T(8,128)(2,1)S(1)}, u32[]{:S(2)}, u32[]{:S(2)}) collective-permute-start(bf16[112,1024]{1,0:T(8,128)(2,1)S(1)} %get-tuple-element.174), channel_id=1, source_target_pairs={{0,2},{2,0},{4,6},{6,4},{8,10},{10,8},{12,14},{14,12},{1,3},{3,1},... | collective-permute-start | bytes 688136 | tf_op jit(solution)/shard_map/ppermute | solution.py:239
  125.1 8.4 %collective-permute-start.27 = (bf16[112,1024]{1,0:T(8,128)(2,1)S(1)}, bf16[112,1024]{1,0:T(8,128)(2,1)S(1)}, u32[]{:S(2)}, u32[]{:S(2)}) collective-permute-start(bf16[112,1024]{1,0:T(8,128)(2,1)S(1)} %get-tuple-element.172), channel_id=1, source_target_pairs={{0,2},{2,0},{4,6},{6,4},{8,10},{10,8},{12,14},{14,12},{1,3},{3,1},... | collective-permute-start | bytes 688136 | tf_op jit(solution)/shard_map/ppermute | solution.py:239
  125.5 12.3 %collective-permute-start.31 = (bf16[144,1024]{1,0:T(8,128)(2,1)S(1)}, bf16[144,1024]{1,0:T(8,128)(2,1)S(1)}, u32[]{:S(2)}, u32[]{:S(2)}) collective-permute-start(bf16[144,1024]{1,0:T(8,128)(2,1)S(1)} %shard_map.135), channel_id=1, source_target_pairs={{0,4},{2,6},{4,8},{6,10},{8,12},{10,14},{12,0},{14,2},{1,5},{3,7},... | collective-permute-start | bytes 884744 | tf_op jit(solution)/shard_map/ppermute | solution.py:242
  126.0 23.0 %collective-permute-start.30 = (bf16[144,1024]{1,0:T(8,128)(2,1)S(1)}, bf16[144,1024]{1,0:T(8,128)(2,1)S(1)}, u32[]{:S(2)}, u32[]{:S(2)}) collective-permute-start(bf16[144,1024]{1,0:T(8,128)(2,1)S(1)} %shard_map.134), channel_id=1, source_target_pairs={{0,8},{2,10},{4,12},{6,14},{8,0},{10,2},{12,4},{14,6},{1,9},{3,11}... | collective-permute-start | bytes 884744 | tf_op jit(solution)/shard_map/ppermute | solution.py:242
  130.7 23.7 %collective-permute-start.29 = (bf16[144,1024]{1,0:T(8,128)(2,1)S(1)}, bf16[144,1024]{1,0:T(8,128)(2,1)S(1)}, u32[]{:S(2)}, u32[]{:S(2)}) collective-permute-start(bf16[144,1024]{1,0:T(8,128)(2,1)S(1)} %shard_map.139), channel_id=1, source_target_pairs={{0,12},{2,14},{4,0},{6,2},{8,4},{10,6},{12,8},{14,10},{1,13},{3,15... | collective-permute-start | bytes 884744 | tf_op jit(solution)/shard_map/ppermute | solution.py:242
  154.4 1.4 collective-permute-start.32
